TPU v7x, 32 devices: a whole 2x2x4 slice. The times are simulated.
32 devices in a mesh: groups: 2 (over y), dp: 4 (over z), tensor: 4 (over x, core).
Axes of the slice: x: 2, y: 2, z: 4, core: 2. Of those that a mesh axis runs over, the one named last changes fastest.
Arguments:
- partner: int32 [8], P('groups'), parts along dimension 0, may hold values from 0 to 3, as said below
- block_tenant_index: int32 [104], P(('groups', 'dp')), parts along dimension 0, may hold values from 0 to 15, as said below
- block_live_length: int32 [104], P(('groups', 'dp')), parts along dimension 0, may hold values from 9 to 128
- tenant_table_row: int32 [32], P('groups'), parts along dimension 0, may hold values from 0 to 15, as said below
- hidden: bfloat16 [13312, 8192], P(('groups', 'dp'), 'tensor'), parts along dimension 0, may hold values from -6 to 6
- cotangent: bfloat16 [13312, 1024], P(('groups', 'dp'), 'tensor'), parts along dimension 0, may hold values from -0.59765625 to 0.59765625
- frozen_value_weight: bfloat16 [8192, 1024], P('tensor'), may hold values from -0.0625 to 0.0625
- adapter_down_rows: bfloat16 [104, 64, 8192], P(('groups', 'dp'), None, 'tensor'), parts along dimension 0, as said below
- adapter_up_matrix: bfloat16 [104, 64, 1024], P(('groups', 'dp'), None, 'tensor'), parts along dimension 0, as said below
Outputs:
- projected_values: bfloat16 [13312, 1024], P(('groups', 'dp'), 'tensor'), parts along dimension 0
- down_grad_table: bfloat16 [32, 64, 8192], P(('groups', 'dp'), None, 'tensor'), parts along dimension 0
- up_grad_table: bfloat16 [32, 64, 1024], P(('groups', 'dp'), None, 'tensor'), parts along dimension 0
There are 2 independent parts, one for each index of `groups`. A program takes and returns all parts, laid end to end along the dimension named above; an argument that names none is the same for every part. Nothing has to cross between parts.
Inputs may be any that keep to these rules, and one draw needn't show every extreme that they name: partner is a permutation of the dp indices; a device may be its own partner. `block_tenant_index`: the worked blocks of one dp device have distinct tenants; with owner tenant_table_row[t] // 4, at most 4 of them share an owner, and some owner takes exactly 4 of them. `tenant_table_row`: each value once; the table rows of dp device o are o * 4 to o * 4 + 3. `adapter_down_rows`: worked blocks with the same tenant hold the same adapter. `adapter_up_matrix`: worked blocks with the same tenant hold the same adapter.
All inputs are finite; a program needn't handle non-finite values.
Results may differ from a plain program's by a relative error of at most 0.015.
Values may be sent and summed in bfloat16 or wider, within the bound.
No kernel may reach another device: no remote copies, remote signals or barrier semaphores. Data moves between devices by JAX's collectives and lax.ppermute only.
A program may use at most 192 MiB of HBM per device.

v0:
```python
import jax
import jax.numpy as jnp
from jax import lax
from jax.sharding import PartitionSpec as P

BLOCK = 128
SW = 1
OWN = 4


ADAPTER_SCALE = 0.5


def body(
    partner,
    block_tenant_index,
    block_live_length,
    tenant_table_row,
    hidden,
    cotangent,
    frozen_value_weight,
    adapter_down_rows,
    adapter_up_matrix,
):
    blocks = block_tenant_index.shape[0]
    in_width = hidden.shape[1]
    output_width = cotangent.shape[1]
    adapter_rank = adapter_down_rows.shape[1]
    kept_blocks = blocks - SW
    kept_rows = kept_blocks * BLOCK
    moving = jnp.concatenate([hidden[kept_rows:], cotangent[kept_rows:]], axis=1)
    labels = jnp.stack([block_tenant_index[kept_blocks:], block_live_length[kept_blocks:]], axis=1)
    devices = lax.axis_size("dp")
    my_index = lax.axis_index("dp")
    source_dev = partner[my_index]
    is_target = partner == my_index
    outgoing = jnp.where(is_target[:, None, None], moving[None], jnp.zeros((), moving.dtype))
    outgoing_labels = jnp.where(is_target[:, None, None], labels[None], 0)
    arrived = (
        lax.all_to_all(outgoing, "dp", split_axis=0, concat_axis=0, tiled=True),
        lax.all_to_all(outgoing_labels, "dp", split_axis=0, concat_axis=0, tiled=True),
    )
    moving = lax.dynamic_index_in_dim(arrived[0], source_dev, 0, keepdims=False)
    labels = lax.dynamic_index_in_dim(arrived[1], source_dev, 0, keepdims=False)
    worked_in = jnp.concatenate([hidden[:kept_rows], moving[:, :in_width]], axis=0).reshape(
        blocks, BLOCK, in_width
    )
    worked_cot = jnp.concatenate([cotangent[:kept_rows], moving[:, in_width:]], axis=0).reshape(
        blocks, BLOCK, output_width
    )
    tenants = jnp.concatenate([block_tenant_index[:kept_blocks], labels[:, 0]])
    lengths = jnp.concatenate([block_live_length[:kept_blocks], labels[:, 1]])
    valid = (jnp.arange(BLOCK, dtype=jnp.int32)[None, :] < lengths[:, None])[:, :, None]
    masked_input = jnp.where(valid, worked_in, jnp.zeros((), worked_in.dtype))
    masked_output_gradient = jnp.where(valid, worked_cot, jnp.zeros((), worked_cot.dtype))
    base_terms = jnp.dot(
        masked_input.reshape(-1, in_width), frozen_value_weight, preferred_element_type=jnp.float32
    )
    rank_terms = jnp.concatenate(
        [
            jnp.einsum(
                "xhf,xlf->xhl", masked_input, adapter_down_rows, preferred_element_type=jnp.float32
            ),
            jnp.einsum(
                "zuj,zaj->zua",
                masked_output_gradient,
                adapter_up_matrix,
                preferred_element_type=jnp.float32,
            ),
        ],
        axis=2,
    )
    rank_total = lax.psum(rank_terms.astype(jnp.bfloat16), "tensor").astype(jnp.float32)
    frozen_values = lax.psum_scatter(
        base_terms.astype(jnp.bfloat16), "tensor", scatter_dimension=1, tiled=True
    ).astype(jnp.float32)
    rank_input = rank_total[:, :, :adapter_rank].astype(jnp.bfloat16)
    rank_gradient = rank_total[:, :, adapter_rank:].astype(jnp.bfloat16)
    adapter_terms = jnp.einsum(
        "wfx,wxm->wfm", rank_input, adapter_up_matrix, preferred_element_type=jnp.float32
    )
    projected_values = (
        frozen_values + ADAPTER_SCALE * adapter_terms.reshape(-1, output_width)
    ).astype(jnp.bfloat16)
    down_gradients = (
        ADAPTER_SCALE
        * jnp.einsum(
            "nbr,nbd->nrd", rank_gradient, masked_input, preferred_element_type=jnp.float32
        )
    ).astype(jnp.bfloat16)
    up_gradients = (
        ADAPTER_SCALE
        * jnp.einsum(
            "nbr,nbk->nrk", rank_input, masked_output_gradient, preferred_element_type=jnp.float32
        )
    ).astype(jnp.bfloat16)
    packed = jnp.concatenate([down_gradients, up_gradients], axis=2)
    table_rows = tenant_table_row[tenants]
    owners = table_rows // OWN
    places = table_rows % OWN
    capacity = max(2, (blocks + devices - 1) // devices)
    order_ids = jnp.arange(blocks, dtype=jnp.int32)
    earlier = jnp.sum(
        (owners[None, :] == owners[:, None]) & (order_ids[None, :] < order_ids[:, None]), axis=1
    )
    targets = owners * capacity + earlier
    select = jnp.arange(devices * capacity, dtype=jnp.int32)[:, None] == targets[None, :]
    outgoing_grads = jnp.einsum(
        "sn,nrc->src", select.astype(jnp.bfloat16), packed, preferred_element_type=jnp.float32
    ).astype(jnp.bfloat16)
    outgoing_places = jnp.sum(jnp.where(select, places[None, :] + 1, 0), axis=1) - 1
    outgoing_grads = outgoing_grads.reshape(devices, capacity, adapter_rank, packed.shape[2])
    outgoing_places = outgoing_places.reshape(devices, capacity)
    arrived_grads, arrived_places = (
        lax.all_to_all(outgoing_grads, "dp", split_axis=0, concat_axis=0, tiled=True),
        lax.all_to_all(outgoing_places, "dp", split_axis=0, concat_axis=0, tiled=True),
    )
    received = arrived_grads.reshape(devices * capacity, adapter_rank, packed.shape[2])
    owned = (
        jnp.arange(OWN, dtype=jnp.int32)[:, None] == arrived_places.reshape(-1)[None, :]
    ).astype(jnp.bfloat16)
    summed = jnp.einsum("os,src->orc", owned, received, preferred_element_type=jnp.float32).astype(
        jnp.bfloat16
    )
    return (projected_values, summed[:, :, :in_width], summed[:, :, in_width:])


def solution(mesh):
    in_specs = (
        P("groups"),
        P(("groups", "dp")),
        P(("groups", "dp")),
        P("groups"),
        P(("groups", "dp"), "tensor"),
        P(("groups", "dp"), "tensor"),
        P("tensor", None),
        P(("groups", "dp"), None, "tensor"),
        P(("groups", "dp"), None, "tensor"),
    )
    out_specs = (
        P(("groups", "dp"), "tensor"),
        P(("groups", "dp"), None, "tensor"),
        P(("groups", "dp"), None, "tensor"),
    )
    return jax.shard_map(body, mesh=mesh, in_specs=in_specs, out_specs=out_specs, check_vma=False)
```

profile of v0, /device:TPU:0, one launch (start us, length us, event | category | flops | bytes accessed | tf_op | source)
XLA Modules:
  0.0 301.8 jit_solution(14208250214729025861)
XLA Ops:
  7.2 1.4 slice.52
  8.6 1.2 slice.51
  9.8 1.4 add_bitcast_fusion
  12.5 6.3 %all-to-all-start = ((s32[4,1,2]{2,1,0:T(1,128)}), s32[4,1,2]{2,1,0:T(1,128)S(1)}, u32[]{:S(2)}, u32[]{:S(2)}) async-start(s32[4,1,2]{2,1,0:T(1,128)} %broadcast_select_fusion.11), calls=%async_computation | async-start | bytes 4096 | tf_op jit(solution)/shard_map/all_to_all | solution.py:41
  19.7 1.1 slice.55
  20.8 1.7 broadcast_select_fusion.5
  22.5 1.8 all-to-all-done
  24.3 4.5 %all-to-all-start.1 = ((bf16[4,128,2304]{2,1,0:T(8,128)(2,1)}), bf16[4,128,2304]{2,1,0:T(8,128)(2,1)}, u32[]{:S(2)}, u32[]{:S(2)}) async-start(bf16[4,128,2304]{2,1,0:T(8,128)(2,1)} %broadcast_select_fusion.5), calls=%async_computation.1 | async-start | bytes 4718592 | tf_op jit(solution)/shard_map/all_to_all | solution.py:40
  30.7 2.1 slice.58
  32.8 6.6 %slice.54 = bf16[1536,2048]{1,0:T(8,128)(2,1)} slice(bf16[1664,2048]{1,0:T(8,128)(2,1)} %param.13), slice={[0:1536], [0:2048]} | slice | bytes 12582912 | tf_op jit(solution)/shard_map/slice | solution.py:45
  43.8 37.7 %all-to-all-done.1 = bf16[4,128,2304]{2,1,0:T(8,128)(2,1)} async-done(((bf16[4,128,2304]{2,1,0:T(8,128)(2,1)}), bf16[4,128,2304]{2,1,0:T(8,128)(2,1)}, u32[]{:S(2)}, u32[]{:S(2)}) %all-to-all-start.1) | async-done | bytes 2359328 | tf_op jit(solution)/shard_map/all_to_all | solution.py:40
  81.5 3.2 %all-to-all-start.2 = ((s32[4,1,4]{2,1,0:T(1,128)}), s32[4,1,4]{2,1,0:T(1,128)S(1)}, u32[]{:S(2)}, u32[]{:S(2)}) async-start(s32[4,1,4]{2,1,0:T(1,128)} %bitcast.14), calls=%async_computation.3 | async-start | bytes 4096 | tf_op jit(solution)/shard_map/all_to_all | solution.py:116
  84.8 1.1 dynamic-slice_bitcast_fusion
  85.9 0.9 slice.68
  86.8 2.1 pad_maximum_fusion.2
  88.9 7.1 %pad_maximum_fusion = bf16[1664,2048]{1,0:T(8,128)(2,1)} fusion(bf16[128,2048]{1,0:T(8,128)(2,1)} %slice.68, bf16[1536,2048]{1,0:T(8,128)(2,1)} %slice.54), kind=kLoop, calls=%fused_computation.1 | loop fusion | flops 13631488 | bytes 13631488 | tf_op jit(solution)/shard_map/concatenate | solution.py:45
  95.9 1.8 convolution_convert_fusion.2
  97.7 5.5 %fusion.14 = bf16[13,128,64]{1,2,0:T(8,128)(2,1)S(1)} fusion(bf16[13,64,2048]{2,1,0:T(8,128)(2,1)S(1)} %copy-done, bf16[13,128,2048]{2,1,0:T(8,128)(2,1)} %bitcast.40, pred[13,128]{1,0:T(8,128)(4,1)S(1)} %get-tuple-element.20), kind=kOutput, calls=%fused_computation.23 | convolution fusion | flops 439721984 | bytes 10438272 | tf_op jit(solution)/shard_map/xhf,xlf->xhl/dot_general | solution.py:61
  104.2 12.4 %fusion.6 = bf16[1664,1024]{1,0:T(8,128)(2,1)} fusion(bf16[2048,1024]{1,0:T(8,128)(2,1)} %param.15, pred[1664]{0:T(1024)(128)(4,1)S(1)} %get-tuple-element.19, bf16[128,2048]{1,0:T(8,128)(2,1)} %slice.68, bf16[1536,2048]{1,0:T(8,128)(2,1)} %slice.54), kind=kOutput, calls=%fused_computation.13 | convolution fusion | flops 6998065152 | bytes 14419584 | tf_op jit(solution)/shard_map/dot_general | solution.py:56
  116.6 21.8 %all-reduce.2.cloned.1.call-done = bf16[13,128,128]{1,2,0:T(8,128)(2,1)} async-done(((bf16[13,128,128]{1,2,0:T(8,128)(2,1)}), bf16[13,128,128]{1,2,0:T(8,128)(2,1)}) %all-reduce.2.cloned.1.call-update) | async-done | bytes 426000 | tf_op jit(solution)/shard_map/psum | solution.py:73
  138.4 4.3 %multiply_convert_fusion = bf16[13,64,2048]{2,1,0:T(8,128)(2,1)S(1)} fusion(bf16[13,128,2048]{2,1,0:T(8,128)(2,1)} %bitcast.41, pred[13,128]{1,0:T(8,128)(4,1)S(1)} %get-tuple-element.20, bf16[13,128,128]{1,2,0:T(8,128)(2,1)} %all-reduce.2.cloned.1.call-done), kind=kOutput, calls=%fused_computation.2 | convolution fusion | flops 443023360 | bytes 10438272 | tf_op jit(solution)/shard_map/nbr,nbd->nrd/dot_general | solution.py:87
  143.6 6.8 %convolution_convert_fusion = bf16[16,64,2304]{2,0,1:T(8,128)(2,1)} fusion(bf16[13,64,2304]{2,1,0:T(8,128)(2,1)S(1)} %pad_maximum_fusion.1, s32[13]{0:T(128)S(1)} %multiply_add_fusion), kind=kOutput, calls=%fused_computation.9 | convolution fusion | flops 63701200 | bytes 8552500 | tf_op jit(solution)/shard_map/sn,nrc->src/dot_general | solution.py:108
  150.4 8.8 %reshape.250 = bf16[4,4,64,2304]{3,1,0,2:T(4,128)(2,1)} reshape(bf16[16,64,2304]{2,0,1:T(8,128)(2,1)} %convolution_convert_fusion) | data formatting | bytes 9437184 | tf_op jit(solution)/shard_map/reshape | solution.py:112
  159.2 6.2 %copy.28 = bf16[4,4,64,2304]{3,1,2,0:T(4,128)(2,1)} copy(bf16[4,4,64,2304]{3,1,0,2:T(4,128)(2,1)} %reshape.250) | data formatting | bytes 9437184 | tf_op jit(solution)/shard_map/reshape | solution.py:112
  165.4 5.3 %all-to-all-start.3 = ((bf16[4,4,64,2304]{3,1,2,0:T(4,128)(2,1)}), bf16[4,4,64,2304]{3,1,2,0:T(4,128)(2,1)}, u32[]{:S(2)}, u32[]{:S(2)}) async-start(bf16[4,4,64,2304]{3,1,2,0:T(4,128)(2,1)} %copy.28), calls=%async_computation.4 | async-start | bytes 9437184 | tf_op jit(solution)/shard_map/all_to_all | solution.py:115
  172.5 8.3 %reduce-scatter.2.cloned.1.call-done = bf16[1664,256]{1,0:T(8,128)(2,1)} async-done(((bf16[1664,1024]{1,0:T(8,128)(2,1)}), bf16[1664,256]{1,0:T(8,128)(2,1)}) %reduce-scatter.2.cloned.1.call-update) | async-done | bytes 851984 | tf_op jit(solution)/shard_map/reduce_scatter | solution.py:74
  180.7 2.5 fusion.12
  183.2 91.0 %all-to-all-done.3 = bf16[4,4,64,2304]{3,1,2,0:T(4,128)(2,1)} async-done(((bf16[4,4,64,2304]{3,1,2,0:T(4,128)(2,1)}), bf16[4,4,64,2304]{3,1,2,0:T(4,128)(2,1)}, u32[]{:S(2)}, u32[]{:S(2)}) %all-to-all-start.3) | async-done | bytes 4718624 | tf_op jit(solution)/shard_map/all_to_all | solution.py:115
  274.2 6.1 %copy.29 = bf16[4,4,64,2304]{3,1,0,2:T(4,128)(2,1)} copy(bf16[4,4,64,2304]{3,1,2,0:T(4,128)(2,1)} %all-to-all-done.3) | data formatting | bytes 9437184 | tf_op jit(solution)/shard_map/all_to_all | solution.py:115
  280.3 8.6 %reshape.251 = bf16[16,64,2304]{2,0,1:T(8,128)(2,1)} reshape(bf16[4,4,64,2304]{3,1,0,2:T(4,128)(2,1)} %copy.29) | data formatting | bytes 9437184 | tf_op jit(solution)/shard_map/reshape | solution.py:118
  288.9 3.1 %convolution_convert_fusion.1 = bf16[4,64,2304]{2,0,1:T(4,128)(2,1)S(1)} fusion(bf16[16,64,2304]{2,0,1:T(8,128)(2,1)} %reshape.251, s32[16]{0:T(128)S(1)} %eq.58), kind=kOutput, calls=%fused_computation.11 | convolution fusion | flops 19464256 | bytes 5898304 | tf_op jit(solution)/shard_map/os,src->orc/dot_general | solution.py:122
  292.7 1.6 copy.30
  (55 shorter events, 11.5 us)
Async XLA Ops:
  7.2 90.5 %copy-start = (bf16[13,64,2048]{2,1,0:T(8,128)(2,1)S(1)}, bf16[13,64,2048]{2,1,0:T(8,128)(2,1)}, u32[]{:S(2)}) copy-start(bf16[13,64,2048]{2,1,0:T(8,128)(2,1)} %param.16) | copy-start | bytes 10223620
  12.5 11.8 %all-to-all-start = ((s32[4,1,2]{2,1,0:T(1,128)}), s32[4,1,2]{2,1,0:T(1,128)S(1)}, u32[]{:S(2)}, u32[]{:S(2)}) async-start(s32[4,1,2]{2,1,0:T(1,128)} %broadcast_select_fusion.11), calls=%async_computation | async-start | bytes 4096 | tf_op jit(solution)/shard_map/all_to_all | solution.py:41
  19.7 9.1 %copy-start.7 = (s32[4]{0:T(128)S(1)}, s32[4]{0:T(128)}, u32[]{:S(2)}) copy-start(s32[4]{0:T(128)} %param.9) | copy-start | bytes 52
  24.3 57.2 %all-to-all-start.1 = ((bf16[4,128,2304]{2,1,0:T(8,128)(2,1)}), bf16[4,128,2304]{2,1,0:T(8,128)(2,1)}, u32[]{:S(2)}, u32[]{:S(2)}) async-start(bf16[4,128,2304]{2,1,0:T(8,128)(2,1)} %broadcast_select_fusion.5), calls=%async_computation.1 | async-start | bytes 4718592 | tf_op jit(solution)/shard_map/all_to_all | solution.py:40
  32.7 7.3 %copy-start.8 = (s32[13]{0:T(128)S(1)}, s32[13]{0:T(128)}, u32[]{:S(2)}) copy-start(s32[13]{0:T(128)} %param.10) | copy-start | bytes 160
  32.8 8.6 %copy-start.2 = (s32[16]{0:T(128)S(1)}, s32[16]{0:T(128)}, u32[]{:S(2)}) copy-start(s32[16]{0:T(128)} %param.12) | copy-start | bytes 196
  32.8 10.3 %copy-start.9 = (s32[13]{0:T(128)S(1)}, s32[13]{0:T(128)}, u32[]{:S(2)}) copy-start(s32[13]{0:T(128)} %param.11) | copy-start | bytes 160
  81.5 83.9 %all-to-all-start.2 = ((s32[4,1,4]{2,1,0:T(1,128)}), s32[4,1,4]{2,1,0:T(1,128)S(1)}, u32[]{:S(2)}, u32[]{:S(2)}) async-start(s32[4,1,4]{2,1,0:T(1,128)} %bitcast.14), calls=%async_computation.3 | async-start | bytes 4096 | tf_op jit(solution)/shard_map/all_to_all | solution.py:116
  84.7 53.6 %all-reduce.2.cloned.1.call-start = ((), (), s32[]{:S(2)}) async-start(), calls=%async_computation.6 | async-start | bytes 851968 | tf_op jit(solution)/shard_map/psum | solution.py:73
  104.0 76.8 %reduce-scatter.2.cloned.1.call-start = ((), (), s32[]{:S(2)}) async-start(), calls=%async_computation.5 | async-start | bytes 4259840 | tf_op jit(solution)/shard_map/reduce_scatter | solution.py:74
  138.4 4.3 %copy-start.3 = (bf16[1664,256]{1,0:T(8,128)(2,1)S(1)}, bf16[1664,256]{1,0:T(8,128)(2,1)}, u32[]{:S(2)}) copy-start(bf16[1664,256]{1,0:T(8,128)(2,1)} %pad_maximum_fusion.2) | copy-start | bytes 2555908
  138.4 4.4 %copy-start.5 = (bf16[13,128,128]{1,2,0:T(8,128)(2,1)S(1)}, bf16[13,128,128]{1,2,0:T(8,128)(2,1)}, u32[]{:S(2)}) copy-start(bf16[13,128,128]{1,2,0:T(8,128)(2,1)} %all-reduce.2.cloned.1.call-done) | copy-start | bytes 1277956
  165.4 6.6 %copy-start.4 = (bf16[13,64,256]{2,1,0:T(8,128)(2,1)S(1)}, bf16[13,64,256]{2,1,0:T(8,128)(2,1)}, u32[]{:S(2)}) copy-start(bf16[13,64,256]{2,1,0:T(8,128)(2,1)} %param.17) | copy-start | bytes 1277956
  165.4 6.6 %copy-start.6 = (bf16[13,128,128]{1,2,0:T(8,128)(2,1)S(1)}, bf16[13,128,128]{1,2,0:T(8,128)(2,1)}, u32[]{:S(2)}) copy-start(bf16[13,128,128]{1,2,0:T(8,128)(2,1)} %all-reduce.2.cloned.1.call-done) | copy-start | bytes 1277956
  165.4 108.8 %all-to-all-start.3 = ((bf16[4,4,64,2304]{3,1,2,0:T(4,128)(2,1)}), bf16[4,4,64,2304]{3,1,2,0:T(4,128)(2,1)}, u32[]{:S(2)}, u32[]{:S(2)}) async-start(bf16[4,4,64,2304]{3,1,2,0:T(4,128)(2,1)} %copy.28), calls=%async_computation.4 | async-start | bytes 9437184 | tf_op jit(solution)/shard_map/all_to_all | solution.py:115
  280.3 14.6 %copy-start.1 = (bf16[13,64,2048]{2,1,0:T(8,128)(2,1)S(1)}, bf16[13,64,2048]{2,1,0:T(8,128)(2,1)}, u32[]{:S(2)}) copy-start(bf16[13,64,2048]{2,1,0:T(8,128)(2,1)} %param.16) | copy-start | bytes 10223620
Sparse Core Ops, SparseCore 0:
  104.1 34.2 all-reduce.1
  141.1 39.6 reduce-scatter.1
where the time goes:
time: 303 us; the launch traced here: 302 us
  waiting for transfers between devices  161 us (53%)
  local copies, waits for them, and re-layouts  50.9 us (17%)
  matrix products  34.8 us (11%)
  other arithmetic  19.6 us (6%)
  starting transfers between devices  19.6 us (6%)
  between operations  16.2 us (5%)
    all_to_all x1, waiting for transfers between devices, body(): lax.all_to_all(outgoing_grads, 'dp', split_axis=0, concat_axis=0, tiled=T...  91 us
    all_to_all x1, waiting for transfers between devices, body(): lax.all_to_all(outgoing, 'dp', split_axis=0, concat_axis=0, tiled=True)  37.7 us
    psum x1, waiting for transfers between devices, body(): lax.psum(rank_terms.astype(jnp.bfloat16), 'tensor').astype(jnp.float32)  21.8 us
    reshape x2, local copies, waits for them, and re-layouts, body(): outgoing_grads.reshape(devices, capacity, adapter_rank, packed.shape[2])  15 us
    dot_general x1, matrix products, body(): jnp.dot(masked_input.reshape(-1, in_width), frozen_value_weight, preferre...  12.4 us
    reshape x1, local copies, waits for them, and re-layouts, body(): arrived_grads.reshape(devices * capacity, adapter_rank, packed.shape[2])  8.57 us
    reduce_scatter x1, waiting for transfers between devices, body(): lax.psum_scatter(base_terms.astype(jnp.bfloat16), 'tensor', scatter_dimen...  8.28 us
    concatenate x1, other arithmetic, body(): jnp.concatenate([hidden[:kept_rows], moving[:, :in_width]], axis=0)  7.06 us
  transfers between devices with their start and end apart: 6, of which 5 were waited for; matrix products, arithmetic and copies ran while one was open for 26% of the time, Pallas kernels for 0%

commit v1 on v0

v1 whole, which is shorter than its diff:
```python
import functools

import jax
import jax.numpy as jnp
from jax import lax
from jax.experimental import pallas as pl
from jax.experimental.pallas import tpu as pltpu
from jax.sharding import PartitionSpec as P

BLOCK = 128
SW = 1
OWN = 4


ADAPTER_SCALE = 0.5


def table_kernel(block_of, has_block, has_last, first_row, rank_ref, rows_ref, last_ref, out_ref):
    row = first_row[0] + pl.program_id(0)
    mine = rank_ref[block_of[row]]
    mine = jnp.where(has_block[row] > 0, mine, jnp.zeros_like(mine))
    total = jnp.dot(mine, rows_ref[...], preferred_element_type=jnp.float32)

    @pl.when(has_last[row] == 0)
    def _():
        out_ref[0] = (ADAPTER_SCALE * total).astype(out_ref.dtype)

    @pl.when(has_last[row] > 0)
    def _():
        late = jnp.dot(rank_ref[rank_ref.shape[0] - 1], last_ref[...], preferred_element_type=jnp.float32)
        out_ref[0] = (ADAPTER_SCALE * (total + late)).astype(out_ref.dtype)


def grad_table(labels, first_row, rows, rank, features):
    blocks, rank_width, _ = rank.shape
    width = features.shape[1]
    return pl.pallas_call(
        table_kernel,
        grid_spec=pltpu.PrefetchScalarGridSpec(
            num_scalar_prefetch=4,
            grid=(rows,),
            in_specs=[
                pl.BlockSpec(rank.shape, lambda r, *refs: (0, 0, 0)),
                pl.BlockSpec((BLOCK, width), lambda r, at, a, b, first: (at[first[0] + r], 0)),
                pl.BlockSpec((BLOCK, width), lambda r, *refs: (blocks - 1, 0)),
            ],
            out_specs=pl.BlockSpec((1, rank_width, width), lambda r, *refs: (r, 0, 0)),
        ),
        out_shape=jax.ShapeDtypeStruct((rows, rank_width, width), rank.dtype),
        compiler_params=pltpu.CompilerParams(vmem_limit_bytes=24 * 1024 * 1024),
        cost_estimate=pl.CostEstimate(
            flops=2 * rows * rank_width * BLOCK * width,
            bytes_accessed=2 * rows * (BLOCK + rank_width) * width,
            transcendentals=0,
        ),
    )(*labels, first_row, rank, features, features)


def fetch(array, axis, source):
    size = lax.axis_size(axis)
    me = lax.axis_index(axis)
    if size > 4:
        return lax.dynamic_index_in_dim(lax.all_gather(array, axis), source, 0, keepdims=False)
    taken = array
    for shift in range(1, size):
        arrived = lax.ppermute(array, axis, [(i, (i + shift) % size) for i in range(size)])
        taken = jnp.where((me - shift) % size == source, arrived, taken)
    return taken


def exchange_sum(array, axis):
    size = lax.axis_size(axis)
    stride = 1
    while stride < size:
        arrived = lax.ppermute(array, axis, [(i, i ^ stride) for i in range(size)])
        array = (array.astype(jnp.float32) + arrived.astype(jnp.float32)).astype(array.dtype)
        stride *= 2
    return array


def line_reduce_scatter(table, axis):
    size = lax.axis_size(axis)
    me = lax.axis_index(axis)

    def entry(index):
        index = jnp.clip(index, 0, size - 1)
        return lax.dynamic_index_in_dim(table, index, 0, keepdims=False).astype(jnp.float32)

    from_left = from_right = None
    for step in range(size - 1):
        right = entry(size - 1 - step + me)
        left = entry(step - (size - 1 - me))
        if step > 0:
            right = right + from_left.astype(jnp.float32)
            left = left + from_right.astype(jnp.float32)
        from_left = lax.ppermute(
            right.astype(table.dtype), axis, [(i, i + 1) for i in range(step + 1)]
        )
        from_right = lax.ppermute(
            left.astype(table.dtype), axis, [(i, i - 1) for i in range(size - 1 - step, size)]
        )
    own = entry(me)
    if size > 1:
        own = own + from_left.astype(jnp.float32) + from_right.astype(jnp.float32)
    return own.astype(table.dtype)


def base_sum(hidden, weight, axis):
    size = lax.axis_size(axis)
    me = lax.axis_index(axis)
    width = weight.shape[1] // size

    def term(columns):
        part = lax.dynamic_slice_in_dim(weight, columns * width, width, 1)
        return jnp.dot(hidden, part, preferred_element_type=jnp.float32).astype(hidden.dtype)

    near = [(i, i ^ 1) for i in range(size)]
    far = [(i, i ^ 2) for i in range(size)]
    first = lax.ppermute(term(me ^ 3), axis, near)
    away = (term(me ^ 2).astype(jnp.float32) + first.astype(jnp.float32)).astype(hidden.dtype)
    second = lax.ppermute(away, axis, far)
    third = lax.ppermute(term(me ^ 1), axis, near)
    return (
        term(me).astype(jnp.float32) + third.astype(jnp.float32) + second.astype(jnp.float32)
    )


def body(
    partner,
    block_tenant_index,
    block_live_length,
    tenant_table_row,
    hidden,
    cotangent,
    frozen_value_weight,
    adapter_down_rows,
    adapter_up_matrix,
):
    blocks = block_tenant_index.shape[0]
    output_width = cotangent.shape[1]
    rank_width = adapter_down_rows.shape[1]
    kept = blocks - SW
    kind = hidden.dtype
    devices = lax.axis_size("dp")
    me = lax.axis_index("dp")
    holder = jnp.sum(jnp.where(partner == me, jnp.arange(devices, dtype=jnp.int32), 0))
    source = partner[me]
    up_last = fetch(adapter_up_matrix[kept:], "dp", holder)
    up_maps = jnp.concatenate([adapter_up_matrix[:kept], up_last], axis=0)
    live = (jnp.arange(BLOCK, dtype=jnp.int32)[None, :] < block_live_length[:, None])[:, None, :]
    cot_blocks = cotangent.reshape(blocks, BLOCK, output_width)
    hidden_blocks = hidden.reshape(blocks, BLOCK, hidden.shape[1])

    cot_terms = jnp.einsum("zaj,zuj->zau", up_maps, cot_blocks, preferred_element_type=jnp.float32)
    rank_cot = exchange_sum(jnp.where(live, cot_terms, 0.0).astype(kind), "tensor")

    table_rows = jnp.sum(
        jnp.where(
            block_tenant_index[:, None] == jnp.arange(tenant_table_row.shape[0], dtype=jnp.int32)[None, :],
            tenant_table_row[None, :],
            0,
        ),
        axis=1,
    )
    rows = devices * OWN
    matches = jnp.arange(rows, dtype=jnp.int32)[:, None] == table_rows[None, :]
    block_of = jnp.sum(jnp.where(matches[:, :kept], jnp.arange(kept, dtype=jnp.int32)[None, :], 0), axis=1)
    has_block = jnp.any(matches[:, :kept], axis=1).astype(jnp.int32)
    has_last = matches[:, kept].astype(jnp.int32)
    labels = (block_of, has_block, has_last)
    start = jnp.zeros((1,), jnp.int32)

    down_table = grad_table(labels, start, rows, rank_cot, hidden)
    down_out = line_reduce_scatter(
        down_table.reshape(devices, OWN, rank_width, hidden.shape[1]), "dp"
    )

    down_last = fetch(adapter_down_rows[kept:], "dp", holder)
    in_terms = jnp.concatenate(
        [
            jnp.einsum(
                "xlf,xhf->xlh", adapter_down_rows[:kept], hidden_blocks[:kept], preferred_element_type=jnp.float32
            ),
            jnp.einsum("xlf,xhf->xlh", down_last, hidden_blocks[kept:], preferred_element_type=jnp.float32),
        ],
        axis=0,
    )
    rank_in = exchange_sum(jnp.where(live, in_terms, 0.0).astype(kind), "tensor")
    up_table = grad_table(labels, start, rows, rank_in, cotangent)
    up_out = line_reduce_scatter(up_table.reshape(devices, OWN, rank_width, output_width), "dp")

    frozen_values = base_sum(hidden, frozen_value_weight, "tensor")
    adapter_terms = jnp.einsum("wxf,wxm->wfm", rank_in, up_maps, preferred_element_type=jnp.float32)
    values = frozen_values + ADAPTER_SCALE * adapter_terms.reshape(-1, output_width)
    values = jnp.where(live.reshape(-1, 1), values, 0.0).astype(kind)
    last_values = fetch(values[kept * BLOCK :], "dp", source)
    projected_values = jnp.concatenate([values[: kept * BLOCK], last_values], axis=0)
    return (projected_values, down_out, up_out)


def solution(mesh):
    in_specs = (
        P("groups"),
        P(("groups", "dp")),
        P(("groups", "dp")),
        P("groups"),
        P(("groups", "dp"), "tensor"),
        P(("groups", "dp"), "tensor"),
        P("tensor", None),
        P(("groups", "dp"), None, "tensor"),
        P(("groups", "dp"), None, "tensor"),
    )
    out_specs = (
        P(("groups", "dp"), "tensor"),
        P(("groups", "dp"), None, "tensor"),
        P(("groups", "dp"), None, "tensor"),
    )
    return jax.shard_map(body, mesh=mesh, in_specs=in_specs, out_specs=out_specs, check_vma=False)
```

time: 303 us -> 193 us (0.64)
  waiting for transfers between devices: 161 us -> 47.4 us
  starting transfers between devices: 19.6 us -> 61.5 us
  local copies, waits for them, and re-layouts: 50.9 us -> 17.3 us
  between operations: 16.2 us -> 5.02 us
  Pallas kernels: 0 us -> 7.99 us
  matrix products: 34.8 us -> 31.4 us
    all_to_all x4 -> x0, waiting for transfers between devices: 131 us -> none  [the longest x1 91 us: body(): lax.all_to_all(outgoing_grads, 'dp', split_axis=0, concat_axis=0, tiled=T...]
    ppermute x0 -> x28, starting transfers between devices: none -> 61.5 us  [the longest x6 33.4 us: line_reduce_scatter(): lax.ppermute(right.astype(table.dtype), axis, [(i, i + 1) for i in range(...]
    ppermute x0 -> x28, waiting for transfers between devices: none -> 47.4 us  [the longest x9 23.6 us: fetch(): lax.ppermute(array, axis, [(i, (i + shift) % size) for i in range(size)])]
    reshape x3 -> x0, local copies, waits for them, and re-layouts: 23.6 us -> none  [the longest x2 15 us: body(): outgoing_grads.reshape(devices, capacity, adapter_rank, packed.shape[2])]
    psum x1 -> x0, waiting for transfers between devices: 21.8 us -> none  [body(): lax.psum(rank_terms.astype(jnp.bfloat16), 'tensor').astype(jnp.float32)]
    all_to_all x4 -> x0, starting transfers between devices: 19.4 us -> none  [the longest x1 6.32 us: body(): lax.all_to_all(outgoing_labels, 'dp', split_axis=0, concat_axis=0, tiled=...]
    convert_element_type x1 -> x16, other arithmetic: 2.45 us -> 19.5 us  [the longest x4 7.11 us: line_reduce_scatter(): right.astype(table.dtype)]
    concatenate x6 -> x1, other arithmetic: 11.1 us -> 0.06 us  [body(): jnp.concatenate([values[:kept * BLOCK], last_values], axis=0)]
  transfers between devices with their start and end apart: 6 -> 28, of which waited for: 5 -> 7; matrix products, arithmetic and copies ran while one was open for 26% -> 29% of each run, Pallas kernels for 0% -> 4%
where the time goes in v1:
time: 193 us; the launch traced here: 192 us
  starting transfers between devices  61.5 us (32%)
  waiting for transfers between devices  47.4 us (25%)
  matrix products  31.4 us (16%)
  other arithmetic  21.3 us (11%)
  local copies, waits for them, and re-layouts  17.3 us (9%)
  Pallas kernels  7.99 us (4%)
  between operations  5.02 us (3%)
    ppermute x6, starting transfers between devices, line_reduce_scatter(): lax.ppermute(right.astype(table.dtype), axis, [(i, i + 1) for i in range(...  33.4 us
    dot_general x4, matrix products, term(): jnp.dot(hidden, part, preferred_element_type=jnp.float32)  23.8 us
    ppermute x9, waiting for transfers between devices, fetch(): lax.ppermute(array, axis, [(i, (i + shift) % size) for i in range(size)])  23.6 us
    ppermute x6, waiting for transfers between devices, line_reduce_scatter(): lax.ppermute(right.astype(table.dtype), axis, [(i, i + 1) for i in range(...  21 us
    ppermute x9, starting transfers between devices, fetch(): lax.ppermute(array, axis, [(i, (i + shift) % size) for i in range(size)])  16.2 us
    pallas_call x2, Pallas kernels, grad_table(): pl.pallas_call(table_kernel, grid_spec=pltpu.PrefetchScalarGridSpec(num_s...  7.99 us
    unnamed x31, local copies, waits for them, and re-layouts  7.28 us
    convert_element_type x4, other arithmetic, line_reduce_scatter(): right.astype(table.dtype)  7.11 us
  transfers between devices with their start and end apart: 28, of which 7 were waited for; matrix products, arithmetic and copies ran while one was open for 29% of the time, Pallas kernels for 4%

profile of v1, /device:TPU:0, one launch (start us, length us, event | category | flops | bytes accessed | tf_op | source)
XLA Modules:
  0.0 191.9 jit_solution(8020709575525852074)
XLA Ops:
  0.6 1.7 slice.38
  2.3 5.0 %collective-permute-start.3 = (bf16[1,64,2048]{2,1,0:T(8,128)(2,1)}, bf16[1,64,2048]{2,1,0:T(8,128)(2,1)}, u32[]{:S(2)}, u32[]{:S(2)}) collective-permute-start(bf16[1,64,2048]{2,1,0:T(8,128)(2,1)} %slice.38), channel_id=1, source_target_pairs={{0,12},{4,0},{8,4},{12,8},{1,13},{5,1},{9,5},{13,9},{2,14},{6,2},{... | collective-permute-start | bytes 786440 | tf_op jit(solution)/shard_map/ppermute | solution.py:66
  9.1 2.8 %collective-permute-start.8 = (bf16[1,64,256]{2,1,0:T(8,128)(2,1)S(1)}, bf16[1,64,256]{2,1,0:T(8,128)(2,1)S(1)}, u32[]{:S(2)}, u32[]{:S(2)}) collective-permute-start(bf16[1,64,256]{2,1,0:T(8,128)(2,1)S(1)} %slice.41), channel_id=1, source_target_pairs={{0,12},{4,0},{8,4},{12,8},{1,13},{5,1},{9,5},{13,9},{2,14},{6,2},{... | collective-permute-start | bytes 98312 | tf_op jit(solution)/shard_map/ppermute | solution.py:66
  13.8 2.8 %slice-done.2 = bf16[1536,2048]{1,0:T(8,128)(2,1)S(1)} async-done(((bf16[1664,2048]{1,0:T(8,128)(2,1)}), bf16[1536,2048]{1,0:T(8,128)(2,1)S(1)}, s32[]{:S(2)}) %slice-start.2) | async-done | bytes 6291480 | tf_op jit(solution)/shard_map/slice | solution.py:182
  17.6 3.0 %fusion.44 = bf16[12,64,128]{2,1,0:T(8,128)(2,1)} fusion(bf16[13,64,2048]{2,1,0:T(8,128)(2,1)S(1)} %copy-done.3, bf16[12,128,2048]{2,1,0:T(8,128)(2,1)S(1)} %bitcast.73), kind=kOutput, calls=%fused_computation.82 | convolution fusion | flops 402653184 | bytes 9895936 | tf_op jit(solution)/shard_map/xlf,xhf->xlh/dot_general | solution.py:181
  20.9 6.4 %fusion.5 = bf16[1664,256]{0,1:T(8,128)(2,1)} fusion(bf16[1664,2048]{1,0:T(8,128)(2,1)} %last_ref.2, bf16[2048,1024]{1,0:T(8,128)(2,1)} %param.15, s32[]{:T(128)S(6)} %select_n.144), kind=kOutput, calls=%fused_computation.9 | convolution fusion | flops 1745256448 | bytes 8716292 | tf_op jit(solution)/shard_map/dot_general | solution.py:115
  36.4 3.0 %collective-permute-done.5 = bf16[1,64,2048]{2,1,0:T(8,128)(2,1)} collective-permute-done((bf16[1,64,2048]{2,1,0:T(8,128)(2,1)}, bf16[1,64,2048]{2,1,0:T(8,128)(2,1)}, u32[]{:S(2)}, u32[]{:S(2)}) %collective-permute-start.5) | collective-permute-done | bytes 262176 | tf_op jit(solution)/shard_map/ppermute | solution.py:66
  41.0 1.7 collective-permute-done.15
  43.8 2.9 %copy-done = bf16[1664,2048]{1,0:T(8,128)(2,1)S(1)} copy-done((bf16[1664,2048]{1,0:T(8,128)(2,1)S(1)}, bf16[1664,2048]{1,0:T(8,128)(2,1)}, u32[]{:S(2)}) %copy-start) | copy-done | bytes 6815768
  46.7 5.1 %shard_map.112 = bf16[16,64,2048]{2,1,0:T(8,128)(2,1)S(1)} custom-call(s32[16]{0:T(128)S(1)} %select_reduce_fusion.block_of, s32[16]{0:T(128)S(1)} %convert_element_type.253.has_block, s32[16]{0:T(128)S(1)} %fusion.39.has_last, s32[1]{0:T(128)} %constant.102.clone.1.first_row, bf16[13,64,128]{2,1,0:T(8,128)(2,1)S(1)} %add_convert_fusion.1.rank_ref, ...), custom_call_target="tpu_custom_call" | custom-call | flops 536870912 | bytes 12582912 | tf_op jit(solution)/shard_map/pallas_call | solution.py:37
  54.4 5.3 %collective-permute-start.16 = (bf16[4,64,2048]{2,1,0:T(8,128)(2,1)}, bf16[4,64,2048]{2,1,0:T(8,128)(2,1)}, u32[]{:S(2)}, u32[]{:S(2)}) collective-permute-start(bf16[4,64,2048]{2,1,0:T(8,128)(2,1)} %get-tuple-element.14), channel_id=1, source_target_pairs={{0,4},{1,5},{2,6},{3,7},{16,20},{17,21},{18,22},{19,23}} | collective-permute-start | bytes 3145736 | tf_op jit(solution)/shard_map/ppermute | solution.py:96
  60.5 4.3 %fusion.4 = bf16[1664,256]{0,1:T(8,128)(2,1)} fusion(bf16[1664,2048]{1,0:T(8,128)(2,1)S(1)} %bitcast.72, bf16[2048,1024]{1,0:T(8,128)(2,1)} %param.15, s32[]{:T(128)S(6)} %select_n.142), kind=kOutput, calls=%fused_computation.8 | convolution fusion | flops 1745256448 | bytes 8716292 | tf_op jit(solution)/shard_map/dot_general | solution.py:115
  65.2 1.6 collective-permute-start.19
  69.5 11.5 %collective-permute-done.16 = bf16[4,64,2048]{2,1,0:T(8,128)(2,1)} collective-permute-done((bf16[4,64,2048]{2,1,0:T(8,128)(2,1)}, bf16[4,64,2048]{2,1,0:T(8,128)(2,1)}, u32[]{:S(2)}, u32[]{:S(2)}) %collective-permute-start.16) | collective-permute-done | bytes 1048608 | tf_op jit(solution)/shard_map/ppermute | solution.py:96
  81.0 1.9 %fusion.8 = bf16[4,64,2048]{2,1,0:T(8,128)(2,1)S(1)} fusion(bf16[4,64,2048]{2,1,0:T(8,128)(2,1)} %collective-permute-done.16, bf16[4,4,64,2048]{3,2,1,0:T(8,128)(2,1)} %bitcast.75, s32[]{:T(128)S(6)} %min.31), kind=kLoop, calls=%fused_computation.15 | loop fusion | flops 2097152 | bytes 3145732 | tf_op jit(solution)/shard_map/convert_element_type | solution.py:97
  83.0 5.4 %collective-permute-start.17 = (bf16[4,64,2048]{2,1,0:T(8,128)(2,1)S(1)}, bf16[4,64,2048]{2,1,0:T(8,128)(2,1)}, u32[]{:S(2)}, u32[]{:S(2)}) collective-permute-start(bf16[4,64,2048]{2,1,0:T(8,128)(2,1)S(1)} %fusion.8), channel_id=1, source_target_pairs={{0,4},{4,8},{1,5},{5,9},{2,6},{6,10},{3,7},{7,11},{16,20},{20,24},... | collective-permute-start | bytes 3145736 | tf_op jit(solution)/shard_map/ppermute | solution.py:96
  88.4 2.9 %shard_map.113 = bf16[16,64,256]{2,1,0:T(8,128)(2,1)S(1)} custom-call(s32[16]{0:T(128)S(1)} %select_reduce_fusion.block_of, s32[16]{0:T(128)S(1)} %convert_element_type.253.has_block, s32[16]{0:T(128)S(1)} %fusion.39.has_last, s32[1]{0:T(128)} %constant.102.clone.1.first_row, bf16[13,64,128]{2,1,0:T(8,128)(2,1)S(1)} %add_convert_fusion.3.rank_ref, ...), custom_call_target="tpu_custom_call" | custom-call | flops 67108864 | bytes 1572864 | tf_op jit(solution)/shard_map/pallas_call | solution.py:37
  92.7 6.7 %fusion.3 = f32[1664,256]{0,1:T(8,128)} fusion(bf16[1664,2048]{1,0:T(8,128)(2,1)} %last_ref.2, bf16[2048,1024]{1,0:T(8,128)(2,1)} %param.15, s32[]{:T(128)S(6)} %select_n.141), kind=kOutput, calls=%fused_computation.7 | convolution fusion | flops 1745682432 | bytes 9568260 | tf_op jit(solution)/shard_map/dot_general | solution.py:115
  101.9 9.5 %collective-permute-done.22 = bf16[4,64,256]{2,1,0:T(8,128)(2,1)S(1)} collective-permute-done((bf16[4,64,256]{2,1,0:T(8,128)(2,1)S(1)}, bf16[4,64,256]{2,1,0:T(8,128)(2,1)S(1)}, u32[]{:S(2)}, u32[]{:S(2)}) %collective-permute-start.22) | collective-permute-done | bytes 131104 | tf_op jit(solution)/shard_map/ppermute | solution.py:96
  112.1 4.6 %collective-permute-start.23 = (bf16[4,64,256]{2,1,0:T(8,128)(2,1)S(1)}, bf16[4,64,256]{2,1,0:T(8,128)(2,1)S(1)}, u32[]{:S(2)}, u32[]{:S(2)}) collective-permute-start(bf16[4,64,256]{2,1,0:T(8,128)(2,1)S(1)} %fusion.23), channel_id=1, source_target_pairs={{0,4},{4,8},{1,5},{5,9},{2,6},{6,10},{3,7},{7,11},{16,20},{20,24},... | collective-permute-start | bytes 393224 | tf_op jit(solution)/shard_map/ppermute | solution.py:96
  116.7 4.4 %fusion.9 = (bf16[4,64,2048]{2,1,0:T(8,128)(2,1)}, bf16[4,64,2048]{2,1,0:T(8,128)(2,1)}) fusion(bf16[4,64,2048]{2,1,0:T(8,128)(2,1)} %collective-permute-done.17, bf16[4,4,64,2048]{3,2,1,0:T(8,128)(2,1)} %bitcast.76, s32[]{:T(128)S(6)} %min.30, bf16[4,64,2048]{2,1,0:T(8,128)(2,1)} %collective-permute-done.19, s32[]{:T(128)S(6)} %min.34), kind=kLoop, calls=%fused_computation.17 | loop fusion | flops 4194304 | bytes 6291464 | tf_op jit(solution)/shard_map/convert_element_type | solution.py:97
  122.0 6.4 %add_convert_fusion = bf16[1664,256]{0,1:T(8,128)(2,1)} fusion(bf16[1664,256]{0,1:T(8,128)(2,1)} %collective-permute-done.1, bf16[1664,2048]{1,0:T(8,128)(2,1)} %last_ref.2, bf16[2048,1024]{1,0:T(8,128)(2,1)} %param.15, s32[]{:T(128)S(6)} %select_n.143), kind=kOutput, calls=%fused_computation.22 | convolution fusion | flops 1746960384 | bytes 9568260 | tf_op jit(solution)/shard_map/dot_general | solution.py:115
  131.3 1.6 convolution_multiply_fusion
  132.9 1.8 copy.16
  134.8 3.2 %collective-permute-start.24 = (bf16[4,64,256]{2,1,0:T(8,128)(2,1)S(1)}, bf16[4,64,256]{2,1,0:T(8,128)(2,1)S(1)}, u32[]{:S(2)}, u32[]{:S(2)}) collective-permute-start(bf16[4,64,256]{2,1,0:T(8,128)(2,1)S(1)} %copy-done.9), channel_id=1, source_target_pairs={{0,4},{4,8},{8,12},{1,5},{5,9},{9,13},{2,6},{6,10},{10,14},{3,7},{... | collective-permute-start | bytes 393224 | tf_op jit(solution)/shard_map/ppermute | solution.py:96
  140.4 13.6 %collective-permute-start.18 = (bf16[4,64,2048]{2,1,0:T(8,128)(2,1)}, bf16[4,64,2048]{2,1,0:T(8,128)(2,1)S(1)}, u32[]{:S(2)}, u32[]{:S(2)}) collective-permute-start(bf16[4,64,2048]{2,1,0:T(8,128)(2,1)} %get-tuple-element.12), channel_id=1, source_target_pairs={{0,4},{4,8},{8,12},{1,5},{5,9},{9,13},{2,6},{6,10},{10,14},{3,7},{... | collective-permute-start | bytes 3145736 | tf_op jit(solution)/shard_map/ppermute | solution.py:96
  154.0 2.9 %fusion.7 = bf16[4,64,2048]{2,1,0:T(8,128)(2,1)} fusion(bf16[4,64,2048]{2,1,0:T(8,128)(2,1)} %copy-done.7, bf16[4,4,64,2048]{3,2,1,0:T(8,128)(2,1)} %bitcast.77, s32[]{:T(128)S(6)} %min.33), kind=kLoop, calls=%fused_computation.13 | loop fusion | flops 2097152 | bytes 3145732 | tf_op jit(solution)/shard_map/convert_element_type | solution.py:100
  158.2 1.9 select_convert_fusion
  160.1 4.5 %collective-permute-start.11 = (bf16[128,256]{0,1:T(8,128)(2,1)S(1)}, bf16[128,256]{0,1:T(8,128)(2,1)S(1)}, u32[]{:S(2)}, u32[]{:S(2)}) collective-permute-start(bf16[128,256]{0,1:T(8,128)(2,1)S(1)} %slice.47), channel_id=1, source_target_pairs={{0,12},{4,0},{8,4},{12,8},{1,13},{5,1},{9,5},{13,9},{2,14},{6,2},{... | collective-permute-start | bytes 196616 | tf_op jit(solution)/shard_map/ppermute | solution.py:66
  167.0 16.6 %collective-permute-done.11 = bf16[128,256]{0,1:T(8,128)(2,1)S(1)} collective-permute-done((bf16[128,256]{0,1:T(8,128)(2,1)S(1)}, bf16[128,256]{0,1:T(8,128)(2,1)S(1)}, u32[]{:S(2)}, u32[]{:S(2)}) %collective-permute-start.11) | collective-permute-done | bytes 65568 | tf_op jit(solution)/shard_map/ppermute | solution.py:66
  183.6 3.9 %collective-permute-done.12 = bf16[128,256]{0,1:T(8,128)(2,1)S(1)} collective-permute-done((bf16[128,256]{0,1:T(8,128)(2,1)S(1)}, bf16[128,256]{0,1:T(8,128)(2,1)S(1)}, u32[]{:S(2)}, u32[]{:S(2)}) %collective-permute-start.12) | collective-permute-done | bytes 65568 | tf_op jit(solution)/shard_map/ppermute | solution.py:66
  188.9 3.1 %fusion.11 = bf16[4,64,2048]{2,1,0:T(8,128)(2,1)} fusion(bf16[4,64,2048]{2,1,0:T(8,128)(2,1)} %collective-permute-done.21, bf16[4,64,2048]{2,1,0:T(8,128)(2,1)S(1)} %collective-permute-done.18, bf16[4,4,64,2048]{3,2,1,0:T(8,128)(2,1)} %bitcast.78, s32[]{:T(128)S(6)} %min.29), kind=kLoop, calls=%fused_computation.20 | loop fusion | flops 3145728 | bytes 4194308 | tf_op jit(solution)/shard_map/convert_element_type | solution.py:105
  (102 shorter events, 34.9 us)
Async XLA Ops:
  2.3 34.1 %collective-permute-start.3 = (bf16[1,64,2048]{2,1,0:T(8,128)(2,1)}, bf16[1,64,2048]{2,1,0:T(8,128)(2,1)}, u32[]{:S(2)}, u32[]{:S(2)}) collective-permute-start(bf16[1,64,2048]{2,1,0:T(8,128)(2,1)} %slice.38), channel_id=1, source_target_pairs={{0,12},{4,0},{8,4},{12,8},{1,13},{5,1},{9,5},{13,9},{2,14},{6,2},{... | collective-permute-start | bytes 786440 | tf_op jit(solution)/shard_map/ppermute | solution.py:66
  7.4 29.1 %collective-permute-start.4 = (bf16[1,64,2048]{2,1,0:T(8,128)(2,1)}, bf16[1,64,2048]{2,1,0:T(8,128)(2,1)}, u32[]{:S(2)}, u32[]{:S(2)}) collective-permute-start(bf16[1,64,2048]{2,1,0:T(8,128)(2,1)} %slice.38), channel_id=1, source_target_pairs={{0,8},{4,12},{8,0},{12,4},{1,9},{5,13},{9,1},{13,5},{2,10},{6,14},... | collective-permute-start | bytes 786440 | tf_op jit(solution)/shard_map/ppermute | solution.py:66
  8.1 22.5 %collective-permute-start.10 = (bf16[1,64,256]{2,1,0:T(8,128)(2,1)S(1)}, bf16[1,64,256]{2,1,0:T(8,128)(2,1)S(1)}, u32[]{:S(2)}, u32[]{:S(2)}) collective-permute-start(bf16[1,64,256]{2,1,0:T(8,128)(2,1)S(1)} %slice.41), channel_id=1, source_target_pairs={{0,4},{4,8},{8,12},{12,0},{1,5},{5,9},{9,13},{13,1},{2,6},{6,10},{... | collective-permute-start | bytes 98312 | tf_op jit(solution)/shard_map/ppermute | solution.py:66
  9.1 21.6 %collective-permute-start.8 = (bf16[1,64,256]{2,1,0:T(8,128)(2,1)S(1)}, bf16[1,64,256]{2,1,0:T(8,128)(2,1)S(1)}, u32[]{:S(2)}, u32[]{:S(2)}) collective-permute-start(bf16[1,64,256]{2,1,0:T(8,128)(2,1)S(1)} %slice.41), channel_id=1, source_target_pairs={{0,12},{4,0},{8,4},{12,8},{1,13},{5,1},{9,5},{13,9},{2,14},{6,2},{... | collective-permute-start | bytes 98312 | tf_op jit(solution)/shard_map/ppermute | solution.py:66
  11.9 18.9 %collective-permute-start.9 = (bf16[1,64,256]{2,1,0:T(8,128)(2,1)S(1)}, bf16[1,64,256]{2,1,0:T(8,128)(2,1)S(1)}, u32[]{:S(2)}, u32[]{:S(2)}) collective-permute-start(bf16[1,64,256]{2,1,0:T(8,128)(2,1)S(1)} %slice.41), channel_id=1, source_target_pairs={{0,8},{4,12},{8,0},{12,4},{1,9},{5,13},{9,1},{13,5},{2,10},{6,14},... | collective-permute-start | bytes 98312 | tf_op jit(solution)/shard_map/ppermute | solution.py:66
  30.7 8.8 %collective-permute-start.5 = (bf16[1,64,2048]{2,1,0:T(8,128)(2,1)}, bf16[1,64,2048]{2,1,0:T(8,128)(2,1)}, u32[]{:S(2)}, u32[]{:S(2)}) collective-permute-start(bf16[1,64,2048]{2,1,0:T(8,128)(2,1)} %slice.38), channel_id=1, source_target_pairs={{0,4},{4,8},{8,12},{12,0},{1,5},{5,9},{9,13},{13,1},{2,6},{6,10},{... | collective-permute-start | bytes 786440 | tf_op jit(solution)/shard_map/ppermute | solution.py:66
  30.7 91.2 %collective-permute-start.1 = (bf16[1664,256]{0,1:T(8,128)(2,1)}, bf16[1664,256]{0,1:T(8,128)(2,1)}, u32[]{:S(2)}, u32[]{:S(2)}) collective-permute-start(bf16[1664,256]{0,1:T(8,128)(2,1)} %fusion.5), channel_id=1, source_target_pairs={{0,1},{1,0},{2,3},{3,2},{4,5},{5,4},{6,7},{7,6},{8,9},{9,8},{10,11... | collective-permute-start | bytes 2555912 | tf_op jit(solution)/shard_map/ppermute | solution.py:119
  30.9 29.6 %slice-start = ((s8[6815744]{0:T(1024)(128)(4,1)}), s8[2621440]{0:T(1024)(128)(4,1)S(1)}, s32[]{:S(2)}) async-start(s8[6815744]{0:T(1024)(128)(4,1)} %bitcast.71), calls=%async_computation | async-start | bytes 5242880
  32.5 1.6 collective-permute-start.14
  34.9 7.8 %collective-permute-start.15 = (bf16[13,64,128]{2,1,0:T(8,128)(2,1)}, bf16[13,64,128]{2,1,0:T(8,128)(2,1)}, u32[]{:S(2)}, u32[]{:S(2)}) collective-permute-start(bf16[13,64,128]{2,1,0:T(8,128)(2,1)} %add_convert_fusion.2), channel_id=1, source_target_pairs={{0,2},{1,3},{2,0},{3,1},{4,6},{5,7},{6,4},{7,5},{8,10},{9,11},{10,... | collective-permute-start | bytes 638984 | tf_op jit(solution)/shard_map/ppermute | solution.py:75
  46.7 13.7 %slice-start.1 = ((s8[6815744]{0:T(1024)(128)(4,1)}), s8[4194304]{0:T(1024)(128)(4,1)S(1)}, s32[]{:S(2)}) async-start(s8[6815744]{0:T(1024)(128)(4,1)} %bitcast.71), calls=%async_computation.1 | async-start | bytes 8388608
  54.4 26.6 %collective-permute-start.16 = (bf16[4,64,2048]{2,1,0:T(8,128)(2,1)}, bf16[4,64,2048]{2,1,0:T(8,128)(2,1)}, u32[]{:S(2)}, u32[]{:S(2)}) collective-permute-start(bf16[4,64,2048]{2,1,0:T(8,128)(2,1)} %get-tuple-element.14), channel_id=1, source_target_pairs={{0,4},{1,5},{2,6},{3,7},{16,20},{17,21},{18,22},{19,23}} | collective-permute-start | bytes 3145736 | tf_op jit(solution)/shard_map/ppermute | solution.py:96
  60.4 6.4 %collective-permute-start.6 = (bf16[13,64,128]{2,1,0:T(8,128)(2,1)}, bf16[13,64,128]{2,1,0:T(8,128)(2,1)}, u32[]{:S(2)}, u32[]{:S(2)}) collective-permute-start(bf16[13,64,128]{2,1,0:T(8,128)(2,1)} %fusion.20), channel_id=1, source_target_pairs={{0,1},{1,0},{2,3},{3,2},{4,5},{5,4},{6,7},{7,6},{8,9},{9,8},{10,11... | collective-permute-start | bytes 638984 | tf_op jit(solution)/shard_map/ppermute | solution.py:75
  64.7 92.2 %collective-permute-start = (bf16[1664,256]{0,1:T(8,128)(2,1)}, bf16[1664,256]{0,1:T(8,128)(2,1)}, u32[]{:S(2)}, u32[]{:S(2)}) collective-permute-start(bf16[1664,256]{0,1:T(8,128)(2,1)} %fusion.4), channel_id=1, source_target_pairs={{0,1},{1,0},{2,3},{3,2},{4,5},{5,4},{6,7},{7,6},{8,9},{9,8},{10,11... | collective-permute-start | bytes 2555912 | tf_op jit(solution)/shard_map/ppermute | solution.py:122
  65.2 46.9 %collective-permute-start.19 = (bf16[4,64,2048]{2,1,0:T(8,128)(2,1)}, bf16[4,64,2048]{2,1,0:T(8,128)(2,1)}, u32[]{:S(2)}, u32[]{:S(2)}) collective-permute-start(bf16[4,64,2048]{2,1,0:T(8,128)(2,1)} %get-tuple-element.15), channel_id=1, source_target_pairs={{12,8},{13,9},{14,10},{15,11},{28,24},{29,25},{30,26},{31,27}} | collective-permute-start | bytes 3145736 | tf_op jit(solution)/shard_map/ppermute | solution.py:99
  68.0 20.4 %collective-permute-start.7 = (bf16[13,64,128]{2,1,0:T(8,128)(2,1)S(1)}, bf16[13,64,128]{2,1,0:T(8,128)(2,1)S(1)}, u32[]{:S(2)}, u32[]{:S(2)}) collective-permute-start(bf16[13,64,128]{2,1,0:T(8,128)(2,1)S(1)} %add_convert_fusion.4), channel_id=1, source_target_pairs={{0,2},{1,3},{2,0},{3,1},{4,6},{5,7},{6,4},{7,5},{8,10},{9,11},{10,... | collective-permute-start | bytes 638984 | tf_op jit(solution)/shard_map/ppermute | solution.py:75
  83.0 33.7 %collective-permute-start.17 = (bf16[4,64,2048]{2,1,0:T(8,128)(2,1)S(1)}, bf16[4,64,2048]{2,1,0:T(8,128)(2,1)}, u32[]{:S(2)}, u32[]{:S(2)}) collective-permute-start(bf16[4,64,2048]{2,1,0:T(8,128)(2,1)S(1)} %fusion.8), channel_id=1, source_target_pairs={{0,4},{4,8},{1,5},{5,9},{2,6},{6,10},{3,7},{7,11},{16,20},{20,24},... | collective-permute-start | bytes 3145736 | tf_op jit(solution)/shard_map/ppermute | solution.py:96
  91.4 20.0 %collective-permute-start.22 = (bf16[4,64,256]{2,1,0:T(8,128)(2,1)S(1)}, bf16[4,64,256]{2,1,0:T(8,128)(2,1)S(1)}, u32[]{:S(2)}, u32[]{:S(2)}) collective-permute-start(bf16[4,64,256]{2,1,0:T(8,128)(2,1)S(1)} %get-tuple-element.18), channel_id=1, source_target_pairs={{0,4},{1,5},{2,6},{3,7},{16,20},{17,21},{18,22},{19,23}} | collective-permute-start | bytes 393224 | tf_op jit(solution)/shard_map/ppermute | solution.py:96
  111.4 18.5 %collective-permute-start.25 = (bf16[4,64,256]{2,1,0:T(8,128)(2,1)S(1)}, bf16[4,64,256]{2,1,0:T(8,128)(2,1)S(1)}, u32[]{:S(2)}, u32[]{:S(2)}) collective-permute-start(bf16[4,64,256]{2,1,0:T(8,128)(2,1)S(1)} %get-tuple-element.19), channel_id=1, source_target_pairs={{12,8},{13,9},{14,10},{15,11},{28,24},{29,25},{30,26},{31,27}} | collective-permute-start | bytes 393224 | tf_op jit(solution)/shard_map/ppermute | solution.py:99
  112.1 17.8 %collective-permute-start.23 = (bf16[4,64,256]{2,1,0:T(8,128)(2,1)S(1)}, bf16[4,64,256]{2,1,0:T(8,128)(2,1)S(1)}, u32[]{:S(2)}, u32[]{:S(2)}) collective-permute-start(bf16[4,64,256]{2,1,0:T(8,128)(2,1)S(1)} %fusion.23), channel_id=1, source_target_pairs={{0,4},{4,8},{1,5},{5,9},{2,6},{6,10},{3,7},{7,11},{16,20},{20,24},... | collective-permute-start | bytes 393224 | tf_op jit(solution)/shard_map/ppermute | solution.py:96
  121.1 10.2 %copy-start.6 = (bf16[12,64,256]{2,1,0:T(8,128)(2,1)S(1)}, bf16[12,64,256]{2,1,0:T(8,128)(2,1)}, u32[]{:S(2)}) copy-start(bf16[12,64,256]{2,1,0:T(8,128)(2,1)} %slice.40) | copy-start | bytes 1179652
  121.1 18.3 %collective-permute-start.20 = (bf16[4,64,2048]{2,1,0:T(8,128)(2,1)}, bf16[4,64,2048]{2,1,0:T(8,128)(2,1)S(1)}, u32[]{:S(2)}, u32[]{:S(2)}) collective-permute-start(bf16[4,64,2048]{2,1,0:T(8,128)(2,1)} %get-tuple-element.13), channel_id=1, source_target_pairs={{8,4},{12,8},{9,5},{13,9},{10,6},{14,10},{11,7},{15,11},{24,20},{2... | collective-permute-start | bytes 3145736 | tf_op jit(solution)/shard_map/ppermute | solution.py:99
  128.4 29.8 %collective-permute-start.2 = (bf16[1664,256]{0,1:T(8,128)(2,1)}, bf16[1664,256]{0,1:T(8,128)(2,1)}, u32[]{:S(2)}, u32[]{:S(2)}) collective-permute-start(bf16[1664,256]{0,1:T(8,128)(2,1)} %add_convert_fusion), channel_id=1, source_target_pairs={{0,2},{1,3},{2,0},{3,1},{4,6},{5,7},{6,4},{7,5},{8,10},{9,11},{10,... | collective-permute-start | bytes 2555912 | tf_op jit(solution)/shard_map/ppermute | solution.py:121
  130.6 7.4 %collective-permute-start.26 = (bf16[4,64,256]{2,1,0:T(8,128)(2,1)}, bf16[4,64,256]{2,1,0:T(8,128)(2,1)S(1)}, u32[]{:S(2)}, u32[]{:S(2)}) collective-permute-start(bf16[4,64,256]{2,1,0:T(8,128)(2,1)} %get-tuple-element.17), channel_id=1, source_target_pairs={{8,4},{12,8},{9,5},{13,9},{10,6},{14,10},{11,7},{15,11},{24,20},{2... | collective-permute-start | bytes 393224 | tf_op jit(solution)/shard_map/ppermute | solution.py:99
  134.7 23.4 %copy-start.5 = (f32[1664,256]{0,1:T(8,128)S(1)}, f32[1664,256]{0,1:T(8,128)}, u32[]{:S(2)}) copy-start(f32[1664,256]{0,1:T(8,128)} %fusion.3) | copy-start | bytes 5111812
  134.8 29.8 %collective-permute-start.24 = (bf16[4,64,256]{2,1,0:T(8,128)(2,1)S(1)}, bf16[4,64,256]{2,1,0:T(8,128)(2,1)S(1)}, u32[]{:S(2)}, u32[]{:S(2)}) collective-permute-start(bf16[4,64,256]{2,1,0:T(8,128)(2,1)S(1)} %copy-done.9), channel_id=1, source_target_pairs={{0,4},{4,8},{8,12},{1,5},{5,9},{9,13},{2,6},{6,10},{10,14},{3,7},{... | collective-permute-start | bytes 393224 | tf_op jit(solution)/shard_map/ppermute | solution.py:96
  138.1 26.5 %collective-permute-start.27 = (bf16[4,64,256]{2,1,0:T(8,128)(2,1)S(1)}, bf16[4,64,256]{2,1,0:T(8,128)(2,1)S(1)}, u32[]{:S(2)}, u32[]{:S(2)}) collective-permute-start(bf16[4,64,256]{2,1,0:T(8,128)(2,1)S(1)} %fusion.22), channel_id=1, source_target_pairs={{4,0},{8,4},{12,8},{5,1},{9,5},{13,9},{6,2},{10,6},{14,10},{7,3},{... | collective-permute-start | bytes 393224 | tf_op jit(solution)/shard_map/ppermute | solution.py:99
  140.4 48.5 %collective-permute-start.18 = (bf16[4,64,2048]{2,1,0:T(8,128)(2,1)}, bf16[4,64,2048]{2,1,0:T(8,128)(2,1)S(1)}, u32[]{:S(2)}, u32[]{:S(2)}) collective-permute-start(bf16[4,64,2048]{2,1,0:T(8,128)(2,1)} %get-tuple-element.12), channel_id=1, source_target_pairs={{0,4},{4,8},{8,12},{1,5},{5,9},{9,13},{2,6},{6,10},{10,14},{3,7},{... | collective-permute-start | bytes 3145736 | tf_op jit(solution)/shard_map/ppermute | solution.py:96
  156.9 32.0 %collective-permute-start.21 = (bf16[4,64,2048]{2,1,0:T(8,128)(2,1)}, bf16[4,64,2048]{2,1,0:T(8,128)(2,1)}, u32[]{:S(2)}, u32[]{:S(2)}) collective-permute-start(bf16[4,64,2048]{2,1,0:T(8,128)(2,1)} %fusion.7), channel_id=1, source_target_pairs={{4,0},{8,4},{12,8},{5,1},{9,5},{13,9},{6,2},{10,6},{14,10},{7,3},{... | collective-permute-start | bytes 3145736 | tf_op jit(solution)/shard_map/ppermute | solution.py:99
  160.1 23.5 %collective-permute-start.11 = (bf16[128,256]{0,1:T(8,128)(2,1)S(1)}, bf16[128,256]{0,1:T(8,128)(2,1)S(1)}, u32[]{:S(2)}, u32[]{:S(2)}) collective-permute-start(bf16[128,256]{0,1:T(8,128)(2,1)S(1)} %slice.47), channel_id=1, source_target_pairs={{0,12},{4,0},{8,4},{12,8},{1,13},{5,1},{9,5},{13,9},{2,14},{6,2},{... | collective-permute-start | bytes 196616 | tf_op jit(solution)/shard_map/ppermute | solution.py:66
  164.6 22.9 %collective-permute-start.12 = (bf16[128,256]{0,1:T(8,128)(2,1)S(1)}, bf16[128,256]{0,1:T(8,128)(2,1)S(1)}, u32[]{:S(2)}, u32[]{:S(2)}) collective-permute-start(bf16[128,256]{0,1:T(8,128)(2,1)S(1)} %slice.47), channel_id=1, source_target_pairs={{0,8},{4,12},{8,0},{12,4},{1,9},{5,13},{9,1},{13,5},{2,10},{6,14},... | collective-permute-start | bytes 196616 | tf_op jit(solution)/shard_map/ppermute | solution.py:66
  164.6 22.9 %collective-permute-start.13 = (bf16[128,256]{0,1:T(8,128)(2,1)S(1)}, bf16[128,256]{0,1:T(8,128)(2,1)S(1)}, u32[]{:S(2)}, u32[]{:S(2)}) collective-permute-start(bf16[128,256]{0,1:T(8,128)(2,1)S(1)} %slice.47), channel_id=1, source_target_pairs={{0,4},{4,8},{8,12},{12,0},{1,5},{5,9},{9,13},{13,1},{2,6},{6,10},{... | collective-permute-start | bytes 196616 | tf_op jit(solution)/shard_map/ppermute | solution.py:66
  (12 other events, 52.2 us)

commit v2 on v1

v2 whole, which is shorter than its diff:
```python
import functools

import jax
import jax.numpy as jnp
from jax import lax
from jax.experimental import pallas as pl
from jax.experimental.pallas import tpu as pltpu
from jax.sharding import PartitionSpec as P

BLOCK = 128
SW = 1
OWN = 4


ADAPTER_SCALE = 0.5

ANYWHERE = pl.BlockSpec(memory_space=pl.ANY)
ROW_PRODUCT = (((1,), (1,)), ((), ()))


def call(kernel, scalars, grid, inputs, outputs, tokens=(), work=0, aliases=None):
    def run(*refs):
        cut = len(scalars) + len(inputs)
        return kernel(*refs[:cut], *refs[cut + len(tokens) :])

    moved = sum(array.size * array.dtype.itemsize for array, _ in inputs)
    moved += sum(2 * functools.reduce(lambda a, b: a * b, shape) for shape, _, _ in outputs)
    return pl.pallas_call(
        run,
        grid_spec=pltpu.PrefetchScalarGridSpec(
            num_scalar_prefetch=len(scalars),
            grid=grid,
            in_specs=[spec for _, spec in inputs] + [ANYWHERE] * len(tokens),
            out_specs=[spec for _, _, spec in outputs],
        ),
        out_shape=[jax.ShapeDtypeStruct(shape, kind) for shape, kind, _ in outputs],
        input_output_aliases=aliases or {},
        cost_estimate=pl.CostEstimate(flops=work, bytes_accessed=moved, transcendentals=0),
    )(*scalars, *[array for array, _ in inputs], *tokens)


def whole(array):
    return (array, pl.BlockSpec(array.shape, lambda *_: (0,) * array.ndim))


def nothing(*refs):
    pass


def after(array, *tokens):
    return call(nothing, (), (1,), [(array, ANYWHERE)], [(array.shape, array.dtype, ANYWHERE)], tokens, aliases={0: 0})[0]


def masked_rank(adapter, rows, length):
    ranks = lax.dot_general(adapter, rows, ROW_PRODUCT, preferred_element_type=jnp.float32)
    live = lax.broadcasted_iota(jnp.int32, ranks.shape, 1) < length
    return jnp.where(live, ranks, 0.0).astype(rows.dtype)


def rank_terms(lengths, maps, features, blocks, each, tokens=()):
    rank, width = maps.shape[1:]

    def kernel(lengths_ref, maps_ref, rows_ref, out_ref):
        for k in range(each):
            out_ref[k] = masked_rank(
                maps_ref[k], rows_ref[k * BLOCK : (k + 1) * BLOCK], lengths_ref[pl.program_id(0) * each + k]
            )

    return call(
        kernel,
        (lengths,),
        (blocks // each,),
        [
            (maps, pl.BlockSpec((each, rank, width), lambda i, *_: (i, 0, 0))),
            (features, pl.BlockSpec((each * BLOCK, width), lambda i, *_: (i, 0))),
        ],
        [((blocks, rank, BLOCK), features.dtype, pl.BlockSpec((each, rank, BLOCK), lambda i, *_: (i, 0, 0)))],
        tokens,
        work=2 * blocks * rank * BLOCK * width,
    )[0]


def last_rank(lengths, pick, choices, features, tokens=()):
    shape = choices[0].shape
    block = features.shape[0] // BLOCK - 1

    def kernel(lengths_ref, pick_ref, *refs):
        rows_ref, out_ref, chosen_ref = refs[-3:]
        for k, choice in enumerate(refs[:-3]):

            @pl.when(pick_ref[0] == k)
            def _():
                chosen_ref[...] = choice[...]

        out_ref[0] = masked_rank(chosen_ref[0], rows_ref[...], lengths_ref[block])

    return call(
        kernel,
        (lengths, pick),
        (1,),
        [whole(choice) for choice in choices]
        + [(features, pl.BlockSpec((BLOCK, shape[2]), lambda i, *_: (block, 0)))],
        [
            ((1, shape[1], BLOCK), features.dtype, pl.BlockSpec((1, shape[1], BLOCK), lambda i, *_: (0, 0, 0))),
            (shape, features.dtype, pl.BlockSpec(shape, lambda i, *_: (0, 0, 0))),
        ],
        tokens,
        work=2 * shape[1] * BLOCK * shape[2],
    )


def table_row(labels, row, ranks, last_ranks, rows_of, last_rows):
    block_of, has_block, has_last = labels
    at = block_of[row]
    mine = ranks[0][at].astype(jnp.float32) + ranks[1][at].astype(jnp.float32)
    mine = jnp.where(has_block[row] > 0, mine, 0.0).astype(last_rows.dtype)
    total = jnp.dot(mine, rows_of(at), preferred_element_type=jnp.float32)

    def with_last():
        late = (last_ranks[0][0].astype(jnp.float32) + last_ranks[1][0].astype(jnp.float32)).astype(last_rows.dtype)
        return total + jnp.dot(late, last_rows[...], preferred_element_type=jnp.float32)

    return has_last[row] > 0, total, with_last


def down_rows(labels, first_row, rows, ranks, last_ranks, features, tokens=()):
    _, rank, _ = ranks[0].shape
    width = features.shape[1]
    block = features.shape[0] // BLOCK - 1

    def kernel(block_of, has_block, has_last, first, a, b, c, d, rows_ref, last_ref, out_ref):
        more, total, with_last = table_row(
            (block_of, has_block, has_last),
            first[0] + pl.program_id(0),
            (a, b),
            (c, d),
            lambda _: rows_ref[...],
            last_ref,
        )

        @pl.when(jnp.logical_not(more))
        def _():
            out_ref[0] = (ADAPTER_SCALE * total).astype(out_ref.dtype)

        @pl.when(more)
        def _():
            out_ref[0] = (ADAPTER_SCALE * with_last()).astype(out_ref.dtype)

    return call(
        kernel,
        (*labels, first_row),
        (rows,),
        [whole(array) for array in (*ranks, *last_ranks)]
        + [
            (features, pl.BlockSpec((BLOCK, width), lambda r, at, x, y, first: (at[first[0] + r], 0))),
            (features, pl.BlockSpec((BLOCK, width), lambda r, *_: (block, 0))),
        ],
        [((rows, rank, width), features.dtype, pl.BlockSpec((1, rank, width), lambda r, *_: (r, 0, 0)))],
        tokens,
        work=2 * rows * rank * BLOCK * width,
    )[0]


def up_rows(labels, row_of, parts, ranks, last_ranks, features, tokens=()):
    _, rank, _ = ranks[0].shape
    width = features.shape[1]
    block = features.shape[0] // BLOCK - 1

    def kernel(block_of, has_block, has_last, row_ref, a, b, c, d, rows_ref, *outs):
        done = 0
        for out_ref in outs:

            def one(r, carry, out_ref=out_ref, done=done):
                more, total, with_last = table_row(
                    (block_of, has_block, has_last),
                    row_ref[done + r],
                    (a, b),
                    (c, d),
                    lambda at: rows_ref[pl.ds(pl.multiple_of(at * BLOCK, BLOCK), BLOCK), :],
                    rows_ref.at[pl.ds(block * BLOCK, BLOCK), :],
                )
                out_ref[r] = (ADAPTER_SCALE * total).astype(out_ref.dtype)

                @pl.when(more)
                def _():
                    out_ref[r] = (ADAPTER_SCALE * with_last()).astype(out_ref.dtype)

                return carry

            lax.fori_loop(0, out_ref.shape[0], one, 0)
            done += out_ref.shape[0]

    return call(
        kernel,
        (*labels, row_of),
        (1,),
        [whole(array) for array in (*ranks, *last_ranks, features)],
        [
            ((rows, rank, width), features.dtype, pl.BlockSpec((rows, rank, width), lambda i, *_: (0, 0, 0)))
            for rows in parts
        ],
        tokens,
        work=2 * sum(parts) * rank * BLOCK * width,
    )


def base_terms(columns, hidden, weight, width, tokens=()):
    rows, depth = hidden.shape
    tile = rows // 4

    def kernel(columns_ref, rows_ref, one_ref, two_ref, one_out, two_out):
        one_out[...] = jnp.dot(rows_ref[...], one_ref[...], preferred_element_type=jnp.float32).astype(one_out.dtype)
        two_out[...] = jnp.dot(rows_ref[...], two_ref[...], preferred_element_type=jnp.float32).astype(two_out.dtype)

    return call(
        kernel,
        (columns,),
        (rows // tile,),
        [
            (hidden, pl.BlockSpec((tile, depth), lambda i, *_: (i, 0))),
            (weight, pl.BlockSpec((depth, width), lambda i, at: (0, at[0]))),
            (weight, pl.BlockSpec((depth, width), lambda i, at: (0, at[1]))),
        ],
        [((rows, width), hidden.dtype, pl.BlockSpec((tile, width), lambda i, *_: (i, 0)))] * 2,
        tokens,
        work=4 * rows * depth * width,
    )


def values_of(lengths, base, ranks, last_ranks, maps, last_map, tokens=()):
    rows, width = base[0].shape
    blocks = rows // BLOCK

    def kernel(lengths_ref, one, two, three, a, b, c, d, maps_ref, last_ref, out_ref, last_out):
        for k in range(blocks):
            at = slice(k * BLOCK, (k + 1) * BLOCK)
            pair = (a[k], b[k]) if k < blocks - 1 else (c[0], d[0])
            adapter = maps_ref[k] if k < blocks - 1 else last_ref[0]
            ranks_k = (pair[0].astype(jnp.float32) + pair[1].astype(jnp.float32)).astype(adapter.dtype)
            added = lax.dot_general(
                ranks_k, adapter, (((0,), (0,)), ((), ())), preferred_element_type=jnp.float32
            )
            frozen = one[at].astype(jnp.float32) + two[at].astype(jnp.float32) + three[at].astype(jnp.float32)
            live = lax.broadcasted_iota(jnp.int32, frozen.shape, 0) < lengths_ref[k]
            values = jnp.where(live, frozen + ADAPTER_SCALE * added, 0.0).astype(out_ref.dtype)
            out_ref[at] = values
            if k == blocks - 1:
                last_out[...] = values

    return call(
        kernel,
        (lengths,),
        (1,),
        [whole(array) for array in (*base, *ranks, *last_ranks, maps, last_map)],
        [
            ((rows, width), maps.dtype, pl.BlockSpec((rows, width), lambda i, *_: (0, 0))),
            ((BLOCK, width), maps.dtype, pl.BlockSpec((BLOCK, width), lambda i, *_: (0, 0))),
        ],
        tokens,
        work=2 * rows * maps.shape[1] * width,
    )


def put_last(pick, values, choices):
    width = values.shape[1]
    block = values.shape[0] // BLOCK - 1

    def kernel(pick_ref, *refs):
        for k, choice in enumerate(refs[:-2]):

            @pl.when(pick_ref[0] == k)
            def _():
                refs[-1][...] = choice[...]

    return call(
        kernel,
        (pick,),
        (1,),
        [whole(choice) for choice in choices] + [(values, ANYWHERE)],
        [(values.shape, values.dtype, pl.BlockSpec((BLOCK, width), lambda i, *_: (block, 0)))],
        aliases={1 + len(choices): 0},
    )[0]


def shifted(array, source):
    size = lax.axis_size("dp")
    me = lax.axis_index("dp")
    if size > 4:
        taken = lax.dynamic_index_in_dim(lax.all_gather(array, "dp"), source, 0, keepdims=False)
        return [taken], jnp.zeros((1,), jnp.int32)
    choices = [array] + [
        lax.ppermute(array, "dp", [(i, (i + shift) % size) for i in range(size)]) for shift in range(1, size)
    ]
    return choices, ((me - source) % size).reshape(1)


def routed(array, holders):
    if lax.axis_size("dp") != 4:
        return shifted(array, holders[lax.axis_index("dp")])
    me = lax.axis_index("dp")
    source = holders[me]
    from_left = lax.ppermute(array, "dp", [(0, 1), (1, 2)])
    from_right = lax.ppermute(array, "dp", [(3, 2), (2, 1)])
    passed = lax.ppermute(jnp.where(me == 1, from_left, from_right), "dp", [(1, 2), (2, 1)])
    wanted = jnp.where(me == 1, holders[0], holders[3])
    onward = jnp.where(wanted == me - 1, from_left, jnp.where(wanted == me + 1, from_right, passed))
    onward = jnp.where(wanted == me, array, onward)
    outward = lax.ppermute(onward, "dp", [(2, 3), (1, 0)])
    inner = (me == 1) | (me == 2)
    pick = jnp.where(
        source == me,
        0,
        jnp.where(inner, jnp.where(source == me - 1, 1, jnp.where(source == me + 1, 2, 3)), 4),
    )
    return [array, from_left, from_right, passed, outward], pick.reshape(1).astype(jnp.int32)


def add(*arrays):
    return sum(array.astype(jnp.float32) for array in arrays).astype(arrays[0].dtype)


def near_sum(array):
    size = lax.axis_size("tensor")
    return add(array, lax.ppermute(array, "tensor", [(i, i ^ 1) for i in range(size)]))


def far(array):
    size = lax.axis_size("tensor")
    return lax.ppermute(array, "tensor", [(i, i ^ 2) for i in range(size)])


def exchanged(array):
    array = near_sum(array)
    return array, far(array)


def line_reduce_scatter(table):
    size = lax.axis_size("dp")
    me = lax.axis_index("dp")

    def entry(index):
        return lax.dynamic_index_in_dim(table, jnp.clip(index, 0, size - 1), 0, keepdims=False)

    from_left = from_right = None
    for step in range(size - 1):
        right = entry(size - 1 - step + me)
        left = entry(step - (size - 1 - me))
        if step > 0:
            right = add(right, from_left)
            left = add(left, from_right)
        from_left = lax.ppermute(right, "dp", [(i, i + 1) for i in range(step + 1)])
        from_right = lax.ppermute(left, "dp", [(i, i - 1) for i in range(size - 1 - step, size)])
    return entry(me) if size == 1 else add(entry(me), from_left, from_right)


TO_INNER = [(0, 1), (3, 2)]
ACROSS = [(1, 2), (2, 1)]
TO_OUTER = [(2, 3), (1, 0)]


def body(
    partner,
    block_tenant_index,
    block_live_length,
    tenant_table_row,
    hidden,
    cotangent,
    frozen_value_weight,
    adapter_down_rows,
    adapter_up_matrix,
):
    blocks = block_tenant_index.shape[0]
    output_width = cotangent.shape[1]
    kept = blocks - SW
    devices = lax.axis_size("dp")
    me = lax.axis_index("dp")
    column = lax.axis_index("tensor")
    lengths = block_live_length
    order = jnp.arange(devices, dtype=jnp.int32)
    holders = jnp.sum(jnp.where(partner[None, :] == order[:, None], order[None, :], 0), axis=1)

    up_choices, up_pick = shifted(adapter_up_matrix[kept:], holders[me])
    cot_terms = rank_terms(lengths, adapter_up_matrix, cotangent, kept, 4)
    rank_cot = exchanged(cot_terms)
    last_terms, up_last = last_rank(lengths, up_pick, up_choices, cotangent, [cot_terms])
    last_cot = exchanged(last_terms)

    table_rows = jnp.sum(
        jnp.where(
            block_tenant_index[:, None] == jnp.arange(tenant_table_row.shape[0], dtype=jnp.int32)[None, :],
            tenant_table_row[None, :],
            0,
        ),
        axis=1,
    )
    rows = devices * OWN
    matches = jnp.arange(rows, dtype=jnp.int32)[:, None] == table_rows[None, :]
    block_of = jnp.sum(jnp.where(matches[:, :kept], jnp.arange(kept, dtype=jnp.int32)[None, :], 0), axis=1)
    has_block = jnp.any(matches[:, :kept], axis=1).astype(jnp.int32)
    has_last = matches[:, kept].astype(jnp.int32)
    labels = (block_of, has_block, has_last)

    owners = jnp.where(me < devices // 2, order[::-1], order)
    line = devices == 4

    def down_part(owner, count=OWN, tokens=()):
        return down_rows(
            labels, (owner * OWN).reshape(1).astype(jnp.int32), count, rank_cot, last_cot, hidden, tokens
        )

    if line:
        part0 = down_part(owners[0])
        token = part0
    else:
        token = down_part(jnp.zeros((), jnp.int32), rows)
        down_out = line_reduce_scatter(token.reshape(devices, OWN, *token.shape[1:]))

    def copy_kernel(in_ref, out_ref):
        out_ref[...] = in_ref[...]

    down_own = call(
        copy_kernel,
        (),
        (1,),
        [(adapter_down_rows, pl.BlockSpec((SW, *adapter_down_rows.shape[1:]), lambda i: (kept, 0, 0)))],
        [
            (
                (SW, *adapter_down_rows.shape[1:]),
                hidden.dtype,
                pl.BlockSpec((SW, *adapter_down_rows.shape[1:]), lambda i: (0, 0, 0)),
            )
        ],
        [cot_terms],
    )[0]
    down_choices, down_pick = routed(down_own, holders)
    in_terms = rank_terms(lengths, adapter_down_rows, hidden, kept, 2, [token])
    rank_in = exchanged(in_terms)
    last_in = exchanged(last_rank(lengths, down_pick, down_choices, hidden, [in_terms])[0])

    if line:
        from0 = lax.ppermute(part0, "dp", TO_INNER)
        part1 = down_part(owners[1], tokens=[part0])
        part2 = down_part(owners[2], tokens=[part1])
        part3 = down_part(owners[3], tokens=[part2])
        part_own = down_part(me, tokens=[part3])
        part1 = after(part1, from0)
        from1 = lax.ppermute(part1, "dp", TO_INNER)
        across0 = lax.ppermute(add(part0, from0), "dp", ACROSS)
        from2 = lax.ppermute(after(part2, from1), "dp", TO_INNER)
        across1 = lax.ppermute(add(part1, from1), "dp", ACROSS)
        outer = lax.ppermute(add(part3, across0), "dp", TO_OUTER)
        down_out = add(part_own, from2, across1, outer)

        row_of = (owners[:, None] * OWN + jnp.arange(OWN, dtype=jnp.int32)[None, :]).reshape(-1)
        up_sent, up_kept = up_rows(labels, row_of, (3 * OWN, OWN), rank_in, last_in, cotangent)
        up_in = lax.ppermute(up_sent, "dp", TO_INNER)
        up_across = lax.ppermute(add(up_sent[: 2 * OWN], up_in[: 2 * OWN]), "dp", ACROSS)
        up_outer = lax.ppermute(add(up_kept, up_across[:OWN]), "dp", TO_OUTER)
        inner = (me == 1) | (me == 2)
        up_out = jnp.where(
            inner,
            add(up_sent[2 * OWN :], up_in[2 * OWN :], up_across[OWN:]),
            add(up_kept, up_outer),
        )
    else:
        (up_table,) = up_rows(labels, jnp.arange(rows, dtype=jnp.int32), (rows,), rank_in, last_in, cotangent)
        up_out = line_reduce_scatter(up_table.reshape(devices, OWN, *up_table.shape[1:]))

    pair = jnp.stack([column ^ 3, column ^ 2]).astype(jnp.int32)
    given, away = base_terms(pair, hidden, frozen_value_weight, output_width, [in_terms])
    size = lax.axis_size("tensor")
    near = [(i, i ^ 1) for i in range(size)]
    across = far(add(away, lax.ppermute(given, "tensor", near)))
    pair = jnp.stack([column ^ 1, column]).astype(jnp.int32)
    given, mine = base_terms(pair, hidden, frozen_value_weight, output_width, [away])
    base = (mine, lax.ppermute(given, "tensor", near), across)
    values, last_values = values_of(lengths, base, rank_in, last_in, adapter_up_matrix, up_last)
    value_choices, value_pick = shifted(last_values, partner[me])
    projected_values = put_last(value_pick, values, value_choices)
    return (projected_values, down_out, up_out)


def solution(mesh):
    in_specs = (
        P("groups"),
        P(("groups", "dp")),
        P(("groups", "dp")),
        P("groups"),
        P(("groups", "dp"), "tensor"),
        P(("groups", "dp"), "tensor"),
        P("tensor", None),
        P(("groups", "dp"), None, "tensor"),
        P(("groups", "dp"), None, "tensor"),
    )
    out_specs = (
        P(("groups", "dp"), "tensor"),
        P(("groups", "dp"), None, "tensor"),
        P(("groups", "dp"), None, "tensor"),
    )
    return jax.shard_map(body, mesh=mesh, in_specs=in_specs, out_specs=out_specs, check_vma=False)
```

time: 193 us -> 187 us (0.969)
  Pallas kernels: 7.99 us -> 71.5 us
  matrix products: 31.4 us -> 0 us
  waiting for transfers between devices: 47.4 us -> 30 us
  starting transfers between devices: 61.5 us -> 49.5 us
  local copies, waits for them, and re-layouts: 17.3 us -> 7.93 us
  between operations: 5.02 us -> 8.16 us
  other arithmetic: 21.3 us -> 18.2 us
    pallas_call x2 -> x17, Pallas kernels: 7.99 us -> 71.5 us  [call(): pl.pallas_call(run, grid_spec=pltpu.PrefetchScalarGridSpec(num_scalar_pre...]
    dot_general x8 -> x0, matrix products: 31.4 us -> none  [the longest x4 23.8 us: term(): jnp.dot(hidden, part, preferred_element_type=jnp.float32)]
    ppermute x28 -> x30, waiting for transfers between devices: 47.4 us -> 30 us  [the longest x1 16.7 us: body(): from1 = lax.ppermute(part1, 'dp', TO_INNER)]
    ppermute x28 -> x30, starting transfers between devices: 61.5 us -> 49.5 us  [the longest x6 10.3 us: shifted(): lax.ppermute(array, 'dp', [(i, (i + shift) % size) for i in range(size)])]
    convert_element_type x14 -> x11, other arithmetic: 19.5 us -> 13.1 us  [add(): sum((array.astype(jnp.float32) for array in arrays)).astype(arrays[0].dtype)]
    slice x7 -> x3, local copies, waits for them, and re-layouts: 6.08 us -> 2.04 us  [the longest x1 0.76 us: body(): up_choices, up_pick = shifted(adapter_up_matrix[kept:], holders[me])]
    unnamed x31 -> x70, local copies, waits for them, and re-layouts: 7.28 us -> 4.55 us
  transfers between devices with their start and end apart: 28 -> 30, of which waited for: 7 -> 4; matrix products, arithmetic and copies ran while one was open for 29% -> 10% of each run, Pallas kernels for 4% -> 39%
where the time goes in v2:
time: 187 us; the launch traced here: 185 us
  Pallas kernels  71.5 us (38%)
  starting transfers between devices  49.5 us (26%)
  waiting for transfers between devices  30 us (16%)
  other arithmetic  18.2 us (10%)
  between operations  8.16 us (4%)
  local copies, waits for them, and re-layouts  7.93 us (4%)
    pallas_call x17, Pallas kernels, call(): pl.pallas_call(run, grid_spec=pltpu.PrefetchScalarGridSpec(num_scalar_pre...  71.5 us
    ppermute x1, waiting for transfers between devices, body(): from1 = lax.ppermute(part1, 'dp', TO_INNER)  16.7 us
    convert_element_type x11, other arithmetic, add(): sum((array.astype(jnp.float32) for array in arrays)).astype(arrays[0].dtype)  13.1 us
    ppermute x6, waiting for transfers between devices, shifted(): lax.ppermute(array, 'dp', [(i, (i + shift) % size) for i in range(size)])  12.9 us
    ppermute x6, starting transfers between devices, shifted(): lax.ppermute(array, 'dp', [(i, (i + shift) % size) for i in range(size)])  10.3 us
    ppermute x1, starting transfers between devices, body(): from0 = lax.ppermute(part0, 'dp', TO_INNER)  8.16 us
    ppermute x1, starting transfers between devices, body(): from2 = lax.ppermute(after(part2, from1), 'dp', TO_INNER)  6.41 us
    ppermute x5, starting transfers between devices, far(): return lax.ppermute(array, 'tensor', [(i, i ^ 2) for i in range(size)])  4.84 us
  transfers between devices with their start and end apart: 30, of which 4 were waited for; matrix products, arithmetic and copies ran while one was open for 10% of the time, Pallas kernels for 39%

profile of v2, /device:TPU:0, one launch (start us, length us, event | category | flops | bytes accessed | tf_op | source)
XLA Modules:
  0.0 185.3 jit_solution(1501833839468137497)
XLA Ops:
  1.4 3.0 %collective-permute-start.2 = (bf16[1,64,256]{2,1,0:T(8,128)(2,1)S(1)}, bf16[1,64,256]{2,1,0:T(8,128)(2,1)S(1)}, u32[]{:S(2)}, u32[]{:S(2)}) collective-permute-start(bf16[1,64,256]{2,1,0:T(8,128)(2,1)S(1)} %slice.49.refs_2_), channel_id=1, source_target_pairs={{0,4},{4,8},{8,12},{12,0},{1,5},{5,9},{9,13},{13,1},{2,6},{6,10},{... | collective-permute-start | bytes 98312 | tf_op jit(solution)/shard_map/ppermute | solution.py:292
  4.4 2.6 %collective-permute-start.3 = (bf16[1,64,256]{2,1,0:T(8,128)(2,1)S(1)}, bf16[1,64,256]{2,1,0:T(8,128)(2,1)S(1)}, u32[]{:S(2)}, u32[]{:S(2)}) collective-permute-start(bf16[1,64,256]{2,1,0:T(8,128)(2,1)S(1)} %slice.49.refs_2_), channel_id=1, source_target_pairs={{0,8},{4,12},{8,0},{12,4},{1,9},{5,13},{9,1},{13,5},{2,10},{6,14},... | collective-permute-start | bytes 98312 | tf_op jit(solution)/shard_map/ppermute | solution.py:292
  8.4 3.8 %shard_map.112.refs_7_.refs_1_ = bf16[12,64,128]{2,1,0:T(8,128)(2,1)} custom-call(s32[13]{0:T(128)} %refs_0_.11, bf16[13,64,256]{2,1,0:T(8,128)(2,1)} %refs_8_.8, bf16[1664,256]{1,0:T(8,128)(2,1)} %refs_8_.13), custom_call_target="tpu_custom_call" | custom-call | flops 50331648 | bytes 1474560 | tf_op jit(solution)/shard_map/pallas_call | solution.py:28
  12.3 1.7 shard_map.118.refs_2_
  14.0 2.6 %collective-permute-start.12 = (bf16[1,64,2048]{2,1,0:T(8,128)(2,1)}, bf16[1,64,2048]{2,1,0:T(8,128)(2,1)S(1)}, u32[]{:S(2)}, u32[]{:S(2)}) collective-permute-start(bf16[1,64,2048]{2,1,0:T(8,128)(2,1)} %shard_map.118.refs_2_), channel_id=1, source_target_pairs={{0,4},{4,8},{1,5},{5,9},{2,6},{6,10},{3,7},{7,11},{16,20},{20,24},... | collective-permute-start | bytes 786440 | tf_op jit(solution)/shard_map/ppermute | solution.py:302
  20.8 2.3 %shard_map.113 = (bf16[1,64,128]{2,1,0:T(8,128)(2,1)}, bf16[1,64,256]{2,1,0:T(8,128)(2,1)}) custom-call(s32[13]{0:T(128)} %refs_0_.11, s32[1]{0:T(128)} %bitcast.8.refs_1_, bf16[1,64,256]{2,1,0:T(8,128)(2,1)} %copy-done.24, bf16[1,64,256]{2,1,0:T(8,128)(2,1)} %copy-done.28, bf16[1,64,256]{2,1,0:T(8,128)(2,1)} %copy-done.29, bf16[1,64,256]{2,1,0:T(8,128)(2,1)} %copy-done.30, ...), custom_call_target="tpu_custom_call" | custom-call | flops 4194304 | bytes 1032192 | tf_op jit(solution)/shard_map/pallas_call | solution.py:28
  23.4 1.6 collective-permute-start.1
  35.9 5.0 %shard_map.114.refs_3_.refs_10_ = bf16[4,64,2048]{2,1,0:T(8,128)(2,1)} custom-call(s32[16]{0:T(128)} %select_reduce_fusion.refs_0_, s32[16]{0:T(128)} %convert_element_type.132.refs_1_, s32[16]{0:T(128)} %fusion.3.refs_2_, s32[1]{0:T(128)S(6)} %mul.23.refs_3_, bf16[12,64,128]{2,1,0:T(8,128)(2,1)} %copy-done.3, bf16[12,64,128]{2,1,0:T(8,128)(2,1)} %copy-done.4, ...), custom_call_target="tpu_custom_call" | custom-call | flops 134217728 | bytes 15106048 | tf_op jit(solution)/shard_map/pallas_call | solution.py:28
  42.3 8.2 %collective-permute-start.21 = (bf16[4,64,2048]{2,1,0:T(8,128)(2,1)}, bf16[4,64,2048]{2,1,0:T(8,128)(2,1)S(1)}, u32[]{:S(2)}, u32[]{:S(2)}) collective-permute-start(bf16[4,64,2048]{2,1,0:T(8,128)(2,1)} %shard_map.114.refs_3_.refs_10_), channel_id=1, source_target_pairs={{0,4},{12,8},{1,5},{13,9},{2,6},{14,10},{3,7},{15,11},{16,20},{28,... | collective-permute-start | bytes 3145736 | tf_op jit(solution)/shard_map/ppermute | solution.py:441
  50.5 7.8 %shard_map.115.refs_4_.refs_8_ = bf16[12,64,128]{2,1,0:T(8,128)(2,1)} custom-call(s32[13]{0:T(128)} %refs_0_.11, bf16[13,64,2048]{2,1,0:T(8,128)(2,1)} %refs_0_.9, bf16[1664,2048]{1,0:T(8,128)(2,1)} %refs_9_.9, bf16[4,64,2048]{2,1,0:T(8,128)(2,1)} %shard_map.114.refs_3_.refs_10_), custom_call_target="tpu_custom_call" | custom-call | flops 402653184 | bytes 10420224 | tf_op jit(solution)/shard_map/pallas_call | solution.py:28
  60.3 3.2 %shard_map.119 = (bf16[1,64,128]{2,1,0:T(8,128)(2,1)}, bf16[1,64,2048]{2,1,0:T(8,128)(2,1)}) custom-call(s32[13]{0:T(128)} %refs_0_.11, s32[1]{0:T(128)} %bitcast.9.refs_1_, bf16[1,64,2048]{2,1,0:T(8,128)(2,1)} %shard_map.118.refs_2_, bf16[1,64,2048]{2,1,0:T(8,128)(2,1)} %copy-done.11, bf16[1,64,2048]{2,1,0:T(8,128)(2,1)} %copy-done.12, ...), custom_call_target="tpu_custom_call" | custom-call | flops 33554432 | bytes 8404992 | tf_op jit(solution)/shard_map/pallas_call | solution.py:28
  67.0 8.4 %shard_map.116 = (bf16[1664,256]{1,0:T(8,128)(2,1)}, bf16[1664,256]{1,0:T(8,128)(2,1)}) custom-call(s32[2]{0:T(128)} %pad_add_fusion.1.refs_0_, bf16[1664,2048]{1,0:T(8,128)(2,1)} %refs_9_.9, bf16[2048,1024]{1,0:T(8,128)(2,1)} %refs_3_.3, bf16[2048,1024]{1,0:T(8,128)(2,1)} %refs_3_.3, bf16[12,64,128]{2,1,0:T(8,128)(2,1)} %shard_map.115.refs_4_.refs_8_), custom_call_target="tpu_custom_call" | custom-call | flops 3489660928 | bytes 16908288 | tf_op jit(solution)/shard_map/pallas_call | solution.py:28
  76.7 5.2 %shard_map.128 = (bf16[12,64,256]{2,1,0:T(8,128)(2,1)}, bf16[4,64,256]{2,1,0:T(8,128)(2,1)}) custom-call(s32[16]{0:T(128)} %select_reduce_fusion.refs_0_, s32[16]{0:T(128)} %convert_element_type.132.refs_1_, s32[16]{0:T(128)} %fusion.3.refs_2_, s32[16]{0:T(128)} %add.97.refs_3_, bf16[12,64,128]{2,1,0:T(8,128)(2,1)} %copy-done.14, ...), custom_call_target="tpu_custom_call" | custom-call | flops 67108864 | bytes 1802240 | tf_op jit(solution)/shard_map/pallas_call | solution.py:28
  84.7 1.6 collective-permute-start.25
  86.3 8.5 %shard_map.117 = (bf16[1664,256]{1,0:T(8,128)(2,1)}, bf16[1664,256]{1,0:T(8,128)(2,1)}) custom-call(s32[2]{0:T(128)} %pad_add_fusion.refs_0_, bf16[1664,2048]{1,0:T(8,128)(2,1)} %refs_9_.9, bf16[2048,1024]{1,0:T(8,128)(2,1)} %refs_3_.3, bf16[2048,1024]{1,0:T(8,128)(2,1)} %refs_3_.3, bf16[1664,256]{1,0:T(8,128)(2,1)} %get-tuple-element.15.refs_4_), custom_call_target="tpu_custom_call" | custom-call | flops 3489660928 | bytes 16908288 | tf_op jit(solution)/shard_map/pallas_call | solution.py:28
  95.3 4.5 %shard_map.122.refs_10_.refs_0_ = bf16[4,64,2048]{2,1,0:T(8,128)(2,1)} custom-call(s32[16]{0:T(128)} %select_reduce_fusion.refs_0_, s32[16]{0:T(128)} %convert_element_type.132.refs_1_, s32[16]{0:T(128)} %fusion.3.refs_2_, s32[1]{0:T(128)S(6)} %mul.27.refs_3_, bf16[12,64,128]{2,1,0:T(8,128)(2,1)} %copy-done.3, bf16[12,64,128]{2,1,0:T(8,128)(2,1)} %copy-done.4, ...), custom_call_target="tpu_custom_call" | custom-call | flops 134217728 | bytes 15106048 | tf_op jit(solution)/shard_map/pallas_call | solution.py:28
  99.8 5.0 %shard_map.123.refs_10_.refs_0_ = bf16[4,64,2048]{2,1,0:T(8,128)(2,1)} custom-call(s32[16]{0:T(128)} %select_reduce_fusion.refs_0_, s32[16]{0:T(128)} %convert_element_type.132.refs_1_, s32[16]{0:T(128)} %fusion.3.refs_2_, s32[1]{0:T(128)S(6)} %mul.26.refs_3_, bf16[12,64,128]{2,1,0:T(8,128)(2,1)} %copy-done.3, bf16[12,64,128]{2,1,0:T(8,128)(2,1)} %copy-done.4, ...), custom_call_target="tpu_custom_call" | custom-call | flops 134217728 | bytes 15106048 | tf_op jit(solution)/shard_map/pallas_call | solution.py:28
  104.8 5.2 %shard_map.124.refs_10_ = bf16[4,64,2048]{2,1,0:T(8,128)(2,1)} custom-call(s32[16]{0:T(128)} %select_reduce_fusion.refs_0_, s32[16]{0:T(128)} %convert_element_type.132.refs_1_, s32[16]{0:T(128)} %fusion.3.refs_2_, s32[1]{0:T(128)S(6)} %mul.25.refs_3_, bf16[12,64,128]{2,1,0:T(8,128)(2,1)} %copy-done.3, bf16[12,64,128]{2,1,0:T(8,128)(2,1)} %copy-done.4, ...), custom_call_target="tpu_custom_call" | custom-call | flops 134217728 | bytes 15106048 | tf_op jit(solution)/shard_map/pallas_call | solution.py:28
  112.3 4.4 %collective-permute-start.22 = (bf16[4,64,2048]{2,1,0:T(8,128)(2,1)}, bf16[4,64,2048]{2,1,0:T(8,128)(2,1)S(1)}, u32[]{:S(2)}, u32[]{:S(2)}) collective-permute-start(bf16[4,64,2048]{2,1,0:T(8,128)(2,1)} %shard_map.126), channel_id=1, source_target_pairs={{0,4},{12,8},{1,5},{13,9},{2,6},{14,10},{3,7},{15,11},{16,20},{28,... | collective-permute-start | bytes 3145736 | tf_op jit(solution)/shard_map/ppermute | solution.py:447
  116.7 2.3 %add_convert_fusion.4 = bf16[1664,256]{1,0:T(8,128)(2,1)} fusion(bf16[1664,256]{1,0:T(8,128)(2,1)} %collective-permute-done.8, bf16[1664,256]{1,0:T(8,128)(2,1)S(1)} %copy-done.8), kind=kLoop, calls=%fused_computation.4 | loop fusion | flops 1703936 | bytes 2555904 | tf_op jit(solution)/shard_map/convert_element_type | solution.py:319
  119.9 1.6 add_convert_fusion.1
  122.8 16.7 %collective-permute-done.22.refs_1_ = bf16[4,64,2048]{2,1,0:T(8,128)(2,1)S(1)} collective-permute-done((bf16[4,64,2048]{2,1,0:T(8,128)(2,1)}, bf16[4,64,2048]{2,1,0:T(8,128)(2,1)S(1)}, u32[]{:S(2)}, u32[]{:S(2)}) %collective-permute-start.22) | collective-permute-done | bytes 1048608 | tf_op jit(solution)/shard_map/ppermute | solution.py:447
  140.9 1.8 collective-permute-start.24
  142.7 6.4 %collective-permute-start.23 = (bf16[4,64,2048]{2,1,0:T(8,128)(2,1)}, bf16[4,64,2048]{2,1,0:T(8,128)(2,1)}, u32[]{:S(2)}, u32[]{:S(2)}) collective-permute-start(bf16[4,64,2048]{2,1,0:T(8,128)(2,1)} %shard_map.127), channel_id=1, source_target_pairs={{0,4},{12,8},{1,5},{13,9},{2,6},{14,10},{3,7},{15,11},{16,20},{28,... | collective-permute-start | bytes 3145736 | tf_op jit(solution)/shard_map/ppermute | solution.py:449
  151.4 4.2 %shard_map.120 = (bf16[1664,256]{1,0:T(8,128)(2,1)}, bf16[128,256]{1,0:T(8,128)(2,1)}) custom-call(s32[13]{0:T(128)} %refs_0_.11, bf16[1664,256]{1,0:T(8,128)(2,1)} %get-tuple-element.16.refs_1_, bf16[1664,256]{1,0:T(8,128)(2,1)} %collective-permute-done.7.refs_2_, bf16[1664,256]{1,0:T(8,128)(2,1)} %collective-permute-done.9.refs_3_, ...), custom_call_target="tpu_custom_call" | custom-call | flops 54525952 | bytes 4358144 | tf_op jit(solution)/shard_map/pallas_call | solution.py:28
  155.6 2.6 %collective-permute-start.18 = (bf16[128,256]{1,0:T(8,128)(2,1)}, bf16[128,256]{1,0:T(8,128)(2,1)}, u32[]{:S(2)}, u32[]{:S(2)}) collective-permute-start(bf16[128,256]{1,0:T(8,128)(2,1)} %get-tuple-element.21.refs_1_), channel_id=1, source_target_pairs={{0,4},{4,8},{8,12},{12,0},{1,5},{5,9},{9,13},{13,1},{2,6},{6,10},{... | collective-permute-start | bytes 196616 | tf_op jit(solution)/shard_map/ppermute | solution.py:292
  159.5 5.1 %shard_map.125 = bf16[4,64,2048]{2,1,0:T(8,128)(2,1)} custom-call(s32[16]{0:T(128)} %select_reduce_fusion.refs_0_, s32[16]{0:T(128)} %convert_element_type.132.refs_1_, s32[16]{0:T(128)} %fusion.3.refs_2_, s32[1]{0:T(128)} %bitcast.12.refs_3_, bf16[12,64,128]{2,1,0:T(8,128)(2,1)} %copy-done.3, bf16[12,64,128]{2,1,0:T(8,128)(2,1)} %copy-done.4, ...), custom_call_target="tpu_custom_call" | custom-call | flops 134217728 | bytes 15106048 | tf_op jit(solution)/shard_map/pallas_call | solution.py:28
  165.2 10.2 %collective-permute-done.18.refs_2_ = bf16[128,256]{1,0:T(8,128)(2,1)} collective-permute-done((bf16[128,256]{1,0:T(8,128)(2,1)}, bf16[128,256]{1,0:T(8,128)(2,1)}, u32[]{:S(2)}, u32[]{:S(2)}) %collective-permute-start.18) | collective-permute-done | bytes 65568 | tf_op jit(solution)/shard_map/ppermute | solution.py:292
  175.4 1.8 fusion.2
  177.2 2.7 %collective-permute-done.20.refs_4_ = bf16[128,256]{1,0:T(8,128)(2,1)S(1)} collective-permute-done((bf16[128,256]{1,0:T(8,128)(2,1)}, bf16[128,256]{1,0:T(8,128)(2,1)S(1)}, u32[]{:S(2)}, u32[]{:S(2)}) %collective-permute-start.20) | collective-permute-done | bytes 65568 | tf_op jit(solution)/shard_map/ppermute | solution.py:292
  180.5 1.6 shard_map.121
  182.1 3.2 %add_convert_fusion = bf16[4,64,2048]{2,1,0:T(8,128)(2,1)} fusion(bf16[4,64,2048]{2,1,0:T(8,128)(2,1)S(1)} %collective-permute-done.26, bf16[4,64,2048]{2,1,0:T(8,128)(2,1)} %collective-permute-done.24, bf16[4,64,2048]{2,1,0:T(8,128)(2,1)} %collective-permute-done.23, bf16[4,64,2048]{2,1,0:T(8,128)(2,1)S(1)} %copy-done.6), kind=kLoop, calls=%fused_computation | loop fusion | flops 4194304 | bytes 5242880 | tf_op jit(solution)/shard_map/convert_element_type | solution.py:319
  (147 shorter events, 32.4 us)
Async XLA Ops:
  1.4 16.8 %collective-permute-start.2 = (bf16[1,64,256]{2,1,0:T(8,128)(2,1)S(1)}, bf16[1,64,256]{2,1,0:T(8,128)(2,1)S(1)}, u32[]{:S(2)}, u32[]{:S(2)}) collective-permute-start(bf16[1,64,256]{2,1,0:T(8,128)(2,1)S(1)} %slice.49.refs_2_), channel_id=1, source_target_pairs={{0,4},{4,8},{8,12},{12,0},{1,5},{5,9},{9,13},{13,1},{2,6},{6,10},{... | collective-permute-start | bytes 98312 | tf_op jit(solution)/shard_map/ppermute | solution.py:292
  4.4 15.8 %collective-permute-start.3 = (bf16[1,64,256]{2,1,0:T(8,128)(2,1)S(1)}, bf16[1,64,256]{2,1,0:T(8,128)(2,1)S(1)}, u32[]{:S(2)}, u32[]{:S(2)}) collective-permute-start(bf16[1,64,256]{2,1,0:T(8,128)(2,1)S(1)} %slice.49.refs_2_), channel_id=1, source_target_pairs={{0,8},{4,12},{8,0},{12,4},{1,9},{5,13},{9,1},{13,5},{2,10},{6,14},... | collective-permute-start | bytes 98312 | tf_op jit(solution)/shard_map/ppermute | solution.py:292
  7.0 13.2 %collective-permute-start.4 = (bf16[1,64,256]{2,1,0:T(8,128)(2,1)S(1)}, bf16[1,64,256]{2,1,0:T(8,128)(2,1)S(1)}, u32[]{:S(2)}, u32[]{:S(2)}) collective-permute-start(bf16[1,64,256]{2,1,0:T(8,128)(2,1)S(1)} %slice.49.refs_2_), channel_id=1, source_target_pairs={{0,12},{4,0},{8,4},{12,8},{1,13},{5,1},{9,5},{13,9},{2,14},{6,2},{... | collective-permute-start | bytes 98312 | tf_op jit(solution)/shard_map/ppermute | solution.py:292
  12.2 11.2 %collective-permute-start = (bf16[12,64,128]{2,1,0:T(8,128)(2,1)}, bf16[12,64,128]{2,1,0:T(8,128)(2,1)S(1)}, u32[]{:S(2)}, u32[]{:S(2)}) collective-permute-start(bf16[12,64,128]{2,1,0:T(8,128)(2,1)} %shard_map.112.refs_7_.refs_1_), channel_id=1, source_target_pairs={{0,1},{1,0},{2,3},{3,2},{4,5},{5,4},{6,7},{7,6},{8,9},{9,8},{10,11... | collective-permute-start | bytes 589832 | tf_op jit(solution)/shard_map/ppermute | solution.py:324
  14.0 11.0 %collective-permute-start.12 = (bf16[1,64,2048]{2,1,0:T(8,128)(2,1)}, bf16[1,64,2048]{2,1,0:T(8,128)(2,1)S(1)}, u32[]{:S(2)}, u32[]{:S(2)}) collective-permute-start(bf16[1,64,2048]{2,1,0:T(8,128)(2,1)} %shard_map.118.refs_2_), channel_id=1, source_target_pairs={{0,4},{4,8},{1,5},{5,9},{2,6},{6,10},{3,7},{7,11},{16,20},{20,24},... | collective-permute-start | bytes 786440 | tf_op jit(solution)/shard_map/ppermute | solution.py:302
  18.2 6.8 %collective-permute-start.13 = (bf16[1,64,2048]{2,1,0:T(8,128)(2,1)}, bf16[1,64,2048]{2,1,0:T(8,128)(2,1)S(1)}, u32[]{:S(2)}, u32[]{:S(2)}) collective-permute-start(bf16[1,64,2048]{2,1,0:T(8,128)(2,1)} %shard_map.118.refs_2_), channel_id=1, source_target_pairs={{12,8},{8,4},{13,9},{9,5},{14,10},{10,6},{15,11},{11,7},{28,24},{2... | collective-permute-start | bytes 786440 | tf_op jit(solution)/shard_map/ppermute | solution.py:303
  23.2 2.6 %collective-permute-start.5 = (bf16[1,64,128]{2,1,0:T(8,128)(2,1)}, bf16[1,64,128]{2,1,0:T(8,128)(2,1)S(1)}, u32[]{:S(2)}, u32[]{:S(2)}) collective-permute-start(bf16[1,64,128]{2,1,0:T(8,128)(2,1)} %get-tuple-element.14), channel_id=1, source_target_pairs={{0,1},{1,0},{2,3},{3,2},{4,5},{5,4},{6,7},{7,6},{8,9},{9,8},{10,11... | collective-permute-start | bytes 49160 | tf_op jit(solution)/shard_map/ppermute | solution.py:324
  23.4 11.2 %collective-permute-start.1 = (bf16[12,64,128]{2,1,0:T(8,128)(2,1)S(1)}, bf16[12,64,128]{2,1,0:T(8,128)(2,1)S(1)}, u32[]{:S(2)}, u32[]{:S(2)}) collective-permute-start(bf16[12,64,128]{2,1,0:T(8,128)(2,1)S(1)} %add_convert_fusion.7.refs_4_), channel_id=1, source_target_pairs={{0,2},{1,3},{2,0},{3,1},{4,6},{5,7},{6,4},{7,5},{8,10},{9,11},{10,... | collective-permute-start | bytes 589832 | tf_op jit(solution)/shard_map/ppermute | solution.py:329
  25.0 15.9 %collective-permute-start.14 = (bf16[1,64,2048]{2,1,0:T(8,128)(2,1)S(1)}, bf16[1,64,2048]{2,1,0:T(8,128)(2,1)S(1)}, u32[]{:S(2)}, u32[]{:S(2)}) collective-permute-start(bf16[1,64,2048]{2,1,0:T(8,128)(2,1)S(1)} %broadcast_select_fusion), channel_id=1, source_target_pairs={{4,8},{8,4},{5,9},{9,5},{6,10},{10,6},{7,11},{11,7},{20,24},{24,20... | collective-permute-start | bytes 786440 | tf_op jit(solution)/shard_map/ppermute | solution.py:304
  26.5 8.1 %collective-permute-start.6 = (bf16[1,64,128]{2,1,0:T(8,128)(2,1)S(1)}, bf16[1,64,128]{2,1,0:T(8,128)(2,1)S(1)}, u32[]{:S(2)}, u32[]{:S(2)}) collective-permute-start(bf16[1,64,128]{2,1,0:T(8,128)(2,1)S(1)} %add_convert_fusion.10.refs_6_), channel_id=1, source_target_pairs={{0,2},{1,3},{2,0},{3,1},{4,6},{5,7},{6,4},{7,5},{8,10},{9,11},{10,... | collective-permute-start | bytes 49160 | tf_op jit(solution)/shard_map/ppermute | solution.py:329
  41.0 18.5 %collective-permute-start.15 = (bf16[1,64,2048]{2,1,0:T(8,128)(2,1)S(1)}, bf16[1,64,2048]{2,1,0:T(8,128)(2,1)S(1)}, u32[]{:S(2)}, u32[]{:S(2)}) collective-permute-start(bf16[1,64,2048]{2,1,0:T(8,128)(2,1)S(1)} %select_select_fusion), channel_id=1, source_target_pairs={{8,12},{4,0},{9,13},{5,1},{10,14},{6,2},{11,15},{7,3},{24,28},{20,... | collective-permute-start | bytes 786440 | tf_op jit(solution)/shard_map/ppermute | solution.py:308
  42.3 41.0 %collective-permute-start.21 = (bf16[4,64,2048]{2,1,0:T(8,128)(2,1)}, bf16[4,64,2048]{2,1,0:T(8,128)(2,1)S(1)}, u32[]{:S(2)}, u32[]{:S(2)}) collective-permute-start(bf16[4,64,2048]{2,1,0:T(8,128)(2,1)} %shard_map.114.refs_3_.refs_10_), channel_id=1, source_target_pairs={{0,4},{12,8},{1,5},{13,9},{2,6},{14,10},{3,7},{15,11},{16,20},{28,... | collective-permute-start | bytes 3145736 | tf_op jit(solution)/shard_map/ppermute | solution.py:441
  58.3 5.7 %collective-permute-start.10 = (bf16[12,64,128]{2,1,0:T(8,128)(2,1)}, bf16[12,64,128]{2,1,0:T(8,128)(2,1)S(1)}, u32[]{:S(2)}, u32[]{:S(2)}) collective-permute-start(bf16[12,64,128]{2,1,0:T(8,128)(2,1)} %shard_map.115.refs_4_.refs_8_), channel_id=1, source_target_pairs={{0,1},{1,0},{2,3},{3,2},{4,5},{5,4},{6,7},{7,6},{8,9},{9,8},{10,11... | collective-permute-start | bytes 589832 | tf_op jit(solution)/shard_map/ppermute | solution.py:324
  63.5 1.5 collective-permute-start.16
  64.0 11.4 %collective-permute-start.11 = (bf16[12,64,128]{2,1,0:T(8,128)(2,1)S(1)}, bf16[12,64,128]{2,1,0:T(8,128)(2,1)S(1)}, u32[]{:S(2)}, u32[]{:S(2)}) collective-permute-start(bf16[12,64,128]{2,1,0:T(8,128)(2,1)S(1)} %add_convert_fusion.6.refs_4_), channel_id=1, source_target_pairs={{0,2},{1,3},{2,0},{3,1},{4,6},{5,7},{6,4},{7,5},{8,10},{9,11},{10,... | collective-permute-start | bytes 589832 | tf_op jit(solution)/shard_map/ppermute | solution.py:329
  65.8 9.7 %collective-permute-start.17 = (bf16[1,64,128]{2,1,0:T(8,128)(2,1)S(1)}, bf16[1,64,128]{2,1,0:T(8,128)(2,1)S(1)}, u32[]{:S(2)}, u32[]{:S(2)}) collective-permute-start(bf16[1,64,128]{2,1,0:T(8,128)(2,1)S(1)} %add_convert_fusion.9.refs_6_), channel_id=1, source_target_pairs={{0,2},{1,3},{2,0},{3,1},{4,6},{5,7},{6,4},{7,5},{8,10},{9,11},{10,... | collective-permute-start | bytes 49160 | tf_op jit(solution)/shard_map/ppermute | solution.py:329
  75.4 41.3 %collective-permute-start.8 = (bf16[1664,256]{1,0:T(8,128)(2,1)}, bf16[1664,256]{1,0:T(8,128)(2,1)}, u32[]{:S(2)}, u32[]{:S(2)}) collective-permute-start(bf16[1664,256]{1,0:T(8,128)(2,1)} %get-tuple-element.18), channel_id=1, source_target_pairs={{0,1},{1,0},{2,3},{3,2},{4,5},{5,4},{6,7},{7,6},{8,9},{9,8},{10,11... | collective-permute-start | bytes 2555912 | tf_op jit(solution)/shard_map/ppermute | solution.py:473
  82.0 28.0 %collective-permute-start.27 = (bf16[12,64,256]{2,1,0:T(8,128)(2,1)}, bf16[12,64,256]{2,1,0:T(8,128)(2,1)S(1)}, u32[]{:S(2)}, u32[]{:S(2)}) collective-permute-start(bf16[12,64,256]{2,1,0:T(8,128)(2,1)} %get-tuple-element.23), channel_id=1, source_target_pairs={{0,4},{12,8},{1,5},{13,9},{2,6},{14,10},{3,7},{15,11},{16,20},{28,... | collective-permute-start | bytes 1179656 | tf_op jit(solution)/shard_map/ppermute | solution.py:456
  84.7 35.2 %collective-permute-start.25 = (bf16[4,64,2048]{2,1,0:T(8,128)(2,1)}, bf16[4,64,2048]{2,1,0:T(8,128)(2,1)}, u32[]{:S(2)}, u32[]{:S(2)}) collective-permute-start(bf16[4,64,2048]{2,1,0:T(8,128)(2,1)} %add_convert_fusion.2), channel_id=1, source_target_pairs={{4,8},{8,4},{5,9},{9,5},{6,10},{10,6},{7,11},{11,7},{20,24},{24,20... | collective-permute-start | bytes 3145736 | tf_op jit(solution)/shard_map/ppermute | solution.py:448
  94.8 55.3 %collective-permute-start.7 = (bf16[1664,256]{1,0:T(8,128)(2,1)}, bf16[1664,256]{1,0:T(8,128)(2,1)}, u32[]{:S(2)}, u32[]{:S(2)}) collective-permute-start(bf16[1664,256]{1,0:T(8,128)(2,1)} %get-tuple-element.17), channel_id=1, source_target_pairs={{0,1},{1,0},{2,3},{3,2},{4,5},{5,4},{6,7},{7,6},{8,9},{9,8},{10,11... | collective-permute-start | bytes 2555912 | tf_op jit(solution)/shard_map/ppermute | solution.py:476
  110.8 31.9 %collective-permute-start.28 = (bf16[8,64,256]{2,1,0:T(8,128)(2,1)}, bf16[8,64,256]{2,1,0:T(8,128)(2,1)}, u32[]{:S(2)}, u32[]{:S(2)}) collective-permute-start(bf16[8,64,256]{2,1,0:T(8,128)(2,1)} %add_convert_fusion.5), channel_id=1, source_target_pairs={{4,8},{8,4},{5,9},{9,5},{6,10},{10,6},{7,11},{11,7},{20,24},{24,20... | collective-permute-start | bytes 786440 | tf_op jit(solution)/shard_map/ppermute | solution.py:457
  112.3 27.3 %collective-permute-start.22 = (bf16[4,64,2048]{2,1,0:T(8,128)(2,1)}, bf16[4,64,2048]{2,1,0:T(8,128)(2,1)S(1)}, u32[]{:S(2)}, u32[]{:S(2)}) collective-permute-start(bf16[4,64,2048]{2,1,0:T(8,128)(2,1)} %shard_map.126), channel_id=1, source_target_pairs={{0,4},{12,8},{1,5},{13,9},{2,6},{14,10},{3,7},{15,11},{16,20},{28,... | collective-permute-start | bytes 3145736 | tf_op jit(solution)/shard_map/ppermute | solution.py:447
  119.0 20.5 %copy-start.1 = (bf16[4,64,2048]{2,1,0:T(8,128)(2,1)S(1)}, bf16[4,64,2048]{2,1,0:T(8,128)(2,1)}, u32[]{:S(2)}) copy-start(bf16[4,64,2048]{2,1,0:T(8,128)(2,1)} %shard_map.126) | copy-start | bytes 3145732
  119.0 32.4 %collective-permute-start.9 = (bf16[1664,256]{1,0:T(8,128)(2,1)}, bf16[1664,256]{1,0:T(8,128)(2,1)}, u32[]{:S(2)}, u32[]{:S(2)}) collective-permute-start(bf16[1664,256]{1,0:T(8,128)(2,1)} %add_convert_fusion.4), channel_id=1, source_target_pairs={{0,2},{1,3},{2,0},{3,1},{4,6},{5,7},{6,4},{7,5},{8,10},{9,11},{10,... | collective-permute-start | bytes 2555912 | tf_op jit(solution)/shard_map/ppermute | solution.py:329
  121.5 60.6 %collective-permute-start.26 = (bf16[4,64,2048]{2,1,0:T(8,128)(2,1)S(1)}, bf16[4,64,2048]{2,1,0:T(8,128)(2,1)S(1)}, u32[]{:S(2)}, u32[]{:S(2)}) collective-permute-start(bf16[4,64,2048]{2,1,0:T(8,128)(2,1)S(1)} %add_convert_fusion.1), channel_id=1, source_target_pairs={{8,12},{4,0},{9,13},{5,1},{10,14},{6,2},{11,15},{7,3},{24,28},{20,... | collective-permute-start | bytes 3145736 | tf_op jit(solution)/shard_map/ppermute | solution.py:451
  140.9 41.2 %collective-permute-start.24 = (bf16[4,64,2048]{2,1,0:T(8,128)(2,1)}, bf16[4,64,2048]{2,1,0:T(8,128)(2,1)}, u32[]{:S(2)}, u32[]{:S(2)}) collective-permute-start(bf16[4,64,2048]{2,1,0:T(8,128)(2,1)} %add_convert_fusion.3), channel_id=1, source_target_pairs={{4,8},{8,4},{5,9},{9,5},{6,10},{10,6},{7,11},{11,7},{20,24},{24,20... | collective-permute-start | bytes 3145736 | tf_op jit(solution)/shard_map/ppermute | solution.py:450
  142.7 39.4 %collective-permute-start.23 = (bf16[4,64,2048]{2,1,0:T(8,128)(2,1)}, bf16[4,64,2048]{2,1,0:T(8,128)(2,1)}, u32[]{:S(2)}, u32[]{:S(2)}) collective-permute-start(bf16[4,64,2048]{2,1,0:T(8,128)(2,1)} %shard_map.127), channel_id=1, source_target_pairs={{0,4},{12,8},{1,5},{13,9},{2,6},{14,10},{3,7},{15,11},{16,20},{28,... | collective-permute-start | bytes 3145736 | tf_op jit(solution)/shard_map/ppermute | solution.py:449
  150.1 14.5 %collective-permute-start.29 = (bf16[4,64,256]{2,1,0:T(8,128)(2,1)S(1)}, bf16[4,64,256]{2,1,0:T(8,128)(2,1)S(1)}, u32[]{:S(2)}, u32[]{:S(2)}) collective-permute-start(bf16[4,64,256]{2,1,0:T(8,128)(2,1)S(1)} %fusion), channel_id=1, source_target_pairs={{8,12},{4,0},{9,13},{5,1},{10,14},{6,2},{11,15},{7,3},{24,28},{20,... | collective-permute-start | bytes 393224 | tf_op jit(solution)/shard_map/ppermute | solution.py:458
  155.6 19.9 %collective-permute-start.18 = (bf16[128,256]{1,0:T(8,128)(2,1)}, bf16[128,256]{1,0:T(8,128)(2,1)}, u32[]{:S(2)}, u32[]{:S(2)}) collective-permute-start(bf16[128,256]{1,0:T(8,128)(2,1)} %get-tuple-element.21.refs_1_), channel_id=1, source_target_pairs={{0,4},{4,8},{8,12},{12,0},{1,5},{5,9},{9,13},{13,1},{2,6},{6,10},{... | collective-permute-start | bytes 196616 | tf_op jit(solution)/shard_map/ppermute | solution.py:292
  164.5 17.6 %copy-start.6 = (bf16[4,64,2048]{2,1,0:T(8,128)(2,1)S(1)}, bf16[4,64,2048]{2,1,0:T(8,128)(2,1)}, u32[]{:S(2)}) copy-start(bf16[4,64,2048]{2,1,0:T(8,128)(2,1)} %shard_map.125) | copy-start | bytes 3145732
  164.5 12.7 %collective-permute-start.19 = (bf16[128,256]{1,0:T(8,128)(2,1)}, bf16[128,256]{1,0:T(8,128)(2,1)S(1)}, u32[]{:S(2)}, u32[]{:S(2)}) collective-permute-start(bf16[128,256]{1,0:T(8,128)(2,1)} %get-tuple-element.21.refs_1_), channel_id=1, source_target_pairs={{0,8},{4,12},{8,0},{12,4},{1,9},{5,13},{9,1},{13,5},{2,10},{6,14},... | collective-permute-start | bytes 196616 | tf_op jit(solution)/shard_map/ppermute | solution.py:292
  175.4 4.5 %collective-permute-start.20 = (bf16[128,256]{1,0:T(8,128)(2,1)}, bf16[128,256]{1,0:T(8,128)(2,1)S(1)}, u32[]{:S(2)}, u32[]{:S(2)}) collective-permute-start(bf16[128,256]{1,0:T(8,128)(2,1)} %get-tuple-element.21.refs_1_), channel_id=1, source_target_pairs={{0,12},{4,0},{8,4},{12,8},{1,13},{5,1},{9,5},{13,9},{2,14},{6,2},{... | collective-permute-start | bytes 196616 | tf_op jit(solution)/shard_map/ppermute | solution.py:292
  (33 other events, 233.8 us)

commit v3 on v2

v3 whole, which is shorter than its diff:
```python
import jax
import jax.numpy as jnp
from jax import lax
from jax.experimental import pallas as pl
from jax.experimental.pallas import tpu as pltpu
from jax.sharding import PartitionSpec as P

BLOCK = 128
SW = 1
OWN = 4


ADAPTER_SCALE = 0.5

ANYWHERE = pl.BlockSpec(memory_space=pl.ANY)
ROW_PRODUCT = (((1,), (1,)), ((), ()))


def call(kernel, scalars, grid, inputs, outputs, tokens=(), us=1.0, scratch=(), aliases=None):
    def run(*refs):
        cut = len(scalars) + len(inputs)
        return kernel(*refs[:cut], *refs[cut + len(tokens) :])

    return pl.pallas_call(
        run,
        grid_spec=pltpu.PrefetchScalarGridSpec(
            num_scalar_prefetch=len(scalars),
            grid=grid,
            in_specs=[spec for _, spec in inputs] + [ANYWHERE] * len(tokens),
            out_specs=[spec for _, _, spec in outputs],
            scratch_shapes=scratch,
        ),
        out_shape=[jax.ShapeDtypeStruct(shape, kind) for shape, kind, _ in outputs],
        input_output_aliases=aliases or {},
        cost_estimate=pl.CostEstimate(flops=0, bytes_accessed=int(us * 3.6e6), transcendentals=0),
    )(*scalars, *[array for array, _ in inputs], *tokens)


def constant_spec(shape):
    return pl.BlockSpec(shape, lambda *_: (0,) * len(shape), pipeline_mode=pl.Buffered(1))


def whole(array):
    return (array, constant_spec(array.shape))


def nothing(*refs):
    pass


def after(array, *tokens):
    return call(
        nothing, (), (1,), [(array, ANYWHERE)], [(array.shape, array.dtype, ANYWHERE)], tokens, 0.1, aliases={0: 0}
    )[0]


def own_last(maps, us, tokens=()):
    shape = (SW, *maps.shape[1:])
    last = maps.shape[0] - SW

    def kernel(in_ref, out_ref):
        out_ref[...] = in_ref[...]

    return call(
        kernel,
        (),
        (1,),
        [(maps, pl.BlockSpec(shape, lambda i: (last, 0, 0)))],
        [(shape, maps.dtype, pl.BlockSpec(shape, lambda i: (0, 0, 0)))],
        tokens,
        us,
    )[0]


def masked_rank(adapter, rows, length):
    ranks = lax.dot_general(adapter, rows, ROW_PRODUCT, preferred_element_type=jnp.float32)
    live = lax.broadcasted_iota(jnp.int32, ranks.shape, 1) < length
    return jnp.where(live, ranks, 0.0).astype(rows.dtype)


def rank_terms(lengths, maps, pick, choices, features, each, us, tokens=()):
    blocks, rank, width = maps.shape
    steps = pl.cdiv(blocks, each)

    def kernel(lengths_ref, pick_ref, *refs):
        maps_refs, rows_refs, (out_ref, chosen_ref) = refs[:each], refs[each : 2 * each], refs[-2:]
        step = pl.program_id(0)

        def one(k):
            block = step * each + k
            out_ref[block] = masked_rank(maps_refs[k][0], rows_refs[k][...], lengths_ref[block])

        def last(k):
            for j, choice in enumerate(refs[2 * each : -2]):

                @pl.when(pick_ref[0] == j)
                def _():
                    chosen_ref[...] = choice[...]

            out_ref[blocks - 1] = masked_rank(chosen_ref[0], rows_refs[k][...], lengths_ref[blocks - 1])

        end = blocks - 1 - (steps - 1) * each

        @pl.when(step < steps - 1)
        def _():
            for k in range(each):
                one(k)

        @pl.when(step == steps - 1)
        def _():
            for k in range(end):
                one(k)
            last(end)

    def at(i, k):
        block = i * each + k
        return jnp.where(block < blocks, block, block - each)

    return call(
        kernel,
        (lengths, pick),
        (steps,),
        [(maps, pl.BlockSpec((1, rank, width), lambda i, *_, k=k: (at(i, k), 0, 0))) for k in range(each)]
        + [(features, pl.BlockSpec((BLOCK, width), lambda i, *_, k=k: (at(i, k), 0))) for k in range(each)]
        + [whole(choice) for choice in choices],
        [
            ((blocks, rank, BLOCK), features.dtype, constant_spec((blocks, rank, BLOCK))),
            (choices[0].shape, features.dtype, constant_spec(choices[0].shape)),
        ],
        tokens,
        us,
    )


def summed(pair, at):
    return (pair[0][at].astype(jnp.float32) + pair[1][at].astype(jnp.float32)).astype(pair[0].dtype)


def down_rows(codes, first, parts, copies, ranks, features, us, tokens=()):
    blocks, rank, _ = ranks[0].shape
    width = features.shape[1]

    def block_at(code):
        return jnp.maximum((code >> 1) - 1, 0)

    def kernel(codes_ref, a, b, *refs):
        rows_refs, last_ref, outs, late = refs[:OWN], refs[OWN], refs[OWN + 1 : -1], refs[-1]
        step = pl.program_id(0)

        @pl.when(step == 0)
        def _():
            late[...] = jnp.dot(summed((a, b), blocks - 1), last_ref[...], preferred_element_type=jnp.float32)

        for k in range(OWN):
            code = codes_ref[first + step * OWN + k]
            mine = summed((a, b), block_at(code))
            mine = jnp.where(code > 1, mine, jnp.zeros_like(mine))
            total = jnp.dot(mine, rows_refs[k][...], preferred_element_type=jnp.float32)
            total = total + jnp.where((code & 1) > 0, late[...], 0.0)
            value = (ADAPTER_SCALE * total).astype(features.dtype)
            for part, out_ref in enumerate(outs):
                if len(outs) == 1:
                    out_ref[k] = value
                    continue

                @pl.when(step == min(part, parts - 1))
                def _():
                    out_ref[k] = value

    def rows_spec(k):
        return pl.BlockSpec((BLOCK, width), lambda r, at: (block_at(at[first + r * OWN + k]), 0))

    shape = (OWN, rank, width)
    if copies:
        outs = [(shape, features.dtype, constant_spec(shape))] * (parts - 1 + copies)
    else:
        outs = [((parts * OWN, rank, width), features.dtype, pl.BlockSpec(shape, lambda r, *_: (r, 0, 0)))]
    return call(
        kernel,
        (codes,),
        (parts,),
        [whole(array) for array in ranks]
        + [(features, rows_spec(k)) for k in range(OWN)]
        + [(features, pl.BlockSpec((BLOCK, width), lambda r, *_: (blocks - 1, 0), pipeline_mode=pl.Buffered(1)))],
        outs,
        tokens,
        us,
        [pltpu.VMEM((rank, width), jnp.float32)],
    )


def up_rows(codes, parts, ranks, features, us, tokens=()):
    blocks, rank, _ = ranks[0].shape
    width = features.shape[1]

    def kernel(codes_ref, a, b, rows_ref, *outs):
        late = jnp.dot(
            summed((a, b), blocks - 1), rows_ref[(blocks - 1) * BLOCK :], preferred_element_type=jnp.float32
        )
        done = 0
        for out_ref in outs:

            def one(r, carry, out_ref=out_ref, done=done):
                code = codes_ref[done + r]
                at = jnp.maximum((code >> 1) - 1, 0)
                mine = summed((a, b), at)
                mine = jnp.where(code > 1, mine, jnp.zeros_like(mine))
                mine_rows = rows_ref[pl.ds(pl.multiple_of(at * BLOCK, BLOCK), BLOCK), :]
                total = jnp.dot(mine, mine_rows, preferred_element_type=jnp.float32)
                total = total + jnp.where((code & 1) > 0, late, 0.0)
                out_ref[r] = (ADAPTER_SCALE * total).astype(out_ref.dtype)
                return carry

            if out_ref.shape[0] <= OWN:
                for r in range(out_ref.shape[0]):
                    one(r, 0)
            else:
                lax.fori_loop(0, out_ref.shape[0], one, 0)
            done += out_ref.shape[0]

    return call(
        kernel,
        (codes,),
        (1,),
        [whole(array) for array in (*ranks, features)],
        [((rows, rank, width), features.dtype, constant_spec((rows, rank, width))) for rows in parts],
        tokens,
        us,
    )


def base_terms(columns, hidden, weight, us, tokens=()):
    rows, depth = hidden.shape
    width = weight.shape[1] // 4
    tile = rows // 4

    def kernel(columns_ref, rows_ref, *refs):
        for k in range(4):
            out_ref = refs[4 + k // 2]
            out_ref[k % 2] = jnp.dot(rows_ref[...], refs[k][...], preferred_element_type=jnp.float32).astype(
                out_ref.dtype
            )

    def column(k):
        return pl.BlockSpec((depth, width), lambda i, at: (0, at[k]), pipeline_mode=pl.Buffered(1))

    return call(
        kernel,
        (columns,),
        (rows // tile,),
        [(hidden, pl.BlockSpec((tile, depth), lambda i, *_: (i, 0)))]
        + [(weight, column(k)) for k in range(4)],
        [((2, rows, width), hidden.dtype, pl.BlockSpec((2, tile, width), lambda i, *_: (0, i, 0)))] * 2,
        tokens,
        us,
    )


def values_of(lengths, base, ranks, maps, last_map, us, tokens=()):
    _, rows, width = base[0].shape
    blocks = rows // BLOCK

    def kernel(lengths_ref, one, two, three, a, b, maps_ref, last_ref, out_ref, last_out):
        for k in range(blocks):
            at = slice(k * BLOCK, (k + 1) * BLOCK)
            adapter = maps_ref[k] if k < blocks - 1 else last_ref[0]
            added = lax.dot_general(
                summed((a, b), k), adapter, (((0,), (0,)), ((), ())), preferred_element_type=jnp.float32
            )
            frozen = one[0, at].astype(jnp.float32) + two[0, at].astype(jnp.float32) + three[at].astype(jnp.float32)
            live = lax.broadcasted_iota(jnp.int32, frozen.shape, 0) < lengths_ref[k]
            values = jnp.where(live, frozen + ADAPTER_SCALE * added, 0.0).astype(out_ref.dtype)
            out_ref[at] = values
            if k == blocks - 1:
                last_out[...] = values

    second = pl.BlockSpec((1, rows, width), lambda *_: (1, 0, 0), pipeline_mode=pl.Buffered(1))
    return call(
        kernel,
        (lengths,),
        (1,),
        [(base[0], second), (base[1], second)] + [whole(array) for array in (base[2], *ranks, maps, last_map)],
        [
            ((rows, width), maps.dtype, constant_spec((rows, width))),
            ((BLOCK, width), maps.dtype, constant_spec((BLOCK, width))),
        ],
        tokens,
        us,
    )


def put_last(pick, values, choices, us):
    width = values.shape[1]
    block = values.shape[0] // BLOCK - 1

    def kernel(pick_ref, *refs):
        for k, choice in enumerate(refs[:-2]):

            @pl.when(pick_ref[0] == k)
            def _():
                refs[-1][...] = choice[...]

    return call(
        kernel,
        (pick,),
        (1,),
        [whole(choice) for choice in choices] + [(values, ANYWHERE)],
        [(values.shape, values.dtype, pl.BlockSpec((BLOCK, width), lambda i, *_: (block, 0)))],
        us=us,
        aliases={1 + len(choices): 0},
    )[0]


def shift(array, by):
    size = lax.axis_size("dp")
    return lax.ppermute(array, "dp", [(i, (i + by) % size) for i in range(size)])


def shifted(array, source):
    size = lax.axis_size("dp")
    me = lax.axis_index("dp")
    if size > 4:
        taken = lax.dynamic_index_in_dim(lax.all_gather(array, "dp"), source, 0, keepdims=False)
        return [taken], jnp.zeros((1,), jnp.int32)
    choices = [array] + [shift(array, by) for by in range(1, size)]
    return choices, ((me - source) % size).reshape(1)


def add(*arrays):
    return sum(array.astype(jnp.float32) for array in arrays).astype(arrays[0].dtype)


def near(array):
    size = lax.axis_size("tensor")
    return lax.ppermute(array, "tensor", [(i, i ^ 1) for i in range(size)])


def far(array):
    size = lax.axis_size("tensor")
    return lax.ppermute(array, "tensor", [(i, i ^ 2) for i in range(size)])


def exchanged(array):
    array = add(array, near(array))
    return array, far(array)


def line_reduce_scatter(table):
    size = lax.axis_size("dp")
    me = lax.axis_index("dp")

    def entry(index):
        return lax.dynamic_index_in_dim(table, jnp.clip(index, 0, size - 1), 0, keepdims=False)

    from_left = from_right = None
    for step in range(size - 1):
        right = entry(size - 1 - step + me)
        left = entry(step - (size - 1 - me))
        if step > 0:
            right = add(right, from_left)
            left = add(left, from_right)
        from_left = lax.ppermute(right, "dp", [(i, i + 1) for i in range(step + 1)])
        from_right = lax.ppermute(left, "dp", [(i, i - 1) for i in range(size - 1 - step, size)])
    return entry(me) if size == 1 else add(entry(me), from_left, from_right)


ROLES = ((3, 2, 0, 1), (0, 3, 1, 2), (3, 0, 2, 1), (0, 1, 3, 2))


def body(
    partner,
    block_tenant_index,
    block_live_length,
    tenant_table_row,
    hidden,
    cotangent,
    frozen_value_weight,
    adapter_down_rows,
    adapter_up_matrix,
):
    blocks = block_tenant_index.shape[0]
    kept = blocks - SW
    devices = lax.axis_size("dp")
    me = lax.axis_index("dp")
    column = lax.axis_index("tensor")
    lengths = block_live_length
    line = devices == 4
    order = jnp.arange(devices, dtype=jnp.int32)
    holder = jnp.sum(jnp.where(partner == me, order, 0))

    up_choices, up_pick = shifted(own_last(adapter_up_matrix, 1.0), holder)
    cot_terms, up_last = rank_terms(
        lengths, adapter_up_matrix, up_pick, up_choices, cotangent, blocks, 3.0
    )
    rank_cot = exchanged(cot_terms)
    down_choices, down_pick = shifted(own_last(adapter_down_rows, 1.5, [cot_terms]), holder)

    table_rows = jnp.sum(
        jnp.where(
            block_tenant_index[:, None] == jnp.arange(tenant_table_row.shape[0], dtype=jnp.int32)[None, :],
            tenant_table_row[None, :],
            0,
        ),
        axis=1,
    )
    weights = jnp.where(jnp.arange(blocks) < kept, 2 * (jnp.arange(blocks, dtype=jnp.int32) + 1), 1)

    def codes_of(owners):
        rows = (owners[:, None] * OWN + jnp.arange(OWN, dtype=jnp.int32)[None, :]).reshape(-1)
        return jnp.sum(jnp.where(rows[:, None] == table_rows[None, :], weights[None, :], 0), axis=1)

    if line:
        inner = (me == 1) | (me == 2)
        codes = codes_of(jnp.array(ROLES, jnp.int32)[me])
        (first,) = down_rows(codes, 0, 1, 1, rank_cot, hidden, 3.0)
        from_first = lax.ppermute(first, "dp", [(0, 1), (3, 2), (1, 0), (2, 3)])
        second, own, third, third_too = down_rows(codes, OWN, 3, 2, rank_cot, hidden, 6.0, [first])
        from_inner = lax.ppermute(third, "dp", [(1, 2), (2, 1)])
        second = add(second, jnp.where(inner, from_first, jnp.zeros((), first.dtype)))
        from_second = lax.ppermute(second, "dp", [(0, 2), (3, 1), (1, 3), (2, 0)])
        from_third = lax.ppermute(after(third_too, from_first), "dp", [(0, 1), (3, 2)])
        near_total = lax.optimization_barrier(
            own.astype(jnp.float32)
            + jnp.where(inner, from_inner, from_first).astype(jnp.float32)
        )
        down_out = (near_total + from_second.astype(jnp.float32) + from_third.astype(jnp.float32)).astype(own.dtype)
        start, window = third, second
    else:
        codes = codes_of(order)
        (start,) = down_rows(codes, 0, devices, 0, rank_cot, hidden, 3.0)
        down_out = line_reduce_scatter(start.reshape(devices, OWN, *start.shape[1:]))
        window = start

    in_terms, _ = rank_terms(
        lengths, adapter_down_rows, down_pick, down_choices, hidden, 4, 6.0, [start]
    )
    rank_in = exchanged(in_terms)

    columns = jnp.stack([column ^ 3, column ^ 1, column ^ 2, column]).astype(jnp.int32)
    given, mine = base_terms(columns, hidden, frozen_value_weight, 10.0, [in_terms])
    taken = near(given)
    across = far(add(mine[0], taken[0]))

    if line:
        up_codes = codes_of((me + jnp.array([1, 2, 3, 0], jnp.int32)) % devices)
        *sent, up_own = up_rows(up_codes, [OWN] * 4, rank_in, cotangent, 3.0, [window])
        up_out = add(up_own, *[shift(array, by + 1) for by, array in enumerate(sent)])
    else:
        (up_table,) = up_rows(codes, [devices * OWN], rank_in, cotangent, 3.0)
        up_out = line_reduce_scatter(up_table.reshape(devices, OWN, *up_table.shape[1:]))

    values, last_values = values_of(
        lengths, (mine, taken, across), rank_in, adapter_up_matrix, up_last, 4.0, [window]
    )
    value_choices, value_pick = shifted(last_values, partner[me])
    projected_values = put_last(value_pick, values, value_choices, 1.5)
    return (projected_values, down_out, up_out)


def solution(mesh):
    in_specs = (
        P("groups"),
        P(("groups", "dp")),
        P(("groups", "dp")),
        P("groups"),
        P(("groups", "dp"), "tensor"),
        P(("groups", "dp"), "tensor"),
        P("tensor", None),
        P(("groups", "dp"), None, "tensor"),
        P(("groups", "dp"), None, "tensor"),
    )
    out_specs = (
        P(("groups", "dp"), "tensor"),
        P(("groups", "dp"), None, "tensor"),
        P(("groups", "dp"), None, "tensor"),
    )
    return jax.shard_map(body, mesh=mesh, in_specs=in_specs, out_specs=out_specs, check_vma=False)
```

time: 187 us -> 178 us (0.952)
  waiting for transfers between devices: 30 us -> 80 us
  Pallas kernels: 71.5 us -> 48.1 us
  starting transfers between devices: 49.5 us -> 27.7 us
  between operations: 8.16 us -> 2.16 us
  other arithmetic: 18.2 us -> 14.6 us
  local copies, waits for them, and re-layouts: 7.93 us -> 5.16 us
    ppermute x5 -> x3, waiting for transfers between devices: 0.01 us -> 26.2 us  [far(): return lax.ppermute(array, 'tensor', [(i, i ^ 2) for i in range(size)])]
    ppermute x25 -> x19, waiting for transfers between devices: 30 us -> 53.8 us  [the longest x12 30.4 us: shift(): lax.ppermute(array, 'dp', [(i, (i + by) % size) for i in range(size)])]
    pallas_call x17 -> x11, Pallas kernels: 71.5 us -> 48.1 us  [call(): pl.pallas_call(run, grid_spec=pltpu.PrefetchScalarGridSpec(num_scalar_pre...]
    ppermute x25 -> x19, starting transfers between devices: 44.6 us -> 24 us  [the longest x12 18.4 us: shift(): lax.ppermute(array, 'dp', [(i, (i + by) % size) for i in range(size)])]
    convert_element_type x11 -> x4, other arithmetic: 13.1 us -> 5.19 us  [add(): sum((array.astype(jnp.float32) for array in arrays)).astype(arrays[0].dtype)]
    add x1 -> x3, other arithmetic: 0.07 us -> 2.89 us  [the longest x1 2.74 us: body(): own.astype(jnp.float32)]
    slice x3 -> x0, local copies, waits for them, and re-layouts: 2.04 us -> none  [the longest x1 0.76 us: body(): up_choices, up_pick = shifted(adapter_up_matrix[kept:], holders[me])]
    convert_element_type x2 -> x1, other arithmetic: 1.02 us -> 3.02 us  [body(): (near_total + from_second.astype(jnp.float32) + from_third.astype(jnp.flo...]
  transfers between devices with their start and end apart: 30 -> 22, of which waited for: 4 -> 11; matrix products, arithmetic and copies ran while one was open for 10% -> 9% of each run, Pallas kernels for 39% -> 12%
where the time goes in v3:
time: 178 us
  waiting for transfers between devices  80 us (45%)
  Pallas kernels  48.1 us (27%)
  starting transfers between devices  27.7 us (16%)
  other arithmetic  14.6 us (8%)
  local copies, waits for them, and re-layouts  5.16 us (3%)
  between operations  2.16 us (1%)
    pallas_call x11, Pallas kernels, call(): pl.pallas_call(run, grid_spec=pltpu.PrefetchScalarGridSpec(num_scalar_pre...  48.1 us
    ppermute x12, waiting for transfers between devices, shift(): lax.ppermute(array, 'dp', [(i, (i + by) % size) for i in range(size)])  30.4 us
    ppermute x3, waiting for transfers between devices, far(): return lax.ppermute(array, 'tensor', [(i, i ^ 2) for i in range(size)])  26.2 us
    ppermute x1, waiting for transfers between devices, body(): from_first = lax.ppermute(first, 'dp', [(0, 1), (3, 2), (1, 0), (2, 3)])  23.4 us
    ppermute x12, starting transfers between devices, shift(): lax.ppermute(array, 'dp', [(i, (i + by) % size) for i in range(size)])  18.4 us
    convert_element_type x4, other arithmetic, add(): sum((array.astype(jnp.float32) for array in arrays)).astype(arrays[0].dtype)  5.19 us
    unnamed x48, local copies, waits for them, and re-layouts  4.41 us
    ppermute x3, starting transfers between devices, far(): return lax.ppermute(array, 'tensor', [(i, i ^ 2) for i in range(size)])  3.65 us
  transfers between devices with their start and end apart: 22, of which 11 were waited for; matrix products, arithmetic and copies ran while one was open for 9% of the time, Pallas kernels for 12%

profile of v3, /device:TPU:0, one launch (start us, length us, event | category | flops | bytes accessed | tf_op | source)
XLA Modules:
  0.0 177.6 jit_solution(15652380217892677772)
XLA Ops:
  0.6 1.4 shard_map.130.refs_28_
  2.0 5.0 %collective-permute-start.2 = (bf16[1,64,256]{2,1,0:T(8,128)(2,1)}, bf16[1,64,256]{2,1,0:T(8,128)(2,1)S(1)}, u32[]{:S(2)}, u32[]{:S(2)}) collective-permute-start(bf16[1,64,256]{2,1,0:T(8,128)(2,1)} %shard_map.130.refs_28_), channel_id=1, source_target_pairs={{0,12},{4,0},{8,4},{12,8},{1,13},{5,1},{9,5},{13,9},{2,14},{6,2},{... | collective-permute-start | bytes 98312 | tf_op jit(solution)/shard_map/ppermute | solution.py:316
  8.1 1.3 fusion.2
  13.6 3.4 %shard_map.131 = (bf16[13,64,128]{2,1,0:T(8,128)(2,1)}, bf16[1,64,256]{2,1,0:T(8,128)(2,1)}) custom-call(s32[13]{0:T(128)} %refs_0_.9, s32[1]{0:T(128)} %bitcast.6.refs_1_, bf16[13,64,256]{2,1,0:T(8,128)(2,1)} %refs_6_.9, bf16[13,64,256]{2,1,0:T(8,128)(2,1)} %refs_6_.9, bf16[13,64,256]{2,1,0:T(8,128)(2,1)} %refs_6_.9, bf16[13,64,256]{2,1,0:T(8,128)(2,1)} %refs_6_.9, ...), custom_call_target="tpu_custom_call" | custom-call | bytes 10800000 | tf_op jit(solution)/shard_map/pallas_call | solution.py:24
  17.3 1.7 shard_map.132.refs_10_
  19.9 1.1 collective-permute-start.4
  21.0 1.1 collective-permute-start.3
  22.2 1.6 collective-permute-start.7
  25.1 4.0 %collective-permute-done.7.refs_2_ = bf16[13,64,128]{2,1,0:T(8,128)(2,1)S(1)} collective-permute-done((bf16[13,64,128]{2,1,0:T(8,128)(2,1)S(1)}, bf16[13,64,128]{2,1,0:T(8,128)(2,1)S(1)}, u32[]{:S(2)}, u32[]{:S(2)}) %collective-permute-start.7) | collective-permute-done | bytes 213024 | tf_op jit(solution)/shard_map/ppermute | solution.py:340
  29.8 4.0 %shard_map.133.refs_8_ = bf16[4,64,2048]{2,1,0:T(8,128)(2,1)} custom-call(s32[16]{0:T(128)} %get-tuple-element.34.refs_0_, bf16[13,64,128]{2,1,0:T(8,128)(2,1)} %copy-done.4, bf16[13,64,128]{2,1,0:T(8,128)(2,1)} %copy-done.7, bf16[1664,2048]{1,0:T(8,128)(2,1)} %refs_1_.1, bf16[1664,2048]{1,0:T(8,128)(2,1)} %refs_1_.1, bf16[1664,2048]{1,0:T(8,128)(2,1)} %refs_1_.1, ...), custom_call_target="tpu_custom_call" | custom-call | bytes 10800000 | tf_op jit(solution)/shard_map/pallas_call | solution.py:24
  33.8 8.6 %shard_map.134 = (bf16[4,64,2048]{2,1,0:T(8,128)(2,1)}, bf16[4,64,2048]{2,1,0:T(8,128)(2,1)}, bf16[4,64,2048]{2,1,0:T(8,128)(2,1)}, bf16[4,64,2048]{2,1,0:T(8,128)(2,1)}) custom-call(s32[16]{0:T(128)} %get-tuple-element.34.refs_0_, bf16[13,64,128]{2,1,0:T(8,128)(2,1)} %copy-done.4, bf16[13,64,128]{2,1,0:T(8,128)(2,1)} %copy-done.7, ...), custom_call_target="tpu_custom_call" | custom-call | bytes 21600000 | tf_op jit(solution)/shard_map/pallas_call | solution.py:24
  42.4 2.4 %collective-permute-done.4.refs_12_ = bf16[1,64,2048]{2,1,0:T(8,128)(2,1)S(1)} collective-permute-done((bf16[1,64,2048]{2,1,0:T(8,128)(2,1)}, bf16[1,64,2048]{2,1,0:T(8,128)(2,1)S(1)}, u32[]{:S(2)}, u32[]{:S(2)}) %collective-permute-start.4) | collective-permute-done | bytes 262176 | tf_op jit(solution)/shard_map/ppermute | solution.py:316
  45.5 8.0 %shard_map.135 = (bf16[13,64,128]{2,1,0:T(8,128)(2,1)}, bf16[1,64,2048]{2,1,0:T(8,128)(2,1)}) custom-call(s32[13]{0:T(128)} %refs_0_.9, s32[1]{0:T(128)} %bitcast.6.refs_1_, bf16[13,64,2048]{2,1,0:T(8,128)(2,1)} %refs_5_.8, bf16[13,64,2048]{2,1,0:T(8,128)(2,1)} %refs_5_.8, bf16[13,64,2048]{2,1,0:T(8,128)(2,1)} %refs_5_.8, bf16[13,64,2048]{2,1,0:T(8,128)(2,1)} %refs_5_.8, ...), custom_call_target="tpu_custom_call" | custom-call | bytes 21600000 | tf_op jit(solution)/shard_map/pallas_call | solution.py:24
  53.5 12.3 %shard_map.136 = (bf16[2,1664,256]{2,1,0:T(8,128)(2,1)}, bf16[2,1664,256]{2,1,0:T(8,128)(2,1)}) custom-call(s32[4]{0:T(128)} %pad_add_fusion.refs_0_, bf16[1664,2048]{1,0:T(8,128)(2,1)} %refs_1_.1, bf16[2048,1024]{1,0:T(8,128)(2,1)} %refs_5_.9, bf16[2048,1024]{1,0:T(8,128)(2,1)} %refs_5_.9, bf16[2048,1024]{1,0:T(8,128)(2,1)} %refs_5_.9, ...), custom_call_target="tpu_custom_call" | custom-call | bytes 36000000 | tf_op jit(solution)/shard_map/pallas_call | solution.py:24
  66.0 1.7 collective-permute-start.16
  68.1 23.4 %collective-permute-done.12.refs_1_ = bf16[4,64,2048]{2,1,0:T(8,128)(2,1)S(1)} collective-permute-done((bf16[4,64,2048]{2,1,0:T(8,128)(2,1)S(1)}, bf16[4,64,2048]{2,1,0:T(8,128)(2,1)S(1)}, u32[]{:S(2)}, u32[]{:S(2)}) %collective-permute-start.12) | collective-permute-done | bytes 1048608 | tf_op jit(solution)/shard_map/ppermute | solution.py:416
  92.4 3.2 %collective-permute-start.18 = (bf16[4,64,2048]{2,1,0:T(8,128)(2,1)}, bf16[4,64,2048]{2,1,0:T(8,128)(2,1)}, u32[]{:S(2)}, u32[]{:S(2)}) collective-permute-start(bf16[4,64,2048]{2,1,0:T(8,128)(2,1)} %shard_map.139), channel_id=1, source_target_pairs={{0,4},{12,8},{1,5},{13,9},{2,6},{14,10},{3,7},{15,11},{16,20},{28,... | collective-permute-start | bytes 3145736 | tf_op jit(solution)/shard_map/ppermute | solution.py:421
  95.6 2.7 %convert_add_fusion = (f32[4,64,2048]{2,1,0:T(8,128)S(1)}, bf16[4,64,2048]{2,1,0:T(8,128)(2,1)S(1)}) fusion(bf16[4,64,2048]{2,1,0:T(8,128)(2,1)} %get-tuple-element.27, bf16[4,64,2048]{2,1,0:T(8,128)(2,1)} %collective-permute-done.16, bf16[4,64,2048]{2,1,0:T(8,128)(2,1)} %copy-done.2, pred[]{:T(512)S(6)} %or.3, bf16[4,64,2048]{2,1,0:T(8,128)(2,1)} %get-tuple-element.24), kind=kLoop, calls=%fused_computation.1 | loop fusion | flops 4718592 | bytes 7340033 | tf_op jit(solution)/shard_map/add | solution.py:423
  98.6 2.5 %fusion = bf16[1664,256]{1,0:T(8,128)(2,1)} fusion(bf16[2,1664,256]{2,1,0:T(8,128)(2,1)} %collective-permute-done.8.refs_2_, bf16[2,1664,256]{2,1,0:T(8,128)(2,1)S(1)} %copy-done.3), kind=kLoop, calls=%fused_computation.4 | loop fusion | flops 1703936 | bytes 2555904 | tf_op jit(solution)/shard_map/convert_element_type | solution.py:330
  101.2 1.5 collective-permute-start.9
  104.3 22.2 %collective-permute-done.11.refs_5_.refs_2_ = bf16[13,64,128]{2,1,0:T(8,128)(2,1)S(1)} collective-permute-done((bf16[13,64,128]{2,1,0:T(8,128)(2,1)S(1)}, bf16[13,64,128]{2,1,0:T(8,128)(2,1)S(1)}, u32[]{:S(2)}, u32[]{:S(2)}) %collective-permute-start.11) | collective-permute-done | bytes 213024 | tf_op jit(solution)/shard_map/ppermute | solution.py:340
  127.1 3.0 %shard_map.140 = (bf16[4,64,256]{2,1,0:T(8,128)(2,1)}, bf16[4,64,256]{2,1,0:T(8,128)(2,1)}, bf16[4,64,256]{2,1,0:T(8,128)(2,1)}, bf16[4,64,256]{2,1,0:T(8,128)(2,1)}) custom-call(s32[16]{0:T(128)} %get-tuple-element.33.refs_0_, bf16[13,64,128]{2,1,0:T(8,128)(2,1)} %copy-done.5, bf16[13,64,128]{2,1,0:T(8,128)(2,1)} %copy-done.8, bf16[1664,256]{1,0:T(8,128)(2,1)} %refs_3_.11, ...), custom_call_target="tpu_custom_call" | custom-call | bytes 10800000 | tf_op jit(solution)/shard_map/pallas_call | solution.py:24
  130.2 2.6 %collective-permute-start.19 = (bf16[4,64,256]{2,1,0:T(8,128)(2,1)}, bf16[4,64,256]{2,1,0:T(8,128)(2,1)S(1)}, u32[]{:S(2)}, u32[]{:S(2)}) collective-permute-start(bf16[4,64,256]{2,1,0:T(8,128)(2,1)} %get-tuple-element.30), channel_id=1, source_target_pairs={{0,4},{4,8},{8,12},{12,0},{1,5},{5,9},{9,13},{13,1},{2,6},{6,10},{... | collective-permute-start | bytes 393224 | tf_op jit(solution)/shard_map/ppermute | solution.py:316
  133.5 13.7 %collective-permute-done.19 = bf16[4,64,256]{2,1,0:T(8,128)(2,1)S(1)} collective-permute-done((bf16[4,64,256]{2,1,0:T(8,128)(2,1)}, bf16[4,64,256]{2,1,0:T(8,128)(2,1)S(1)}, u32[]{:S(2)}, u32[]{:S(2)}) %collective-permute-start.19) | collective-permute-done | bytes 131104 | tf_op jit(solution)/shard_map/ppermute | solution.py:316
  148.4 6.6 %collective-permute-done.20 = bf16[4,64,256]{2,1,0:T(8,128)(2,1)S(1)} collective-permute-done((bf16[4,64,256]{2,1,0:T(8,128)(2,1)}, bf16[4,64,256]{2,1,0:T(8,128)(2,1)S(1)}, u32[]{:S(2)}, u32[]{:S(2)}) %collective-permute-start.20) | collective-permute-done | bytes 131104 | tf_op jit(solution)/shard_map/ppermute | solution.py:316
  155.0 4.5 %collective-permute-done.21 = bf16[4,64,256]{2,1,0:T(8,128)(2,1)S(1)} collective-permute-done((bf16[4,64,256]{2,1,0:T(8,128)(2,1)}, bf16[4,64,256]{2,1,0:T(8,128)(2,1)S(1)}, u32[]{:S(2)}, u32[]{:S(2)}) %collective-permute-start.21) | collective-permute-done | bytes 131104 | tf_op jit(solution)/shard_map/ppermute | solution.py:316
  159.6 1.6 add_convert_fusion.5
  161.2 4.2 %shard_map.137 = (bf16[1664,256]{1,0:T(8,128)(2,1)}, bf16[128,256]{1,0:T(8,128)(2,1)}) custom-call(s32[13]{0:T(128)} %refs_0_.9, bf16[2,1664,256]{2,1,0:T(8,128)(2,1)} %get-tuple-element.21.refs_1_, bf16[2,1664,256]{2,1,0:T(8,128)(2,1)} %collective-permute-done.8.refs_2_, bf16[1664,256]{1,0:T(8,128)(2,1)} %collective-permute-done.9.refs_3_, ...), custom_call_target="tpu_custom_call" | custom-call | bytes 14400000 | tf_op jit(solution)/shard_map/pallas_call | solution.py:24
  165.3 3.0 %collective-permute-start.15 = (bf16[128,256]{1,0:T(8,128)(2,1)}, bf16[128,256]{1,0:T(8,128)(2,1)S(1)}, u32[]{:S(2)}, u32[]{:S(2)}) collective-permute-start(bf16[128,256]{1,0:T(8,128)(2,1)} %get-tuple-element.25.refs_1_), channel_id=1, source_target_pairs={{0,12},{4,0},{8,4},{12,8},{1,13},{5,1},{9,5},{13,9},{2,14},{6,2},{... | collective-permute-start | bytes 196616 | tf_op jit(solution)/shard_map/ppermute | solution.py:316
  169.2 2.0 %collective-permute-start.13 = (bf16[128,256]{1,0:T(8,128)(2,1)}, bf16[128,256]{1,0:T(8,128)(2,1)S(1)}, u32[]{:S(2)}, u32[]{:S(2)}) collective-permute-start(bf16[128,256]{1,0:T(8,128)(2,1)} %get-tuple-element.25.refs_1_), channel_id=1, source_target_pairs={{0,4},{4,8},{8,12},{12,0},{1,5},{5,9},{9,13},{13,1},{2,6},{6,10},{... | collective-permute-start | bytes 196616 | tf_op jit(solution)/shard_map/ppermute | solution.py:316
  171.2 3.0 %add_convert_fusion = bf16[4,64,2048]{2,1,0:T(8,128)(2,1)} fusion(bf16[4,64,2048]{2,1,0:T(8,128)(2,1)} %collective-permute-done.18, f32[4,64,2048]{2,1,0:T(8,128)S(1)} %get-tuple-element.35, bf16[4,64,2048]{2,1,0:T(8,128)(2,1)} %collective-permute-done.17), kind=kLoop, calls=%fused_computation | loop fusion | flops 2621440 | bytes 5242880 | tf_op jit(solution)/shard_map/convert_element_type | solution.py:426
  176.1 1.6 shard_map.138
  (88 shorter events, 16.7 us)
Async XLA Ops:
  2.0 9.0 %collective-permute-start.2 = (bf16[1,64,256]{2,1,0:T(8,128)(2,1)}, bf16[1,64,256]{2,1,0:T(8,128)(2,1)S(1)}, u32[]{:S(2)}, u32[]{:S(2)}) collective-permute-start(bf16[1,64,256]{2,1,0:T(8,128)(2,1)} %shard_map.130.refs_28_), channel_id=1, source_target_pairs={{0,12},{4,0},{8,4},{12,8},{1,13},{5,1},{9,5},{13,9},{2,14},{6,2},{... | collective-permute-start | bytes 98312 | tf_op jit(solution)/shard_map/ppermute | solution.py:316
  7.1 5.0 %collective-permute-start.1 = (bf16[1,64,256]{2,1,0:T(8,128)(2,1)}, bf16[1,64,256]{2,1,0:T(8,128)(2,1)S(1)}, u32[]{:S(2)}, u32[]{:S(2)}) collective-permute-start(bf16[1,64,256]{2,1,0:T(8,128)(2,1)} %shard_map.130.refs_28_), channel_id=1, source_target_pairs={{0,8},{4,12},{8,0},{12,4},{1,9},{5,13},{9,1},{13,5},{2,10},{6,14},... | collective-permute-start | bytes 98312 | tf_op jit(solution)/shard_map/ppermute | solution.py:316
  7.1 5.9 %collective-permute-start = (bf16[1,64,256]{2,1,0:T(8,128)(2,1)}, bf16[1,64,256]{2,1,0:T(8,128)(2,1)S(1)}, u32[]{:S(2)}, u32[]{:S(2)}) collective-permute-start(bf16[1,64,256]{2,1,0:T(8,128)(2,1)} %shard_map.130.refs_28_), channel_id=1, source_target_pairs={{0,4},{4,8},{8,12},{12,0},{1,5},{5,9},{9,13},{13,1},{2,6},{6,10},{... | collective-permute-start | bytes 98312 | tf_op jit(solution)/shard_map/ppermute | solution.py:316
  13.6 3.5 %copy-start.23 = (s32[13]{0:T(128)S(1)}, s32[13]{0:T(128)}, u32[]{:S(2)}) copy-start(s32[13]{0:T(128)} %param.12) | copy-start | bytes 160
  17.0 5.1 %copy-start.9 = (bf16[13,64,128]{2,1,0:T(8,128)(2,1)S(1)}, bf16[13,64,128]{2,1,0:T(8,128)(2,1)}, u32[]{:S(2)}) copy-start(bf16[13,64,128]{2,1,0:T(8,128)(2,1)} %get-tuple-element.18.refs_1_) | copy-start | bytes 638980
  17.0 5.1 %collective-permute-start.6 = (bf16[13,64,128]{2,1,0:T(8,128)(2,1)}, bf16[13,64,128]{2,1,0:T(8,128)(2,1)S(1)}, u32[]{:S(2)}, u32[]{:S(2)}) collective-permute-start(bf16[13,64,128]{2,1,0:T(8,128)(2,1)} %get-tuple-element.18.refs_1_), channel_id=1, source_target_pairs={{0,1},{1,0},{2,3},{3,2},{4,5},{5,4},{6,7},{7,6},{8,9},{9,8},{10,11... | collective-permute-start | bytes 638984 | tf_op jit(solution)/shard_map/ppermute | solution.py:335
  19.0 23.4 %collective-permute-start.5 = (bf16[1,64,2048]{2,1,0:T(8,128)(2,1)}, bf16[1,64,2048]{2,1,0:T(8,128)(2,1)S(1)}, u32[]{:S(2)}, u32[]{:S(2)}) collective-permute-start(bf16[1,64,2048]{2,1,0:T(8,128)(2,1)} %shard_map.132.refs_10_), channel_id=1, source_target_pairs={{0,12},{4,0},{8,4},{12,8},{1,13},{5,1},{9,5},{13,9},{2,14},{6,2},{... | collective-permute-start | bytes 786440 | tf_op jit(solution)/shard_map/ppermute | solution.py:316
  19.9 24.9 %collective-permute-start.4 = (bf16[1,64,2048]{2,1,0:T(8,128)(2,1)}, bf16[1,64,2048]{2,1,0:T(8,128)(2,1)S(1)}, u32[]{:S(2)}, u32[]{:S(2)}) collective-permute-start(bf16[1,64,2048]{2,1,0:T(8,128)(2,1)} %shard_map.132.refs_10_), channel_id=1, source_target_pairs={{0,8},{4,12},{8,0},{12,4},{1,9},{5,13},{9,1},{13,5},{2,10},{6,14},... | collective-permute-start | bytes 786440 | tf_op jit(solution)/shard_map/ppermute | solution.py:316
  21.0 23.7 %collective-permute-start.3 = (bf16[1,64,2048]{2,1,0:T(8,128)(2,1)}, bf16[1,64,2048]{2,1,0:T(8,128)(2,1)S(1)}, u32[]{:S(2)}, u32[]{:S(2)}) collective-permute-start(bf16[1,64,2048]{2,1,0:T(8,128)(2,1)} %shard_map.132.refs_10_), channel_id=1, source_target_pairs={{0,4},{4,8},{8,12},{12,0},{1,5},{5,9},{9,13},{13,1},{2,6},{6,10},{... | collective-permute-start | bytes 786440 | tf_op jit(solution)/shard_map/ppermute | solution.py:316
  22.2 6.9 %copy-start.4 = (bf16[13,64,128]{2,1,0:T(8,128)(2,1)}, bf16[13,64,128]{2,1,0:T(8,128)(2,1)S(1)}, u32[]{:S(2)}) copy-start(bf16[13,64,128]{2,1,0:T(8,128)(2,1)S(1)} %add_convert_fusion.4.refs_1_) | copy-start | bytes 638980
  22.2 6.9 %collective-permute-start.7 = (bf16[13,64,128]{2,1,0:T(8,128)(2,1)S(1)}, bf16[13,64,128]{2,1,0:T(8,128)(2,1)S(1)}, u32[]{:S(2)}, u32[]{:S(2)}) collective-permute-start(bf16[13,64,128]{2,1,0:T(8,128)(2,1)S(1)} %add_convert_fusion.4.refs_1_), channel_id=1, source_target_pairs={{0,2},{1,3},{2,0},{3,1},{4,6},{5,7},{6,4},{7,5},{8,10},{9,11},{10,... | collective-permute-start | bytes 638984 | tf_op jit(solution)/shard_map/ppermute | solution.py:340
  53.5 12.4 %copy-start.1 = (bf16[4,64,2048]{2,1,0:T(8,128)(2,1)S(1)}, bf16[4,64,2048]{2,1,0:T(8,128)(2,1)}, u32[]{:S(2)}) copy-start(bf16[4,64,2048]{2,1,0:T(8,128)(2,1)} %shard_map.133.refs_8_) | copy-start | bytes 3145732
  53.5 12.5 %copy-start.6 = (bf16[4,64,2048]{2,1,0:T(8,128)(2,1)S(1)}, bf16[4,64,2048]{2,1,0:T(8,128)(2,1)}, u32[]{:S(2)}) copy-start(bf16[4,64,2048]{2,1,0:T(8,128)(2,1)} %get-tuple-element.19.refs_14_) | copy-start | bytes 3145732
  53.5 14.1 %copy-start.10 = (bf16[13,64,128]{2,1,0:T(8,128)(2,1)S(1)}, bf16[13,64,128]{2,1,0:T(8,128)(2,1)}, u32[]{:S(2)}) copy-start(bf16[13,64,128]{2,1,0:T(8,128)(2,1)} %get-tuple-element.20.refs_6_) | copy-start | bytes 638980
  65.9 32.8 %collective-permute-start.8 = (bf16[2,1664,256]{2,1,0:T(8,128)(2,1)}, bf16[2,1664,256]{2,1,0:T(8,128)(2,1)}, u32[]{:S(2)}, u32[]{:S(2)}) collective-permute-start(bf16[2,1664,256]{2,1,0:T(8,128)(2,1)} %get-tuple-element.22), channel_id=1, source_target_pairs={{0,1},{1,0},{2,3},{3,2},{4,5},{5,4},{6,7},{7,6},{8,9},{9,8},{10,11... | collective-permute-start | bytes 5111816 | tf_op jit(solution)/shard_map/ppermute | solution.py:335
  65.9 25.6 %collective-permute-start.12 = (bf16[4,64,2048]{2,1,0:T(8,128)(2,1)S(1)}, bf16[4,64,2048]{2,1,0:T(8,128)(2,1)S(1)}, u32[]{:S(2)}, u32[]{:S(2)}) collective-permute-start(bf16[4,64,2048]{2,1,0:T(8,128)(2,1)S(1)} %copy-done.1), channel_id=1, source_target_pairs={{0,4},{12,8},{4,0},{8,12},{1,5},{13,9},{5,1},{9,13},{2,6},{14,10},... | collective-permute-start | bytes 3145736 | tf_op jit(solution)/shard_map/ppermute | solution.py:416
  66.0 29.6 %collective-permute-start.16 = (bf16[4,64,2048]{2,1,0:T(8,128)(2,1)S(1)}, bf16[4,64,2048]{2,1,0:T(8,128)(2,1)}, u32[]{:S(2)}, u32[]{:S(2)}) collective-permute-start(bf16[4,64,2048]{2,1,0:T(8,128)(2,1)S(1)} %copy-done.6), channel_id=1, source_target_pairs={{4,8},{8,4},{5,9},{9,5},{6,10},{10,6},{7,11},{11,7},{20,24},{24,20... | collective-permute-start | bytes 3145736 | tf_op jit(solution)/shard_map/ppermute | solution.py:418
  67.6 35.0 %collective-permute-start.10 = (bf16[13,64,128]{2,1,0:T(8,128)(2,1)S(1)}, bf16[13,64,128]{2,1,0:T(8,128)(2,1)}, u32[]{:S(2)}, u32[]{:S(2)}) collective-permute-start(bf16[13,64,128]{2,1,0:T(8,128)(2,1)S(1)} %copy-done.10), channel_id=1, source_target_pairs={{0,1},{1,0},{2,3},{3,2},{4,5},{5,4},{6,7},{7,6},{8,9},{9,8},{10,11... | collective-permute-start | bytes 638984 | tf_op jit(solution)/shard_map/ppermute | solution.py:335
  92.4 78.8 %collective-permute-start.18 = (bf16[4,64,2048]{2,1,0:T(8,128)(2,1)}, bf16[4,64,2048]{2,1,0:T(8,128)(2,1)}, u32[]{:S(2)}, u32[]{:S(2)}) collective-permute-start(bf16[4,64,2048]{2,1,0:T(8,128)(2,1)} %shard_map.139), channel_id=1, source_target_pairs={{0,4},{12,8},{1,5},{13,9},{2,6},{14,10},{3,7},{15,11},{16,20},{28,... | collective-permute-start | bytes 3145736 | tf_op jit(solution)/shard_map/ppermute | solution.py:421
  98.4 28.8 %copy-start = (bf16[4,64,2048]{2,1,0:T(8,128)(2,1)}, bf16[4,64,2048]{2,1,0:T(8,128)(2,1)S(1)}, u32[]{:S(2)}) copy-start(bf16[4,64,2048]{2,1,0:T(8,128)(2,1)S(1)} %get-tuple-element.36.refs_8_.refs_4_) | copy-start | bytes 3145732
  98.4 4.3 %copy-start.11 = (bf16[13,64,128]{2,1,0:T(8,128)(2,1)S(1)}, bf16[13,64,128]{2,1,0:T(8,128)(2,1)}, u32[]{:S(2)}) copy-start(bf16[13,64,128]{2,1,0:T(8,128)(2,1)} %get-tuple-element.20.refs_6_) | copy-start | bytes 638980
  98.4 72.8 %collective-permute-start.17 = (bf16[4,64,2048]{2,1,0:T(8,128)(2,1)S(1)}, bf16[4,64,2048]{2,1,0:T(8,128)(2,1)}, u32[]{:S(2)}, u32[]{:S(2)}) collective-permute-start(bf16[4,64,2048]{2,1,0:T(8,128)(2,1)S(1)} %get-tuple-element.36.refs_8_.refs_4_), channel_id=1, source_target_pairs={{0,8},{12,4},{4,12},{8,0},{1,9},{13,5},{5,13},{9,1},{2,10},{14,6},... | collective-permute-start | bytes 3145736 | tf_op jit(solution)/shard_map/ppermute | solution.py:420
  101.2 46.0 %copy-start.21 = (s32[4]{0:T(128)S(1)}, s32[4]{0:T(128)}, u32[]{:S(2)}) copy-start(s32[4]{0:T(128)} %param.11) | copy-start | bytes 52
  101.2 60.0 %collective-permute-start.9 = (bf16[1664,256]{1,0:T(8,128)(2,1)}, bf16[1664,256]{1,0:T(8,128)(2,1)}, u32[]{:S(2)}, u32[]{:S(2)}) collective-permute-start(bf16[1664,256]{1,0:T(8,128)(2,1)} %fusion), channel_id=1, source_target_pairs={{0,2},{1,3},{2,0},{3,1},{4,6},{5,7},{6,4},{7,5},{8,10},{9,11},{10,... | collective-permute-start | bytes 2555912 | tf_op jit(solution)/shard_map/ppermute | solution.py:340
  103.7 23.5 %copy-start.5 = (bf16[13,64,128]{2,1,0:T(8,128)(2,1)}, bf16[13,64,128]{2,1,0:T(8,128)(2,1)S(1)}, u32[]{:S(2)}) copy-start(bf16[13,64,128]{2,1,0:T(8,128)(2,1)S(1)} %add_convert_fusion.3.refs_4_.refs_1_) | copy-start | bytes 638980
  103.7 22.8 %collective-permute-start.11 = (bf16[13,64,128]{2,1,0:T(8,128)(2,1)S(1)}, bf16[13,64,128]{2,1,0:T(8,128)(2,1)S(1)}, u32[]{:S(2)}, u32[]{:S(2)}) collective-permute-start(bf16[13,64,128]{2,1,0:T(8,128)(2,1)S(1)} %add_convert_fusion.3.refs_4_.refs_1_), channel_id=1, source_target_pairs={{0,2},{1,3},{2,0},{3,1},{4,6},{5,7},{6,4},{7,5},{8,10},{9,11},{10,... | collective-permute-start | bytes 638984 | tf_op jit(solution)/shard_map/ppermute | solution.py:340
  130.2 17.0 %collective-permute-start.19 = (bf16[4,64,256]{2,1,0:T(8,128)(2,1)}, bf16[4,64,256]{2,1,0:T(8,128)(2,1)S(1)}, u32[]{:S(2)}, u32[]{:S(2)}) collective-permute-start(bf16[4,64,256]{2,1,0:T(8,128)(2,1)} %get-tuple-element.30), channel_id=1, source_target_pairs={{0,4},{4,8},{8,12},{12,0},{1,5},{5,9},{9,13},{13,1},{2,6},{6,10},{... | collective-permute-start | bytes 393224 | tf_op jit(solution)/shard_map/ppermute | solution.py:316
  132.8 22.2 %collective-permute-start.20 = (bf16[4,64,256]{2,1,0:T(8,128)(2,1)}, bf16[4,64,256]{2,1,0:T(8,128)(2,1)S(1)}, u32[]{:S(2)}, u32[]{:S(2)}) collective-permute-start(bf16[4,64,256]{2,1,0:T(8,128)(2,1)} %get-tuple-element.31), channel_id=1, source_target_pairs={{0,8},{4,12},{8,0},{12,4},{1,9},{5,13},{9,1},{13,5},{2,10},{6,14},... | collective-permute-start | bytes 393224 | tf_op jit(solution)/shard_map/ppermute | solution.py:316
  147.1 12.4 %collective-permute-start.21 = (bf16[4,64,256]{2,1,0:T(8,128)(2,1)}, bf16[4,64,256]{2,1,0:T(8,128)(2,1)S(1)}, u32[]{:S(2)}, u32[]{:S(2)}) collective-permute-start(bf16[4,64,256]{2,1,0:T(8,128)(2,1)} %get-tuple-element.32), channel_id=1, source_target_pairs={{0,12},{4,0},{8,4},{12,8},{1,13},{5,1},{9,5},{13,9},{2,14},{6,2},{... | collective-permute-start | bytes 393224 | tf_op jit(solution)/shard_map/ppermute | solution.py:316
  165.3 8.9 %collective-permute-start.15 = (bf16[128,256]{1,0:T(8,128)(2,1)}, bf16[128,256]{1,0:T(8,128)(2,1)S(1)}, u32[]{:S(2)}, u32[]{:S(2)}) collective-permute-start(bf16[128,256]{1,0:T(8,128)(2,1)} %get-tuple-element.25.refs_1_), channel_id=1, source_target_pairs={{0,12},{4,0},{8,4},{12,8},{1,13},{5,1},{9,5},{13,9},{2,14},{6,2},{... | collective-permute-start | bytes 196616 | tf_op jit(solution)/shard_map/ppermute | solution.py:316
  168.3 6.1 %collective-permute-start.14 = (bf16[128,256]{1,0:T(8,128)(2,1)}, bf16[128,256]{1,0:T(8,128)(2,1)S(1)}, u32[]{:S(2)}, u32[]{:S(2)}) collective-permute-start(bf16[128,256]{1,0:T(8,128)(2,1)} %get-tuple-element.25.refs_1_), channel_id=1, source_target_pairs={{0,8},{4,12},{8,0},{12,4},{1,9},{5,13},{9,1},{13,5},{2,10},{6,14},... | collective-permute-start | bytes 196616 | tf_op jit(solution)/shard_map/ppermute | solution.py:316
  169.2 6.3 %collective-permute-start.13 = (bf16[128,256]{1,0:T(8,128)(2,1)}, bf16[128,256]{1,0:T(8,128)(2,1)S(1)}, u32[]{:S(2)}, u32[]{:S(2)}) collective-permute-start(bf16[128,256]{1,0:T(8,128)(2,1)} %get-tuple-element.25.refs_1_), channel_id=1, source_target_pairs={{0,4},{4,8},{8,12},{12,0},{1,5},{5,9},{9,13},{13,1},{2,6},{6,10},{... | collective-permute-start | bytes 196616 | tf_op jit(solution)/shard_map/ppermute | solution.py:316
  (14 other events, 19.2 us)

commit v4 on v3

--- a/solution.py
+++ b/solution.py
@@ -32,7 +32,7 @@
         ),
         out_shape=[jax.ShapeDtypeStruct(shape, kind) for shape, kind, _ in outputs],
         input_output_aliases=aliases or {},
-        cost_estimate=pl.CostEstimate(flops=0, bytes_accessed=int(us * 3.6e6), transcendentals=0),
+        cost_estimate=pl.CostEstimate(flops=0, bytes_accessed=int(us * 3.6e5), transcendentals=0),
     )(*scalars, *[array for array, _ in inputs], *tokens)
 
 
@@ -54,7 +54,7 @@
     )[0]
 
 
-def own_last(maps, us, tokens=()):
+def own_last(maps, tokens=()):
     shape = (SW, *maps.shape[1:])
     last = maps.shape[0] - SW
 
@@ -68,7 +68,25 @@
         [(maps, pl.BlockSpec(shape, lambda i: (last, 0, 0)))],
         [(shape, maps.dtype, pl.BlockSpec(shape, lambda i: (0, 0, 0)))],
         tokens,
-        us,
+    )[0]
+
+
+def chosen(pick, choices, tokens=()):
+    def kernel(pick_ref, *refs):
+        for k, choice in enumerate(refs[:-1]):
+
+            @pl.when(pick_ref[0] == k)
+            def _():
+                refs[-1][...] = choice[...]
+
+    shape = choices[0].shape
+    return call(
+        kernel,
+        (pick,),
+        (1,),
+        [whole(choice) for choice in choices],
+        [(shape, choices[0].dtype, constant_spec(shape))],
+        tokens,
     )[0]
 
 
@@ -78,7 +96,55 @@
     return jnp.where(live, ranks, 0.0).astype(rows.dtype)
 
 
-def rank_terms(lengths, maps, pick, choices, features, each, us, tokens=()):
+def kept_ranks(lengths, maps, features):
+    blocks, rank, width = maps.shape
+    kept = blocks - SW
+
+    def kernel(lengths_ref, maps_ref, rows_ref, out_ref, last_ref):
+        last_ref[...] = maps_ref[kept:]
+        for k in range(kept):
+            out_ref[k] = masked_rank(maps_ref[k], rows_ref[k * BLOCK : (k + 1) * BLOCK], lengths_ref[k])
+
+    return call(
+        kernel,
+        (lengths,),
+        (1,),
+        [whole(maps), whole(features)],
+        [
+            ((kept, rank, BLOCK), features.dtype, constant_spec((kept, rank, BLOCK))),
+            ((SW, rank, width), features.dtype, constant_spec((SW, rank, width))),
+        ],
+    )
+
+
+def last_ranks(lengths, pick, choices, features):
+    shape = choices[0].shape
+    block = features.shape[0] // BLOCK - 1
+
+    def kernel(lengths_ref, pick_ref, *refs):
+        rows_ref, out_ref, chosen_ref = refs[-3:]
+        for k, choice in enumerate(refs[:-3]):
+
+            @pl.when(pick_ref[0] == k)
+            def _():
+                chosen_ref[...] = choice[...]
+
+        out_ref[0] = masked_rank(chosen_ref[0], rows_ref[...], lengths_ref[block])
+
+    return call(
+        kernel,
+        (lengths, pick),
+        (1,),
+        [whole(choice) for choice in choices]
+        + [(features, pl.BlockSpec((BLOCK, shape[2]), lambda i, *_: (block, 0), pipeline_mode=pl.Buffered(1)))],
+        [
+            ((1, shape[1], BLOCK), features.dtype, constant_spec((1, shape[1], BLOCK))),
+            (shape, features.dtype, constant_spec(shape)),
+        ],
+    )
+
+
+def rank_terms(lengths, maps, pick, choices, features, each, tokens=()):
     blocks, rank, width = maps.shape
     steps = pl.cdiv(blocks, each)
 
@@ -128,44 +194,58 @@
             (choices[0].shape, features.dtype, constant_spec(choices[0].shape)),
         ],
         tokens,
-        us,
-    )
-
-
-def summed(pair, at):
-    return (pair[0][at].astype(jnp.float32) + pair[1][at].astype(jnp.float32)).astype(pair[0].dtype)
-
-
-def down_rows(codes, first, parts, copies, ranks, features, us, tokens=()):
-    blocks, rank, _ = ranks[0].shape
+    )
+
+
+def summed(terms, at):
+    return sum(term[at].astype(jnp.float32) for term in terms).astype(terms[0].dtype)
+
+
+def down_rows(codes, first, parts, copies, ranks, last, features, tokens=()):
+    kept, rank, _ = ranks[0].shape
     width = features.shape[1]
+    piece = min(width, 512)
 
     def block_at(code):
         return jnp.maximum((code >> 1) - 1, 0)
 
     def kernel(codes_ref, a, b, *refs):
-        rows_refs, last_ref, outs, late = refs[:OWN], refs[OWN], refs[OWN + 1 : -1], refs[-1]
+        lasts, refs = refs[: len(last)], refs[len(last) :]
+        rows_refs, last_ref, outs = refs[:OWN], refs[OWN], refs[OWN + 1 :]
         step = pl.program_id(0)
 
-        @pl.when(step == 0)
-        def _():
-            late[...] = jnp.dot(summed((a, b), blocks - 1), last_ref[...], preferred_element_type=jnp.float32)
-
-        for k in range(OWN):
-            code = codes_ref[first + step * OWN + k]
-            mine = summed((a, b), block_at(code))
-            mine = jnp.where(code > 1, mine, jnp.zeros_like(mine))
-            total = jnp.dot(mine, rows_refs[k][...], preferred_element_type=jnp.float32)
-            total = total + jnp.where((code & 1) > 0, late[...], 0.0)
-            value = (ADAPTER_SCALE * total).astype(features.dtype)
-            for part, out_ref in enumerate(outs):
-                if len(outs) == 1:
-                    out_ref[k] = value
-                    continue
-
-                @pl.when(step == min(part, parts - 1))
+        def fill(to):
+            for k in range(OWN):
+                code = codes_ref[first + step * OWN + k]
+                mine = summed((a, b), block_at(code))
+                mine = jnp.where(code > 1, mine, jnp.zeros_like(mine))
+
+                def put(at, total):
+                    value = (ADAPTER_SCALE * total).astype(features.dtype)
+                    for out_ref in to:
+                        out_ref[k, :, at] = value
+
+                for at in [slice(c, c + piece) for c in range(0, width, piece)]:
+                    put(at, jnp.dot(mine, rows_refs[k][:, at], preferred_element_type=jnp.float32))
+
+                @pl.when((code & 1) > 0)
                 def _():
-                    out_ref[k] = value
+                    late = summed(lasts, 0)
+                    for at in [slice(c, c + piece) for c in range(0, width, piece)]:
+                        put(
+                            at,
+                            jnp.dot(mine, rows_refs[k][:, at], preferred_element_type=jnp.float32)
+                            + jnp.dot(late, last_ref[:, at], preferred_element_type=jnp.float32),
+                        )
+
+        if not copies or parts == 1:
+            fill(outs)
+        else:
+            for part in range(parts):
+
+                @pl.when(step == part)
+                def _():
+                    fill(outs[part:] if part == parts - 1 else outs[part : part + 1])
 
     def rows_spec(k):
         return pl.BlockSpec((BLOCK, width), lambda r, at: (block_at(at[first + r * OWN + k]), 0))
@@ -179,17 +259,15 @@
         kernel,
         (codes,),
         (parts,),
-        [whole(array) for array in ranks]
+        [whole(array) for array in (*ranks, *last)]
         + [(features, rows_spec(k)) for k in range(OWN)]
-        + [(features, pl.BlockSpec((BLOCK, width), lambda r, *_: (blocks - 1, 0), pipeline_mode=pl.Buffered(1)))],
+        + [(features, pl.BlockSpec((BLOCK, width), lambda r, *_: (kept, 0), pipeline_mode=pl.Buffered(1)))],
         outs,
         tokens,
-        us,
-        [pltpu.VMEM((rank, width), jnp.float32)],
-    )
-
-
-def up_rows(codes, parts, ranks, features, us, tokens=()):
+    )
+
+
+def up_rows(codes, parts, ranks, features, tokens=()):
     blocks, rank, _ = ranks[0].shape
     width = features.shape[1]
 
@@ -225,11 +303,10 @@
         [whole(array) for array in (*ranks, features)],
         [((rows, rank, width), features.dtype, constant_spec((rows, rank, width))) for rows in parts],
         tokens,
-        us,
-    )
-
-
-def base_terms(columns, hidden, weight, us, tokens=()):
+    )
+
+
+def base_terms(columns, hidden, weight, tokens=()):
     rows, depth = hidden.shape
     width = weight.shape[1] // 4
     tile = rows // 4
@@ -252,11 +329,10 @@
         + [(weight, column(k)) for k in range(4)],
         [((2, rows, width), hidden.dtype, pl.BlockSpec((2, tile, width), lambda i, *_: (0, i, 0)))] * 2,
         tokens,
-        us,
-    )
-
-
-def values_of(lengths, base, ranks, maps, last_map, us, tokens=()):
+    )
+
+
+def values_of(lengths, base, ranks, maps, last_map, tokens=()):
     _, rows, width = base[0].shape
     blocks = rows // BLOCK
 
@@ -285,11 +361,10 @@
             ((BLOCK, width), maps.dtype, constant_spec((BLOCK, width))),
         ],
         tokens,
-        us,
-    )
-
-
-def put_last(pick, values, choices, us):
+    )
+
+
+def put_last(pick, values, choices):
     width = values.shape[1]
     block = values.shape[0] // BLOCK - 1
 
@@ -306,7 +381,6 @@
         (1,),
         [whole(choice) for choice in choices] + [(values, ANYWHERE)],
         [(values.shape, values.dtype, pl.BlockSpec((BLOCK, width), lambda i, *_: (block, 0)))],
-        us=us,
         aliases={1 + len(choices): 0},
     )[0]
 
@@ -326,18 +400,47 @@
     return choices, ((me - source) % size).reshape(1)
 
 
+def routed(array, partner, tokens):
+    size = lax.axis_size("dp")
+    me = lax.axis_index("dp")
+    order = jnp.arange(size, dtype=jnp.int32)
+    holders = jnp.sum(jnp.where(partner[None, :] == order[:, None], order[None, :], 0), axis=1)
+    source = jnp.sum(jnp.where(partner == me, order, 0))
+    if size != 4:
+        return shifted(array, source)
+    from_left = lax.ppermute(array, "dp", [(0, 1), (1, 2)])
+    from_right = lax.ppermute(array, "dp", [(3, 2), (2, 1)])
+
+    def scalar(value):
+        return value.reshape(1).astype(jnp.int32)
+
+    def place(wanted):
+        return jnp.where(wanted == me, 0, jnp.where(wanted == me - 1, 1, jnp.where(wanted == me + 1, 2, 3)))
+
+    passed = chosen(scalar(jnp.where(me == 1, 0, 1)), [from_left, from_right], tokens[:1])
+    passed = lax.ppermute(passed, "dp", [(1, 2), (2, 1)])
+    choices = [array, from_left, from_right, passed]
+    outward = chosen(scalar(place(jnp.where(me == 1, holders[0], holders[3]))), choices, tokens[1:])
+    outward = lax.ppermute(outward, "dp", [(2, 3), (1, 0)])
+    inner = (me == 1) | (me == 2)
+    pick = jnp.where(inner | (source == me), place(source), 4)
+    return [*choices, outward], scalar(pick)
+
+
 def add(*arrays):
     return sum(array.astype(jnp.float32) for array in arrays).astype(arrays[0].dtype)
 
 
+def crossed(array, by):
+    return lax.ppermute(array, "tensor", [(i, i ^ by) for i in range(lax.axis_size("tensor"))])
+
+
 def near(array):
-    size = lax.axis_size("tensor")
-    return lax.ppermute(array, "tensor", [(i, i ^ 1) for i in range(size)])
+    return crossed(array, 1)
 
 
 def far(array):
-    size = lax.axis_size("tensor")
-    return lax.ppermute(array, "tensor", [(i, i ^ 2) for i in range(size)])
+    return crossed(array, 2)
 
 
 def exchanged(array):
@@ -388,12 +491,10 @@
     order = jnp.arange(devices, dtype=jnp.int32)
     holder = jnp.sum(jnp.where(partner == me, order, 0))
 
-    up_choices, up_pick = shifted(own_last(adapter_up_matrix, 1.0), holder)
-    cot_terms, up_last = rank_terms(
-        lengths, adapter_up_matrix, up_pick, up_choices, cotangent, blocks, 3.0
-    )
+    cot_terms, up_own = kept_ranks(lengths, adapter_up_matrix, cotangent)
     rank_cot = exchanged(cot_terms)
-    down_choices, down_pick = shifted(own_last(adapter_down_rows, 1.5, [cot_terms]), holder)
+    last_terms, up_last = last_ranks(lengths, *shifted(up_own, holder)[::-1], cotangent)
+    last_cot = [last_terms] + [crossed(last_terms, by) for by in range(1, lax.axis_size("tensor"))]
 
     table_rows = jnp.sum(
         jnp.where(
@@ -409,51 +510,52 @@
         rows = (owners[:, None] * OWN + jnp.arange(OWN, dtype=jnp.int32)[None, :]).reshape(-1)
         return jnp.sum(jnp.where(rows[:, None] == table_rows[None, :], weights[None, :], 0), axis=1)
 
+    columns = jnp.stack([column ^ 3, column ^ 1, column ^ 2, column]).astype(jnp.int32)
+
+    def base(token):
+        given, mine = base_terms(columns, hidden, frozen_value_weight, [token])
+        taken = near(given)
+        return mine, taken, far(add(mine[0], taken[0]))
+
+    down_own = own_last(adapter_down_rows, [rank_cot[0]])
     if line:
         inner = (me == 1) | (me == 2)
         codes = codes_of(jnp.array(ROLES, jnp.int32)[me])
-        (first,) = down_rows(codes, 0, 1, 1, rank_cot, hidden, 3.0)
+        (first,) = down_rows(codes, 0, 1, 1, rank_cot, last_cot, hidden)
         from_first = lax.ppermute(first, "dp", [(0, 1), (3, 2), (1, 0), (2, 3)])
-        second, own, third, third_too = down_rows(codes, OWN, 3, 2, rank_cot, hidden, 6.0, [first])
+        second, own, third, third_too = down_rows(codes, OWN, 3, 2, rank_cot, last_cot, hidden, [first])
         from_inner = lax.ppermute(third, "dp", [(1, 2), (2, 1)])
-        second = add(second, jnp.where(inner, from_first, jnp.zeros((), first.dtype)))
+        down_choices, down_pick = routed(down_own, partner, [first, third])
+        base_parts = base(third)
+        second = add(after(second, base_parts[0]), jnp.where(inner, from_first, jnp.zeros((), first.dtype)))
         from_second = lax.ppermute(second, "dp", [(0, 2), (3, 1), (1, 3), (2, 0)])
         from_third = lax.ppermute(after(third_too, from_first), "dp", [(0, 1), (3, 2)])
         near_total = lax.optimization_barrier(
-            own.astype(jnp.float32)
-            + jnp.where(inner, from_inner, from_first).astype(jnp.float32)
+            after(own, second).astype(jnp.float32) + jnp.where(inner, from_inner, from_first).astype(jnp.float32)
         )
         down_out = (near_total + from_second.astype(jnp.float32) + from_third.astype(jnp.float32)).astype(own.dtype)
-        start, window = third, second
+        window = second
     else:
         codes = codes_of(order)
-        (start,) = down_rows(codes, 0, devices, 0, rank_cot, hidden, 3.0)
-        down_out = line_reduce_scatter(start.reshape(devices, OWN, *start.shape[1:]))
-        window = start
-
-    in_terms, _ = rank_terms(
-        lengths, adapter_down_rows, down_pick, down_choices, hidden, 4, 6.0, [start]
-    )
+        (table,) = down_rows(codes, 0, devices, 0, rank_cot, last_cot, hidden)
+        down_out = line_reduce_scatter(table.reshape(devices, OWN, *table.shape[1:]))
+        down_choices, down_pick = routed(down_own, partner, [])
+        base_parts = base(table)
+        window = table
+
+    in_terms, _ = rank_terms(lengths, adapter_down_rows, down_pick, down_choices, hidden, 4, [window])
     rank_in = exchanged(in_terms)
-
-    columns = jnp.stack([column ^ 3, column ^ 1, column ^ 2, column]).astype(jnp.int32)
-    given, mine = base_terms(columns, hidden, frozen_value_weight, 10.0, [in_terms])
-    taken = near(given)
-    across = far(add(mine[0], taken[0]))
-
     if line:
         up_codes = codes_of((me + jnp.array([1, 2, 3, 0], jnp.int32)) % devices)
-        *sent, up_own = up_rows(up_codes, [OWN] * 4, rank_in, cotangent, 3.0, [window])
-        up_out = add(up_own, *[shift(array, by + 1) for by, array in enumerate(sent)])
+        *sent, up_kept = up_rows(up_codes, [OWN] * 4, rank_in, cotangent)
+        up_out = add(up_kept, *[shift(array, by + 1) for by, array in enumerate(sent)])
     else:
-        (up_table,) = up_rows(codes, [devices * OWN], rank_in, cotangent, 3.0)
+        (up_table,) = up_rows(codes, [devices * OWN], rank_in, cotangent)
         up_out = line_reduce_scatter(up_table.reshape(devices, OWN, *up_table.shape[1:]))
 
-    values, last_values = values_of(
-        lengths, (mine, taken, across), rank_in, adapter_up_matrix, up_last, 4.0, [window]
-    )
+    values, last_values = values_of(lengths, base_parts, rank_in, adapter_up_matrix, up_last)
     value_choices, value_pick = shifted(last_values, partner[me])
-    projected_values = put_last(value_pick, values, value_choices, 1.5)
+    projected_values = put_last(value_pick, values, value_choices)
     return (projected_values, down_out, up_out)
 
 

time: 178 us -> 193 us (1.084)
  starting transfers between devices: 27.7 us -> 63.1 us
  waiting for transfers between devices: 80 us -> 45.1 us
  Pallas kernels: 48.1 us -> 53.2 us
  between operations: 2.16 us -> 5.5 us
  other arithmetic: 14.6 us -> 17 us
    ppermute x12 -> x9, starting transfers between devices: 18.4 us -> 41.9 us  [shift(): lax.ppermute(array, 'dp', [(i, (i + by) % size) for i in range(size)])]
    ppermute x1, waiting for transfers between devices: 23.4 us -> 0.01 us  [body(): from_first = lax.ppermute(first, 'dp', [(0, 1), (3, 2), (1, 0), (2, 3)])]
    ppermute x6 -> x13, waiting for transfers between devices: 26.2 us -> 14.2 us  [the longest x1 10.2 us: routed(): outward = lax.ppermute(outward, 'dp', [(2, 3), (1, 0)])]
    ppermute x6 -> x13, starting transfers between devices: 4.14 us -> 12 us  [the longest x9 6.9 us: crossed(): lax.ppermute(array, 'tensor', [(i, i ^ by) for i in range(lax.axis_size('...]
    pallas_call x11 -> x15, Pallas kernels: 48.1 us -> 53.2 us  [call(): pl.pallas_call(run, grid_spec=pltpu.PrefetchScalarGridSpec(num_scalar_pre...]
    ppermute x1, starting transfers between devices: 0.07 us -> 2.48 us  [body(): from_first = lax.ppermute(first, 'dp', [(0, 1), (3, 2), (1, 0), (2, 3)])]
    unnamed x48 -> x56, local copies, waits for them, and re-layouts: 4.41 us -> 5.65 us
    convert_element_type x4 -> x5, other arithmetic: 5.19 us -> 6.34 us  [add(): sum((array.astype(jnp.float32) for array in arrays)).astype(arrays[0].dtype)]
  transfers between devices with their start and end apart: 22 -> 26, of which waited for: 11 -> 10; matrix products, arithmetic and copies ran while one was open for 9% -> 10% of each run, Pallas kernels for 12% -> 23%
where the time goes in v4:
time: 193 us; the launch traced here: 191 us
  starting transfers between devices  63.1 us (33%)
  Pallas kernels  53.2 us (28%)
  waiting for transfers between devices  45.1 us (23%)
  other arithmetic  17 us (9%)
  local copies, waits for them, and re-layouts  7.05 us (4%)
  between operations  5.5 us (3%)
    pallas_call x15, Pallas kernels, call(): pl.pallas_call(run, grid_spec=pltpu.PrefetchScalarGridSpec(num_scalar_pre...  53.2 us
    ppermute x9, starting transfers between devices, shift(): lax.ppermute(array, 'dp', [(i, (i + by) % size) for i in range(size)])  41.9 us
    ppermute x9, waiting for transfers between devices, shift(): lax.ppermute(array, 'dp', [(i, (i + by) % size) for i in range(size)])  30.9 us
    ppermute x1, waiting for transfers between devices, routed(): outward = lax.ppermute(outward, 'dp', [(2, 3), (1, 0)])  10.2 us
    ppermute x9, starting transfers between devices, crossed(): lax.ppermute(array, 'tensor', [(i, i ^ by) for i in range(lax.axis_size('...  6.9 us
    convert_element_type x5, other arithmetic, add(): sum((array.astype(jnp.float32) for array in arrays)).astype(arrays[0].dtype)  6.34 us
    unnamed x56, local copies, waits for them, and re-layouts  5.65 us
  transfers between devices with their start and end apart: 26, of which 10 were waited for; matrix products, arithmetic and copies ran while one was open for 10% of the time, Pallas kernels for 23%

profile of v4, /device:TPU:0, one launch (start us, length us, event | category | flops | bytes accessed | tf_op | source)
XLA Modules:
  0.0 190.9 jit_solution(1470901171352528816)
XLA Ops:
  0.6 3.0 %shard_map.130 = (bf16[12,64,128]{2,1,0:T(8,128)(2,1)}, bf16[1,64,256]{2,1,0:T(8,128)(2,1)}) custom-call(s32[13]{0:T(128)} %refs_0_.9, bf16[13,64,256]{2,1,0:T(8,128)(2,1)} %refs_6_.5, bf16[1664,256]{1,0:T(8,128)(2,1)} %refs_3_.5), custom_call_target="tpu_custom_call" | custom-call | bytes 360000 | tf_op jit(solution)/shard_map/pallas_call | solution.py:24
  3.6 5.1 %collective-permute-start.4 = (bf16[1,64,256]{2,1,0:T(8,128)(2,1)}, bf16[1,64,256]{2,1,0:T(8,128)(2,1)S(1)}, u32[]{:S(2)}, u32[]{:S(2)}) collective-permute-start(bf16[1,64,256]{2,1,0:T(8,128)(2,1)} %get-tuple-element.21.refs_2_), channel_id=1, source_target_pairs={{0,12},{4,0},{8,4},{12,8},{1,13},{5,1},{9,5},{13,9},{2,14},{6,2},{... | collective-permute-start | bytes 98312 | tf_op jit(solution)/shard_map/ppermute | solution.py:390
  13.7 1.6 collective-permute-start.1
  16.8 2.3 %shard_map.131 = (bf16[1,64,128]{2,1,0:T(8,128)(2,1)}, bf16[1,64,256]{2,1,0:T(8,128)(2,1)}) custom-call(s32[13]{0:T(128)} %refs_0_.9, s32[1]{0:T(128)} %bitcast.7.refs_1_, bf16[1,64,256]{2,1,0:T(8,128)(2,1)} %get-tuple-element.21.refs_2_, bf16[1,64,256]{2,1,0:T(8,128)(2,1)} %copy-done.24, bf16[1,64,256]{2,1,0:T(8,128)(2,1)} %copy-done.23, ...), custom_call_target="tpu_custom_call" | custom-call | bytes 360000 | tf_op jit(solution)/shard_map/pallas_call | solution.py:24
  19.5 1.5 collective-permute-start.6
  24.1 4.4 %shard_map.132.refs_12_.refs_3_ = bf16[4,64,2048]{2,1,0:T(8,128)(2,1)} custom-call(s32[16]{0:T(128)} %get-tuple-element.38.refs_0_, bf16[12,64,128]{2,1,0:T(8,128)(2,1)} %copy-done.6, bf16[12,64,128]{2,1,0:T(8,128)(2,1)} %copy-done.13, bf16[1,64,128]{2,1,0:T(8,128)(2,1)} %get-tuple-element.22.refs_3_, bf16[1,64,128]{2,1,0:T(8,128)(2,1)} %copy-done.18, ...), custom_call_target="tpu_custom_call" | custom-call | bytes 360000 | tf_op jit(solution)/shard_map/pallas_call | solution.py:24
  28.5 2.5 %collective-permute-start.14 = (bf16[4,64,2048]{2,1,0:T(8,128)(2,1)}, bf16[4,64,2048]{2,1,0:T(8,128)(2,1)S(1)}, u32[]{:S(2)}, u32[]{:S(2)}) collective-permute-start(bf16[4,64,2048]{2,1,0:T(8,128)(2,1)} %shard_map.132.refs_12_.refs_3_), channel_id=1, source_target_pairs={{0,4},{12,8},{4,0},{8,12},{1,5},{13,9},{5,1},{9,13},{2,6},{14,10},... | collective-permute-start | bytes 3145736 | tf_op jit(solution)/shard_map/ppermute | solution.py:525
  31.0 1.7 shard_map.135.refs_1_.refs_10_
  33.4 2.5 %collective-permute-start.10 = (bf16[1,64,2048]{2,1,0:T(8,128)(2,1)}, bf16[1,64,2048]{2,1,0:T(8,128)(2,1)S(1)}, u32[]{:S(2)}, u32[]{:S(2)}) collective-permute-start(bf16[1,64,2048]{2,1,0:T(8,128)(2,1)} %shard_map.135.refs_1_.refs_10_), channel_id=1, source_target_pairs={{0,4},{4,8},{1,5},{5,9},{2,6},{6,10},{3,7},{7,11},{16,20},{20,24},... | collective-permute-start | bytes 786440 | tf_op jit(solution)/shard_map/ppermute | solution.py:411
  36.5 8.7 %shard_map.133 = (bf16[4,64,2048]{2,1,0:T(8,128)(2,1)}, bf16[4,64,2048]{2,1,0:T(8,128)(2,1)}, bf16[4,64,2048]{2,1,0:T(8,128)(2,1)}, bf16[4,64,2048]{2,1,0:T(8,128)(2,1)}) custom-call(s32[16]{0:T(128)} %get-tuple-element.38.refs_0_, bf16[12,64,128]{2,1,0:T(8,128)(2,1)} %copy-done.6, bf16[12,64,128]{2,1,0:T(8,128)(2,1)} %copy-done.13, ...), custom_call_target="tpu_custom_call" | custom-call | bytes 360000 | tf_op jit(solution)/shard_map/pallas_call | solution.py:24
  45.2 12.3 %shard_map.134 = (bf16[2,1664,256]{2,1,0:T(8,128)(2,1)}, bf16[2,1664,256]{2,1,0:T(8,128)(2,1)}) custom-call(s32[4]{0:T(128)} %pad_add_fusion.refs_0_, bf16[1664,2048]{1,0:T(8,128)(2,1)} %refs_9_.5, bf16[2048,1024]{1,0:T(8,128)(2,1)} %refs_5_.2, bf16[2048,1024]{1,0:T(8,128)(2,1)} %refs_5_.2, bf16[2048,1024]{1,0:T(8,128)(2,1)} %refs_5_.2, ...), custom_call_target="tpu_custom_call" | custom-call | bytes 360000 | tf_op jit(solution)/shard_map/pallas_call | solution.py:24
  59.6 1.8 shard_map.136
  66.7 1.9 %shard_map.137 = bf16[1,64,2048]{2,1,0:T(8,128)(2,1)} custom-call(s32[1]{0:T(128)} %bitcast.13.refs_0_, bf16[1,64,2048]{2,1,0:T(8,128)(2,1)} %shard_map.135.refs_1_.refs_10_, bf16[1,64,2048]{2,1,0:T(8,128)(2,1)} %copy-done.8, bf16[1,64,2048]{2,1,0:T(8,128)(2,1)} %copy-done.7, bf16[1,64,2048]{2,1,0:T(8,128)(2,1)} %copy-done.10, ...), custom_call_target="tpu_custom_call" | custom-call | bytes 360000 | tf_op jit(solution)/shard_map/pallas_call | solution.py:24
  69.9 1.4 add_convert_fusion.1.refs_15_.refs_1_
  71.3 10.2 %collective-permute-done.13.refs_14_ = bf16[1,64,2048]{2,1,0:T(8,128)(2,1)S(1)} collective-permute-done((bf16[1,64,2048]{2,1,0:T(8,128)(2,1)}, bf16[1,64,2048]{2,1,0:T(8,128)(2,1)S(1)}, u32[]{:S(2)}, u32[]{:S(2)}) %collective-permute-start.13) | collective-permute-done | bytes 262176 | tf_op jit(solution)/shard_map/ppermute | solution.py:424
  82.2 8.2 %shard_map.139 = (bf16[13,64,128]{2,1,0:T(8,128)(2,1)}, bf16[1,64,2048]{2,1,0:T(8,128)(2,1)}) custom-call(s32[13]{0:T(128)} %refs_0_.9, s32[1]{0:T(128)} %bitcast.9.refs_1_, bf16[13,64,2048]{2,1,0:T(8,128)(2,1)} %refs_5_.3, bf16[13,64,2048]{2,1,0:T(8,128)(2,1)} %refs_5_.3, bf16[13,64,2048]{2,1,0:T(8,128)(2,1)} %refs_5_.3, bf16[13,64,2048]{2,1,0:T(8,128)(2,1)} %refs_5_.3, ...), custom_call_target="tpu_custom_call" | custom-call | bytes 360000 | tf_op jit(solution)/shard_map/pallas_call | solution.py:24
  90.4 1.7 collective-permute-start.20
  93.2 1.8 collective-permute-start.16
  96.2 3.6 %collective-permute-start.22 = (bf16[4,64,2048]{2,1,0:T(8,128)(2,1)}, bf16[4,64,2048]{2,1,0:T(8,128)(2,1)}, u32[]{:S(2)}, u32[]{:S(2)}) collective-permute-start(bf16[4,64,2048]{2,1,0:T(8,128)(2,1)} %shard_map.143), channel_id=1, source_target_pairs={{0,4},{12,8},{1,5},{13,9},{2,6},{14,10},{3,7},{15,11},{16,20},{28,... | collective-permute-start | bytes 3145736 | tf_op jit(solution)/shard_map/ppermute | solution.py:532
  101.6 3.0 %shard_map.144 = (bf16[4,64,256]{2,1,0:T(8,128)(2,1)}, bf16[4,64,256]{2,1,0:T(8,128)(2,1)}, bf16[4,64,256]{2,1,0:T(8,128)(2,1)}, bf16[4,64,256]{2,1,0:T(8,128)(2,1)}) custom-call(s32[16]{0:T(128)} %get-tuple-element.37.refs_0_, bf16[13,64,128]{2,1,0:T(8,128)(2,1)} %copy-done.9, bf16[13,64,128]{2,1,0:T(8,128)(2,1)} %copy-done.12, bf16[1664,256]{1,0:T(8,128)(2,1)} %refs_3_.5), custom_call_target="tpu_custom_call" | custom-call | bytes 360000 | tf_op jit(solution)/shard_map/pallas_call | solution.py:24
  104.7 2.3 %fusion = bf16[1664,256]{1,0:T(8,128)(2,1)} fusion(bf16[2,1664,256]{2,1,0:T(8,128)(2,1)} %collective-permute-done.8.refs_2_, bf16[2,1664,256]{2,1,0:T(8,128)(2,1)S(1)} %copy-done), kind=kLoop, calls=%fused_computation.4 | loop fusion | flops 1703936 | bytes 2555904 | tf_op jit(solution)/shard_map/convert_element_type | solution.py:431
  107.0 1.7 collective-permute-start.9
  110.0 30.6 %collective-permute-start.24 = (bf16[4,64,256]{2,1,0:T(8,128)(2,1)S(1)}, bf16[4,64,256]{2,1,0:T(8,128)(2,1)S(1)}, u32[]{:S(2)}, u32[]{:S(2)}) collective-permute-start(bf16[4,64,256]{2,1,0:T(8,128)(2,1)S(1)} %copy-done.27), channel_id=1, source_target_pairs={{0,8},{4,12},{8,0},{12,4},{1,9},{5,13},{9,1},{13,5},{2,10},{6,14},... | collective-permute-start | bytes 393224 | tf_op jit(solution)/shard_map/ppermute | solution.py:390
  140.7 6.4 %collective-permute-done.23 = bf16[4,64,256]{2,1,0:T(8,128)(2,1)S(1)} collective-permute-done((bf16[4,64,256]{2,1,0:T(8,128)(2,1)}, bf16[4,64,256]{2,1,0:T(8,128)(2,1)S(1)}, u32[]{:S(2)}, u32[]{:S(2)}) %collective-permute-start.23) | collective-permute-done | bytes 131104 | tf_op jit(solution)/shard_map/ppermute | solution.py:390
  147.1 3.1 %convert_add_fusion = f32[4,64,2048]{2,1,0:T(8,128)} fusion(bf16[4,64,2048]{2,1,0:T(8,128)(2,1)} %shard_map.142, bf16[4,64,2048]{2,1,0:T(8,128)(2,1)} %collective-permute-done.20, bf16[4,64,2048]{2,1,0:T(8,128)(2,1)S(1)} %copy-done.3, pred[]{:T(512)S(6)} %or.7), kind=kLoop, calls=%fused_computation.1 | loop fusion | flops 2097152 | bytes 5242881 | tf_op jit(solution)/shard_map/add | solution.py:534
  150.2 20.5 %collective-permute-done.24 = bf16[4,64,256]{2,1,0:T(8,128)(2,1)S(1)} collective-permute-done((bf16[4,64,256]{2,1,0:T(8,128)(2,1)S(1)}, bf16[4,64,256]{2,1,0:T(8,128)(2,1)S(1)}, u32[]{:S(2)}, u32[]{:S(2)}) %collective-permute-start.24) | collective-permute-done | bytes 131104 | tf_op jit(solution)/shard_map/ppermute | solution.py:390
  170.6 2.7 %collective-permute-done.25 = bf16[4,64,256]{2,1,0:T(8,128)(2,1)S(1)} collective-permute-done((bf16[4,64,256]{2,1,0:T(8,128)(2,1)S(1)}, bf16[4,64,256]{2,1,0:T(8,128)(2,1)S(1)}, u32[]{:S(2)}, u32[]{:S(2)}) %collective-permute-start.25) | collective-permute-done | bytes 131104 | tf_op jit(solution)/shard_map/ppermute | solution.py:390
  175.0 4.3 %shard_map.140 = (bf16[1664,256]{1,0:T(8,128)(2,1)}, bf16[128,256]{1,0:T(8,128)(2,1)}) custom-call(s32[13]{0:T(128)} %refs_0_.9, bf16[2,1664,256]{2,1,0:T(8,128)(2,1)} %get-tuple-element.24.refs_1_, bf16[2,1664,256]{2,1,0:T(8,128)(2,1)} %collective-permute-done.8.refs_2_, bf16[1664,256]{1,0:T(8,128)(2,1)} %copy-done.11, bf16[13,64,128]{2,1,0:T(8,128)(2,1)} %copy-done.9, ...), custom_call_target="tpu_custom_call" | custom-call | bytes 360000 | tf_op jit(solution)/shard_map/pallas_call | solution.py:24
  179.3 2.7 %collective-permute-start.19 = (bf16[128,256]{1,0:T(8,128)(2,1)}, bf16[128,256]{1,0:T(8,128)(2,1)S(1)}, u32[]{:S(2)}, u32[]{:S(2)}) collective-permute-start(bf16[128,256]{1,0:T(8,128)(2,1)} %get-tuple-element.29.refs_1_), channel_id=1, source_target_pairs={{0,12},{4,0},{8,4},{12,8},{1,13},{5,1},{9,5},{13,9},{2,14},{6,2},{... | collective-permute-start | bytes 196616 | tf_op jit(solution)/shard_map/ppermute | solution.py:390
  182.4 2.0 %collective-permute-start.17 = (bf16[128,256]{1,0:T(8,128)(2,1)}, bf16[128,256]{1,0:T(8,128)(2,1)S(1)}, u32[]{:S(2)}, u32[]{:S(2)}) collective-permute-start(bf16[128,256]{1,0:T(8,128)(2,1)} %get-tuple-element.29.refs_1_), channel_id=1, source_target_pairs={{0,4},{4,8},{8,12},{12,0},{1,5},{5,9},{9,13},{13,1},{2,6},{6,10},{... | collective-permute-start | bytes 196616 | tf_op jit(solution)/shard_map/ppermute | solution.py:390
  184.4 3.0 %add_convert_fusion = bf16[4,64,2048]{2,1,0:T(8,128)(2,1)} fusion(bf16[4,64,2048]{2,1,0:T(8,128)(2,1)} %collective-permute-done.22, f32[4,64,2048]{2,1,0:T(8,128)S(1)} %copy-done.4, bf16[4,64,2048]{2,1,0:T(8,128)(2,1)} %collective-permute-done.21), kind=kLoop, calls=%fused_computation | loop fusion | flops 2621440 | bytes 5242880 | tf_op jit(solution)/shard_map/convert_element_type | solution.py:536
  189.3 1.6 shard_map.141
  (111 shorter events, 25.5 us)
Async XLA Ops:
  3.6 12.5 %collective-permute-start.4 = (bf16[1,64,256]{2,1,0:T(8,128)(2,1)}, bf16[1,64,256]{2,1,0:T(8,128)(2,1)S(1)}, u32[]{:S(2)}, u32[]{:S(2)}) collective-permute-start(bf16[1,64,256]{2,1,0:T(8,128)(2,1)} %get-tuple-element.21.refs_2_), channel_id=1, source_target_pairs={{0,12},{4,0},{8,4},{12,8},{1,13},{5,1},{9,5},{13,9},{2,14},{6,2},{... | collective-permute-start | bytes 98312 | tf_op jit(solution)/shard_map/ppermute | solution.py:390
  8.7 7.4 %collective-permute-start.3 = (bf16[1,64,256]{2,1,0:T(8,128)(2,1)}, bf16[1,64,256]{2,1,0:T(8,128)(2,1)S(1)}, u32[]{:S(2)}, u32[]{:S(2)}) collective-permute-start(bf16[1,64,256]{2,1,0:T(8,128)(2,1)} %get-tuple-element.21.refs_2_), channel_id=1, source_target_pairs={{0,8},{4,12},{8,0},{12,4},{1,9},{5,13},{9,1},{13,5},{2,10},{6,14},... | collective-permute-start | bytes 98312 | tf_op jit(solution)/shard_map/ppermute | solution.py:390
  8.7 7.4 %collective-permute-start.2 = (bf16[1,64,256]{2,1,0:T(8,128)(2,1)}, bf16[1,64,256]{2,1,0:T(8,128)(2,1)S(1)}, u32[]{:S(2)}, u32[]{:S(2)}) collective-permute-start(bf16[1,64,256]{2,1,0:T(8,128)(2,1)} %get-tuple-element.21.refs_2_), channel_id=1, source_target_pairs={{0,4},{4,8},{8,12},{12,0},{1,5},{5,9},{9,13},{13,1},{2,6},{6,10},{... | collective-permute-start | bytes 98312 | tf_op jit(solution)/shard_map/ppermute | solution.py:390
  9.7 3.0 %collective-permute-start = (bf16[12,64,128]{2,1,0:T(8,128)(2,1)}, bf16[12,64,128]{2,1,0:T(8,128)(2,1)S(1)}, u32[]{:S(2)}, u32[]{:S(2)}) collective-permute-start(bf16[12,64,128]{2,1,0:T(8,128)(2,1)} %get-tuple-element.20), channel_id=1, source_target_pairs={{0,1},{1,0},{2,3},{3,2},{4,5},{5,4},{6,7},{7,6},{8,9},{9,8},{10,11... | collective-permute-start | bytes 589832 | tf_op jit(solution)/shard_map/ppermute | solution.py:435
  13.7 9.7 %collective-permute-start.1 = (bf16[12,64,128]{2,1,0:T(8,128)(2,1)S(1)}, bf16[12,64,128]{2,1,0:T(8,128)(2,1)S(1)}, u32[]{:S(2)}, u32[]{:S(2)}) collective-permute-start(bf16[12,64,128]{2,1,0:T(8,128)(2,1)S(1)} %add_convert_fusion.4.refs_1_), channel_id=1, source_target_pairs={{0,2},{1,3},{2,0},{3,1},{4,6},{5,7},{6,4},{7,5},{8,10},{9,11},{10,... | collective-permute-start | bytes 589832 | tf_op jit(solution)/shard_map/ppermute | solution.py:435
  19.1 3.4 %collective-permute-start.7 = (bf16[1,64,128]{2,1,0:T(8,128)(2,1)}, bf16[1,64,128]{2,1,0:T(8,128)(2,1)S(1)}, u32[]{:S(2)}, u32[]{:S(2)}) collective-permute-start(bf16[1,64,128]{2,1,0:T(8,128)(2,1)} %get-tuple-element.22.refs_3_), channel_id=1, source_target_pairs={{0,3},{1,2},{2,1},{3,0},{4,7},{5,6},{6,5},{7,4},{8,11},{9,10},{10,... | collective-permute-start | bytes 49160 | tf_op jit(solution)/shard_map/ppermute | solution.py:435
  19.5 3.9 %collective-permute-start.6 = (bf16[1,64,128]{2,1,0:T(8,128)(2,1)}, bf16[1,64,128]{2,1,0:T(8,128)(2,1)S(1)}, u32[]{:S(2)}, u32[]{:S(2)}) collective-permute-start(bf16[1,64,128]{2,1,0:T(8,128)(2,1)} %get-tuple-element.22.refs_3_), channel_id=1, source_target_pairs={{0,2},{1,3},{2,0},{3,1},{4,6},{5,7},{6,4},{7,5},{8,10},{9,11},{10,... | collective-permute-start | bytes 49160 | tf_op jit(solution)/shard_map/ppermute | solution.py:435
  21.0 2.5 %collective-permute-start.5 = (bf16[1,64,128]{2,1,0:T(8,128)(2,1)}, bf16[1,64,128]{2,1,0:T(8,128)(2,1)S(1)}, u32[]{:S(2)}, u32[]{:S(2)}) collective-permute-start(bf16[1,64,128]{2,1,0:T(8,128)(2,1)} %get-tuple-element.22.refs_3_), channel_id=1, source_target_pairs={{0,1},{1,0},{2,3},{3,2},{4,5},{5,4},{6,7},{7,6},{8,9},{9,8},{10,11... | collective-permute-start | bytes 49160 | tf_op jit(solution)/shard_map/ppermute | solution.py:435
  28.5 41.4 %collective-permute-start.14 = (bf16[4,64,2048]{2,1,0:T(8,128)(2,1)}, bf16[4,64,2048]{2,1,0:T(8,128)(2,1)S(1)}, u32[]{:S(2)}, u32[]{:S(2)}) collective-permute-start(bf16[4,64,2048]{2,1,0:T(8,128)(2,1)} %shard_map.132.refs_12_.refs_3_), channel_id=1, source_target_pairs={{0,4},{12,8},{4,0},{8,12},{1,5},{13,9},{5,1},{9,13},{2,6},{14,10},... | collective-permute-start | bytes 3145736 | tf_op jit(solution)/shard_map/ppermute | solution.py:525
  32.7 24.9 %collective-permute-start.11 = (bf16[1,64,2048]{2,1,0:T(8,128)(2,1)}, bf16[1,64,2048]{2,1,0:T(8,128)(2,1)S(1)}, u32[]{:S(2)}, u32[]{:S(2)}) collective-permute-start(bf16[1,64,2048]{2,1,0:T(8,128)(2,1)} %shard_map.135.refs_1_.refs_10_), channel_id=1, source_target_pairs={{12,8},{8,4},{13,9},{9,5},{14,10},{10,6},{15,11},{11,7},{28,24},{2... | collective-permute-start | bytes 786440 | tf_op jit(solution)/shard_map/ppermute | solution.py:412
  33.4 25.5 %collective-permute-start.10 = (bf16[1,64,2048]{2,1,0:T(8,128)(2,1)}, bf16[1,64,2048]{2,1,0:T(8,128)(2,1)S(1)}, u32[]{:S(2)}, u32[]{:S(2)}) collective-permute-start(bf16[1,64,2048]{2,1,0:T(8,128)(2,1)} %shard_map.135.refs_1_.refs_10_), channel_id=1, source_target_pairs={{0,4},{4,8},{1,5},{5,9},{2,6},{6,10},{3,7},{7,11},{16,20},{20,24},... | collective-permute-start | bytes 786440 | tf_op jit(solution)/shard_map/ppermute | solution.py:411
  45.2 16.8 %copy-start.25 = (s32[4]{0:T(128)S(1)}, s32[4]{0:T(128)}, u32[]{:S(2)}) copy-start(s32[4]{0:T(128)} %param.11) | copy-start | bytes 52
  57.5 47.1 %collective-permute-start.8 = (bf16[2,1664,256]{2,1,0:T(8,128)(2,1)}, bf16[2,1664,256]{2,1,0:T(8,128)(2,1)}, u32[]{:S(2)}, u32[]{:S(2)}) collective-permute-start(bf16[2,1664,256]{2,1,0:T(8,128)(2,1)} %get-tuple-element.25), channel_id=1, source_target_pairs={{0,1},{1,0},{2,3},{3,2},{4,5},{5,4},{6,7},{7,6},{8,9},{9,8},{10,11... | collective-permute-start | bytes 5111816 | tf_op jit(solution)/shard_map/ppermute | solution.py:435
  61.3 4.6 %collective-permute-start.12 = (bf16[1,64,2048]{2,1,0:T(8,128)(2,1)}, bf16[1,64,2048]{2,1,0:T(8,128)(2,1)S(1)}, u32[]{:S(2)}, u32[]{:S(2)}) collective-permute-start(bf16[1,64,2048]{2,1,0:T(8,128)(2,1)} %shard_map.136), channel_id=1, source_target_pairs={{4,8},{8,4},{5,9},{9,5},{6,10},{10,6},{7,11},{11,7},{20,24},{24,20... | collective-permute-start | bytes 786440 | tf_op jit(solution)/shard_map/ppermute | solution.py:421
  68.6 12.9 %collective-permute-start.13 = (bf16[1,64,2048]{2,1,0:T(8,128)(2,1)}, bf16[1,64,2048]{2,1,0:T(8,128)(2,1)S(1)}, u32[]{:S(2)}, u32[]{:S(2)}) collective-permute-start(bf16[1,64,2048]{2,1,0:T(8,128)(2,1)} %shard_map.137), channel_id=1, source_target_pairs={{8,12},{4,0},{9,13},{5,1},{10,14},{6,2},{11,15},{7,3},{24,28},{20,... | collective-permute-start | bytes 786440 | tf_op jit(solution)/shard_map/ppermute | solution.py:424
  69.9 11.6 %copy-start.2 = (bf16[4,64,2048]{2,1,0:T(8,128)(2,1)}, bf16[4,64,2048]{2,1,0:T(8,128)(2,1)S(1)}, u32[]{:S(2)}) copy-start(bf16[4,64,2048]{2,1,0:T(8,128)(2,1)S(1)} %collective-permute-done.14.refs_1_) | copy-start | bytes 3145732
  82.2 12.7 %copy-start.1 = (bf16[4,64,2048]{2,1,0:T(8,128)(2,1)S(1)}, bf16[4,64,2048]{2,1,0:T(8,128)(2,1)}, u32[]{:S(2)}) copy-start(bf16[4,64,2048]{2,1,0:T(8,128)(2,1)} %add_convert_fusion.1.refs_15_.refs_1_) | copy-start | bytes 3145732
  90.4 1.8 collective-permute-start.15
  90.4 19.6 %collective-permute-start.20 = (bf16[4,64,2048]{2,1,0:T(8,128)(2,1)}, bf16[4,64,2048]{2,1,0:T(8,128)(2,1)}, u32[]{:S(2)}, u32[]{:S(2)}) collective-permute-start(bf16[4,64,2048]{2,1,0:T(8,128)(2,1)} %get-tuple-element.23.refs_6_.refs_5_), channel_id=1, source_target_pairs={{4,8},{8,4},{5,9},{9,5},{6,10},{10,6},{7,11},{11,7},{20,24},{24,20... | collective-permute-start | bytes 3145736 | tf_op jit(solution)/shard_map/ppermute | solution.py:527
  93.2 7.7 %collective-permute-start.16 = (bf16[13,64,128]{2,1,0:T(8,128)(2,1)S(1)}, bf16[13,64,128]{2,1,0:T(8,128)(2,1)S(1)}, u32[]{:S(2)}, u32[]{:S(2)}) collective-permute-start(bf16[13,64,128]{2,1,0:T(8,128)(2,1)S(1)} %add_convert_fusion.3.refs_4_.refs_1_), channel_id=1, source_target_pairs={{0,2},{1,3},{2,0},{3,1},{4,6},{5,7},{6,4},{7,5},{8,10},{9,11},{10,... | collective-permute-start | bytes 638984 | tf_op jit(solution)/shard_map/ppermute | solution.py:435
  94.9 89.5 %collective-permute-start.21 = (bf16[4,64,2048]{2,1,0:T(8,128)(2,1)S(1)}, bf16[4,64,2048]{2,1,0:T(8,128)(2,1)}, u32[]{:S(2)}, u32[]{:S(2)}) collective-permute-start(bf16[4,64,2048]{2,1,0:T(8,128)(2,1)S(1)} %copy-done.1), channel_id=1, source_target_pairs={{0,8},{12,4},{4,12},{8,0},{1,9},{13,5},{5,13},{9,1},{2,10},{14,6},... | collective-permute-start | bytes 3145736 | tf_op jit(solution)/shard_map/ppermute | solution.py:531
  96.2 88.1 %collective-permute-start.22 = (bf16[4,64,2048]{2,1,0:T(8,128)(2,1)}, bf16[4,64,2048]{2,1,0:T(8,128)(2,1)}, u32[]{:S(2)}, u32[]{:S(2)}) collective-permute-start(bf16[4,64,2048]{2,1,0:T(8,128)(2,1)} %shard_map.143), channel_id=1, source_target_pairs={{0,4},{12,8},{1,5},{13,9},{2,6},{14,10},{3,7},{15,11},{16,20},{28,... | collective-permute-start | bytes 3145736 | tf_op jit(solution)/shard_map/ppermute | solution.py:532
  104.6 42.5 %collective-permute-start.23 = (bf16[4,64,256]{2,1,0:T(8,128)(2,1)}, bf16[4,64,256]{2,1,0:T(8,128)(2,1)S(1)}, u32[]{:S(2)}, u32[]{:S(2)}) collective-permute-start(bf16[4,64,256]{2,1,0:T(8,128)(2,1)} %get-tuple-element.34), channel_id=1, source_target_pairs={{0,4},{4,8},{8,12},{12,0},{1,5},{5,9},{9,13},{13,1},{2,6},{6,10},{... | collective-permute-start | bytes 393224 | tf_op jit(solution)/shard_map/ppermute | solution.py:390
  107.0 40.1 %copy-start.26 = (bf16[4,64,256]{2,1,0:T(8,128)(2,1)S(1)}, bf16[4,64,256]{2,1,0:T(8,128)(2,1)}, u32[]{:S(2)}) copy-start(bf16[4,64,256]{2,1,0:T(8,128)(2,1)} %get-tuple-element.36) | copy-start | bytes 393220
  107.0 40.1 %copy-start.3 = (bf16[4,64,2048]{2,1,0:T(8,128)(2,1)S(1)}, bf16[4,64,2048]{2,1,0:T(8,128)(2,1)}, u32[]{:S(2)}) copy-start(bf16[4,64,2048]{2,1,0:T(8,128)(2,1)} %copy-done.2) | copy-start | bytes 3145732
  107.0 67.1 %collective-permute-start.9 = (bf16[1664,256]{1,0:T(8,128)(2,1)}, bf16[1664,256]{1,0:T(8,128)(2,1)S(1)}, u32[]{:S(2)}, u32[]{:S(2)}) collective-permute-start(bf16[1664,256]{1,0:T(8,128)(2,1)} %fusion), channel_id=1, source_target_pairs={{0,2},{1,3},{2,0},{3,1},{4,6},{5,7},{6,4},{7,5},{8,10},{9,11},{10,... | collective-permute-start | bytes 2555912 | tf_op jit(solution)/shard_map/ppermute | solution.py:435
  110.0 60.6 %collective-permute-start.24 = (bf16[4,64,256]{2,1,0:T(8,128)(2,1)S(1)}, bf16[4,64,256]{2,1,0:T(8,128)(2,1)S(1)}, u32[]{:S(2)}, u32[]{:S(2)}) collective-permute-start(bf16[4,64,256]{2,1,0:T(8,128)(2,1)S(1)} %copy-done.27), channel_id=1, source_target_pairs={{0,8},{4,12},{8,0},{12,4},{1,9},{5,13},{9,1},{13,5},{2,10},{6,14},... | collective-permute-start | bytes 393224 | tf_op jit(solution)/shard_map/ppermute | solution.py:390
  147.0 26.3 %copy-start.15 = (bf16[4,64,256]{2,1,0:T(8,128)(2,1)S(1)}, bf16[4,64,256]{2,1,0:T(8,128)(2,1)}, u32[]{:S(2)}) copy-start(bf16[4,64,256]{2,1,0:T(8,128)(2,1)} %get-tuple-element.33) | copy-start | bytes 393220
  147.0 26.3 %collective-permute-start.25 = (bf16[4,64,256]{2,1,0:T(8,128)(2,1)S(1)}, bf16[4,64,256]{2,1,0:T(8,128)(2,1)S(1)}, u32[]{:S(2)}, u32[]{:S(2)}) collective-permute-start(bf16[4,64,256]{2,1,0:T(8,128)(2,1)S(1)} %copy-done.26), channel_id=1, source_target_pairs={{0,12},{4,0},{8,4},{12,8},{1,13},{5,1},{9,5},{13,9},{2,14},{6,2},{... | collective-permute-start | bytes 393224 | tf_op jit(solution)/shard_map/ppermute | solution.py:390
  179.3 8.1 %collective-permute-start.19 = (bf16[128,256]{1,0:T(8,128)(2,1)}, bf16[128,256]{1,0:T(8,128)(2,1)S(1)}, u32[]{:S(2)}, u32[]{:S(2)}) collective-permute-start(bf16[128,256]{1,0:T(8,128)(2,1)} %get-tuple-element.29.refs_1_), channel_id=1, source_target_pairs={{0,12},{4,0},{8,4},{12,8},{1,13},{5,1},{9,5},{13,9},{2,14},{6,2},{... | collective-permute-start | bytes 196616 | tf_op jit(solution)/shard_map/ppermute | solution.py:390
  181.9 6.1 %collective-permute-start.18 = (bf16[128,256]{1,0:T(8,128)(2,1)}, bf16[128,256]{1,0:T(8,128)(2,1)S(1)}, u32[]{:S(2)}, u32[]{:S(2)}) collective-permute-start(bf16[128,256]{1,0:T(8,128)(2,1)} %get-tuple-element.29.refs_1_), channel_id=1, source_target_pairs={{0,8},{4,12},{8,0},{12,4},{1,9},{5,13},{9,1},{13,5},{2,10},{6,14},... | collective-permute-start | bytes 196616 | tf_op jit(solution)/shard_map/ppermute | solution.py:390
  182.4 6.3 %collective-permute-start.17 = (bf16[128,256]{1,0:T(8,128)(2,1)}, bf16[128,256]{1,0:T(8,128)(2,1)S(1)}, u32[]{:S(2)}, u32[]{:S(2)}) collective-permute-start(bf16[128,256]{1,0:T(8,128)(2,1)} %get-tuple-element.29.refs_1_), channel_id=1, source_target_pairs={{0,4},{4,8},{8,12},{12,0},{1,5},{5,9},{9,13},{13,1},{2,6},{6,10},{... | collective-permute-start | bytes 196616 | tf_op jit(solution)/shard_map/ppermute | solution.py:390
  (22 other events, 54.7 us)

commit v5 on v4

v5 whole, which is shorter than its diff:
```python
import jax
import jax.numpy as jnp
from jax import lax
from jax.experimental import pallas as pl
from jax.experimental.pallas import tpu as pltpu
from jax.sharding import PartitionSpec as P

BLOCK = 128
SW = 1
OWN = 4


ADAPTER_SCALE = 0.5

ANYWHERE = pl.BlockSpec(memory_space=pl.ANY)
ROW_PRODUCT = (((1,), (1,)), ((), ()))


def call(kernel, scalars, grid, inputs, outputs, tokens=(), us=1.0, scratch=(), aliases=None):
    def run(*refs):
        cut = len(scalars) + len(inputs)
        return kernel(*refs[:cut], *refs[cut + len(tokens) :])

    return pl.pallas_call(
        run,
        grid_spec=pltpu.PrefetchScalarGridSpec(
            num_scalar_prefetch=len(scalars),
            grid=grid,
            in_specs=[spec for _, spec in inputs] + [ANYWHERE] * len(tokens),
            out_specs=[spec for _, _, spec in outputs],
            scratch_shapes=scratch,
        ),
        out_shape=[jax.ShapeDtypeStruct(shape, kind) for shape, kind, _ in outputs],
        input_output_aliases=aliases or {},
        cost_estimate=pl.CostEstimate(flops=int(us * 1e9), bytes_accessed=int(us * 3.6e5), transcendentals=0),
    )(*scalars, *[array for array, _ in inputs], *tokens)


def constant_spec(shape):
    return pl.BlockSpec(shape, lambda *_: (0,) * len(shape), pipeline_mode=pl.Buffered(1))


def whole(array):
    return (array, constant_spec(array.shape))


def nothing(*refs):
    pass


def after(array, *tokens):
    return call(
        nothing, (), (1,), [(array, ANYWHERE)], [(array.shape, array.dtype, ANYWHERE)], tokens, 0.1, aliases={0: 0}
    )[0]


def masked_rank(adapter, rows, length):
    ranks = lax.dot_general(adapter, rows, ROW_PRODUCT, preferred_element_type=jnp.float32)
    live = lax.broadcasted_iota(jnp.int32, ranks.shape, 1) < length
    return jnp.where(live, ranks, 0.0).astype(rows.dtype)


def kept_ranks(lengths, maps, features, others):
    blocks, rank, width = maps.shape
    kept = blocks - SW
    last_shapes = [(SW, rank, width), (SW, *others.shape[1:])]

    def kernel(lengths_ref, maps_ref, rows_ref, others_ref, out_ref, last_ref, last_other):
        last_ref[...] = maps_ref[kept:]
        last_other[...] = others_ref[...]
        for k in range(kept):
            out_ref[k] = masked_rank(maps_ref[k], rows_ref[k * BLOCK : (k + 1) * BLOCK], lengths_ref[k])

    return call(
        kernel,
        (lengths,),
        (1,),
        [
            whole(maps),
            whole(features),
            (others, pl.BlockSpec(last_shapes[1], lambda i, *_: (kept, 0, 0), pipeline_mode=pl.Buffered(1))),
        ],
        [((kept, rank, BLOCK), features.dtype, constant_spec((kept, rank, BLOCK)))]
        + [(shape, features.dtype, constant_spec(shape)) for shape in last_shapes],
    )


def streamed_ranks(lengths, maps, features, each, tokens=()):
    blocks, rank, width = maps.shape
    kept = blocks - SW

    def kernel(lengths_ref, *refs):
        step = pl.program_id(0)
        for k in range(each):
            refs[-1][k] = masked_rank(refs[k][0], refs[each + k][...], lengths_ref[step * each + k])

    return call(
        kernel,
        (lengths,),
        (kept // each,),
        [(maps, pl.BlockSpec((1, rank, width), lambda i, *_, k=k: (i * each + k, 0, 0))) for k in range(each)]
        + [(features, pl.BlockSpec((BLOCK, width), lambda i, *_, k=k: (i * each + k, 0))) for k in range(each)],
        [((kept, rank, BLOCK), features.dtype, pl.BlockSpec((each, rank, BLOCK), lambda i, *_: (i, 0, 0)))],
        tokens,
    )[0]


def last_ranks(lengths, pick, choices, features, tokens=()):
    shape = choices[0].shape
    block = features.shape[0] // BLOCK - 1

    def kernel(lengths_ref, pick_ref, *refs):
        rows_ref, out_ref, chosen_ref = refs[-3:]
        for k, choice in enumerate(refs[:-3]):

            @pl.when(pick_ref[0] == k)
            def _():
                chosen_ref[...] = choice[...]

        out_ref[0] = masked_rank(chosen_ref[0], rows_ref[...], lengths_ref[block])

    return call(
        kernel,
        (lengths, pick),
        (1,),
        [whole(choice) for choice in choices]
        + [(features, pl.BlockSpec((BLOCK, shape[2]), lambda i, *_: (block, 0), pipeline_mode=pl.Buffered(1)))],
        [
            ((1, shape[1], BLOCK), features.dtype, constant_spec((1, shape[1], BLOCK))),
            (shape, features.dtype, constant_spec(shape)),
        ],
        tokens,
    )


def summed(terms, at):
    return sum(term[at].astype(jnp.float32) for term in terms).astype(terms[0].dtype)


def down_rows(codes, first, parts, copies, ranks, last, features, tokens=(), us=1.0):
    kept, rank, _ = ranks[0].shape
    width = features.shape[1]
    piece = min(width, 512)

    def block_at(code):
        return jnp.maximum((code >> 1) - 1, 0)

    def kernel(codes_ref, a, b, *refs):
        lasts, refs = refs[: len(last)], refs[len(last) :]
        rows_refs, last_ref, outs = refs[:OWN], refs[OWN], refs[OWN + 1 :]
        step = pl.program_id(0)

        def fill(to):
            for k in range(OWN):
                code = codes_ref[first + step * OWN + k]
                mine = summed((a, b), block_at(code))
                mine = jnp.where(code > 1, mine, jnp.zeros_like(mine))

                def put(at, total):
                    value = (ADAPTER_SCALE * total).astype(features.dtype)
                    for out_ref in to:
                        out_ref[k, :, at] = value

                for at in [slice(c, c + piece) for c in range(0, width, piece)]:
                    put(at, jnp.dot(mine, rows_refs[k][:, at], preferred_element_type=jnp.float32))

                @pl.when((code & 1) > 0)
                def _():
                    late = summed(lasts, 0)
                    for at in [slice(c, c + piece) for c in range(0, width, piece)]:
                        put(
                            at,
                            jnp.dot(mine, rows_refs[k][:, at], preferred_element_type=jnp.float32)
                            + jnp.dot(late, last_ref[:, at], preferred_element_type=jnp.float32),
                        )

        if not copies or parts == 1:
            fill(outs)
        else:
            for part in range(parts):

                @pl.when(step == part)
                def _():
                    fill(outs[part:] if part == parts - 1 else outs[part : part + 1])

    def rows_spec(k):
        return pl.BlockSpec((BLOCK, width), lambda r, at: (block_at(at[first + r * OWN + k]), 0))

    shape = (OWN, rank, width)
    if copies:
        outs = [(shape, features.dtype, constant_spec(shape))] * (parts - 1 + copies)
    else:
        outs = [((parts * OWN, rank, width), features.dtype, pl.BlockSpec(shape, lambda r, *_: (r, 0, 0)))]
    return call(
        kernel,
        (codes,),
        (parts,),
        [whole(array) for array in (*ranks, *last)]
        + [(features, rows_spec(k)) for k in range(OWN)]
        + [(features, pl.BlockSpec((BLOCK, width), lambda r, *_: (kept, 0), pipeline_mode=pl.Buffered(1)))],
        outs,
        tokens,
        us,
    )


def outputs_of(lengths, codes, parts, base, ranks, last, features, maps, last_map):
    rows, width = base[0].shape
    blocks = rows // BLOCK
    rank = maps.shape[1]

    def kernel(lengths_ref, codes_ref, one, two, three, *refs):
        terms, refs = refs[: len(ranks)], refs[len(ranks) :]
        lasts, refs = refs[: len(last)], refs[len(last) :]
        rows_ref, maps_ref, last_ref, out_ref, *outs = refs
        late = summed(lasts, 0)
        for k in range(blocks):
            at = slice(k * BLOCK, (k + 1) * BLOCK)
            adapter = maps_ref[k] if k < blocks - 1 else last_ref[0]
            added = lax.dot_general(
                summed(terms, k) if k < blocks - 1 else late,
                adapter,
                (((0,), (0,)), ((), ())),
                preferred_element_type=jnp.float32,
            )
            frozen = one[at].astype(jnp.float32) + two[at].astype(jnp.float32) + three[at].astype(jnp.float32)
            live = lax.broadcasted_iota(jnp.int32, frozen.shape, 0) < lengths_ref[k]
            values = jnp.where(live, frozen + ADAPTER_SCALE * added, 0.0).astype(out_ref.dtype)
            out_ref[at] = values
            if k == blocks - 1:
                for count, out in zip(parts, outs):
                    out[count * rank :] = values
        late_rows = jnp.dot(late, rows_ref[(blocks - 1) * BLOCK :], preferred_element_type=jnp.float32)
        done = 0
        for count, out in zip(parts, outs):

            def one_row(r, carry, out=out, done=done):
                code = codes_ref[done + r]
                at = jnp.maximum((code >> 1) - 1, 0)
                mine = summed(terms, at)
                mine = jnp.where(code > 1, mine, jnp.zeros_like(mine))
                mine_rows = rows_ref[pl.ds(pl.multiple_of(at * BLOCK, BLOCK), BLOCK), :]
                total = jnp.dot(mine, mine_rows, preferred_element_type=jnp.float32)
                total = total + jnp.where((code & 1) > 0, late_rows, 0.0)
                to = r * rank if isinstance(r, int) else pl.ds(pl.multiple_of(r * rank, rank), rank)
                to = slice(to, to + rank) if isinstance(r, int) else to
                out[to] = (ADAPTER_SCALE * total).astype(out.dtype)
                return carry

            if count <= OWN:
                for r in range(count):
                    one_row(r, 0)
            else:
                lax.fori_loop(0, count, one_row, 0)
            done += count

    return call(
        kernel,
        (lengths, codes),
        (1,),
        [whole(array) for array in (*base, *ranks, *last, features, maps, last_map)],
        [((rows, width), maps.dtype, constant_spec((rows, width)))]
        + [
            ((count * rank + BLOCK, width), maps.dtype, constant_spec((count * rank + BLOCK, width)))
            for count in parts
        ],
    )


def finish(pick, values, own, arrived):
    width = values.shape[1]
    block = values.shape[0] // BLOCK - 1
    rows = own.shape[0] - BLOCK

    def kernel(pick_ref, *refs):
        choices, table_ref, last_ref = refs[:-3], refs[-2], refs[-1]
        table_ref[...] = sum(choice[:rows].astype(jnp.float32) for choice in choices).astype(own.dtype)
        for k, choice in enumerate(choices):

            @pl.when(pick_ref[0] == k)
            def _():
                last_ref[...] = choice[rows:]

    return call(
        kernel,
        (pick,),
        (1,),
        [whole(choice) for choice in (own, *arrived)] + [(values, ANYWHERE)],
        [
            ((rows, width), own.dtype, constant_spec((rows, width))),
            (values.shape, values.dtype, pl.BlockSpec((BLOCK, width), lambda i, *_: (block, 0))),
        ],
        aliases={2 + len(arrived): 1},
    )


def base_terms(columns, hidden, weight, tokens=()):
    rows, depth = hidden.shape
    width = weight.shape[1] // 4
    tile = rows // 4

    def kernel(columns_ref, rows_ref, *refs):
        for k in range(4):
            out_ref = refs[4 + k]
            out_ref[...] = jnp.dot(rows_ref[...], refs[k][...], preferred_element_type=jnp.float32).astype(out_ref.dtype)

    def column(k):
        return pl.BlockSpec((depth, width), lambda i, at: (0, at[k]), pipeline_mode=pl.Buffered(1))

    return call(
        kernel,
        (columns,),
        (rows // tile,),
        [(hidden, pl.BlockSpec((tile, depth), lambda i, *_: (i, 0)))]
        + [(weight, column(k)) for k in range(4)],
        [((rows, width), hidden.dtype, pl.BlockSpec((tile, width), lambda i, *_: (i, 0)))] * 4,
        tokens,
        100.0,
    )


def shift(array, by):
    size = lax.axis_size("dp")
    return lax.ppermute(array, "dp", [(i, (i + by) % size) for i in range(size)])


def shifted(array, source):
    size = lax.axis_size("dp")
    me = lax.axis_index("dp")
    if size > 4:
        taken = lax.dynamic_index_in_dim(lax.all_gather(array, "dp"), source, 0, keepdims=False)
        return [taken], jnp.zeros((1,), jnp.int32)
    choices = [array] + [shift(array, by) for by in range(1, size)]
    return choices, ((me - source) % size).reshape(1)


def add(*arrays):
    return sum(array.astype(jnp.float32) for array in arrays).astype(arrays[0].dtype)


def crossed(array, by):
    return lax.ppermute(array, "tensor", [(i, i ^ by) for i in range(lax.axis_size("tensor"))])


def near(array):
    return crossed(array, 1)


def far(array):
    return crossed(array, 2)


def exchanged(array):
    array = add(array, near(array))
    return array, far(array)


def spread(array):
    return [array] + [crossed(array, by) for by in range(1, lax.axis_size("tensor"))]


def line_reduce_scatter(table):
    size = lax.axis_size("dp")
    me = lax.axis_index("dp")

    def entry(index):
        return lax.dynamic_index_in_dim(table, jnp.clip(index, 0, size - 1), 0, keepdims=False)

    from_left = from_right = None
    for step in range(size - 1):
        right = entry(size - 1 - step + me)
        left = entry(step - (size - 1 - me))
        if step > 0:
            right = add(right, from_left)
            left = add(left, from_right)
        from_left = lax.ppermute(right, "dp", [(i, i + 1) for i in range(step + 1)])
        from_right = lax.ppermute(left, "dp", [(i, i - 1) for i in range(size - 1 - step, size)])
    return entry(me) if size == 1 else add(entry(me), from_left, from_right)


ROLES = ((3, 1, 2, 0), (0, 2, 3, 1), (3, 1, 0, 2), (0, 2, 1, 3))


def body(
    partner,
    block_tenant_index,
    block_live_length,
    tenant_table_row,
    hidden,
    cotangent,
    frozen_value_weight,
    adapter_down_rows,
    adapter_up_matrix,
):
    blocks = block_tenant_index.shape[0]
    kept = blocks - SW
    devices = lax.axis_size("dp")
    me = lax.axis_index("dp")
    column = lax.axis_index("tensor")
    lengths = block_live_length
    line = devices == 4
    order = jnp.arange(devices, dtype=jnp.int32)
    holder = jnp.sum(jnp.where(partner == me, order, 0))

    cot_terms, up_own, down_own = kept_ranks(lengths, adapter_up_matrix, cotangent, adapter_down_rows)
    rank_cot = exchanged(cot_terms)
    up_choices, up_pick = shifted(up_own, holder)
    last_terms, up_last = last_ranks(lengths, up_pick, up_choices, cotangent, [rank_cot[1]])
    last_cot = spread(last_terms)
    down_choices, down_pick = shifted(down_own, holder)

    table_rows = jnp.sum(
        jnp.where(
            block_tenant_index[:, None] == jnp.arange(tenant_table_row.shape[0], dtype=jnp.int32)[None, :],
            tenant_table_row[None, :],
            0,
        ),
        axis=1,
    )
    weights = jnp.where(jnp.arange(blocks) < kept, 2 * (jnp.arange(blocks, dtype=jnp.int32) + 1), 1)

    def codes_of(owners):
        rows = (owners[:, None] * OWN + jnp.arange(OWN, dtype=jnp.int32)[None, :]).reshape(-1)
        return jnp.sum(jnp.where(rows[:, None] == table_rows[None, :], weights[None, :], 0), axis=1)

    columns = jnp.stack([column ^ 3, column ^ 2, column ^ 1, column]).astype(jnp.int32)

    def base(*tokens):
        return base_terms(columns, hidden, frozen_value_weight, tokens)

    def base_parts(terms, *tokens):
        sent, away, given, mine = terms
        away = add(after(away, *tokens), near(sent))
        return (mine, near(given), far(away)), away

    def last_in(token):
        terms, _ = last_ranks(lengths, down_pick, down_choices, hidden, [token])
        return spread(terms)

    def inputs(*tokens):
        return spread(streamed_ranks(lengths, adapter_down_rows, hidden, 4, tokens))

    def outputs(codes, parts, base_sums, rank_in, last):
        return outputs_of(
            lengths, codes, parts, base_sums, rank_in, last, cotangent, adapter_up_matrix, up_last
        )

    if line:
        inner = (me == 1) | (me == 2)
        codes = codes_of(jnp.array(ROLES, jnp.int32)[me])
        first, third, third_too = down_rows(codes, 0, 2, 2, rank_cot, last_cot, hidden)
        from_first = lax.ppermute(first, "dp", [(0, 1), (3, 2), (1, 0), (2, 3)])
        from_inner = lax.ppermute(third, "dp", [(1, 2), (2, 1)])
        last = last_in(first)
        second, own = down_rows(codes, 2 * OWN, 2, 1, rank_cot, last_cot, hidden, [last[0]], 100.0)
        terms = base(second)
        second = add(
            after(second, terms[0], from_inner), jnp.where(inner, from_first, jnp.zeros((), first.dtype))
        )
        from_second = lax.ppermute(second, "dp", [(0, 2), (3, 1), (1, 3), (2, 0)])
        from_third = lax.ppermute(after(third_too, from_first), "dp", [(0, 1), (3, 2)])
        near_total = lax.optimization_barrier(
            after(own, second).astype(jnp.float32) + jnp.where(inner, from_inner, from_first).astype(jnp.float32)
        )
        down_out = (near_total + from_second.astype(jnp.float32) + from_third.astype(jnp.float32)).astype(own.dtype)

        up_codes = codes_of((me + jnp.array([1, 2, 3, 0], jnp.int32)) % devices)
        parts, away = base_parts(terms, second)
        values, *sent, kept_here = outputs(up_codes, [OWN] * 4, parts, inputs(away), last)
        arrived = [shift(array, by + 1) for by, array in enumerate(sent)]
        value_pick = ((me - partner[me]) % devices).reshape(1)
        up_out, values = finish(value_pick, values, kept_here, arrived)
    else:
        codes = codes_of(order)
        (table,) = down_rows(codes, 0, devices, 0, rank_cot, last_cot, hidden)
        down_out = line_reduce_scatter(table.reshape(devices, OWN, *table.shape[1:]))
        parts, _ = base_parts(base(table))
        values, table = outputs(codes, [devices * OWN], parts, inputs(table), last_in(table))
        up_table, last_values = table[:-BLOCK], table[-BLOCK:]
        up_out = line_reduce_scatter(up_table.reshape(devices, OWN, -1, values.shape[1]))
        (last_values,), _ = shifted(last_values, partner[me])
        values = jnp.concatenate([values[: kept * BLOCK], last_values], axis=0)
    return (values, down_out, up_out.reshape(OWN, -1, values.shape[1]))


def solution(mesh):
    in_specs = (
        P("groups"),
        P(("groups", "dp")),
        P(("groups", "dp")),
        P("groups"),
        P(("groups", "dp"), "tensor"),
        P(("groups", "dp"), "tensor"),
        P("tensor", None),
        P(("groups", "dp"), None, "tensor"),
        P(("groups", "dp"), None, "tensor"),
    )
    out_specs = (
        P(("groups", "dp"), "tensor"),
        P(("groups", "dp"), None, "tensor"),
        P(("groups", "dp"), None, "tensor"),
    )
    return jax.shard_map(body, mesh=mesh, in_specs=in_specs, out_specs=out_specs, check_vma=False)
```

time: 193 us -> 132 us (0.68)
  starting transfers between devices: 63.1 us -> 31.8 us
  waiting for transfers between devices: 45.1 us -> 31.1 us
  Pallas kernels: 53.2 us -> 47.3 us
  other arithmetic: 17 us -> 13 us
  between operations: 5.5 us -> 2.13 us
    ppermute x9, starting transfers between devices: 41.9 us -> 14.7 us  [shift(): lax.ppermute(array, 'dp', [(i, (i + by) % size) for i in range(size)])]
    ppermute x9, waiting for transfers between devices: 30.9 us -> 9.96 us  [shift(): lax.ppermute(array, 'dp', [(i, (i + by) % size) for i in range(size)])]
    ppermute x9 -> x14, waiting for transfers between devices: 2.68 us -> 19.9 us  [crossed(): lax.ppermute(array, 'tensor', [(i, i ^ by) for i in range(lax.axis_size('...]
    ppermute x4 -> x0, waiting for transfers between devices: 11.5 us -> none  [the longest x1 10.2 us: routed(): outward = lax.ppermute(outward, 'dp', [(2, 3), (1, 0)])]
    pallas_call x15 -> x13, Pallas kernels: 53.2 us -> 47.3 us  [call(): pl.pallas_call(run, grid_spec=pltpu.PrefetchScalarGridSpec(num_scalar_pre...]
    ppermute x4 -> x0, starting transfers between devices: 5.15 us -> none  [the longest x1 2.54 us: routed(): from_left = lax.ppermute(array, 'dp', [(0, 1), (1, 2)])]
    convert_element_type x5 -> x3, other arithmetic: 6.34 us -> 4.87 us  [add(): sum((array.astype(jnp.float32) for array in arrays)).astype(arrays[0].dtype)]
    ppermute x9 -> x14, starting transfers between devices: 6.9 us -> 7.99 us  [crossed(): lax.ppermute(array, 'tensor', [(i, i ^ by) for i in range(lax.axis_size('...]
  transfers between devices with their start and end apart: 26 -> 27, of which waited for: 10 -> 9; matrix products, arithmetic and copies ran while one was open for 10% -> 11% of each run, Pallas kernels for 23% -> 32%
where the time goes in v5:
time: 132 us; the launch traced here: 131 us
  Pallas kernels  47.3 us (36%)
  starting transfers between devices  31.8 us (24%)
  waiting for transfers between devices  31.1 us (24%)
  other arithmetic  13 us (10%)
  local copies, waits for them, and re-layouts  5.23 us (4%)
  between operations  2.13 us (2%)
    pallas_call x13, Pallas kernels, call(): pl.pallas_call(run, grid_spec=pltpu.PrefetchScalarGridSpec(num_scalar_pre...  47.3 us
    ppermute x14, waiting for transfers between devices, crossed(): lax.ppermute(array, 'tensor', [(i, i ^ by) for i in range(lax.axis_size('...  19.9 us
    ppermute x9, starting transfers between devices, shift(): lax.ppermute(array, 'dp', [(i, (i + by) % size) for i in range(size)])  14.7 us
    ppermute x9, waiting for transfers between devices, shift(): lax.ppermute(array, 'dp', [(i, (i + by) % size) for i in range(size)])  9.96 us
    ppermute x14, starting transfers between devices, crossed(): lax.ppermute(array, 'tensor', [(i, i ^ by) for i in range(lax.axis_size('...  7.99 us
    convert_element_type x3, other arithmetic, add(): sum((array.astype(jnp.float32) for array in arrays)).astype(arrays[0].dtype)  4.87 us
    ppermute x1, starting transfers between devices, body(): lax.ppermute(after(third_too, from_first), 'dp', [(0, 1), (3, 2)])  4.46 us
    unnamed x56, local copies, waits for them, and re-layouts  4.42 us
  transfers between devices with their start and end apart: 27, of which 9 were waited for; matrix products, arithmetic and copies ran while one was open for 11% of the time, Pallas kernels for 32%

profile of v5, /device:TPU:0, one launch (start us, length us, event | category | flops | bytes accessed | tf_op | source)
XLA Modules:
  0.0 130.6 jit_solution(14993734496523237022)
XLA Ops:
  0.7 3.2 %shard_map.130 = (bf16[12,64,128]{2,1,0:T(8,128)(2,1)}, bf16[1,64,256]{2,1,0:T(8,128)(2,1)}, bf16[1,64,2048]{2,1,0:T(8,128)(2,1)}) custom-call(s32[13]{0:T(128)} %refs_0_.9, bf16[13,64,256]{2,1,0:T(8,128)(2,1)} %refs_14_.1, bf16[1664,256]{1,0:T(8,128)(2,1)} %refs_13_.1, bf16[13,64,2048]{2,1,0:T(8,128)(2,1)} %refs_4_.3), custom_call_target="tpu_custom_call" | custom-call | flops 1000000000 | bytes 360000 | tf_op jit(solution)/shard_map/pallas_call | solution.py:24
  3.9 3.0 %collective-permute-start.2 = (bf16[1,64,256]{2,1,0:T(8,128)(2,1)}, bf16[1,64,256]{2,1,0:T(8,128)(2,1)S(1)}, u32[]{:S(2)}, u32[]{:S(2)}) collective-permute-start(bf16[1,64,256]{2,1,0:T(8,128)(2,1)} %get-tuple-element.26.refs_2_), channel_id=1, source_target_pairs={{0,4},{4,8},{8,12},{12,0},{1,5},{5,9},{9,13},{13,1},{2,6},{6,10},{... | collective-permute-start | bytes 98312 | tf_op jit(solution)/shard_map/ppermute | solution.py:324
  6.9 2.6 %collective-permute-start.3 = (bf16[1,64,256]{2,1,0:T(8,128)(2,1)}, bf16[1,64,256]{2,1,0:T(8,128)(2,1)S(1)}, u32[]{:S(2)}, u32[]{:S(2)}) collective-permute-start(bf16[1,64,256]{2,1,0:T(8,128)(2,1)} %get-tuple-element.26.refs_2_), channel_id=1, source_target_pairs={{0,8},{4,12},{8,0},{12,4},{1,9},{5,13},{9,1},{13,5},{2,10},{6,14},... | collective-permute-start | bytes 98312 | tf_op jit(solution)/shard_map/ppermute | solution.py:324
  9.5 1.3 %collective-permute-start.4 = (bf16[1,64,256]{2,1,0:T(8,128)(2,1)}, bf16[1,64,256]{2,1,0:T(8,128)(2,1)S(1)}, u32[]{:S(2)}, u32[]{:S(2)}) collective-permute-start(bf16[1,64,256]{2,1,0:T(8,128)(2,1)} %get-tuple-element.26.refs_2_), channel_id=1, source_target_pairs={{0,12},{4,0},{8,4},{12,8},{1,13},{5,1},{9,5},{13,9},{2,14},{6,2},{... | collective-permute-start | bytes 98312 | tf_op jit(solution)/shard_map/ppermute | solution.py:324
  14.0 1.6 %collective-permute-start.1 = (bf16[12,64,128]{2,1,0:T(8,128)(2,1)S(1)}, bf16[12,64,128]{2,1,0:T(8,128)(2,1)S(1)}, u32[]{:S(2)}, u32[]{:S(2)}) collective-permute-start(bf16[12,64,128]{2,1,0:T(8,128)(2,1)S(1)} %add_convert_fusion.3.refs_1_), channel_id=1, source_target_pairs={{0,2},{1,3},{2,0},{3,1},{4,6},{5,7},{6,4},{7,5},{8,10},{9,11},{10,... | collective-permute-start | bytes 589832 | tf_op jit(solution)/shard_map/ppermute | solution.py:342
  16.9 2.9 %collective-permute-start.10 = (bf16[1,64,2048]{2,1,0:T(8,128)(2,1)}, bf16[1,64,2048]{2,1,0:T(8,128)(2,1)S(1)}, u32[]{:S(2)}, u32[]{:S(2)}) collective-permute-start(bf16[1,64,2048]{2,1,0:T(8,128)(2,1)} %get-tuple-element.28.refs_2_), channel_id=1, source_target_pairs={{0,12},{4,0},{8,4},{12,8},{1,13},{5,1},{9,5},{13,9},{2,14},{6,2},{... | collective-permute-start | bytes 786440 | tf_op jit(solution)/shard_map/ppermute | solution.py:324
  19.8 1.3 %collective-permute-done.1.refs_7_.refs_2_ = bf16[12,64,128]{2,1,0:T(8,128)(2,1)S(1)} collective-permute-done((bf16[12,64,128]{2,1,0:T(8,128)(2,1)S(1)}, bf16[12,64,128]{2,1,0:T(8,128)(2,1)S(1)}, u32[]{:S(2)}, u32[]{:S(2)}) %collective-permute-start.1) | collective-permute-done | bytes 196640 | tf_op jit(solution)/shard_map/ppermute | solution.py:342
  21.8 2.3 %shard_map.131 = (bf16[1,64,128]{2,1,0:T(8,128)(2,1)}, bf16[1,64,256]{2,1,0:T(8,128)(2,1)}) custom-call(s32[13]{0:T(128)} %refs_0_.9, s32[1]{0:T(128)} %bitcast.7.refs_1_, bf16[1,64,256]{2,1,0:T(8,128)(2,1)} %get-tuple-element.26.refs_2_, bf16[1,64,256]{2,1,0:T(8,128)(2,1)} %copy-done.23, bf16[1,64,256]{2,1,0:T(8,128)(2,1)} %copy-done.24, ...), custom_call_target="tpu_custom_call" | custom-call | flops 1000000000 | bytes 360000 | tf_op jit(solution)/shard_map/pallas_call | solution.py:24
  24.9 1.5 %collective-permute-start.6 = (bf16[1,64,128]{2,1,0:T(8,128)(2,1)}, bf16[1,64,128]{2,1,0:T(8,128)(2,1)S(1)}, u32[]{:S(2)}, u32[]{:S(2)}) collective-permute-start(bf16[1,64,128]{2,1,0:T(8,128)(2,1)} %get-tuple-element.27.refs_3_), channel_id=1, source_target_pairs={{0,2},{1,3},{2,0},{3,1},{4,6},{5,7},{6,4},{7,5},{8,10},{9,11},{10,... | collective-permute-start | bytes 49160 | tf_op jit(solution)/shard_map/ppermute | solution.py:342
  27.4 1.4 %collective-permute-done.6.refs_5_ = bf16[1,64,128]{2,1,0:T(8,128)(2,1)S(1)} collective-permute-done((bf16[1,64,128]{2,1,0:T(8,128)(2,1)}, bf16[1,64,128]{2,1,0:T(8,128)(2,1)S(1)}, u32[]{:S(2)}, u32[]{:S(2)}) %collective-permute-start.6) | collective-permute-done | bytes 16416 | tf_op jit(solution)/shard_map/ppermute | solution.py:342
  30.3 7.0 %shard_map.132 = (bf16[4,64,2048]{2,1,0:T(8,128)(2,1)}, bf16[4,64,2048]{2,1,0:T(8,128)(2,1)}, bf16[4,64,2048]{2,1,0:T(8,128)(2,1)}) custom-call(s32[16]{0:T(128)} %get-tuple-element.47.refs_0_, bf16[12,64,128]{2,1,0:T(8,128)(2,1)} %copy-done.4, bf16[12,64,128]{2,1,0:T(8,128)(2,1)} %copy-done.8, bf16[1,64,128]{2,1,0:T(8,128)(2,1)} %get-tuple-element.27.refs_3_, ...), custom_call_target="tpu_custom_call" | custom-call | flops 1000000000 | bytes 360000 | tf_op jit(solution)/shard_map/pallas_call | solution.py:24
  37.4 1.7 %collective-permute-start.12 = (bf16[4,64,2048]{2,1,0:T(8,128)(2,1)}, bf16[4,64,2048]{2,1,0:T(8,128)(2,1)}, u32[]{:S(2)}, u32[]{:S(2)}) collective-permute-start(bf16[4,64,2048]{2,1,0:T(8,128)(2,1)} %get-tuple-element.36), channel_id=1, source_target_pairs={{4,8},{8,4},{5,9},{9,5},{6,10},{10,6},{7,11},{11,7},{20,24},{24,20... | collective-permute-start | bytes 3145736 | tf_op jit(solution)/shard_map/ppermute | solution.py:453
  39.0 1.3 %collective-permute-start.13 = (bf16[4,64,2048]{2,1,0:T(8,128)(2,1)}, bf16[4,64,2048]{2,1,0:T(8,128)(2,1)}, u32[]{:S(2)}, u32[]{:S(2)}) collective-permute-start(bf16[4,64,2048]{2,1,0:T(8,128)(2,1)} %get-tuple-element.29.refs_7_), channel_id=1, source_target_pairs={{0,4},{12,8},{4,0},{8,12},{1,5},{13,9},{5,1},{9,13},{2,6},{14,10},... | collective-permute-start | bytes 3145736 | tf_op jit(solution)/shard_map/ppermute | solution.py:452
  41.9 2.9 %shard_map.133 = (bf16[1,64,128]{2,1,0:T(8,128)(2,1)}, bf16[1,64,2048]{2,1,0:T(8,128)(2,1)}) custom-call(s32[13]{0:T(128)} %refs_0_.9, s32[1]{0:T(128)} %bitcast.7.refs_1_, bf16[1,64,2048]{2,1,0:T(8,128)(2,1)} %get-tuple-element.28.refs_2_, bf16[1,64,2048]{2,1,0:T(8,128)(2,1)} %copy-done.5, bf16[1,64,2048]{2,1,0:T(8,128)(2,1)} %copy-done.6, ...), custom_call_target="tpu_custom_call" | custom-call | flops 1000000000 | bytes 360000 | tf_op jit(solution)/shard_map/pallas_call | solution.py:24
  44.8 5.9 %shard_map.134 = (bf16[4,64,2048]{2,1,0:T(8,128)(2,1)}, bf16[4,64,2048]{2,1,0:T(8,128)(2,1)}) custom-call(s32[16]{0:T(128)} %get-tuple-element.47.refs_0_, bf16[12,64,128]{2,1,0:T(8,128)(2,1)} %copy-done.4, bf16[12,64,128]{2,1,0:T(8,128)(2,1)} %copy-done.8, bf16[1,64,128]{2,1,0:T(8,128)(2,1)} %get-tuple-element.27.refs_3_, bf16[1,64,128]{2,1,0:T(8,128)(2,1)} %copy-done.15, ...), custom_call_target="tpu_custom_call" | custom-call | flops 99999997952 | bytes 36000000 | tf_op jit(solution)/shard_map/pallas_call | solution.py:24
  50.7 12.1 %shard_map.135 = (bf16[1664,256]{1,0:T(8,128)(2,1)}, bf16[1664,256]{1,0:T(8,128)(2,1)}, bf16[1664,256]{1,0:T(8,128)(2,1)}, bf16[1664,256]{1,0:T(8,128)(2,1)}) custom-call(s32[4]{0:T(128)} %pad_add_fusion.refs_0_, bf16[1664,2048]{1,0:T(8,128)(2,1)} %refs_8_.5, bf16[2048,1024]{1,0:T(8,128)(2,1)} %refs_5_.2, bf16[2048,1024]{1,0:T(8,128)(2,1)} %refs_5_.2, ...), custom_call_target="tpu_custom_call" | custom-call | flops 99999997952 | bytes 36000000 | tf_op jit(solution)/shard_map/pallas_call | solution.py:24
  64.9 1.6 %add_convert_fusion.1.refs_1_ = bf16[4,64,2048]{2,1,0:T(8,128)(2,1)S(1)} fusion(bf16[4,64,2048]{2,1,0:T(8,128)(2,1)} %shard_map.136, bf16[4,64,2048]{2,1,0:T(8,128)(2,1)} %collective-permute-done.13.refs_1_, pred[]{:T(512)S(6)} %or.3), kind=kLoop, calls=%fused_computation.2 | loop fusion | flops 2621440 | bytes 3145729 | tf_op jit(solution)/shard_map/convert_element_type | solution.py:338
  66.5 1.6 %collective-permute-start.25 = (bf16[4,64,2048]{2,1,0:T(8,128)(2,1)S(1)}, bf16[4,64,2048]{2,1,0:T(8,128)(2,1)}, u32[]{:S(2)}, u32[]{:S(2)}) collective-permute-start(bf16[4,64,2048]{2,1,0:T(8,128)(2,1)S(1)} %add_convert_fusion.1.refs_1_), channel_id=1, source_target_pairs={{0,8},{12,4},{4,12},{8,0},{1,9},{13,5},{5,13},{9,1},{2,10},{14,6},... | collective-permute-start | bytes 3145736 | tf_op jit(solution)/shard_map/ppermute | solution.py:460
  68.2 4.5 %collective-permute-start.26 = (bf16[4,64,2048]{2,1,0:T(8,128)(2,1)}, bf16[4,64,2048]{2,1,0:T(8,128)(2,1)}, u32[]{:S(2)}, u32[]{:S(2)}) collective-permute-start(bf16[4,64,2048]{2,1,0:T(8,128)(2,1)} %shard_map.142), channel_id=1, source_target_pairs={{0,4},{12,8},{1,5},{13,9},{2,6},{14,10},{3,7},{15,11},{16,20},{28,... | collective-permute-start | bytes 3145736 | tf_op jit(solution)/shard_map/ppermute | solution.py:461
  72.6 2.3 %add_convert_fusion.2.refs_9_ = bf16[1664,256]{1,0:T(8,128)(2,1)} fusion(bf16[1664,256]{1,0:T(8,128)(2,1)} %collective-permute-done.14, bf16[1664,256]{1,0:T(8,128)(2,1)S(1)} %copy-done.1), kind=kLoop, calls=%fused_computation.3 | loop fusion | flops 1703936 | bytes 2555904 | tf_op jit(solution)/shard_map/convert_element_type | solution.py:338
  75.8 6.7 %shard_map.138.refs_5_ = bf16[12,64,128]{2,1,0:T(8,128)(2,1)} custom-call(s32[13]{0:T(128)} %refs_0_.9, bf16[13,64,2048]{2,1,0:T(8,128)(2,1)} %refs_4_.3, bf16[13,64,2048]{2,1,0:T(8,128)(2,1)} %refs_4_.3, bf16[13,64,2048]{2,1,0:T(8,128)(2,1)} %refs_4_.3, bf16[13,64,2048]{2,1,0:T(8,128)(2,1)} %refs_4_.3, bf16[1664,2048]{1,0:T(8,128)(2,1)} %refs_8_.5, ...), custom_call_target="tpu_custom_call" | custom-call | flops 1000000000 | bytes 360000 | tf_op jit(solution)/shard_map/pallas_call | solution.py:24
  82.6 1.1 collective-permute-start.16
  86.5 2.1 %convert_add_fusion = f32[4,64,2048]{2,1,0:T(8,128)S(1)} fusion(bf16[4,64,2048]{2,1,0:T(8,128)(2,1)} %shard_map.141, bf16[4,64,2048]{2,1,0:T(8,128)(2,1)} %collective-permute-done.12.refs_2_, bf16[4,64,2048]{2,1,0:T(8,128)(2,1)} %collective-permute-done.13.refs_1_, pred[]{:T(512)S(6)} %or.3), kind=kLoop, calls=%fused_computation.1 | loop fusion | flops 2097152 | bytes 5242881 | tf_op jit(solution)/shard_map/add | solution.py:463
  88.6 12.6 %collective-permute-done.17.refs_7_ = bf16[12,64,128]{2,1,0:T(8,128)(2,1)S(1)} collective-permute-done((bf16[12,64,128]{2,1,0:T(8,128)(2,1)S(1)}, bf16[12,64,128]{2,1,0:T(8,128)(2,1)S(1)}, u32[]{:S(2)}, u32[]{:S(2)}) %collective-permute-start.17) | collective-permute-done | bytes 196640 | tf_op jit(solution)/shard_map/ppermute | solution.py:342
  101.2 3.6 %collective-permute-done.18.refs_8_ = bf16[12,64,128]{2,1,0:T(8,128)(2,1)S(1)} collective-permute-done((bf16[12,64,128]{2,1,0:T(8,128)(2,1)S(1)}, bf16[12,64,128]{2,1,0:T(8,128)(2,1)S(1)}, u32[]{:S(2)}, u32[]{:S(2)}) %collective-permute-start.18) | collective-permute-done | bytes 196640 | tf_op jit(solution)/shard_map/ppermute | solution.py:342
  105.5 5.0 %shard_map.139 = (bf16[1664,256]{1,0:T(8,128)(2,1)}, bf16[384,256]{1,0:T(8,128)(2,1)}, bf16[384,256]{1,0:T(8,128)(2,1)}, bf16[384,256]{1,0:T(8,128)(2,1)}, bf16[384,256]{1,0:T(8,128)(2,1)}) custom-call(s32[13]{0:T(128)} %refs_0_.9, s32[16]{0:T(128)} %get-tuple-element.48.refs_1_, bf16[1664,256]{1,0:T(8,128)(2,1)} %get-tuple-element.32.refs_2_, ...), custom_call_target="tpu_custom_call" | custom-call | flops 1000000000 | bytes 360000 | tf_op jit(solution)/shard_map/pallas_call | solution.py:24
  110.6 1.8 %collective-permute-start.23 = (bf16[384,256]{1,0:T(8,128)(2,1)}, bf16[384,256]{1,0:T(8,128)(2,1)S(1)}, u32[]{:S(2)}, u32[]{:S(2)}) collective-permute-start(bf16[384,256]{1,0:T(8,128)(2,1)} %get-tuple-element.40), channel_id=1, source_target_pairs={{0,8},{4,12},{8,0},{12,4},{1,9},{5,13},{9,1},{13,5},{2,10},{6,14},... | collective-permute-start | bytes 589832 | tf_op jit(solution)/shard_map/ppermute | solution.py:324
  112.4 2.0 %collective-permute-start.24 = (bf16[384,256]{1,0:T(8,128)(2,1)}, bf16[384,256]{1,0:T(8,128)(2,1)}, u32[]{:S(2)}, u32[]{:S(2)}) collective-permute-start(bf16[384,256]{1,0:T(8,128)(2,1)} %get-tuple-element.41), channel_id=1, source_target_pairs={{0,12},{4,0},{8,4},{12,8},{1,13},{5,1},{9,5},{13,9},{2,14},{6,2},{... | collective-permute-start | bytes 589832 | tf_op jit(solution)/shard_map/ppermute | solution.py:324
  115.0 3.0 %add_convert_fusion = bf16[4,64,2048]{2,1,0:T(8,128)(2,1)} fusion(bf16[4,64,2048]{2,1,0:T(8,128)(2,1)} %collective-permute-done.26, f32[4,64,2048]{2,1,0:T(8,128)S(1)} %convert_add_fusion, bf16[4,64,2048]{2,1,0:T(8,128)(2,1)} %collective-permute-done.25), kind=kLoop, calls=%fused_computation | loop fusion | flops 2621440 | bytes 5242880 | tf_op jit(solution)/shard_map/convert_element_type | solution.py:465
  118.0 2.5 %collective-permute-done.22.refs_2_ = bf16[384,256]{1,0:T(8,128)(2,1)S(1)} collective-permute-done((bf16[384,256]{1,0:T(8,128)(2,1)}, bf16[384,256]{1,0:T(8,128)(2,1)S(1)}, u32[]{:S(2)}, u32[]{:S(2)}) %collective-permute-start.22) | collective-permute-done | bytes 196640 | tf_op jit(solution)/shard_map/ppermute | solution.py:324
  120.4 7.5 %collective-permute-done.23.refs_3_ = bf16[384,256]{1,0:T(8,128)(2,1)S(1)} collective-permute-done((bf16[384,256]{1,0:T(8,128)(2,1)}, bf16[384,256]{1,0:T(8,128)(2,1)S(1)}, u32[]{:S(2)}, u32[]{:S(2)}) %collective-permute-start.23) | collective-permute-done | bytes 196640 | tf_op jit(solution)/shard_map/ppermute | solution.py:324
  128.6 2.0 %shard_map.140 = (bf16[256,256]{1,0:T(8,128)(2,1)}, bf16[1664,256]{1,0:T(8,128)(2,1)}) custom-call(s32[1]{0:T(128)} %bitcast.1.refs_0_, bf16[384,256]{1,0:T(8,128)(2,1)} %get-tuple-element.38.refs_1_, bf16[384,256]{1,0:T(8,128)(2,1)} %copy-done.21, bf16[384,256]{1,0:T(8,128)(2,1)} %copy-done.22, ...), custom_call_target="tpu_custom_call", output_to_operand_aliasing={{1}: (5, {})} | custom-call | flops 1000000000 | bytes 360000 | tf_op jit(solution)/shard_map/pallas_call | solution.py:24
  (107 shorter events, 16.4 us)
Async XLA Ops:
  0.6 11.7 %copy-start.20 = (s32[4]{0:T(128)S(1)}, s32[4]{0:T(128)}, u32[]{:S(2)}) copy-start(s32[4]{0:T(128)} %constant.52.clone) | copy-start | bytes 52
  0.7 14.9 %copy-start.26 = (s32[16]{0:T(128)S(1)}, s32[16]{0:T(128)}, u32[]{:S(2)}) copy-start(s32[16]{0:T(128)} %param.14) | copy-start | bytes 196
  0.7 14.9 %copy-start.27 = (s32[13]{0:T(128)S(1)}, s32[13]{0:T(128)}, u32[]{:S(2)}) copy-start(s32[13]{0:T(128)} %param.12) | copy-start | bytes 160
  3.9 12.6 %collective-permute-start.2 = (bf16[1,64,256]{2,1,0:T(8,128)(2,1)}, bf16[1,64,256]{2,1,0:T(8,128)(2,1)S(1)}, u32[]{:S(2)}, u32[]{:S(2)}) collective-permute-start(bf16[1,64,256]{2,1,0:T(8,128)(2,1)} %get-tuple-element.26.refs_2_), channel_id=1, source_target_pairs={{0,4},{4,8},{8,12},{12,0},{1,5},{5,9},{9,13},{13,1},{2,6},{6,10},{... | collective-permute-start | bytes 98312 | tf_op jit(solution)/shard_map/ppermute | solution.py:324
  6.9 10.0 %collective-permute-start.3 = (bf16[1,64,256]{2,1,0:T(8,128)(2,1)}, bf16[1,64,256]{2,1,0:T(8,128)(2,1)S(1)}, u32[]{:S(2)}, u32[]{:S(2)}) collective-permute-start(bf16[1,64,256]{2,1,0:T(8,128)(2,1)} %get-tuple-element.26.refs_2_), channel_id=1, source_target_pairs={{0,8},{4,12},{8,0},{12,4},{1,9},{5,13},{9,1},{13,5},{2,10},{6,14},... | collective-permute-start | bytes 98312 | tf_op jit(solution)/shard_map/ppermute | solution.py:324
  9.5 10.3 %collective-permute-start.4 = (bf16[1,64,256]{2,1,0:T(8,128)(2,1)}, bf16[1,64,256]{2,1,0:T(8,128)(2,1)S(1)}, u32[]{:S(2)}, u32[]{:S(2)}) collective-permute-start(bf16[1,64,256]{2,1,0:T(8,128)(2,1)} %get-tuple-element.26.refs_2_), channel_id=1, source_target_pairs={{0,12},{4,0},{8,4},{12,8},{1,13},{5,1},{9,5},{13,9},{2,14},{6,2},{... | collective-permute-start | bytes 98312 | tf_op jit(solution)/shard_map/ppermute | solution.py:324
  10.9 2.1 %collective-permute-start = (bf16[12,64,128]{2,1,0:T(8,128)(2,1)}, bf16[12,64,128]{2,1,0:T(8,128)(2,1)S(1)}, u32[]{:S(2)}, u32[]{:S(2)}) collective-permute-start(bf16[12,64,128]{2,1,0:T(8,128)(2,1)} %get-tuple-element.25), channel_id=1, source_target_pairs={{0,1},{1,0},{2,3},{3,2},{4,5},{5,4},{6,7},{7,6},{8,9},{9,8},{10,11... | collective-permute-start | bytes 589832 | tf_op jit(solution)/shard_map/ppermute | solution.py:342
  10.9 29.5 %collective-permute-start.8 = (bf16[1,64,2048]{2,1,0:T(8,128)(2,1)}, bf16[1,64,2048]{2,1,0:T(8,128)(2,1)S(1)}, u32[]{:S(2)}, u32[]{:S(2)}) collective-permute-start(bf16[1,64,2048]{2,1,0:T(8,128)(2,1)} %get-tuple-element.28.refs_2_), channel_id=1, source_target_pairs={{0,4},{4,8},{8,12},{12,0},{1,5},{5,9},{9,13},{13,1},{2,6},{6,10},{... | collective-permute-start | bytes 786440 | tf_op jit(solution)/shard_map/ppermute | solution.py:324
  14.0 15.8 %copy-start.4 = (bf16[12,64,128]{2,1,0:T(8,128)(2,1)}, bf16[12,64,128]{2,1,0:T(8,128)(2,1)S(1)}, u32[]{:S(2)}) copy-start(bf16[12,64,128]{2,1,0:T(8,128)(2,1)S(1)} %add_convert_fusion.3.refs_1_) | copy-start | bytes 589828
  14.0 7.1 %collective-permute-start.1 = (bf16[12,64,128]{2,1,0:T(8,128)(2,1)S(1)}, bf16[12,64,128]{2,1,0:T(8,128)(2,1)S(1)}, u32[]{:S(2)}, u32[]{:S(2)}) collective-permute-start(bf16[12,64,128]{2,1,0:T(8,128)(2,1)S(1)} %add_convert_fusion.3.refs_1_), channel_id=1, source_target_pairs={{0,2},{1,3},{2,0},{3,1},{4,6},{5,7},{6,4},{7,5},{8,10},{9,11},{10,... | collective-permute-start | bytes 589832 | tf_op jit(solution)/shard_map/ppermute | solution.py:342
  16.5 23.9 %collective-permute-start.9 = (bf16[1,64,2048]{2,1,0:T(8,128)(2,1)}, bf16[1,64,2048]{2,1,0:T(8,128)(2,1)S(1)}, u32[]{:S(2)}, u32[]{:S(2)}) collective-permute-start(bf16[1,64,2048]{2,1,0:T(8,128)(2,1)} %get-tuple-element.28.refs_2_), channel_id=1, source_target_pairs={{0,8},{4,12},{8,0},{12,4},{1,9},{5,13},{9,1},{13,5},{2,10},{6,14},... | collective-permute-start | bytes 786440 | tf_op jit(solution)/shard_map/ppermute | solution.py:324
  16.9 23.5 %collective-permute-start.10 = (bf16[1,64,2048]{2,1,0:T(8,128)(2,1)}, bf16[1,64,2048]{2,1,0:T(8,128)(2,1)S(1)}, u32[]{:S(2)}, u32[]{:S(2)}) collective-permute-start(bf16[1,64,2048]{2,1,0:T(8,128)(2,1)} %get-tuple-element.28.refs_2_), channel_id=1, source_target_pairs={{0,12},{4,0},{8,4},{12,8},{1,13},{5,1},{9,5},{13,9},{2,14},{6,2},{... | collective-permute-start | bytes 786440 | tf_op jit(solution)/shard_map/ppermute | solution.py:324
  24.1 2.3 %collective-permute-start.5 = (bf16[1,64,128]{2,1,0:T(8,128)(2,1)}, bf16[1,64,128]{2,1,0:T(8,128)(2,1)S(1)}, u32[]{:S(2)}, u32[]{:S(2)}) collective-permute-start(bf16[1,64,128]{2,1,0:T(8,128)(2,1)} %get-tuple-element.27.refs_3_), channel_id=1, source_target_pairs={{0,1},{1,0},{2,3},{3,2},{4,5},{5,4},{6,7},{7,6},{8,9},{9,8},{10,11... | collective-permute-start | bytes 49160 | tf_op jit(solution)/shard_map/ppermute | solution.py:342
  24.9 3.9 %collective-permute-start.6 = (bf16[1,64,128]{2,1,0:T(8,128)(2,1)}, bf16[1,64,128]{2,1,0:T(8,128)(2,1)S(1)}, u32[]{:S(2)}, u32[]{:S(2)}) collective-permute-start(bf16[1,64,128]{2,1,0:T(8,128)(2,1)} %get-tuple-element.27.refs_3_), channel_id=1, source_target_pairs={{0,2},{1,3},{2,0},{3,1},{4,6},{5,7},{6,4},{7,5},{8,10},{9,11},{10,... | collective-permute-start | bytes 49160 | tf_op jit(solution)/shard_map/ppermute | solution.py:342
  26.4 3.4 %collective-permute-start.7 = (bf16[1,64,128]{2,1,0:T(8,128)(2,1)}, bf16[1,64,128]{2,1,0:T(8,128)(2,1)S(1)}, u32[]{:S(2)}, u32[]{:S(2)}) collective-permute-start(bf16[1,64,128]{2,1,0:T(8,128)(2,1)} %get-tuple-element.27.refs_3_), channel_id=1, source_target_pairs={{0,3},{1,2},{2,1},{3,0},{4,7},{5,6},{6,5},{7,4},{8,11},{9,10},{10,... | collective-permute-start | bytes 49160 | tf_op jit(solution)/shard_map/ppermute | solution.py:342
  37.4 26.9 %collective-permute-start.12 = (bf16[4,64,2048]{2,1,0:T(8,128)(2,1)}, bf16[4,64,2048]{2,1,0:T(8,128)(2,1)}, u32[]{:S(2)}, u32[]{:S(2)}) collective-permute-start(bf16[4,64,2048]{2,1,0:T(8,128)(2,1)} %get-tuple-element.36), channel_id=1, source_target_pairs={{4,8},{8,4},{5,9},{9,5},{6,10},{10,6},{7,11},{11,7},{20,24},{24,20... | collective-permute-start | bytes 3145736 | tf_op jit(solution)/shard_map/ppermute | solution.py:453
  39.0 25.9 %collective-permute-start.13 = (bf16[4,64,2048]{2,1,0:T(8,128)(2,1)}, bf16[4,64,2048]{2,1,0:T(8,128)(2,1)}, u32[]{:S(2)}, u32[]{:S(2)}) collective-permute-start(bf16[4,64,2048]{2,1,0:T(8,128)(2,1)} %get-tuple-element.29.refs_7_), channel_id=1, source_target_pairs={{0,4},{12,8},{4,0},{8,12},{1,5},{13,9},{5,1},{9,13},{2,6},{14,10},... | collective-permute-start | bytes 3145736 | tf_op jit(solution)/shard_map/ppermute | solution.py:452
  50.7 12.2 %copy-start.12 = (bf16[1,64,128]{2,1,0:T(8,128)(2,1)S(1)}, bf16[1,64,128]{2,1,0:T(8,128)(2,1)}, u32[]{:S(2)}) copy-start(bf16[1,64,128]{2,1,0:T(8,128)(2,1)} %get-tuple-element.30.refs_12_.refs_9_) | copy-start | bytes 49156
  62.9 5.3 %collective-permute-start.14 = (bf16[1664,256]{1,0:T(8,128)(2,1)}, bf16[1664,256]{1,0:T(8,128)(2,1)}, u32[]{:S(2)}, u32[]{:S(2)}) collective-permute-start(bf16[1664,256]{1,0:T(8,128)(2,1)} %get-tuple-element.35.refs_1_), channel_id=1, source_target_pairs={{0,1},{1,0},{2,3},{3,2},{4,5},{5,4},{6,7},{7,6},{8,9},{9,8},{10,11... | collective-permute-start | bytes 2555912 | tf_op jit(solution)/shard_map/ppermute | solution.py:342
  62.9 12.0 %collective-permute-start.19 = (bf16[1,64,128]{2,1,0:T(8,128)(2,1)S(1)}, bf16[1,64,128]{2,1,0:T(8,128)(2,1)S(1)}, u32[]{:S(2)}, u32[]{:S(2)}) collective-permute-start(bf16[1,64,128]{2,1,0:T(8,128)(2,1)S(1)} %copy-done.12), channel_id=1, source_target_pairs={{0,1},{1,0},{2,3},{3,2},{4,5},{5,4},{6,7},{7,6},{8,9},{9,8},{10,11... | collective-permute-start | bytes 49160 | tf_op jit(solution)/shard_map/ppermute | solution.py:342
  63.4 11.6 %collective-permute-start.20 = (bf16[1,64,128]{2,1,0:T(8,128)(2,1)S(1)}, bf16[1,64,128]{2,1,0:T(8,128)(2,1)S(1)}, u32[]{:S(2)}, u32[]{:S(2)}) collective-permute-start(bf16[1,64,128]{2,1,0:T(8,128)(2,1)S(1)} %copy-done.12), channel_id=1, source_target_pairs={{0,2},{1,3},{2,0},{3,1},{4,6},{5,7},{6,4},{7,5},{8,10},{9,11},{10,... | collective-permute-start | bytes 49160 | tf_op jit(solution)/shard_map/ppermute | solution.py:342
  64.2 20.8 %collective-permute-start.11 = (bf16[1664,256]{1,0:T(8,128)(2,1)}, bf16[1664,256]{1,0:T(8,128)(2,1)S(1)}, u32[]{:S(2)}, u32[]{:S(2)}) collective-permute-start(bf16[1664,256]{1,0:T(8,128)(2,1)} %get-tuple-element.33), channel_id=1, source_target_pairs={{0,1},{1,0},{2,3},{3,2},{4,5},{5,4},{6,7},{7,6},{8,9},{9,8},{10,11... | collective-permute-start | bytes 2555912 | tf_op jit(solution)/shard_map/ppermute | solution.py:342
  66.5 48.4 %collective-permute-start.25 = (bf16[4,64,2048]{2,1,0:T(8,128)(2,1)S(1)}, bf16[4,64,2048]{2,1,0:T(8,128)(2,1)}, u32[]{:S(2)}, u32[]{:S(2)}) collective-permute-start(bf16[4,64,2048]{2,1,0:T(8,128)(2,1)S(1)} %add_convert_fusion.1.refs_1_), channel_id=1, source_target_pairs={{0,8},{12,4},{4,12},{8,0},{1,9},{13,5},{5,13},{9,1},{2,10},{14,6},... | collective-permute-start | bytes 3145736 | tf_op jit(solution)/shard_map/ppermute | solution.py:460
  68.2 46.2 %collective-permute-start.26 = (bf16[4,64,2048]{2,1,0:T(8,128)(2,1)}, bf16[4,64,2048]{2,1,0:T(8,128)(2,1)}, u32[]{:S(2)}, u32[]{:S(2)}) collective-permute-start(bf16[4,64,2048]{2,1,0:T(8,128)(2,1)} %shard_map.142), channel_id=1, source_target_pairs={{0,4},{12,8},{1,5},{13,9},{2,6},{14,10},{3,7},{15,11},{16,20},{28,... | collective-permute-start | bytes 3145736 | tf_op jit(solution)/shard_map/ppermute | solution.py:461
  74.9 7.6 %collective-permute-start.21 = (bf16[1,64,128]{2,1,0:T(8,128)(2,1)S(1)}, bf16[1,64,128]{2,1,0:T(8,128)(2,1)}, u32[]{:S(2)}, u32[]{:S(2)}) collective-permute-start(bf16[1,64,128]{2,1,0:T(8,128)(2,1)S(1)} %copy-done.12), channel_id=1, source_target_pairs={{0,3},{1,2},{2,1},{3,0},{4,7},{5,6},{6,5},{7,4},{8,11},{9,10},{10,... | collective-permute-start | bytes 49160 | tf_op jit(solution)/shard_map/ppermute | solution.py:342
  75.0 29.9 %collective-permute-start.15 = (bf16[1664,256]{1,0:T(8,128)(2,1)}, bf16[1664,256]{1,0:T(8,128)(2,1)}, u32[]{:S(2)}, u32[]{:S(2)}) collective-permute-start(bf16[1664,256]{1,0:T(8,128)(2,1)} %add_convert_fusion.2.refs_9_), channel_id=1, source_target_pairs={{0,2},{1,3},{2,0},{3,1},{4,6},{5,7},{6,4},{7,5},{8,10},{9,11},{10,... | collective-permute-start | bytes 2555912 | tf_op jit(solution)/shard_map/ppermute | solution.py:342
  82.6 3.1 %collective-permute-start.16 = (bf16[12,64,128]{2,1,0:T(8,128)(2,1)}, bf16[12,64,128]{2,1,0:T(8,128)(2,1)S(1)}, u32[]{:S(2)}, u32[]{:S(2)}) collective-permute-start(bf16[12,64,128]{2,1,0:T(8,128)(2,1)} %shard_map.138.refs_5_), channel_id=1, source_target_pairs={{0,1},{1,0},{2,3},{3,2},{4,5},{5,4},{6,7},{7,6},{8,9},{9,8},{10,11... | collective-permute-start | bytes 589832 | tf_op jit(solution)/shard_map/ppermute | solution.py:342
  85.0 16.2 %collective-permute-start.17 = (bf16[12,64,128]{2,1,0:T(8,128)(2,1)S(1)}, bf16[12,64,128]{2,1,0:T(8,128)(2,1)S(1)}, u32[]{:S(2)}, u32[]{:S(2)}) collective-permute-start(bf16[12,64,128]{2,1,0:T(8,128)(2,1)S(1)} %copy-done.3), channel_id=1, source_target_pairs={{0,2},{1,3},{2,0},{3,1},{4,6},{5,7},{6,4},{7,5},{8,10},{9,11},{10,... | collective-permute-start | bytes 589832 | tf_op jit(solution)/shard_map/ppermute | solution.py:342
  85.9 18.9 %collective-permute-start.18 = (bf16[12,64,128]{2,1,0:T(8,128)(2,1)S(1)}, bf16[12,64,128]{2,1,0:T(8,128)(2,1)S(1)}, u32[]{:S(2)}, u32[]{:S(2)}) collective-permute-start(bf16[12,64,128]{2,1,0:T(8,128)(2,1)S(1)} %copy-done.3), channel_id=1, source_target_pairs={{0,3},{1,2},{2,1},{3,0},{4,7},{5,6},{6,5},{7,4},{8,11},{9,10},{10,... | collective-permute-start | bytes 589832 | tf_op jit(solution)/shard_map/ppermute | solution.py:342
  110.6 9.9 %collective-permute-start.22 = (bf16[384,256]{1,0:T(8,128)(2,1)}, bf16[384,256]{1,0:T(8,128)(2,1)S(1)}, u32[]{:S(2)}, u32[]{:S(2)}) collective-permute-start(bf16[384,256]{1,0:T(8,128)(2,1)} %get-tuple-element.39), channel_id=1, source_target_pairs={{0,4},{4,8},{8,12},{12,0},{1,5},{5,9},{9,13},{13,1},{2,6},{6,10},{... | collective-permute-start | bytes 589832 | tf_op jit(solution)/shard_map/ppermute | solution.py:324
  110.6 17.3 %collective-permute-start.23 = (bf16[384,256]{1,0:T(8,128)(2,1)}, bf16[384,256]{1,0:T(8,128)(2,1)S(1)}, u32[]{:S(2)}, u32[]{:S(2)}) collective-permute-start(bf16[384,256]{1,0:T(8,128)(2,1)} %get-tuple-element.40), channel_id=1, source_target_pairs={{0,8},{4,12},{8,0},{12,4},{1,9},{5,13},{9,1},{13,5},{2,10},{6,14},... | collective-permute-start | bytes 589832 | tf_op jit(solution)/shard_map/ppermute | solution.py:324
  112.4 15.5 %collective-permute-start.24 = (bf16[384,256]{1,0:T(8,128)(2,1)}, bf16[384,256]{1,0:T(8,128)(2,1)}, u32[]{:S(2)}, u32[]{:S(2)}) collective-permute-start(bf16[384,256]{1,0:T(8,128)(2,1)} %get-tuple-element.41), channel_id=1, source_target_pairs={{0,12},{4,0},{8,4},{12,8},{1,13},{5,1},{9,5},{13,9},{2,14},{6,2},{... | collective-permute-start | bytes 589832 | tf_op jit(solution)/shard_map/ppermute | solution.py:324
  (23 other events, 78.2 us)

commit v6 on v5

--- a/solution.py
+++ b/solution.py
@@ -80,38 +80,18 @@
             whole(features),
             (others, pl.BlockSpec(last_shapes[1], lambda i, *_: (kept, 0, 0), pipeline_mode=pl.Buffered(1))),
         ],
-        [((kept, rank, BLOCK), features.dtype, constant_spec((kept, rank, BLOCK)))]
+        [((blocks, rank, BLOCK), features.dtype, pl.BlockSpec((kept, rank, BLOCK), lambda i, *_: (0, 0, 0)))]
         + [(shape, features.dtype, constant_spec(shape)) for shape in last_shapes],
     )
 
 
-def streamed_ranks(lengths, maps, features, each, tokens=()):
-    blocks, rank, width = maps.shape
-    kept = blocks - SW
-
-    def kernel(lengths_ref, *refs):
-        step = pl.program_id(0)
-        for k in range(each):
-            refs[-1][k] = masked_rank(refs[k][0], refs[each + k][...], lengths_ref[step * each + k])
-
-    return call(
-        kernel,
-        (lengths,),
-        (kept // each,),
-        [(maps, pl.BlockSpec((1, rank, width), lambda i, *_, k=k: (i * each + k, 0, 0))) for k in range(each)]
-        + [(features, pl.BlockSpec((BLOCK, width), lambda i, *_, k=k: (i * each + k, 0))) for k in range(each)],
-        [((kept, rank, BLOCK), features.dtype, pl.BlockSpec((each, rank, BLOCK), lambda i, *_: (i, 0, 0)))],
-        tokens,
-    )[0]
-
-
-def last_ranks(lengths, pick, choices, features, tokens=()):
+def with_last_rank(lengths, pick, choices, features, ranks):
     shape = choices[0].shape
-    block = features.shape[0] // BLOCK - 1
+    block = ranks.shape[0] - 1
 
     def kernel(lengths_ref, pick_ref, *refs):
-        rows_ref, out_ref, chosen_ref = refs[-3:]
-        for k, choice in enumerate(refs[:-3]):
+        rows_ref, _, out_ref, chosen_ref = refs[-4:]
+        for k, choice in enumerate(refs[:-4]):
 
             @pl.when(pick_ref[0] == k)
             def _():
@@ -124,21 +104,67 @@
         (lengths, pick),
         (1,),
         [whole(choice) for choice in choices]
-        + [(features, pl.BlockSpec((BLOCK, shape[2]), lambda i, *_: (block, 0), pipeline_mode=pl.Buffered(1)))],
+        + [(features, pl.BlockSpec((BLOCK, shape[2]), lambda i, *_: (block, 0), pipeline_mode=pl.Buffered(1)))]
+        + [(ranks, ANYWHERE)],
         [
-            ((1, shape[1], BLOCK), features.dtype, constant_spec((1, shape[1], BLOCK))),
+            (ranks.shape, ranks.dtype, pl.BlockSpec((1, *ranks.shape[1:]), lambda i, *_: (block, 0, 0))),
             (shape, features.dtype, constant_spec(shape)),
         ],
+        aliases={3 + len(choices): 0},
+    )
+
+
+def streamed_ranks(lengths, maps, pick, choices, features, each, tokens=(), us=1.0):
+    blocks, rank, width = maps.shape
+    steps = pl.cdiv(blocks, each)
+    end = blocks - 1 - (steps - 1) * each
+
+    def kernel(lengths_ref, pick_ref, *refs):
+        maps_refs, rows_refs, choices_refs, out_ref = refs[:each], refs[each : 2 * each], refs[2 * each : -1], refs[-1]
+        step = pl.program_id(0)
+
+        def one(k):
+            block = step * each + k
+            out_ref[block] = masked_rank(maps_refs[k][0], rows_refs[k][...], lengths_ref[block])
+
+        @pl.when(step < steps - 1)
+        def _():
+            for k in range(each):
+                one(k)
+
+        @pl.when(step == steps - 1)
+        def _():
+            for k in range(end):
+                one(k)
+            for j, choice in enumerate(choices_refs):
+
+                @pl.when(pick_ref[0] == j)
+                def _():
+                    out_ref[blocks - 1] = masked_rank(choice[0], rows_refs[end][...], lengths_ref[blocks - 1])
+
+    def at(i, k):
+        block = i * each + k
+        return jnp.where(block < blocks, block, block - each)
+
+    return call(
+        kernel,
+        (lengths, pick),
+        (steps,),
+        [(maps, pl.BlockSpec((1, rank, width), lambda i, *_, k=k: (at(i, k), 0, 0))) for k in range(each)]
+        + [(features, pl.BlockSpec((BLOCK, width), lambda i, *_, k=k: (at(i, k), 0))) for k in range(each)]
+        + [whole(choice) for choice in choices],
+        [((blocks, rank, BLOCK), features.dtype, constant_spec((blocks, rank, BLOCK)))],
         tokens,
-    )
+        us,
+    )[0]
 
 
 def summed(terms, at):
     return sum(term[at].astype(jnp.float32) for term in terms).astype(terms[0].dtype)
 
 
-def down_rows(codes, first, parts, copies, ranks, last, features, tokens=(), us=1.0):
-    kept, rank, _ = ranks[0].shape
+def down_rows(codes, first, parts, copies, ranks, features, tokens=(), us=1.0):
+    blocks, rank, _ = ranks[0].shape
     width = features.shape[1]
     piece = min(width, 512)
 
@@ -146,7 +172,6 @@
         return jnp.maximum((code >> 1) - 1, 0)
 
     def kernel(codes_ref, a, b, *refs):
-        lasts, refs = refs[: len(last)], refs[len(last) :]
         rows_refs, last_ref, outs = refs[:OWN], refs[OWN], refs[OWN + 1 :]
         step = pl.program_id(0)
 
@@ -166,7 +191,7 @@
 
                 @pl.when((code & 1) > 0)
                 def _():
-                    late = summed(lasts, 0)
+                    late = summed((a, b), blocks - 1)
                     for at in [slice(c, c + piece) for c in range(0, width, piece)]:
                         put(
                             at,
@@ -195,25 +220,24 @@
         kernel,
         (codes,),
         (parts,),
-        [whole(array) for array in (*ranks, *last)]
+        [whole(array) for array in ranks]
         + [(features, rows_spec(k)) for k in range(OWN)]
-        + [(features, pl.BlockSpec((BLOCK, width), lambda r, *_: (kept, 0), pipeline_mode=pl.Buffered(1)))],
+        + [(features, pl.BlockSpec((BLOCK, width), lambda r, *_: (blocks - 1, 0), pipeline_mode=pl.Buffered(1)))],
         outs,
         tokens,
         us,
     )
 
 
-def outputs_of(lengths, codes, parts, base, ranks, last, features, maps, last_map):
+def outputs_of(lengths, codes, parts, base, ranks, features, maps, last_map):
     rows, width = base[0].shape
     blocks = rows // BLOCK
     rank = maps.shape[1]
 
     def kernel(lengths_ref, codes_ref, one, two, three, *refs):
         terms, refs = refs[: len(ranks)], refs[len(ranks) :]
-        lasts, refs = refs[: len(last)], refs[len(last) :]
         rows_ref, maps_ref, last_ref, out_ref, *outs = refs
-        late = summed(lasts, 0)
+        late = summed(terms, blocks - 1)
         for k in range(blocks):
             at = slice(k * BLOCK, (k + 1) * BLOCK)
             adapter = maps_ref[k] if k < blocks - 1 else last_ref[0]
@@ -258,7 +282,7 @@
         kernel,
         (lengths, codes),
         (1,),
-        [whole(array) for array in (*base, *ranks, *last, features, maps, last_map)],
+        [whole(array) for array in (*base, *ranks, features, maps, last_map)],
         [((rows, width), maps.dtype, constant_spec((rows, width)))]
         + [
             ((count * rank + BLOCK, width), maps.dtype, constant_spec((count * rank + BLOCK, width)))
@@ -267,7 +291,7 @@
     )
 
 
-def finish(pick, values, own, arrived):
+def finish(pick, values, own, arrived, tokens):
     width = values.shape[1]
     block = values.shape[0] // BLOCK - 1
     rows = own.shape[0] - BLOCK
@@ -290,6 +314,7 @@
             ((rows, width), own.dtype, constant_spec((rows, width))),
             (values.shape, values.dtype, pl.BlockSpec((BLOCK, width), lambda i, *_: (block, 0))),
         ],
+        tokens,
         aliases={2 + len(arrived): 1},
     )
 
@@ -403,11 +428,10 @@
     holder = jnp.sum(jnp.where(partner == me, order, 0))
 
     cot_terms, up_own, down_own = kept_ranks(lengths, adapter_up_matrix, cotangent, adapter_down_rows)
+    up_choices, up_pick = shifted(up_own, holder)
+    down_choices, down_pick = shifted(down_own, holder)
+    cot_terms, up_last = with_last_rank(lengths, up_pick, up_choices, cotangent, cot_terms)
     rank_cot = exchanged(cot_terms)
-    up_choices, up_pick = shifted(up_own, holder)
-    last_terms, up_last = last_ranks(lengths, up_pick, up_choices, cotangent, [rank_cot[1]])
-    last_cot = spread(last_terms)
-    down_choices, down_pick = shifted(down_own, holder)
 
     table_rows = jnp.sum(
         jnp.where(
@@ -426,37 +450,29 @@
     columns = jnp.stack([column ^ 3, column ^ 2, column ^ 1, column]).astype(jnp.int32)
 
     def base(*tokens):
-        return base_terms(columns, hidden, frozen_value_weight, tokens)
-
-    def base_parts(terms, *tokens):
-        sent, away, given, mine = terms
-        away = add(after(away, *tokens), near(sent))
+        sent, away, given, mine = base_terms(columns, hidden, frozen_value_weight, tokens)
+        away = add(away, near(sent))
         return (mine, near(given), far(away)), away
 
-    def last_in(token):
-        terms, _ = last_ranks(lengths, down_pick, down_choices, hidden, [token])
-        return spread(terms)
-
     def inputs(*tokens):
-        return spread(streamed_ranks(lengths, adapter_down_rows, hidden, 4, tokens))
-
-    def outputs(codes, parts, base_sums, rank_in, last):
+        return spread(
+            streamed_ranks(lengths, adapter_down_rows, down_pick, down_choices, hidden, 4, tokens, 100.0)
+        )
+
+    def outputs(codes, parts, base_sums, rank_in):
         return outputs_of(
-            lengths, codes, parts, base_sums, rank_in, last, cotangent, adapter_up_matrix, up_last
+            lengths, codes, parts, base_sums, rank_in, cotangent, adapter_up_matrix, up_last
         )
 
     if line:
         inner = (me == 1) | (me == 2)
         codes = codes_of(jnp.array(ROLES, jnp.int32)[me])
-        first, third, third_too = down_rows(codes, 0, 2, 2, rank_cot, last_cot, hidden)
+        first, third, third_too = down_rows(codes, 0, 2, 2, rank_cot, hidden)
         from_first = lax.ppermute(first, "dp", [(0, 1), (3, 2), (1, 0), (2, 3)])
         from_inner = lax.ppermute(third, "dp", [(1, 2), (2, 1)])
-        last = last_in(first)
-        second, own = down_rows(codes, 2 * OWN, 2, 1, rank_cot, last_cot, hidden, [last[0]], 100.0)
-        terms = base(second)
-        second = add(
-            after(second, terms[0], from_inner), jnp.where(inner, from_first, jnp.zeros((), first.dtype))
-        )
+        base_sums, away = base(first, *down_choices[1:])
+        second, own = down_rows(codes, 2 * OWN, 2, 1, rank_cot, hidden, [base_sums[0]], 100.0)
+        second = add(after(second, away, from_inner), jnp.where(inner, from_first, jnp.zeros((), first.dtype)))
         from_second = lax.ppermute(second, "dp", [(0, 2), (3, 1), (1, 3), (2, 0)])
         from_third = lax.ppermute(after(third_too, from_first), "dp", [(0, 1), (3, 2)])
         near_total = lax.optimization_barrier(
@@ -465,17 +481,15 @@
         down_out = (near_total + from_second.astype(jnp.float32) + from_third.astype(jnp.float32)).astype(own.dtype)
 
         up_codes = codes_of((me + jnp.array([1, 2, 3, 0], jnp.int32)) % devices)
-        parts, away = base_parts(terms, second)
-        values, *sent, kept_here = outputs(up_codes, [OWN] * 4, parts, inputs(away), last)
+        values, *sent, kept_here = outputs(up_codes, [OWN] * 4, base_sums, inputs(second))
         arrived = [shift(array, by + 1) for by, array in enumerate(sent)]
         value_pick = ((me - partner[me]) % devices).reshape(1)
-        up_out, values = finish(value_pick, values, kept_here, arrived)
+        up_out, values = finish(value_pick, values, kept_here, arrived, [down_out])
     else:
         codes = codes_of(order)
-        (table,) = down_rows(codes, 0, devices, 0, rank_cot, last_cot, hidden)
+        (table,) = down_rows(codes, 0, devices, 0, rank_cot, hidden)
         down_out = line_reduce_scatter(table.reshape(devices, OWN, *table.shape[1:]))
-        parts, _ = base_parts(base(table))
-        values, table = outputs(codes, [devices * OWN], parts, inputs(table), last_in(table))
+        values, table = outputs(codes, [devices * OWN], base(table)[0], inputs(table))
         up_table, last_values = table[:-BLOCK], table[-BLOCK:]
         up_out = line_reduce_scatter(up_table.reshape(devices, OWN, -1, values.shape[1]))
         (last_values,), _ = shifted(last_values, partner[me])

time: 132 us -> 143 us (1.083)
  waiting for transfers between devices: 31.1 us -> 39 us
  starting transfers between devices: 31.8 us -> 37.3 us
  Pallas kernels: 47.3 us -> 44.6 us
  local copies, waits for them, and re-layouts: 5.23 us -> 7.18 us
    ppermute x1, waiting for transfers between devices: 0.56 us -> 25.3 us  [body(): from_second = lax.ppermute(second, 'dp', [(0, 2), (3, 1), (1, 3), (2, 0)])]
    ppermute x1, starting transfers between devices: 1.34 us -> 10.9 us  [body(): from_first = lax.ppermute(first, 'dp', [(0, 1), (3, 2), (1, 0), (2, 3)])]
    ppermute x9, waiting for transfers between devices: 9.96 us -> 0.84 us  [shift(): lax.ppermute(array, 'dp', [(i, (i + by) % size) for i in range(size)])]
    ppermute x14 -> x8, waiting for transfers between devices: 19.9 us -> 12.9 us  [crossed(): lax.ppermute(array, 'tensor', [(i, i ^ by) for i in range(lax.axis_size('...]
    pallas_call x13 -> x11, Pallas kernels: 47.3 us -> 44.6 us  [call(): pl.pallas_call(run, grid_spec=pltpu.PrefetchScalarGridSpec(num_scalar_pre...]
    unnamed x56 -> x42, local copies, waits for them, and re-layouts: 4.42 us -> 6.43 us
    ppermute x14 -> x8, starting transfers between devices: 7.99 us -> 6.29 us  [crossed(): lax.ppermute(array, 'tensor', [(i, i ^ by) for i in range(lax.axis_size('...]
    ppermute x1, starting transfers between devices: 1.62 us -> 0.07 us  [body(): from_second = lax.ppermute(second, 'dp', [(0, 2), (3, 1), (1, 3), (2, 0)])]
  transfers between devices with their start and end apart: 27 -> 21, of which waited for: 9 -> 6; matrix products, arithmetic and copies ran while one was open for 11% -> 9% of each run, Pallas kernels for 32% -> 28%
where the time goes in v6:
time: 143 us; the launch traced here: 142 us
  Pallas kernels  44.6 us (31%)
  waiting for transfers between devices  39 us (27%)
  starting transfers between devices  37.3 us (26%)
  other arithmetic  11.9 us (8%)
  local copies, waits for them, and re-layouts  7.18 us (5%)
  between operations  2.22 us (2%)
    pallas_call x11, Pallas kernels, call(): pl.pallas_call(run, grid_spec=pltpu.PrefetchScalarGridSpec(num_scalar_pre...  44.6 us
    ppermute x1, waiting for transfers between devices, body(): from_second = lax.ppermute(second, 'dp', [(0, 2), (3, 1), (1, 3), (2, 0)])  25.3 us
    ppermute x9, starting transfers between devices, shift(): lax.ppermute(array, 'dp', [(i, (i + by) % size) for i in range(size)])  13.9 us
    ppermute x8, waiting for transfers between devices, crossed(): lax.ppermute(array, 'tensor', [(i, i ^ by) for i in range(lax.axis_size('...  12.9 us
    ppermute x1, starting transfers between devices, body(): from_first = lax.ppermute(first, 'dp', [(0, 1), (3, 2), (1, 0), (2, 3)])  10.9 us
    unnamed x42, local copies, waits for them, and re-layouts  6.43 us
    ppermute x8, starting transfers between devices, crossed(): lax.ppermute(array, 'tensor', [(i, i ^ by) for i in range(lax.axis_size('...  6.29 us
    ppermute x1, starting transfers between devices, body(): lax.ppermute(after(third_too, from_first), 'dp', [(0, 1), (3, 2)])  4.51 us
  transfers between devices with their start and end apart: 21, of which 6 were waited for; matrix products, arithmetic and copies ran while one was open for 9% of the time, Pallas kernels for 28%

profile of v6, /device:TPU:0, one launch (start us, length us, event | category | flops | bytes accessed | tf_op | source)
XLA Modules:
  0.0 142.1 jit_solution(16260850166611876100)
XLA Ops:
  0.7 3.2 %shard_map.130 = (bf16[13,64,128]{2,1,0:T(8,128)(2,1)}, bf16[1,64,256]{2,1,0:T(8,128)(2,1)}, bf16[1,64,2048]{2,1,0:T(8,128)(2,1)}) custom-call(s32[13]{0:T(128)} %refs_0_.7, bf16[13,64,256]{2,1,0:T(8,128)(2,1)} %refs_10_.1, bf16[1664,256]{1,0:T(8,128)(2,1)} %refs_9_.3, bf16[13,64,2048]{2,1,0:T(8,128)(2,1)} %refs_5_.7), custom_call_target="tpu_custom_call" | custom-call | flops 1000000000 | bytes 360000 | tf_op jit(solution)/shard_map/pallas_call | solution.py:24
  3.9 5.1 %collective-permute-start.2 = (bf16[1,64,256]{2,1,0:T(8,128)(2,1)}, bf16[1,64,256]{2,1,0:T(8,128)(2,1)S(1)}, u32[]{:S(2)}, u32[]{:S(2)}) collective-permute-start(bf16[1,64,256]{2,1,0:T(8,128)(2,1)} %get-tuple-element.24.refs_2_), channel_id=1, source_target_pairs={{0,12},{4,0},{8,4},{12,8},{1,13},{5,1},{9,5},{13,9},{2,14},{6,2},{... | collective-permute-start | bytes 98312 | tf_op jit(solution)/shard_map/ppermute | solution.py:349
  8.9 1.0 collective-permute-start
  10.0 2.8 %collective-permute-start.7 = (bf16[1,64,2048]{2,1,0:T(8,128)(2,1)}, bf16[1,64,2048]{2,1,0:T(8,128)(2,1)S(1)}, u32[]{:S(2)}, u32[]{:S(2)}) collective-permute-start(bf16[1,64,2048]{2,1,0:T(8,128)(2,1)} %get-tuple-element.28.refs_10_), channel_id=1, source_target_pairs={{0,12},{4,0},{8,4},{12,8},{1,13},{5,1},{9,5},{13,9},{2,14},{6,2},{... | collective-permute-start | bytes 786440 | tf_op jit(solution)/shard_map/ppermute | solution.py:349
  12.8 1.1 collective-permute-start.6
  16.9 2.3 %shard_map.131 = (bf16[13,64,128]{2,1,0:T(8,128)(2,1)}, bf16[1,64,256]{2,1,0:T(8,128)(2,1)}) custom-call(s32[13]{0:T(128)} %refs_0_.7, s32[1]{0:T(128)} %bitcast.7.refs_1_, bf16[1,64,256]{2,1,0:T(8,128)(2,1)} %get-tuple-element.24.refs_2_, bf16[1,64,256]{2,1,0:T(8,128)(2,1)} %copy-done.18, ...), custom_call_target="tpu_custom_call", output_to_operand_aliasing={{0}: (7, {})} | custom-call | flops 1000000000 | bytes 360000 | tf_op jit(solution)/shard_map/pallas_call | solution.py:24
  19.3 1.6 %collective-permute-done.3 = bf16[13,64,128]{2,1,0:T(8,128)(2,1)S(1)} collective-permute-done((bf16[13,64,128]{2,1,0:T(8,128)(2,1)}, bf16[13,64,128]{2,1,0:T(8,128)(2,1)S(1)}, u32[]{:S(2)}, u32[]{:S(2)}) %collective-permute-start.3) | collective-permute-done | bytes 213024 | tf_op jit(solution)/shard_map/ppermute | solution.py:367
  20.9 1.0 add_convert_fusion.3.refs_1_
  21.9 1.6 %collective-permute-start.4 = (bf16[13,64,128]{2,1,0:T(8,128)(2,1)S(1)}, bf16[13,64,128]{2,1,0:T(8,128)(2,1)S(1)}, u32[]{:S(2)}, u32[]{:S(2)}) collective-permute-start(bf16[13,64,128]{2,1,0:T(8,128)(2,1)S(1)} %add_convert_fusion.3.refs_1_), channel_id=1, source_target_pairs={{0,2},{1,3},{2,0},{3,1},{4,6},{5,7},{6,4},{7,5},{8,10},{9,11},{10,... | collective-permute-start | bytes 638984 | tf_op jit(solution)/shard_map/ppermute | solution.py:367
  25.0 4.3 %collective-permute-done.4.refs_2_ = bf16[13,64,128]{2,1,0:T(8,128)(2,1)S(1)} collective-permute-done((bf16[13,64,128]{2,1,0:T(8,128)(2,1)S(1)}, bf16[13,64,128]{2,1,0:T(8,128)(2,1)S(1)}, u32[]{:S(2)}, u32[]{:S(2)}) %collective-permute-start.4) | collective-permute-done | bytes 213024 | tf_op jit(solution)/shard_map/ppermute | solution.py:367
  30.0 6.1 %shard_map.132 = (bf16[4,64,2048]{2,1,0:T(8,128)(2,1)}, bf16[4,64,2048]{2,1,0:T(8,128)(2,1)}, bf16[4,64,2048]{2,1,0:T(8,128)(2,1)}) custom-call(s32[16]{0:T(128)} %get-tuple-element.45.refs_0_, bf16[13,64,128]{2,1,0:T(8,128)(2,1)} %copy-done.1, bf16[13,64,128]{2,1,0:T(8,128)(2,1)} %copy-done.3, bf16[1664,2048]{1,0:T(8,128)(2,1)} %refs_9_.2, ...), custom_call_target="tpu_custom_call" | custom-call | flops 1000000000 | bytes 360000 | tf_op jit(solution)/shard_map/pallas_call | solution.py:24
  36.1 1.6 %collective-permute-start.11 = (bf16[4,64,2048]{2,1,0:T(8,128)(2,1)}, bf16[4,64,2048]{2,1,0:T(8,128)(2,1)}, u32[]{:S(2)}, u32[]{:S(2)}) collective-permute-start(bf16[4,64,2048]{2,1,0:T(8,128)(2,1)} %get-tuple-element.34), channel_id=1, source_target_pairs={{4,8},{8,4},{5,9},{9,5},{6,10},{10,6},{7,11},{11,7},{20,24},{24,20... | collective-permute-start | bytes 3145736 | tf_op jit(solution)/shard_map/ppermute | solution.py:472
  37.7 10.9 %collective-permute-start.12 = (bf16[4,64,2048]{2,1,0:T(8,128)(2,1)}, bf16[4,64,2048]{2,1,0:T(8,128)(2,1)}, u32[]{:S(2)}, u32[]{:S(2)}) collective-permute-start(bf16[4,64,2048]{2,1,0:T(8,128)(2,1)} %get-tuple-element.27.refs_6_), channel_id=1, source_target_pairs={{0,4},{12,8},{4,0},{8,12},{1,5},{13,9},{5,1},{9,13},{2,6},{14,10},... | collective-permute-start | bytes 3145736 | tf_op jit(solution)/shard_map/ppermute | solution.py:471
  50.1 12.0 %shard_map.133 = (bf16[1664,256]{1,0:T(8,128)(2,1)}, bf16[1664,256]{1,0:T(8,128)(2,1)}, bf16[1664,256]{1,0:T(8,128)(2,1)}, bf16[1664,256]{1,0:T(8,128)(2,1)}) custom-call(s32[4]{0:T(128)} %pad_add_fusion.refs_0_, bf16[1664,2048]{1,0:T(8,128)(2,1)} %refs_9_.2, bf16[2048,1024]{1,0:T(8,128)(2,1)} %refs_5_.5, bf16[2048,1024]{1,0:T(8,128)(2,1)} %refs_5_.5, ...), custom_call_target="tpu_custom_call" | custom-call | flops 99999997952 | bytes 36000000 | tf_op jit(solution)/shard_map/pallas_call | solution.py:24
  62.6 6.1 %shard_map.134 = (bf16[4,64,2048]{2,1,0:T(8,128)(2,1)}, bf16[4,64,2048]{2,1,0:T(8,128)(2,1)}) custom-call(s32[16]{0:T(128)} %get-tuple-element.45.refs_0_, bf16[13,64,128]{2,1,0:T(8,128)(2,1)} %copy-done.1, bf16[13,64,128]{2,1,0:T(8,128)(2,1)} %copy-done.3, bf16[1664,2048]{1,0:T(8,128)(2,1)} %refs_9_.2, bf16[1664,2048]{1,0:T(8,128)(2,1)} %refs_9_.2, ...), custom_call_target="tpu_custom_call" | custom-call | flops 99999997952 | bytes 36000000 | tf_op jit(solution)/shard_map/pallas_call | solution.py:24
  68.8 1.1 add_convert_fusion.2.refs_1_
  69.9 1.5 %collective-permute-start.10 = (bf16[1664,256]{1,0:T(8,128)(2,1)}, bf16[1664,256]{1,0:T(8,128)(2,1)}, u32[]{:S(2)}, u32[]{:S(2)}) collective-permute-start(bf16[1664,256]{1,0:T(8,128)(2,1)} %add_convert_fusion.2.refs_1_), channel_id=1, source_target_pairs={{0,2},{1,3},{2,0},{3,1},{4,6},{5,7},{6,4},{7,5},{8,10},{9,11},{10,... | collective-permute-start | bytes 2555912 | tf_op jit(solution)/shard_map/ppermute | solution.py:367
  71.4 4.5 %collective-permute-start.20 = (bf16[4,64,2048]{2,1,0:T(8,128)(2,1)}, bf16[4,64,2048]{2,1,0:T(8,128)(2,1)}, u32[]{:S(2)}, u32[]{:S(2)}) collective-permute-start(bf16[4,64,2048]{2,1,0:T(8,128)(2,1)} %shard_map.139), channel_id=1, source_target_pairs={{0,4},{12,8},{1,5},{13,9},{2,6},{14,10},{3,7},{15,11},{16,20},{28,... | collective-permute-start | bytes 3145736 | tf_op jit(solution)/shard_map/ppermute | solution.py:477
  75.9 1.6 %add_convert_fusion.1.refs_14_.refs_1_ = bf16[4,64,2048]{2,1,0:T(8,128)(2,1)S(1)} fusion(bf16[4,64,2048]{2,1,0:T(8,128)(2,1)} %shard_map.135, bf16[4,64,2048]{2,1,0:T(8,128)(2,1)} %collective-permute-done.12.refs_1_, pred[]{:T(512)S(6)} %or.3), kind=kLoop, calls=%fused_computation.2 | loop fusion | flops 2621440 | bytes 3145729 | tf_op jit(solution)/shard_map/convert_element_type | solution.py:363
  77.6 0.9 copy-done
  78.5 7.8 %shard_map.136.refs_5_ = bf16[13,64,128]{2,1,0:T(8,128)(2,1)} custom-call(s32[13]{0:T(128)} %refs_0_.7, s32[1]{0:T(128)} %bitcast.7.refs_1_, bf16[13,64,2048]{2,1,0:T(8,128)(2,1)} %refs_5_.7, bf16[13,64,2048]{2,1,0:T(8,128)(2,1)} %refs_5_.7, bf16[13,64,2048]{2,1,0:T(8,128)(2,1)} %refs_5_.7, bf16[13,64,2048]{2,1,0:T(8,128)(2,1)} %refs_5_.7, ...), custom_call_target="tpu_custom_call" | custom-call | flops 99999997952 | bytes 36000000 | tf_op jit(solution)/shard_map/pallas_call | solution.py:24
  87.7 1.6 %collective-permute-start.14 = (bf16[13,64,128]{2,1,0:T(8,128)(2,1)S(1)}, bf16[13,64,128]{2,1,0:T(8,128)(2,1)S(1)}, u32[]{:S(2)}, u32[]{:S(2)}) collective-permute-start(bf16[13,64,128]{2,1,0:T(8,128)(2,1)S(1)} %copy-done.4), channel_id=1, source_target_pairs={{0,2},{1,3},{2,0},{3,1},{4,6},{5,7},{6,4},{7,5},{8,10},{9,11},{10,... | collective-permute-start | bytes 638984 | tf_op jit(solution)/shard_map/ppermute | solution.py:367
  89.2 6.3 %collective-permute-done.15.refs_8_ = bf16[13,64,128]{2,1,0:T(8,128)(2,1)S(1)} collective-permute-done((bf16[13,64,128]{2,1,0:T(8,128)(2,1)}, bf16[13,64,128]{2,1,0:T(8,128)(2,1)S(1)}, u32[]{:S(2)}, u32[]{:S(2)}) %collective-permute-start.15) | collective-permute-done | bytes 213024 | tf_op jit(solution)/shard_map/ppermute | solution.py:367
  96.3 1.1 collective-permute-start.13
  97.4 2.1 %convert_add_fusion = f32[4,64,2048]{2,1,0:T(8,128)S(1)} fusion(bf16[4,64,2048]{2,1,0:T(8,128)(2,1)} %shard_map.138, bf16[4,64,2048]{2,1,0:T(8,128)(2,1)} %collective-permute-done.11.refs_2_, bf16[4,64,2048]{2,1,0:T(8,128)(2,1)} %collective-permute-done.12.refs_1_, pred[]{:T(512)S(6)} %or.3), kind=kLoop, calls=%fused_computation.1 | loop fusion | flops 2097152 | bytes 5242881 | tf_op jit(solution)/shard_map/add | solution.py:479
  101.5 5.0 %shard_map.137 = (bf16[1664,256]{1,0:T(8,128)(2,1)}, bf16[384,256]{1,0:T(8,128)(2,1)}, bf16[384,256]{1,0:T(8,128)(2,1)}, bf16[384,256]{1,0:T(8,128)(2,1)}, bf16[384,256]{1,0:T(8,128)(2,1)}) custom-call(s32[13]{0:T(128)} %refs_0_.7, s32[16]{0:T(128)} %get-tuple-element.46.refs_1_, bf16[1664,256]{1,0:T(8,128)(2,1)} %get-tuple-element.29.refs_8_.refs_2_, ...), custom_call_target="tpu_custom_call" | custom-call | flops 1000000000 | bytes 360000 | tf_op jit(solution)/shard_map/pallas_call | solution.py:24
  106.5 0.8 collective-permute-start.16
  107.6 2.7 %collective-permute-start.18 = (bf16[384,256]{1,0:T(8,128)(2,1)}, bf16[384,256]{1,0:T(8,128)(2,1)}, u32[]{:S(2)}, u32[]{:S(2)}) collective-permute-start(bf16[384,256]{1,0:T(8,128)(2,1)} %get-tuple-element.39), channel_id=1, source_target_pairs={{0,12},{4,0},{8,4},{12,8},{1,13},{5,1},{9,5},{13,9},{2,14},{6,2},{... | collective-permute-start | bytes 589832 | tf_op jit(solution)/shard_map/ppermute | solution.py:349
  110.3 25.3 %collective-permute-done.19 = bf16[4,64,2048]{2,1,0:T(8,128)(2,1)} collective-permute-done((bf16[4,64,2048]{2,1,0:T(8,128)(2,1)S(1)}, bf16[4,64,2048]{2,1,0:T(8,128)(2,1)}, u32[]{:S(2)}, u32[]{:S(2)}) %collective-permute-start.19) | collective-permute-done | bytes 1048608 | tf_op jit(solution)/shard_map/ppermute | solution.py:476
  135.6 3.0 %add_convert_fusion.refs_6_ = bf16[4,64,2048]{2,1,0:T(8,128)(2,1)} fusion(bf16[4,64,2048]{2,1,0:T(8,128)(2,1)} %collective-permute-done.20, f32[4,64,2048]{2,1,0:T(8,128)S(1)} %convert_add_fusion, bf16[4,64,2048]{2,1,0:T(8,128)(2,1)} %collective-permute-done.19), kind=kLoop, calls=%fused_computation | loop fusion | flops 2621440 | bytes 5242880 | tf_op jit(solution)/shard_map/convert_element_type | solution.py:481
  138.6 0.8 collective-permute-done.17.refs_3_
  140.1 2.0 %shard_map.140 = (bf16[256,256]{1,0:T(8,128)(2,1)}, bf16[1664,256]{1,0:T(8,128)(2,1)}) custom-call(s32[1]{0:T(128)} %bitcast.1.refs_0_, bf16[384,256]{1,0:T(8,128)(2,1)} %get-tuple-element.36.refs_1_, bf16[384,256]{1,0:T(8,128)(2,1)} %copy-done.14, bf16[384,256]{1,0:T(8,128)(2,1)} %copy-done.15, ...), custom_call_target="tpu_custom_call", output_to_operand_aliasing={{1}: (5, {})} | custom-call | flops 1000000000 | bytes 360000 | tf_op jit(solution)/shard_map/pallas_call | solution.py:24
  (79 shorter events, 11.2 us)
Async XLA Ops:
  0.6 13.3 %copy-start.10 = (s32[4]{0:T(128)S(1)}, s32[4]{0:T(128)}, u32[]{:S(2)}) copy-start(s32[4]{0:T(128)} %constant.52.clone) | copy-start | bytes 52
  0.6 13.3 %copy-start.8 = (s32[4]{0:T(128)S(1)}, s32[4]{0:T(128)}, u32[]{:S(2)}) copy-start(s32[4]{0:T(128)} %param.11) | copy-start | bytes 52
  0.7 14.0 %copy-start.19 = (s32[16]{0:T(128)S(1)}, s32[16]{0:T(128)}, u32[]{:S(2)}) copy-start(s32[16]{0:T(128)} %param.14) | copy-start | bytes 196
  0.7 13.9 %copy-start.20 = (s32[13]{0:T(128)S(1)}, s32[13]{0:T(128)}, u32[]{:S(2)}) copy-start(s32[13]{0:T(128)} %param.12) | copy-start | bytes 160
  3.9 12.3 %collective-permute-start.2 = (bf16[1,64,256]{2,1,0:T(8,128)(2,1)}, bf16[1,64,256]{2,1,0:T(8,128)(2,1)S(1)}, u32[]{:S(2)}, u32[]{:S(2)}) collective-permute-start(bf16[1,64,256]{2,1,0:T(8,128)(2,1)} %get-tuple-element.24.refs_2_), channel_id=1, source_target_pairs={{0,12},{4,0},{8,4},{12,8},{1,13},{5,1},{9,5},{13,9},{2,14},{6,2},{... | collective-permute-start | bytes 98312 | tf_op jit(solution)/shard_map/ppermute | solution.py:349
  8.9 7.3 %collective-permute-start.1 = (bf16[1,64,256]{2,1,0:T(8,128)(2,1)}, bf16[1,64,256]{2,1,0:T(8,128)(2,1)S(1)}, u32[]{:S(2)}, u32[]{:S(2)}) collective-permute-start(bf16[1,64,256]{2,1,0:T(8,128)(2,1)} %get-tuple-element.24.refs_2_), channel_id=1, source_target_pairs={{0,8},{4,12},{8,0},{12,4},{1,9},{5,13},{9,1},{13,5},{2,10},{6,14},... | collective-permute-start | bytes 98312 | tf_op jit(solution)/shard_map/ppermute | solution.py:349
  8.9 7.3 %collective-permute-start = (bf16[1,64,256]{2,1,0:T(8,128)(2,1)}, bf16[1,64,256]{2,1,0:T(8,128)(2,1)S(1)}, u32[]{:S(2)}, u32[]{:S(2)}) collective-permute-start(bf16[1,64,256]{2,1,0:T(8,128)(2,1)} %get-tuple-element.24.refs_2_), channel_id=1, source_target_pairs={{0,4},{4,8},{8,12},{12,0},{1,5},{5,9},{9,13},{13,1},{2,6},{6,10},{... | collective-permute-start | bytes 98312 | tf_op jit(solution)/shard_map/ppermute | solution.py:349
  10.0 38.6 %collective-permute-start.7 = (bf16[1,64,2048]{2,1,0:T(8,128)(2,1)}, bf16[1,64,2048]{2,1,0:T(8,128)(2,1)S(1)}, u32[]{:S(2)}, u32[]{:S(2)}) collective-permute-start(bf16[1,64,2048]{2,1,0:T(8,128)(2,1)} %get-tuple-element.28.refs_10_), channel_id=1, source_target_pairs={{0,12},{4,0},{8,4},{12,8},{1,13},{5,1},{9,5},{13,9},{2,14},{6,2},{... | collective-permute-start | bytes 786440 | tf_op jit(solution)/shard_map/ppermute | solution.py:349
  12.8 35.8 %collective-permute-start.6 = (bf16[1,64,2048]{2,1,0:T(8,128)(2,1)}, bf16[1,64,2048]{2,1,0:T(8,128)(2,1)S(1)}, u32[]{:S(2)}, u32[]{:S(2)}) collective-permute-start(bf16[1,64,2048]{2,1,0:T(8,128)(2,1)} %get-tuple-element.28.refs_10_), channel_id=1, source_target_pairs={{0,8},{4,12},{8,0},{12,4},{1,9},{5,13},{9,1},{13,5},{2,10},{6,14},... | collective-permute-start | bytes 786440 | tf_op jit(solution)/shard_map/ppermute | solution.py:349
  16.2 32.4 %collective-permute-start.5 = (bf16[1,64,2048]{2,1,0:T(8,128)(2,1)}, bf16[1,64,2048]{2,1,0:T(8,128)(2,1)S(1)}, u32[]{:S(2)}, u32[]{:S(2)}) collective-permute-start(bf16[1,64,2048]{2,1,0:T(8,128)(2,1)} %get-tuple-element.28.refs_10_), channel_id=1, source_target_pairs={{0,4},{4,8},{8,12},{12,0},{1,5},{5,9},{9,13},{13,1},{2,6},{6,10},{... | collective-permute-start | bytes 786440 | tf_op jit(solution)/shard_map/ppermute | solution.py:349
  19.2 1.7 %collective-permute-start.3 = (bf16[13,64,128]{2,1,0:T(8,128)(2,1)}, bf16[13,64,128]{2,1,0:T(8,128)(2,1)S(1)}, u32[]{:S(2)}, u32[]{:S(2)}) collective-permute-start(bf16[13,64,128]{2,1,0:T(8,128)(2,1)} %get-tuple-element.26), channel_id=1, source_target_pairs={{0,1},{1,0},{2,3},{3,2},{4,5},{5,4},{6,7},{7,6},{8,9},{9,8},{10,11... | collective-permute-start | bytes 638984 | tf_op jit(solution)/shard_map/ppermute | solution.py:367
  21.9 7.4 %copy-start.1 = (bf16[13,64,128]{2,1,0:T(8,128)(2,1)}, bf16[13,64,128]{2,1,0:T(8,128)(2,1)S(1)}, u32[]{:S(2)}) copy-start(bf16[13,64,128]{2,1,0:T(8,128)(2,1)S(1)} %add_convert_fusion.3.refs_1_) | copy-start | bytes 638980
  21.9 7.4 %collective-permute-start.4 = (bf16[13,64,128]{2,1,0:T(8,128)(2,1)S(1)}, bf16[13,64,128]{2,1,0:T(8,128)(2,1)S(1)}, u32[]{:S(2)}, u32[]{:S(2)}) collective-permute-start(bf16[13,64,128]{2,1,0:T(8,128)(2,1)S(1)} %add_convert_fusion.3.refs_1_), channel_id=1, source_target_pairs={{0,2},{1,3},{2,0},{3,1},{4,6},{5,7},{6,4},{7,5},{8,10},{9,11},{10,... | collective-permute-start | bytes 638984 | tf_op jit(solution)/shard_map/ppermute | solution.py:367
  36.1 39.8 %collective-permute-start.11 = (bf16[4,64,2048]{2,1,0:T(8,128)(2,1)}, bf16[4,64,2048]{2,1,0:T(8,128)(2,1)}, u32[]{:S(2)}, u32[]{:S(2)}) collective-permute-start(bf16[4,64,2048]{2,1,0:T(8,128)(2,1)} %get-tuple-element.34), channel_id=1, source_target_pairs={{4,8},{8,4},{5,9},{9,5},{6,10},{10,6},{7,11},{11,7},{20,24},{24,20... | collective-permute-start | bytes 3145736 | tf_op jit(solution)/shard_map/ppermute | solution.py:472
  37.7 33.7 %collective-permute-start.12 = (bf16[4,64,2048]{2,1,0:T(8,128)(2,1)}, bf16[4,64,2048]{2,1,0:T(8,128)(2,1)}, u32[]{:S(2)}, u32[]{:S(2)}) collective-permute-start(bf16[4,64,2048]{2,1,0:T(8,128)(2,1)} %get-tuple-element.27.refs_6_), channel_id=1, source_target_pairs={{0,4},{12,8},{4,0},{8,12},{1,5},{13,9},{5,1},{9,13},{2,6},{14,10},... | collective-permute-start | bytes 3145736 | tf_op jit(solution)/shard_map/ppermute | solution.py:471
  48.6 0.8 copy-start.12
  62.1 25.6 %collective-permute-start.8 = (bf16[1664,256]{1,0:T(8,128)(2,1)}, bf16[1664,256]{1,0:T(8,128)(2,1)}, u32[]{:S(2)}, u32[]{:S(2)}) collective-permute-start(bf16[1664,256]{1,0:T(8,128)(2,1)} %get-tuple-element.30), channel_id=1, source_target_pairs={{0,1},{1,0},{2,3},{3,2},{4,5},{5,4},{6,7},{7,6},{8,9},{9,8},{10,11... | collective-permute-start | bytes 2555912 | tf_op jit(solution)/shard_map/ppermute | solution.py:367
  62.1 6.7 %collective-permute-start.9 = (bf16[1664,256]{1,0:T(8,128)(2,1)}, bf16[1664,256]{1,0:T(8,128)(2,1)S(1)}, u32[]{:S(2)}, u32[]{:S(2)}) collective-permute-start(bf16[1664,256]{1,0:T(8,128)(2,1)} %get-tuple-element.32), channel_id=1, source_target_pairs={{0,1},{1,0},{2,3},{3,2},{4,5},{5,4},{6,7},{7,6},{8,9},{9,8},{10,11... | collective-permute-start | bytes 2555912 | tf_op jit(solution)/shard_map/ppermute | solution.py:367
  62.6 6.2 %copy-start.2 = (bf16[1664,256]{1,0:T(8,128)(2,1)S(1)}, bf16[1664,256]{1,0:T(8,128)(2,1)}, u32[]{:S(2)}) copy-start(bf16[1664,256]{1,0:T(8,128)(2,1)} %get-tuple-element.31) | copy-start | bytes 2555908
  69.9 31.0 %collective-permute-start.10 = (bf16[1664,256]{1,0:T(8,128)(2,1)}, bf16[1664,256]{1,0:T(8,128)(2,1)}, u32[]{:S(2)}, u32[]{:S(2)}) collective-permute-start(bf16[1664,256]{1,0:T(8,128)(2,1)} %add_convert_fusion.2.refs_1_), channel_id=1, source_target_pairs={{0,2},{1,3},{2,0},{3,1},{4,6},{5,7},{6,4},{7,5},{8,10},{9,11},{10,... | collective-permute-start | bytes 2555912 | tf_op jit(solution)/shard_map/ppermute | solution.py:367
  71.4 38.9 %collective-permute-start.20 = (bf16[4,64,2048]{2,1,0:T(8,128)(2,1)}, bf16[4,64,2048]{2,1,0:T(8,128)(2,1)}, u32[]{:S(2)}, u32[]{:S(2)}) collective-permute-start(bf16[4,64,2048]{2,1,0:T(8,128)(2,1)} %shard_map.139), channel_id=1, source_target_pairs={{0,4},{12,8},{1,5},{13,9},{2,6},{14,10},{3,7},{15,11},{16,20},{28,... | collective-permute-start | bytes 3145736 | tf_op jit(solution)/shard_map/ppermute | solution.py:477
  77.5 1.0 copy-start
  77.5 8.9 %copy-start.9 = (s32[4]{0:T(128)S(1)}, s32[4]{0:T(128)}, u32[]{:S(2)}) copy-start(s32[4]{0:T(128)} %param.11) | copy-start | bytes 52
  77.5 58.1 %collective-permute-start.19 = (bf16[4,64,2048]{2,1,0:T(8,128)(2,1)S(1)}, bf16[4,64,2048]{2,1,0:T(8,128)(2,1)}, u32[]{:S(2)}, u32[]{:S(2)}) collective-permute-start(bf16[4,64,2048]{2,1,0:T(8,128)(2,1)S(1)} %add_convert_fusion.1.refs_14_.refs_1_), channel_id=1, source_target_pairs={{0,8},{12,4},{4,12},{8,0},{1,9},{13,5},{5,13},{9,1},{2,10},{14,6},... | collective-permute-start | bytes 3145736 | tf_op jit(solution)/shard_map/ppermute | solution.py:476
  86.3 1.4 copy-start.4
  86.3 9.3 %collective-permute-start.15 = (bf16[13,64,128]{2,1,0:T(8,128)(2,1)}, bf16[13,64,128]{2,1,0:T(8,128)(2,1)S(1)}, u32[]{:S(2)}, u32[]{:S(2)}) collective-permute-start(bf16[13,64,128]{2,1,0:T(8,128)(2,1)} %shard_map.136.refs_5_), channel_id=1, source_target_pairs={{0,3},{1,2},{2,1},{3,0},{4,7},{5,6},{6,5},{7,4},{8,11},{9,10},{10,... | collective-permute-start | bytes 638984 | tf_op jit(solution)/shard_map/ppermute | solution.py:367
  87.7 12.5 %collective-permute-start.14 = (bf16[13,64,128]{2,1,0:T(8,128)(2,1)S(1)}, bf16[13,64,128]{2,1,0:T(8,128)(2,1)S(1)}, u32[]{:S(2)}, u32[]{:S(2)}) collective-permute-start(bf16[13,64,128]{2,1,0:T(8,128)(2,1)S(1)} %copy-done.4), channel_id=1, source_target_pairs={{0,2},{1,3},{2,0},{3,1},{4,6},{5,7},{6,4},{7,5},{8,10},{9,11},{10,... | collective-permute-start | bytes 638984 | tf_op jit(solution)/shard_map/ppermute | solution.py:367
  96.3 3.9 %collective-permute-start.13 = (bf16[13,64,128]{2,1,0:T(8,128)(2,1)S(1)}, bf16[13,64,128]{2,1,0:T(8,128)(2,1)S(1)}, u32[]{:S(2)}, u32[]{:S(2)}) collective-permute-start(bf16[13,64,128]{2,1,0:T(8,128)(2,1)S(1)} %copy-done.4), channel_id=1, source_target_pairs={{0,1},{1,0},{2,3},{3,2},{4,5},{5,4},{6,7},{7,6},{8,9},{9,8},{10,11... | collective-permute-start | bytes 638984 | tf_op jit(solution)/shard_map/ppermute | solution.py:367
  106.5 32.1 %collective-permute-start.16 = (bf16[384,256]{1,0:T(8,128)(2,1)}, bf16[384,256]{1,0:T(8,128)(2,1)S(1)}, u32[]{:S(2)}, u32[]{:S(2)}) collective-permute-start(bf16[384,256]{1,0:T(8,128)(2,1)} %get-tuple-element.37), channel_id=1, source_target_pairs={{0,4},{4,8},{8,12},{12,0},{1,5},{5,9},{9,13},{13,1},{2,6},{6,10},{... | collective-permute-start | bytes 589832 | tf_op jit(solution)/shard_map/ppermute | solution.py:349
  107.2 32.2 %collective-permute-start.17 = (bf16[384,256]{1,0:T(8,128)(2,1)}, bf16[384,256]{1,0:T(8,128)(2,1)S(1)}, u32[]{:S(2)}, u32[]{:S(2)}) collective-permute-start(bf16[384,256]{1,0:T(8,128)(2,1)} %get-tuple-element.38), channel_id=1, source_target_pairs={{0,8},{4,12},{8,0},{12,4},{1,9},{5,13},{9,1},{13,5},{2,10},{6,14},... | collective-permute-start | bytes 589832 | tf_op jit(solution)/shard_map/ppermute | solution.py:349
  107.6 31.8 %collective-permute-start.18 = (bf16[384,256]{1,0:T(8,128)(2,1)}, bf16[384,256]{1,0:T(8,128)(2,1)}, u32[]{:S(2)}, u32[]{:S(2)}) collective-permute-start(bf16[384,256]{1,0:T(8,128)(2,1)} %get-tuple-element.39), channel_id=1, source_target_pairs={{0,12},{4,0},{8,4},{12,8},{1,13},{5,1},{9,5},{13,9},{2,14},{6,2},{... | collective-permute-start | bytes 589832 | tf_op jit(solution)/shard_map/ppermute | solution.py:349
  138.6 0.8 copy-start.14
  (10 other events, 6.7 us)

commit v7 on v6

--- a/solution.py
+++ b/solution.py
@@ -60,13 +60,12 @@
     return jnp.where(live, ranks, 0.0).astype(rows.dtype)
 
 
-def kept_ranks(lengths, maps, features, others):
+def kept_ranks(lengths, maps, features, others, tokens=()):
     blocks, rank, width = maps.shape
     kept = blocks - SW
-    last_shapes = [(SW, rank, width), (SW, *others.shape[1:])]
-
-    def kernel(lengths_ref, maps_ref, rows_ref, others_ref, out_ref, last_ref, last_other):
-        last_ref[...] = maps_ref[kept:]
+    last_shape = (SW, *others.shape[1:])
+
+    def kernel(lengths_ref, maps_ref, rows_ref, others_ref, out_ref, last_other):
         last_other[...] = others_ref[...]
         for k in range(kept):
             out_ref[k] = masked_rank(maps_ref[k], rows_ref[k * BLOCK : (k + 1) * BLOCK], lengths_ref[k])
@@ -76,12 +75,15 @@
         (lengths,),
         (1,),
         [
-            whole(maps),
-            whole(features),
-            (others, pl.BlockSpec(last_shapes[1], lambda i, *_: (kept, 0, 0), pipeline_mode=pl.Buffered(1))),
+            (maps, pl.BlockSpec((kept, rank, width), lambda i, *_: (0, 0, 0), pipeline_mode=pl.Buffered(1))),
+            (features, pl.BlockSpec((kept * BLOCK, width), lambda i, *_: (0, 0), pipeline_mode=pl.Buffered(1))),
+            (others, pl.BlockSpec(last_shape, lambda i, *_: (kept, 0, 0), pipeline_mode=pl.Buffered(1))),
         ],
-        [((blocks, rank, BLOCK), features.dtype, pl.BlockSpec((kept, rank, BLOCK), lambda i, *_: (0, 0, 0)))]
-        + [(shape, features.dtype, constant_spec(shape)) for shape in last_shapes],
+        [
+            ((blocks, rank, BLOCK), features.dtype, pl.BlockSpec((kept, rank, BLOCK), lambda i, *_: (0, 0, 0))),
+            (last_shape, features.dtype, constant_spec(last_shape)),
+        ],
+        tokens,
     )
 
 
@@ -427,11 +429,12 @@
     order = jnp.arange(devices, dtype=jnp.int32)
     holder = jnp.sum(jnp.where(partner == me, order, 0))
 
-    cot_terms, up_own, down_own = kept_ranks(lengths, adapter_up_matrix, cotangent, adapter_down_rows)
+    up_own = adapter_up_matrix[kept:]
     up_choices, up_pick = shifted(up_own, holder)
-    down_choices, down_pick = shifted(down_own, holder)
+    cot_terms, down_own = kept_ranks(lengths, adapter_up_matrix, cotangent, adapter_down_rows, [up_own])
     cot_terms, up_last = with_last_rank(lengths, up_pick, up_choices, cotangent, cot_terms)
     rank_cot = exchanged(cot_terms)
+    down_choices, down_pick = shifted(after(down_own, rank_cot[0]), holder)
 
     table_rows = jnp.sum(
         jnp.where(
@@ -450,9 +453,11 @@
     columns = jnp.stack([column ^ 3, column ^ 2, column ^ 1, column]).astype(jnp.int32)
 
     def base(*tokens):
-        sent, away, given, mine = base_terms(columns, hidden, frozen_value_weight, tokens)
-        away = add(away, near(sent))
-        return (mine, near(given), far(away)), away
+        return base_terms(columns, hidden, frozen_value_weight, tokens)
+
+    def base_parts(terms, *tokens):
+        sent, away, given, mine = terms
+        return mine, near(given), far(add(after(away, *tokens), near(sent)))
 
     def inputs(*tokens):
         return spread(
@@ -470,11 +475,12 @@
         first, third, third_too = down_rows(codes, 0, 2, 2, rank_cot, hidden)
         from_first = lax.ppermute(first, "dp", [(0, 1), (3, 2), (1, 0), (2, 3)])
         from_inner = lax.ppermute(third, "dp", [(1, 2), (2, 1)])
-        base_sums, away = base(first, *down_choices[1:])
-        second, own = down_rows(codes, 2 * OWN, 2, 1, rank_cot, hidden, [base_sums[0]], 100.0)
-        second = add(after(second, away, from_inner), jnp.where(inner, from_first, jnp.zeros((), first.dtype)))
+        second, own = down_rows(codes, 2 * OWN, 2, 1, rank_cot, hidden, [first], 1.0)
+        terms = base(second, *down_choices[1:])
+        second = add(after(second, terms[0], from_inner), jnp.where(inner, from_first, jnp.zeros((), first.dtype)))
+        base_sums = base_parts(terms, second)
         from_second = lax.ppermute(second, "dp", [(0, 2), (3, 1), (1, 3), (2, 0)])
-        from_third = lax.ppermute(after(third_too, from_first), "dp", [(0, 1), (3, 2)])
+        from_third = lax.ppermute(after(third_too, second), "dp", [(0, 1), (3, 2)])
         near_total = lax.optimization_barrier(
             after(own, second).astype(jnp.float32) + jnp.where(inner, from_inner, from_first).astype(jnp.float32)
         )
@@ -489,7 +495,7 @@
         codes = codes_of(order)
         (table,) = down_rows(codes, 0, devices, 0, rank_cot, hidden)
         down_out = line_reduce_scatter(table.reshape(devices, OWN, *table.shape[1:]))
-        values, table = outputs(codes, [devices * OWN], base(table)[0], inputs(table))
+        values, table = outputs(codes, [devices * OWN], base_parts(base(table)), inputs(table))
         up_table, last_values = table[:-BLOCK], table[-BLOCK:]
         up_out = line_reduce_scatter(up_table.reshape(devices, OWN, -1, values.shape[1]))
         (last_values,), _ = shifted(last_values, partner[me])

time: 143 us -> 138 us (0.965)
  starting transfers between devices: 37.3 us -> 31.5 us
  other arithmetic: 11.9 us -> 14.3 us
  waiting for transfers between devices: 39 us -> 36.7 us
    ppermute x1, waiting for transfers between devices: 25.3 us -> 6.78 us  [body(): from_second = lax.ppermute(second, 'dp', [(0, 2), (3, 1), (1, 3), (2, 0)])]
    ppermute x9, waiting for transfers between devices: 0.84 us -> 7.52 us  [shift(): lax.ppermute(array, 'dp', [(i, (i + by) % size) for i in range(size)])]
    ppermute x1, starting transfers between devices: 10.9 us -> 4.35 us  [body(): from_first = lax.ppermute(first, 'dp', [(0, 1), (3, 2), (1, 0), (2, 3)])]
    ppermute x1, waiting for transfers between devices: 0.01 us -> 6.15 us  [body(): from_first = lax.ppermute(first, 'dp', [(0, 1), (3, 2), (1, 0), (2, 3)])]
    ppermute x1, waiting for transfers between devices: 0.01 us -> 3.79 us  [body(): from_third = lax.ppermute(after(third_too, second), 'dp', [(0, 1), (3, 2)])]
    ppermute x1, starting transfers between devices: 0.07 us -> 3.18 us  [body(): from_second = lax.ppermute(second, 'dp', [(0, 2), (3, 1), (1, 3), (2, 0)])]
    convert_element_type x3, other arithmetic: 3.73 us -> 5.52 us  [add(): sum((array.astype(jnp.float32) for array in arrays)).astype(arrays[0].dtype)]
    unnamed x42 -> x44, local copies, waits for them, and re-layouts: 6.43 us -> 5.91 us
  transfers between devices with their start and end apart: 21 -> 21, of which waited for: 6 -> 8; matrix products, arithmetic and copies ran while one was open for 9% -> 10% of each run, Pallas kernels for 28% -> 30%
where the time goes in v7:
time: 138 us; the launch traced here: 137 us
  Pallas kernels  45 us (33%)
  waiting for transfers between devices  36.7 us (27%)
  starting transfers between devices  31.5 us (23%)
  other arithmetic  14.3 us (10%)
  local copies, waits for them, and re-layouts  7.43 us (5%)
  between operations  2.22 us (2%)
    pallas_call x13, Pallas kernels, call(): pl.pallas_call(run, grid_spec=pltpu.PrefetchScalarGridSpec(num_scalar_pre...  45 us
    ppermute x9, starting transfers between devices, shift(): lax.ppermute(array, 'dp', [(i, (i + by) % size) for i in range(size)])  13.8 us
    ppermute x8, waiting for transfers between devices, crossed(): lax.ppermute(array, 'tensor', [(i, i ^ by) for i in range(lax.axis_size('...  12.4 us
    ppermute x9, waiting for transfers between devices, shift(): lax.ppermute(array, 'dp', [(i, (i + by) % size) for i in range(size)])  7.52 us
    ppermute x1, waiting for transfers between devices, body(): from_second = lax.ppermute(second, 'dp', [(0, 2), (3, 1), (1, 3), (2, 0)])  6.78 us
    ppermute x8, starting transfers between devices, crossed(): lax.ppermute(array, 'tensor', [(i, i ^ by) for i in range(lax.axis_size('...  6.28 us
    ppermute x1, waiting for transfers between devices, body(): from_first = lax.ppermute(first, 'dp', [(0, 1), (3, 2), (1, 0), (2, 3)])  6.15 us
    unnamed x44, local copies, waits for them, and re-layouts  5.91 us
  transfers between devices with their start and end apart: 21, of which 8 were waited for; matrix products, arithmetic and copies ran while one was open for 10% of the time, Pallas kernels for 30%

profile of v7, /device:TPU:0, one launch (start us, length us, event | category | flops | bytes accessed | tf_op | source)
XLA Modules:
  0.0 137.0 jit_solution(1470079451920951855)
XLA Ops:
  1.4 5.0 %collective-permute-start.2 = (bf16[1,64,256]{2,1,0:T(8,128)(2,1)S(1)}, bf16[1,64,256]{2,1,0:T(8,128)(2,1)S(1)}, u32[]{:S(2)}, u32[]{:S(2)}) collective-permute-start(bf16[1,64,256]{2,1,0:T(8,128)(2,1)S(1)} %slice.3.refs_4_.refs_2_), channel_id=1, source_target_pairs={{0,12},{4,0},{8,4},{12,8},{1,13},{5,1},{9,5},{13,9},{2,14},{6,2},{... | collective-permute-start | bytes 98312 | tf_op jit(solution)/shard_map/ppermute | solution.py:351
  7.5 1.3 fusion.1
  9.6 3.0 %shard_map.130 = (bf16[13,64,128]{2,1,0:T(8,128)(2,1)}, bf16[1,64,2048]{2,1,0:T(8,128)(2,1)}) custom-call(s32[13]{0:T(128)} %refs_0_.7, bf16[13,64,256]{2,1,0:T(8,128)(2,1)} %refs_10_.1, bf16[1664,256]{1,0:T(8,128)(2,1)} %refs_9_.3, bf16[13,64,2048]{2,1,0:T(8,128)(2,1)} %refs_5_.7, bf16[1,64,256]{2,1,0:T(8,128)(2,1)} %copy-done.10), custom_call_target="tpu_custom_call" | custom-call | flops 1000000000 | bytes 360000 | tf_op jit(solution)/shard_map/pallas_call | solution.py:24
  14.2 2.3 %shard_map.131 = (bf16[13,64,128]{2,1,0:T(8,128)(2,1)}, bf16[1,64,256]{2,1,0:T(8,128)(2,1)}) custom-call(s32[13]{0:T(128)} %refs_0_.7, s32[1]{0:T(128)} %bitcast.7.refs_1_, bf16[1,64,256]{2,1,0:T(8,128)(2,1)} %copy-done.10, bf16[1,64,256]{2,1,0:T(8,128)(2,1)} %copy-done.19, bf16[1,64,256]{2,1,0:T(8,128)(2,1)} %copy-done.18, ...), custom_call_target="tpu_custom_call", output_to_operand_aliasing={{0}: (7, {})} | custom-call | flops 1000000000 | bytes 360000 | tf_op jit(solution)/shard_map/pallas_call | solution.py:24
  16.7 1.5 %collective-permute-done.3 = bf16[13,64,128]{2,1,0:T(8,128)(2,1)S(1)} collective-permute-done((bf16[13,64,128]{2,1,0:T(8,128)(2,1)}, bf16[13,64,128]{2,1,0:T(8,128)(2,1)S(1)}, u32[]{:S(2)}, u32[]{:S(2)}) %collective-permute-start.3) | collective-permute-done | bytes 213024 | tf_op jit(solution)/shard_map/ppermute | solution.py:369
  19.2 1.6 %collective-permute-start.4 = (bf16[13,64,128]{2,1,0:T(8,128)(2,1)S(1)}, bf16[13,64,128]{2,1,0:T(8,128)(2,1)S(1)}, u32[]{:S(2)}, u32[]{:S(2)}) collective-permute-start(bf16[13,64,128]{2,1,0:T(8,128)(2,1)S(1)} %add_convert_fusion.3.refs_1_), channel_id=1, source_target_pairs={{0,2},{1,3},{2,0},{3,1},{4,6},{5,7},{6,4},{7,5},{8,10},{9,11},{10,... | collective-permute-start | bytes 638984 | tf_op jit(solution)/shard_map/ppermute | solution.py:369
  21.5 2.8 %collective-permute-start.7 = (bf16[1,64,2048]{2,1,0:T(8,128)(2,1)}, bf16[1,64,2048]{2,1,0:T(8,128)(2,1)S(1)}, u32[]{:S(2)}, u32[]{:S(2)}) collective-permute-start(bf16[1,64,2048]{2,1,0:T(8,128)(2,1)} %shard_map.134.refs_10_), channel_id=1, source_target_pairs={{0,12},{4,0},{8,4},{12,8},{1,13},{5,1},{9,5},{13,9},{2,14},{6,2},{... | collective-permute-start | bytes 786440 | tf_op jit(solution)/shard_map/ppermute | solution.py:351
  24.3 1.1 collective-permute-start.6
  27.3 6.1 %shard_map.132 = (bf16[4,64,2048]{2,1,0:T(8,128)(2,1)}, bf16[4,64,2048]{2,1,0:T(8,128)(2,1)}, bf16[4,64,2048]{2,1,0:T(8,128)(2,1)}) custom-call(s32[16]{0:T(128)} %get-tuple-element.43.refs_0_, bf16[13,64,128]{2,1,0:T(8,128)(2,1)} %copy-done.3, bf16[13,64,128]{2,1,0:T(8,128)(2,1)} %copy-done.4, bf16[1664,2048]{1,0:T(8,128)(2,1)} %refs_9_.2, ...), custom_call_target="tpu_custom_call" | custom-call | flops 1000000000 | bytes 360000 | tf_op jit(solution)/shard_map/pallas_call | solution.py:24
  34.0 4.3 %collective-permute-start.10 = (bf16[4,64,2048]{2,1,0:T(8,128)(2,1)}, bf16[4,64,2048]{2,1,0:T(8,128)(2,1)S(1)}, u32[]{:S(2)}, u32[]{:S(2)}) collective-permute-start(bf16[4,64,2048]{2,1,0:T(8,128)(2,1)} %get-tuple-element.25.refs_8_), channel_id=1, source_target_pairs={{0,4},{12,8},{4,0},{8,12},{1,5},{13,9},{5,1},{9,13},{2,6},{14,10},... | collective-permute-start | bytes 3145736 | tf_op jit(solution)/shard_map/ppermute | solution.py:476
  38.4 6.8 %shard_map.133 = (bf16[4,64,2048]{2,1,0:T(8,128)(2,1)}, bf16[4,64,2048]{2,1,0:T(8,128)(2,1)}) custom-call(s32[16]{0:T(128)} %get-tuple-element.43.refs_0_, bf16[13,64,128]{2,1,0:T(8,128)(2,1)} %copy-done.3, bf16[13,64,128]{2,1,0:T(8,128)(2,1)} %copy-done.4, bf16[1664,2048]{1,0:T(8,128)(2,1)} %refs_9_.2, bf16[1664,2048]{1,0:T(8,128)(2,1)} %refs_9_.2, ...), custom_call_target="tpu_custom_call" | custom-call | flops 1000000000 | bytes 360000 | tf_op jit(solution)/shard_map/pallas_call | solution.py:24
  45.2 4.5 %collective-permute-done.6.refs_8_.refs_12_ = bf16[1,64,2048]{2,1,0:T(8,128)(2,1)S(1)} collective-permute-done((bf16[1,64,2048]{2,1,0:T(8,128)(2,1)}, bf16[1,64,2048]{2,1,0:T(8,128)(2,1)S(1)}, u32[]{:S(2)}, u32[]{:S(2)}) %collective-permute-start.6) | collective-permute-done | bytes 262176 | tf_op jit(solution)/shard_map/ppermute | solution.py:351
  50.5 12.0 %shard_map.135 = (bf16[1664,256]{1,0:T(8,128)(2,1)}, bf16[1664,256]{1,0:T(8,128)(2,1)}, bf16[1664,256]{1,0:T(8,128)(2,1)}, bf16[1664,256]{1,0:T(8,128)(2,1)}) custom-call(s32[4]{0:T(128)} %pad_add_fusion.refs_0_, bf16[1664,2048]{1,0:T(8,128)(2,1)} %refs_9_.2, bf16[2048,1024]{1,0:T(8,128)(2,1)} %refs_5_.6, bf16[2048,1024]{1,0:T(8,128)(2,1)} %refs_5_.6, ...), custom_call_target="tpu_custom_call" | custom-call | flops 99999997952 | bytes 36000000 | tf_op jit(solution)/shard_map/pallas_call | solution.py:24
  63.0 1.0 copy-done.2
  64.0 6.1 %collective-permute-done.10 = bf16[4,64,2048]{2,1,0:T(8,128)(2,1)S(1)} collective-permute-done((bf16[4,64,2048]{2,1,0:T(8,128)(2,1)}, bf16[4,64,2048]{2,1,0:T(8,128)(2,1)S(1)}, u32[]{:S(2)}, u32[]{:S(2)}) %collective-permute-start.10) | collective-permute-done | bytes 1048608 | tf_op jit(solution)/shard_map/ppermute | solution.py:476
  70.2 2.0 %add_convert_fusion.1.refs_1_.refs_14_ = bf16[4,64,2048]{2,1,0:T(8,128)(2,1)S(1)} fusion(bf16[4,64,2048]{2,1,0:T(8,128)(2,1)} %shard_map.136, bf16[4,64,2048]{2,1,0:T(8,128)(2,1)S(1)} %collective-permute-done.10, pred[]{:T(512)S(6)} %or.3), kind=kLoop, calls=%fused_computation.2 | loop fusion | flops 2621440 | bytes 3145729 | tf_op jit(solution)/shard_map/convert_element_type | solution.py:365
  72.2 3.2 %collective-permute-start.19 = (bf16[4,64,2048]{2,1,0:T(8,128)(2,1)S(1)}, bf16[4,64,2048]{2,1,0:T(8,128)(2,1)}, u32[]{:S(2)}, u32[]{:S(2)}) collective-permute-start(bf16[4,64,2048]{2,1,0:T(8,128)(2,1)S(1)} %add_convert_fusion.1.refs_1_.refs_14_), channel_id=1, source_target_pairs={{0,8},{12,4},{4,12},{8,0},{1,9},{13,5},{5,13},{9,1},{2,10},{14,6},... | collective-permute-start | bytes 3145736 | tf_op jit(solution)/shard_map/ppermute | solution.py:482
  75.4 2.5 %add_convert_fusion.2 = bf16[1664,256]{1,0:T(8,128)(2,1)} fusion(bf16[1664,256]{1,0:T(8,128)(2,1)} %collective-permute-done.11, bf16[1664,256]{1,0:T(8,128)(2,1)} %shard_map.137), kind=kLoop, calls=%fused_computation.3 | loop fusion | flops 1703936 | bytes 2555904 | tf_op jit(solution)/shard_map/convert_element_type | solution.py:365
  78.5 3.1 %collective-permute-start.20 = (bf16[4,64,2048]{2,1,0:T(8,128)(2,1)}, bf16[4,64,2048]{2,1,0:T(8,128)(2,1)}, u32[]{:S(2)}, u32[]{:S(2)}) collective-permute-start(bf16[4,64,2048]{2,1,0:T(8,128)(2,1)} %shard_map.141), channel_id=1, source_target_pairs={{0,4},{12,8},{1,5},{13,9},{2,6},{14,10},{3,7},{15,11},{16,20},{28,... | collective-permute-start | bytes 3145736 | tf_op jit(solution)/shard_map/ppermute | solution.py:483
  81.6 7.8 %shard_map.138.refs_5_ = bf16[13,64,128]{2,1,0:T(8,128)(2,1)} custom-call(s32[13]{0:T(128)} %refs_0_.7, s32[1]{0:T(128)} %bitcast.7.refs_1_, bf16[13,64,2048]{2,1,0:T(8,128)(2,1)} %refs_5_.7, bf16[13,64,2048]{2,1,0:T(8,128)(2,1)} %refs_5_.7, bf16[13,64,2048]{2,1,0:T(8,128)(2,1)} %refs_5_.7, bf16[13,64,2048]{2,1,0:T(8,128)(2,1)} %refs_5_.7, ...), custom_call_target="tpu_custom_call" | custom-call | flops 99999997952 | bytes 36000000 | tf_op jit(solution)/shard_map/pallas_call | solution.py:24
  90.8 1.6 %collective-permute-start.14 = (bf16[13,64,128]{2,1,0:T(8,128)(2,1)S(1)}, bf16[13,64,128]{2,1,0:T(8,128)(2,1)S(1)}, u32[]{:S(2)}, u32[]{:S(2)}) collective-permute-start(bf16[13,64,128]{2,1,0:T(8,128)(2,1)S(1)} %copy-done.6), channel_id=1, source_target_pairs={{0,2},{1,3},{2,0},{3,1},{4,6},{5,7},{6,4},{7,5},{8,10},{9,11},{10,... | collective-permute-start | bytes 638984 | tf_op jit(solution)/shard_map/ppermute | solution.py:369
  92.3 10.4 %collective-permute-done.15.refs_8_ = bf16[13,64,128]{2,1,0:T(8,128)(2,1)S(1)} collective-permute-done((bf16[13,64,128]{2,1,0:T(8,128)(2,1)}, bf16[13,64,128]{2,1,0:T(8,128)(2,1)S(1)}, u32[]{:S(2)}, u32[]{:S(2)}) %collective-permute-start.15) | collective-permute-done | bytes 213024 | tf_op jit(solution)/shard_map/ppermute | solution.py:369
  103.4 2.1 %collective-permute-start.13 = (bf16[13,64,128]{2,1,0:T(8,128)(2,1)S(1)}, bf16[13,64,128]{2,1,0:T(8,128)(2,1)S(1)}, u32[]{:S(2)}, u32[]{:S(2)}) collective-permute-start(bf16[13,64,128]{2,1,0:T(8,128)(2,1)S(1)} %copy-done.6), channel_id=1, source_target_pairs={{0,1},{1,0},{2,3},{3,2},{4,5},{5,4},{6,7},{7,6},{8,9},{9,8},{10,11... | collective-permute-start | bytes 638984 | tf_op jit(solution)/shard_map/ppermute | solution.py:369
  105.5 2.1 %convert_add_fusion = f32[4,64,2048]{2,1,0:T(8,128)S(1)} fusion(bf16[4,64,2048]{2,1,0:T(8,128)(2,1)} %shard_map.140, bf16[4,64,2048]{2,1,0:T(8,128)(2,1)} %copy-done.2, bf16[4,64,2048]{2,1,0:T(8,128)(2,1)} %copy-done.1, pred[]{:T(512)S(6)} %or.3), kind=kLoop, calls=%fused_computation.1 | loop fusion | flops 2097152 | bytes 5242881 | tf_op jit(solution)/shard_map/add | solution.py:485
  109.0 5.0 %shard_map.139 = (bf16[1664,256]{1,0:T(8,128)(2,1)}, bf16[384,256]{1,0:T(8,128)(2,1)}, bf16[384,256]{1,0:T(8,128)(2,1)}, bf16[384,256]{1,0:T(8,128)(2,1)}, bf16[384,256]{1,0:T(8,128)(2,1)}) custom-call(s32[13]{0:T(128)} %refs_0_.7, s32[16]{0:T(128)} %get-tuple-element.44.refs_1_, bf16[1664,256]{1,0:T(8,128)(2,1)} %get-tuple-element.28.refs_2_, ...), custom_call_target="tpu_custom_call" | custom-call | flops 1000000000 | bytes 360000 | tf_op jit(solution)/shard_map/pallas_call | solution.py:24
  114.2 2.0 %collective-permute-start.17 = (bf16[384,256]{1,0:T(8,128)(2,1)}, bf16[384,256]{1,0:T(8,128)(2,1)S(1)}, u32[]{:S(2)}, u32[]{:S(2)}) collective-permute-start(bf16[384,256]{1,0:T(8,128)(2,1)} %get-tuple-element.36), channel_id=1, source_target_pairs={{0,8},{4,12},{8,0},{12,4},{1,9},{5,13},{9,1},{13,5},{2,10},{6,14},... | collective-permute-start | bytes 589832 | tf_op jit(solution)/shard_map/ppermute | solution.py:351
  116.2 1.6 %collective-permute-start.18 = (bf16[384,256]{1,0:T(8,128)(2,1)}, bf16[384,256]{1,0:T(8,128)(2,1)}, u32[]{:S(2)}, u32[]{:S(2)}) collective-permute-start(bf16[384,256]{1,0:T(8,128)(2,1)} %get-tuple-element.37), channel_id=1, source_target_pairs={{0,12},{4,0},{8,4},{12,8},{1,13},{5,1},{9,5},{13,9},{2,14},{6,2},{... | collective-permute-start | bytes 589832 | tf_op jit(solution)/shard_map/ppermute | solution.py:351
  117.8 3.8 %collective-permute-done.20 = bf16[4,64,2048]{2,1,0:T(8,128)(2,1)} collective-permute-done((bf16[4,64,2048]{2,1,0:T(8,128)(2,1)}, bf16[4,64,2048]{2,1,0:T(8,128)(2,1)}, u32[]{:S(2)}, u32[]{:S(2)}) %collective-permute-start.20) | collective-permute-done | bytes 1048608 | tf_op jit(solution)/shard_map/ppermute | solution.py:483
  121.6 6.8 %collective-permute-done.19 = bf16[4,64,2048]{2,1,0:T(8,128)(2,1)} collective-permute-done((bf16[4,64,2048]{2,1,0:T(8,128)(2,1)S(1)}, bf16[4,64,2048]{2,1,0:T(8,128)(2,1)}, u32[]{:S(2)}, u32[]{:S(2)}) %collective-permute-start.19) | collective-permute-done | bytes 1048608 | tf_op jit(solution)/shard_map/ppermute | solution.py:482
  128.3 3.0 %add_convert_fusion.refs_6_ = bf16[4,64,2048]{2,1,0:T(8,128)(2,1)} fusion(bf16[4,64,2048]{2,1,0:T(8,128)(2,1)} %collective-permute-done.20, f32[4,64,2048]{2,1,0:T(8,128)S(1)} %convert_add_fusion, bf16[4,64,2048]{2,1,0:T(8,128)(2,1)} %collective-permute-done.19), kind=kLoop, calls=%fused_computation | loop fusion | flops 2621440 | bytes 5242880 | tf_op jit(solution)/shard_map/convert_element_type | solution.py:487
  131.4 3.0 %collective-permute-done.17.refs_3_ = bf16[384,256]{1,0:T(8,128)(2,1)S(1)} collective-permute-done((bf16[384,256]{1,0:T(8,128)(2,1)}, bf16[384,256]{1,0:T(8,128)(2,1)S(1)}, u32[]{:S(2)}, u32[]{:S(2)}) %collective-permute-start.17) | collective-permute-done | bytes 196640 | tf_op jit(solution)/shard_map/ppermute | solution.py:351
  135.0 2.0 %shard_map.142 = (bf16[256,256]{1,0:T(8,128)(2,1)}, bf16[1664,256]{1,0:T(8,128)(2,1)}) custom-call(s32[1]{0:T(128)} %bitcast.1.refs_0_, bf16[384,256]{1,0:T(8,128)(2,1)} %get-tuple-element.34.refs_1_, bf16[384,256]{1,0:T(8,128)(2,1)} %copy-done.15, bf16[384,256]{1,0:T(8,128)(2,1)} %copy-done.16, ...), custom_call_target="tpu_custom_call", output_to_operand_aliasing={{1}: (5, {})} | custom-call | flops 1000000000 | bytes 360000 | tf_op jit(solution)/shard_map/pallas_call | solution.py:24
  (84 shorter events, 13.3 us)
Async XLA Ops:
  1.4 8.2 %copy-start.10 = (bf16[1,64,256]{2,1,0:T(8,128)(2,1)}, bf16[1,64,256]{2,1,0:T(8,128)(2,1)S(1)}, u32[]{:S(2)}) copy-start(bf16[1,64,256]{2,1,0:T(8,128)(2,1)S(1)} %slice.3.refs_4_.refs_2_) | copy-start | bytes 98308
  1.4 12.1 %collective-permute-start.2 = (bf16[1,64,256]{2,1,0:T(8,128)(2,1)S(1)}, bf16[1,64,256]{2,1,0:T(8,128)(2,1)S(1)}, u32[]{:S(2)}, u32[]{:S(2)}) collective-permute-start(bf16[1,64,256]{2,1,0:T(8,128)(2,1)S(1)} %slice.3.refs_4_.refs_2_), channel_id=1, source_target_pairs={{0,12},{4,0},{8,4},{12,8},{1,13},{5,1},{9,5},{13,9},{2,14},{6,2},{... | collective-permute-start | bytes 98312 | tf_op jit(solution)/shard_map/ppermute | solution.py:351
  6.4 7.1 %collective-permute-start.1 = (bf16[1,64,256]{2,1,0:T(8,128)(2,1)S(1)}, bf16[1,64,256]{2,1,0:T(8,128)(2,1)S(1)}, u32[]{:S(2)}, u32[]{:S(2)}) collective-permute-start(bf16[1,64,256]{2,1,0:T(8,128)(2,1)S(1)} %slice.3.refs_4_.refs_2_), channel_id=1, source_target_pairs={{0,8},{4,12},{8,0},{12,4},{1,9},{5,13},{9,1},{13,5},{2,10},{6,14},... | collective-permute-start | bytes 98312 | tf_op jit(solution)/shard_map/ppermute | solution.py:351
  6.4 7.1 %collective-permute-start = (bf16[1,64,256]{2,1,0:T(8,128)(2,1)S(1)}, bf16[1,64,256]{2,1,0:T(8,128)(2,1)S(1)}, u32[]{:S(2)}, u32[]{:S(2)}) collective-permute-start(bf16[1,64,256]{2,1,0:T(8,128)(2,1)S(1)} %slice.3.refs_4_.refs_2_), channel_id=1, source_target_pairs={{0,4},{4,8},{8,12},{12,0},{1,5},{5,9},{9,13},{13,1},{2,6},{6,10},{... | collective-permute-start | bytes 98312 | tf_op jit(solution)/shard_map/ppermute | solution.py:351
  12.7 3.9 %copy-start.20 = (s32[16]{0:T(128)S(1)}, s32[16]{0:T(128)}, u32[]{:S(2)}) copy-start(s32[16]{0:T(128)} %param.14) | copy-start | bytes 196
  12.7 3.9 %copy-start.21 = (s32[13]{0:T(128)S(1)}, s32[13]{0:T(128)}, u32[]{:S(2)}) copy-start(s32[13]{0:T(128)} %param.12) | copy-start | bytes 160
  16.5 1.7 %collective-permute-start.3 = (bf16[13,64,128]{2,1,0:T(8,128)(2,1)}, bf16[13,64,128]{2,1,0:T(8,128)(2,1)S(1)}, u32[]{:S(2)}, u32[]{:S(2)}) collective-permute-start(bf16[13,64,128]{2,1,0:T(8,128)(2,1)} %get-tuple-element.24), channel_id=1, source_target_pairs={{0,1},{1,0},{2,3},{3,2},{4,5},{5,4},{6,7},{7,6},{8,9},{9,8},{10,11... | collective-permute-start | bytes 638984 | tf_op jit(solution)/shard_map/ppermute | solution.py:369
  19.2 2.3 %copy-start.3 = (bf16[13,64,128]{2,1,0:T(8,128)(2,1)}, bf16[13,64,128]{2,1,0:T(8,128)(2,1)S(1)}, u32[]{:S(2)}) copy-start(bf16[13,64,128]{2,1,0:T(8,128)(2,1)S(1)} %add_convert_fusion.3.refs_1_) | copy-start | bytes 638980
  19.2 7.4 %collective-permute-start.4 = (bf16[13,64,128]{2,1,0:T(8,128)(2,1)S(1)}, bf16[13,64,128]{2,1,0:T(8,128)(2,1)S(1)}, u32[]{:S(2)}, u32[]{:S(2)}) collective-permute-start(bf16[13,64,128]{2,1,0:T(8,128)(2,1)S(1)} %add_convert_fusion.3.refs_1_), channel_id=1, source_target_pairs={{0,2},{1,3},{2,0},{3,1},{4,6},{5,7},{6,4},{7,5},{8,10},{9,11},{10,... | collective-permute-start | bytes 638984 | tf_op jit(solution)/shard_map/ppermute | solution.py:369
  21.5 23.7 %collective-permute-start.7 = (bf16[1,64,2048]{2,1,0:T(8,128)(2,1)}, bf16[1,64,2048]{2,1,0:T(8,128)(2,1)S(1)}, u32[]{:S(2)}, u32[]{:S(2)}) collective-permute-start(bf16[1,64,2048]{2,1,0:T(8,128)(2,1)} %shard_map.134.refs_10_), channel_id=1, source_target_pairs={{0,12},{4,0},{8,4},{12,8},{1,13},{5,1},{9,5},{13,9},{2,14},{6,2},{... | collective-permute-start | bytes 786440 | tf_op jit(solution)/shard_map/ppermute | solution.py:351
  24.3 25.4 %collective-permute-start.6 = (bf16[1,64,2048]{2,1,0:T(8,128)(2,1)}, bf16[1,64,2048]{2,1,0:T(8,128)(2,1)S(1)}, u32[]{:S(2)}, u32[]{:S(2)}) collective-permute-start(bf16[1,64,2048]{2,1,0:T(8,128)(2,1)} %shard_map.134.refs_10_), channel_id=1, source_target_pairs={{0,8},{4,12},{8,0},{12,4},{1,9},{5,13},{9,1},{13,5},{2,10},{6,14},... | collective-permute-start | bytes 786440 | tf_op jit(solution)/shard_map/ppermute | solution.py:351
  25.4 24.3 %collective-permute-start.5 = (bf16[1,64,2048]{2,1,0:T(8,128)(2,1)}, bf16[1,64,2048]{2,1,0:T(8,128)(2,1)S(1)}, u32[]{:S(2)}, u32[]{:S(2)}) collective-permute-start(bf16[1,64,2048]{2,1,0:T(8,128)(2,1)} %shard_map.134.refs_10_), channel_id=1, source_target_pairs={{0,4},{4,8},{8,12},{12,0},{1,5},{5,9},{9,13},{13,1},{2,6},{6,10},{... | collective-permute-start | bytes 786440 | tf_op jit(solution)/shard_map/ppermute | solution.py:351
  33.3 29.7 %collective-permute-start.9 = (bf16[4,64,2048]{2,1,0:T(8,128)(2,1)}, bf16[4,64,2048]{2,1,0:T(8,128)(2,1)S(1)}, u32[]{:S(2)}, u32[]{:S(2)}) collective-permute-start(bf16[4,64,2048]{2,1,0:T(8,128)(2,1)} %get-tuple-element.32), channel_id=1, source_target_pairs={{4,8},{8,4},{5,9},{9,5},{6,10},{10,6},{7,11},{11,7},{20,24},{24,20... | collective-permute-start | bytes 3145736 | tf_op jit(solution)/shard_map/ppermute | solution.py:477
  34.0 36.1 %collective-permute-start.10 = (bf16[4,64,2048]{2,1,0:T(8,128)(2,1)}, bf16[4,64,2048]{2,1,0:T(8,128)(2,1)S(1)}, u32[]{:S(2)}, u32[]{:S(2)}) collective-permute-start(bf16[4,64,2048]{2,1,0:T(8,128)(2,1)} %get-tuple-element.25.refs_8_), channel_id=1, source_target_pairs={{0,4},{12,8},{4,0},{8,12},{1,5},{13,9},{5,1},{9,13},{2,6},{14,10},... | collective-permute-start | bytes 3145736 | tf_op jit(solution)/shard_map/ppermute | solution.py:476
  45.1 4.5 %copy-start.12 = (bf16[1,64,2048]{2,1,0:T(8,128)(2,1)}, bf16[1,64,2048]{2,1,0:T(8,128)(2,1)S(1)}, u32[]{:S(2)}) copy-start(bf16[1,64,2048]{2,1,0:T(8,128)(2,1)S(1)} %collective-permute-done.7.refs_9_.refs_13_) | copy-start | bytes 786436
  62.5 12.9 %collective-permute-start.11 = (bf16[1664,256]{1,0:T(8,128)(2,1)}, bf16[1664,256]{1,0:T(8,128)(2,1)}, u32[]{:S(2)}, u32[]{:S(2)}) collective-permute-start(bf16[1664,256]{1,0:T(8,128)(2,1)} %get-tuple-element.31.refs_1_), channel_id=1, source_target_pairs={{0,1},{1,0},{2,3},{3,2},{4,5},{5,4},{6,7},{7,6},{8,9},{9,8},{10,11... | collective-permute-start | bytes 2555912 | tf_op jit(solution)/shard_map/ppermute | solution.py:369
  62.5 28.3 %collective-permute-start.8 = (bf16[1664,256]{1,0:T(8,128)(2,1)}, bf16[1664,256]{1,0:T(8,128)(2,1)S(1)}, u32[]{:S(2)}, u32[]{:S(2)}) collective-permute-start(bf16[1664,256]{1,0:T(8,128)(2,1)} %get-tuple-element.29), channel_id=1, source_target_pairs={{0,1},{1,0},{2,3},{3,2},{4,5},{5,4},{6,7},{7,6},{8,9},{9,8},{10,11... | collective-permute-start | bytes 2555912 | tf_op jit(solution)/shard_map/ppermute | solution.py:369
  70.2 5.2 %copy-start.1 = (bf16[4,64,2048]{2,1,0:T(8,128)(2,1)}, bf16[4,64,2048]{2,1,0:T(8,128)(2,1)S(1)}, u32[]{:S(2)}) copy-start(bf16[4,64,2048]{2,1,0:T(8,128)(2,1)S(1)} %collective-permute-done.10) | copy-start | bytes 3145732
  72.2 3.2 %copy-start = (bf16[4,64,2048]{2,1,0:T(8,128)(2,1)}, bf16[4,64,2048]{2,1,0:T(8,128)(2,1)S(1)}, u32[]{:S(2)}) copy-start(bf16[4,64,2048]{2,1,0:T(8,128)(2,1)S(1)} %add_convert_fusion.1.refs_1_.refs_14_) | copy-start | bytes 3145732
  72.2 56.2 %collective-permute-start.19 = (bf16[4,64,2048]{2,1,0:T(8,128)(2,1)S(1)}, bf16[4,64,2048]{2,1,0:T(8,128)(2,1)}, u32[]{:S(2)}, u32[]{:S(2)}) collective-permute-start(bf16[4,64,2048]{2,1,0:T(8,128)(2,1)S(1)} %add_convert_fusion.1.refs_1_.refs_14_), channel_id=1, source_target_pairs={{0,8},{12,4},{4,12},{8,0},{1,9},{13,5},{5,13},{9,1},{2,10},{14,6},... | collective-permute-start | bytes 3145736 | tf_op jit(solution)/shard_map/ppermute | solution.py:482
  77.9 11.5 %copy-start.11 = (s32[4]{0:T(128)S(1)}, s32[4]{0:T(128)}, u32[]{:S(2)}) copy-start(s32[4]{0:T(128)} %param.11) | copy-start | bytes 52
  77.9 30.4 %collective-permute-start.12 = (bf16[1664,256]{1,0:T(8,128)(2,1)}, bf16[1664,256]{1,0:T(8,128)(2,1)}, u32[]{:S(2)}, u32[]{:S(2)}) collective-permute-start(bf16[1664,256]{1,0:T(8,128)(2,1)} %add_convert_fusion.2), channel_id=1, source_target_pairs={{0,2},{1,3},{2,0},{3,1},{4,6},{5,7},{6,4},{7,5},{8,10},{9,11},{10,... | collective-permute-start | bytes 2555912 | tf_op jit(solution)/shard_map/ppermute | solution.py:369
  78.5 43.1 %collective-permute-start.20 = (bf16[4,64,2048]{2,1,0:T(8,128)(2,1)}, bf16[4,64,2048]{2,1,0:T(8,128)(2,1)}, u32[]{:S(2)}, u32[]{:S(2)}) collective-permute-start(bf16[4,64,2048]{2,1,0:T(8,128)(2,1)} %shard_map.141), channel_id=1, source_target_pairs={{0,4},{12,8},{1,5},{13,9},{2,6},{14,10},{3,7},{15,11},{16,20},{28,... | collective-permute-start | bytes 3145736 | tf_op jit(solution)/shard_map/ppermute | solution.py:483
  89.4 1.4 %copy-start.6 = (bf16[13,64,128]{2,1,0:T(8,128)(2,1)S(1)}, bf16[13,64,128]{2,1,0:T(8,128)(2,1)}, u32[]{:S(2)}) copy-start(bf16[13,64,128]{2,1,0:T(8,128)(2,1)} %shard_map.138.refs_5_) | copy-start | bytes 638980
  89.4 13.4 %collective-permute-start.15 = (bf16[13,64,128]{2,1,0:T(8,128)(2,1)}, bf16[13,64,128]{2,1,0:T(8,128)(2,1)S(1)}, u32[]{:S(2)}, u32[]{:S(2)}) collective-permute-start(bf16[13,64,128]{2,1,0:T(8,128)(2,1)} %shard_map.138.refs_5_), channel_id=1, source_target_pairs={{0,3},{1,2},{2,1},{3,0},{4,7},{5,6},{6,5},{7,4},{8,11},{9,10},{10,... | collective-permute-start | bytes 638984 | tf_op jit(solution)/shard_map/ppermute | solution.py:369
  90.8 12.0 %copy-start.5 = (bf16[1664,256]{1,0:T(8,128)(2,1)}, bf16[1664,256]{1,0:T(8,128)(2,1)S(1)}, u32[]{:S(2)}) copy-start(bf16[1664,256]{1,0:T(8,128)(2,1)S(1)} %collective-permute-done.8.refs_3_) | copy-start | bytes 2555908
  90.8 16.8 %collective-permute-start.14 = (bf16[13,64,128]{2,1,0:T(8,128)(2,1)S(1)}, bf16[13,64,128]{2,1,0:T(8,128)(2,1)S(1)}, u32[]{:S(2)}, u32[]{:S(2)}) collective-permute-start(bf16[13,64,128]{2,1,0:T(8,128)(2,1)S(1)} %copy-done.6), channel_id=1, source_target_pairs={{0,2},{1,3},{2,0},{3,1},{4,6},{5,7},{6,4},{7,5},{8,10},{9,11},{10,... | collective-permute-start | bytes 638984 | tf_op jit(solution)/shard_map/ppermute | solution.py:369
  103.4 4.2 %collective-permute-start.13 = (bf16[13,64,128]{2,1,0:T(8,128)(2,1)S(1)}, bf16[13,64,128]{2,1,0:T(8,128)(2,1)S(1)}, u32[]{:S(2)}, u32[]{:S(2)}) collective-permute-start(bf16[13,64,128]{2,1,0:T(8,128)(2,1)S(1)} %copy-done.6), channel_id=1, source_target_pairs={{0,1},{1,0},{2,3},{3,2},{4,5},{5,4},{6,7},{7,6},{8,9},{9,8},{10,11... | collective-permute-start | bytes 638984 | tf_op jit(solution)/shard_map/ppermute | solution.py:369
  113.9 17.4 %collective-permute-start.16 = (bf16[384,256]{1,0:T(8,128)(2,1)}, bf16[384,256]{1,0:T(8,128)(2,1)S(1)}, u32[]{:S(2)}, u32[]{:S(2)}) collective-permute-start(bf16[384,256]{1,0:T(8,128)(2,1)} %get-tuple-element.35), channel_id=1, source_target_pairs={{0,4},{4,8},{8,12},{12,0},{1,5},{5,9},{9,13},{13,1},{2,6},{6,10},{... | collective-permute-start | bytes 589832 | tf_op jit(solution)/shard_map/ppermute | solution.py:351
  114.2 20.2 %collective-permute-start.17 = (bf16[384,256]{1,0:T(8,128)(2,1)}, bf16[384,256]{1,0:T(8,128)(2,1)S(1)}, u32[]{:S(2)}, u32[]{:S(2)}) collective-permute-start(bf16[384,256]{1,0:T(8,128)(2,1)} %get-tuple-element.36), channel_id=1, source_target_pairs={{0,8},{4,12},{8,0},{12,4},{1,9},{5,13},{9,1},{13,5},{2,10},{6,14},... | collective-permute-start | bytes 589832 | tf_op jit(solution)/shard_map/ppermute | solution.py:351
  116.2 18.2 %collective-permute-start.18 = (bf16[384,256]{1,0:T(8,128)(2,1)}, bf16[384,256]{1,0:T(8,128)(2,1)}, u32[]{:S(2)}, u32[]{:S(2)}) collective-permute-start(bf16[384,256]{1,0:T(8,128)(2,1)} %get-tuple-element.37), channel_id=1, source_target_pairs={{0,12},{4,0},{8,4},{12,8},{1,13},{5,1},{9,5},{13,9},{2,14},{6,2},{... | collective-permute-start | bytes 589832 | tf_op jit(solution)/shard_map/ppermute | solution.py:351
  131.4 3.0 %copy-start.15 = (bf16[384,256]{1,0:T(8,128)(2,1)}, bf16[384,256]{1,0:T(8,128)(2,1)S(1)}, u32[]{:S(2)}) copy-start(bf16[384,256]{1,0:T(8,128)(2,1)S(1)} %collective-permute-done.16.refs_2_) | copy-start | bytes 589828
  (11 other events, 7.8 us)

commit v8 on v7

--- a/solution.py
+++ b/solution.py
@@ -405,7 +405,7 @@
     return entry(me) if size == 1 else add(entry(me), from_left, from_right)
 
 
-ROLES = ((3, 1, 2, 0), (0, 2, 3, 1), (3, 1, 0, 2), (0, 2, 1, 3))
+ROLES = ((3, 2, 1, 0), (0, 3, 2, 1), (3, 0, 1, 2), (0, 1, 2, 3))
 
 
 def body(
@@ -457,7 +457,8 @@
 
     def base_parts(terms, *tokens):
         sent, away, given, mine = terms
-        return mine, near(given), far(add(after(away, *tokens), near(sent)))
+        away = add(after(away, *tokens), near(sent))
+        return (mine, near(given), far(away)), away
 
     def inputs(*tokens):
         return spread(
@@ -472,22 +473,25 @@
     if line:
         inner = (me == 1) | (me == 2)
         codes = codes_of(jnp.array(ROLES, jnp.int32)[me])
-        first, third, third_too = down_rows(codes, 0, 2, 2, rank_cot, hidden)
+        (first,) = down_rows(codes, 0, 1, 1, rank_cot, hidden)
         from_first = lax.ppermute(first, "dp", [(0, 1), (3, 2), (1, 0), (2, 3)])
+        second, third, own = down_rows(codes, OWN, 3, 1, rank_cot, hidden, [first], 1.0)
+        terms = base(second, *down_choices[1:])
+        second = add(after(second, terms[0]), jnp.where(inner, from_first, jnp.zeros((), first.dtype)))
+        from_second = lax.ppermute(second, "dp", [(0, 1), (3, 2), (1, 3), (2, 0)])
+        base_sums, away = base_parts(terms, second)
+        rank_in = inputs(away)
+        third = add(after(third, rank_in[0]), jnp.where(inner, from_second, jnp.zeros((), first.dtype)))
         from_inner = lax.ppermute(third, "dp", [(1, 2), (2, 1)])
-        second, own = down_rows(codes, 2 * OWN, 2, 1, rank_cot, hidden, [first], 1.0)
-        terms = base(second, *down_choices[1:])
-        second = add(after(second, terms[0], from_inner), jnp.where(inner, from_first, jnp.zeros((), first.dtype)))
-        base_sums = base_parts(terms, second)
-        from_second = lax.ppermute(second, "dp", [(0, 2), (3, 1), (1, 3), (2, 0)])
-        from_third = lax.ppermute(after(third_too, second), "dp", [(0, 1), (3, 2)])
+        from_third = lax.ppermute(third, "dp", [(0, 1), (3, 2)])
         near_total = lax.optimization_barrier(
-            after(own, second).astype(jnp.float32) + jnp.where(inner, from_inner, from_first).astype(jnp.float32)
+            after(own, third).astype(jnp.float32)
+            + jnp.where(inner, 0.0, from_first.astype(jnp.float32) + from_second.astype(jnp.float32))
         )
-        down_out = (near_total + from_second.astype(jnp.float32) + from_third.astype(jnp.float32)).astype(own.dtype)
+        down_out = (near_total + from_inner.astype(jnp.float32) + from_third.astype(jnp.float32)).astype(own.dtype)
 
         up_codes = codes_of((me + jnp.array([1, 2, 3, 0], jnp.int32)) % devices)
-        values, *sent, kept_here = outputs(up_codes, [OWN] * 4, base_sums, inputs(second))
+        values, *sent, kept_here = outputs(up_codes, [OWN] * 4, base_sums, rank_in)
         arrived = [shift(array, by + 1) for by, array in enumerate(sent)]
         value_pick = ((me - partner[me]) % devices).reshape(1)
         up_out, values = finish(value_pick, values, kept_here, arrived, [down_out])
@@ -495,7 +499,7 @@
         codes = codes_of(order)
         (table,) = down_rows(codes, 0, devices, 0, rank_cot, hidden)
         down_out = line_reduce_scatter(table.reshape(devices, OWN, *table.shape[1:]))
-        values, table = outputs(codes, [devices * OWN], base_parts(base(table)), inputs(table))
+        values, table = outputs(codes, [devices * OWN], base_parts(base(table))[0], inputs(table))
         up_table, last_values = table[:-BLOCK], table[-BLOCK:]
         up_out = line_reduce_scatter(up_table.reshape(devices, OWN, -1, values.shape[1]))
         (last_values,), _ = shifted(last_values, partner[me])

time: 138 us -> 139 us (level)
  waiting for transfers between devices: 36.7 us -> 45.5 us
  starting transfers between devices: 31.5 us -> 25.8 us
  local copies, waits for them, and re-layouts: 7.43 us -> 5.25 us
    ppermute x9, waiting for transfers between devices: 7.52 us -> 18.6 us  [shift(): lax.ppermute(array, 'dp', [(i, (i + by) % size) for i in range(size)])]
    ppermute x8, waiting for transfers between devices: 12.4 us -> 4.68 us  [crossed(): lax.ppermute(array, 'tensor', [(i, i ^ by) for i in range(lax.axis_size('...]
    ppermute x2, waiting for transfers between devices: 10.6 us -> 16.4 us  [the longest x1 11.9 us: body(): from_second = lax.ppermute(second, 'dp', [(0, 1), (3, 2), (1, 3), (2, 0)])]
    ppermute x2, starting transfers between devices: 6.29 us -> 2.32 us  [the longest x1 2.27 us: body(): from_third = lax.ppermute(third, 'dp', [(0, 1), (3, 2)])]
    unnamed x44 -> x34, local copies, waits for them, and re-layouts: 5.91 us -> 3.73 us
    ppermute x1, starting transfers between devices: 4.35 us -> 2.48 us  [body(): from_first = lax.ppermute(first, 'dp', [(0, 1), (3, 2), (1, 0), (2, 3)])]
    convert_element_type x3 -> x4, other arithmetic: 5.52 us -> 6.75 us  [add(): sum((array.astype(jnp.float32) for array in arrays)).astype(arrays[0].dtype)]
  transfers between devices with their start and end apart: 21 -> 21, of which waited for: 8 -> 9; matrix products, arithmetic and copies ran while one was open for 10% -> 11% of each run, Pallas kernels for 30% -> 29%
where the time goes in v8:
time: 139 us
  waiting for transfers between devices  45.5 us (33%)
  Pallas kernels  44.6 us (32%)
  starting transfers between devices  25.8 us (19%)
  other arithmetic  15.2 us (11%)
  local copies, waits for them, and re-layouts  5.25 us (4%)
  between operations  2.2 us (2%)
    pallas_call x13, Pallas kernels, call(): pl.pallas_call(run, grid_spec=pltpu.PrefetchScalarGridSpec(num_scalar_pre...  44.6 us
    ppermute x9, waiting for transfers between devices, shift(): lax.ppermute(array, 'dp', [(i, (i + by) % size) for i in range(size)])  18.6 us
    ppermute x9, starting transfers between devices, shift(): lax.ppermute(array, 'dp', [(i, (i + by) % size) for i in range(size)])  13.8 us
    ppermute x1, waiting for transfers between devices, body(): from_second = lax.ppermute(second, 'dp', [(0, 1), (3, 2), (1, 3), (2, 0)])  11.9 us
    convert_element_type x4, other arithmetic, add(): sum((array.astype(jnp.float32) for array in arrays)).astype(arrays[0].dtype)  6.75 us
    ppermute x1, waiting for transfers between devices, body(): from_first = lax.ppermute(first, 'dp', [(0, 1), (3, 2), (1, 0), (2, 3)])  5.88 us
    ppermute x8, starting transfers between devices, crossed(): lax.ppermute(array, 'tensor', [(i, i ^ by) for i in range(lax.axis_size('...  5.53 us
    ppermute x8, waiting for transfers between devices, crossed(): lax.ppermute(array, 'tensor', [(i, i ^ by) for i in range(lax.axis_size('...  4.68 us
  transfers between devices with their start and end apart: 21, of which 9 were waited for; matrix products, arithmetic and copies ran while one was open for 11% of the time, Pallas kernels for 29%

profile of v8, /device:TPU:0, one launch (start us, length us, event | category | flops | bytes accessed | tf_op | source)
XLA Modules:
  0.0 138.6 jit_solution(13397428208282904466)
XLA Ops:
  1.4 5.0 %collective-permute-start.2 = (bf16[1,64,256]{2,1,0:T(8,128)(2,1)S(1)}, bf16[1,64,256]{2,1,0:T(8,128)(2,1)S(1)}, u32[]{:S(2)}, u32[]{:S(2)}) collective-permute-start(bf16[1,64,256]{2,1,0:T(8,128)(2,1)S(1)} %slice.3.refs_4_.refs_2_), channel_id=1, source_target_pairs={{0,12},{4,0},{8,4},{12,8},{1,13},{5,1},{9,5},{13,9},{2,14},{6,2},{... | collective-permute-start | bytes 98312 | tf_op jit(solution)/shard_map/ppermute | solution.py:351
  7.5 1.3 fusion.1
  9.6 3.0 %shard_map.130 = (bf16[13,64,128]{2,1,0:T(8,128)(2,1)}, bf16[1,64,2048]{2,1,0:T(8,128)(2,1)}) custom-call(s32[13]{0:T(128)} %refs_0_.7, bf16[13,64,256]{2,1,0:T(8,128)(2,1)} %refs_10_.1, bf16[1664,256]{1,0:T(8,128)(2,1)} %refs_9_.3, bf16[13,64,2048]{2,1,0:T(8,128)(2,1)} %refs_5_.7, bf16[1,64,256]{2,1,0:T(8,128)(2,1)} %copy-done.5), custom_call_target="tpu_custom_call" | custom-call | flops 1000000000 | bytes 360000 | tf_op jit(solution)/shard_map/pallas_call | solution.py:24
  14.2 2.3 %shard_map.131 = (bf16[13,64,128]{2,1,0:T(8,128)(2,1)}, bf16[1,64,256]{2,1,0:T(8,128)(2,1)}) custom-call(s32[13]{0:T(128)} %refs_0_.7, s32[1]{0:T(128)} %bitcast.7.refs_1_, bf16[1,64,256]{2,1,0:T(8,128)(2,1)} %copy-done.5, bf16[1,64,256]{2,1,0:T(8,128)(2,1)} %copy-done.14, bf16[1,64,256]{2,1,0:T(8,128)(2,1)} %copy-done.13, ...), custom_call_target="tpu_custom_call", output_to_operand_aliasing={{0}: (7, {})} | custom-call | flops 1000000000 | bytes 360000 | tf_op jit(solution)/shard_map/pallas_call | solution.py:24
  16.7 1.5 %collective-permute-done.3 = bf16[13,64,128]{2,1,0:T(8,128)(2,1)S(1)} collective-permute-done((bf16[13,64,128]{2,1,0:T(8,128)(2,1)}, bf16[13,64,128]{2,1,0:T(8,128)(2,1)S(1)}, u32[]{:S(2)}, u32[]{:S(2)}) %collective-permute-start.3) | collective-permute-done | bytes 213024 | tf_op jit(solution)/shard_map/ppermute | solution.py:369
  19.2 1.6 %collective-permute-start.4 = (bf16[13,64,128]{2,1,0:T(8,128)(2,1)S(1)}, bf16[13,64,128]{2,1,0:T(8,128)(2,1)S(1)}, u32[]{:S(2)}, u32[]{:S(2)}) collective-permute-start(bf16[13,64,128]{2,1,0:T(8,128)(2,1)S(1)} %add_convert_fusion.4.refs_1_), channel_id=1, source_target_pairs={{0,2},{1,3},{2,0},{3,1},{4,6},{5,7},{6,4},{7,5},{8,10},{9,11},{10,... | collective-permute-start | bytes 638984 | tf_op jit(solution)/shard_map/ppermute | solution.py:369
  21.5 2.8 %collective-permute-start.7 = (bf16[1,64,2048]{2,1,0:T(8,128)(2,1)}, bf16[1,64,2048]{2,1,0:T(8,128)(2,1)S(1)}, u32[]{:S(2)}, u32[]{:S(2)}) collective-permute-start(bf16[1,64,2048]{2,1,0:T(8,128)(2,1)} %shard_map.134.refs_10_), channel_id=1, source_target_pairs={{0,12},{4,0},{8,4},{12,8},{1,13},{5,1},{9,5},{13,9},{2,14},{6,2},{... | collective-permute-start | bytes 786440 | tf_op jit(solution)/shard_map/ppermute | solution.py:351
  27.2 4.4 %shard_map.132.refs_8_ = bf16[4,64,2048]{2,1,0:T(8,128)(2,1)} custom-call(s32[16]{0:T(128)} %get-tuple-element.39.refs_0_, bf16[13,64,128]{2,1,0:T(8,128)(2,1)} %copy-done.2, bf16[13,64,128]{2,1,0:T(8,128)(2,1)} %copy-done.3, bf16[1664,2048]{1,0:T(8,128)(2,1)} %refs_9_.2, bf16[1664,2048]{1,0:T(8,128)(2,1)} %refs_9_.2, bf16[1664,2048]{1,0:T(8,128)(2,1)} %refs_9_.2, ...), custom_call_target="tpu_custom_call" | custom-call | flops 1000000000 | bytes 360000 | tf_op jit(solution)/shard_map/pallas_call | solution.py:24
  31.6 2.5 %collective-permute-start.9 = (bf16[4,64,2048]{2,1,0:T(8,128)(2,1)}, bf16[4,64,2048]{2,1,0:T(8,128)(2,1)S(1)}, u32[]{:S(2)}, u32[]{:S(2)}) collective-permute-start(bf16[4,64,2048]{2,1,0:T(8,128)(2,1)} %shard_map.132.refs_8_), channel_id=1, source_target_pairs={{0,4},{12,8},{4,0},{8,12},{1,5},{13,9},{5,1},{9,13},{2,6},{14,10},... | collective-permute-start | bytes 3145736 | tf_op jit(solution)/shard_map/ppermute | solution.py:477
  34.1 8.0 %shard_map.133 = (bf16[4,64,2048]{2,1,0:T(8,128)(2,1)}, bf16[4,64,2048]{2,1,0:T(8,128)(2,1)}, bf16[4,64,2048]{2,1,0:T(8,128)(2,1)}) custom-call(s32[16]{0:T(128)} %get-tuple-element.39.refs_0_, bf16[13,64,128]{2,1,0:T(8,128)(2,1)} %copy-done.2, bf16[13,64,128]{2,1,0:T(8,128)(2,1)} %copy-done.3, bf16[1664,2048]{1,0:T(8,128)(2,1)} %refs_9_.2, ...), custom_call_target="tpu_custom_call" | custom-call | flops 1000000000 | bytes 360000 | tf_op jit(solution)/shard_map/pallas_call | solution.py:24
  42.1 6.5 %collective-permute-done.6.refs_8_.refs_12_ = bf16[1,64,2048]{2,1,0:T(8,128)(2,1)S(1)} collective-permute-done((bf16[1,64,2048]{2,1,0:T(8,128)(2,1)}, bf16[1,64,2048]{2,1,0:T(8,128)(2,1)S(1)}, u32[]{:S(2)}, u32[]{:S(2)}) %collective-permute-start.6) | collective-permute-done | bytes 262176 | tf_op jit(solution)/shard_map/ppermute | solution.py:351
  49.4 12.0 %shard_map.135 = (bf16[1664,256]{1,0:T(8,128)(2,1)}, bf16[1664,256]{1,0:T(8,128)(2,1)}, bf16[1664,256]{1,0:T(8,128)(2,1)}, bf16[1664,256]{1,0:T(8,128)(2,1)}) custom-call(s32[4]{0:T(128)} %pad_add_fusion.refs_0_, bf16[1664,2048]{1,0:T(8,128)(2,1)} %refs_9_.2, bf16[2048,1024]{1,0:T(8,128)(2,1)} %refs_5_.6, bf16[2048,1024]{1,0:T(8,128)(2,1)} %refs_5_.6, ...), custom_call_target="tpu_custom_call" | custom-call | flops 99999997952 | bytes 36000000 | tf_op jit(solution)/shard_map/pallas_call | solution.py:24
  62.0 5.9 %collective-permute-done.9 = bf16[4,64,2048]{2,1,0:T(8,128)(2,1)S(1)} collective-permute-done((bf16[4,64,2048]{2,1,0:T(8,128)(2,1)}, bf16[4,64,2048]{2,1,0:T(8,128)(2,1)S(1)}, u32[]{:S(2)}, u32[]{:S(2)}) %collective-permute-start.9) | collective-permute-done | bytes 1048608 | tf_op jit(solution)/shard_map/ppermute | solution.py:477
  67.8 1.6 %add_convert_fusion.2.refs_1_ = bf16[4,64,2048]{2,1,0:T(8,128)(2,1)S(1)} fusion(bf16[4,64,2048]{2,1,0:T(8,128)(2,1)} %shard_map.136, bf16[4,64,2048]{2,1,0:T(8,128)(2,1)S(1)} %collective-permute-done.9, pred[]{:T(512)S(6)} %or.3), kind=kLoop, calls=%fused_computation.3 | loop fusion | flops 2621440 | bytes 3145729 | tf_op jit(solution)/shard_map/convert_element_type | solution.py:365
  70.4 2.5 %add_convert_fusion.3.refs_14_ = bf16[1664,256]{1,0:T(8,128)(2,1)} fusion(bf16[1664,256]{1,0:T(8,128)(2,1)} %collective-permute-done.10, bf16[1664,256]{1,0:T(8,128)(2,1)} %shard_map.137), kind=kLoop, calls=%fused_computation.4 | loop fusion | flops 1703936 | bytes 2555904 | tf_op jit(solution)/shard_map/convert_element_type | solution.py:365
  73.0 1.5 %collective-permute-start.11 = (bf16[1664,256]{1,0:T(8,128)(2,1)}, bf16[1664,256]{1,0:T(8,128)(2,1)}, u32[]{:S(2)}, u32[]{:S(2)}) collective-permute-start(bf16[1664,256]{1,0:T(8,128)(2,1)} %add_convert_fusion.3.refs_14_), channel_id=1, source_target_pairs={{0,2},{1,3},{2,0},{3,1},{4,6},{5,7},{6,4},{7,5},{8,10},{9,11},{10,... | collective-permute-start | bytes 2555912 | tf_op jit(solution)/shard_map/ppermute | solution.py:369
  74.5 7.8 %shard_map.138.refs_5_.refs_1_ = bf16[13,64,128]{2,1,0:T(8,128)(2,1)} custom-call(s32[13]{0:T(128)} %refs_0_.7, s32[1]{0:T(128)} %bitcast.7.refs_1_, bf16[13,64,2048]{2,1,0:T(8,128)(2,1)} %refs_5_.7, bf16[13,64,2048]{2,1,0:T(8,128)(2,1)} %refs_5_.7, bf16[13,64,2048]{2,1,0:T(8,128)(2,1)} %refs_5_.7, bf16[13,64,2048]{2,1,0:T(8,128)(2,1)} %refs_5_.7, ...), custom_call_target="tpu_custom_call" | custom-call | flops 99999997952 | bytes 36000000 | tf_op jit(solution)/shard_map/pallas_call | solution.py:24
  82.3 11.9 %collective-permute-done.18 = bf16[4,64,2048]{2,1,0:T(8,128)(2,1)S(1)} collective-permute-done((bf16[4,64,2048]{2,1,0:T(8,128)(2,1)S(1)}, bf16[4,64,2048]{2,1,0:T(8,128)(2,1)S(1)}, u32[]{:S(2)}, u32[]{:S(2)}) %collective-permute-start.18) | collective-permute-done | bytes 1048608 | tf_op jit(solution)/shard_map/ppermute | solution.py:481
  94.2 1.6 %add_convert_fusion.1.refs_1_ = bf16[4,64,2048]{2,1,0:T(8,128)(2,1)S(1)} fusion(bf16[4,64,2048]{2,1,0:T(8,128)(2,1)} %shard_map.140, bf16[4,64,2048]{2,1,0:T(8,128)(2,1)S(1)} %collective-permute-done.18, pred[]{:T(512)S(6)} %or.3), kind=kLoop, calls=%fused_computation.2 | loop fusion | flops 2621440 | bytes 3145729 | tf_op jit(solution)/shard_map/convert_element_type | solution.py:365
  95.9 2.3 %collective-permute-start.20 = (bf16[4,64,2048]{2,1,0:T(8,128)(2,1)S(1)}, bf16[4,64,2048]{2,1,0:T(8,128)(2,1)}, u32[]{:S(2)}, u32[]{:S(2)}) collective-permute-start(bf16[4,64,2048]{2,1,0:T(8,128)(2,1)S(1)} %add_convert_fusion.1.refs_1_), channel_id=1, source_target_pairs={{0,4},{12,8},{1,5},{13,9},{2,6},{14,10},{3,7},{15,11},{16,20},{28,... | collective-permute-start | bytes 3145736 | tf_op jit(solution)/shard_map/ppermute | solution.py:486
  98.2 1.7 %collective-permute-start.19 = (bf16[4,64,2048]{2,1,0:T(8,128)(2,1)S(1)}, bf16[4,64,2048]{2,1,0:T(8,128)(2,1)}, u32[]{:S(2)}, u32[]{:S(2)}) collective-permute-start(bf16[4,64,2048]{2,1,0:T(8,128)(2,1)S(1)} %add_convert_fusion.1.refs_1_), channel_id=1, source_target_pairs={{4,8},{8,4},{5,9},{9,5},{6,10},{10,6},{7,11},{11,7},{20,24},{24,20... | collective-permute-start | bytes 3145736 | tf_op jit(solution)/shard_map/ppermute | solution.py:485
  99.8 2.0 %collective-permute-start.13 = (bf16[13,64,128]{2,1,0:T(8,128)(2,1)S(1)}, bf16[13,64,128]{2,1,0:T(8,128)(2,1)}, u32[]{:S(2)}, u32[]{:S(2)}) collective-permute-start(bf16[13,64,128]{2,1,0:T(8,128)(2,1)S(1)} %copy-done.4), channel_id=1, source_target_pairs={{0,2},{1,3},{2,0},{3,1},{4,6},{5,7},{6,4},{7,5},{8,10},{9,11},{10,... | collective-permute-start | bytes 638984 | tf_op jit(solution)/shard_map/ppermute | solution.py:369
  103.1 2.7 %collective-permute-done.13.refs_7_ = bf16[13,64,128]{2,1,0:T(8,128)(2,1)} collective-permute-done((bf16[13,64,128]{2,1,0:T(8,128)(2,1)S(1)}, bf16[13,64,128]{2,1,0:T(8,128)(2,1)}, u32[]{:S(2)}, u32[]{:S(2)}) %collective-permute-start.13) | collective-permute-done | bytes 213024 | tf_op jit(solution)/shard_map/ppermute | solution.py:369
  105.8 5.0 %shard_map.139 = (bf16[1664,256]{1,0:T(8,128)(2,1)}, bf16[384,256]{1,0:T(8,128)(2,1)}, bf16[384,256]{1,0:T(8,128)(2,1)}, bf16[384,256]{1,0:T(8,128)(2,1)}, bf16[384,256]{1,0:T(8,128)(2,1)}) custom-call(s32[13]{0:T(128)} %refs_0_.7, s32[16]{0:T(128)} %get-tuple-element.40.refs_1_, bf16[1664,256]{1,0:T(8,128)(2,1)} %get-tuple-element.25.refs_2_, ...), custom_call_target="tpu_custom_call" | custom-call | flops 1000000000 | bytes 360000 | tf_op jit(solution)/shard_map/pallas_call | solution.py:24
  110.8 2.2 %collective-permute-start.16 = (bf16[384,256]{1,0:T(8,128)(2,1)}, bf16[384,256]{1,0:T(8,128)(2,1)S(1)}, u32[]{:S(2)}, u32[]{:S(2)}) collective-permute-start(bf16[384,256]{1,0:T(8,128)(2,1)} %get-tuple-element.32), channel_id=1, source_target_pairs={{0,8},{4,12},{8,0},{12,4},{1,9},{5,13},{9,1},{13,5},{2,10},{6,14},... | collective-permute-start | bytes 589832 | tf_op jit(solution)/shard_map/ppermute | solution.py:351
  112.9 1.7 %collective-permute-start.17 = (bf16[384,256]{1,0:T(8,128)(2,1)}, bf16[384,256]{1,0:T(8,128)(2,1)}, u32[]{:S(2)}, u32[]{:S(2)}) collective-permute-start(bf16[384,256]{1,0:T(8,128)(2,1)} %get-tuple-element.33), channel_id=1, source_target_pairs={{0,12},{4,0},{8,4},{12,8},{1,13},{5,1},{9,5},{13,9},{2,14},{6,2},{... | collective-permute-start | bytes 589832 | tf_op jit(solution)/shard_map/ppermute | solution.py:351
  114.6 1.7 %select_add_fusion = f32[4,64,2048]{2,1,0:T(8,128)S(1)} fusion(bf16[4,64,2048]{2,1,0:T(8,128)(2,1)S(1)} %collective-permute-done.18, bf16[4,64,2048]{2,1,0:T(8,128)(2,1)S(1)} %collective-permute-done.9, bf16[4,64,2048]{2,1,0:T(8,128)(2,1)} %shard_map.141, pred[]{:T(512)S(6)} %or.3), kind=kLoop, calls=%fused_computation.1 | loop fusion | flops 3145728 | bytes 5242881 | tf_op jit(solution)/shard_map/add | solution.py:488
  116.3 4.5 %collective-permute-done.20 = bf16[4,64,2048]{2,1,0:T(8,128)(2,1)} collective-permute-done((bf16[4,64,2048]{2,1,0:T(8,128)(2,1)S(1)}, bf16[4,64,2048]{2,1,0:T(8,128)(2,1)}, u32[]{:S(2)}, u32[]{:S(2)}) %collective-permute-start.20) | collective-permute-done | bytes 1048608 | tf_op jit(solution)/shard_map/ppermute | solution.py:486
  120.8 3.1 %add_convert_fusion.refs_6_ = bf16[4,64,2048]{2,1,0:T(8,128)(2,1)} fusion(bf16[4,64,2048]{2,1,0:T(8,128)(2,1)} %collective-permute-done.20, f32[4,64,2048]{2,1,0:T(8,128)S(1)} %select_add_fusion, bf16[4,64,2048]{2,1,0:T(8,128)(2,1)} %collective-permute-done.19), kind=kLoop, calls=%fused_computation | loop fusion | flops 2621440 | bytes 5242880 | tf_op jit(solution)/shard_map/convert_element_type | solution.py:491
  123.8 3.3 %collective-permute-done.15.refs_2_ = bf16[384,256]{1,0:T(8,128)(2,1)S(1)} collective-permute-done((bf16[384,256]{1,0:T(8,128)(2,1)}, bf16[384,256]{1,0:T(8,128)(2,1)S(1)}, u32[]{:S(2)}, u32[]{:S(2)}) %collective-permute-start.15) | collective-permute-done | bytes 196640 | tf_op jit(solution)/shard_map/ppermute | solution.py:351
  127.1 8.8 %collective-permute-done.16.refs_3_ = bf16[384,256]{1,0:T(8,128)(2,1)S(1)} collective-permute-done((bf16[384,256]{1,0:T(8,128)(2,1)}, bf16[384,256]{1,0:T(8,128)(2,1)S(1)}, u32[]{:S(2)}, u32[]{:S(2)}) %collective-permute-start.16) | collective-permute-done | bytes 196640 | tf_op jit(solution)/shard_map/ppermute | solution.py:351
  136.6 2.0 %shard_map.142 = (bf16[256,256]{1,0:T(8,128)(2,1)}, bf16[1664,256]{1,0:T(8,128)(2,1)}) custom-call(s32[1]{0:T(128)} %bitcast.1.refs_0_, bf16[384,256]{1,0:T(8,128)(2,1)} %get-tuple-element.30.refs_1_, bf16[384,256]{1,0:T(8,128)(2,1)} %copy-done.10, bf16[384,256]{1,0:T(8,128)(2,1)} %copy-done.11, ...), custom_call_target="tpu_custom_call", output_to_operand_aliasing={{1}: (5, {})} | custom-call | flops 1000000000 | bytes 360000 | tf_op jit(solution)/shard_map/pallas_call | solution.py:24
  (75 shorter events, 11.9 us)
Async XLA Ops:
  1.4 8.2 %copy-start.5 = (bf16[1,64,256]{2,1,0:T(8,128)(2,1)}, bf16[1,64,256]{2,1,0:T(8,128)(2,1)S(1)}, u32[]{:S(2)}) copy-start(bf16[1,64,256]{2,1,0:T(8,128)(2,1)S(1)} %slice.3.refs_4_.refs_2_) | copy-start | bytes 98308
  1.4 12.1 %collective-permute-start.2 = (bf16[1,64,256]{2,1,0:T(8,128)(2,1)S(1)}, bf16[1,64,256]{2,1,0:T(8,128)(2,1)S(1)}, u32[]{:S(2)}, u32[]{:S(2)}) collective-permute-start(bf16[1,64,256]{2,1,0:T(8,128)(2,1)S(1)} %slice.3.refs_4_.refs_2_), channel_id=1, source_target_pairs={{0,12},{4,0},{8,4},{12,8},{1,13},{5,1},{9,5},{13,9},{2,14},{6,2},{... | collective-permute-start | bytes 98312 | tf_op jit(solution)/shard_map/ppermute | solution.py:351
  6.4 7.1 %collective-permute-start.1 = (bf16[1,64,256]{2,1,0:T(8,128)(2,1)S(1)}, bf16[1,64,256]{2,1,0:T(8,128)(2,1)S(1)}, u32[]{:S(2)}, u32[]{:S(2)}) collective-permute-start(bf16[1,64,256]{2,1,0:T(8,128)(2,1)S(1)} %slice.3.refs_4_.refs_2_), channel_id=1, source_target_pairs={{0,8},{4,12},{8,0},{12,4},{1,9},{5,13},{9,1},{13,5},{2,10},{6,14},... | collective-permute-start | bytes 98312 | tf_op jit(solution)/shard_map/ppermute | solution.py:351
  6.4 7.1 %collective-permute-start = (bf16[1,64,256]{2,1,0:T(8,128)(2,1)S(1)}, bf16[1,64,256]{2,1,0:T(8,128)(2,1)S(1)}, u32[]{:S(2)}, u32[]{:S(2)}) collective-permute-start(bf16[1,64,256]{2,1,0:T(8,128)(2,1)S(1)} %slice.3.refs_4_.refs_2_), channel_id=1, source_target_pairs={{0,4},{4,8},{8,12},{12,0},{1,5},{5,9},{9,13},{13,1},{2,6},{6,10},{... | collective-permute-start | bytes 98312 | tf_op jit(solution)/shard_map/ppermute | solution.py:351
  12.7 3.9 %copy-start.15 = (s32[16]{0:T(128)S(1)}, s32[16]{0:T(128)}, u32[]{:S(2)}) copy-start(s32[16]{0:T(128)} %param.14) | copy-start | bytes 196
  12.7 3.9 %copy-start.16 = (s32[13]{0:T(128)S(1)}, s32[13]{0:T(128)}, u32[]{:S(2)}) copy-start(s32[13]{0:T(128)} %param.12) | copy-start | bytes 160
  16.5 1.7 %collective-permute-start.3 = (bf16[13,64,128]{2,1,0:T(8,128)(2,1)}, bf16[13,64,128]{2,1,0:T(8,128)(2,1)S(1)}, u32[]{:S(2)}, u32[]{:S(2)}) collective-permute-start(bf16[13,64,128]{2,1,0:T(8,128)(2,1)} %get-tuple-element.22), channel_id=1, source_target_pairs={{0,1},{1,0},{2,3},{3,2},{4,5},{5,4},{6,7},{7,6},{8,9},{9,8},{10,11... | collective-permute-start | bytes 638984 | tf_op jit(solution)/shard_map/ppermute | solution.py:369
  19.2 2.3 %copy-start.2 = (bf16[13,64,128]{2,1,0:T(8,128)(2,1)}, bf16[13,64,128]{2,1,0:T(8,128)(2,1)S(1)}, u32[]{:S(2)}) copy-start(bf16[13,64,128]{2,1,0:T(8,128)(2,1)S(1)} %add_convert_fusion.4.refs_1_) | copy-start | bytes 638980
  19.2 7.4 %collective-permute-start.4 = (bf16[13,64,128]{2,1,0:T(8,128)(2,1)S(1)}, bf16[13,64,128]{2,1,0:T(8,128)(2,1)S(1)}, u32[]{:S(2)}, u32[]{:S(2)}) collective-permute-start(bf16[13,64,128]{2,1,0:T(8,128)(2,1)S(1)} %add_convert_fusion.4.refs_1_), channel_id=1, source_target_pairs={{0,2},{1,3},{2,0},{3,1},{4,6},{5,7},{6,4},{7,5},{8,10},{9,11},{10,... | collective-permute-start | bytes 638984 | tf_op jit(solution)/shard_map/ppermute | solution.py:369
  21.5 20.7 %collective-permute-start.7 = (bf16[1,64,2048]{2,1,0:T(8,128)(2,1)}, bf16[1,64,2048]{2,1,0:T(8,128)(2,1)S(1)}, u32[]{:S(2)}, u32[]{:S(2)}) collective-permute-start(bf16[1,64,2048]{2,1,0:T(8,128)(2,1)} %shard_map.134.refs_10_), channel_id=1, source_target_pairs={{0,12},{4,0},{8,4},{12,8},{1,13},{5,1},{9,5},{13,9},{2,14},{6,2},{... | collective-permute-start | bytes 786440 | tf_op jit(solution)/shard_map/ppermute | solution.py:351
  24.3 24.3 %collective-permute-start.6 = (bf16[1,64,2048]{2,1,0:T(8,128)(2,1)}, bf16[1,64,2048]{2,1,0:T(8,128)(2,1)S(1)}, u32[]{:S(2)}, u32[]{:S(2)}) collective-permute-start(bf16[1,64,2048]{2,1,0:T(8,128)(2,1)} %shard_map.134.refs_10_), channel_id=1, source_target_pairs={{0,8},{4,12},{8,0},{12,4},{1,9},{5,13},{9,1},{13,5},{2,10},{6,14},... | collective-permute-start | bytes 786440 | tf_op jit(solution)/shard_map/ppermute | solution.py:351
  25.4 23.2 %collective-permute-start.5 = (bf16[1,64,2048]{2,1,0:T(8,128)(2,1)}, bf16[1,64,2048]{2,1,0:T(8,128)(2,1)S(1)}, u32[]{:S(2)}, u32[]{:S(2)}) collective-permute-start(bf16[1,64,2048]{2,1,0:T(8,128)(2,1)} %shard_map.134.refs_10_), channel_id=1, source_target_pairs={{0,4},{4,8},{8,12},{12,0},{1,5},{5,9},{9,13},{13,1},{2,6},{6,10},{... | collective-permute-start | bytes 786440 | tf_op jit(solution)/shard_map/ppermute | solution.py:351
  31.6 36.2 %collective-permute-start.9 = (bf16[4,64,2048]{2,1,0:T(8,128)(2,1)}, bf16[4,64,2048]{2,1,0:T(8,128)(2,1)S(1)}, u32[]{:S(2)}, u32[]{:S(2)}) collective-permute-start(bf16[4,64,2048]{2,1,0:T(8,128)(2,1)} %shard_map.132.refs_8_), channel_id=1, source_target_pairs={{0,4},{12,8},{4,0},{8,12},{1,5},{13,9},{5,1},{9,13},{2,6},{14,10},... | collective-permute-start | bytes 3145736 | tf_op jit(solution)/shard_map/ppermute | solution.py:477
  42.1 6.5 %copy-start.7 = (bf16[1,64,2048]{2,1,0:T(8,128)(2,1)}, bf16[1,64,2048]{2,1,0:T(8,128)(2,1)S(1)}, u32[]{:S(2)}) copy-start(bf16[1,64,2048]{2,1,0:T(8,128)(2,1)S(1)} %collective-permute-done.7.refs_9_.refs_13_) | copy-start | bytes 786436
  48.6 0.8 copy-start.9
  61.4 9.0 %collective-permute-start.10 = (bf16[1664,256]{1,0:T(8,128)(2,1)}, bf16[1664,256]{1,0:T(8,128)(2,1)}, u32[]{:S(2)}, u32[]{:S(2)}) collective-permute-start(bf16[1664,256]{1,0:T(8,128)(2,1)} %get-tuple-element.28.refs_1_), channel_id=1, source_target_pairs={{0,1},{1,0},{2,3},{3,2},{4,5},{5,4},{6,7},{7,6},{8,9},{9,8},{10,11... | collective-permute-start | bytes 2555912 | tf_op jit(solution)/shard_map/ppermute | solution.py:369
  61.5 38.4 %collective-permute-start.8 = (bf16[1664,256]{1,0:T(8,128)(2,1)}, bf16[1664,256]{1,0:T(8,128)(2,1)}, u32[]{:S(2)}, u32[]{:S(2)}) collective-permute-start(bf16[1664,256]{1,0:T(8,128)(2,1)} %get-tuple-element.26), channel_id=1, source_target_pairs={{0,1},{1,0},{2,3},{3,2},{4,5},{5,4},{6,7},{7,6},{8,9},{9,8},{10,11... | collective-permute-start | bytes 2555912 | tf_op jit(solution)/shard_map/ppermute | solution.py:369
  69.5 1.0 copy-start.1
  69.5 24.8 %collective-permute-start.18 = (bf16[4,64,2048]{2,1,0:T(8,128)(2,1)S(1)}, bf16[4,64,2048]{2,1,0:T(8,128)(2,1)S(1)}, u32[]{:S(2)}, u32[]{:S(2)}) collective-permute-start(bf16[4,64,2048]{2,1,0:T(8,128)(2,1)S(1)} %add_convert_fusion.2.refs_1_), channel_id=1, source_target_pairs={{0,4},{12,8},{4,12},{8,0},{1,5},{13,9},{5,13},{9,1},{2,6},{14,10},... | collective-permute-start | bytes 3145736 | tf_op jit(solution)/shard_map/ppermute | solution.py:481
  73.0 32.8 %collective-permute-start.11 = (bf16[1664,256]{1,0:T(8,128)(2,1)}, bf16[1664,256]{1,0:T(8,128)(2,1)}, u32[]{:S(2)}, u32[]{:S(2)}) collective-permute-start(bf16[1664,256]{1,0:T(8,128)(2,1)} %add_convert_fusion.3.refs_14_), channel_id=1, source_target_pairs={{0,2},{1,3},{2,0},{3,1},{4,6},{5,7},{6,4},{7,5},{8,10},{9,11},{10,... | collective-permute-start | bytes 2555912 | tf_op jit(solution)/shard_map/ppermute | solution.py:369
  82.3 19.5 %collective-permute-start.14 = (bf16[13,64,128]{2,1,0:T(8,128)(2,1)}, bf16[13,64,128]{2,1,0:T(8,128)(2,1)}, u32[]{:S(2)}, u32[]{:S(2)}) collective-permute-start(bf16[13,64,128]{2,1,0:T(8,128)(2,1)} %shard_map.138.refs_5_.refs_1_), channel_id=1, source_target_pairs={{0,3},{1,2},{2,1},{3,0},{4,7},{5,6},{6,5},{7,4},{8,11},{9,10},{10,... | collective-permute-start | bytes 638984 | tf_op jit(solution)/shard_map/ppermute | solution.py:369
  82.3 17.5 %copy-start.4 = (bf16[13,64,128]{2,1,0:T(8,128)(2,1)S(1)}, bf16[13,64,128]{2,1,0:T(8,128)(2,1)}, u32[]{:S(2)}) copy-start(bf16[13,64,128]{2,1,0:T(8,128)(2,1)} %shard_map.138.refs_5_.refs_1_) | copy-start | bytes 638980
  82.3 19.5 %copy-start.6 = (s32[4]{0:T(128)S(1)}, s32[4]{0:T(128)}, u32[]{:S(2)}) copy-start(s32[4]{0:T(128)} %param.11) | copy-start | bytes 52
  95.9 14.9 %copy-start = (bf16[4,64,2048]{2,1,0:T(8,128)(2,1)}, bf16[4,64,2048]{2,1,0:T(8,128)(2,1)S(1)}, u32[]{:S(2)}) copy-start(bf16[4,64,2048]{2,1,0:T(8,128)(2,1)S(1)} %add_convert_fusion.1.refs_1_) | copy-start | bytes 3145732
  95.9 24.9 %collective-permute-start.20 = (bf16[4,64,2048]{2,1,0:T(8,128)(2,1)S(1)}, bf16[4,64,2048]{2,1,0:T(8,128)(2,1)}, u32[]{:S(2)}, u32[]{:S(2)}) collective-permute-start(bf16[4,64,2048]{2,1,0:T(8,128)(2,1)S(1)} %add_convert_fusion.1.refs_1_), channel_id=1, source_target_pairs={{0,4},{12,8},{1,5},{13,9},{2,6},{14,10},{3,7},{15,11},{16,20},{28,... | collective-permute-start | bytes 3145736 | tf_op jit(solution)/shard_map/ppermute | solution.py:486
  98.2 22.6 %collective-permute-start.19 = (bf16[4,64,2048]{2,1,0:T(8,128)(2,1)S(1)}, bf16[4,64,2048]{2,1,0:T(8,128)(2,1)}, u32[]{:S(2)}, u32[]{:S(2)}) collective-permute-start(bf16[4,64,2048]{2,1,0:T(8,128)(2,1)S(1)} %add_convert_fusion.1.refs_1_), channel_id=1, source_target_pairs={{4,8},{8,4},{5,9},{9,5},{6,10},{10,6},{7,11},{11,7},{20,24},{24,20... | collective-permute-start | bytes 3145736 | tf_op jit(solution)/shard_map/ppermute | solution.py:485
  99.8 6.0 %collective-permute-start.13 = (bf16[13,64,128]{2,1,0:T(8,128)(2,1)S(1)}, bf16[13,64,128]{2,1,0:T(8,128)(2,1)}, u32[]{:S(2)}, u32[]{:S(2)}) collective-permute-start(bf16[13,64,128]{2,1,0:T(8,128)(2,1)S(1)} %copy-done.4), channel_id=1, source_target_pairs={{0,2},{1,3},{2,0},{3,1},{4,6},{5,7},{6,4},{7,5},{8,10},{9,11},{10,... | collective-permute-start | bytes 638984 | tf_op jit(solution)/shard_map/ppermute | solution.py:369
  101.8 4.0 %collective-permute-start.12 = (bf16[13,64,128]{2,1,0:T(8,128)(2,1)S(1)}, bf16[13,64,128]{2,1,0:T(8,128)(2,1)}, u32[]{:S(2)}, u32[]{:S(2)}) collective-permute-start(bf16[13,64,128]{2,1,0:T(8,128)(2,1)S(1)} %copy-done.4), channel_id=1, source_target_pairs={{0,1},{1,0},{2,3},{3,2},{4,5},{5,4},{6,7},{7,6},{8,9},{9,8},{10,11... | collective-permute-start | bytes 638984 | tf_op jit(solution)/shard_map/ppermute | solution.py:369
  110.8 16.4 %collective-permute-start.15 = (bf16[384,256]{1,0:T(8,128)(2,1)}, bf16[384,256]{1,0:T(8,128)(2,1)S(1)}, u32[]{:S(2)}, u32[]{:S(2)}) collective-permute-start(bf16[384,256]{1,0:T(8,128)(2,1)} %get-tuple-element.31), channel_id=1, source_target_pairs={{0,4},{4,8},{8,12},{12,0},{1,5},{5,9},{9,13},{13,1},{2,6},{6,10},{... | collective-permute-start | bytes 589832 | tf_op jit(solution)/shard_map/ppermute | solution.py:351
  110.8 25.2 %collective-permute-start.16 = (bf16[384,256]{1,0:T(8,128)(2,1)}, bf16[384,256]{1,0:T(8,128)(2,1)S(1)}, u32[]{:S(2)}, u32[]{:S(2)}) collective-permute-start(bf16[384,256]{1,0:T(8,128)(2,1)} %get-tuple-element.32), channel_id=1, source_target_pairs={{0,8},{4,12},{8,0},{12,4},{1,9},{5,13},{9,1},{13,5},{2,10},{6,14},... | collective-permute-start | bytes 589832 | tf_op jit(solution)/shard_map/ppermute | solution.py:351
  112.9 23.0 %collective-permute-start.17 = (bf16[384,256]{1,0:T(8,128)(2,1)}, bf16[384,256]{1,0:T(8,128)(2,1)}, u32[]{:S(2)}, u32[]{:S(2)}) collective-permute-start(bf16[384,256]{1,0:T(8,128)(2,1)} %get-tuple-element.33), channel_id=1, source_target_pairs={{0,12},{4,0},{8,4},{12,8},{1,13},{5,1},{9,5},{13,9},{2,14},{6,2},{... | collective-permute-start | bytes 589832 | tf_op jit(solution)/shard_map/ppermute | solution.py:351
  127.1 8.8 %copy-start.10 = (bf16[384,256]{1,0:T(8,128)(2,1)}, bf16[384,256]{1,0:T(8,128)(2,1)S(1)}, u32[]{:S(2)}) copy-start(bf16[384,256]{1,0:T(8,128)(2,1)S(1)} %collective-permute-done.15.refs_2_) | copy-start | bytes 589828
  (6 other events, 4.0 us)

commit v9 on v8

--- a/solution.py
+++ b/solution.py
@@ -32,6 +32,7 @@
         ),
         out_shape=[jax.ShapeDtypeStruct(shape, kind) for shape, kind, _ in outputs],
         input_output_aliases=aliases or {},
+        compiler_params=pltpu.CompilerParams(vmem_limit_bytes=16 * 1024 * 1024),
         cost_estimate=pl.CostEstimate(flops=int(us * 1e9), bytes_accessed=int(us * 3.6e5), transcendentals=0),
     )(*scalars, *[array for array, _ in inputs], *tokens)
 
@@ -65,8 +66,9 @@
     kept = blocks - SW
     last_shape = (SW, *others.shape[1:])
 
-    def kernel(lengths_ref, maps_ref, rows_ref, others_ref, out_ref, last_other):
+    def kernel(lengths_ref, maps_ref, rows_ref, others_ref, out_ref, last_other, last_again):
         last_other[...] = others_ref[...]
+        last_again[...] = others_ref[...]
         for k in range(kept):
             out_ref[k] = masked_rank(maps_ref[k], rows_ref[k * BLOCK : (k + 1) * BLOCK], lengths_ref[k])
 
@@ -82,20 +84,25 @@
         [
             ((blocks, rank, BLOCK), features.dtype, pl.BlockSpec((kept, rank, BLOCK), lambda i, *_: (0, 0, 0))),
             (last_shape, features.dtype, constant_spec(last_shape)),
+            (last_shape, features.dtype, constant_spec(last_shape)),
         ],
         tokens,
     )
 
 
-def with_last_rank(lengths, pick, choices, features, ranks):
+def with_last_rank(lengths, partner, me, choices, features, ranks):
     shape = choices[0].shape
     block = ranks.shape[0] - 1
-
-    def kernel(lengths_ref, pick_ref, *refs):
+    size = partner.shape[0]
+
+    def kernel(lengths_ref, partner_ref, me_ref, *refs):
         rows_ref, _, out_ref, chosen_ref = refs[-4:]
         for k, choice in enumerate(refs[:-4]):
-
-            @pl.when(pick_ref[0] == k)
+            if len(choices) == 1:
+                chosen_ref[...] = choice[...]
+                continue
+
+            @pl.when(partner_ref[lax.rem(me_ref[0] + (size - k), size)] == me_ref[0])
             def _():
                 chosen_ref[...] = choice[...]
 
@@ -103,7 +110,7 @@
 
     return call(
         kernel,
-        (lengths, pick),
+        (lengths, partner, me.reshape(1)),
         (1,),
         [whole(choice) for choice in choices]
         + [(features, pl.BlockSpec((BLOCK, shape[2]), lambda i, *_: (block, 0), pipeline_mode=pl.Buffered(1)))]
@@ -112,7 +119,7 @@
             (ranks.shape, ranks.dtype, pl.BlockSpec((1, *ranks.shape[1:]), lambda i, *_: (block, 0, 0))),
             (shape, features.dtype, constant_spec(shape)),
         ],
-        aliases={3 + len(choices): 0},
+        aliases={4 + len(choices): 0},
     )
 
 
@@ -427,14 +434,16 @@
     lengths = block_live_length
     line = devices == 4
     order = jnp.arange(devices, dtype=jnp.int32)
-    holder = jnp.sum(jnp.where(partner == me, order, 0))
+    holders = jnp.sum(jnp.where(partner[None, :] == order[:, None], order[None, :], 0), axis=1)
+    holder = holders[me]
 
     up_own = adapter_up_matrix[kept:]
-    up_choices, up_pick = shifted(up_own, holder)
-    cot_terms, down_own = kept_ranks(lengths, adapter_up_matrix, cotangent, adapter_down_rows, [up_own])
-    cot_terms, up_last = with_last_rank(lengths, up_pick, up_choices, cotangent, cot_terms)
+    cot_terms, down_own, down_kept = kept_ranks(lengths, adapter_up_matrix, cotangent, adapter_down_rows, [up_own])
+    up_choices, _ = shifted(up_own, holder)
+    cot_terms, up_last = with_last_rank(lengths, partner, me, up_choices, cotangent, cot_terms)
     rank_cot = exchanged(cot_terms)
-    down_choices, down_pick = shifted(after(down_own, rank_cot[0]), holder)
+    me = after(me.reshape(1), rank_cot[0])[0]
+    down_own = after(down_own, rank_cot[0])
 
     table_rows = jnp.sum(
         jnp.where(
@@ -460,7 +469,7 @@
         away = add(after(away, *tokens), near(sent))
         return (mine, near(given), far(away)), away
 
-    def inputs(*tokens):
+    def inputs(down_pick, down_choices, *tokens):
         return spread(
             streamed_ranks(lengths, adapter_down_rows, down_pick, down_choices, hidden, 4, tokens, 100.0)
         )
@@ -475,12 +484,26 @@
         codes = codes_of(jnp.array(ROLES, jnp.int32)[me])
         (first,) = down_rows(codes, 0, 1, 1, rank_cot, hidden)
         from_first = lax.ppermute(first, "dp", [(0, 1), (3, 2), (1, 0), (2, 3)])
-        second, third, own = down_rows(codes, OWN, 3, 1, rank_cot, hidden, [first], 1.0)
-        terms = base(second, *down_choices[1:])
+        from_left = lax.ppermute(down_own, "dp", [(0, 1), (1, 2)])
+        from_right = lax.ppermute(down_own, "dp", [(3, 2), (2, 1)])
+        second, third, own = down_rows(codes, OWN, 3, 1, rank_cot, hidden, [first])
+        passing = jnp.where(after(me.reshape(1), second)[0] == 1, from_left, from_right)
+        passed = lax.ppermute(passing, "dp", [(1, 2), (2, 1)])
+        terms = base(second, passing)
         second = add(after(second, terms[0]), jnp.where(inner, from_first, jnp.zeros((), first.dtype)))
         from_second = lax.ppermute(second, "dp", [(0, 1), (3, 2), (1, 3), (2, 0)])
+        down_kept = after(down_kept, second)
+
+        def place(wanted):
+            return jnp.where(wanted == me, 0, jnp.where(wanted == me - 1, 1, jnp.where(wanted == me + 1, 2, 3)))
+
+        wanted = place(jnp.where(me == 1, holders[0], holders[3]))
+        outward = jnp.where(wanted == 1, from_left, jnp.where(wanted == 2, from_right, passed))
+        outward = lax.ppermute(jnp.where(wanted == 0, down_kept, outward), "dp", [(2, 3), (1, 0)])
+        down_choices = [down_kept, from_left, from_right, passed, outward]
+        down_pick = jnp.where(inner | (holder == me), place(holder), 4).reshape(1).astype(jnp.int32)
         base_sums, away = base_parts(terms, second)
-        rank_in = inputs(away)
+        rank_in = inputs(down_pick, down_choices, away)
         third = add(after(third, rank_in[0]), jnp.where(inner, from_second, jnp.zeros((), first.dtype)))
         from_inner = lax.ppermute(third, "dp", [(1, 2), (2, 1)])
         from_third = lax.ppermute(third, "dp", [(0, 1), (3, 2)])
@@ -498,8 +521,9 @@
     else:
         codes = codes_of(order)
         (table,) = down_rows(codes, 0, devices, 0, rank_cot, hidden)
+        down_choices, down_pick = shifted(down_kept, holder)
         down_out = line_reduce_scatter(table.reshape(devices, OWN, *table.shape[1:]))
-        values, table = outputs(codes, [devices * OWN], base_parts(base(table))[0], inputs(table))
+        values, table = outputs(codes, [devices * OWN], base_parts(base(table))[0], inputs(down_pick, down_choices, table))
         up_table, last_values = table[:-BLOCK], table[-BLOCK:]
         up_out = line_reduce_scatter(up_table.reshape(devices, OWN, -1, values.shape[1]))
         (last_values,), _ = shifted(last_values, partner[me])

time: 139 us -> 147 us (1.058); the launches traced: 139 us -> 144 us
  Pallas kernels: 44.6 us -> 26.1 us
  local copies, waits for them, and re-layouts: 5.25 us -> 15.2 us
  between operations: 2.2 us -> 11.9 us
  other arithmetic: 15.2 us -> 7.39 us
  waiting for transfers between devices: 45.5 us -> 52.9 us
  starting transfers between devices: 25.8 us -> 30.8 us
    ppermute x0 -> x4, waiting for transfers between devices: none -> 25.4 us  [the longest x1 25.4 us: body(): lax.ppermute(jnp.where(wanted == 0, down_kept, outward), 'dp', [(2, 3), (...]
    pallas_call x13 -> x16, Pallas kernels: 44.6 us -> 26.1 us  [call(): pl.pallas_call(run, grid_spec=pltpu.PrefetchScalarGridSpec(num_scalar_pre...]
    ppermute x1, waiting for transfers between devices: 11.9 us -> 0.01 us  [body(): from_second = lax.ppermute(second, 'dp', [(0, 1), (3, 2), (1, 3), (2, 0)])]
    unnamed x34 -> x56, local copies, waits for them, and re-layouts: 3.73 us -> 13.1 us
    ppermute x0 -> x4, starting transfers between devices: none -> 7.64 us  [the longest x1 5.01 us: body(): from_left = lax.ppermute(down_own, 'dp', [(0, 1), (1, 2)])]
    ppermute x9 -> x6, waiting for transfers between devices: 18.6 us -> 13.8 us  [shift(): lax.ppermute(array, 'dp', [(i, (i + by) % size) for i in range(size)])]
    convert_element_type x4, other arithmetic: 6.75 us -> 2.02 us  [add(): sum((array.astype(jnp.float32) for array in arrays)).astype(arrays[0].dtype)]
    ppermute x9 -> x6, starting transfers between devices: 13.8 us -> 9.89 us  [shift(): lax.ppermute(array, 'dp', [(i, (i + by) % size) for i in range(size)])]
  transfers between devices with their start and end apart: 21 -> 22, of which waited for: 9 -> 8; matrix products, arithmetic and copies ran while one was open for 11% -> 6% of each run, Pallas kernels for 29% -> 17%
where the time goes in v9:
time: 147 us; the launch traced here: 144 us
  waiting for transfers between devices  52.9 us (36%)
  starting transfers between devices  30.8 us (21%)
  Pallas kernels  26.1 us (18%)
  local copies, waits for them, and re-layouts  15.2 us (10%)
  between operations  11.9 us (8%)
  other arithmetic  7.39 us (5%)
    pallas_call x16, Pallas kernels, call(): pl.pallas_call(run, grid_spec=pltpu.PrefetchScalarGridSpec(num_scalar_pre...  26.1 us
    ppermute x1, waiting for transfers between devices, body(): lax.ppermute(jnp.where(wanted == 0, down_kept, outward), 'dp', [(2, 3), (...  25.4 us
    ppermute x6, waiting for transfers between devices, shift(): lax.ppermute(array, 'dp', [(i, (i + by) % size) for i in range(size)])  13.8 us
    unnamed x56, local copies, waits for them, and re-layouts  13.1 us
    ppermute x6, starting transfers between devices, shift(): lax.ppermute(array, 'dp', [(i, (i + by) % size) for i in range(size)])  9.89 us
    ppermute x8, waiting for transfers between devices, crossed(): lax.ppermute(array, 'tensor', [(i, i ^ by) for i in range(lax.axis_size('...  6.73 us
    ppermute x1, waiting for transfers between devices, body(): from_first = lax.ppermute(first, 'dp', [(0, 1), (3, 2), (1, 0), (2, 3)])  6.48 us
    ppermute x1, starting transfers between devices, body(): from_left = lax.ppermute(down_own, 'dp', [(0, 1), (1, 2)])  5.01 us
  transfers between devices with their start and end apart: 22, of which 8 were waited for; matrix products, arithmetic and copies ran while one was open for 6% of the time, Pallas kernels for 17%

profile of v9, /device:TPU:0, one launch (start us, length us, event | category | flops | bytes accessed | tf_op | source)
XLA Modules:
  0.0 144.4 jit_solution(1610853907361093481)
XLA Ops:
  1.4 5.0 %collective-permute-start.2 = (bf16[1,64,256]{2,1,0:T(8,128)(2,1)S(1)}, bf16[1,64,256]{2,1,0:T(8,128)(2,1)S(1)}, u32[]{:S(2)}, u32[]{:S(2)}) collective-permute-start(bf16[1,64,256]{2,1,0:T(8,128)(2,1)S(1)} %slice.9.refs_4_.refs_3_), channel_id=1, source_target_pairs={{0,12},{4,0},{8,4},{12,8},{1,13},{5,1},{9,5},{13,9},{2,14},{6,2},{... | collective-permute-start | bytes 98312 | tf_op jit(solution)/shard_map/ppermute | solution.py:358
  6.4 1.0 collective-permute-start
  8.9 1.2 copy-done.1
  10.0 2.0 %copy-done.4 = bf16[13,64,2048]{2,1,0:T(8,128)(2,1)S(1)} copy-done((bf16[13,64,2048]{2,1,0:T(8,128)(2,1)S(1)}, bf16[13,64,2048]{2,1,0:T(8,128)(2,1)}, u32[]{:S(2)}) %copy-start.4) | copy-done | bytes 3407896
  12.0 1.0 copy-done.6
  15.9 1.2 collective-permute-done.3
  22.7 1.6 %collective-permute-start.4 = (bf16[13,64,128]{2,1,0:T(8,128)(2,1)S(1)}, bf16[13,64,128]{2,1,0:T(8,128)(2,1)S(1)}, u32[]{:S(2)}, u32[]{:S(2)}) collective-permute-start(bf16[13,64,128]{2,1,0:T(8,128)(2,1)S(1)} %add_convert_fusion.4.refs_1_), channel_id=1, source_target_pairs={{0,2},{1,3},{2,0},{3,1},{4,6},{5,7},{6,4},{7,5},{8,10},{9,11},{10,... | collective-permute-start | bytes 638984 | tf_op jit(solution)/shard_map/ppermute | solution.py:376
  24.9 5.0 %collective-permute-start.5 = (bf16[1,64,2048]{2,1,0:T(8,128)(2,1)S(1)}, bf16[1,64,2048]{2,1,0:T(8,128)(2,1)S(1)}, u32[]{:S(2)}, u32[]{:S(2)}) collective-permute-start(bf16[1,64,2048]{2,1,0:T(8,128)(2,1)S(1)} %shard_map.136), channel_id=1, source_target_pairs={{0,4},{4,8},{1,5},{5,9},{2,6},{6,10},{3,7},{7,11},{16,20},{20,24},... | collective-permute-start | bytes 786440 | tf_op jit(solution)/shard_map/ppermute | solution.py:487
  37.5 2.9 %copy-done = bf16[1664,2048]{1,0:T(8,128)(2,1)S(1)} copy-done((bf16[1664,2048]{1,0:T(8,128)(2,1)S(1)}, bf16[1664,2048]{1,0:T(8,128)(2,1)}, u32[]{:S(2)}) %copy-start) | copy-done | bytes 6815768
  40.5 1.4 shard_map.133.refs_8_
  41.9 2.7 %collective-permute-start.8 = (bf16[4,64,2048]{2,1,0:T(8,128)(2,1)S(1)}, bf16[4,64,2048]{2,1,0:T(8,128)(2,1)S(1)}, u32[]{:S(2)}, u32[]{:S(2)}) collective-permute-start(bf16[4,64,2048]{2,1,0:T(8,128)(2,1)S(1)} %shard_map.133.refs_8_), channel_id=1, source_target_pairs={{0,4},{12,8},{4,0},{8,12},{1,5},{13,9},{5,1},{9,13},{2,6},{14,10},... | collective-permute-start | bytes 3145736 | tf_op jit(solution)/shard_map/ppermute | solution.py:486
  44.6 3.6 %shard_map.134 = (bf16[4,64,2048]{2,1,0:T(8,128)(2,1)S(1)}, bf16[4,64,2048]{2,1,0:T(8,128)(2,1)S(1)}, bf16[4,64,2048]{2,1,0:T(8,128)(2,1)S(1)}) custom-call(s32[16]{0:T(128)S(1)} %get-tuple-element.41.refs_0_, bf16[13,64,128]{2,1,0:T(8,128)(2,1)S(1)} %add_convert_fusion.4.refs_1_, bf16[13,64,128]{2,1,0:T(8,128)(2,1)S(1)} %collective-permute-done.4.refs_2_, ...), custom_call_target="tpu_custom_call" | custom-call | flops 1000000000 | bytes 360000 | tf_op jit(solution)/shard_map/pallas_call | solution.py:24
  48.3 1.2 shard_map.135
  50.9 9.0 %shard_map.137 = (bf16[1664,256]{1,0:T(8,128)(2,1)S(1)}, bf16[1664,256]{1,0:T(8,128)(2,1)S(1)}, bf16[1664,256]{1,0:T(8,128)(2,1)S(1)}, bf16[1664,256]{1,0:T(8,128)(2,1)S(1)}) custom-call(s32[4]{0:T(128)S(1)} %pad_add_fusion.refs_0_, bf16[1664,2048]{1,0:T(8,128)(2,1)S(1)} %bitcast.17, bf16[2048,1024]{1,0:T(8,128)(2,1)S(1)} %copy-done.17, ...), custom_call_target="tpu_custom_call" | custom-call | flops 99999997952 | bytes 36000000 | tf_op jit(solution)/shard_map/pallas_call | solution.py:24
  60.8 6.5 %collective-permute-done.8 = bf16[4,64,2048]{2,1,0:T(8,128)(2,1)S(1)} collective-permute-done((bf16[4,64,2048]{2,1,0:T(8,128)(2,1)S(1)}, bf16[4,64,2048]{2,1,0:T(8,128)(2,1)S(1)}, u32[]{:S(2)}, u32[]{:S(2)}) %collective-permute-start.8) | collective-permute-done | bytes 1048608 | tf_op jit(solution)/shard_map/ppermute | solution.py:486
  67.7 1.8 %collective-permute-start.19 = (bf16[4,64,2048]{2,1,0:T(8,128)(2,1)S(1)}, bf16[4,64,2048]{2,1,0:T(8,128)(2,1)S(1)}, u32[]{:S(2)}, u32[]{:S(2)}) collective-permute-start(bf16[4,64,2048]{2,1,0:T(8,128)(2,1)S(1)} %add_convert_fusion.2.refs_1_), channel_id=1, source_target_pairs={{0,4},{12,8},{4,12},{8,0},{1,5},{13,9},{5,13},{9,1},{2,6},{14,10},... | collective-permute-start | bytes 3145736 | tf_op jit(solution)/shard_map/ppermute | solution.py:494
  69.5 1.3 collective-permute-start.12
  70.8 1.2 add_convert_fusion.3.refs_15_
  72.6 25.4 %collective-permute-done.12.refs_14_ = bf16[1,64,2048]{2,1,0:T(8,128)(2,1)S(1)} collective-permute-done((bf16[1,64,2048]{2,1,0:T(8,128)(2,1)S(1)}, bf16[1,64,2048]{2,1,0:T(8,128)(2,1)S(1)}, u32[]{:S(2)}, u32[]{:S(2)}) %collective-permute-start.12) | collective-permute-done | bytes 262176 | tf_op jit(solution)/shard_map/ppermute | solution.py:502
  98.0 4.2 %shard_map.141.refs_5_.refs_1_ = bf16[13,64,128]{2,1,0:T(8,128)(2,1)} custom-call(s32[13]{0:T(128)S(1)} %copy-done.16, s32[1]{0:T(128)} %bitcast.11.refs_1_, bf16[13,64,2048]{2,1,0:T(8,128)(2,1)S(1)} %copy-done.5, bf16[13,64,2048]{2,1,0:T(8,128)(2,1)S(1)} %copy-done.5, bf16[13,64,2048]{2,1,0:T(8,128)(2,1)S(1)} %copy-done.5, ...), custom_call_target="tpu_custom_call" | custom-call | flops 99999997952 | bytes 36000000 | tf_op jit(solution)/shard_map/pallas_call | solution.py:24
  102.7 2.6 %collective-permute-start.21 = (bf16[4,64,2048]{2,1,0:T(8,128)(2,1)S(1)}, bf16[4,64,2048]{2,1,0:T(8,128)(2,1)}, u32[]{:S(2)}, u32[]{:S(2)}) collective-permute-start(bf16[4,64,2048]{2,1,0:T(8,128)(2,1)S(1)} %add_convert_fusion.1.refs_1_), channel_id=1, source_target_pairs={{0,4},{12,8},{1,5},{13,9},{2,6},{14,10},{3,7},{15,11},{16,20},{28,... | collective-permute-start | bytes 3145736 | tf_op jit(solution)/shard_map/ppermute | solution.py:509
  105.3 1.8 %collective-permute-start.20 = (bf16[4,64,2048]{2,1,0:T(8,128)(2,1)S(1)}, bf16[4,64,2048]{2,1,0:T(8,128)(2,1)}, u32[]{:S(2)}, u32[]{:S(2)}) collective-permute-start(bf16[4,64,2048]{2,1,0:T(8,128)(2,1)S(1)} %add_convert_fusion.1.refs_1_), channel_id=1, source_target_pairs={{4,8},{8,4},{5,9},{9,5},{6,10},{10,6},{7,11},{11,7},{20,24},{24,20... | collective-permute-start | bytes 3145736 | tf_op jit(solution)/shard_map/ppermute | solution.py:508
  108.1 1.5 %collective-permute-start.14 = (bf16[13,64,128]{2,1,0:T(8,128)(2,1)}, bf16[13,64,128]{2,1,0:T(8,128)(2,1)}, u32[]{:S(2)}, u32[]{:S(2)}) collective-permute-start(bf16[13,64,128]{2,1,0:T(8,128)(2,1)} %shard_map.141.refs_5_.refs_1_), channel_id=1, source_target_pairs={{0,2},{1,3},{2,0},{3,1},{4,6},{5,7},{6,4},{7,5},{8,10},{9,11},{10,... | collective-permute-start | bytes 638984 | tf_op jit(solution)/shard_map/ppermute | solution.py:376
  110.5 5.3 %collective-permute-done.14.refs_7_ = bf16[13,64,128]{2,1,0:T(8,128)(2,1)} collective-permute-done((bf16[13,64,128]{2,1,0:T(8,128)(2,1)}, bf16[13,64,128]{2,1,0:T(8,128)(2,1)}, u32[]{:S(2)}, u32[]{:S(2)}) %collective-permute-start.14) | collective-permute-done | bytes 213024 | tf_op jit(solution)/shard_map/ppermute | solution.py:376
  115.9 1.1 copy-done.10
  117.0 1.2 copy-done.12
  119.1 3.7 %shard_map.142 = (bf16[1664,256]{1,0:T(8,128)(2,1)}, bf16[384,256]{1,0:T(8,128)(2,1)S(1)}, bf16[384,256]{1,0:T(8,128)(2,1)S(1)}, bf16[384,256]{1,0:T(8,128)(2,1)S(1)}, bf16[384,256]{1,0:T(8,128)(2,1)S(1)}) custom-call(s32[13]{0:T(128)S(1)} %copy-done.16, s32[16]{0:T(128)S(1)} %get-tuple-element.42.refs_1_, bf16[1664,256]{1,0:T(8,128)(2,1)S(1)} %copy-done.10, ...), custom_call_target="tpu_custom_call" | custom-call | flops 1000000000 | bytes 360000 | tf_op jit(solution)/shard_map/pallas_call | solution.py:24
  122.9 1.7 %collective-permute-start.17 = (bf16[384,256]{1,0:T(8,128)(2,1)S(1)}, bf16[384,256]{1,0:T(8,128)(2,1)S(1)}, u32[]{:S(2)}, u32[]{:S(2)}) collective-permute-start(bf16[384,256]{1,0:T(8,128)(2,1)S(1)} %get-tuple-element.34), channel_id=1, source_target_pairs={{0,8},{4,12},{8,0},{12,4},{1,9},{5,13},{9,1},{13,5},{2,10},{6,14},... | collective-permute-start | bytes 589832 | tf_op jit(solution)/shard_map/ppermute | solution.py:358
  124.6 2.1 %collective-permute-start.18 = (bf16[384,256]{1,0:T(8,128)(2,1)S(1)}, bf16[384,256]{1,0:T(8,128)(2,1)S(1)}, u32[]{:S(2)}, u32[]{:S(2)}) collective-permute-start(bf16[384,256]{1,0:T(8,128)(2,1)S(1)} %get-tuple-element.35), channel_id=1, source_target_pairs={{0,12},{4,0},{8,4},{12,8},{1,13},{5,1},{9,5},{13,9},{2,14},{6,2},{... | collective-permute-start | bytes 589832 | tf_op jit(solution)/shard_map/ppermute | solution.py:358
  127.8 2.1 %add_convert_fusion.refs_6_ = bf16[4,64,2048]{2,1,0:T(8,128)(2,1)S(1)} fusion(bf16[4,64,2048]{2,1,0:T(8,128)(2,1)} %collective-permute-done.21, f32[4,64,2048]{2,1,0:T(8,128)S(1)} %select_add_fusion, bf16[4,64,2048]{2,1,0:T(8,128)(2,1)} %collective-permute-done.20), kind=kLoop, calls=%fused_computation | loop fusion | flops 2621440 | bytes 5242880 | tf_op jit(solution)/shard_map/convert_element_type | solution.py:514
  129.9 3.8 %collective-permute-done.16.refs_2_ = bf16[384,256]{1,0:T(8,128)(2,1)S(1)} collective-permute-done((bf16[384,256]{1,0:T(8,128)(2,1)S(1)}, bf16[384,256]{1,0:T(8,128)(2,1)S(1)}, u32[]{:S(2)}, u32[]{:S(2)}) %collective-permute-start.16) | collective-permute-done | bytes 196640 | tf_op jit(solution)/shard_map/ppermute | solution.py:358
  133.7 9.9 %collective-permute-done.17.refs_3_ = bf16[384,256]{1,0:T(8,128)(2,1)S(1)} collective-permute-done((bf16[384,256]{1,0:T(8,128)(2,1)S(1)}, bf16[384,256]{1,0:T(8,128)(2,1)S(1)}, u32[]{:S(2)}, u32[]{:S(2)}) %collective-permute-start.17) | collective-permute-done | bytes 196640 | tf_op jit(solution)/shard_map/ppermute | solution.py:358
  (107 shorter events, 16.5 us)
Async XLA Ops:
  1.4 13.3 %collective-permute-start.2 = (bf16[1,64,256]{2,1,0:T(8,128)(2,1)S(1)}, bf16[1,64,256]{2,1,0:T(8,128)(2,1)S(1)}, u32[]{:S(2)}, u32[]{:S(2)}) collective-permute-start(bf16[1,64,256]{2,1,0:T(8,128)(2,1)S(1)} %slice.9.refs_4_.refs_3_), channel_id=1, source_target_pairs={{0,12},{4,0},{8,4},{12,8},{1,13},{5,1},{9,5},{13,9},{2,14},{6,2},{... | collective-permute-start | bytes 98312 | tf_op jit(solution)/shard_map/ppermute | solution.py:358
  6.4 8.2 %collective-permute-start.1 = (bf16[1,64,256]{2,1,0:T(8,128)(2,1)S(1)}, bf16[1,64,256]{2,1,0:T(8,128)(2,1)S(1)}, u32[]{:S(2)}, u32[]{:S(2)}) collective-permute-start(bf16[1,64,256]{2,1,0:T(8,128)(2,1)S(1)} %slice.9.refs_4_.refs_3_), channel_id=1, source_target_pairs={{0,8},{4,12},{8,0},{12,4},{1,9},{5,13},{9,1},{13,5},{2,10},{6,14},... | collective-permute-start | bytes 98312 | tf_op jit(solution)/shard_map/ppermute | solution.py:358
  6.4 8.2 %collective-permute-start = (bf16[1,64,256]{2,1,0:T(8,128)(2,1)S(1)}, bf16[1,64,256]{2,1,0:T(8,128)(2,1)S(1)}, u32[]{:S(2)}, u32[]{:S(2)}) collective-permute-start(bf16[1,64,256]{2,1,0:T(8,128)(2,1)S(1)} %slice.9.refs_4_.refs_3_), channel_id=1, source_target_pairs={{0,4},{4,8},{8,12},{12,0},{1,5},{5,9},{9,13},{13,1},{2,6},{6,10},{... | collective-permute-start | bytes 98312 | tf_op jit(solution)/shard_map/ppermute | solution.py:358
  14.8 17.1 %copy-start.25 = (s32[4]{0:T(128)S(1)}, s32[4]{0:T(128)}, u32[]{:S(2)}) copy-start(s32[4]{0:T(128)} %constant.52.clone) | copy-start | bytes 52
  15.6 1.5 %collective-permute-start.3 = (bf16[13,64,128]{2,1,0:T(8,128)(2,1)S(1)}, bf16[13,64,128]{2,1,0:T(8,128)(2,1)S(1)}, u32[]{:S(2)}, u32[]{:S(2)}) collective-permute-start(bf16[13,64,128]{2,1,0:T(8,128)(2,1)S(1)} %get-tuple-element.23), channel_id=1, source_target_pairs={{0,1},{1,0},{2,3},{3,2},{4,5},{5,4},{6,7},{7,6},{8,9},{9,8},{10,11... | collective-permute-start | bytes 638984 | tf_op jit(solution)/shard_map/ppermute | solution.py:376
  22.7 14.8 %collective-permute-start.4 = (bf16[13,64,128]{2,1,0:T(8,128)(2,1)S(1)}, bf16[13,64,128]{2,1,0:T(8,128)(2,1)S(1)}, u32[]{:S(2)}, u32[]{:S(2)}) collective-permute-start(bf16[13,64,128]{2,1,0:T(8,128)(2,1)S(1)} %add_convert_fusion.4.refs_1_), channel_id=1, source_target_pairs={{0,2},{1,3},{2,0},{3,1},{4,6},{5,7},{6,4},{7,5},{8,10},{9,11},{10,... | collective-permute-start | bytes 638984 | tf_op jit(solution)/shard_map/ppermute | solution.py:376
  24.3 25.8 %collective-permute-start.6 = (bf16[1,64,2048]{2,1,0:T(8,128)(2,1)S(1)}, bf16[1,64,2048]{2,1,0:T(8,128)(2,1)S(1)}, u32[]{:S(2)}, u32[]{:S(2)}) collective-permute-start(bf16[1,64,2048]{2,1,0:T(8,128)(2,1)S(1)} %shard_map.136), channel_id=1, source_target_pairs={{12,8},{8,4},{13,9},{9,5},{14,10},{10,6},{15,11},{11,7},{28,24},{2... | collective-permute-start | bytes 786440 | tf_op jit(solution)/shard_map/ppermute | solution.py:488
  24.9 25.1 %collective-permute-start.5 = (bf16[1,64,2048]{2,1,0:T(8,128)(2,1)S(1)}, bf16[1,64,2048]{2,1,0:T(8,128)(2,1)S(1)}, u32[]{:S(2)}, u32[]{:S(2)}) collective-permute-start(bf16[1,64,2048]{2,1,0:T(8,128)(2,1)S(1)} %shard_map.136), channel_id=1, source_target_pairs={{0,4},{4,8},{1,5},{5,9},{2,6},{6,10},{3,7},{7,11},{16,20},{20,24},... | collective-permute-start | bytes 786440 | tf_op jit(solution)/shard_map/ppermute | solution.py:487
  40.5 10.3 %slice-start = ((s8[6815744]{0:T(1024)(128)(4,1)}), s8[4194304]{0:T(1024)(128)(4,1)S(1)}, s32[]{:S(2)}) async-start(s8[6815744]{0:T(1024)(128)(4,1)} %bitcast.16), calls=%async_computation | async-start | bytes 8388608
  41.9 8.9 %slice-start.1 = ((s8[6815744]{0:T(1024)(128)(4,1)}), s8[2621440]{0:T(1024)(128)(4,1)S(1)}, s32[]{:S(2)}) async-start(s8[6815744]{0:T(1024)(128)(4,1)} %bitcast.16), calls=%async_computation.1 | async-start | bytes 5242880
  41.9 8.9 %copy-start.17 = (bf16[2048,1024]{1,0:T(8,128)(2,1)S(1)}, bf16[2048,1024]{1,0:T(8,128)(2,1)}, u32[]{:S(2)}) copy-start(bf16[2048,1024]{1,0:T(8,128)(2,1)} %refs_5_.6) | copy-start | bytes 12582916
  41.9 25.3 %collective-permute-start.8 = (bf16[4,64,2048]{2,1,0:T(8,128)(2,1)S(1)}, bf16[4,64,2048]{2,1,0:T(8,128)(2,1)S(1)}, u32[]{:S(2)}, u32[]{:S(2)}) collective-permute-start(bf16[4,64,2048]{2,1,0:T(8,128)(2,1)S(1)} %shard_map.133.refs_8_), channel_id=1, source_target_pairs={{0,4},{12,8},{4,0},{8,12},{1,5},{13,9},{5,1},{9,13},{2,6},{14,10},... | collective-permute-start | bytes 3145736 | tf_op jit(solution)/shard_map/ppermute | solution.py:486
  50.1 19.3 %collective-permute-start.11 = (bf16[1,64,2048]{2,1,0:T(8,128)(2,1)S(1)}, bf16[1,64,2048]{2,1,0:T(8,128)(2,1)S(1)}, u32[]{:S(2)}, u32[]{:S(2)}) collective-permute-start(bf16[1,64,2048]{2,1,0:T(8,128)(2,1)S(1)} %broadcast_select_fusion.refs_7_), channel_id=1, source_target_pairs={{4,8},{8,4},{5,9},{9,5},{6,10},{10,6},{7,11},{11,7},{20,24},{24,20... | collective-permute-start | bytes 786440 | tf_op jit(solution)/shard_map/ppermute | solution.py:491
  59.9 47.3 %collective-permute-start.7 = (bf16[1664,256]{1,0:T(8,128)(2,1)S(1)}, bf16[1664,256]{1,0:T(8,128)(2,1)S(1)}, u32[]{:S(2)}, u32[]{:S(2)}) collective-permute-start(bf16[1664,256]{1,0:T(8,128)(2,1)S(1)} %get-tuple-element.27), channel_id=1, source_target_pairs={{0,1},{1,0},{2,3},{3,2},{4,5},{5,4},{6,7},{7,6},{8,9},{9,8},{10,11... | collective-permute-start | bytes 2555912 | tf_op jit(solution)/shard_map/ppermute | solution.py:376
  60.0 10.9 %collective-permute-start.9 = (bf16[1664,256]{1,0:T(8,128)(2,1)S(1)}, bf16[1664,256]{1,0:T(8,128)(2,1)S(1)}, u32[]{:S(2)}, u32[]{:S(2)}) collective-permute-start(bf16[1664,256]{1,0:T(8,128)(2,1)S(1)} %get-tuple-element.29.refs_1_), channel_id=1, source_target_pairs={{0,1},{1,0},{2,3},{3,2},{4,5},{5,4},{6,7},{7,6},{8,9},{9,8},{10,11... | collective-permute-start | bytes 2555912 | tf_op jit(solution)/shard_map/ppermute | solution.py:376
  67.7 34.7 %collective-permute-start.19 = (bf16[4,64,2048]{2,1,0:T(8,128)(2,1)S(1)}, bf16[4,64,2048]{2,1,0:T(8,128)(2,1)S(1)}, u32[]{:S(2)}, u32[]{:S(2)}) collective-permute-start(bf16[4,64,2048]{2,1,0:T(8,128)(2,1)S(1)} %add_convert_fusion.2.refs_1_), channel_id=1, source_target_pairs={{0,4},{12,8},{4,12},{8,0},{1,5},{13,9},{5,13},{9,1},{2,6},{14,10},... | collective-permute-start | bytes 3145736 | tf_op jit(solution)/shard_map/ppermute | solution.py:494
  69.5 28.4 %collective-permute-start.12 = (bf16[1,64,2048]{2,1,0:T(8,128)(2,1)S(1)}, bf16[1,64,2048]{2,1,0:T(8,128)(2,1)S(1)}, u32[]{:S(2)}, u32[]{:S(2)}) collective-permute-start(bf16[1,64,2048]{2,1,0:T(8,128)(2,1)S(1)} %select_select_fusion), channel_id=1, source_target_pairs={{8,12},{4,0},{9,13},{5,1},{10,14},{6,2},{11,15},{7,3},{24,28},{20,... | collective-permute-start | bytes 786440 | tf_op jit(solution)/shard_map/ppermute | solution.py:502
  70.8 27.1 %copy-start.5 = (bf16[13,64,2048]{2,1,0:T(8,128)(2,1)S(1)}, bf16[13,64,2048]{2,1,0:T(8,128)(2,1)}, u32[]{:S(2)}) copy-start(bf16[13,64,2048]{2,1,0:T(8,128)(2,1)} %refs_5_.7) | copy-start | bytes 10223620
  72.0 43.8 %collective-permute-start.10 = (bf16[1664,256]{1,0:T(8,128)(2,1)}, bf16[1664,256]{1,0:T(8,128)(2,1)}, u32[]{:S(2)}, u32[]{:S(2)}) collective-permute-start(bf16[1664,256]{1,0:T(8,128)(2,1)} %add_convert_fusion.3.refs_15_), channel_id=1, source_target_pairs={{0,2},{1,3},{2,0},{3,1},{4,6},{5,7},{6,4},{7,5},{8,10},{9,11},{10,... | collective-permute-start | bytes 2555912 | tf_op jit(solution)/shard_map/ppermute | solution.py:376
  102.2 7.6 %collective-permute-start.15 = (bf16[13,64,128]{2,1,0:T(8,128)(2,1)}, bf16[13,64,128]{2,1,0:T(8,128)(2,1)S(1)}, u32[]{:S(2)}, u32[]{:S(2)}) collective-permute-start(bf16[13,64,128]{2,1,0:T(8,128)(2,1)} %shard_map.141.refs_5_.refs_1_), channel_id=1, source_target_pairs={{0,3},{1,2},{2,1},{3,0},{4,7},{5,6},{6,5},{7,4},{8,11},{9,10},{10,... | collective-permute-start | bytes 638984 | tf_op jit(solution)/shard_map/ppermute | solution.py:376
  102.3 13.5 %copy-start.3 = (bf16[1664,256]{1,0:T(8,128)(2,1)S(1)}, bf16[1664,256]{1,0:T(8,128)(2,1)}, u32[]{:S(2)}) copy-start(bf16[1664,256]{1,0:T(8,128)(2,1)} %refs_9_.3) | copy-start | bytes 2555908
  102.3 13.5 %copy-start.7 = (bf16[13,64,256]{2,1,0:T(8,128)(2,1)S(1)}, bf16[13,64,256]{2,1,0:T(8,128)(2,1)}, u32[]{:S(2)}) copy-start(bf16[13,64,256]{2,1,0:T(8,128)(2,1)} %refs_10_.1) | copy-start | bytes 1277956
  102.3 7.4 %copy-start.21 = (bf16[4,64,2048]{2,1,0:T(8,128)(2,1)}, bf16[4,64,2048]{2,1,0:T(8,128)(2,1)S(1)}, u32[]{:S(2)}) copy-start(bf16[4,64,2048]{2,1,0:T(8,128)(2,1)S(1)} %collective-permute-done.19) | copy-start | bytes 3145732
  102.7 25.0 %collective-permute-start.21 = (bf16[4,64,2048]{2,1,0:T(8,128)(2,1)S(1)}, bf16[4,64,2048]{2,1,0:T(8,128)(2,1)}, u32[]{:S(2)}, u32[]{:S(2)}) collective-permute-start(bf16[4,64,2048]{2,1,0:T(8,128)(2,1)S(1)} %add_convert_fusion.1.refs_1_), channel_id=1, source_target_pairs={{0,4},{12,8},{1,5},{13,9},{2,6},{14,10},{3,7},{15,11},{16,20},{28,... | collective-permute-start | bytes 3145736 | tf_op jit(solution)/shard_map/ppermute | solution.py:509
  105.3 22.4 %collective-permute-start.20 = (bf16[4,64,2048]{2,1,0:T(8,128)(2,1)S(1)}, bf16[4,64,2048]{2,1,0:T(8,128)(2,1)}, u32[]{:S(2)}, u32[]{:S(2)}) collective-permute-start(bf16[4,64,2048]{2,1,0:T(8,128)(2,1)S(1)} %add_convert_fusion.1.refs_1_), channel_id=1, source_target_pairs={{4,8},{8,4},{5,9},{9,5},{6,10},{10,6},{7,11},{11,7},{20,24},{24,20... | collective-permute-start | bytes 3145736 | tf_op jit(solution)/shard_map/ppermute | solution.py:508
  108.1 7.8 %collective-permute-start.14 = (bf16[13,64,128]{2,1,0:T(8,128)(2,1)}, bf16[13,64,128]{2,1,0:T(8,128)(2,1)}, u32[]{:S(2)}, u32[]{:S(2)}) collective-permute-start(bf16[13,64,128]{2,1,0:T(8,128)(2,1)} %shard_map.141.refs_5_.refs_1_), channel_id=1, source_target_pairs={{0,2},{1,3},{2,0},{3,1},{4,6},{5,7},{6,4},{7,5},{8,10},{9,11},{10,... | collective-permute-start | bytes 638984 | tf_op jit(solution)/shard_map/ppermute | solution.py:376
  110.4 5.4 %collective-permute-start.13 = (bf16[13,64,128]{2,1,0:T(8,128)(2,1)}, bf16[13,64,128]{2,1,0:T(8,128)(2,1)}, u32[]{:S(2)}, u32[]{:S(2)}) collective-permute-start(bf16[13,64,128]{2,1,0:T(8,128)(2,1)} %shard_map.141.refs_5_.refs_1_), channel_id=1, source_target_pairs={{0,1},{1,0},{2,3},{3,2},{4,5},{5,4},{6,7},{7,6},{8,9},{9,8},{10,11... | collective-permute-start | bytes 638984 | tf_op jit(solution)/shard_map/ppermute | solution.py:376
  122.9 3.8 %copy-start.22 = (bf16[4,64,2048]{2,1,0:T(8,128)(2,1)S(1)}, bf16[4,64,2048]{2,1,0:T(8,128)(2,1)}, u32[]{:S(2)}) copy-start(bf16[4,64,2048]{2,1,0:T(8,128)(2,1)} %copy-done.21) | copy-start | bytes 3145732
  122.9 10.8 %collective-permute-start.16 = (bf16[384,256]{1,0:T(8,128)(2,1)S(1)}, bf16[384,256]{1,0:T(8,128)(2,1)S(1)}, u32[]{:S(2)}, u32[]{:S(2)}) collective-permute-start(bf16[384,256]{1,0:T(8,128)(2,1)S(1)} %get-tuple-element.33), channel_id=1, source_target_pairs={{0,4},{4,8},{8,12},{12,0},{1,5},{5,9},{9,13},{13,1},{2,6},{6,10},{... | collective-permute-start | bytes 589832 | tf_op jit(solution)/shard_map/ppermute | solution.py:358
  122.9 20.8 %collective-permute-start.17 = (bf16[384,256]{1,0:T(8,128)(2,1)S(1)}, bf16[384,256]{1,0:T(8,128)(2,1)S(1)}, u32[]{:S(2)}, u32[]{:S(2)}) collective-permute-start(bf16[384,256]{1,0:T(8,128)(2,1)S(1)} %get-tuple-element.34), channel_id=1, source_target_pairs={{0,8},{4,12},{8,0},{12,4},{1,9},{5,13},{9,1},{13,5},{2,10},{6,14},... | collective-permute-start | bytes 589832 | tf_op jit(solution)/shard_map/ppermute | solution.py:358
  124.6 19.0 %collective-permute-start.18 = (bf16[384,256]{1,0:T(8,128)(2,1)S(1)}, bf16[384,256]{1,0:T(8,128)(2,1)S(1)}, u32[]{:S(2)}, u32[]{:S(2)}) collective-permute-start(bf16[384,256]{1,0:T(8,128)(2,1)S(1)} %get-tuple-element.35), channel_id=1, source_target_pairs={{0,12},{4,0},{8,4},{12,8},{1,13},{5,1},{9,5},{13,9},{2,14},{6,2},{... | collective-permute-start | bytes 589832 | tf_op jit(solution)/shard_map/ppermute | solution.py:358
  129.8 14.6 %copy-start.8 = (bf16[4,64,2048]{2,1,0:T(8,128)(2,1)}, bf16[4,64,2048]{2,1,0:T(8,128)(2,1)S(1)}, u32[]{:S(2)}) copy-start(bf16[4,64,2048]{2,1,0:T(8,128)(2,1)S(1)} %add_convert_fusion.refs_6_) | copy-start | bytes 3145732
  (18 other events, 25.0 us)

commit v10 on v9

--- a/solution.py
+++ b/solution.py
@@ -16,7 +16,7 @@
 ROW_PRODUCT = (((1,), (1,)), ((), ()))
 
 
-def call(kernel, scalars, grid, inputs, outputs, tokens=(), us=1.0, scratch=(), aliases=None):
+def call(kernel, scalars, grid, inputs, outputs, tokens=(), us=1.0, scratch=(), aliases=None, vmem=16):
     def run(*refs):
         cut = len(scalars) + len(inputs)
         return kernel(*refs[:cut], *refs[cut + len(tokens) :])
@@ -32,7 +32,7 @@
         ),
         out_shape=[jax.ShapeDtypeStruct(shape, kind) for shape, kind, _ in outputs],
         input_output_aliases=aliases or {},
-        compiler_params=pltpu.CompilerParams(vmem_limit_bytes=16 * 1024 * 1024),
+        compiler_params=pltpu.CompilerParams(vmem_limit_bytes=vmem * 1024 * 1024),
         cost_estimate=pl.CostEstimate(flops=int(us * 1e9), bytes_accessed=int(us * 3.6e5), transcendentals=0),
     )(*scalars, *[array for array, _ in inputs], *tokens)
 
@@ -65,12 +65,18 @@
     blocks, rank, width = maps.shape
     kept = blocks - SW
     last_shape = (SW, *others.shape[1:])
-
-    def kernel(lengths_ref, maps_ref, rows_ref, others_ref, out_ref, last_other, last_again):
-        last_other[...] = others_ref[...]
-        last_again[...] = others_ref[...]
+    in_hbm = pl.BlockSpec(memory_space=pltpu.HBM)
+
+    def kernel(lengths_ref, maps_ref, rows_ref, others_ref, out_ref, one_ref, two_ref, done):
+        copies = [
+            pltpu.make_async_copy(others_ref.at[kept:], to, done.at[k]) for k, to in enumerate((one_ref, two_ref))
+        ]
+        for copy in copies:
+            copy.start()
         for k in range(kept):
             out_ref[k] = masked_rank(maps_ref[k], rows_ref[k * BLOCK : (k + 1) * BLOCK], lengths_ref[k])
+        for copy in copies:
+            copy.wait()
 
     return call(
         kernel,
@@ -79,15 +85,34 @@
         [
             (maps, pl.BlockSpec((kept, rank, width), lambda i, *_: (0, 0, 0), pipeline_mode=pl.Buffered(1))),
             (features, pl.BlockSpec((kept * BLOCK, width), lambda i, *_: (0, 0), pipeline_mode=pl.Buffered(1))),
-            (others, pl.BlockSpec(last_shape, lambda i, *_: (kept, 0, 0), pipeline_mode=pl.Buffered(1))),
+            (others, in_hbm),
         ],
-        [
-            ((blocks, rank, BLOCK), features.dtype, pl.BlockSpec((kept, rank, BLOCK), lambda i, *_: (0, 0, 0))),
-            (last_shape, features.dtype, constant_spec(last_shape)),
-            (last_shape, features.dtype, constant_spec(last_shape)),
-        ],
+        [((blocks, rank, BLOCK), features.dtype, pl.BlockSpec((kept, rank, BLOCK), lambda i, *_: (0, 0, 0)))]
+        + [(last_shape, features.dtype, in_hbm)] * 2,
         tokens,
-    )
+        scratch=[pltpu.SemaphoreType.DMA((2,))],
+        vmem=40,
+    )
+
+
+def chosen(pick, choices, tokens):
+    shape = choices[0].shape
+
+    def kernel(pick_ref, *refs):
+        for k, choice in enumerate(refs[:-1]):
+
+            @pl.when(pick_ref[0] == k)
+            def _():
+                refs[-1][...] = choice[...]
+
+    return call(
+        kernel,
+        (pick,),
+        (1,),
+        [whole(choice) for choice in choices],
+        [(shape, choices[0].dtype, constant_spec(shape))],
+        tokens,
+    )[0]
 
 
 def with_last_rank(lengths, partner, me, choices, features, ranks):
@@ -442,7 +467,6 @@
     up_choices, _ = shifted(up_own, holder)
     cot_terms, up_last = with_last_rank(lengths, partner, me, up_choices, cotangent, cot_terms)
     rank_cot = exchanged(cot_terms)
-    me = after(me.reshape(1), rank_cot[0])[0]
     down_own = after(down_own, rank_cot[0])
 
     table_rows = jnp.sum(
@@ -487,21 +511,19 @@
         from_left = lax.ppermute(down_own, "dp", [(0, 1), (1, 2)])
         from_right = lax.ppermute(down_own, "dp", [(3, 2), (2, 1)])
         second, third, own = down_rows(codes, OWN, 3, 1, rank_cot, hidden, [first])
-        passing = jnp.where(after(me.reshape(1), second)[0] == 1, from_left, from_right)
-        passed = lax.ppermute(passing, "dp", [(1, 2), (2, 1)])
-        terms = base(second, passing)
-        second = add(after(second, terms[0]), jnp.where(inner, from_first, jnp.zeros((), first.dtype)))
+        def place(wanted):
+            place = jnp.where(wanted == me, 0, jnp.where(wanted == me - 1, 1, jnp.where(wanted == me + 1, 2, 3)))
+            return place.reshape(1).astype(jnp.int32)
+
+        passed = chosen(jnp.where(me == 1, 0, 1).reshape(1), [from_left, from_right], [second])
+        terms = base(second, passed)
+        passed = lax.ppermute(passed, "dp", [(1, 2), (2, 1)])
+        choices = [down_kept, from_left, from_right, passed]
+        outward = chosen(place(jnp.where(me == 1, holders[0], holders[3])), choices, [terms[0]])
+        second = add(after(second, terms[0], outward), jnp.where(inner, from_first, jnp.zeros((), first.dtype)))
         from_second = lax.ppermute(second, "dp", [(0, 1), (3, 2), (1, 3), (2, 0)])
-        down_kept = after(down_kept, second)
-
-        def place(wanted):
-            return jnp.where(wanted == me, 0, jnp.where(wanted == me - 1, 1, jnp.where(wanted == me + 1, 2, 3)))
-
-        wanted = place(jnp.where(me == 1, holders[0], holders[3]))
-        outward = jnp.where(wanted == 1, from_left, jnp.where(wanted == 2, from_right, passed))
-        outward = lax.ppermute(jnp.where(wanted == 0, down_kept, outward), "dp", [(2, 3), (1, 0)])
-        down_choices = [down_kept, from_left, from_right, passed, outward]
-        down_pick = jnp.where(inner | (holder == me), place(holder), 4).reshape(1).astype(jnp.int32)
+        down_choices = [*choices, lax.ppermute(outward, "dp", [(2, 3), (1, 0)])]
+        down_pick = jnp.where(inner | (holder == me), place(holder), 4)
         base_sums, away = base_parts(terms, second)
         rank_in = inputs(down_pick, down_choices, away)
         third = add(after(third, rank_in[0]), jnp.where(inner, from_second, jnp.zeros((), first.dtype)))

time: 147 us -> 144 us (0.980)
  the two profiles are of different devices: /device:TPU:0 before, /device:TPU:9 now
where the time goes in v10:
time: 144 us; the launch traced here: 143 us
  waiting for transfers between devices  43.3 us (30%)
  starting transfers between devices  31.8 us (22%)
  Pallas kernels  26.7 us (19%)
  local copies, waits for them, and re-layouts  25.6 us (18%)
  other arithmetic  10.5 us (7%)
  between operations  4.77 us (3%)
    pallas_call x15, Pallas kernels, call(): pl.pallas_call(run, grid_spec=pltpu.PrefetchScalarGridSpec(num_scalar_pre...  26.7 us
    unnamed x78, local copies, waits for them, and re-layouts  23.4 us
    ppermute x1, waiting for transfers between devices, body(): down_choices = [*choices, lax.ppermute(outward, 'dp', [(2, 3), (1, 0)])]  22.4 us
    ppermute x1, waiting for transfers between devices, body(): from_inner = lax.ppermute(third, 'dp', [(1, 2), (2, 1)])  9.57 us
    ppermute x6, starting transfers between devices, shift(): lax.ppermute(array, 'dp', [(i, (i + by) % size) for i in range(size)])  9.38 us
    ppermute x8, starting transfers between devices, crossed(): lax.ppermute(array, 'tensor', [(i, i ^ by) for i in range(lax.axis_size('...  8.85 us
    ppermute x6, waiting for transfers between devices, shift(): lax.ppermute(array, 'dp', [(i, (i + by) % size) for i in range(size)])  6.1 us
    ppermute x8, waiting for transfers between devices, crossed(): lax.ppermute(array, 'tensor', [(i, i ^ by) for i in range(lax.axis_size('...  5.05 us
  transfers between devices with their start and end apart: 22, of which 9 were waited for; matrix products, arithmetic and copies ran while one was open for 8% of the time, Pallas kernels for 18%

profile of v10, /device:TPU:9, one launch (start us, length us, event | category | flops | bytes accessed | tf_op | source)
XLA Modules:
  0.0 142.7 jit_solution(7002538753660880996)
XLA Ops:
  1.4 2.5 %collective-permute-start.1 = (bf16[1,64,256]{2,1,0:T(8,128)(2,1)S(1)}, bf16[1,64,256]{2,1,0:T(8,128)(2,1)S(1)}, u32[]{:S(2)}, u32[]{:S(2)}) collective-permute-start(bf16[1,64,256]{2,1,0:T(8,128)(2,1)S(1)} %slice.9.refs_4_.refs_3_), channel_id=1, source_target_pairs={{0,8},{4,12},{8,0},{12,4},{1,9},{5,13},{9,1},{13,5},{2,10},{6,14},... | collective-permute-start | bytes 98312 | tf_op jit(solution)/shard_map/ppermute | solution.py:383
  3.9 2.2 %collective-permute-start = (bf16[1,64,256]{2,1,0:T(8,128)(2,1)S(1)}, bf16[1,64,256]{2,1,0:T(8,128)(2,1)S(1)}, u32[]{:S(2)}, u32[]{:S(2)}) collective-permute-start(bf16[1,64,256]{2,1,0:T(8,128)(2,1)S(1)} %slice.9.refs_4_.refs_3_), channel_id=1, source_target_pairs={{0,4},{4,8},{8,12},{12,0},{1,5},{5,9},{9,13},{13,1},{2,6},{6,10},{... | collective-permute-start | bytes 98312 | tf_op jit(solution)/shard_map/ppermute | solution.py:383
  7.6 1.2 copy-done.4
  8.7 2.0 %copy-done.7 = bf16[13,64,2048]{2,1,0:T(8,128)(2,1)S(1)} copy-done((bf16[13,64,2048]{2,1,0:T(8,128)(2,1)S(1)}, bf16[13,64,2048]{2,1,0:T(8,128)(2,1)}, u32[]{:S(2)}) %copy-start.7) | copy-done | bytes 3407896
  14.4 1.5 %collective-permute-start.3 = (bf16[13,64,128]{2,1,0:T(8,128)(2,1)S(1)}, bf16[13,64,128]{2,1,0:T(8,128)(2,1)S(1)}, u32[]{:S(2)}, u32[]{:S(2)}) collective-permute-start(bf16[13,64,128]{2,1,0:T(8,128)(2,1)S(1)} %get-tuple-element.23), channel_id=1, source_target_pairs={{0,1},{1,0},{2,3},{3,2},{4,5},{5,4},{6,7},{7,6},{8,9},{9,8},{10,11... | collective-permute-start | bytes 638984 | tf_op jit(solution)/shard_map/ppermute | solution.py:401
  17.1 1.3 collective-permute-start.4
  18.5 1.3 collective-permute-start.6
  19.8 4.0 %collective-permute-start.5 = (bf16[1,64,2048]{2,1,0:T(8,128)(2,1)S(1)}, bf16[1,64,2048]{2,1,0:T(8,128)(2,1)S(1)}, u32[]{:S(2)}, u32[]{:S(2)}) collective-permute-start(bf16[1,64,2048]{2,1,0:T(8,128)(2,1)S(1)} %shard_map.134), channel_id=1, source_target_pairs={{0,4},{4,8},{1,5},{5,9},{2,6},{6,10},{3,7},{7,11},{16,20},{20,24},... | collective-permute-start | bytes 786440 | tf_op jit(solution)/shard_map/ppermute | solution.py:511
  23.9 2.9 %copy-done = bf16[1664,2048]{1,0:T(8,128)(2,1)S(1)} copy-done((bf16[1664,2048]{1,0:T(8,128)(2,1)S(1)}, bf16[1664,2048]{1,0:T(8,128)(2,1)}, u32[]{:S(2)}) %copy-start) | copy-done | bytes 6815768
  26.9 1.7 %shard_map.132.refs_8_ = bf16[4,64,2048]{2,1,0:T(8,128)(2,1)S(1)} custom-call(s32[16]{0:T(128)S(1)} %get-tuple-element.41.refs_0_, bf16[13,64,128]{2,1,0:T(8,128)(2,1)S(1)} %add_convert_fusion.4.refs_1_, bf16[13,64,128]{2,1,0:T(8,128)(2,1)S(1)} %collective-permute-done.4.refs_2_, bf16[1664,2048]{1,0:T(8,128)(2,1)S(1)} %copy-done, ...), custom_call_target="tpu_custom_call" | custom-call | flops 1000000000 | bytes 360000 | tf_op jit(solution)/shard_map/pallas_call | solution.py:24
  28.7 3.3 %shard_map.133 = (bf16[4,64,2048]{2,1,0:T(8,128)(2,1)S(1)}, bf16[4,64,2048]{2,1,0:T(8,128)(2,1)S(1)}, bf16[4,64,2048]{2,1,0:T(8,128)(2,1)S(1)}) custom-call(s32[16]{0:T(128)S(1)} %get-tuple-element.41.refs_0_, bf16[13,64,128]{2,1,0:T(8,128)(2,1)S(1)} %add_convert_fusion.4.refs_1_, bf16[13,64,128]{2,1,0:T(8,128)(2,1)S(1)} %collective-permute-done.4.refs_2_, ...), custom_call_target="tpu_custom_call" | custom-call | flops 1000000000 | bytes 360000 | tf_op jit(solution)/shard_map/pallas_call | solution.py:24
  33.8 2.9 %collective-permute-start.8 = (bf16[1,64,2048]{2,1,0:T(8,128)(2,1)}, bf16[1,64,2048]{2,1,0:T(8,128)(2,1)}, u32[]{:S(2)}, u32[]{:S(2)}) collective-permute-start(bf16[1,64,2048]{2,1,0:T(8,128)(2,1)} %shard_map.135.refs_7_), channel_id=1, source_target_pairs={{4,8},{8,4},{5,9},{9,5},{6,10},{10,6},{7,11},{11,7},{20,24},{24,20... | collective-permute-start | bytes 786440 | tf_op jit(solution)/shard_map/ppermute | solution.py:520
  36.7 9.4 %shard_map.136 = (bf16[1664,256]{1,0:T(8,128)(2,1)}, bf16[1664,256]{1,0:T(8,128)(2,1)S(1)}, bf16[1664,256]{1,0:T(8,128)(2,1)S(1)}, bf16[1664,256]{1,0:T(8,128)(2,1)S(1)}) custom-call(s32[4]{0:T(128)S(1)} %pad_add_fusion.refs_0_, bf16[1664,2048]{1,0:T(8,128)(2,1)S(1)} %bitcast.17, bf16[2048,1024]{1,0:T(8,128)(2,1)S(1)} %copy-done.22, ...), custom_call_target="tpu_custom_call" | custom-call | flops 99999997952 | bytes 36000000 | tf_op jit(solution)/shard_map/pallas_call | solution.py:24
  48.8 1.8 %collective-permute-start.10 = (bf16[1664,256]{1,0:T(8,128)(2,1)}, bf16[1664,256]{1,0:T(8,128)(2,1)}, u32[]{:S(2)}, u32[]{:S(2)}) collective-permute-start(bf16[1664,256]{1,0:T(8,128)(2,1)} %get-tuple-element.29.refs_5_.refs_1_), channel_id=1, source_target_pairs={{0,1},{1,0},{2,3},{3,2},{4,5},{5,4},{6,7},{7,6},{8,9},{9,8},{10,11... | collective-permute-start | bytes 2555912 | tf_op jit(solution)/shard_map/ppermute | solution.py:401
  57.4 1.9 %collective-permute-start.12 = (bf16[1,64,2048]{2,1,0:T(8,128)(2,1)S(1)}, bf16[1,64,2048]{2,1,0:T(8,128)(2,1)S(1)}, u32[]{:S(2)}, u32[]{:S(2)}) collective-permute-start(bf16[1,64,2048]{2,1,0:T(8,128)(2,1)S(1)} %shard_map.137.refs_2_), channel_id=1, source_target_pairs={{8,12},{4,0},{9,13},{5,1},{10,14},{6,2},{11,15},{7,3},{24,28},{20,... | collective-permute-start | bytes 786440 | tf_op jit(solution)/shard_map/ppermute | solution.py:525
  59.4 1.7 %add_convert_fusion.2.refs_1_ = bf16[4,64,2048]{2,1,0:T(8,128)(2,1)S(1)} fusion(bf16[4,64,2048]{2,1,0:T(8,128)(2,1)S(1)} %shard_map.138, bf16[4,64,2048]{2,1,0:T(8,128)(2,1)} %collective-permute-done.9, pred[]{:T(512)S(6)} %or.6), kind=kLoop, calls=%fused_computation.3 | loop fusion | flops 2621440 | bytes 3145729 | tf_op jit(solution)/shard_map/convert_element_type | solution.py:397
  61.2 2.5 %add_convert_fusion.3.refs_15_ = bf16[1664,256]{1,0:T(8,128)(2,1)} fusion(bf16[1664,256]{1,0:T(8,128)(2,1)} %collective-permute-done.10, bf16[1664,256]{1,0:T(8,128)(2,1)S(1)} %shard_map.139), kind=kLoop, calls=%fused_computation.4 | loop fusion | flops 1703936 | bytes 2555904 | tf_op jit(solution)/shard_map/convert_element_type | solution.py:397
  64.6 22.4 %collective-permute-done.12.refs_14_ = bf16[1,64,2048]{2,1,0:T(8,128)(2,1)S(1)} collective-permute-done((bf16[1,64,2048]{2,1,0:T(8,128)(2,1)S(1)}, bf16[1,64,2048]{2,1,0:T(8,128)(2,1)S(1)}, u32[]{:S(2)}, u32[]{:S(2)}) %collective-permute-start.12) | collective-permute-done | bytes 262176 | tf_op jit(solution)/shard_map/ppermute | solution.py:525
  87.0 2.9 %copy-done.1 = bf16[1664,2048]{1,0:T(8,128)(2,1)S(1)} copy-done((bf16[1664,2048]{1,0:T(8,128)(2,1)S(1)}, bf16[1664,2048]{1,0:T(8,128)(2,1)}, u32[]{:S(2)}) %copy-start.1) | copy-done | bytes 6815768
  89.9 4.5 %shard_map.140.refs_5_.refs_1_ = bf16[13,64,128]{2,1,0:T(8,128)(2,1)S(1)} custom-call(s32[13]{0:T(128)S(1)} %copy-done.21, s32[1]{0:T(128)} %bitcast.13.refs_1_, bf16[13,64,2048]{2,1,0:T(8,128)(2,1)S(1)} %copy-done.8, bf16[13,64,2048]{2,1,0:T(8,128)(2,1)S(1)} %copy-done.8, bf16[13,64,2048]{2,1,0:T(8,128)(2,1)S(1)} %copy-done.8, ...), custom_call_target="tpu_custom_call" | custom-call | flops 99999997952 | bytes 36000000 | tf_op jit(solution)/shard_map/pallas_call | solution.py:24
  94.4 2.2 %collective-permute-start.15 = (bf16[13,64,128]{2,1,0:T(8,128)(2,1)S(1)}, bf16[13,64,128]{2,1,0:T(8,128)(2,1)S(1)}, u32[]{:S(2)}, u32[]{:S(2)}) collective-permute-start(bf16[13,64,128]{2,1,0:T(8,128)(2,1)S(1)} %shard_map.140.refs_5_.refs_1_), channel_id=1, source_target_pairs={{0,3},{1,2},{2,1},{3,0},{4,7},{5,6},{6,5},{7,4},{8,11},{9,10},{10,... | collective-permute-start | bytes 638984 | tf_op jit(solution)/shard_map/ppermute | solution.py:401
  97.0 1.3 collective-permute-start.21
  98.3 2.1 %collective-permute-start.20 = (bf16[4,64,2048]{2,1,0:T(8,128)(2,1)S(1)}, bf16[4,64,2048]{2,1,0:T(8,128)(2,1)}, u32[]{:S(2)}, u32[]{:S(2)}) collective-permute-start(bf16[4,64,2048]{2,1,0:T(8,128)(2,1)S(1)} %add_convert_fusion.1.refs_1_), channel_id=1, source_target_pairs={{4,8},{8,4},{5,9},{9,5},{6,10},{10,6},{7,11},{11,7},{20,24},{24,20... | collective-permute-start | bytes 3145736 | tf_op jit(solution)/shard_map/ppermute | solution.py:530
  105.1 3.6 %collective-permute-done.14.refs_7_ = bf16[13,64,128]{2,1,0:T(8,128)(2,1)S(1)} collective-permute-done((bf16[13,64,128]{2,1,0:T(8,128)(2,1)S(1)}, bf16[13,64,128]{2,1,0:T(8,128)(2,1)S(1)}, u32[]{:S(2)}, u32[]{:S(2)}) %collective-permute-start.14) | collective-permute-done | bytes 213024 | tf_op jit(solution)/shard_map/ppermute | solution.py:401
  114.1 3.5 %shard_map.141 = (bf16[1664,256]{1,0:T(8,128)(2,1)}, bf16[384,256]{1,0:T(8,128)(2,1)S(1)}, bf16[384,256]{1,0:T(8,128)(2,1)S(1)}, bf16[384,256]{1,0:T(8,128)(2,1)S(1)}, bf16[384,256]{1,0:T(8,128)(2,1)S(1)}) custom-call(s32[13]{0:T(128)S(1)} %copy-done.21, s32[16]{0:T(128)S(1)} %get-tuple-element.42.refs_1_, bf16[1664,256]{1,0:T(8,128)(2,1)S(1)} %copy-done.15, ...), custom_call_target="tpu_custom_call" | custom-call | flops 1000000000 | bytes 360000 | tf_op jit(solution)/shard_map/pallas_call | solution.py:24
  117.6 1.5 %collective-permute-start.16 = (bf16[384,256]{1,0:T(8,128)(2,1)S(1)}, bf16[384,256]{1,0:T(8,128)(2,1)S(1)}, u32[]{:S(2)}, u32[]{:S(2)}) collective-permute-start(bf16[384,256]{1,0:T(8,128)(2,1)S(1)} %get-tuple-element.33), channel_id=1, source_target_pairs={{0,4},{4,8},{8,12},{12,0},{1,5},{5,9},{9,13},{13,1},{2,6},{6,10},{... | collective-permute-start | bytes 589832 | tf_op jit(solution)/shard_map/ppermute | solution.py:383
  119.1 3.2 %collective-permute-start.17 = (bf16[384,256]{1,0:T(8,128)(2,1)S(1)}, bf16[384,256]{1,0:T(8,128)(2,1)S(1)}, u32[]{:S(2)}, u32[]{:S(2)}) collective-permute-start(bf16[384,256]{1,0:T(8,128)(2,1)S(1)} %get-tuple-element.34), channel_id=1, source_target_pairs={{0,8},{4,12},{8,0},{12,4},{1,9},{5,13},{9,1},{13,5},{2,10},{6,14},... | collective-permute-start | bytes 589832 | tf_op jit(solution)/shard_map/ppermute | solution.py:383
  122.3 1.7 %select_add_fusion = f32[4,64,2048]{2,1,0:T(8,128)S(1)} fusion(bf16[4,64,2048]{2,1,0:T(8,128)(2,1)S(1)} %copy-done.34, bf16[4,64,2048]{2,1,0:T(8,128)(2,1)} %collective-permute-done.9, bf16[4,64,2048]{2,1,0:T(8,128)(2,1)S(1)} %shard_map.143, pred[]{:T(512)S(6)} %or.6), kind=kLoop, calls=%fused_computation.1 | loop fusion | flops 3145728 | bytes 5242881 | tf_op jit(solution)/shard_map/add | solution.py:533
  124.2 9.6 %collective-permute-done.20 = bf16[4,64,2048]{2,1,0:T(8,128)(2,1)} collective-permute-done((bf16[4,64,2048]{2,1,0:T(8,128)(2,1)S(1)}, bf16[4,64,2048]{2,1,0:T(8,128)(2,1)}, u32[]{:S(2)}, u32[]{:S(2)}) %collective-permute-start.20) | collective-permute-done | bytes 1048608 | tf_op jit(solution)/shard_map/ppermute | solution.py:530
  133.8 2.0 %add_convert_fusion.refs_6_ = bf16[4,64,2048]{2,1,0:T(8,128)(2,1)S(1)} fusion(bf16[4,64,2048]{2,1,0:T(8,128)(2,1)} %collective-permute-done.21, f32[4,64,2048]{2,1,0:T(8,128)S(1)} %select_add_fusion, bf16[4,64,2048]{2,1,0:T(8,128)(2,1)} %collective-permute-done.20), kind=kLoop, calls=%fused_computation | loop fusion | flops 2621440 | bytes 5242880 | tf_op jit(solution)/shard_map/convert_element_type | solution.py:536
  135.9 4.0 %collective-permute-done.17.refs_3_ = bf16[384,256]{1,0:T(8,128)(2,1)S(1)} collective-permute-done((bf16[384,256]{1,0:T(8,128)(2,1)S(1)}, bf16[384,256]{1,0:T(8,128)(2,1)S(1)}, u32[]{:S(2)}, u32[]{:S(2)}) %collective-permute-start.17) | collective-permute-done | bytes 196640 | tf_op jit(solution)/shard_map/ppermute | solution.py:383
  139.9 2.0 %collective-permute-done.18.refs_4_ = bf16[384,256]{1,0:T(8,128)(2,1)S(1)} collective-permute-done((bf16[384,256]{1,0:T(8,128)(2,1)S(1)}, bf16[384,256]{1,0:T(8,128)(2,1)S(1)}, u32[]{:S(2)}, u32[]{:S(2)}) %collective-permute-start.18) | collective-permute-done | bytes 196640 | tf_op jit(solution)/shard_map/ppermute | solution.py:383
  (126 shorter events, 27.5 us)
Async XLA Ops:
  1.4 12.2 %collective-permute-start.2 = (bf16[1,64,256]{2,1,0:T(8,128)(2,1)S(1)}, bf16[1,64,256]{2,1,0:T(8,128)(2,1)S(1)}, u32[]{:S(2)}, u32[]{:S(2)}) collective-permute-start(bf16[1,64,256]{2,1,0:T(8,128)(2,1)S(1)} %slice.9.refs_4_.refs_3_), channel_id=1, source_target_pairs={{0,12},{4,0},{8,4},{12,8},{1,13},{5,1},{9,5},{13,9},{2,14},{6,2},{... | collective-permute-start | bytes 98312 | tf_op jit(solution)/shard_map/ppermute | solution.py:383
  1.4 12.2 %collective-permute-start.1 = (bf16[1,64,256]{2,1,0:T(8,128)(2,1)S(1)}, bf16[1,64,256]{2,1,0:T(8,128)(2,1)S(1)}, u32[]{:S(2)}, u32[]{:S(2)}) collective-permute-start(bf16[1,64,256]{2,1,0:T(8,128)(2,1)S(1)} %slice.9.refs_4_.refs_3_), channel_id=1, source_target_pairs={{0,8},{4,12},{8,0},{12,4},{1,9},{5,13},{9,1},{13,5},{2,10},{6,14},... | collective-permute-start | bytes 98312 | tf_op jit(solution)/shard_map/ppermute | solution.py:383
  3.9 9.7 %collective-permute-start = (bf16[1,64,256]{2,1,0:T(8,128)(2,1)S(1)}, bf16[1,64,256]{2,1,0:T(8,128)(2,1)S(1)}, u32[]{:S(2)}, u32[]{:S(2)}) collective-permute-start(bf16[1,64,256]{2,1,0:T(8,128)(2,1)S(1)} %slice.9.refs_4_.refs_3_), channel_id=1, source_target_pairs={{0,4},{4,8},{8,12},{12,0},{1,5},{5,9},{9,13},{13,1},{2,6},{6,10},{... | collective-permute-start | bytes 98312 | tf_op jit(solution)/shard_map/ppermute | solution.py:383
  14.4 2.6 %collective-permute-start.3 = (bf16[13,64,128]{2,1,0:T(8,128)(2,1)S(1)}, bf16[13,64,128]{2,1,0:T(8,128)(2,1)S(1)}, u32[]{:S(2)}, u32[]{:S(2)}) collective-permute-start(bf16[13,64,128]{2,1,0:T(8,128)(2,1)S(1)} %get-tuple-element.23), channel_id=1, source_target_pairs={{0,1},{1,0},{2,3},{3,2},{4,5},{5,4},{6,7},{7,6},{8,9},{9,8},{10,11... | collective-permute-start | bytes 638984 | tf_op jit(solution)/shard_map/ppermute | solution.py:401
  17.1 6.8 %collective-permute-start.4 = (bf16[13,64,128]{2,1,0:T(8,128)(2,1)S(1)}, bf16[13,64,128]{2,1,0:T(8,128)(2,1)S(1)}, u32[]{:S(2)}, u32[]{:S(2)}) collective-permute-start(bf16[13,64,128]{2,1,0:T(8,128)(2,1)S(1)} %add_convert_fusion.4.refs_1_), channel_id=1, source_target_pairs={{0,2},{1,3},{2,0},{3,1},{4,6},{5,7},{6,4},{7,5},{8,10},{9,11},{10,... | collective-permute-start | bytes 638984 | tf_op jit(solution)/shard_map/ppermute | solution.py:401
  18.5 14.4 %collective-permute-start.6 = (bf16[1,64,2048]{2,1,0:T(8,128)(2,1)S(1)}, bf16[1,64,2048]{2,1,0:T(8,128)(2,1)S(1)}, u32[]{:S(2)}, u32[]{:S(2)}) collective-permute-start(bf16[1,64,2048]{2,1,0:T(8,128)(2,1)S(1)} %shard_map.134), channel_id=1, source_target_pairs={{12,8},{8,4},{13,9},{9,5},{14,10},{10,6},{15,11},{11,7},{28,24},{2... | collective-permute-start | bytes 786440 | tf_op jit(solution)/shard_map/ppermute | solution.py:512
  19.8 13.1 %collective-permute-start.5 = (bf16[1,64,2048]{2,1,0:T(8,128)(2,1)S(1)}, bf16[1,64,2048]{2,1,0:T(8,128)(2,1)S(1)}, u32[]{:S(2)}, u32[]{:S(2)}) collective-permute-start(bf16[1,64,2048]{2,1,0:T(8,128)(2,1)S(1)} %shard_map.134), channel_id=1, source_target_pairs={{0,4},{4,8},{1,5},{5,9},{2,6},{6,10},{3,7},{7,11},{16,20},{20,24},... | collective-permute-start | bytes 786440 | tf_op jit(solution)/shard_map/ppermute | solution.py:511
  26.9 9.8 %slice-start = ((s8[6815744]{0:T(1024)(128)(4,1)}), s8[4194304]{0:T(1024)(128)(4,1)S(1)}, s32[]{:S(2)}) async-start(s8[6815744]{0:T(1024)(128)(4,1)} %bitcast.16), calls=%async_computation | async-start | bytes 8388608
  28.6 8.1 %slice-start.1 = ((s8[6815744]{0:T(1024)(128)(4,1)}), s8[2621440]{0:T(1024)(128)(4,1)S(1)}, s32[]{:S(2)}) async-start(s8[6815744]{0:T(1024)(128)(4,1)} %bitcast.16), calls=%async_computation.1 | async-start | bytes 5242880
  28.6 30.8 %collective-permute-start.9 = (bf16[4,64,2048]{2,1,0:T(8,128)(2,1)S(1)}, bf16[4,64,2048]{2,1,0:T(8,128)(2,1)}, u32[]{:S(2)}, u32[]{:S(2)}) collective-permute-start(bf16[4,64,2048]{2,1,0:T(8,128)(2,1)S(1)} %shard_map.132.refs_8_), channel_id=1, source_target_pairs={{0,4},{12,8},{4,0},{8,12},{1,5},{13,9},{5,1},{9,13},{2,6},{14,10},... | collective-permute-start | bytes 3145736 | tf_op jit(solution)/shard_map/ppermute | solution.py:510
  28.7 8.0 %copy-start.22 = (bf16[2048,1024]{1,0:T(8,128)(2,1)S(1)}, bf16[2048,1024]{1,0:T(8,128)(2,1)}, u32[]{:S(2)}) copy-start(bf16[2048,1024]{1,0:T(8,128)(2,1)} %refs_5_.6) | copy-start | bytes 12582916
  33.0 13.1 %copy-start.26 = (bf16[1,64,2048]{2,1,0:T(8,128)(2,1)}, bf16[1,64,2048]{2,1,0:T(8,128)(2,1)S(1)}, u32[]{:S(2)}) copy-start(bf16[1,64,2048]{2,1,0:T(8,128)(2,1)S(1)} %collective-permute-done.6.refs_2_.refs_3_.refs_12_) | copy-start | bytes 786436
  33.0 13.1 %copy-start.29 = (bf16[1,64,2048]{2,1,0:T(8,128)(2,1)}, bf16[1,64,2048]{2,1,0:T(8,128)(2,1)S(1)}, u32[]{:S(2)}) copy-start(bf16[1,64,2048]{2,1,0:T(8,128)(2,1)S(1)} %collective-permute-done.5.refs_1_.refs_2_.refs_11_) | copy-start | bytes 786436
  33.8 20.7 %copy-start.25 = (bf16[1,64,2048]{2,1,0:T(8,128)(2,1)S(1)}, bf16[1,64,2048]{2,1,0:T(8,128)(2,1)}, u32[]{:S(2)}) copy-start(bf16[1,64,2048]{2,1,0:T(8,128)(2,1)} %copy-done.24) | copy-start | bytes 786436
  33.8 20.7 %collective-permute-start.8 = (bf16[1,64,2048]{2,1,0:T(8,128)(2,1)}, bf16[1,64,2048]{2,1,0:T(8,128)(2,1)}, u32[]{:S(2)}, u32[]{:S(2)}) collective-permute-start(bf16[1,64,2048]{2,1,0:T(8,128)(2,1)} %shard_map.135.refs_7_), channel_id=1, source_target_pairs={{4,8},{8,4},{5,9},{9,5},{6,10},{10,6},{7,11},{11,7},{20,24},{24,20... | collective-permute-start | bytes 786440 | tf_op jit(solution)/shard_map/ppermute | solution.py:520
  48.8 12.4 %collective-permute-start.10 = (bf16[1664,256]{1,0:T(8,128)(2,1)}, bf16[1664,256]{1,0:T(8,128)(2,1)}, u32[]{:S(2)}, u32[]{:S(2)}) collective-permute-start(bf16[1664,256]{1,0:T(8,128)(2,1)} %get-tuple-element.29.refs_5_.refs_1_), channel_id=1, source_target_pairs={{0,1},{1,0},{2,3},{3,2},{4,5},{5,4},{6,7},{7,6},{8,9},{9,8},{10,11... | collective-permute-start | bytes 2555912 | tf_op jit(solution)/shard_map/ppermute | solution.py:401
  54.4 46.0 %collective-permute-start.7 = (bf16[1664,256]{1,0:T(8,128)(2,1)}, bf16[1664,256]{1,0:T(8,128)(2,1)S(1)}, u32[]{:S(2)}, u32[]{:S(2)}) collective-permute-start(bf16[1664,256]{1,0:T(8,128)(2,1)} %copy-done.23), channel_id=1, source_target_pairs={{0,1},{1,0},{2,3},{3,2},{4,5},{5,4},{6,7},{7,6},{8,9},{9,8},{10,11... | collective-permute-start | bytes 2555912 | tf_op jit(solution)/shard_map/ppermute | solution.py:401
  57.4 29.6 %collective-permute-start.12 = (bf16[1,64,2048]{2,1,0:T(8,128)(2,1)S(1)}, bf16[1,64,2048]{2,1,0:T(8,128)(2,1)S(1)}, u32[]{:S(2)}, u32[]{:S(2)}) collective-permute-start(bf16[1,64,2048]{2,1,0:T(8,128)(2,1)S(1)} %shard_map.137.refs_2_), channel_id=1, source_target_pairs={{8,12},{4,0},{9,13},{5,1},{10,14},{6,2},{11,15},{7,3},{24,28},{20,... | collective-permute-start | bytes 786440 | tf_op jit(solution)/shard_map/ppermute | solution.py:525
  61.1 35.5 %collective-permute-start.19 = (bf16[4,64,2048]{2,1,0:T(8,128)(2,1)S(1)}, bf16[4,64,2048]{2,1,0:T(8,128)(2,1)S(1)}, u32[]{:S(2)}, u32[]{:S(2)}) collective-permute-start(bf16[4,64,2048]{2,1,0:T(8,128)(2,1)S(1)} %add_convert_fusion.2.refs_1_), channel_id=1, source_target_pairs={{0,4},{12,8},{4,12},{8,0},{1,5},{13,9},{5,13},{9,1},{2,6},{14,10},... | collective-permute-start | bytes 3145736 | tf_op jit(solution)/shard_map/ppermute | solution.py:524
  61.2 25.8 %copy-start.8 = (bf16[13,64,2048]{2,1,0:T(8,128)(2,1)S(1)}, bf16[13,64,2048]{2,1,0:T(8,128)(2,1)}, u32[]{:S(2)}) copy-start(bf16[13,64,2048]{2,1,0:T(8,128)(2,1)} %refs_5_.7) | copy-start | bytes 10223620
  61.2 25.8 %copy-start.28 = (bf16[1,64,2048]{2,1,0:T(8,128)(2,1)S(1)}, bf16[1,64,2048]{2,1,0:T(8,128)(2,1)}, u32[]{:S(2)}) copy-start(bf16[1,64,2048]{2,1,0:T(8,128)(2,1)} %copy-done.26) | copy-start | bytes 786436
  61.2 25.8 %copy-start.31 = (bf16[1,64,2048]{2,1,0:T(8,128)(2,1)S(1)}, bf16[1,64,2048]{2,1,0:T(8,128)(2,1)}, u32[]{:S(2)}) copy-start(bf16[1,64,2048]{2,1,0:T(8,128)(2,1)} %copy-done.29) | copy-start | bytes 786436
  63.7 45.0 %collective-permute-start.11 = (bf16[1664,256]{1,0:T(8,128)(2,1)}, bf16[1664,256]{1,0:T(8,128)(2,1)}, u32[]{:S(2)}, u32[]{:S(2)}) collective-permute-start(bf16[1664,256]{1,0:T(8,128)(2,1)} %add_convert_fusion.3.refs_15_), channel_id=1, source_target_pairs={{0,2},{1,3},{2,0},{3,1},{4,6},{5,7},{6,4},{7,5},{8,10},{9,11},{10,... | collective-permute-start | bytes 2555912 | tf_op jit(solution)/shard_map/ppermute | solution.py:401
  94.4 8.1 %collective-permute-start.15 = (bf16[13,64,128]{2,1,0:T(8,128)(2,1)S(1)}, bf16[13,64,128]{2,1,0:T(8,128)(2,1)S(1)}, u32[]{:S(2)}, u32[]{:S(2)}) collective-permute-start(bf16[13,64,128]{2,1,0:T(8,128)(2,1)S(1)} %shard_map.140.refs_5_.refs_1_), channel_id=1, source_target_pairs={{0,3},{1,2},{2,1},{3,0},{4,7},{5,6},{6,5},{7,4},{8,11},{9,10},{10,... | collective-permute-start | bytes 638984 | tf_op jit(solution)/shard_map/ppermute | solution.py:401
  96.6 7.9 %copy-start.33 = (bf16[4,64,2048]{2,1,0:T(8,128)(2,1)}, bf16[4,64,2048]{2,1,0:T(8,128)(2,1)S(1)}, u32[]{:S(2)}) copy-start(bf16[4,64,2048]{2,1,0:T(8,128)(2,1)S(1)} %collective-permute-done.19) | copy-start | bytes 3145732
  97.0 27.2 %collective-permute-start.21 = (bf16[4,64,2048]{2,1,0:T(8,128)(2,1)S(1)}, bf16[4,64,2048]{2,1,0:T(8,128)(2,1)}, u32[]{:S(2)}, u32[]{:S(2)}) collective-permute-start(bf16[4,64,2048]{2,1,0:T(8,128)(2,1)S(1)} %add_convert_fusion.1.refs_1_), channel_id=1, source_target_pairs={{0,4},{12,8},{1,5},{13,9},{2,6},{14,10},{3,7},{15,11},{16,20},{28,... | collective-permute-start | bytes 3145736 | tf_op jit(solution)/shard_map/ppermute | solution.py:531
  98.3 35.5 %collective-permute-start.20 = (bf16[4,64,2048]{2,1,0:T(8,128)(2,1)S(1)}, bf16[4,64,2048]{2,1,0:T(8,128)(2,1)}, u32[]{:S(2)}, u32[]{:S(2)}) collective-permute-start(bf16[4,64,2048]{2,1,0:T(8,128)(2,1)S(1)} %add_convert_fusion.1.refs_1_), channel_id=1, source_target_pairs={{4,8},{8,4},{5,9},{9,5},{6,10},{10,6},{7,11},{11,7},{20,24},{24,20... | collective-permute-start | bytes 3145736 | tf_op jit(solution)/shard_map/ppermute | solution.py:530
  101.4 7.3 %collective-permute-start.14 = (bf16[13,64,128]{2,1,0:T(8,128)(2,1)S(1)}, bf16[13,64,128]{2,1,0:T(8,128)(2,1)S(1)}, u32[]{:S(2)}, u32[]{:S(2)}) collective-permute-start(bf16[13,64,128]{2,1,0:T(8,128)(2,1)S(1)} %shard_map.140.refs_5_.refs_1_), channel_id=1, source_target_pairs={{0,2},{1,3},{2,0},{3,1},{4,6},{5,7},{6,4},{7,5},{8,10},{9,11},{10,... | collective-permute-start | bytes 638984 | tf_op jit(solution)/shard_map/ppermute | solution.py:401
  103.2 5.5 %collective-permute-start.13 = (bf16[13,64,128]{2,1,0:T(8,128)(2,1)S(1)}, bf16[13,64,128]{2,1,0:T(8,128)(2,1)S(1)}, u32[]{:S(2)}, u32[]{:S(2)}) collective-permute-start(bf16[13,64,128]{2,1,0:T(8,128)(2,1)S(1)} %shard_map.140.refs_5_.refs_1_), channel_id=1, source_target_pairs={{0,1},{1,0},{2,3},{3,2},{4,5},{5,4},{6,7},{7,6},{8,9},{9,8},{10,11... | collective-permute-start | bytes 638984 | tf_op jit(solution)/shard_map/ppermute | solution.py:401
  117.6 18.3 %collective-permute-start.16 = (bf16[384,256]{1,0:T(8,128)(2,1)S(1)}, bf16[384,256]{1,0:T(8,128)(2,1)S(1)}, u32[]{:S(2)}, u32[]{:S(2)}) collective-permute-start(bf16[384,256]{1,0:T(8,128)(2,1)S(1)} %get-tuple-element.33), channel_id=1, source_target_pairs={{0,4},{4,8},{8,12},{12,0},{1,5},{5,9},{9,13},{13,1},{2,6},{6,10},{... | collective-permute-start | bytes 589832 | tf_op jit(solution)/shard_map/ppermute | solution.py:383
  119.1 20.8 %collective-permute-start.17 = (bf16[384,256]{1,0:T(8,128)(2,1)S(1)}, bf16[384,256]{1,0:T(8,128)(2,1)S(1)}, u32[]{:S(2)}, u32[]{:S(2)}) collective-permute-start(bf16[384,256]{1,0:T(8,128)(2,1)S(1)} %get-tuple-element.34), channel_id=1, source_target_pairs={{0,8},{4,12},{8,0},{12,4},{1,9},{5,13},{9,1},{13,5},{2,10},{6,14},... | collective-permute-start | bytes 589832 | tf_op jit(solution)/shard_map/ppermute | solution.py:383
  122.3 19.6 %collective-permute-start.18 = (bf16[384,256]{1,0:T(8,128)(2,1)S(1)}, bf16[384,256]{1,0:T(8,128)(2,1)S(1)}, u32[]{:S(2)}, u32[]{:S(2)}) collective-permute-start(bf16[384,256]{1,0:T(8,128)(2,1)S(1)} %get-tuple-element.35), channel_id=1, source_target_pairs={{0,12},{4,0},{8,4},{12,8},{1,13},{5,1},{9,5},{13,9},{2,14},{6,2},{... | collective-permute-start | bytes 589832 | tf_op jit(solution)/shard_map/ppermute | solution.py:383
  (29 other events, 55.9 us)

commit v11 on v10

--- a/solution.py
+++ b/solution.py
@@ -91,7 +91,7 @@
         + [(last_shape, features.dtype, in_hbm)] * 2,
         tokens,
         scratch=[pltpu.SemaphoreType.DMA((2,))],
-        vmem=40,
+        vmem=60,
     )
 
 
@@ -112,6 +112,7 @@
         [whole(choice) for choice in choices],
         [(shape, choices[0].dtype, constant_spec(shape))],
         tokens,
+        1.0,
     )[0]
 
 
@@ -322,6 +323,7 @@
             ((count * rank + BLOCK, width), maps.dtype, constant_spec((count * rank + BLOCK, width)))
             for count in parts
         ],
+        vmem=60,
     )
 
 
@@ -510,17 +512,17 @@
         from_first = lax.ppermute(first, "dp", [(0, 1), (3, 2), (1, 0), (2, 3)])
         from_left = lax.ppermute(down_own, "dp", [(0, 1), (1, 2)])
         from_right = lax.ppermute(down_own, "dp", [(3, 2), (2, 1)])
-        second, third, own = down_rows(codes, OWN, 3, 1, rank_cot, hidden, [first])
         def place(wanted):
             place = jnp.where(wanted == me, 0, jnp.where(wanted == me - 1, 1, jnp.where(wanted == me + 1, 2, 3)))
             return place.reshape(1).astype(jnp.int32)
 
-        passed = chosen(jnp.where(me == 1, 0, 1).reshape(1), [from_left, from_right], [second])
-        terms = base(second, passed)
+        passed = chosen(jnp.where(me == 1, 0, 1).reshape(1), [from_left, from_right], [first])
+        second, third, own = down_rows(codes, OWN, 3, 1, rank_cot, hidden, [passed], 100.0)
         passed = lax.ppermute(passed, "dp", [(1, 2), (2, 1)])
         choices = [down_kept, from_left, from_right, passed]
-        outward = chosen(place(jnp.where(me == 1, holders[0], holders[3])), choices, [terms[0]])
-        second = add(after(second, terms[0], outward), jnp.where(inner, from_first, jnp.zeros((), first.dtype)))
+        outward = chosen(place(jnp.where(me == 1, holders[0], holders[3])), choices, [second])
+        terms = base(second, outward)
+        second = add(after(second, terms[0]), jnp.where(inner, from_first, jnp.zeros((), first.dtype)))
         from_second = lax.ppermute(second, "dp", [(0, 1), (3, 2), (1, 3), (2, 0)])
         down_choices = [*choices, lax.ppermute(outward, "dp", [(2, 3), (1, 0)])]
         down_pick = jnp.where(inner | (holder == me), place(holder), 4)

time: 144 us -> 163 us (1.13)
  the two profiles are of different devices: /device:TPU:9 before, /device:TPU:0 now
where the time goes in v11:
time: 163 us; the launch traced here: 160 us
  Pallas kernels  48.3 us (30%)
  waiting for transfers between devices  47 us (29%)
  starting transfers between devices  31.6 us (19%)
  local copies, waits for them, and re-layouts  16.3 us (10%)
  other arithmetic  12.3 us (8%)
  between operations  4.61 us (3%)
    pallas_call x15, Pallas kernels, call(): pl.pallas_call(run, grid_spec=pltpu.PrefetchScalarGridSpec(num_scalar_pre...  48.3 us
    ppermute x1, waiting for transfers between devices, body(): down_choices = [*choices, lax.ppermute(outward, 'dp', [(2, 3), (1, 0)])]  23.2 us
    unnamed x82, local copies, waits for them, and re-layouts  14.1 us
    ppermute x6, waiting for transfers between devices, shift(): lax.ppermute(array, 'dp', [(i, (i + by) % size) for i in range(size)])  14 us
    ppermute x6, starting transfers between devices, shift(): lax.ppermute(array, 'dp', [(i, (i + by) % size) for i in range(size)])  9.88 us
    ppermute x8, waiting for transfers between devices, crossed(): lax.ppermute(array, 'tensor', [(i, i ^ by) for i in range(lax.axis_size('...  6.95 us
    ppermute x1, starting transfers between devices, body(): from_left = lax.ppermute(down_own, 'dp', [(0, 1), (1, 2)])  5.71 us
    ppermute x8, starting transfers between devices, crossed(): lax.ppermute(array, 'tensor', [(i, i ^ by) for i in range(lax.axis_size('...  4.39 us
  transfers between devices with their start and end apart: 22, of which 7 were waited for; matrix products, arithmetic and copies ran while one was open for 8% of the time, Pallas kernels for 29%

profile of v11, /device:TPU:0, one launch (start us, length us, event | category | flops | bytes accessed | tf_op | source)
XLA Modules:
  0.0 160.0 jit_solution(7026502834111197683)
XLA Ops:
  1.4 5.0 %collective-permute-start.2 = (bf16[1,64,256]{2,1,0:T(8,128)(2,1)S(1)}, bf16[1,64,256]{2,1,0:T(8,128)(2,1)S(1)}, u32[]{:S(2)}, u32[]{:S(2)}) collective-permute-start(bf16[1,64,256]{2,1,0:T(8,128)(2,1)S(1)} %slice.9.refs_4_.refs_3_), channel_id=1, source_target_pairs={{0,12},{4,0},{8,4},{12,8},{1,13},{5,1},{9,5},{13,9},{2,14},{6,2},{... | collective-permute-start | bytes 98312 | tf_op jit(solution)/shard_map/ppermute | solution.py:385
  6.4 1.0 collective-permute-start
  10.8 1.4 select_reduce_fusion.2
  12.3 19.7 %shard_map.130 = (bf16[13,64,128]{2,1,0:T(8,128)(2,1)}, bf16[1,64,2048]{2,1,0:T(8,128)(2,1)}, bf16[1,64,2048]{2,1,0:T(8,128)(2,1)}) custom-call(s32[13]{0:T(128)} %refs_0_.7, bf16[13,64,256]{2,1,0:T(8,128)(2,1)} %refs_10_.1, bf16[1664,256]{1,0:T(8,128)(2,1)} %refs_9_.3, bf16[13,64,2048]{2,1,0:T(8,128)(2,1)} %refs_5_.7, bf16[1,64,256]{2,1,0:T(8,128)(2,1)} %copy-done.15), custom_call_target="tpu_custom_call" | custom-call | flops 1000000000 | bytes 360000 | tf_op jit(solution)/shard_map/pallas_call | solution.py:24
  37.3 1.4 collective-permute-done.3
  38.7 1.6 collective-permute-start.4
  41.0 5.7 %collective-permute-start.5 = (bf16[1,64,2048]{2,1,0:T(8,128)(2,1)}, bf16[1,64,2048]{2,1,0:T(8,128)(2,1)}, u32[]{:S(2)}, u32[]{:S(2)}) collective-permute-start(bf16[1,64,2048]{2,1,0:T(8,128)(2,1)} %shard_map.132), channel_id=1, source_target_pairs={{0,4},{4,8},{1,5},{5,9},{2,6},{6,10},{3,7},{7,11},{16,20},{20,24},... | collective-permute-start | bytes 786440 | tf_op jit(solution)/shard_map/ppermute | solution.py:513
  48.2 1.4 select_reduce_fusion
  49.6 2.9 %copy-done = bf16[1664,2048]{1,0:T(8,128)(2,1)S(1)} copy-done((bf16[1664,2048]{1,0:T(8,128)(2,1)S(1)}, bf16[1664,2048]{1,0:T(8,128)(2,1)}, u32[]{:S(2)}) %copy-start) | copy-done | bytes 6815768
  52.6 2.4 %shard_map.133.refs_3_ = bf16[4,64,2048]{2,1,0:T(8,128)(2,1)} custom-call(s32[16]{0:T(128)S(1)} %get-tuple-element.41.refs_0_, bf16[13,64,128]{2,1,0:T(8,128)(2,1)S(1)} %add_convert_fusion.4.refs_1_, bf16[13,64,128]{2,1,0:T(8,128)(2,1)S(1)} %collective-permute-done.4.refs_2_, bf16[1664,2048]{1,0:T(8,128)(2,1)S(1)} %copy-done, ...), custom_call_target="tpu_custom_call" | custom-call | flops 1000000000 | bytes 360000 | tf_op jit(solution)/shard_map/pallas_call | solution.py:24
  55.0 1.9 %collective-permute-start.9 = (bf16[4,64,2048]{2,1,0:T(8,128)(2,1)}, bf16[4,64,2048]{2,1,0:T(8,128)(2,1)}, u32[]{:S(2)}, u32[]{:S(2)}) collective-permute-start(bf16[4,64,2048]{2,1,0:T(8,128)(2,1)} %shard_map.133.refs_3_), channel_id=1, source_target_pairs={{0,4},{12,8},{4,0},{8,12},{1,5},{13,9},{5,1},{9,13},{2,6},{14,10},... | collective-permute-start | bytes 3145736 | tf_op jit(solution)/shard_map/ppermute | solution.py:512
  59.5 3.6 %shard_map.135 = (bf16[4,64,2048]{2,1,0:T(8,128)(2,1)S(1)}, bf16[4,64,2048]{2,1,0:T(8,128)(2,1)S(1)}, bf16[4,64,2048]{2,1,0:T(8,128)(2,1)S(1)}) custom-call(s32[16]{0:T(128)S(1)} %get-tuple-element.41.refs_0_, bf16[13,64,128]{2,1,0:T(8,128)(2,1)S(1)} %add_convert_fusion.4.refs_1_, bf16[13,64,128]{2,1,0:T(8,128)(2,1)S(1)} %collective-permute-done.4.refs_2_, ...), custom_call_target="tpu_custom_call" | custom-call | flops 99999997952 | bytes 36000000 | tf_op jit(solution)/shard_map/pallas_call | solution.py:24
  65.1 1.2 shard_map.136.refs_7_
  66.3 9.4 %shard_map.137 = (bf16[1664,256]{1,0:T(8,128)(2,1)}, bf16[1664,256]{1,0:T(8,128)(2,1)S(1)}, bf16[1664,256]{1,0:T(8,128)(2,1)S(1)}, bf16[1664,256]{1,0:T(8,128)(2,1)S(1)}) custom-call(s32[4]{0:T(128)S(1)} %pad_add_fusion.refs_0_, bf16[1664,2048]{1,0:T(8,128)(2,1)S(1)} %bitcast.17, bf16[2048,1024]{1,0:T(8,128)(2,1)S(1)} %copy-done.19, ...), custom_call_target="tpu_custom_call" | custom-call | flops 99999997952 | bytes 36000000 | tf_op jit(solution)/shard_map/pallas_call | solution.py:24
  79.2 1.3 collective-permute-start.12
  81.0 1.2 copy-done.3
  83.2 2.4 %add_convert_fusion.2.refs_1_ = bf16[4,64,2048]{2,1,0:T(8,128)(2,1)S(1)} fusion(bf16[4,64,2048]{2,1,0:T(8,128)(2,1)} %copy-done.4, bf16[4,64,2048]{2,1,0:T(8,128)(2,1)} %collective-permute-done.9, pred[]{:T(512)S(6)} %or.6), kind=kLoop, calls=%fused_computation.3 | loop fusion | flops 2621440 | bytes 3145729 | tf_op jit(solution)/shard_map/convert_element_type | solution.py:399
  85.6 3.5 %collective-permute-start.19 = (bf16[4,64,2048]{2,1,0:T(8,128)(2,1)S(1)}, bf16[4,64,2048]{2,1,0:T(8,128)(2,1)S(1)}, u32[]{:S(2)}, u32[]{:S(2)}) collective-permute-start(bf16[4,64,2048]{2,1,0:T(8,128)(2,1)S(1)} %add_convert_fusion.2.refs_1_), channel_id=1, source_target_pairs={{0,4},{12,8},{4,12},{8,0},{1,5},{13,9},{5,13},{9,1},{2,6},{14,10},... | collective-permute-start | bytes 3145736 | tf_op jit(solution)/shard_map/ppermute | solution.py:526
  89.9 23.2 %collective-permute-done.12.refs_14_ = bf16[1,64,2048]{2,1,0:T(8,128)(2,1)S(1)} collective-permute-done((bf16[1,64,2048]{2,1,0:T(8,128)(2,1)}, bf16[1,64,2048]{2,1,0:T(8,128)(2,1)S(1)}, u32[]{:S(2)}, u32[]{:S(2)}) %collective-permute-start.12) | collective-permute-done | bytes 262176 | tf_op jit(solution)/shard_map/ppermute | solution.py:527
  113.2 4.5 %shard_map.140.refs_5_.refs_1_ = bf16[13,64,128]{2,1,0:T(8,128)(2,1)S(1)} custom-call(s32[13]{0:T(128)S(1)} %copy-done.18, s32[1]{0:T(128)} %bitcast.13.refs_1_, bf16[13,64,2048]{2,1,0:T(8,128)(2,1)S(1)} %copy-done.10, bf16[13,64,2048]{2,1,0:T(8,128)(2,1)S(1)} %copy-done.10, bf16[13,64,2048]{2,1,0:T(8,128)(2,1)S(1)} %copy-done.10, ...), custom_call_target="tpu_custom_call" | custom-call | flops 99999997952 | bytes 36000000 | tf_op jit(solution)/shard_map/pallas_call | solution.py:24
  118.2 1.8 %collective-permute-start.21 = (bf16[4,64,2048]{2,1,0:T(8,128)(2,1)S(1)}, bf16[4,64,2048]{2,1,0:T(8,128)(2,1)S(1)}, u32[]{:S(2)}, u32[]{:S(2)}) collective-permute-start(bf16[4,64,2048]{2,1,0:T(8,128)(2,1)S(1)} %add_convert_fusion.1.refs_1_), channel_id=1, source_target_pairs={{0,4},{12,8},{1,5},{13,9},{2,6},{14,10},{3,7},{15,11},{16,20},{28,... | collective-permute-start | bytes 3145736 | tf_op jit(solution)/shard_map/ppermute | solution.py:533
  120.0 1.6 %collective-permute-start.20 = (bf16[4,64,2048]{2,1,0:T(8,128)(2,1)S(1)}, bf16[4,64,2048]{2,1,0:T(8,128)(2,1)}, u32[]{:S(2)}, u32[]{:S(2)}) collective-permute-start(bf16[4,64,2048]{2,1,0:T(8,128)(2,1)S(1)} %add_convert_fusion.1.refs_1_), channel_id=1, source_target_pairs={{4,8},{8,4},{5,9},{9,5},{6,10},{10,6},{7,11},{11,7},{20,24},{24,20... | collective-permute-start | bytes 3145736 | tf_op jit(solution)/shard_map/ppermute | solution.py:532
  121.7 1.4 collective-permute-start.14
  123.1 2.2 %collective-permute-done.15.refs_8_ = bf16[13,64,128]{2,1,0:T(8,128)(2,1)S(1)} collective-permute-done((bf16[13,64,128]{2,1,0:T(8,128)(2,1)S(1)}, bf16[13,64,128]{2,1,0:T(8,128)(2,1)S(1)}, u32[]{:S(2)}, u32[]{:S(2)}) %collective-permute-start.15) | collective-permute-done | bytes 213024 | tf_op jit(solution)/shard_map/ppermute | solution.py:403
  126.6 3.4 %collective-permute-done.14.refs_7_ = bf16[13,64,128]{2,1,0:T(8,128)(2,1)} collective-permute-done((bf16[13,64,128]{2,1,0:T(8,128)(2,1)S(1)}, bf16[13,64,128]{2,1,0:T(8,128)(2,1)}, u32[]{:S(2)}, u32[]{:S(2)}) %collective-permute-start.14) | collective-permute-done | bytes 213024 | tf_op jit(solution)/shard_map/ppermute | solution.py:403
  130.0 5.1 %shard_map.141 = (bf16[1664,256]{1,0:T(8,128)(2,1)}, bf16[384,256]{1,0:T(8,128)(2,1)}, bf16[384,256]{1,0:T(8,128)(2,1)}, bf16[384,256]{1,0:T(8,128)(2,1)}, bf16[384,256]{1,0:T(8,128)(2,1)}) custom-call(s32[13]{0:T(128)} %refs_0_.7, s32[16]{0:T(128)} %get-tuple-element.42.refs_1_, bf16[1664,256]{1,0:T(8,128)(2,1)} %copy-done.12, ...), custom_call_target="tpu_custom_call" | custom-call | flops 1000000000 | bytes 360000 | tf_op jit(solution)/shard_map/pallas_call | solution.py:24
  135.6 3.4 %collective-permute-start.18 = (bf16[384,256]{1,0:T(8,128)(2,1)}, bf16[384,256]{1,0:T(8,128)(2,1)S(1)}, u32[]{:S(2)}, u32[]{:S(2)}) collective-permute-start(bf16[384,256]{1,0:T(8,128)(2,1)} %get-tuple-element.35), channel_id=1, source_target_pairs={{0,12},{4,0},{8,4},{12,8},{1,13},{5,1},{9,5},{13,9},{2,14},{6,2},{... | collective-permute-start | bytes 589832 | tf_op jit(solution)/shard_map/ppermute | solution.py:385
  139.0 1.7 %select_add_fusion = f32[4,64,2048]{2,1,0:T(8,128)S(1)} fusion(bf16[4,64,2048]{2,1,0:T(8,128)(2,1)S(1)} %copy-done.36, bf16[4,64,2048]{2,1,0:T(8,128)(2,1)} %collective-permute-done.9, bf16[4,64,2048]{2,1,0:T(8,128)(2,1)S(1)} %shard_map.143, pred[]{:T(512)S(6)} %or.6), kind=kLoop, calls=%fused_computation.1 | loop fusion | flops 3145728 | bytes 5242881 | tf_op jit(solution)/shard_map/add | solution.py:535
  140.7 2.8 %collective-permute-done.21 = bf16[4,64,2048]{2,1,0:T(8,128)(2,1)S(1)} collective-permute-done((bf16[4,64,2048]{2,1,0:T(8,128)(2,1)S(1)}, bf16[4,64,2048]{2,1,0:T(8,128)(2,1)S(1)}, u32[]{:S(2)}, u32[]{:S(2)}) %collective-permute-start.21) | collective-permute-done | bytes 1048608 | tf_op jit(solution)/shard_map/ppermute | solution.py:533
  143.5 1.8 %add_convert_fusion.refs_6_ = bf16[4,64,2048]{2,1,0:T(8,128)(2,1)S(1)} fusion(bf16[4,64,2048]{2,1,0:T(8,128)(2,1)S(1)} %collective-permute-done.21, f32[4,64,2048]{2,1,0:T(8,128)S(1)} %select_add_fusion, bf16[4,64,2048]{2,1,0:T(8,128)(2,1)} %collective-permute-done.20), kind=kLoop, calls=%fused_computation | loop fusion | flops 2621440 | bytes 5242880 | tf_op jit(solution)/shard_map/convert_element_type | solution.py:538
  145.3 2.5 %collective-permute-done.16.refs_2_ = bf16[384,256]{1,0:T(8,128)(2,1)S(1)} collective-permute-done((bf16[384,256]{1,0:T(8,128)(2,1)}, bf16[384,256]{1,0:T(8,128)(2,1)S(1)}, u32[]{:S(2)}, u32[]{:S(2)}) %collective-permute-start.16) | collective-permute-done | bytes 196640 | tf_op jit(solution)/shard_map/ppermute | solution.py:385
  147.8 11.4 %collective-permute-done.17.refs_3_ = bf16[384,256]{1,0:T(8,128)(2,1)S(1)} collective-permute-done((bf16[384,256]{1,0:T(8,128)(2,1)}, bf16[384,256]{1,0:T(8,128)(2,1)S(1)}, u32[]{:S(2)}, u32[]{:S(2)}) %collective-permute-start.17) | collective-permute-done | bytes 196640 | tf_op jit(solution)/shard_map/ppermute | solution.py:385
  (130 shorter events, 21.5 us)
Async XLA Ops:
  1.4 30.6 %collective-permute-start.2 = (bf16[1,64,256]{2,1,0:T(8,128)(2,1)S(1)}, bf16[1,64,256]{2,1,0:T(8,128)(2,1)S(1)}, u32[]{:S(2)}, u32[]{:S(2)}) collective-permute-start(bf16[1,64,256]{2,1,0:T(8,128)(2,1)S(1)} %slice.9.refs_4_.refs_3_), channel_id=1, source_target_pairs={{0,12},{4,0},{8,4},{12,8},{1,13},{5,1},{9,5},{13,9},{2,14},{6,2},{... | collective-permute-start | bytes 98312 | tf_op jit(solution)/shard_map/ppermute | solution.py:385
  6.4 25.6 %collective-permute-start.1 = (bf16[1,64,256]{2,1,0:T(8,128)(2,1)S(1)}, bf16[1,64,256]{2,1,0:T(8,128)(2,1)S(1)}, u32[]{:S(2)}, u32[]{:S(2)}) collective-permute-start(bf16[1,64,256]{2,1,0:T(8,128)(2,1)S(1)} %slice.9.refs_4_.refs_3_), channel_id=1, source_target_pairs={{0,8},{4,12},{8,0},{12,4},{1,9},{5,13},{9,1},{13,5},{2,10},{6,14},... | collective-permute-start | bytes 98312 | tf_op jit(solution)/shard_map/ppermute | solution.py:385
  6.4 26.2 %collective-permute-start = (bf16[1,64,256]{2,1,0:T(8,128)(2,1)S(1)}, bf16[1,64,256]{2,1,0:T(8,128)(2,1)S(1)}, u32[]{:S(2)}, u32[]{:S(2)}) collective-permute-start(bf16[1,64,256]{2,1,0:T(8,128)(2,1)S(1)} %slice.9.refs_4_.refs_3_), channel_id=1, source_target_pairs={{0,4},{4,8},{8,12},{12,0},{1,5},{5,9},{9,13},{13,1},{2,6},{6,10},{... | collective-permute-start | bytes 98312 | tf_op jit(solution)/shard_map/ppermute | solution.py:385
  12.2 21.0 %copy-start.9 = (bf16[1664,256]{1,0:T(8,128)(2,1)S(1)}, bf16[1664,256]{1,0:T(8,128)(2,1)}, u32[]{:S(2)}) copy-start(bf16[1664,256]{1,0:T(8,128)(2,1)} %refs_9_.3) | copy-start | bytes 2555908
  12.2 21.0 %copy-start.18 = (s32[13]{0:T(128)S(1)}, s32[13]{0:T(128)}, u32[]{:S(2)}) copy-start(s32[13]{0:T(128)} %refs_0_.7) | copy-start | bytes 160
  12.2 21.0 %copy-start.34 = (s32[4]{0:T(128)S(1)}, s32[4]{0:T(128)}, u32[]{:S(2)}) copy-start(s32[4]{0:T(128)} %refs_1_.4) | copy-start | bytes 52
  36.4 23.0 %slice-start = ((s8[6815744]{0:T(1024)(128)(4,1)}), s8[2621440]{0:T(1024)(128)(4,1)S(1)}, s32[]{:S(2)}) async-start(s8[6815744]{0:T(1024)(128)(4,1)} %bitcast.16), calls=%async_computation | async-start | bytes 5242880
  37.2 1.5 collective-permute-start.3
  38.7 10.9 %collective-permute-start.4 = (bf16[13,64,128]{2,1,0:T(8,128)(2,1)S(1)}, bf16[13,64,128]{2,1,0:T(8,128)(2,1)S(1)}, u32[]{:S(2)}, u32[]{:S(2)}) collective-permute-start(bf16[13,64,128]{2,1,0:T(8,128)(2,1)S(1)} %add_convert_fusion.4.refs_1_), channel_id=1, source_target_pairs={{0,2},{1,3},{2,0},{3,1},{4,6},{5,7},{6,4},{7,5},{8,10},{9,11},{10,... | collective-permute-start | bytes 638984 | tf_op jit(solution)/shard_map/ppermute | solution.py:403
  40.3 16.6 %collective-permute-start.6 = (bf16[1,64,2048]{2,1,0:T(8,128)(2,1)}, bf16[1,64,2048]{2,1,0:T(8,128)(2,1)S(1)}, u32[]{:S(2)}, u32[]{:S(2)}) collective-permute-start(bf16[1,64,2048]{2,1,0:T(8,128)(2,1)} %shard_map.132), channel_id=1, source_target_pairs={{12,8},{8,4},{13,9},{9,5},{14,10},{10,6},{15,11},{11,7},{28,24},{2... | collective-permute-start | bytes 786440 | tf_op jit(solution)/shard_map/ppermute | solution.py:514
  41.0 16.0 %collective-permute-start.5 = (bf16[1,64,2048]{2,1,0:T(8,128)(2,1)}, bf16[1,64,2048]{2,1,0:T(8,128)(2,1)}, u32[]{:S(2)}, u32[]{:S(2)}) collective-permute-start(bf16[1,64,2048]{2,1,0:T(8,128)(2,1)} %shard_map.132), channel_id=1, source_target_pairs={{0,4},{4,8},{1,5},{5,9},{2,6},{6,10},{3,7},{7,11},{16,20},{20,24},... | collective-permute-start | bytes 786440 | tf_op jit(solution)/shard_map/ppermute | solution.py:513
  55.0 28.3 %collective-permute-start.9 = (bf16[4,64,2048]{2,1,0:T(8,128)(2,1)}, bf16[4,64,2048]{2,1,0:T(8,128)(2,1)}, u32[]{:S(2)}, u32[]{:S(2)}) collective-permute-start(bf16[4,64,2048]{2,1,0:T(8,128)(2,1)} %shard_map.133.refs_3_), channel_id=1, source_target_pairs={{0,4},{12,8},{4,0},{8,12},{1,5},{13,9},{5,1},{9,13},{2,6},{14,10},... | collective-permute-start | bytes 3145736 | tf_op jit(solution)/shard_map/ppermute | solution.py:512
  58.6 6.4 %collective-permute-start.7 = (bf16[1,64,2048]{2,1,0:T(8,128)(2,1)S(1)}, bf16[1,64,2048]{2,1,0:T(8,128)(2,1)S(1)}, u32[]{:S(2)}, u32[]{:S(2)}) collective-permute-start(bf16[1,64,2048]{2,1,0:T(8,128)(2,1)S(1)} %shard_map.134.refs_8_), channel_id=1, source_target_pairs={{4,8},{8,4},{5,9},{9,5},{6,10},{10,6},{7,11},{11,7},{20,24},{24,20... | collective-permute-start | bytes 786440 | tf_op jit(solution)/shard_map/ppermute | solution.py:521
  77.5 11.6 %collective-permute-start.10 = (bf16[1664,256]{1,0:T(8,128)(2,1)}, bf16[1664,256]{1,0:T(8,128)(2,1)S(1)}, u32[]{:S(2)}, u32[]{:S(2)}) collective-permute-start(bf16[1664,256]{1,0:T(8,128)(2,1)} %get-tuple-element.30.refs_1_), channel_id=1, source_target_pairs={{0,1},{1,0},{2,3},{3,2},{4,5},{5,4},{6,7},{7,6},{8,9},{9,8},{10,11... | collective-permute-start | bytes 2555912 | tf_op jit(solution)/shard_map/ppermute | solution.py:403
  79.2 34.0 %collective-permute-start.12 = (bf16[1,64,2048]{2,1,0:T(8,128)(2,1)}, bf16[1,64,2048]{2,1,0:T(8,128)(2,1)S(1)}, u32[]{:S(2)}, u32[]{:S(2)}) collective-permute-start(bf16[1,64,2048]{2,1,0:T(8,128)(2,1)} %copy-done.28), channel_id=1, source_target_pairs={{8,12},{4,0},{9,13},{5,1},{10,14},{6,2},{11,15},{7,3},{24,28},{20,... | collective-permute-start | bytes 786440 | tf_op jit(solution)/shard_map/ppermute | solution.py:527
  80.5 41.2 %collective-permute-start.8 = (bf16[1664,256]{1,0:T(8,128)(2,1)}, bf16[1664,256]{1,0:T(8,128)(2,1)S(1)}, u32[]{:S(2)}, u32[]{:S(2)}) collective-permute-start(bf16[1664,256]{1,0:T(8,128)(2,1)} %copy-done.20), channel_id=1, source_target_pairs={{0,1},{1,0},{2,3},{3,2},{4,5},{5,4},{6,7},{7,6},{8,9},{9,8},{10,11... | collective-permute-start | bytes 2555912 | tf_op jit(solution)/shard_map/ppermute | solution.py:403
  82.3 30.9 %copy-start.1 = (bf16[1664,2048]{1,0:T(8,128)(2,1)S(1)}, bf16[1664,2048]{1,0:T(8,128)(2,1)}, u32[]{:S(2)}) copy-start(bf16[1664,2048]{1,0:T(8,128)(2,1)} %refs_9_.2) | copy-start | bytes 20447236
  85.6 32.2 %collective-permute-start.19 = (bf16[4,64,2048]{2,1,0:T(8,128)(2,1)S(1)}, bf16[4,64,2048]{2,1,0:T(8,128)(2,1)S(1)}, u32[]{:S(2)}, u32[]{:S(2)}) collective-permute-start(bf16[4,64,2048]{2,1,0:T(8,128)(2,1)S(1)} %add_convert_fusion.2.refs_1_), channel_id=1, source_target_pairs={{0,4},{12,8},{4,12},{8,0},{1,5},{13,9},{5,13},{9,1},{2,6},{14,10},... | collective-permute-start | bytes 3145736 | tf_op jit(solution)/shard_map/ppermute | solution.py:526
  89.1 24.1 %copy-start.10 = (bf16[13,64,2048]{2,1,0:T(8,128)(2,1)S(1)}, bf16[13,64,2048]{2,1,0:T(8,128)(2,1)}, u32[]{:S(2)}) copy-start(bf16[13,64,2048]{2,1,0:T(8,128)(2,1)} %refs_5_.7) | copy-start | bytes 10223620
  89.1 24.1 %copy-start.22 = (bf16[1,64,2048]{2,1,0:T(8,128)(2,1)S(1)}, bf16[1,64,2048]{2,1,0:T(8,128)(2,1)}, u32[]{:S(2)}) copy-start(bf16[1,64,2048]{2,1,0:T(8,128)(2,1)} %get-tuple-element.26.refs_1_.refs_10_) | copy-start | bytes 786436
  89.1 24.1 %copy-start.25 = (bf16[1,64,2048]{2,1,0:T(8,128)(2,1)S(1)}, bf16[1,64,2048]{2,1,0:T(8,128)(2,1)}, u32[]{:S(2)}) copy-start(bf16[1,64,2048]{2,1,0:T(8,128)(2,1)} %copy-done.23) | copy-start | bytes 786436
  89.1 24.1 %copy-start.27 = (bf16[1,64,2048]{2,1,0:T(8,128)(2,1)S(1)}, bf16[1,64,2048]{2,1,0:T(8,128)(2,1)}, u32[]{:S(2)}) copy-start(bf16[1,64,2048]{2,1,0:T(8,128)(2,1)} %copy-done.26) | copy-start | bytes 786436
  89.3 40.7 %collective-permute-start.11 = (bf16[1664,256]{1,0:T(8,128)(2,1)S(1)}, bf16[1664,256]{1,0:T(8,128)(2,1)}, u32[]{:S(2)}, u32[]{:S(2)}) collective-permute-start(bf16[1664,256]{1,0:T(8,128)(2,1)S(1)} %add_convert_fusion.3.refs_15_), channel_id=1, source_target_pairs={{0,2},{1,3},{2,0},{3,1},{4,6},{5,7},{6,4},{7,5},{8,10},{9,11},{10,... | collective-permute-start | bytes 2555912 | tf_op jit(solution)/shard_map/ppermute | solution.py:403
  117.7 7.5 %collective-permute-start.15 = (bf16[13,64,128]{2,1,0:T(8,128)(2,1)S(1)}, bf16[13,64,128]{2,1,0:T(8,128)(2,1)S(1)}, u32[]{:S(2)}, u32[]{:S(2)}) collective-permute-start(bf16[13,64,128]{2,1,0:T(8,128)(2,1)S(1)} %shard_map.140.refs_5_.refs_1_), channel_id=1, source_target_pairs={{0,3},{1,2},{2,1},{3,0},{4,7},{5,6},{6,5},{7,4},{8,11},{9,10},{10,... | collective-permute-start | bytes 638984 | tf_op jit(solution)/shard_map/ppermute | solution.py:403
  118.2 25.2 %collective-permute-start.21 = (bf16[4,64,2048]{2,1,0:T(8,128)(2,1)S(1)}, bf16[4,64,2048]{2,1,0:T(8,128)(2,1)S(1)}, u32[]{:S(2)}, u32[]{:S(2)}) collective-permute-start(bf16[4,64,2048]{2,1,0:T(8,128)(2,1)S(1)} %add_convert_fusion.1.refs_1_), channel_id=1, source_target_pairs={{0,4},{12,8},{1,5},{13,9},{2,6},{14,10},{3,7},{15,11},{16,20},{28,... | collective-permute-start | bytes 3145736 | tf_op jit(solution)/shard_map/ppermute | solution.py:533
  120.0 23.5 %collective-permute-start.20 = (bf16[4,64,2048]{2,1,0:T(8,128)(2,1)S(1)}, bf16[4,64,2048]{2,1,0:T(8,128)(2,1)}, u32[]{:S(2)}, u32[]{:S(2)}) collective-permute-start(bf16[4,64,2048]{2,1,0:T(8,128)(2,1)S(1)} %add_convert_fusion.1.refs_1_), channel_id=1, source_target_pairs={{4,8},{8,4},{5,9},{9,5},{6,10},{10,6},{7,11},{11,7},{20,24},{24,20... | collective-permute-start | bytes 3145736 | tf_op jit(solution)/shard_map/ppermute | solution.py:532
  121.7 8.3 %collective-permute-start.14 = (bf16[13,64,128]{2,1,0:T(8,128)(2,1)S(1)}, bf16[13,64,128]{2,1,0:T(8,128)(2,1)}, u32[]{:S(2)}, u32[]{:S(2)}) collective-permute-start(bf16[13,64,128]{2,1,0:T(8,128)(2,1)S(1)} %shard_map.140.refs_5_.refs_1_), channel_id=1, source_target_pairs={{0,2},{1,3},{2,0},{3,1},{4,6},{5,7},{6,4},{7,5},{8,10},{9,11},{10,... | collective-permute-start | bytes 638984 | tf_op jit(solution)/shard_map/ppermute | solution.py:403
  125.2 4.8 %collective-permute-start.13 = (bf16[13,64,128]{2,1,0:T(8,128)(2,1)S(1)}, bf16[13,64,128]{2,1,0:T(8,128)(2,1)}, u32[]{:S(2)}, u32[]{:S(2)}) collective-permute-start(bf16[13,64,128]{2,1,0:T(8,128)(2,1)S(1)} %shard_map.140.refs_5_.refs_1_), channel_id=1, source_target_pairs={{0,1},{1,0},{2,3},{3,2},{4,5},{5,4},{6,7},{7,6},{8,9},{9,8},{10,11... | collective-permute-start | bytes 638984 | tf_op jit(solution)/shard_map/ppermute | solution.py:403
  135.1 12.7 %collective-permute-start.16 = (bf16[384,256]{1,0:T(8,128)(2,1)}, bf16[384,256]{1,0:T(8,128)(2,1)S(1)}, u32[]{:S(2)}, u32[]{:S(2)}) collective-permute-start(bf16[384,256]{1,0:T(8,128)(2,1)} %get-tuple-element.33), channel_id=1, source_target_pairs={{0,4},{4,8},{8,12},{12,0},{1,5},{5,9},{9,13},{13,1},{2,6},{6,10},{... | collective-permute-start | bytes 589832 | tf_op jit(solution)/shard_map/ppermute | solution.py:385
  135.1 24.1 %collective-permute-start.17 = (bf16[384,256]{1,0:T(8,128)(2,1)}, bf16[384,256]{1,0:T(8,128)(2,1)S(1)}, u32[]{:S(2)}, u32[]{:S(2)}) collective-permute-start(bf16[384,256]{1,0:T(8,128)(2,1)} %get-tuple-element.34), channel_id=1, source_target_pairs={{0,8},{4,12},{8,0},{12,4},{1,9},{5,13},{9,1},{13,5},{2,10},{6,14},... | collective-permute-start | bytes 589832 | tf_op jit(solution)/shard_map/ppermute | solution.py:385
  135.6 23.7 %collective-permute-start.18 = (bf16[384,256]{1,0:T(8,128)(2,1)}, bf16[384,256]{1,0:T(8,128)(2,1)S(1)}, u32[]{:S(2)}, u32[]{:S(2)}) collective-permute-start(bf16[384,256]{1,0:T(8,128)(2,1)} %get-tuple-element.35), channel_id=1, source_target_pairs={{0,12},{4,0},{8,4},{12,8},{1,13},{5,1},{9,5},{13,9},{2,14},{6,2},{... | collective-permute-start | bytes 589832 | tf_op jit(solution)/shard_map/ppermute | solution.py:385
  140.7 18.6 %copy-start.29 = (bf16[384,256]{1,0:T(8,128)(2,1)S(1)}, bf16[384,256]{1,0:T(8,128)(2,1)}, u32[]{:S(2)}) copy-start(bf16[384,256]{1,0:T(8,128)(2,1)} %get-tuple-element.32.refs_1_) | copy-start | bytes 589828
  (31 other events, 135.5 us)

commit v12 on v8

--- a/solution.py
+++ b/solution.py
@@ -16,7 +16,7 @@
 ROW_PRODUCT = (((1,), (1,)), ((), ()))
 
 
-def call(kernel, scalars, grid, inputs, outputs, tokens=(), us=1.0, scratch=(), aliases=None):
+def call(kernel, scalars, grid, inputs, outputs, tokens=(), us=1.0, scratch=(), aliases=None, vmem=16):
     def run(*refs):
         cut = len(scalars) + len(inputs)
         return kernel(*refs[:cut], *refs[cut + len(tokens) :])
@@ -32,6 +32,7 @@
         ),
         out_shape=[jax.ShapeDtypeStruct(shape, kind) for shape, kind, _ in outputs],
         input_output_aliases=aliases or {},
+        compiler_params=pltpu.CompilerParams(vmem_limit_bytes=vmem * 1024 * 1024),
         cost_estimate=pl.CostEstimate(flops=int(us * 1e9), bytes_accessed=int(us * 3.6e5), transcendentals=0),
     )(*scalars, *[array for array, _ in inputs], *tokens)
 
@@ -84,18 +85,54 @@
             (last_shape, features.dtype, constant_spec(last_shape)),
         ],
         tokens,
-    )
-
-
-def with_last_rank(lengths, pick, choices, features, ranks):
+        vmem=60,
+    )
+
+
+def passed_on(partner, me, own, from_left, from_right, tokens):
+    shape = own.shape
+
+    def kernel(partner_ref, me_ref, own_ref, left_ref, right_ref, inner_ref, outer_ref):
+        left = me_ref[0] == 1
+
+        @pl.when(left)
+        def _():
+            inner_ref[...] = left_ref[...]
+            outer_ref[...] = left_ref[...]
+
+        @pl.when(jnp.logical_not(left))
+        def _():
+            inner_ref[...] = right_ref[...]
+            outer_ref[...] = right_ref[...]
+
+        @pl.when(partner_ref[me_ref[0]] == jnp.where(left, 3, 0))
+        def _():
+            outer_ref[...] = own_ref[...]
+
+    return call(
+        kernel,
+        (partner, me.reshape(1)),
+        (1,),
+        [whole(array) for array in (own, from_left, from_right)],
+        [(shape, own.dtype, constant_spec(shape))] * 2,
+        tokens,
+        1.0,
+    )
+
+
+def with_last_rank(lengths, partner, me, choices, features, ranks):
     shape = choices[0].shape
     block = ranks.shape[0] - 1
-
-    def kernel(lengths_ref, pick_ref, *refs):
+    size = partner.shape[0]
+
+    def kernel(lengths_ref, partner_ref, me_ref, *refs):
         rows_ref, _, out_ref, chosen_ref = refs[-4:]
         for k, choice in enumerate(refs[:-4]):
-
-            @pl.when(pick_ref[0] == k)
+            if len(choices) == 1:
+                chosen_ref[...] = choice[...]
+                continue
+
+            @pl.when(partner_ref[lax.rem(me_ref[0] + (size - k), size)] == me_ref[0])
             def _():
                 chosen_ref[...] = choice[...]
 
@@ -103,7 +140,7 @@
 
     return call(
         kernel,
-        (lengths, pick),
+        (lengths, partner, me.reshape(1)),
         (1,),
         [whole(choice) for choice in choices]
         + [(features, pl.BlockSpec((BLOCK, shape[2]), lambda i, *_: (block, 0), pipeline_mode=pl.Buffered(1)))]
@@ -112,16 +149,28 @@
             (ranks.shape, ranks.dtype, pl.BlockSpec((1, *ranks.shape[1:]), lambda i, *_: (block, 0, 0))),
             (shape, features.dtype, constant_spec(shape)),
         ],
-        aliases={3 + len(choices): 0},
-    )
-
-
-def streamed_ranks(lengths, maps, pick, choices, features, each, tokens=(), us=1.0):
+        aliases={4 + len(choices): 0},
+    )
+
+
+def streamed_ranks(lengths, partner, me, maps, choices, features, each, tokens=(), us=1.0):
     blocks, rank, width = maps.shape
     steps = pl.cdiv(blocks, each)
     end = blocks - 1 - (steps - 1) * each
 
-    def kernel(lengths_ref, pick_ref, *refs):
+    def picked(partner_ref, at):
+        if len(choices) == 1:
+            return [at == at]
+        held = [
+            partner_ref[at] == at,
+            (partner_ref[jnp.maximum(at - 1, 0)] == at) & (at > 0),
+            (partner_ref[jnp.minimum(at + 1, 3)] == at) & (at < 3),
+        ]
+        other = jnp.logical_not(held[0] | held[1] | held[2])
+        inner = (at == 1) | (at == 2)
+        return [*held, other & inner, other & jnp.logical_not(inner)]
+
+    def kernel(lengths_ref, partner_ref, me_ref, *refs):
         maps_refs, rows_refs, choices_refs, out_ref = refs[:each], refs[each : 2 * each], refs[2 * each : -1], refs[-1]
         step = pl.program_id(0)
 
@@ -138,9 +187,9 @@
         def _():
             for k in range(end):
                 one(k)
-            for j, choice in enumerate(choices_refs):
-
-                @pl.when(pick_ref[0] == j)
+            for choice, use in zip(choices_refs, picked(partner_ref, me_ref[0])):
+
+                @pl.when(use)
                 def _():
                     out_ref[blocks - 1] = masked_rank(choice[0], rows_refs[end][...], lengths_ref[blocks - 1])
 
@@ -150,7 +199,7 @@
 
     return call(
         kernel,
-        (lengths, pick),
+        (lengths, partner, me.reshape(1)),
         (steps,),
         [(maps, pl.BlockSpec((1, rank, width), lambda i, *_, k=k: (at(i, k), 0, 0))) for k in range(each)]
         + [(features, pl.BlockSpec((BLOCK, width), lambda i, *_, k=k: (at(i, k), 0))) for k in range(each)]
@@ -290,6 +339,7 @@
             ((count * rank + BLOCK, width), maps.dtype, constant_spec((count * rank + BLOCK, width)))
             for count in parts
         ],
+        vmem=60,
     )
 
 
@@ -430,11 +480,11 @@
     holder = jnp.sum(jnp.where(partner == me, order, 0))
 
     up_own = adapter_up_matrix[kept:]
-    up_choices, up_pick = shifted(up_own, holder)
     cot_terms, down_own = kept_ranks(lengths, adapter_up_matrix, cotangent, adapter_down_rows, [up_own])
-    cot_terms, up_last = with_last_rank(lengths, up_pick, up_choices, cotangent, cot_terms)
+    up_choices, _ = shifted(up_own, holder)
+    cot_terms, up_last = with_last_rank(lengths, partner, me, up_choices, cotangent, cot_terms)
     rank_cot = exchanged(cot_terms)
-    down_choices, down_pick = shifted(after(down_own, rank_cot[0]), holder)
+    down_own = after(down_own, rank_cot[0])
 
     table_rows = jnp.sum(
         jnp.where(
@@ -460,9 +510,9 @@
         away = add(after(away, *tokens), near(sent))
         return (mine, near(given), far(away)), away
 
-    def inputs(*tokens):
+    def inputs(down_choices, *tokens):
         return spread(
-            streamed_ranks(lengths, adapter_down_rows, down_pick, down_choices, hidden, 4, tokens, 100.0)
+            streamed_ranks(lengths, partner, me, adapter_down_rows, down_choices, hidden, 4, tokens, 100.0)
         )
 
     def outputs(codes, parts, base_sums, rank_in):
@@ -475,12 +525,18 @@
         codes = codes_of(jnp.array(ROLES, jnp.int32)[me])
         (first,) = down_rows(codes, 0, 1, 1, rank_cot, hidden)
         from_first = lax.ppermute(first, "dp", [(0, 1), (3, 2), (1, 0), (2, 3)])
-        second, third, own = down_rows(codes, OWN, 3, 1, rank_cot, hidden, [first], 1.0)
-        terms = base(second, *down_choices[1:])
-        second = add(after(second, terms[0]), jnp.where(inner, from_first, jnp.zeros((), first.dtype)))
+        from_left = lax.ppermute(down_own, "dp", [(0, 1), (1, 2), (2, 3)])
+        from_right = lax.ppermute(down_own, "dp", [(3, 2), (2, 1), (1, 0)])
+        passed, outward = passed_on(partner, me, down_own, from_left, from_right, [first])
+        terms = base(first, passed)
+        passed = lax.ppermute(passed, "dp", [(1, 2), (2, 1)])
+        outward = lax.ppermute(outward, "dp", [(1, 3), (2, 0)])
+        down_choices = [down_own, from_left, from_right, passed, outward]
+        second, third, own = down_rows(codes, OWN, 3, 1, rank_cot, hidden, [terms[0], passed, outward], 100.0)
+        second = add(second, jnp.where(inner, from_first, jnp.zeros((), first.dtype)))
         from_second = lax.ppermute(second, "dp", [(0, 1), (3, 2), (1, 3), (2, 0)])
         base_sums, away = base_parts(terms, second)
-        rank_in = inputs(away)
+        rank_in = inputs(down_choices, away)
         third = add(after(third, rank_in[0]), jnp.where(inner, from_second, jnp.zeros((), first.dtype)))
         from_inner = lax.ppermute(third, "dp", [(1, 2), (2, 1)])
         from_third = lax.ppermute(third, "dp", [(0, 1), (3, 2)])
@@ -498,8 +554,9 @@
     else:
         codes = codes_of(order)
         (table,) = down_rows(codes, 0, devices, 0, rank_cot, hidden)
+        down_choices, _ = shifted(down_own, holder)
         down_out = line_reduce_scatter(table.reshape(devices, OWN, *table.shape[1:]))
-        values, table = outputs(codes, [devices * OWN], base_parts(base(table))[0], inputs(table))
+        values, table = outputs(codes, [devices * OWN], base_parts(base(table))[0], inputs(down_choices, table))
         up_table, last_values = table[:-BLOCK], table[-BLOCK:]
         up_out = line_reduce_scatter(up_table.reshape(devices, OWN, -1, values.shape[1]))
         (last_values,), _ = shifted(last_values, partner[me])

time: 139 us -> 132 us (0.950)
  the two profiles are of different devices: /device:TPU:0 before, /device:TPU:9 now
where the time goes in v12:
time: 132 us; the launch traced here: 131 us
  waiting for transfers between devices  37 us (28%)
  starting transfers between devices  36.5 us (28%)
  Pallas kernels  32.2 us (24%)
  local copies, waits for them, and re-layouts  12.9 us (10%)
  other arithmetic  11.2 us (8%)
  between operations  1.59 us (1%)
    pallas_call x13, Pallas kernels, call(): pl.pallas_call(run, grid_spec=pltpu.PrefetchScalarGridSpec(num_scalar_pre...  32.2 us
    ppermute x6, waiting for transfers between devices, shift(): lax.ppermute(array, 'dp', [(i, (i + by) % size) for i in range(size)])  12.7 us
    ppermute x8, starting transfers between devices, crossed(): lax.ppermute(array, 'tensor', [(i, i ^ by) for i in range(lax.axis_size('...  12.4 us
    ppermute x1, waiting for transfers between devices, body(): from_second = lax.ppermute(second, 'dp', [(0, 1), (3, 2), (1, 3), (2, 0)])  11.6 us
    unnamed x56, local copies, waits for them, and re-layouts  11.4 us
    ppermute x6, starting transfers between devices, shift(): lax.ppermute(array, 'dp', [(i, (i + by) % size) for i in range(size)])  8.52 us
    ppermute x8, waiting for transfers between devices, crossed(): lax.ppermute(array, 'tensor', [(i, i ^ by) for i in range(lax.axis_size('...  8.43 us
    ppermute x1, waiting for transfers between devices, body(): from_first = lax.ppermute(first, 'dp', [(0, 1), (3, 2), (1, 0), (2, 3)])  4.34 us
  transfers between devices with their start and end apart: 22, of which 6 were waited for; matrix products, arithmetic and copies ran while one was open for 9% of the time, Pallas kernels for 23%

profile of v12, /device:TPU:9, one launch (start us, length us, event | category | flops | bytes accessed | tf_op | source)
XLA Modules:
  0.0 131.4 jit_solution(17671660067399283986)
XLA Ops:
  3.7 1.5 %collective-permute-start.2 = (bf16[1,64,256]{2,1,0:T(8,128)(2,1)S(1)}, bf16[1,64,256]{2,1,0:T(8,128)(2,1)S(1)}, u32[]{:S(2)}, u32[]{:S(2)}) collective-permute-start(bf16[1,64,256]{2,1,0:T(8,128)(2,1)S(1)} %slice.3.refs_4_.refs_3_), channel_id=1, source_target_pairs={{0,12},{4,0},{8,4},{12,8},{1,13},{5,1},{9,5},{13,9},{2,14},{6,2},{... | collective-permute-start | bytes 98312 | tf_op jit(solution)/shard_map/ppermute | solution.py:401
  7.2 1.4 %select_reduce_fusion.2 = s32[13]{0:T(128)} fusion(s32[16]{0:T(128)} %param.14, s32[13]{0:T(128)} %param.12), kind=kLoop, calls=%fused_computation.8 | loop fusion | flops 611 | bytes 168 | tf_op jit(solution)/shard_map/reduce_sum | solution.py:489
  8.6 3.2 %shard_map.130 = (bf16[13,64,128]{2,1,0:T(8,128)(2,1)}, bf16[1,64,2048]{2,1,0:T(8,128)(2,1)}) custom-call(s32[13]{0:T(128)} %refs_0_.9, bf16[13,64,256]{2,1,0:T(8,128)(2,1)} %refs_10_.3, bf16[1664,256]{1,0:T(8,128)(2,1)} %refs_9_.3, bf16[13,64,2048]{2,1,0:T(8,128)(2,1)} %refs_6_.5, bf16[1,64,256]{2,1,0:T(8,128)(2,1)} %copy-done.8), custom_call_target="tpu_custom_call" | custom-call | flops 1000000000 | bytes 360000 | tf_op jit(solution)/shard_map/pallas_call | solution.py:24
  17.0 1.5 %collective-permute-start.3 = (bf16[13,64,128]{2,1,0:T(8,128)(2,1)S(1)}, bf16[13,64,128]{2,1,0:T(8,128)(2,1)S(1)}, u32[]{:S(2)}, u32[]{:S(2)}) collective-permute-start(bf16[13,64,128]{2,1,0:T(8,128)(2,1)S(1)} %get-tuple-element.24), channel_id=1, source_target_pairs={{0,1},{1,0},{2,3},{3,2},{4,5},{5,4},{6,7},{7,6},{8,9},{9,8},{10,11... | collective-permute-start | bytes 638984 | tf_op jit(solution)/shard_map/ppermute | solution.py:419
  21.0 1.9 %collective-permute-start.5 = (bf16[1,64,2048]{2,1,0:T(8,128)(2,1)}, bf16[1,64,2048]{2,1,0:T(8,128)(2,1)S(1)}, u32[]{:S(2)}, u32[]{:S(2)}) collective-permute-start(bf16[1,64,2048]{2,1,0:T(8,128)(2,1)} %shard_map.133.refs_2_.refs_11_), channel_id=1, source_target_pairs={{0,4},{4,8},{8,12},{1,5},{5,9},{9,13},{2,6},{6,10},{10,14},{3,7},{... | collective-permute-start | bytes 786440 | tf_op jit(solution)/shard_map/ppermute | solution.py:528
  22.9 3.4 %collective-permute-start.6 = (bf16[1,64,2048]{2,1,0:T(8,128)(2,1)}, bf16[1,64,2048]{2,1,0:T(8,128)(2,1)}, u32[]{:S(2)}, u32[]{:S(2)}) collective-permute-start(bf16[1,64,2048]{2,1,0:T(8,128)(2,1)} %shard_map.133.refs_2_.refs_11_), channel_id=1, source_target_pairs={{12,8},{8,4},{4,0},{13,9},{9,5},{5,1},{14,10},{10,6},{6,2},{15,11}... | collective-permute-start | bytes 786440 | tf_op jit(solution)/shard_map/ppermute | solution.py:529
  26.5 1.4 %select_reduce_fusion = (s32[16]{0:T(128)S(1)}, s32[16]{0:T(128)}) fusion(s32[13]{0:T(128)} %compare_select_fusion.2, s32[13]{0:T(128)} %select_reduce_fusion.2, s32[16]{0:T(128)S(1)} %add.106, s32[16]{0:T(128)S(1)} %add.101), kind=kLoop, calls=%fused_computation.6 | loop fusion | flops 1216 | bytes 360 | tf_op jit(solution)/shard_map/reduce_sum | solution.py:501
  27.9 2.9 %copy-done = bf16[1664,2048]{1,0:T(8,128)(2,1)S(1)} copy-done((bf16[1664,2048]{1,0:T(8,128)(2,1)S(1)}, bf16[1664,2048]{1,0:T(8,128)(2,1)}, u32[]{:S(2)}) %copy-start) | copy-done | bytes 6815768
  30.8 2.4 %shard_map.132.refs_5_.refs_6_ = bf16[4,64,2048]{2,1,0:T(8,128)(2,1)} custom-call(s32[16]{0:T(128)S(1)} %get-tuple-element.43.refs_0_, bf16[13,64,128]{2,1,0:T(8,128)(2,1)S(1)} %add_convert_fusion.4.refs_1_, bf16[13,64,128]{2,1,0:T(8,128)(2,1)S(1)} %collective-permute-done.4.refs_2_, bf16[1664,2048]{1,0:T(8,128)(2,1)S(1)} %copy-done, ...), custom_call_target="tpu_custom_call" | custom-call | flops 1000000000 | bytes 360000 | tf_op jit(solution)/shard_map/pallas_call | solution.py:24
  33.2 1.6 %shard_map.134 = (bf16[1,64,2048]{2,1,0:T(8,128)(2,1)S(1)}, bf16[1,64,2048]{2,1,0:T(8,128)(2,1)S(1)}) custom-call(s32[4]{0:T(128)S(1)} %copy-done.20, s32[1]{0:T(128)} %bitcast.7.refs_2_.refs_1_, bf16[1,64,2048]{2,1,0:T(8,128)(2,1)} %shard_map.133.refs_2_.refs_11_, bf16[1,64,2048]{2,1,0:T(8,128)(2,1)S(1)} %collective-permute-done.5.refs_3_.refs_12_, ...), custom_call_target="tpu_custom_call" | custom-call | flops 1000000000 | bytes 360000 | tf_op jit(solution)/shard_map/pallas_call | solution.py:24
  34.9 3.2 %collective-permute-start.8 = (bf16[1,64,2048]{2,1,0:T(8,128)(2,1)S(1)}, bf16[1,64,2048]{2,1,0:T(8,128)(2,1)S(1)}, u32[]{:S(2)}, u32[]{:S(2)}) collective-permute-start(bf16[1,64,2048]{2,1,0:T(8,128)(2,1)S(1)} %get-tuple-element.26.refs_7_), channel_id=1, source_target_pairs={{4,8},{8,4},{5,9},{9,5},{6,10},{10,6},{7,11},{11,7},{20,24},{24,20... | collective-permute-start | bytes 786440 | tf_op jit(solution)/shard_map/ppermute | solution.py:532
  38.1 1.3 collective-permute-start.9
  39.5 9.6 %shard_map.135 = (bf16[1664,256]{1,0:T(8,128)(2,1)S(1)}, bf16[1664,256]{1,0:T(8,128)(2,1)S(1)}, bf16[1664,256]{1,0:T(8,128)(2,1)}, bf16[1664,256]{1,0:T(8,128)(2,1)S(1)}) custom-call(s32[4]{0:T(128)S(1)} %pad_add_fusion.refs_0_, bf16[1664,2048]{1,0:T(8,128)(2,1)S(1)} %bitcast.11, bf16[2048,1024]{1,0:T(8,128)(2,1)S(1)} %copy-done.12, ...), custom_call_target="tpu_custom_call" | custom-call | flops 99999997952 | bytes 36000000 | tf_op jit(solution)/shard_map/pallas_call | solution.py:24
  50.0 1.8 %collective-permute-start.11 = (bf16[1664,256]{1,0:T(8,128)(2,1)S(1)}, bf16[1664,256]{1,0:T(8,128)(2,1)S(1)}, u32[]{:S(2)}, u32[]{:S(2)}) collective-permute-start(bf16[1664,256]{1,0:T(8,128)(2,1)S(1)} %get-tuple-element.30.refs_8_), channel_id=1, source_target_pairs={{0,1},{1,0},{2,3},{3,2},{4,5},{5,4},{6,7},{7,6},{8,9},{9,8},{10,11... | collective-permute-start | bytes 2555912 | tf_op jit(solution)/shard_map/ppermute | solution.py:419
  51.8 3.6 %shard_map.136 = (bf16[4,64,2048]{2,1,0:T(8,128)(2,1)S(1)}, bf16[4,64,2048]{2,1,0:T(8,128)(2,1)S(1)}, bf16[4,64,2048]{2,1,0:T(8,128)(2,1)S(1)}) custom-call(s32[16]{0:T(128)S(1)} %get-tuple-element.43.refs_0_, bf16[13,64,128]{2,1,0:T(8,128)(2,1)S(1)} %add_convert_fusion.4.refs_1_, bf16[13,64,128]{2,1,0:T(8,128)(2,1)S(1)} %collective-permute-done.4.refs_2_, ...), custom_call_target="tpu_custom_call" | custom-call | flops 99999997952 | bytes 36000000 | tf_op jit(solution)/shard_map/pallas_call | solution.py:24
  56.4 4.3 %collective-permute-done.10 = bf16[4,64,2048]{2,1,0:T(8,128)(2,1)} collective-permute-done((bf16[4,64,2048]{2,1,0:T(8,128)(2,1)}, bf16[4,64,2048]{2,1,0:T(8,128)(2,1)}, u32[]{:S(2)}, u32[]{:S(2)}) %collective-permute-start.10) | collective-permute-done | bytes 1048608 | tf_op jit(solution)/shard_map/ppermute | solution.py:527
  60.7 1.6 %add_convert_fusion.2.refs_1_ = bf16[4,64,2048]{2,1,0:T(8,128)(2,1)S(1)} fusion(bf16[4,64,2048]{2,1,0:T(8,128)(2,1)S(1)} %get-tuple-element.32, bf16[4,64,2048]{2,1,0:T(8,128)(2,1)} %collective-permute-done.10, pred[]{:T(512)S(6)} %or.3), kind=kLoop, calls=%fused_computation.3 | loop fusion | flops 2621440 | bytes 3145729 | tf_op jit(solution)/shard_map/convert_element_type | solution.py:415
  62.3 1.8 %collective-permute-start.19 = (bf16[4,64,2048]{2,1,0:T(8,128)(2,1)S(1)}, bf16[4,64,2048]{2,1,0:T(8,128)(2,1)S(1)}, u32[]{:S(2)}, u32[]{:S(2)}) collective-permute-start(bf16[4,64,2048]{2,1,0:T(8,128)(2,1)S(1)} %add_convert_fusion.2.refs_1_), channel_id=1, source_target_pairs={{0,4},{12,8},{4,12},{8,0},{1,5},{13,9},{5,13},{9,1},{2,6},{14,10},... | collective-permute-start | bytes 3145736 | tf_op jit(solution)/shard_map/ppermute | solution.py:537
  64.7 1.4 %copy-done.4 = bf16[13,64,2048]{2,1,0:T(8,128)(2,1)S(1)} copy-done((bf16[13,64,2048]{2,1,0:T(8,128)(2,1)S(1)}, bf16[13,64,2048]{2,1,0:T(8,128)(2,1)}, u32[]{:S(2)}) %copy-start.4) | copy-done | bytes 3407896
  66.1 5.2 %shard_map.138.refs_5_.refs_1_ = bf16[13,64,128]{2,1,0:T(8,128)(2,1)} custom-call(s32[13]{0:T(128)S(1)} %copy-done.11, s32[4]{0:T(128)S(1)} %copy-done.20, s32[1]{0:T(128)} %bitcast.7.refs_2_.refs_1_, bf16[13,64,2048]{2,1,0:T(8,128)(2,1)S(1)} %copy-done.4, bf16[13,64,2048]{2,1,0:T(8,128)(2,1)S(1)} %copy-done.4, bf16[13,64,2048]{2,1,0:T(8,128)(2,1)S(1)} %copy-done.4, ...), custom_call_target="tpu_custom_call" | custom-call | flops 99999997952 | bytes 36000000 | tf_op jit(solution)/shard_map/pallas_call | solution.py:24
  71.3 2.4 %collective-permute-start.13 = (bf16[13,64,128]{2,1,0:T(8,128)(2,1)}, bf16[13,64,128]{2,1,0:T(8,128)(2,1)S(1)}, u32[]{:S(2)}, u32[]{:S(2)}) collective-permute-start(bf16[13,64,128]{2,1,0:T(8,128)(2,1)} %shard_map.138.refs_5_.refs_1_), channel_id=1, source_target_pairs={{0,1},{1,0},{2,3},{3,2},{4,5},{5,4},{6,7},{7,6},{8,9},{9,8},{10,11... | collective-permute-start | bytes 638984 | tf_op jit(solution)/shard_map/ppermute | solution.py:419
  73.7 11.6 %collective-permute-done.19 = bf16[4,64,2048]{2,1,0:T(8,128)(2,1)S(1)} collective-permute-done((bf16[4,64,2048]{2,1,0:T(8,128)(2,1)S(1)}, bf16[4,64,2048]{2,1,0:T(8,128)(2,1)S(1)}, u32[]{:S(2)}, u32[]{:S(2)}) %collective-permute-start.19) | collective-permute-done | bytes 1048608 | tf_op jit(solution)/shard_map/ppermute | solution.py:537
  85.8 2.5 %collective-permute-start.20 = (bf16[4,64,2048]{2,1,0:T(8,128)(2,1)S(1)}, bf16[4,64,2048]{2,1,0:T(8,128)(2,1)}, u32[]{:S(2)}, u32[]{:S(2)}) collective-permute-start(bf16[4,64,2048]{2,1,0:T(8,128)(2,1)S(1)} %add_convert_fusion.1.refs_1_), channel_id=1, source_target_pairs={{4,8},{8,4},{5,9},{9,5},{6,10},{10,6},{7,11},{11,7},{20,24},{24,20... | collective-permute-start | bytes 3145736 | tf_op jit(solution)/shard_map/ppermute | solution.py:541
  88.3 1.5 %collective-permute-start.21 = (bf16[4,64,2048]{2,1,0:T(8,128)(2,1)S(1)}, bf16[4,64,2048]{2,1,0:T(8,128)(2,1)}, u32[]{:S(2)}, u32[]{:S(2)}) collective-permute-start(bf16[4,64,2048]{2,1,0:T(8,128)(2,1)S(1)} %add_convert_fusion.1.refs_1_), channel_id=1, source_target_pairs={{0,4},{12,8},{1,5},{13,9},{2,6},{14,10},{3,7},{15,11},{16,20},{28,... | collective-permute-start | bytes 3145736 | tf_op jit(solution)/shard_map/ppermute | solution.py:542
  90.2 4.6 %collective-permute-start.15 = (bf16[13,64,128]{2,1,0:T(8,128)(2,1)}, bf16[13,64,128]{2,1,0:T(8,128)(2,1)S(1)}, u32[]{:S(2)}, u32[]{:S(2)}) collective-permute-start(bf16[13,64,128]{2,1,0:T(8,128)(2,1)} %shard_map.138.refs_5_.refs_1_), channel_id=1, source_target_pairs={{0,3},{1,2},{2,1},{3,0},{4,7},{5,6},{6,5},{7,4},{8,11},{9,10},{10,... | collective-permute-start | bytes 638984 | tf_op jit(solution)/shard_map/ppermute | solution.py:419
  96.1 7.4 %collective-permute-done.15.refs_8_ = bf16[13,64,128]{2,1,0:T(8,128)(2,1)S(1)} collective-permute-done((bf16[13,64,128]{2,1,0:T(8,128)(2,1)}, bf16[13,64,128]{2,1,0:T(8,128)(2,1)S(1)}, u32[]{:S(2)}, u32[]{:S(2)}) %collective-permute-start.15) | collective-permute-done | bytes 213024 | tf_op jit(solution)/shard_map/ppermute | solution.py:419
  104.2 5.1 %shard_map.139 = (bf16[1664,256]{1,0:T(8,128)(2,1)}, bf16[384,256]{1,0:T(8,128)(2,1)}, bf16[384,256]{1,0:T(8,128)(2,1)}, bf16[384,256]{1,0:T(8,128)(2,1)}, bf16[384,256]{1,0:T(8,128)(2,1)}) custom-call(s32[13]{0:T(128)} %refs_0_.9, s32[16]{0:T(128)} %get-tuple-element.44.refs_1_, bf16[1664,256]{1,0:T(8,128)(2,1)} %copy-done.6, ...), custom_call_target="tpu_custom_call" | custom-call | flops 1000000000 | bytes 360000 | tf_op jit(solution)/shard_map/pallas_call | solution.py:24
  109.8 4.3 %collective-permute-start.17 = (bf16[384,256]{1,0:T(8,128)(2,1)}, bf16[384,256]{1,0:T(8,128)(2,1)S(1)}, u32[]{:S(2)}, u32[]{:S(2)}) collective-permute-start(bf16[384,256]{1,0:T(8,128)(2,1)} %get-tuple-element.36), channel_id=1, source_target_pairs={{0,8},{4,12},{8,0},{12,4},{1,9},{5,13},{9,1},{13,5},{2,10},{6,14},... | collective-permute-start | bytes 589832 | tf_op jit(solution)/shard_map/ppermute | solution.py:401
  114.1 1.7 %select_add_fusion = f32[4,64,2048]{2,1,0:T(8,128)S(1)} fusion(bf16[4,64,2048]{2,1,0:T(8,128)(2,1)S(1)} %copy-done.22, bf16[4,64,2048]{2,1,0:T(8,128)(2,1)} %collective-permute-done.10, bf16[4,64,2048]{2,1,0:T(8,128)(2,1)S(1)} %shard_map.141, pred[]{:T(512)S(6)} %or.3), kind=kLoop, calls=%fused_computation.1 | loop fusion | flops 3145728 | bytes 5242881 | tf_op jit(solution)/shard_map/add | solution.py:544
  115.9 2.1 %add_convert_fusion.refs_6_ = bf16[4,64,2048]{2,1,0:T(8,128)(2,1)S(1)} fusion(bf16[4,64,2048]{2,1,0:T(8,128)(2,1)} %collective-permute-done.21, f32[4,64,2048]{2,1,0:T(8,128)S(1)} %select_add_fusion, bf16[4,64,2048]{2,1,0:T(8,128)(2,1)} %collective-permute-done.20), kind=kLoop, calls=%fused_computation | loop fusion | flops 2621440 | bytes 5242880 | tf_op jit(solution)/shard_map/convert_element_type | solution.py:547
  118.0 9.4 %collective-permute-done.17.refs_3_ = bf16[384,256]{1,0:T(8,128)(2,1)S(1)} collective-permute-done((bf16[384,256]{1,0:T(8,128)(2,1)}, bf16[384,256]{1,0:T(8,128)(2,1)S(1)}, u32[]{:S(2)}, u32[]{:S(2)}) %collective-permute-start.17) | collective-permute-done | bytes 196640 | tf_op jit(solution)/shard_map/ppermute | solution.py:401
  127.5 3.2 %collective-permute-done.18.refs_4_ = bf16[384,256]{1,0:T(8,128)(2,1)S(1)} collective-permute-done((bf16[384,256]{1,0:T(8,128)(2,1)}, bf16[384,256]{1,0:T(8,128)(2,1)S(1)}, u32[]{:S(2)}, u32[]{:S(2)}) %collective-permute-start.18) | collective-permute-done | bytes 196640 | tf_op jit(solution)/shard_map/ppermute | solution.py:401
  (100 shorter events, 18.9 us)
Async XLA Ops:
  1.4 10.4 %collective-permute-start = (bf16[1,64,256]{2,1,0:T(8,128)(2,1)S(1)}, bf16[1,64,256]{2,1,0:T(8,128)(2,1)S(1)}, u32[]{:S(2)}, u32[]{:S(2)}) collective-permute-start(bf16[1,64,256]{2,1,0:T(8,128)(2,1)S(1)} %slice.3.refs_4_.refs_3_), channel_id=1, source_target_pairs={{0,4},{4,8},{8,12},{12,0},{1,5},{5,9},{9,13},{13,1},{2,6},{6,10},{... | collective-permute-start | bytes 98312 | tf_op jit(solution)/shard_map/ppermute | solution.py:401
  2.7 9.1 %collective-permute-start.1 = (bf16[1,64,256]{2,1,0:T(8,128)(2,1)S(1)}, bf16[1,64,256]{2,1,0:T(8,128)(2,1)S(1)}, u32[]{:S(2)}, u32[]{:S(2)}) collective-permute-start(bf16[1,64,256]{2,1,0:T(8,128)(2,1)S(1)} %slice.3.refs_4_.refs_3_), channel_id=1, source_target_pairs={{0,8},{4,12},{8,0},{12,4},{1,9},{5,13},{9,1},{13,5},{2,10},{6,14},... | collective-permute-start | bytes 98312 | tf_op jit(solution)/shard_map/ppermute | solution.py:401
  3.7 8.7 %collective-permute-start.2 = (bf16[1,64,256]{2,1,0:T(8,128)(2,1)S(1)}, bf16[1,64,256]{2,1,0:T(8,128)(2,1)S(1)}, u32[]{:S(2)}, u32[]{:S(2)}) collective-permute-start(bf16[1,64,256]{2,1,0:T(8,128)(2,1)S(1)} %slice.3.refs_4_.refs_3_), channel_id=1, source_target_pairs={{0,12},{4,0},{8,4},{12,8},{1,13},{5,1},{9,5},{13,9},{2,14},{6,2},{... | collective-permute-start | bytes 98312 | tf_op jit(solution)/shard_map/ppermute | solution.py:401
  16.2 23.2 %slice-start = ((s8[6815744]{0:T(1024)(128)(4,1)}), s8[2621440]{0:T(1024)(128)(4,1)S(1)}, s32[]{:S(2)}) async-start(s8[6815744]{0:T(1024)(128)(4,1)} %bitcast.10), calls=%async_computation | async-start | bytes 5242880
  17.0 2.6 %collective-permute-start.3 = (bf16[13,64,128]{2,1,0:T(8,128)(2,1)S(1)}, bf16[13,64,128]{2,1,0:T(8,128)(2,1)S(1)}, u32[]{:S(2)}, u32[]{:S(2)}) collective-permute-start(bf16[13,64,128]{2,1,0:T(8,128)(2,1)S(1)} %get-tuple-element.24), channel_id=1, source_target_pairs={{0,1},{1,0},{2,3},{3,2},{4,5},{5,4},{6,7},{7,6},{8,9},{9,8},{10,11... | collective-permute-start | bytes 638984 | tf_op jit(solution)/shard_map/ppermute | solution.py:419
  19.7 8.2 %collective-permute-start.4 = (bf16[13,64,128]{2,1,0:T(8,128)(2,1)S(1)}, bf16[13,64,128]{2,1,0:T(8,128)(2,1)S(1)}, u32[]{:S(2)}, u32[]{:S(2)}) collective-permute-start(bf16[13,64,128]{2,1,0:T(8,128)(2,1)S(1)} %add_convert_fusion.4.refs_1_), channel_id=1, source_target_pairs={{0,2},{1,3},{2,0},{3,1},{4,6},{5,7},{6,4},{7,5},{8,10},{9,11},{10,... | collective-permute-start | bytes 638984 | tf_op jit(solution)/shard_map/ppermute | solution.py:419
  21.0 12.3 %collective-permute-start.5 = (bf16[1,64,2048]{2,1,0:T(8,128)(2,1)}, bf16[1,64,2048]{2,1,0:T(8,128)(2,1)S(1)}, u32[]{:S(2)}, u32[]{:S(2)}) collective-permute-start(bf16[1,64,2048]{2,1,0:T(8,128)(2,1)} %shard_map.133.refs_2_.refs_11_), channel_id=1, source_target_pairs={{0,4},{4,8},{8,12},{1,5},{5,9},{9,13},{2,6},{6,10},{10,14},{3,7},{... | collective-permute-start | bytes 786440 | tf_op jit(solution)/shard_map/ppermute | solution.py:528
  22.9 10.4 %collective-permute-start.6 = (bf16[1,64,2048]{2,1,0:T(8,128)(2,1)}, bf16[1,64,2048]{2,1,0:T(8,128)(2,1)}, u32[]{:S(2)}, u32[]{:S(2)}) collective-permute-start(bf16[1,64,2048]{2,1,0:T(8,128)(2,1)} %shard_map.133.refs_2_.refs_11_), channel_id=1, source_target_pairs={{12,8},{8,4},{4,0},{13,9},{9,5},{5,1},{14,10},{10,6},{6,2},{15,11}... | collective-permute-start | bytes 786440 | tf_op jit(solution)/shard_map/ppermute | solution.py:529
  30.8 8.6 %slice-start.1 = ((s8[6815744]{0:T(1024)(128)(4,1)}), s8[4194304]{0:T(1024)(128)(4,1)S(1)}, s32[]{:S(2)}) async-start(s8[6815744]{0:T(1024)(128)(4,1)} %bitcast.10), calls=%async_computation.1 | async-start | bytes 8388608
  30.8 8.6 %copy-start.12 = (bf16[2048,1024]{1,0:T(8,128)(2,1)S(1)}, bf16[2048,1024]{1,0:T(8,128)(2,1)}, u32[]{:S(2)}) copy-start(bf16[2048,1024]{1,0:T(8,128)(2,1)} %refs_5_.5) | copy-start | bytes 12582916
  33.2 27.5 %collective-permute-start.10 = (bf16[4,64,2048]{2,1,0:T(8,128)(2,1)}, bf16[4,64,2048]{2,1,0:T(8,128)(2,1)}, u32[]{:S(2)}, u32[]{:S(2)}) collective-permute-start(bf16[4,64,2048]{2,1,0:T(8,128)(2,1)} %shard_map.132.refs_5_.refs_6_), channel_id=1, source_target_pairs={{0,4},{12,8},{4,0},{8,12},{1,5},{13,9},{5,1},{9,13},{2,6},{14,10},... | collective-permute-start | bytes 3145736 | tf_op jit(solution)/shard_map/ppermute | solution.py:527
  33.2 15.8 %copy-start.13 = (bf16[1,64,2048]{2,1,0:T(8,128)(2,1)}, bf16[1,64,2048]{2,1,0:T(8,128)(2,1)S(1)}, u32[]{:S(2)}) copy-start(bf16[1,64,2048]{2,1,0:T(8,128)(2,1)S(1)} %collective-permute-done.5.refs_3_.refs_12_) | copy-start | bytes 786436
  34.9 16.9 %collective-permute-start.8 = (bf16[1,64,2048]{2,1,0:T(8,128)(2,1)S(1)}, bf16[1,64,2048]{2,1,0:T(8,128)(2,1)S(1)}, u32[]{:S(2)}, u32[]{:S(2)}) collective-permute-start(bf16[1,64,2048]{2,1,0:T(8,128)(2,1)S(1)} %get-tuple-element.26.refs_7_), channel_id=1, source_target_pairs={{4,8},{8,4},{5,9},{9,5},{6,10},{10,6},{7,11},{11,7},{20,24},{24,20... | collective-permute-start | bytes 786440 | tf_op jit(solution)/shard_map/ppermute | solution.py:532
  38.1 13.7 %collective-permute-start.9 = (bf16[1,64,2048]{2,1,0:T(8,128)(2,1)S(1)}, bf16[1,64,2048]{2,1,0:T(8,128)(2,1)S(1)}, u32[]{:S(2)}, u32[]{:S(2)}) collective-permute-start(bf16[1,64,2048]{2,1,0:T(8,128)(2,1)S(1)} %get-tuple-element.31), channel_id=1, source_target_pairs={{4,12},{8,0},{5,13},{9,1},{6,14},{10,2},{7,15},{11,3},{20,28},{24,... | collective-permute-start | bytes 786440 | tf_op jit(solution)/shard_map/ppermute | solution.py:533
  50.0 14.1 %collective-permute-start.11 = (bf16[1664,256]{1,0:T(8,128)(2,1)S(1)}, bf16[1664,256]{1,0:T(8,128)(2,1)S(1)}, u32[]{:S(2)}, u32[]{:S(2)}) collective-permute-start(bf16[1664,256]{1,0:T(8,128)(2,1)S(1)} %get-tuple-element.30.refs_8_), channel_id=1, source_target_pairs={{0,1},{1,0},{2,3},{3,2},{4,5},{5,4},{6,7},{7,6},{8,9},{9,8},{10,11... | collective-permute-start | bytes 2555912 | tf_op jit(solution)/shard_map/ppermute | solution.py:419
  51.8 38.0 %collective-permute-start.7 = (bf16[1664,256]{1,0:T(8,128)(2,1)}, bf16[1664,256]{1,0:T(8,128)(2,1)}, u32[]{:S(2)}, u32[]{:S(2)}) collective-permute-start(bf16[1664,256]{1,0:T(8,128)(2,1)} %get-tuple-element.28), channel_id=1, source_target_pairs={{0,1},{1,0},{2,3},{3,2},{4,5},{5,4},{6,7},{7,6},{8,9},{9,8},{10,11... | collective-permute-start | bytes 2555912 | tf_op jit(solution)/shard_map/ppermute | solution.py:419
  62.3 23.0 %collective-permute-start.19 = (bf16[4,64,2048]{2,1,0:T(8,128)(2,1)S(1)}, bf16[4,64,2048]{2,1,0:T(8,128)(2,1)S(1)}, u32[]{:S(2)}, u32[]{:S(2)}) collective-permute-start(bf16[4,64,2048]{2,1,0:T(8,128)(2,1)S(1)} %add_convert_fusion.2.refs_1_), channel_id=1, source_target_pairs={{0,4},{12,8},{4,12},{8,0},{1,5},{13,9},{5,13},{9,1},{2,6},{14,10},... | collective-permute-start | bytes 3145736 | tf_op jit(solution)/shard_map/ppermute | solution.py:537
  64.3 39.2 %collective-permute-start.12 = (bf16[1664,256]{1,0:T(8,128)(2,1)S(1)}, bf16[1664,256]{1,0:T(8,128)(2,1)}, u32[]{:S(2)}, u32[]{:S(2)}) collective-permute-start(bf16[1664,256]{1,0:T(8,128)(2,1)S(1)} %add_convert_fusion.3.refs_16_), channel_id=1, source_target_pairs={{0,2},{1,3},{2,0},{3,1},{4,6},{5,7},{6,4},{7,5},{8,10},{9,11},{10,... | collective-permute-start | bytes 2555912 | tf_op jit(solution)/shard_map/ppermute | solution.py:419
  71.3 18.9 %collective-permute-start.13 = (bf16[13,64,128]{2,1,0:T(8,128)(2,1)}, bf16[13,64,128]{2,1,0:T(8,128)(2,1)S(1)}, u32[]{:S(2)}, u32[]{:S(2)}) collective-permute-start(bf16[13,64,128]{2,1,0:T(8,128)(2,1)} %shard_map.138.refs_5_.refs_1_), channel_id=1, source_target_pairs={{0,1},{1,0},{2,3},{3,2},{4,5},{5,4},{6,7},{7,6},{8,9},{9,8},{10,11... | collective-permute-start | bytes 638984 | tf_op jit(solution)/shard_map/ppermute | solution.py:419
  85.3 10.1 %copy-start.21 = (bf16[4,64,2048]{2,1,0:T(8,128)(2,1)}, bf16[4,64,2048]{2,1,0:T(8,128)(2,1)S(1)}, u32[]{:S(2)}) copy-start(bf16[4,64,2048]{2,1,0:T(8,128)(2,1)S(1)} %collective-permute-done.19) | copy-start | bytes 3145732
  85.8 30.1 %collective-permute-start.20 = (bf16[4,64,2048]{2,1,0:T(8,128)(2,1)S(1)}, bf16[4,64,2048]{2,1,0:T(8,128)(2,1)}, u32[]{:S(2)}, u32[]{:S(2)}) collective-permute-start(bf16[4,64,2048]{2,1,0:T(8,128)(2,1)S(1)} %add_convert_fusion.1.refs_1_), channel_id=1, source_target_pairs={{4,8},{8,4},{5,9},{9,5},{6,10},{10,6},{7,11},{11,7},{20,24},{24,20... | collective-permute-start | bytes 3145736 | tf_op jit(solution)/shard_map/ppermute | solution.py:541
  88.3 27.5 %collective-permute-start.21 = (bf16[4,64,2048]{2,1,0:T(8,128)(2,1)S(1)}, bf16[4,64,2048]{2,1,0:T(8,128)(2,1)}, u32[]{:S(2)}, u32[]{:S(2)}) collective-permute-start(bf16[4,64,2048]{2,1,0:T(8,128)(2,1)S(1)} %add_convert_fusion.1.refs_1_), channel_id=1, source_target_pairs={{0,4},{12,8},{1,5},{13,9},{2,6},{14,10},{3,7},{15,11},{16,20},{28,... | collective-permute-start | bytes 3145736 | tf_op jit(solution)/shard_map/ppermute | solution.py:542
  89.8 6.3 %collective-permute-start.14 = (bf16[13,64,128]{2,1,0:T(8,128)(2,1)}, bf16[13,64,128]{2,1,0:T(8,128)(2,1)S(1)}, u32[]{:S(2)}, u32[]{:S(2)}) collective-permute-start(bf16[13,64,128]{2,1,0:T(8,128)(2,1)} %shard_map.138.refs_5_.refs_1_), channel_id=1, source_target_pairs={{0,2},{1,3},{2,0},{3,1},{4,6},{5,7},{6,4},{7,5},{8,10},{9,11},{10,... | collective-permute-start | bytes 638984 | tf_op jit(solution)/shard_map/ppermute | solution.py:419
  90.2 14.0 %copy-start.23 = (bf16[13,64,128]{2,1,0:T(8,128)(2,1)}, bf16[13,64,128]{2,1,0:T(8,128)(2,1)S(1)}, u32[]{:S(2)}) copy-start(bf16[13,64,128]{2,1,0:T(8,128)(2,1)S(1)} %collective-permute-done.13.refs_6_) | copy-start | bytes 638980
  90.2 13.3 %collective-permute-start.15 = (bf16[13,64,128]{2,1,0:T(8,128)(2,1)}, bf16[13,64,128]{2,1,0:T(8,128)(2,1)S(1)}, u32[]{:S(2)}, u32[]{:S(2)}) collective-permute-start(bf16[13,64,128]{2,1,0:T(8,128)(2,1)} %shard_map.138.refs_5_.refs_1_), channel_id=1, source_target_pairs={{0,3},{1,2},{2,1},{3,0},{4,7},{5,6},{6,5},{7,4},{8,11},{9,10},{10,... | collective-permute-start | bytes 638984 | tf_op jit(solution)/shard_map/ppermute | solution.py:419
  96.1 8.1 %copy-start.24 = (bf16[13,64,128]{2,1,0:T(8,128)(2,1)}, bf16[13,64,128]{2,1,0:T(8,128)(2,1)S(1)}, u32[]{:S(2)}) copy-start(bf16[13,64,128]{2,1,0:T(8,128)(2,1)S(1)} %collective-permute-done.14.refs_7_) | copy-start | bytes 638980
  104.2 9.8 %copy-start.2 = (bf16[4,64,2048]{2,1,0:T(8,128)(2,1)S(1)}, bf16[4,64,2048]{2,1,0:T(8,128)(2,1)}, u32[]{:S(2)}) copy-start(bf16[4,64,2048]{2,1,0:T(8,128)(2,1)} %copy-done.1) | copy-start | bytes 3145732
  109.3 8.7 %collective-permute-start.16 = (bf16[384,256]{1,0:T(8,128)(2,1)}, bf16[384,256]{1,0:T(8,128)(2,1)S(1)}, u32[]{:S(2)}, u32[]{:S(2)}) collective-permute-start(bf16[384,256]{1,0:T(8,128)(2,1)} %get-tuple-element.35), channel_id=1, source_target_pairs={{0,4},{4,8},{8,12},{12,0},{1,5},{5,9},{9,13},{13,1},{2,6},{6,10},{... | collective-permute-start | bytes 589832 | tf_op jit(solution)/shard_map/ppermute | solution.py:401
  109.8 17.7 %collective-permute-start.17 = (bf16[384,256]{1,0:T(8,128)(2,1)}, bf16[384,256]{1,0:T(8,128)(2,1)S(1)}, u32[]{:S(2)}, u32[]{:S(2)}) collective-permute-start(bf16[384,256]{1,0:T(8,128)(2,1)} %get-tuple-element.36), channel_id=1, source_target_pairs={{0,8},{4,12},{8,0},{12,4},{1,9},{5,13},{9,1},{13,5},{2,10},{6,14},... | collective-permute-start | bytes 589832 | tf_op jit(solution)/shard_map/ppermute | solution.py:401
  114.1 16.6 %collective-permute-start.18 = (bf16[384,256]{1,0:T(8,128)(2,1)}, bf16[384,256]{1,0:T(8,128)(2,1)S(1)}, u32[]{:S(2)}, u32[]{:S(2)}) collective-permute-start(bf16[384,256]{1,0:T(8,128)(2,1)} %get-tuple-element.37), channel_id=1, source_target_pairs={{0,12},{4,0},{8,4},{12,8},{1,13},{5,1},{9,5},{13,9},{2,14},{6,2},{... | collective-permute-start | bytes 589832 | tf_op jit(solution)/shard_map/ppermute | solution.py:401
  115.8 14.8 %copy-start.15 = (bf16[384,256]{1,0:T(8,128)(2,1)S(1)}, bf16[384,256]{1,0:T(8,128)(2,1)}, u32[]{:S(2)}) copy-start(bf16[384,256]{1,0:T(8,128)(2,1)} %get-tuple-element.34.refs_1_) | copy-start | bytes 589828
  118.0 13.4 %copy-start.5 = (bf16[4,64,2048]{2,1,0:T(8,128)(2,1)}, bf16[4,64,2048]{2,1,0:T(8,128)(2,1)S(1)}, u32[]{:S(2)}) copy-start(bf16[4,64,2048]{2,1,0:T(8,128)(2,1)S(1)} %add_convert_fusion.refs_6_) | copy-start | bytes 3145732
  (18 other events, 41.9 us)

commit v13 on v12

--- a/solution.py
+++ b/solution.py
@@ -61,12 +61,13 @@
     return jnp.where(live, ranks, 0.0).astype(rows.dtype)
 
 
-def kept_ranks(lengths, maps, features, others, tokens=()):
+def kept_ranks(lengths, maps, features, others):
     blocks, rank, width = maps.shape
     kept = blocks - SW
-    last_shape = (SW, *others.shape[1:])
-
-    def kernel(lengths_ref, maps_ref, rows_ref, others_ref, out_ref, last_other):
+    last_shapes = [(SW, rank, width), (SW, *others.shape[1:])]
+
+    def kernel(lengths_ref, maps_ref, rows_ref, others_ref, out_ref, last_ref, last_other):
+        last_ref[...] = maps_ref[kept:]
         last_other[...] = others_ref[...]
         for k in range(kept):
             out_ref[k] = masked_rank(maps_ref[k], rows_ref[k * BLOCK : (k + 1) * BLOCK], lengths_ref[k])
@@ -76,15 +77,12 @@
         (lengths,),
         (1,),
         [
-            (maps, pl.BlockSpec((kept, rank, width), lambda i, *_: (0, 0, 0), pipeline_mode=pl.Buffered(1))),
+            whole(maps),
             (features, pl.BlockSpec((kept * BLOCK, width), lambda i, *_: (0, 0), pipeline_mode=pl.Buffered(1))),
-            (others, pl.BlockSpec(last_shape, lambda i, *_: (kept, 0, 0), pipeline_mode=pl.Buffered(1))),
+            (others, pl.BlockSpec(last_shapes[1], lambda i, *_: (kept, 0, 0), pipeline_mode=pl.Buffered(1))),
         ],
-        [
-            ((blocks, rank, BLOCK), features.dtype, pl.BlockSpec((kept, rank, BLOCK), lambda i, *_: (0, 0, 0))),
-            (last_shape, features.dtype, constant_spec(last_shape)),
-        ],
-        tokens,
+        [((blocks, rank, BLOCK), features.dtype, pl.BlockSpec((kept, rank, BLOCK), lambda i, *_: (0, 0, 0)))]
+        + [(shape, features.dtype, constant_spec(shape)) for shape in last_shapes],
         vmem=60,
     )
 
@@ -455,7 +453,7 @@
     return entry(me) if size == 1 else add(entry(me), from_left, from_right)
 
 
-ROLES = ((3, 2, 1, 0), (0, 3, 2, 1), (3, 0, 1, 2), (0, 1, 2, 3))
+ROLES = ((3, 2, 1, 0), (2, 3, 0, 1), (1, 0, 3, 2), (0, 1, 2, 3))
 
 
 def body(
@@ -479,8 +477,7 @@
     order = jnp.arange(devices, dtype=jnp.int32)
     holder = jnp.sum(jnp.where(partner == me, order, 0))
 
-    up_own = adapter_up_matrix[kept:]
-    cot_terms, down_own = kept_ranks(lengths, adapter_up_matrix, cotangent, adapter_down_rows, [up_own])
+    cot_terms, up_own, down_own = kept_ranks(lengths, adapter_up_matrix, cotangent, adapter_down_rows)
     up_choices, _ = shifted(up_own, holder)
     cot_terms, up_last = with_last_rank(lengths, partner, me, up_choices, cotangent, cot_terms)
     rank_cot = exchanged(cot_terms)
@@ -524,7 +521,7 @@
         inner = (me == 1) | (me == 2)
         codes = codes_of(jnp.array(ROLES, jnp.int32)[me])
         (first,) = down_rows(codes, 0, 1, 1, rank_cot, hidden)
-        from_first = lax.ppermute(first, "dp", [(0, 1), (3, 2), (1, 0), (2, 3)])
+        from_end = lax.ppermute(first, "dp", [(0, 1), (3, 2)])
         from_left = lax.ppermute(down_own, "dp", [(0, 1), (1, 2), (2, 3)])
         from_right = lax.ppermute(down_own, "dp", [(3, 2), (2, 1), (1, 0)])
         passed, outward = passed_on(partner, me, down_own, from_left, from_right, [first])
@@ -533,16 +530,15 @@
         outward = lax.ppermute(outward, "dp", [(1, 3), (2, 0)])
         down_choices = [down_own, from_left, from_right, passed, outward]
         second, third, own = down_rows(codes, OWN, 3, 1, rank_cot, hidden, [terms[0], passed, outward], 100.0)
-        second = add(second, jnp.where(inner, from_first, jnp.zeros((), first.dtype)))
+        second = add(second, jnp.where(inner, from_end, jnp.zeros((), first.dtype)))
         from_second = lax.ppermute(second, "dp", [(0, 1), (3, 2), (1, 3), (2, 0)])
-        base_sums, away = base_parts(terms, second)
-        rank_in = inputs(down_choices, away)
-        third = add(after(third, rank_in[0]), jnp.where(inner, from_second, jnp.zeros((), first.dtype)))
-        from_inner = lax.ppermute(third, "dp", [(1, 2), (2, 1)])
-        from_third = lax.ppermute(third, "dp", [(0, 1), (3, 2)])
+        rank_in = inputs(down_choices, second)
+        base_sums, _ = base_parts(terms, rank_in[0])
+        middle = add(after(first, *rank_in[1:]), from_second)
+        from_inner = lax.ppermute(middle, "dp", [(1, 2), (2, 1)])
+        from_third = lax.ppermute(after(third, middle), "dp", [(0, 1), (3, 2), (1, 0), (2, 3)])
         near_total = lax.optimization_barrier(
-            after(own, third).astype(jnp.float32)
-            + jnp.where(inner, 0.0, from_first.astype(jnp.float32) + from_second.astype(jnp.float32))
+            after(own, middle).astype(jnp.float32) + jnp.where(inner, 0.0, from_second.astype(jnp.float32))
         )
         down_out = (near_total + from_inner.astype(jnp.float32) + from_third.astype(jnp.float32)).astype(own.dtype)
 

time: 132 us -> 132 us (level)
  the two profiles are of different devices: /device:TPU:9 before, /device:TPU:0 now
where the time goes in v13:
time: 132 us; the launch traced here: 131 us
  waiting for transfers between devices  42.3 us (32%)
  starting transfers between devices  34.2 us (26%)
  Pallas kernels  32.5 us (25%)
  other arithmetic  10.5 us (8%)
  local copies, waits for them, and re-layouts  9.62 us (7%)
  between operations  1.62 us (1%)
    pallas_call x14, Pallas kernels, call(): pl.pallas_call(run, grid_spec=pltpu.PrefetchScalarGridSpec(num_scalar_pre...  32.5 us
    ppermute x8, waiting for transfers between devices, crossed(): lax.ppermute(array, 'tensor', [(i, i ^ by) for i in range(lax.axis_size('...  14.1 us
    ppermute x6, waiting for transfers between devices, shift(): lax.ppermute(array, 'dp', [(i, (i + by) % size) for i in range(size)])  11.8 us
    ppermute x6, starting transfers between devices, shift(): lax.ppermute(array, 'dp', [(i, (i + by) % size) for i in range(size)])  11 us
    ppermute x1, waiting for transfers between devices, body(): lax.ppermute(after(third, middle), 'dp', [(0, 1), (3, 2), (1, 0), (2, 3)])  8.92 us
    unnamed x56, local copies, waits for them, and re-layouts  8.88 us
    ppermute x1, waiting for transfers between devices, body(): from_second = lax.ppermute(second, 'dp', [(0, 1), (3, 2), (1, 3), (2, 0)])  6.58 us
    ppermute x1, starting transfers between devices, body(): from_end = lax.ppermute(first, 'dp', [(0, 1), (3, 2)])  4.99 us
  transfers between devices with their start and end apart: 22, of which 12 were waited for; matrix products, arithmetic and copies ran while one was open for 9% of the time, Pallas kernels for 21%

profile of v13, /device:TPU:0, one launch (start us, length us, event | category | flops | bytes accessed | tf_op | source)
XLA Modules:
  0.0 130.9 jit_solution(3294769482699260393)
XLA Ops:
  0.7 3.2 %shard_map.130 = (bf16[13,64,128]{2,1,0:T(8,128)(2,1)}, bf16[1,64,256]{2,1,0:T(8,128)(2,1)}, bf16[1,64,2048]{2,1,0:T(8,128)(2,1)}) custom-call(s32[13]{0:T(128)} %refs_0_.9, bf16[13,64,256]{2,1,0:T(8,128)(2,1)} %refs_10_.3, bf16[1664,256]{1,0:T(8,128)(2,1)} %refs_9_.3, bf16[13,64,2048]{2,1,0:T(8,128)(2,1)} %refs_6_.5), custom_call_target="tpu_custom_call" | custom-call | flops 1000000000 | bytes 360000 | tf_op jit(solution)/shard_map/pallas_call | solution.py:24
  3.9 3.0 %collective-permute-start = (bf16[1,64,256]{2,1,0:T(8,128)(2,1)}, bf16[1,64,256]{2,1,0:T(8,128)(2,1)S(1)}, u32[]{:S(2)}, u32[]{:S(2)}) collective-permute-start(bf16[1,64,256]{2,1,0:T(8,128)(2,1)} %get-tuple-element.24.refs_3_), channel_id=1, source_target_pairs={{0,4},{4,8},{8,12},{12,0},{1,5},{5,9},{9,13},{13,1},{2,6},{6,10},{... | collective-permute-start | bytes 98312 | tf_op jit(solution)/shard_map/ppermute | solution.py:399
  6.9 2.6 %collective-permute-start.1 = (bf16[1,64,256]{2,1,0:T(8,128)(2,1)}, bf16[1,64,256]{2,1,0:T(8,128)(2,1)S(1)}, u32[]{:S(2)}, u32[]{:S(2)}) collective-permute-start(bf16[1,64,256]{2,1,0:T(8,128)(2,1)} %get-tuple-element.24.refs_3_), channel_id=1, source_target_pairs={{0,8},{4,12},{8,0},{12,4},{1,9},{5,13},{9,1},{13,5},{2,10},{6,14},... | collective-permute-start | bytes 98312 | tf_op jit(solution)/shard_map/ppermute | solution.py:399
  9.5 1.3 %collective-permute-start.2 = (bf16[1,64,256]{2,1,0:T(8,128)(2,1)}, bf16[1,64,256]{2,1,0:T(8,128)(2,1)S(1)}, u32[]{:S(2)}, u32[]{:S(2)}) collective-permute-start(bf16[1,64,256]{2,1,0:T(8,128)(2,1)} %get-tuple-element.24.refs_3_), channel_id=1, source_target_pairs={{0,12},{4,0},{8,4},{12,8},{1,13},{5,1},{9,5},{13,9},{2,14},{6,2},{... | collective-permute-start | bytes 98312 | tf_op jit(solution)/shard_map/ppermute | solution.py:399
  17.6 1.4 %collective-permute-done.3 = bf16[13,64,128]{2,1,0:T(8,128)(2,1)S(1)} collective-permute-done((bf16[13,64,128]{2,1,0:T(8,128)(2,1)S(1)}, bf16[13,64,128]{2,1,0:T(8,128)(2,1)S(1)}, u32[]{:S(2)}, u32[]{:S(2)}) %collective-permute-start.3) | collective-permute-done | bytes 213024 | tf_op jit(solution)/shard_map/ppermute | solution.py:417
  19.0 1.6 %collective-permute-start.4 = (bf16[13,64,128]{2,1,0:T(8,128)(2,1)S(1)}, bf16[13,64,128]{2,1,0:T(8,128)(2,1)S(1)}, u32[]{:S(2)}, u32[]{:S(2)}) collective-permute-start(bf16[13,64,128]{2,1,0:T(8,128)(2,1)S(1)} %add_convert_fusion.3.refs_1_), channel_id=1, source_target_pairs={{0,2},{1,3},{2,0},{3,1},{4,6},{5,7},{6,4},{7,5},{8,10},{9,11},{10,... | collective-permute-start | bytes 638984 | tf_op jit(solution)/shard_map/ppermute | solution.py:417
  20.6 2.1 %collective-permute-start.5 = (bf16[1,64,2048]{2,1,0:T(8,128)(2,1)}, bf16[1,64,2048]{2,1,0:T(8,128)(2,1)S(1)}, u32[]{:S(2)}, u32[]{:S(2)}) collective-permute-start(bf16[1,64,2048]{2,1,0:T(8,128)(2,1)} %shard_map.133.refs_2_.refs_11_), channel_id=1, source_target_pairs={{0,4},{4,8},{8,12},{1,5},{5,9},{9,13},{2,6},{6,10},{10,14},{3,7},{... | collective-permute-start | bytes 786440 | tf_op jit(solution)/shard_map/ppermute | solution.py:525
  22.7 1.3 collective-permute-start.6
  24.3 1.4 %select_reduce_fusion = (s32[16]{0:T(128)S(1)}, s32[16]{0:T(128)}) fusion(s32[13]{0:T(128)} %compare_select_fusion.2, s32[13]{0:T(128)} %select_reduce_fusion.2, s32[16]{0:T(128)S(1)} %add.103, s32[16]{0:T(128)S(1)} %add.98), kind=kLoop, calls=%fused_computation.8 | loop fusion | flops 1216 | bytes 360 | tf_op jit(solution)/shard_map/reduce_sum | solution.py:498
  26.4 2.9 %copy-done = bf16[1664,2048]{1,0:T(8,128)(2,1)S(1)} copy-done((bf16[1664,2048]{1,0:T(8,128)(2,1)S(1)}, bf16[1664,2048]{1,0:T(8,128)(2,1)}, u32[]{:S(2)}) %copy-start) | copy-done | bytes 6815768
  29.3 2.4 %shard_map.132.refs_5_.refs_6_.refs_0_ = bf16[4,64,2048]{2,1,0:T(8,128)(2,1)} custom-call(s32[16]{0:T(128)S(1)} %get-tuple-element.45.refs_0_, bf16[13,64,128]{2,1,0:T(8,128)(2,1)S(1)} %add_convert_fusion.3.refs_1_, bf16[13,64,128]{2,1,0:T(8,128)(2,1)S(1)} %collective-permute-done.4.refs_2_, bf16[1664,2048]{1,0:T(8,128)(2,1)S(1)} %copy-done, ...), custom_call_target="tpu_custom_call" | custom-call | flops 1000000000 | bytes 360000 | tf_op jit(solution)/shard_map/pallas_call | solution.py:24
  31.7 5.0 %collective-permute-start.10 = (bf16[4,64,2048]{2,1,0:T(8,128)(2,1)}, bf16[4,64,2048]{2,1,0:T(8,128)(2,1)}, u32[]{:S(2)}, u32[]{:S(2)}) collective-permute-start(bf16[4,64,2048]{2,1,0:T(8,128)(2,1)} %shard_map.132.refs_5_.refs_6_.refs_0_), channel_id=1, source_target_pairs={{0,4},{12,8},{1,5},{13,9},{2,6},{14,10},{3,7},{15,11},{16,20},{28,... | collective-permute-start | bytes 3145736 | tf_op jit(solution)/shard_map/ppermute | solution.py:524
  36.7 1.6 %shard_map.134 = (bf16[1,64,2048]{2,1,0:T(8,128)(2,1)S(1)}, bf16[1,64,2048]{2,1,0:T(8,128)(2,1)S(1)}) custom-call(s32[4]{0:T(128)S(1)} %copy-done.19, s32[1]{0:T(128)} %bitcast.7.refs_2_.refs_1_, bf16[1,64,2048]{2,1,0:T(8,128)(2,1)} %shard_map.133.refs_2_.refs_11_, bf16[1,64,2048]{2,1,0:T(8,128)(2,1)S(1)} %collective-permute-done.5.refs_3_.refs_12_, ...), custom_call_target="tpu_custom_call" | custom-call | flops 1000000000 | bytes 360000 | tf_op jit(solution)/shard_map/pallas_call | solution.py:24
  39.0 1.3 collective-permute-start.9
  40.4 9.6 %shard_map.135 = (bf16[1664,256]{1,0:T(8,128)(2,1)}, bf16[1664,256]{1,0:T(8,128)(2,1)S(1)}, bf16[1664,256]{1,0:T(8,128)(2,1)}, bf16[1664,256]{1,0:T(8,128)(2,1)S(1)}) custom-call(s32[4]{0:T(128)S(1)} %pad_add_fusion.refs_0_, bf16[1664,2048]{1,0:T(8,128)(2,1)S(1)} %bitcast.11, bf16[2048,1024]{1,0:T(8,128)(2,1)S(1)} %copy-done.14, ...), custom_call_target="tpu_custom_call" | custom-call | flops 99999997952 | bytes 36000000 | tf_op jit(solution)/shard_map/pallas_call | solution.py:24
  51.8 4.6 %shard_map.136 = (bf16[4,64,2048]{2,1,0:T(8,128)(2,1)S(1)}, bf16[4,64,2048]{2,1,0:T(8,128)(2,1)}, bf16[4,64,2048]{2,1,0:T(8,128)(2,1)S(1)}) custom-call(s32[16]{0:T(128)S(1)} %get-tuple-element.45.refs_0_, bf16[13,64,128]{2,1,0:T(8,128)(2,1)S(1)} %add_convert_fusion.3.refs_1_, bf16[13,64,128]{2,1,0:T(8,128)(2,1)S(1)} %collective-permute-done.4.refs_2_, ...), custom_call_target="tpu_custom_call" | custom-call | flops 99999997952 | bytes 36000000 | tf_op jit(solution)/shard_map/pallas_call | solution.py:24
  58.3 4.5 %collective-permute-start.19 = (bf16[4,64,2048]{2,1,0:T(8,128)(2,1)S(1)}, bf16[4,64,2048]{2,1,0:T(8,128)(2,1)S(1)}, u32[]{:S(2)}, u32[]{:S(2)}) collective-permute-start(bf16[4,64,2048]{2,1,0:T(8,128)(2,1)S(1)} %add_convert_fusion.1.refs_16_), channel_id=1, source_target_pairs={{0,4},{12,8},{4,12},{8,0},{1,5},{13,9},{5,13},{9,1},{2,6},{14,10},... | collective-permute-start | bytes 3145736 | tf_op jit(solution)/shard_map/ppermute | solution.py:534
  62.8 4.6 %shard_map.137.refs_1_.refs_5_ = bf16[13,64,128]{2,1,0:T(8,128)(2,1)S(1)} custom-call(s32[13]{0:T(128)S(1)} %copy-done.13, s32[4]{0:T(128)S(1)} %copy-done.19, s32[1]{0:T(128)} %bitcast.7.refs_2_.refs_1_, bf16[13,64,2048]{2,1,0:T(8,128)(2,1)S(1)} %copy-done.4, bf16[13,64,2048]{2,1,0:T(8,128)(2,1)S(1)} %copy-done.4, bf16[13,64,2048]{2,1,0:T(8,128)(2,1)S(1)} %copy-done.4, ...), custom_call_target="tpu_custom_call" | custom-call | flops 99999997952 | bytes 36000000 | tf_op jit(solution)/shard_map/pallas_call | solution.py:24
  68.1 1.3 collective-permute-start.15
  69.3 2.3 %add_convert_fusion.2 = bf16[1664,256]{1,0:T(8,128)(2,1)} fusion(bf16[1664,256]{1,0:T(8,128)(2,1)} %collective-permute-done.11, bf16[1664,256]{1,0:T(8,128)(2,1)S(1)} %shard_map.138), kind=kLoop, calls=%fused_computation.6 | loop fusion | flops 1703936 | bytes 2555904 | tf_op jit(solution)/shard_map/convert_element_type | solution.py:413
  72.2 3.3 %collective-permute-done.14.refs_7_.refs_2_ = bf16[13,64,128]{2,1,0:T(8,128)(2,1)S(1)} collective-permute-done((bf16[13,64,128]{2,1,0:T(8,128)(2,1)S(1)}, bf16[13,64,128]{2,1,0:T(8,128)(2,1)S(1)}, u32[]{:S(2)}, u32[]{:S(2)}) %collective-permute-start.14) | collective-permute-done | bytes 213024 | tf_op jit(solution)/shard_map/ppermute | solution.py:417
  75.6 3.7 %collective-permute-done.15.refs_8_.refs_3_ = bf16[13,64,128]{2,1,0:T(8,128)(2,1)S(1)} collective-permute-done((bf16[13,64,128]{2,1,0:T(8,128)(2,1)S(1)}, bf16[13,64,128]{2,1,0:T(8,128)(2,1)S(1)}, u32[]{:S(2)}, u32[]{:S(2)}) %collective-permute-start.15) | collective-permute-done | bytes 213024 | tf_op jit(solution)/shard_map/ppermute | solution.py:417
  79.2 6.6 %collective-permute-done.19 = bf16[4,64,2048]{2,1,0:T(8,128)(2,1)S(1)} collective-permute-done((bf16[4,64,2048]{2,1,0:T(8,128)(2,1)S(1)}, bf16[4,64,2048]{2,1,0:T(8,128)(2,1)S(1)}, u32[]{:S(2)}, u32[]{:S(2)}) %collective-permute-start.19) | collective-permute-done | bytes 1048608 | tf_op jit(solution)/shard_map/ppermute | solution.py:534
  85.8 2.0 %fusion.refs_1_ = bf16[4,64,2048]{2,1,0:T(8,128)(2,1)S(1)} fusion(bf16[4,64,2048]{2,1,0:T(8,128)(2,1)S(1)} %collective-permute-done.19, bf16[4,64,2048]{2,1,0:T(8,128)(2,1)} %shard_map.140), kind=kLoop, calls=%fused_computation.2 | loop fusion | flops 2097152 | bytes 3145728 | tf_op jit(solution)/shard_map/convert_element_type | solution.py:413
  87.9 2.1 %collective-permute-start.21 = (bf16[4,64,2048]{2,1,0:T(8,128)(2,1)}, bf16[4,64,2048]{2,1,0:T(8,128)(2,1)S(1)}, u32[]{:S(2)}, u32[]{:S(2)}) collective-permute-start(bf16[4,64,2048]{2,1,0:T(8,128)(2,1)} %shard_map.142), channel_id=1, source_target_pairs={{0,4},{12,8},{4,0},{8,12},{1,5},{13,9},{5,1},{9,13},{2,6},{14,10},... | collective-permute-start | bytes 3145736 | tf_op jit(solution)/shard_map/ppermute | solution.py:539
  90.0 1.6 %collective-permute-start.20 = (bf16[4,64,2048]{2,1,0:T(8,128)(2,1)S(1)}, bf16[4,64,2048]{2,1,0:T(8,128)(2,1)}, u32[]{:S(2)}, u32[]{:S(2)}) collective-permute-start(bf16[4,64,2048]{2,1,0:T(8,128)(2,1)S(1)} %fusion.refs_1_), channel_id=1, source_target_pairs={{4,8},{8,4},{5,9},{9,5},{6,10},{10,6},{7,11},{11,7},{20,24},{24,20... | collective-permute-start | bytes 3145736 | tf_op jit(solution)/shard_map/ppermute | solution.py:538
  92.9 5.1 %collective-permute-done.12.refs_4_ = bf16[1664,256]{1,0:T(8,128)(2,1)S(1)} collective-permute-done((bf16[1664,256]{1,0:T(8,128)(2,1)}, bf16[1664,256]{1,0:T(8,128)(2,1)S(1)}, u32[]{:S(2)}, u32[]{:S(2)}) %collective-permute-start.12) | collective-permute-done | bytes 852000 | tf_op jit(solution)/shard_map/ppermute | solution.py:417
  98.9 5.1 %shard_map.139 = (bf16[1664,256]{1,0:T(8,128)(2,1)}, bf16[384,256]{1,0:T(8,128)(2,1)}, bf16[384,256]{1,0:T(8,128)(2,1)}, bf16[384,256]{1,0:T(8,128)(2,1)}, bf16[384,256]{1,0:T(8,128)(2,1)}) custom-call(s32[13]{0:T(128)} %refs_0_.9, s32[16]{0:T(128)} %get-tuple-element.46.refs_1_, bf16[1664,256]{1,0:T(8,128)(2,1)} %copy-done.6, ...), custom_call_target="tpu_custom_call" | custom-call | flops 1000000000 | bytes 360000 | tf_op jit(solution)/shard_map/pallas_call | solution.py:24
  104.0 3.0 %collective-permute-start.17 = (bf16[384,256]{1,0:T(8,128)(2,1)}, bf16[384,256]{1,0:T(8,128)(2,1)S(1)}, u32[]{:S(2)}, u32[]{:S(2)}) collective-permute-start(bf16[384,256]{1,0:T(8,128)(2,1)} %get-tuple-element.38), channel_id=1, source_target_pairs={{0,8},{4,12},{8,0},{12,4},{1,9},{5,13},{9,1},{13,5},{2,10},{6,14},... | collective-permute-start | bytes 589832 | tf_op jit(solution)/shard_map/ppermute | solution.py:399
  108.3 8.9 %collective-permute-done.21 = bf16[4,64,2048]{2,1,0:T(8,128)(2,1)S(1)} collective-permute-done((bf16[4,64,2048]{2,1,0:T(8,128)(2,1)}, bf16[4,64,2048]{2,1,0:T(8,128)(2,1)S(1)}, u32[]{:S(2)}, u32[]{:S(2)}) %collective-permute-start.21) | collective-permute-done | bytes 1048608 | tf_op jit(solution)/shard_map/ppermute | solution.py:539
  117.3 1.8 %add_convert_fusion.refs_6_ = bf16[4,64,2048]{2,1,0:T(8,128)(2,1)S(1)} fusion(bf16[4,64,2048]{2,1,0:T(8,128)(2,1)S(1)} %collective-permute-done.21, f32[4,64,2048]{2,1,0:T(8,128)S(1)} %fusion.1, bf16[4,64,2048]{2,1,0:T(8,128)(2,1)} %collective-permute-done.20), kind=kLoop, calls=%fused_computation.4 | loop fusion | flops 2621440 | bytes 5242880 | tf_op jit(solution)/shard_map/convert_element_type | solution.py:543
  119.8 10.3 %collective-permute-done.17.refs_3_ = bf16[384,256]{1,0:T(8,128)(2,1)S(1)} collective-permute-done((bf16[384,256]{1,0:T(8,128)(2,1)}, bf16[384,256]{1,0:T(8,128)(2,1)S(1)}, u32[]{:S(2)}, u32[]{:S(2)}) %collective-permute-start.17) | collective-permute-done | bytes 196640 | tf_op jit(solution)/shard_map/ppermute | solution.py:399
  (100 shorter events, 17.7 us)
Async XLA Ops:
  0.6 13.6 %copy-start.13 = (s32[13]{0:T(128)S(1)}, s32[13]{0:T(128)}, u32[]{:S(2)}) copy-start(s32[13]{0:T(128)} %refs_0_.9) | copy-start | bytes 160
  0.7 13.6 %copy-start.3 = (bf16[1664,256]{1,0:T(8,128)(2,1)S(1)}, bf16[1664,256]{1,0:T(8,128)(2,1)}, u32[]{:S(2)}) copy-start(bf16[1664,256]{1,0:T(8,128)(2,1)} %refs_9_.3) | copy-start | bytes 2555908
  0.7 13.6 %copy-start.19 = (s32[4]{0:T(128)S(1)}, s32[4]{0:T(128)}, u32[]{:S(2)}) copy-start(s32[4]{0:T(128)} %refs_1_.7) | copy-start | bytes 52
  3.9 9.0 %collective-permute-start = (bf16[1,64,256]{2,1,0:T(8,128)(2,1)}, bf16[1,64,256]{2,1,0:T(8,128)(2,1)S(1)}, u32[]{:S(2)}, u32[]{:S(2)}) collective-permute-start(bf16[1,64,256]{2,1,0:T(8,128)(2,1)} %get-tuple-element.24.refs_3_), channel_id=1, source_target_pairs={{0,4},{4,8},{8,12},{12,0},{1,5},{5,9},{9,13},{13,1},{2,6},{6,10},{... | collective-permute-start | bytes 98312 | tf_op jit(solution)/shard_map/ppermute | solution.py:399
  6.9 6.0 %collective-permute-start.1 = (bf16[1,64,256]{2,1,0:T(8,128)(2,1)}, bf16[1,64,256]{2,1,0:T(8,128)(2,1)S(1)}, u32[]{:S(2)}, u32[]{:S(2)}) collective-permute-start(bf16[1,64,256]{2,1,0:T(8,128)(2,1)} %get-tuple-element.24.refs_3_), channel_id=1, source_target_pairs={{0,8},{4,12},{8,0},{12,4},{1,9},{5,13},{9,1},{13,5},{2,10},{6,14},... | collective-permute-start | bytes 98312 | tf_op jit(solution)/shard_map/ppermute | solution.py:399
  9.5 4.1 %collective-permute-start.2 = (bf16[1,64,256]{2,1,0:T(8,128)(2,1)}, bf16[1,64,256]{2,1,0:T(8,128)(2,1)S(1)}, u32[]{:S(2)}, u32[]{:S(2)}) collective-permute-start(bf16[1,64,256]{2,1,0:T(8,128)(2,1)} %get-tuple-element.24.refs_3_), channel_id=1, source_target_pairs={{0,12},{4,0},{8,4},{12,8},{1,13},{5,1},{9,5},{13,9},{2,14},{6,2},{... | collective-permute-start | bytes 98312 | tf_op jit(solution)/shard_map/ppermute | solution.py:399
  16.7 23.6 %slice-start = ((s8[6815744]{0:T(1024)(128)(4,1)}), s8[2621440]{0:T(1024)(128)(4,1)S(1)}, s32[]{:S(2)}) async-start(s8[6815744]{0:T(1024)(128)(4,1)} %bitcast.10), calls=%async_computation | async-start | bytes 5242880
  17.4 1.5 %collective-permute-start.3 = (bf16[13,64,128]{2,1,0:T(8,128)(2,1)S(1)}, bf16[13,64,128]{2,1,0:T(8,128)(2,1)S(1)}, u32[]{:S(2)}, u32[]{:S(2)}) collective-permute-start(bf16[13,64,128]{2,1,0:T(8,128)(2,1)S(1)} %get-tuple-element.26), channel_id=1, source_target_pairs={{0,1},{1,0},{2,3},{3,2},{4,5},{5,4},{6,7},{7,6},{8,9},{9,8},{10,11... | collective-permute-start | bytes 638984 | tf_op jit(solution)/shard_map/ppermute | solution.py:417
  19.0 7.4 %collective-permute-start.4 = (bf16[13,64,128]{2,1,0:T(8,128)(2,1)S(1)}, bf16[13,64,128]{2,1,0:T(8,128)(2,1)S(1)}, u32[]{:S(2)}, u32[]{:S(2)}) collective-permute-start(bf16[13,64,128]{2,1,0:T(8,128)(2,1)S(1)} %add_convert_fusion.3.refs_1_), channel_id=1, source_target_pairs={{0,2},{1,3},{2,0},{3,1},{4,6},{5,7},{6,4},{7,5},{8,10},{9,11},{10,... | collective-permute-start | bytes 638984 | tf_op jit(solution)/shard_map/ppermute | solution.py:417
  20.6 16.1 %collective-permute-start.5 = (bf16[1,64,2048]{2,1,0:T(8,128)(2,1)}, bf16[1,64,2048]{2,1,0:T(8,128)(2,1)S(1)}, u32[]{:S(2)}, u32[]{:S(2)}) collective-permute-start(bf16[1,64,2048]{2,1,0:T(8,128)(2,1)} %shard_map.133.refs_2_.refs_11_), channel_id=1, source_target_pairs={{0,4},{4,8},{8,12},{1,5},{5,9},{9,13},{2,6},{6,10},{10,14},{3,7},{... | collective-permute-start | bytes 786440 | tf_op jit(solution)/shard_map/ppermute | solution.py:525
  22.7 14.0 %collective-permute-start.6 = (bf16[1,64,2048]{2,1,0:T(8,128)(2,1)}, bf16[1,64,2048]{2,1,0:T(8,128)(2,1)}, u32[]{:S(2)}, u32[]{:S(2)}) collective-permute-start(bf16[1,64,2048]{2,1,0:T(8,128)(2,1)} %shard_map.133.refs_2_.refs_11_), channel_id=1, source_target_pairs={{12,8},{8,4},{4,0},{13,9},{9,5},{5,1},{14,10},{10,6},{6,2},{15,11}... | collective-permute-start | bytes 786440 | tf_op jit(solution)/shard_map/ppermute | solution.py:526
  29.3 11.0 %slice-start.1 = ((s8[6815744]{0:T(1024)(128)(4,1)}), s8[4194304]{0:T(1024)(128)(4,1)S(1)}, s32[]{:S(2)}) async-start(s8[6815744]{0:T(1024)(128)(4,1)} %bitcast.10), calls=%async_computation.1 | async-start | bytes 8388608
  29.3 11.1 %copy-start.14 = (bf16[2048,1024]{1,0:T(8,128)(2,1)S(1)}, bf16[2048,1024]{1,0:T(8,128)(2,1)}, u32[]{:S(2)}) copy-start(bf16[2048,1024]{1,0:T(8,128)(2,1)} %refs_5_.5) | copy-start | bytes 12582916
  31.7 26.2 %collective-permute-start.10 = (bf16[4,64,2048]{2,1,0:T(8,128)(2,1)}, bf16[4,64,2048]{2,1,0:T(8,128)(2,1)}, u32[]{:S(2)}, u32[]{:S(2)}) collective-permute-start(bf16[4,64,2048]{2,1,0:T(8,128)(2,1)} %shard_map.132.refs_5_.refs_6_.refs_0_), channel_id=1, source_target_pairs={{0,4},{12,8},{1,5},{13,9},{2,6},{14,10},{3,7},{15,11},{16,20},{28,... | collective-permute-start | bytes 3145736 | tf_op jit(solution)/shard_map/ppermute | solution.py:524
  38.4 13.1 %collective-permute-start.8 = (bf16[1,64,2048]{2,1,0:T(8,128)(2,1)S(1)}, bf16[1,64,2048]{2,1,0:T(8,128)(2,1)S(1)}, u32[]{:S(2)}, u32[]{:S(2)}) collective-permute-start(bf16[1,64,2048]{2,1,0:T(8,128)(2,1)S(1)} %get-tuple-element.28.refs_7_), channel_id=1, source_target_pairs={{4,8},{8,4},{5,9},{9,5},{6,10},{10,6},{7,11},{11,7},{20,24},{24,20... | collective-permute-start | bytes 786440 | tf_op jit(solution)/shard_map/ppermute | solution.py:529
  39.0 12.7 %collective-permute-start.9 = (bf16[1,64,2048]{2,1,0:T(8,128)(2,1)S(1)}, bf16[1,64,2048]{2,1,0:T(8,128)(2,1)S(1)}, u32[]{:S(2)}, u32[]{:S(2)}) collective-permute-start(bf16[1,64,2048]{2,1,0:T(8,128)(2,1)S(1)} %get-tuple-element.32), channel_id=1, source_target_pairs={{4,12},{8,0},{5,13},{9,1},{6,14},{10,2},{7,15},{11,3},{20,28},{24,... | collective-permute-start | bytes 786440 | tf_op jit(solution)/shard_map/ppermute | solution.py:530
  50.9 42.0 %collective-permute-start.7 = (bf16[1664,256]{1,0:T(8,128)(2,1)}, bf16[1664,256]{1,0:T(8,128)(2,1)}, u32[]{:S(2)}, u32[]{:S(2)}) collective-permute-start(bf16[1664,256]{1,0:T(8,128)(2,1)} %get-tuple-element.30), channel_id=1, source_target_pairs={{0,1},{1,0},{2,3},{3,2},{4,5},{5,4},{6,7},{7,6},{8,9},{9,8},{10,11... | collective-permute-start | bytes 2555912 | tf_op jit(solution)/shard_map/ppermute | solution.py:417
  50.9 17.2 %collective-permute-start.11 = (bf16[1664,256]{1,0:T(8,128)(2,1)}, bf16[1664,256]{1,0:T(8,128)(2,1)}, u32[]{:S(2)}, u32[]{:S(2)}) collective-permute-start(bf16[1664,256]{1,0:T(8,128)(2,1)} %get-tuple-element.33.refs_8_), channel_id=1, source_target_pairs={{0,1},{1,0},{2,3},{3,2},{4,5},{5,4},{6,7},{7,6},{8,9},{9,8},{10,11... | collective-permute-start | bytes 2555912 | tf_op jit(solution)/shard_map/ppermute | solution.py:417
  58.3 27.5 %collective-permute-start.19 = (bf16[4,64,2048]{2,1,0:T(8,128)(2,1)S(1)}, bf16[4,64,2048]{2,1,0:T(8,128)(2,1)S(1)}, u32[]{:S(2)}, u32[]{:S(2)}) collective-permute-start(bf16[4,64,2048]{2,1,0:T(8,128)(2,1)S(1)} %add_convert_fusion.1.refs_16_), channel_id=1, source_target_pairs={{0,4},{12,8},{4,12},{8,0},{1,5},{13,9},{5,13},{9,1},{2,6},{14,10},... | collective-permute-start | bytes 3145736 | tf_op jit(solution)/shard_map/ppermute | solution.py:534
  67.4 4.3 %collective-permute-start.13 = (bf16[13,64,128]{2,1,0:T(8,128)(2,1)S(1)}, bf16[13,64,128]{2,1,0:T(8,128)(2,1)S(1)}, u32[]{:S(2)}, u32[]{:S(2)}) collective-permute-start(bf16[13,64,128]{2,1,0:T(8,128)(2,1)S(1)} %shard_map.137.refs_1_.refs_5_), channel_id=1, source_target_pairs={{0,1},{1,0},{2,3},{3,2},{4,5},{5,4},{6,7},{7,6},{8,9},{9,8},{10,11... | collective-permute-start | bytes 638984 | tf_op jit(solution)/shard_map/ppermute | solution.py:417
  67.5 8.1 %collective-permute-start.14 = (bf16[13,64,128]{2,1,0:T(8,128)(2,1)S(1)}, bf16[13,64,128]{2,1,0:T(8,128)(2,1)S(1)}, u32[]{:S(2)}, u32[]{:S(2)}) collective-permute-start(bf16[13,64,128]{2,1,0:T(8,128)(2,1)S(1)} %shard_map.137.refs_1_.refs_5_), channel_id=1, source_target_pairs={{0,2},{1,3},{2,0},{3,1},{4,6},{5,7},{6,4},{7,5},{8,10},{9,11},{10,... | collective-permute-start | bytes 638984 | tf_op jit(solution)/shard_map/ppermute | solution.py:417
  68.1 11.2 %collective-permute-start.15 = (bf16[13,64,128]{2,1,0:T(8,128)(2,1)S(1)}, bf16[13,64,128]{2,1,0:T(8,128)(2,1)S(1)}, u32[]{:S(2)}, u32[]{:S(2)}) collective-permute-start(bf16[13,64,128]{2,1,0:T(8,128)(2,1)S(1)} %shard_map.137.refs_1_.refs_5_), channel_id=1, source_target_pairs={{0,3},{1,2},{2,1},{3,0},{4,7},{5,6},{6,5},{7,4},{8,11},{9,10},{10,... | collective-permute-start | bytes 638984 | tf_op jit(solution)/shard_map/ppermute | solution.py:417
  71.6 16.2 %copy-start.8 = (bf16[13,64,128]{2,1,0:T(8,128)(2,1)}, bf16[13,64,128]{2,1,0:T(8,128)(2,1)S(1)}, u32[]{:S(2)}) copy-start(bf16[13,64,128]{2,1,0:T(8,128)(2,1)S(1)} %collective-permute-done.13.refs_6_.refs_1_) | copy-start | bytes 638980
  71.6 26.3 %collective-permute-start.12 = (bf16[1664,256]{1,0:T(8,128)(2,1)}, bf16[1664,256]{1,0:T(8,128)(2,1)S(1)}, u32[]{:S(2)}, u32[]{:S(2)}) collective-permute-start(bf16[1664,256]{1,0:T(8,128)(2,1)} %add_convert_fusion.2), channel_id=1, source_target_pairs={{0,2},{1,3},{2,0},{3,1},{4,6},{5,7},{6,4},{7,5},{8,10},{9,11},{10,... | collective-permute-start | bytes 2555912 | tf_op jit(solution)/shard_map/ppermute | solution.py:417
  75.6 12.3 %copy-start.9 = (bf16[13,64,128]{2,1,0:T(8,128)(2,1)}, bf16[13,64,128]{2,1,0:T(8,128)(2,1)S(1)}, u32[]{:S(2)}) copy-start(bf16[13,64,128]{2,1,0:T(8,128)(2,1)S(1)} %collective-permute-done.14.refs_7_.refs_2_) | copy-start | bytes 638980
  87.9 29.4 %collective-permute-start.21 = (bf16[4,64,2048]{2,1,0:T(8,128)(2,1)}, bf16[4,64,2048]{2,1,0:T(8,128)(2,1)S(1)}, u32[]{:S(2)}, u32[]{:S(2)}) collective-permute-start(bf16[4,64,2048]{2,1,0:T(8,128)(2,1)} %shard_map.142), channel_id=1, source_target_pairs={{0,4},{12,8},{4,0},{8,12},{1,5},{13,9},{5,1},{9,13},{2,6},{14,10},... | collective-permute-start | bytes 3145736 | tf_op jit(solution)/shard_map/ppermute | solution.py:539
  90.0 27.3 %collective-permute-start.20 = (bf16[4,64,2048]{2,1,0:T(8,128)(2,1)S(1)}, bf16[4,64,2048]{2,1,0:T(8,128)(2,1)}, u32[]{:S(2)}, u32[]{:S(2)}) collective-permute-start(bf16[4,64,2048]{2,1,0:T(8,128)(2,1)S(1)} %fusion.refs_1_), channel_id=1, source_target_pairs={{4,8},{8,4},{5,9},{9,5},{6,10},{10,6},{7,11},{11,7},{20,24},{24,20... | collective-permute-start | bytes 3145736 | tf_op jit(solution)/shard_map/ppermute | solution.py:538
  103.9 15.8 %collective-permute-start.16 = (bf16[384,256]{1,0:T(8,128)(2,1)}, bf16[384,256]{1,0:T(8,128)(2,1)S(1)}, u32[]{:S(2)}, u32[]{:S(2)}) collective-permute-start(bf16[384,256]{1,0:T(8,128)(2,1)} %get-tuple-element.37), channel_id=1, source_target_pairs={{0,4},{4,8},{8,12},{12,0},{1,5},{5,9},{9,13},{13,1},{2,6},{6,10},{... | collective-permute-start | bytes 589832 | tf_op jit(solution)/shard_map/ppermute | solution.py:399
  104.0 26.1 %collective-permute-start.17 = (bf16[384,256]{1,0:T(8,128)(2,1)}, bf16[384,256]{1,0:T(8,128)(2,1)S(1)}, u32[]{:S(2)}, u32[]{:S(2)}) collective-permute-start(bf16[384,256]{1,0:T(8,128)(2,1)} %get-tuple-element.38), channel_id=1, source_target_pairs={{0,8},{4,12},{8,0},{12,4},{1,9},{5,13},{9,1},{13,5},{2,10},{6,14},... | collective-permute-start | bytes 589832 | tf_op jit(solution)/shard_map/ppermute | solution.py:399
  107.0 23.1 %collective-permute-start.18 = (bf16[384,256]{1,0:T(8,128)(2,1)}, bf16[384,256]{1,0:T(8,128)(2,1)S(1)}, u32[]{:S(2)}, u32[]{:S(2)}) collective-permute-start(bf16[384,256]{1,0:T(8,128)(2,1)} %get-tuple-element.39), channel_id=1, source_target_pairs={{0,12},{4,0},{8,4},{12,8},{1,13},{5,1},{9,5},{13,9},{2,14},{6,2},{... | collective-permute-start | bytes 589832 | tf_op jit(solution)/shard_map/ppermute | solution.py:399
  108.3 21.8 %copy-start.15 = (bf16[384,256]{1,0:T(8,128)(2,1)S(1)}, bf16[384,256]{1,0:T(8,128)(2,1)}, u32[]{:S(2)}) copy-start(bf16[384,256]{1,0:T(8,128)(2,1)} %get-tuple-element.36.refs_1_) | copy-start | bytes 589828
  119.0 11.8 %copy-start.5 = (bf16[4,64,2048]{2,1,0:T(8,128)(2,1)}, bf16[4,64,2048]{2,1,0:T(8,128)(2,1)S(1)}, u32[]{:S(2)}) copy-start(bf16[4,64,2048]{2,1,0:T(8,128)(2,1)S(1)} %add_convert_fusion.refs_6_) | copy-start | bytes 3145732
  (18 other events, 82.3 us)

commit v14 on v13

--- a/solution.py
+++ b/solution.py
@@ -278,32 +278,15 @@
     )
 
 
-def outputs_of(lengths, codes, parts, base, ranks, features, maps, last_map):
-    rows, width = base[0].shape
-    blocks = rows // BLOCK
-    rank = maps.shape[1]
-
-    def kernel(lengths_ref, codes_ref, one, two, three, *refs):
-        terms, refs = refs[: len(ranks)], refs[len(ranks) :]
-        rows_ref, maps_ref, last_ref, out_ref, *outs = refs
-        late = summed(terms, blocks - 1)
-        for k in range(blocks):
-            at = slice(k * BLOCK, (k + 1) * BLOCK)
-            adapter = maps_ref[k] if k < blocks - 1 else last_ref[0]
-            added = lax.dot_general(
-                summed(terms, k) if k < blocks - 1 else late,
-                adapter,
-                (((0,), (0,)), ((), ())),
-                preferred_element_type=jnp.float32,
-            )
-            frozen = one[at].astype(jnp.float32) + two[at].astype(jnp.float32) + three[at].astype(jnp.float32)
-            live = lax.broadcasted_iota(jnp.int32, frozen.shape, 0) < lengths_ref[k]
-            values = jnp.where(live, frozen + ADAPTER_SCALE * added, 0.0).astype(out_ref.dtype)
-            out_ref[at] = values
-            if k == blocks - 1:
-                for count, out in zip(parts, outs):
-                    out[count * rank :] = values
-        late_rows = jnp.dot(late, rows_ref[(blocks - 1) * BLOCK :], preferred_element_type=jnp.float32)
+def up_rows(codes, parts, ranks, features):
+    blocks, rank, _ = ranks[0].shape
+    width = features.shape[1]
+
+    def kernel(codes_ref, *refs):
+        terms, rows_ref, outs = refs[: len(ranks)], refs[len(ranks)], refs[len(ranks) + 1 :]
+        late = jnp.dot(
+            summed(terms, blocks - 1), rows_ref[(blocks - 1) * BLOCK :], preferred_element_type=jnp.float32
+        )
         done = 0
         for count, out in zip(parts, outs):
 
@@ -314,10 +297,8 @@
                 mine = jnp.where(code > 1, mine, jnp.zeros_like(mine))
                 mine_rows = rows_ref[pl.ds(pl.multiple_of(at * BLOCK, BLOCK), BLOCK), :]
                 total = jnp.dot(mine, mine_rows, preferred_element_type=jnp.float32)
-                total = total + jnp.where((code & 1) > 0, late_rows, 0.0)
-                to = r * rank if isinstance(r, int) else pl.ds(pl.multiple_of(r * rank, rank), rank)
-                to = slice(to, to + rank) if isinstance(r, int) else to
-                out[to] = (ADAPTER_SCALE * total).astype(out.dtype)
+                total = total + jnp.where((code & 1) > 0, late, 0.0)
+                out[r] = (ADAPTER_SCALE * total).astype(out.dtype)
                 return carry
 
             if count <= OWN:
@@ -329,44 +310,71 @@
 
     return call(
         kernel,
-        (lengths, codes),
+        (codes,),
         (1,),
-        [whole(array) for array in (*base, *ranks, features, maps, last_map)],
-        [((rows, width), maps.dtype, constant_spec((rows, width)))]
-        + [
-            ((count * rank + BLOCK, width), maps.dtype, constant_spec((count * rank + BLOCK, width)))
-            for count in parts
+        [whole(array) for array in (*ranks, features)],
+        [((count, rank, width), features.dtype, constant_spec((count, rank, width))) for count in parts],
+    )
+
+
+def values_of(lengths, base, ranks, maps, last_map, tokens=()):
+    rows, width = base[0].shape
+    blocks = rows // BLOCK
+
+    def kernel(lengths_ref, one, two, three, *refs):
+        terms, (maps_ref, last_ref, out_ref, last_out) = refs[: len(ranks)], refs[len(ranks) :]
+        for k in range(blocks):
+            at = slice(k * BLOCK, (k + 1) * BLOCK)
+            adapter = maps_ref[k] if k < blocks - 1 else last_ref[0]
+            added = lax.dot_general(
+                summed(terms, k), adapter, (((0,), (0,)), ((), ())), preferred_element_type=jnp.float32
+            )
+            frozen = one[at].astype(jnp.float32) + two[at].astype(jnp.float32) + three[at].astype(jnp.float32)
+            live = lax.broadcasted_iota(jnp.int32, frozen.shape, 0) < lengths_ref[k]
+            values = jnp.where(live, frozen + ADAPTER_SCALE * added, 0.0).astype(out_ref.dtype)
+            out_ref[at] = values
+            if k == blocks - 1:
+                last_out[...] = values
+
+    return call(
+        kernel,
+        (lengths,),
+        (1,),
+        [whole(array) for array in (*base, *ranks, maps, last_map)],
+        [
+            ((rows, width), maps.dtype, constant_spec((rows, width))),
+            ((BLOCK, width), maps.dtype, constant_spec((BLOCK, width))),
         ],
+        tokens,
+        100.0,
         vmem=60,
     )
 
 
-def finish(pick, values, own, arrived, tokens):
+def put_last(partner, me, values, choices, tokens):
     width = values.shape[1]
     block = values.shape[0] // BLOCK - 1
-    rows = own.shape[0] - BLOCK
-
-    def kernel(pick_ref, *refs):
-        choices, table_ref, last_ref = refs[:-3], refs[-2], refs[-1]
-        table_ref[...] = sum(choice[:rows].astype(jnp.float32) for choice in choices).astype(own.dtype)
-        for k, choice in enumerate(choices):
-
-            @pl.when(pick_ref[0] == k)
+    size = partner.shape[0]
+
+    def kernel(partner_ref, me_ref, *refs):
+        for k, choice in enumerate(refs[:-2]):
+            if len(choices) == 1:
+                refs[-1][...] = choice[...]
+                continue
+
+            @pl.when(partner_ref[me_ref[0]] == lax.rem(me_ref[0] + (size - k), size))
             def _():
-                last_ref[...] = choice[rows:]
-
-    return call(
-        kernel,
-        (pick,),
+                refs[-1][...] = choice[...]
+
+    return call(
+        kernel,
+        (partner, me.reshape(1)),
         (1,),
-        [whole(choice) for choice in (own, *arrived)] + [(values, ANYWHERE)],
-        [
-            ((rows, width), own.dtype, constant_spec((rows, width))),
-            (values.shape, values.dtype, pl.BlockSpec((BLOCK, width), lambda i, *_: (block, 0))),
-        ],
+        [whole(choice) for choice in choices] + [(values, ANYWHERE)],
+        [(values.shape, values.dtype, pl.BlockSpec((BLOCK, width), lambda i, *_: (block, 0)))],
         tokens,
-        aliases={2 + len(arrived): 1},
-    )
+        aliases={2 + len(choices): 0},
+    )[0]
 
 
 def base_terms(columns, hidden, weight, tokens=()):
@@ -512,11 +520,6 @@
             streamed_ranks(lengths, partner, me, adapter_down_rows, down_choices, hidden, 4, tokens, 100.0)
         )
 
-    def outputs(codes, parts, base_sums, rank_in):
-        return outputs_of(
-            lengths, codes, parts, base_sums, rank_in, cotangent, adapter_up_matrix, up_last
-        )
-
     if line:
         inner = (me == 1) | (me == 2)
         codes = codes_of(jnp.array(ROLES, jnp.int32)[me])
@@ -534,30 +537,35 @@
         from_second = lax.ppermute(second, "dp", [(0, 1), (3, 2), (1, 3), (2, 0)])
         rank_in = inputs(down_choices, second)
         base_sums, _ = base_parts(terms, rank_in[0])
-        middle = add(after(first, *rank_in[1:]), from_second)
+        up_codes = codes_of((me + jnp.array([1, 2, 3, 0], jnp.int32)) % devices)
+        *sent, up_kept = up_rows(up_codes, [OWN] * 4, rank_in, cotangent)
+        arrived = [shift(array, by + 1) for by, array in enumerate(sent)]
+        middle = add(after(first, up_kept), from_second)
         from_inner = lax.ppermute(middle, "dp", [(1, 2), (2, 1)])
+        up_out = add(after(up_kept, middle), *arrived)
         from_third = lax.ppermute(after(third, middle), "dp", [(0, 1), (3, 2), (1, 0), (2, 3)])
         near_total = lax.optimization_barrier(
             after(own, middle).astype(jnp.float32) + jnp.where(inner, 0.0, from_second.astype(jnp.float32))
         )
         down_out = (near_total + from_inner.astype(jnp.float32) + from_third.astype(jnp.float32)).astype(own.dtype)
 
-        up_codes = codes_of((me + jnp.array([1, 2, 3, 0], jnp.int32)) % devices)
-        values, *sent, kept_here = outputs(up_codes, [OWN] * 4, base_sums, rank_in)
-        arrived = [shift(array, by + 1) for by, array in enumerate(sent)]
-        value_pick = ((me - partner[me]) % devices).reshape(1)
-        up_out, values = finish(value_pick, values, kept_here, arrived, [down_out])
+        values, last_values = values_of(lengths, base_sums, rank_in, adapter_up_matrix, up_last, [up_out])
+        tokens = [down_out]
     else:
         codes = codes_of(order)
         (table,) = down_rows(codes, 0, devices, 0, rank_cot, hidden)
         down_choices, _ = shifted(down_own, holder)
         down_out = line_reduce_scatter(table.reshape(devices, OWN, *table.shape[1:]))
-        values, table = outputs(codes, [devices * OWN], base_parts(base(table))[0], inputs(down_choices, table))
-        up_table, last_values = table[:-BLOCK], table[-BLOCK:]
-        up_out = line_reduce_scatter(up_table.reshape(devices, OWN, -1, values.shape[1]))
-        (last_values,), _ = shifted(last_values, partner[me])
-        values = jnp.concatenate([values[: kept * BLOCK], last_values], axis=0)
-    return (values, down_out, up_out.reshape(OWN, -1, values.shape[1]))
+        rank_in = inputs(down_choices, table)
+        values, last_values = values_of(
+            lengths, base_parts(base(table))[0], rank_in, adapter_up_matrix, up_last
+        )
+        (up_table,) = up_rows(codes, [devices * OWN], rank_in, cotangent)
+        up_out = line_reduce_scatter(up_table.reshape(devices, OWN, *up_table.shape[1:]))
+        tokens = []
+    value_choices, _ = shifted(last_values, partner[me])
+    values = put_last(partner, me, values, value_choices, tokens)
+    return (values, down_out, up_out)
 
 
 def solution(mesh):

time: 132 us -> 128 us (0.970)
  waiting for transfers between devices: 42.3 us -> 39.4 us
  local copies, waits for them, and re-layouts: 9.62 us -> 8.15 us
    ppermute x1, waiting for transfers between devices: 8.92 us -> 14.4 us  [body(): lax.ppermute(after(third, middle), 'dp', [(0, 1), (3, 2), (1, 0), (2, 3)])]
    ppermute x6 -> x9, starting transfers between devices: 11 us -> 15 us  [shift(): lax.ppermute(array, 'dp', [(i, (i + by) % size) for i in range(size)])]
    ppermute x8, waiting for transfers between devices: 14.1 us -> 10.5 us  [crossed(): lax.ppermute(array, 'tensor', [(i, i ^ by) for i in range(lax.axis_size('...]
    ppermute x6 -> x9, waiting for transfers between devices: 11.8 us -> 8.19 us  [shift(): lax.ppermute(array, 'dp', [(i, (i + by) % size) for i in range(size)])]
    ppermute x1, starting transfers between devices: 2.12 us -> 0.01 us  [body(): lax.ppermute(after(third, middle), 'dp', [(0, 1), (3, 2), (1, 0), (2, 3)])]
    ppermute x1, waiting for transfers between devices: 6.58 us -> 4.48 us  [body(): from_second = lax.ppermute(second, 'dp', [(0, 1), (3, 2), (1, 3), (2, 0)])]
    unnamed x56 -> x58, local copies, waits for them, and re-layouts: 8.88 us -> 7.99 us
    pallas_call x14 -> x16, Pallas kernels: 32.5 us -> 33.2 us  [call(): pl.pallas_call(run, grid_spec=pltpu.PrefetchScalarGridSpec(num_scalar_pre...]
  transfers between devices with their start and end apart: 22 -> 25, of which waited for: 12 -> 10; matrix products, arithmetic and copies ran while one was open for 9% -> 8% of each run, Pallas kernels for 21% -> 22%
where the time goes in v14:
time: 128 us; the launch traced here: 127 us
  waiting for transfers between devices  39.4 us (31%)
  starting transfers between devices  34.9 us (27%)
  Pallas kernels  33.2 us (26%)
  other arithmetic  10 us (8%)
  local copies, waits for them, and re-layouts  8.15 us (6%)
    pallas_call x16, Pallas kernels, call(): pl.pallas_call(run, grid_spec=pltpu.PrefetchScalarGridSpec(num_scalar_pre...  33.2 us
    ppermute x9, starting transfers between devices, shift(): lax.ppermute(array, 'dp', [(i, (i + by) % size) for i in range(size)])  15 us
    ppermute x1, waiting for transfers between devices, body(): lax.ppermute(after(third, middle), 'dp', [(0, 1), (3, 2), (1, 0), (2, 3)])  14.4 us
    ppermute x8, waiting for transfers between devices, crossed(): lax.ppermute(array, 'tensor', [(i, i ^ by) for i in range(lax.axis_size('...  10.5 us
    ppermute x9, waiting for transfers between devices, shift(): lax.ppermute(array, 'dp', [(i, (i + by) % size) for i in range(size)])  8.19 us
    unnamed x58, local copies, waits for them, and re-layouts  7.99 us
    ppermute x8, starting transfers between devices, crossed(): lax.ppermute(array, 'tensor', [(i, i ^ by) for i in range(lax.axis_size('...  4.64 us
    ppermute x1, waiting for transfers between devices, body(): from_second = lax.ppermute(second, 'dp', [(0, 1), (3, 2), (1, 3), (2, 0)])  4.48 us
  transfers between devices with their start and end apart: 25, of which 10 were waited for; matrix products, arithmetic and copies ran while one was open for 8% of the time, Pallas kernels for 22%

profile of v14, /device:TPU:0, one launch (start us, length us, event | category | flops | bytes accessed | tf_op | source)
XLA Modules:
  0.0 126.7 jit_solution(3009903317083568923)
XLA Ops:
  0.7 3.2 %shard_map.130 = (bf16[13,64,128]{2,1,0:T(8,128)(2,1)}, bf16[1,64,256]{2,1,0:T(8,128)(2,1)}, bf16[1,64,2048]{2,1,0:T(8,128)(2,1)}) custom-call(s32[13]{0:T(128)} %refs_0_.10, bf16[13,64,256]{2,1,0:T(8,128)(2,1)} %refs_8_.3, bf16[1664,256]{1,0:T(8,128)(2,1)} %refs_5_.9, bf16[13,64,2048]{2,1,0:T(8,128)(2,1)} %refs_6_.5), custom_call_target="tpu_custom_call" | custom-call | flops 1000000000 | bytes 360000 | tf_op jit(solution)/shard_map/pallas_call | solution.py:24
  3.9 3.0 %collective-permute-start = (bf16[1,64,256]{2,1,0:T(8,128)(2,1)}, bf16[1,64,256]{2,1,0:T(8,128)(2,1)S(1)}, u32[]{:S(2)}, u32[]{:S(2)}) collective-permute-start(bf16[1,64,256]{2,1,0:T(8,128)(2,1)} %get-tuple-element.23.refs_3_), channel_id=1, source_target_pairs={{0,4},{4,8},{8,12},{12,0},{1,5},{5,9},{9,13},{13,1},{2,6},{6,10},{... | collective-permute-start | bytes 98312 | tf_op jit(solution)/shard_map/ppermute | solution.py:407
  6.9 2.6 %collective-permute-start.1 = (bf16[1,64,256]{2,1,0:T(8,128)(2,1)}, bf16[1,64,256]{2,1,0:T(8,128)(2,1)S(1)}, u32[]{:S(2)}, u32[]{:S(2)}) collective-permute-start(bf16[1,64,256]{2,1,0:T(8,128)(2,1)} %get-tuple-element.23.refs_3_), channel_id=1, source_target_pairs={{0,8},{4,12},{8,0},{12,4},{1,9},{5,13},{9,1},{13,5},{2,10},{6,14},... | collective-permute-start | bytes 98312 | tf_op jit(solution)/shard_map/ppermute | solution.py:407
  9.5 1.3 %collective-permute-start.2 = (bf16[1,64,256]{2,1,0:T(8,128)(2,1)}, bf16[1,64,256]{2,1,0:T(8,128)(2,1)S(1)}, u32[]{:S(2)}, u32[]{:S(2)}) collective-permute-start(bf16[1,64,256]{2,1,0:T(8,128)(2,1)} %get-tuple-element.23.refs_3_), channel_id=1, source_target_pairs={{0,12},{4,0},{8,4},{12,8},{1,13},{5,1},{9,5},{13,9},{2,14},{6,2},{... | collective-permute-start | bytes 98312 | tf_op jit(solution)/shard_map/ppermute | solution.py:407
  17.6 1.4 %collective-permute-done.3 = bf16[13,64,128]{2,1,0:T(8,128)(2,1)S(1)} collective-permute-done((bf16[13,64,128]{2,1,0:T(8,128)(2,1)S(1)}, bf16[13,64,128]{2,1,0:T(8,128)(2,1)S(1)}, u32[]{:S(2)}, u32[]{:S(2)}) %collective-permute-start.3) | collective-permute-done | bytes 213024 | tf_op jit(solution)/shard_map/ppermute | solution.py:425
  19.0 1.6 %collective-permute-start.4 = (bf16[13,64,128]{2,1,0:T(8,128)(2,1)S(1)}, bf16[13,64,128]{2,1,0:T(8,128)(2,1)S(1)}, u32[]{:S(2)}, u32[]{:S(2)}) collective-permute-start(bf16[13,64,128]{2,1,0:T(8,128)(2,1)S(1)} %add_convert_fusion.3.refs_1_), channel_id=1, source_target_pairs={{0,2},{1,3},{2,0},{3,1},{4,6},{5,7},{6,4},{7,5},{8,10},{9,11},{10,... | collective-permute-start | bytes 638984 | tf_op jit(solution)/shard_map/ppermute | solution.py:425
  20.6 2.1 %collective-permute-start.5 = (bf16[1,64,2048]{2,1,0:T(8,128)(2,1)}, bf16[1,64,2048]{2,1,0:T(8,128)(2,1)S(1)}, u32[]{:S(2)}, u32[]{:S(2)}) collective-permute-start(bf16[1,64,2048]{2,1,0:T(8,128)(2,1)} %shard_map.133.refs_2_.refs_11_), channel_id=1, source_target_pairs={{0,4},{4,8},{8,12},{1,5},{5,9},{9,13},{2,6},{6,10},{10,14},{3,7},{... | collective-permute-start | bytes 786440 | tf_op jit(solution)/shard_map/ppermute | solution.py:528
  22.7 1.3 %collective-permute-start.6 = (bf16[1,64,2048]{2,1,0:T(8,128)(2,1)}, bf16[1,64,2048]{2,1,0:T(8,128)(2,1)}, u32[]{:S(2)}, u32[]{:S(2)}) collective-permute-start(bf16[1,64,2048]{2,1,0:T(8,128)(2,1)} %shard_map.133.refs_2_.refs_11_), channel_id=1, source_target_pairs={{12,8},{8,4},{4,0},{13,9},{9,5},{5,1},{14,10},{10,6},{6,2},{15,11}... | collective-permute-start | bytes 786440 | tf_op jit(solution)/shard_map/ppermute | solution.py:529
  25.1 1.2 collective-permute-done.4.refs_2_
  26.4 2.9 %copy-done = bf16[1664,2048]{1,0:T(8,128)(2,1)S(1)} copy-done((bf16[1664,2048]{1,0:T(8,128)(2,1)S(1)}, bf16[1664,2048]{1,0:T(8,128)(2,1)}, u32[]{:S(2)}) %copy-start) | copy-done | bytes 6815768
  29.3 2.4 %shard_map.132.refs_5_.refs_6_.refs_0_ = bf16[4,64,2048]{2,1,0:T(8,128)(2,1)} custom-call(s32[16]{0:T(128)S(1)} %get-tuple-element.44.refs_0_, bf16[13,64,128]{2,1,0:T(8,128)(2,1)S(1)} %add_convert_fusion.3.refs_1_, bf16[13,64,128]{2,1,0:T(8,128)(2,1)S(1)} %collective-permute-done.4.refs_2_, bf16[1664,2048]{1,0:T(8,128)(2,1)S(1)} %copy-done, ...), custom_call_target="tpu_custom_call" | custom-call | flops 1000000000 | bytes 360000 | tf_op jit(solution)/shard_map/pallas_call | solution.py:24
  31.7 4.4 %collective-permute-start.10 = (bf16[4,64,2048]{2,1,0:T(8,128)(2,1)}, bf16[4,64,2048]{2,1,0:T(8,128)(2,1)}, u32[]{:S(2)}, u32[]{:S(2)}) collective-permute-start(bf16[4,64,2048]{2,1,0:T(8,128)(2,1)} %shard_map.132.refs_5_.refs_6_.refs_0_), channel_id=1, source_target_pairs={{0,4},{12,8},{1,5},{13,9},{2,6},{14,10},{3,7},{15,11},{16,20},{28,... | collective-permute-start | bytes 3145736 | tf_op jit(solution)/shard_map/ppermute | solution.py:527
  36.1 1.6 %shard_map.134 = (bf16[1,64,2048]{2,1,0:T(8,128)(2,1)S(1)}, bf16[1,64,2048]{2,1,0:T(8,128)(2,1)S(1)}) custom-call(s32[4]{0:T(128)S(1)} %copy-done.18, s32[1]{0:T(128)} %bitcast.refs_2_.refs_1_, bf16[1,64,2048]{2,1,0:T(8,128)(2,1)} %shard_map.133.refs_2_.refs_11_, bf16[1,64,2048]{2,1,0:T(8,128)(2,1)S(1)} %collective-permute-done.5.refs_3_.refs_12_, ...), custom_call_target="tpu_custom_call" | custom-call | flops 1000000000 | bytes 360000 | tf_op jit(solution)/shard_map/pallas_call | solution.py:24
  38.4 1.3 %collective-permute-start.9 = (bf16[1,64,2048]{2,1,0:T(8,128)(2,1)S(1)}, bf16[1,64,2048]{2,1,0:T(8,128)(2,1)S(1)}, u32[]{:S(2)}, u32[]{:S(2)}) collective-permute-start(bf16[1,64,2048]{2,1,0:T(8,128)(2,1)S(1)} %get-tuple-element.31), channel_id=1, source_target_pairs={{4,12},{8,0},{5,13},{9,1},{6,14},{10,2},{7,15},{11,3},{20,28},{24,... | collective-permute-start | bytes 786440 | tf_op jit(solution)/shard_map/ppermute | solution.py:533
  39.8 9.6 %shard_map.135 = (bf16[1664,256]{1,0:T(8,128)(2,1)}, bf16[1664,256]{1,0:T(8,128)(2,1)S(1)}, bf16[1664,256]{1,0:T(8,128)(2,1)}, bf16[1664,256]{1,0:T(8,128)(2,1)S(1)}) custom-call(s32[4]{0:T(128)S(1)} %pad_add_fusion.refs_0_, bf16[1664,2048]{1,0:T(8,128)(2,1)S(1)} %bitcast.8, bf16[2048,1024]{1,0:T(8,128)(2,1)S(1)} %copy-done.10, ...), custom_call_target="tpu_custom_call" | custom-call | flops 99999997952 | bytes 36000000 | tf_op jit(solution)/shard_map/pallas_call | solution.py:24
  49.9 1.3 %collective-permute-done.9.refs_10_.refs_15_ = bf16[1,64,2048]{2,1,0:T(8,128)(2,1)S(1)} collective-permute-done((bf16[1,64,2048]{2,1,0:T(8,128)(2,1)S(1)}, bf16[1,64,2048]{2,1,0:T(8,128)(2,1)S(1)}, u32[]{:S(2)}, u32[]{:S(2)}) %collective-permute-start.9) | collective-permute-done | bytes 262176 | tf_op jit(solution)/shard_map/ppermute | solution.py:533
  51.2 4.6 %shard_map.136 = (bf16[4,64,2048]{2,1,0:T(8,128)(2,1)S(1)}, bf16[4,64,2048]{2,1,0:T(8,128)(2,1)}, bf16[4,64,2048]{2,1,0:T(8,128)(2,1)S(1)}) custom-call(s32[16]{0:T(128)S(1)} %get-tuple-element.44.refs_0_, bf16[13,64,128]{2,1,0:T(8,128)(2,1)S(1)} %add_convert_fusion.3.refs_1_, bf16[13,64,128]{2,1,0:T(8,128)(2,1)S(1)} %collective-permute-done.4.refs_2_, ...), custom_call_target="tpu_custom_call" | custom-call | flops 99999997952 | bytes 36000000 | tf_op jit(solution)/shard_map/pallas_call | solution.py:24
  57.7 3.8 %collective-permute-start.16 = (bf16[4,64,2048]{2,1,0:T(8,128)(2,1)S(1)}, bf16[4,64,2048]{2,1,0:T(8,128)(2,1)S(1)}, u32[]{:S(2)}, u32[]{:S(2)}) collective-permute-start(bf16[4,64,2048]{2,1,0:T(8,128)(2,1)S(1)} %add_convert_fusion.1.refs_16_), channel_id=1, source_target_pairs={{0,4},{12,8},{4,12},{8,0},{1,5},{13,9},{5,13},{9,1},{2,6},{14,10},... | collective-permute-start | bytes 3145736 | tf_op jit(solution)/shard_map/ppermute | solution.py:537
  61.5 4.6 %shard_map.137.refs_1_.refs_4_ = bf16[13,64,128]{2,1,0:T(8,128)(2,1)S(1)} custom-call(s32[13]{0:T(128)S(1)} %copy-done.9, s32[4]{0:T(128)S(1)} %copy-done.18, s32[1]{0:T(128)} %bitcast.refs_2_.refs_1_, bf16[13,64,2048]{2,1,0:T(8,128)(2,1)S(1)} %copy-done.3, bf16[13,64,2048]{2,1,0:T(8,128)(2,1)S(1)} %copy-done.3, bf16[13,64,2048]{2,1,0:T(8,128)(2,1)S(1)} %copy-done.3, ...), custom_call_target="tpu_custom_call" | custom-call | flops 99999997952 | bytes 36000000 | tf_op jit(solution)/shard_map/pallas_call | solution.py:24
  66.8 1.3 collective-permute-start.15
  68.0 1.4 %add_convert_fusion.2 = bf16[1664,256]{1,0:T(8,128)(2,1)S(1)} fusion(bf16[1664,256]{1,0:T(8,128)(2,1)} %collective-permute-done.11, bf16[1664,256]{1,0:T(8,128)(2,1)S(1)} %shard_map.138), kind=kLoop, calls=%fused_computation.6 | loop fusion | flops 1703936 | bytes 2555904 | tf_op jit(solution)/shard_map/convert_element_type | solution.py:421
  70.0 4.2 %collective-permute-done.14.refs_3_.refs_6_ = bf16[13,64,128]{2,1,0:T(8,128)(2,1)S(1)} collective-permute-done((bf16[13,64,128]{2,1,0:T(8,128)(2,1)S(1)}, bf16[13,64,128]{2,1,0:T(8,128)(2,1)S(1)}, u32[]{:S(2)}, u32[]{:S(2)}) %collective-permute-start.14) | collective-permute-done | bytes 213024 | tf_op jit(solution)/shard_map/ppermute | solution.py:425
  74.3 3.7 %collective-permute-done.15.refs_4_.refs_7_ = bf16[13,64,128]{2,1,0:T(8,128)(2,1)S(1)} collective-permute-done((bf16[13,64,128]{2,1,0:T(8,128)(2,1)S(1)}, bf16[13,64,128]{2,1,0:T(8,128)(2,1)S(1)}, u32[]{:S(2)}, u32[]{:S(2)}) %collective-permute-start.15) | collective-permute-done | bytes 213024 | tf_op jit(solution)/shard_map/ppermute | solution.py:425
  78.8 3.5 %collective-permute-start.19 = (bf16[4,64,256]{2,1,0:T(8,128)(2,1)S(1)}, bf16[4,64,256]{2,1,0:T(8,128)(2,1)S(1)}, u32[]{:S(2)}, u32[]{:S(2)}) collective-permute-start(bf16[4,64,256]{2,1,0:T(8,128)(2,1)S(1)} %get-tuple-element.38), channel_id=1, source_target_pairs={{0,12},{4,0},{8,4},{12,8},{1,13},{5,1},{9,5},{13,9},{2,14},{6,2},{... | collective-permute-start | bytes 393224 | tf_op jit(solution)/shard_map/ppermute | solution.py:407
  82.3 4.5 %collective-permute-done.16 = bf16[4,64,2048]{2,1,0:T(8,128)(2,1)S(1)} collective-permute-done((bf16[4,64,2048]{2,1,0:T(8,128)(2,1)S(1)}, bf16[4,64,2048]{2,1,0:T(8,128)(2,1)S(1)}, u32[]{:S(2)}, u32[]{:S(2)}) %collective-permute-start.16) | collective-permute-done | bytes 1048608 | tf_op jit(solution)/shard_map/ppermute | solution.py:537
  86.9 1.9 %fusion.refs_1_ = bf16[4,64,2048]{2,1,0:T(8,128)(2,1)S(1)} fusion(bf16[4,64,2048]{2,1,0:T(8,128)(2,1)S(1)} %collective-permute-done.16, bf16[4,64,2048]{2,1,0:T(8,128)(2,1)} %shard_map.140), kind=kLoop, calls=%fused_computation.2 | loop fusion | flops 2097152 | bytes 3145728 | tf_op jit(solution)/shard_map/convert_element_type | solution.py:421
  88.9 1.7 %collective-permute-start.23 = (bf16[4,64,2048]{2,1,0:T(8,128)(2,1)S(1)}, bf16[4,64,2048]{2,1,0:T(8,128)(2,1)}, u32[]{:S(2)}, u32[]{:S(2)}) collective-permute-start(bf16[4,64,2048]{2,1,0:T(8,128)(2,1)S(1)} %fusion.refs_1_), channel_id=1, source_target_pairs={{4,8},{8,4},{5,9},{9,5},{6,10},{10,6},{7,11},{11,7},{20,24},{24,20... | collective-permute-start | bytes 3145736 | tf_op jit(solution)/shard_map/ppermute | solution.py:544
  90.5 7.5 %collective-permute-done.18 = bf16[4,64,256]{2,1,0:T(8,128)(2,1)S(1)} collective-permute-done((bf16[4,64,256]{2,1,0:T(8,128)(2,1)S(1)}, bf16[4,64,256]{2,1,0:T(8,128)(2,1)S(1)}, u32[]{:S(2)}, u32[]{:S(2)}) %collective-permute-start.18) | collective-permute-done | bytes 131104 | tf_op jit(solution)/shard_map/ppermute | solution.py:407
  99.6 4.4 %shard_map.142 = (bf16[1664,256]{1,0:T(8,128)(2,1)}, bf16[128,256]{1,0:T(8,128)(2,1)}) custom-call(s32[13]{0:T(128)} %refs_0_.10, bf16[1664,256]{1,0:T(8,128)(2,1)} %copy-done.20, bf16[1664,256]{1,0:T(8,128)(2,1)} %collective-permute-done.7.refs_2_, bf16[1664,256]{1,0:T(8,128)(2,1)} %copy-done.23, bf16[13,64,128]{2,1,0:T(8,128)(2,1)} %copy-done.8, ...), custom_call_target="tpu_custom_call" | custom-call | flops 99999997952 | bytes 36000000 | tf_op jit(solution)/shard_map/pallas_call | solution.py:24
  104.1 2.0 %collective-permute-start.20 = (bf16[128,256]{1,0:T(8,128)(2,1)}, bf16[128,256]{1,0:T(8,128)(2,1)S(1)}, u32[]{:S(2)}, u32[]{:S(2)}) collective-permute-start(bf16[128,256]{1,0:T(8,128)(2,1)} %get-tuple-element.39.refs_2_), channel_id=1, source_target_pairs={{0,4},{4,8},{8,12},{12,0},{1,5},{5,9},{9,13},{13,1},{2,6},{6,10},{... | collective-permute-start | bytes 196616 | tf_op jit(solution)/shard_map/ppermute | solution.py:407
  108.9 14.4 %collective-permute-done.24 = bf16[4,64,2048]{2,1,0:T(8,128)(2,1)} collective-permute-done((bf16[4,64,2048]{2,1,0:T(8,128)(2,1)}, bf16[4,64,2048]{2,1,0:T(8,128)(2,1)}, u32[]{:S(2)}, u32[]{:S(2)}) %collective-permute-start.24) | collective-permute-done | bytes 1048608 | tf_op jit(solution)/shard_map/ppermute | solution.py:546
  123.3 2.1 %add_convert_fusion.refs_7_ = bf16[4,64,2048]{2,1,0:T(8,128)(2,1)S(1)} fusion(bf16[4,64,2048]{2,1,0:T(8,128)(2,1)} %collective-permute-done.24, f32[4,64,2048]{2,1,0:T(8,128)S(1)} %fusion.1, bf16[4,64,2048]{2,1,0:T(8,128)(2,1)} %collective-permute-done.23), kind=kLoop, calls=%fused_computation.4 | loop fusion | flops 2621440 | bytes 5242880 | tf_op jit(solution)/shard_map/convert_element_type | solution.py:550
  (110 shorter events, 19.0 us)
Async XLA Ops:
  0.6 13.6 %copy-start.9 = (s32[13]{0:T(128)S(1)}, s32[13]{0:T(128)}, u32[]{:S(2)}) copy-start(s32[13]{0:T(128)} %refs_0_.10) | copy-start | bytes 160
  0.7 13.6 %copy-start.5 = (bf16[1664,256]{1,0:T(8,128)(2,1)S(1)}, bf16[1664,256]{1,0:T(8,128)(2,1)}, u32[]{:S(2)}) copy-start(bf16[1664,256]{1,0:T(8,128)(2,1)} %refs_5_.9) | copy-start | bytes 2555908
  0.7 13.6 %copy-start.18 = (s32[4]{0:T(128)S(1)}, s32[4]{0:T(128)}, u32[]{:S(2)}) copy-start(s32[4]{0:T(128)} %refs_0_.11) | copy-start | bytes 52
  3.9 9.0 %collective-permute-start = (bf16[1,64,256]{2,1,0:T(8,128)(2,1)}, bf16[1,64,256]{2,1,0:T(8,128)(2,1)S(1)}, u32[]{:S(2)}, u32[]{:S(2)}) collective-permute-start(bf16[1,64,256]{2,1,0:T(8,128)(2,1)} %get-tuple-element.23.refs_3_), channel_id=1, source_target_pairs={{0,4},{4,8},{8,12},{12,0},{1,5},{5,9},{9,13},{13,1},{2,6},{6,10},{... | collective-permute-start | bytes 98312 | tf_op jit(solution)/shard_map/ppermute | solution.py:407
  6.9 6.0 %collective-permute-start.1 = (bf16[1,64,256]{2,1,0:T(8,128)(2,1)}, bf16[1,64,256]{2,1,0:T(8,128)(2,1)S(1)}, u32[]{:S(2)}, u32[]{:S(2)}) collective-permute-start(bf16[1,64,256]{2,1,0:T(8,128)(2,1)} %get-tuple-element.23.refs_3_), channel_id=1, source_target_pairs={{0,8},{4,12},{8,0},{12,4},{1,9},{5,13},{9,1},{13,5},{2,10},{6,14},... | collective-permute-start | bytes 98312 | tf_op jit(solution)/shard_map/ppermute | solution.py:407
  9.5 4.1 %collective-permute-start.2 = (bf16[1,64,256]{2,1,0:T(8,128)(2,1)}, bf16[1,64,256]{2,1,0:T(8,128)(2,1)S(1)}, u32[]{:S(2)}, u32[]{:S(2)}) collective-permute-start(bf16[1,64,256]{2,1,0:T(8,128)(2,1)} %get-tuple-element.23.refs_3_), channel_id=1, source_target_pairs={{0,12},{4,0},{8,4},{12,8},{1,13},{5,1},{9,5},{13,9},{2,14},{6,2},{... | collective-permute-start | bytes 98312 | tf_op jit(solution)/shard_map/ppermute | solution.py:407
  16.7 23.0 %slice-start = ((s8[6815744]{0:T(1024)(128)(4,1)}), s8[2621440]{0:T(1024)(128)(4,1)S(1)}, s32[]{:S(2)}) async-start(s8[6815744]{0:T(1024)(128)(4,1)} %bitcast.7), calls=%async_computation | async-start | bytes 5242880
  17.4 1.5 %collective-permute-start.3 = (bf16[13,64,128]{2,1,0:T(8,128)(2,1)S(1)}, bf16[13,64,128]{2,1,0:T(8,128)(2,1)S(1)}, u32[]{:S(2)}, u32[]{:S(2)}) collective-permute-start(bf16[13,64,128]{2,1,0:T(8,128)(2,1)S(1)} %get-tuple-element.25), channel_id=1, source_target_pairs={{0,1},{1,0},{2,3},{3,2},{4,5},{5,4},{6,7},{7,6},{8,9},{9,8},{10,11... | collective-permute-start | bytes 638984 | tf_op jit(solution)/shard_map/ppermute | solution.py:425
  19.0 7.4 %collective-permute-start.4 = (bf16[13,64,128]{2,1,0:T(8,128)(2,1)S(1)}, bf16[13,64,128]{2,1,0:T(8,128)(2,1)S(1)}, u32[]{:S(2)}, u32[]{:S(2)}) collective-permute-start(bf16[13,64,128]{2,1,0:T(8,128)(2,1)S(1)} %add_convert_fusion.3.refs_1_), channel_id=1, source_target_pairs={{0,2},{1,3},{2,0},{3,1},{4,6},{5,7},{6,4},{7,5},{8,10},{9,11},{10,... | collective-permute-start | bytes 638984 | tf_op jit(solution)/shard_map/ppermute | solution.py:425
  20.6 15.6 %collective-permute-start.5 = (bf16[1,64,2048]{2,1,0:T(8,128)(2,1)}, bf16[1,64,2048]{2,1,0:T(8,128)(2,1)S(1)}, u32[]{:S(2)}, u32[]{:S(2)}) collective-permute-start(bf16[1,64,2048]{2,1,0:T(8,128)(2,1)} %shard_map.133.refs_2_.refs_11_), channel_id=1, source_target_pairs={{0,4},{4,8},{8,12},{1,5},{5,9},{9,13},{2,6},{6,10},{10,14},{3,7},{... | collective-permute-start | bytes 786440 | tf_op jit(solution)/shard_map/ppermute | solution.py:528
  22.7 13.4 %collective-permute-start.6 = (bf16[1,64,2048]{2,1,0:T(8,128)(2,1)}, bf16[1,64,2048]{2,1,0:T(8,128)(2,1)}, u32[]{:S(2)}, u32[]{:S(2)}) collective-permute-start(bf16[1,64,2048]{2,1,0:T(8,128)(2,1)} %shard_map.133.refs_2_.refs_11_), channel_id=1, source_target_pairs={{12,8},{8,4},{4,0},{13,9},{9,5},{5,1},{14,10},{10,6},{6,2},{15,11}... | collective-permute-start | bytes 786440 | tf_op jit(solution)/shard_map/ppermute | solution.py:529
  31.7 25.6 %collective-permute-start.10 = (bf16[4,64,2048]{2,1,0:T(8,128)(2,1)}, bf16[4,64,2048]{2,1,0:T(8,128)(2,1)}, u32[]{:S(2)}, u32[]{:S(2)}) collective-permute-start(bf16[4,64,2048]{2,1,0:T(8,128)(2,1)} %shard_map.132.refs_5_.refs_6_.refs_0_), channel_id=1, source_target_pairs={{0,4},{12,8},{1,5},{13,9},{2,6},{14,10},{3,7},{15,11},{16,20},{28,... | collective-permute-start | bytes 3145736 | tf_op jit(solution)/shard_map/ppermute | solution.py:527
  37.7 12.2 %collective-permute-start.8 = (bf16[1,64,2048]{2,1,0:T(8,128)(2,1)S(1)}, bf16[1,64,2048]{2,1,0:T(8,128)(2,1)S(1)}, u32[]{:S(2)}, u32[]{:S(2)}) collective-permute-start(bf16[1,64,2048]{2,1,0:T(8,128)(2,1)S(1)} %get-tuple-element.27.refs_7_), channel_id=1, source_target_pairs={{4,8},{8,4},{5,9},{9,5},{6,10},{10,6},{7,11},{11,7},{20,24},{24,20... | collective-permute-start | bytes 786440 | tf_op jit(solution)/shard_map/ppermute | solution.py:532
  38.4 12.8 %collective-permute-start.9 = (bf16[1,64,2048]{2,1,0:T(8,128)(2,1)S(1)}, bf16[1,64,2048]{2,1,0:T(8,128)(2,1)S(1)}, u32[]{:S(2)}, u32[]{:S(2)}) collective-permute-start(bf16[1,64,2048]{2,1,0:T(8,128)(2,1)S(1)} %get-tuple-element.31), channel_id=1, source_target_pairs={{4,12},{8,0},{5,13},{9,1},{6,14},{10,2},{7,15},{11,3},{20,28},{24,... | collective-permute-start | bytes 786440 | tf_op jit(solution)/shard_map/ppermute | solution.py:533
  49.4 49.3 %collective-permute-start.7 = (bf16[1664,256]{1,0:T(8,128)(2,1)}, bf16[1664,256]{1,0:T(8,128)(2,1)}, u32[]{:S(2)}, u32[]{:S(2)}) collective-permute-start(bf16[1664,256]{1,0:T(8,128)(2,1)} %get-tuple-element.29), channel_id=1, source_target_pairs={{0,1},{1,0},{2,3},{3,2},{4,5},{5,4},{6,7},{7,6},{8,9},{9,8},{10,11... | collective-permute-start | bytes 2555912 | tf_op jit(solution)/shard_map/ppermute | solution.py:425
  49.4 17.3 %collective-permute-start.11 = (bf16[1664,256]{1,0:T(8,128)(2,1)}, bf16[1664,256]{1,0:T(8,128)(2,1)}, u32[]{:S(2)}, u32[]{:S(2)}) collective-permute-start(bf16[1664,256]{1,0:T(8,128)(2,1)} %get-tuple-element.32.refs_8_), channel_id=1, source_target_pairs={{0,1},{1,0},{2,3},{3,2},{4,5},{5,4},{6,7},{7,6},{8,9},{9,8},{10,11... | collective-permute-start | bytes 2555912 | tf_op jit(solution)/shard_map/ppermute | solution.py:425
  57.7 29.1 %collective-permute-start.16 = (bf16[4,64,2048]{2,1,0:T(8,128)(2,1)S(1)}, bf16[4,64,2048]{2,1,0:T(8,128)(2,1)S(1)}, u32[]{:S(2)}, u32[]{:S(2)}) collective-permute-start(bf16[4,64,2048]{2,1,0:T(8,128)(2,1)S(1)} %add_convert_fusion.1.refs_16_), channel_id=1, source_target_pairs={{0,4},{12,8},{4,12},{8,0},{1,5},{13,9},{5,13},{9,1},{2,6},{14,10},... | collective-permute-start | bytes 3145736 | tf_op jit(solution)/shard_map/ppermute | solution.py:537
  66.1 11.9 %copy-start.8 = (bf16[13,64,128]{2,1,0:T(8,128)(2,1)}, bf16[13,64,128]{2,1,0:T(8,128)(2,1)S(1)}, u32[]{:S(2)}) copy-start(bf16[13,64,128]{2,1,0:T(8,128)(2,1)S(1)} %shard_map.137.refs_1_.refs_4_) | copy-start | bytes 638980
  66.1 3.4 %collective-permute-start.13 = (bf16[13,64,128]{2,1,0:T(8,128)(2,1)S(1)}, bf16[13,64,128]{2,1,0:T(8,128)(2,1)S(1)}, u32[]{:S(2)}, u32[]{:S(2)}) collective-permute-start(bf16[13,64,128]{2,1,0:T(8,128)(2,1)S(1)} %shard_map.137.refs_1_.refs_4_), channel_id=1, source_target_pairs={{0,1},{1,0},{2,3},{3,2},{4,5},{5,4},{6,7},{7,6},{8,9},{9,8},{10,11... | collective-permute-start | bytes 638984 | tf_op jit(solution)/shard_map/ppermute | solution.py:425
  66.1 8.1 %collective-permute-start.14 = (bf16[13,64,128]{2,1,0:T(8,128)(2,1)S(1)}, bf16[13,64,128]{2,1,0:T(8,128)(2,1)S(1)}, u32[]{:S(2)}, u32[]{:S(2)}) collective-permute-start(bf16[13,64,128]{2,1,0:T(8,128)(2,1)S(1)} %shard_map.137.refs_1_.refs_4_), channel_id=1, source_target_pairs={{0,2},{1,3},{2,0},{3,1},{4,6},{5,7},{6,4},{7,5},{8,10},{9,11},{10,... | collective-permute-start | bytes 638984 | tf_op jit(solution)/shard_map/ppermute | solution.py:425
  66.8 11.2 %collective-permute-start.15 = (bf16[13,64,128]{2,1,0:T(8,128)(2,1)S(1)}, bf16[13,64,128]{2,1,0:T(8,128)(2,1)S(1)}, u32[]{:S(2)}, u32[]{:S(2)}) collective-permute-start(bf16[13,64,128]{2,1,0:T(8,128)(2,1)S(1)} %shard_map.137.refs_1_.refs_4_), channel_id=1, source_target_pairs={{0,3},{1,2},{2,1},{3,0},{4,7},{5,6},{6,5},{7,4},{8,11},{9,10},{10,... | collective-permute-start | bytes 638984 | tf_op jit(solution)/shard_map/ppermute | solution.py:425
  69.4 12.9 %copy-start.11 = (bf16[13,64,128]{2,1,0:T(8,128)(2,1)}, bf16[13,64,128]{2,1,0:T(8,128)(2,1)S(1)}, u32[]{:S(2)}) copy-start(bf16[13,64,128]{2,1,0:T(8,128)(2,1)S(1)} %collective-permute-done.13.refs_2_.refs_5_) | copy-start | bytes 638980
  69.4 29.3 %collective-permute-start.12 = (bf16[1664,256]{1,0:T(8,128)(2,1)S(1)}, bf16[1664,256]{1,0:T(8,128)(2,1)S(1)}, u32[]{:S(2)}, u32[]{:S(2)}) collective-permute-start(bf16[1664,256]{1,0:T(8,128)(2,1)S(1)} %add_convert_fusion.2), channel_id=1, source_target_pairs={{0,2},{1,3},{2,0},{3,1},{4,6},{5,7},{6,4},{7,5},{8,10},{9,11},{10,... | collective-permute-start | bytes 2555912 | tf_op jit(solution)/shard_map/ppermute | solution.py:425
  78.8 10.0 %collective-permute-start.19 = (bf16[4,64,256]{2,1,0:T(8,128)(2,1)S(1)}, bf16[4,64,256]{2,1,0:T(8,128)(2,1)S(1)}, u32[]{:S(2)}, u32[]{:S(2)}) collective-permute-start(bf16[4,64,256]{2,1,0:T(8,128)(2,1)S(1)} %get-tuple-element.38), channel_id=1, source_target_pairs={{0,12},{4,0},{8,4},{12,8},{1,13},{5,1},{9,5},{13,9},{2,14},{6,2},{... | collective-permute-start | bytes 393224 | tf_op jit(solution)/shard_map/ppermute | solution.py:407
  82.3 15.7 %collective-permute-start.18 = (bf16[4,64,256]{2,1,0:T(8,128)(2,1)S(1)}, bf16[4,64,256]{2,1,0:T(8,128)(2,1)S(1)}, u32[]{:S(2)}, u32[]{:S(2)}) collective-permute-start(bf16[4,64,256]{2,1,0:T(8,128)(2,1)S(1)} %get-tuple-element.37), channel_id=1, source_target_pairs={{0,8},{4,12},{8,0},{12,4},{1,9},{5,13},{9,1},{13,5},{2,10},{6,14},... | collective-permute-start | bytes 393224 | tf_op jit(solution)/shard_map/ppermute | solution.py:407
  86.8 11.2 %collective-permute-start.17 = (bf16[4,64,256]{2,1,0:T(8,128)(2,1)S(1)}, bf16[4,64,256]{2,1,0:T(8,128)(2,1)S(1)}, u32[]{:S(2)}, u32[]{:S(2)}) collective-permute-start(bf16[4,64,256]{2,1,0:T(8,128)(2,1)S(1)} %get-tuple-element.36), channel_id=1, source_target_pairs={{0,4},{4,8},{8,12},{12,0},{1,5},{5,9},{9,13},{13,1},{2,6},{6,10},{... | collective-permute-start | bytes 393224 | tf_op jit(solution)/shard_map/ppermute | solution.py:407
  88.9 34.4 %collective-permute-start.23 = (bf16[4,64,2048]{2,1,0:T(8,128)(2,1)S(1)}, bf16[4,64,2048]{2,1,0:T(8,128)(2,1)}, u32[]{:S(2)}, u32[]{:S(2)}) collective-permute-start(bf16[4,64,2048]{2,1,0:T(8,128)(2,1)S(1)} %fusion.refs_1_), channel_id=1, source_target_pairs={{4,8},{8,4},{5,9},{9,5},{6,10},{10,6},{7,11},{11,7},{20,24},{24,20... | collective-permute-start | bytes 3145736 | tf_op jit(solution)/shard_map/ppermute | solution.py:544
  98.0 25.3 %collective-permute-start.24 = (bf16[4,64,2048]{2,1,0:T(8,128)(2,1)}, bf16[4,64,2048]{2,1,0:T(8,128)(2,1)}, u32[]{:S(2)}, u32[]{:S(2)}) collective-permute-start(bf16[4,64,2048]{2,1,0:T(8,128)(2,1)} %shard_map.144), channel_id=1, source_target_pairs={{0,4},{12,8},{4,0},{8,12},{1,5},{13,9},{5,1},{9,13},{2,6},{14,10},... | collective-permute-start | bytes 3145736 | tf_op jit(solution)/shard_map/ppermute | solution.py:546
  104.1 21.3 %collective-permute-start.20 = (bf16[128,256]{1,0:T(8,128)(2,1)}, bf16[128,256]{1,0:T(8,128)(2,1)S(1)}, u32[]{:S(2)}, u32[]{:S(2)}) collective-permute-start(bf16[128,256]{1,0:T(8,128)(2,1)} %get-tuple-element.39.refs_2_), channel_id=1, source_target_pairs={{0,4},{4,8},{8,12},{12,0},{1,5},{5,9},{9,13},{13,1},{2,6},{6,10},{... | collective-permute-start | bytes 196616 | tf_op jit(solution)/shard_map/ppermute | solution.py:407
  106.1 19.3 %collective-permute-start.21 = (bf16[128,256]{1,0:T(8,128)(2,1)}, bf16[128,256]{1,0:T(8,128)(2,1)S(1)}, u32[]{:S(2)}, u32[]{:S(2)}) collective-permute-start(bf16[128,256]{1,0:T(8,128)(2,1)} %get-tuple-element.39.refs_2_), channel_id=1, source_target_pairs={{0,8},{4,12},{8,0},{12,4},{1,9},{5,13},{9,1},{13,5},{2,10},{6,14},... | collective-permute-start | bytes 196616 | tf_op jit(solution)/shard_map/ppermute | solution.py:407
  107.3 18.1 %collective-permute-start.22 = (bf16[128,256]{1,0:T(8,128)(2,1)}, bf16[128,256]{1,0:T(8,128)(2,1)S(1)}, u32[]{:S(2)}, u32[]{:S(2)}) collective-permute-start(bf16[128,256]{1,0:T(8,128)(2,1)} %get-tuple-element.39.refs_2_), channel_id=1, source_target_pairs={{0,12},{4,0},{8,4},{12,8},{1,13},{5,1},{9,5},{13,9},{2,14},{6,2},{... | collective-permute-start | bytes 196616 | tf_op jit(solution)/shard_map/ppermute | solution.py:407
  108.9 16.5 %copy-start.14 = (bf16[128,256]{1,0:T(8,128)(2,1)S(1)}, bf16[128,256]{1,0:T(8,128)(2,1)}, u32[]{:S(2)}) copy-start(bf16[128,256]{1,0:T(8,128)(2,1)} %get-tuple-element.39.refs_2_) | copy-start | bytes 196612
  (22 other events, 119.7 us)

commit v15 on v14

--- a/solution.py
+++ b/solution.py
@@ -541,15 +541,17 @@
         *sent, up_kept = up_rows(up_codes, [OWN] * 4, rank_in, cotangent)
         arrived = [shift(array, by + 1) for by, array in enumerate(sent)]
         middle = add(after(first, up_kept), from_second)
-        from_inner = lax.ppermute(middle, "dp", [(1, 2), (2, 1)])
+        third = after(third, from_second)
+        from_inner = lax.ppermute(after(middle, third), "dp", [(1, 2), (2, 1)])
         up_out = add(after(up_kept, middle), *arrived)
-        from_third = lax.ppermute(after(third, middle), "dp", [(0, 1), (3, 2), (1, 0), (2, 3)])
+        from_third = lax.ppermute(third, "dp", [(0, 1), (3, 2), (1, 0), (2, 3)])
         near_total = lax.optimization_barrier(
             after(own, middle).astype(jnp.float32) + jnp.where(inner, 0.0, from_second.astype(jnp.float32))
         )
         down_out = (near_total + from_inner.astype(jnp.float32) + from_third.astype(jnp.float32)).astype(own.dtype)
 
-        values, last_values = values_of(lengths, base_sums, rank_in, adapter_up_matrix, up_last, [up_out])
+        values, last_values = values_of(lengths, base_sums, rank_in, adapter_up_matrix, up_last)
+        last_values = after(last_values, up_out)
         tokens = [down_out]
     else:
         codes = codes_of(order)

time: 128 us -> 131 us (1.023)
  starting transfers between devices: 34.9 us -> 37.3 us
  Pallas kernels: 33.2 us -> 34.6 us
    ppermute x8, waiting for transfers between devices: 10.5 us -> 15.4 us  [crossed(): lax.ppermute(array, 'tensor', [(i, i ^ by) for i in range(lax.axis_size('...]
    ppermute x2, waiting for transfers between devices: 14.4 us -> 9.74 us  [the longest x1 9.74 us: body(): from_third = lax.ppermute(third, 'dp', [(0, 1), (3, 2), (1, 0), (2, 3)])]
    ppermute x2, starting transfers between devices: 1.66 us -> 3.71 us  [the longest x1 2.08 us: body(): from_third = lax.ppermute(third, 'dp', [(0, 1), (3, 2), (1, 0), (2, 3)])]
    pallas_call x16 -> x18, Pallas kernels: 33.2 us -> 34.6 us  [call(): pl.pallas_call(run, grid_spec=pltpu.PrefetchScalarGridSpec(num_scalar_pre...]
  transfers between devices with their start and end apart: 25 -> 25, of which waited for: 10 -> 11; matrix products, arithmetic and copies ran while one was open for 8% -> 8% of each run, Pallas kernels for 22% -> 22%
where the time goes in v15:
time: 131 us; the launch traced here: 130 us
  waiting for transfers between devices  39 us (30%)
  starting transfers between devices  37.3 us (28%)
  Pallas kernels  34.6 us (26%)
  other arithmetic  10.3 us (8%)
  local copies, waits for them, and re-layouts  8.11 us (6%)
    pallas_call x18, Pallas kernels, call(): pl.pallas_call(run, grid_spec=pltpu.PrefetchScalarGridSpec(num_scalar_pre...  34.6 us
    ppermute x9, starting transfers between devices, shift(): lax.ppermute(array, 'dp', [(i, (i + by) % size) for i in range(size)])  15.4 us
    ppermute x8, waiting for transfers between devices, crossed(): lax.ppermute(array, 'tensor', [(i, i ^ by) for i in range(lax.axis_size('...  15.4 us
    ppermute x1, waiting for transfers between devices, body(): from_third = lax.ppermute(third, 'dp', [(0, 1), (3, 2), (1, 0), (2, 3)])  9.74 us
    unnamed x58, local copies, waits for them, and re-layouts  7.95 us
    ppermute x9, waiting for transfers between devices, shift(): lax.ppermute(array, 'dp', [(i, (i + by) % size) for i in range(size)])  7.93 us
    convert_element_type x5, other arithmetic, add(): sum((array.astype(jnp.float32) for array in arrays)).astype(arrays[0].dtype)  4.82 us
    ppermute x8, starting transfers between devices, crossed(): lax.ppermute(array, 'tensor', [(i, i ^ by) for i in range(lax.axis_size('...  4.64 us
  transfers between devices with their start and end apart: 25, of which 11 were waited for; matrix products, arithmetic and copies ran while one was open for 8% of the time, Pallas kernels for 22%

profile of v15, /device:TPU:0, one launch (start us, length us, event | category | flops | bytes accessed | tf_op | source)
XLA Modules:
  0.0 130.4 jit_solution(16496274459394970502)
XLA Ops:
  0.7 3.2 %shard_map.130 = (bf16[13,64,128]{2,1,0:T(8,128)(2,1)}, bf16[1,64,256]{2,1,0:T(8,128)(2,1)}, bf16[1,64,2048]{2,1,0:T(8,128)(2,1)}) custom-call(s32[13]{0:T(128)} %refs_0_.10, bf16[13,64,256]{2,1,0:T(8,128)(2,1)} %refs_8_.3, bf16[1664,256]{1,0:T(8,128)(2,1)} %refs_5_.9, bf16[13,64,2048]{2,1,0:T(8,128)(2,1)} %refs_6_.5), custom_call_target="tpu_custom_call" | custom-call | flops 1000000000 | bytes 360000 | tf_op jit(solution)/shard_map/pallas_call | solution.py:24
  3.9 3.0 %collective-permute-start = (bf16[1,64,256]{2,1,0:T(8,128)(2,1)}, bf16[1,64,256]{2,1,0:T(8,128)(2,1)S(1)}, u32[]{:S(2)}, u32[]{:S(2)}) collective-permute-start(bf16[1,64,256]{2,1,0:T(8,128)(2,1)} %get-tuple-element.23.refs_3_), channel_id=1, source_target_pairs={{0,4},{4,8},{8,12},{12,0},{1,5},{5,9},{9,13},{13,1},{2,6},{6,10},{... | collective-permute-start | bytes 98312 | tf_op jit(solution)/shard_map/ppermute | solution.py:407
  6.9 2.6 %collective-permute-start.1 = (bf16[1,64,256]{2,1,0:T(8,128)(2,1)}, bf16[1,64,256]{2,1,0:T(8,128)(2,1)S(1)}, u32[]{:S(2)}, u32[]{:S(2)}) collective-permute-start(bf16[1,64,256]{2,1,0:T(8,128)(2,1)} %get-tuple-element.23.refs_3_), channel_id=1, source_target_pairs={{0,8},{4,12},{8,0},{12,4},{1,9},{5,13},{9,1},{13,5},{2,10},{6,14},... | collective-permute-start | bytes 98312 | tf_op jit(solution)/shard_map/ppermute | solution.py:407
  9.5 1.3 %collective-permute-start.2 = (bf16[1,64,256]{2,1,0:T(8,128)(2,1)}, bf16[1,64,256]{2,1,0:T(8,128)(2,1)S(1)}, u32[]{:S(2)}, u32[]{:S(2)}) collective-permute-start(bf16[1,64,256]{2,1,0:T(8,128)(2,1)} %get-tuple-element.23.refs_3_), channel_id=1, source_target_pairs={{0,12},{4,0},{8,4},{12,8},{1,13},{5,1},{9,5},{13,9},{2,14},{6,2},{... | collective-permute-start | bytes 98312 | tf_op jit(solution)/shard_map/ppermute | solution.py:407
  17.6 1.4 %collective-permute-done.3 = bf16[13,64,128]{2,1,0:T(8,128)(2,1)S(1)} collective-permute-done((bf16[13,64,128]{2,1,0:T(8,128)(2,1)S(1)}, bf16[13,64,128]{2,1,0:T(8,128)(2,1)S(1)}, u32[]{:S(2)}, u32[]{:S(2)}) %collective-permute-start.3) | collective-permute-done | bytes 213024 | tf_op jit(solution)/shard_map/ppermute | solution.py:425
  19.0 1.6 %collective-permute-start.4 = (bf16[13,64,128]{2,1,0:T(8,128)(2,1)S(1)}, bf16[13,64,128]{2,1,0:T(8,128)(2,1)S(1)}, u32[]{:S(2)}, u32[]{:S(2)}) collective-permute-start(bf16[13,64,128]{2,1,0:T(8,128)(2,1)S(1)} %add_convert_fusion.3.refs_1_), channel_id=1, source_target_pairs={{0,2},{1,3},{2,0},{3,1},{4,6},{5,7},{6,4},{7,5},{8,10},{9,11},{10,... | collective-permute-start | bytes 638984 | tf_op jit(solution)/shard_map/ppermute | solution.py:425
  20.6 2.1 %collective-permute-start.5 = (bf16[1,64,2048]{2,1,0:T(8,128)(2,1)}, bf16[1,64,2048]{2,1,0:T(8,128)(2,1)S(1)}, u32[]{:S(2)}, u32[]{:S(2)}) collective-permute-start(bf16[1,64,2048]{2,1,0:T(8,128)(2,1)} %shard_map.133.refs_2_.refs_11_), channel_id=1, source_target_pairs={{0,4},{4,8},{8,12},{1,5},{5,9},{9,13},{2,6},{6,10},{10,14},{3,7},{... | collective-permute-start | bytes 786440 | tf_op jit(solution)/shard_map/ppermute | solution.py:528
  26.4 2.9 %copy-done = bf16[1664,2048]{1,0:T(8,128)(2,1)S(1)} copy-done((bf16[1664,2048]{1,0:T(8,128)(2,1)S(1)}, bf16[1664,2048]{1,0:T(8,128)(2,1)}, u32[]{:S(2)}) %copy-start) | copy-done | bytes 6815768
  29.3 2.4 %shard_map.132.refs_5_.refs_6_.refs_0_ = bf16[4,64,2048]{2,1,0:T(8,128)(2,1)} custom-call(s32[16]{0:T(128)S(1)} %get-tuple-element.44.refs_0_, bf16[13,64,128]{2,1,0:T(8,128)(2,1)S(1)} %add_convert_fusion.3.refs_1_, bf16[13,64,128]{2,1,0:T(8,128)(2,1)S(1)} %collective-permute-done.4.refs_2_, bf16[1664,2048]{1,0:T(8,128)(2,1)S(1)} %copy-done, ...), custom_call_target="tpu_custom_call" | custom-call | flops 1000000000 | bytes 360000 | tf_op jit(solution)/shard_map/pallas_call | solution.py:24
  31.7 4.4 %collective-permute-start.10 = (bf16[4,64,2048]{2,1,0:T(8,128)(2,1)}, bf16[4,64,2048]{2,1,0:T(8,128)(2,1)}, u32[]{:S(2)}, u32[]{:S(2)}) collective-permute-start(bf16[4,64,2048]{2,1,0:T(8,128)(2,1)} %shard_map.132.refs_5_.refs_6_.refs_0_), channel_id=1, source_target_pairs={{0,4},{12,8},{1,5},{13,9},{2,6},{14,10},{3,7},{15,11},{16,20},{28,... | collective-permute-start | bytes 3145736 | tf_op jit(solution)/shard_map/ppermute | solution.py:527
  36.1 1.6 %shard_map.134 = (bf16[1,64,2048]{2,1,0:T(8,128)(2,1)S(1)}, bf16[1,64,2048]{2,1,0:T(8,128)(2,1)S(1)}) custom-call(s32[4]{0:T(128)S(1)} %copy-done.20, s32[1]{0:T(128)} %bitcast.refs_2_.refs_1_, bf16[1,64,2048]{2,1,0:T(8,128)(2,1)} %shard_map.133.refs_2_.refs_11_, bf16[1,64,2048]{2,1,0:T(8,128)(2,1)S(1)} %collective-permute-done.5.refs_3_.refs_12_, ...), custom_call_target="tpu_custom_call" | custom-call | flops 1000000000 | bytes 360000 | tf_op jit(solution)/shard_map/pallas_call | solution.py:24
  39.8 9.6 %shard_map.135 = (bf16[1664,256]{1,0:T(8,128)(2,1)}, bf16[1664,256]{1,0:T(8,128)(2,1)S(1)}, bf16[1664,256]{1,0:T(8,128)(2,1)}, bf16[1664,256]{1,0:T(8,128)(2,1)S(1)}) custom-call(s32[4]{0:T(128)S(1)} %pad_add_fusion.refs_0_, bf16[1664,2048]{1,0:T(8,128)(2,1)S(1)} %bitcast.8, bf16[2048,1024]{1,0:T(8,128)(2,1)S(1)} %copy-done.13, ...), custom_call_target="tpu_custom_call" | custom-call | flops 99999997952 | bytes 36000000 | tf_op jit(solution)/shard_map/pallas_call | solution.py:24
  51.2 4.6 %shard_map.136 = (bf16[4,64,2048]{2,1,0:T(8,128)(2,1)S(1)}, bf16[4,64,2048]{2,1,0:T(8,128)(2,1)}, bf16[4,64,2048]{2,1,0:T(8,128)(2,1)S(1)}) custom-call(s32[16]{0:T(128)S(1)} %get-tuple-element.44.refs_0_, bf16[13,64,128]{2,1,0:T(8,128)(2,1)S(1)} %add_convert_fusion.3.refs_1_, bf16[13,64,128]{2,1,0:T(8,128)(2,1)S(1)} %collective-permute-done.4.refs_2_, ...), custom_call_target="tpu_custom_call" | custom-call | flops 99999997952 | bytes 36000000 | tf_op jit(solution)/shard_map/pallas_call | solution.py:24
  55.7 1.6 %collective-permute-done.10 = bf16[4,64,2048]{2,1,0:T(8,128)(2,1)} collective-permute-done((bf16[4,64,2048]{2,1,0:T(8,128)(2,1)}, bf16[4,64,2048]{2,1,0:T(8,128)(2,1)}, u32[]{:S(2)}, u32[]{:S(2)}) %collective-permute-start.10) | collective-permute-done | bytes 1048608 | tf_op jit(solution)/shard_map/ppermute | solution.py:527
  57.7 3.8 %collective-permute-start.16 = (bf16[4,64,2048]{2,1,0:T(8,128)(2,1)S(1)}, bf16[4,64,2048]{2,1,0:T(8,128)(2,1)S(1)}, u32[]{:S(2)}, u32[]{:S(2)}) collective-permute-start(bf16[4,64,2048]{2,1,0:T(8,128)(2,1)S(1)} %add_convert_fusion.1.refs_16_), channel_id=1, source_target_pairs={{0,4},{12,8},{4,12},{8,0},{1,5},{13,9},{5,13},{9,1},{2,6},{14,10},... | collective-permute-start | bytes 3145736 | tf_op jit(solution)/shard_map/ppermute | solution.py:537
  61.5 4.6 %shard_map.137.refs_1_.refs_4_ = bf16[13,64,128]{2,1,0:T(8,128)(2,1)S(1)} custom-call(s32[13]{0:T(128)S(1)} %copy-done.12, s32[4]{0:T(128)S(1)} %copy-done.20, s32[1]{0:T(128)} %bitcast.refs_2_.refs_1_, bf16[13,64,2048]{2,1,0:T(8,128)(2,1)S(1)} %copy-done.5, bf16[13,64,2048]{2,1,0:T(8,128)(2,1)S(1)} %copy-done.5, bf16[13,64,2048]{2,1,0:T(8,128)(2,1)S(1)} %copy-done.5, ...), custom_call_target="tpu_custom_call" | custom-call | flops 99999997952 | bytes 36000000 | tf_op jit(solution)/shard_map/pallas_call | solution.py:24
  68.0 1.4 %add_convert_fusion.2 = bf16[1664,256]{1,0:T(8,128)(2,1)S(1)} fusion(bf16[1664,256]{1,0:T(8,128)(2,1)} %collective-permute-done.11, bf16[1664,256]{1,0:T(8,128)(2,1)S(1)} %shard_map.138), kind=kLoop, calls=%fused_computation.6 | loop fusion | flops 1703936 | bytes 2555904 | tf_op jit(solution)/shard_map/convert_element_type | solution.py:421
  70.0 4.2 %collective-permute-done.14.refs_6_.refs_3_ = bf16[13,64,128]{2,1,0:T(8,128)(2,1)S(1)} collective-permute-done((bf16[13,64,128]{2,1,0:T(8,128)(2,1)S(1)}, bf16[13,64,128]{2,1,0:T(8,128)(2,1)S(1)}, u32[]{:S(2)}, u32[]{:S(2)}) %collective-permute-start.14) | collective-permute-done | bytes 213024 | tf_op jit(solution)/shard_map/ppermute | solution.py:425
  74.2 3.7 %collective-permute-done.15.refs_7_.refs_4_ = bf16[13,64,128]{2,1,0:T(8,128)(2,1)S(1)} collective-permute-done((bf16[13,64,128]{2,1,0:T(8,128)(2,1)S(1)}, bf16[13,64,128]{2,1,0:T(8,128)(2,1)S(1)}, u32[]{:S(2)}, u32[]{:S(2)}) %collective-permute-start.15) | collective-permute-done | bytes 213024 | tf_op jit(solution)/shard_map/ppermute | solution.py:425
  77.9 1.5 %shard_map.140 = (bf16[4,64,256]{2,1,0:T(8,128)(2,1)S(1)}, bf16[4,64,256]{2,1,0:T(8,128)(2,1)}, bf16[4,64,256]{2,1,0:T(8,128)(2,1)}, bf16[4,64,256]{2,1,0:T(8,128)(2,1)S(1)}) custom-call(s32[16]{0:T(128)S(1)} %get-tuple-element.43.refs_0_, bf16[13,64,128]{2,1,0:T(8,128)(2,1)S(1)} %shard_map.137.refs_1_.refs_4_, ...), custom_call_target="tpu_custom_call" | custom-call | flops 1000000000 | bytes 360000 | tf_op jit(solution)/shard_map/pallas_call | solution.py:24
  79.4 3.3 %collective-permute-start.19 = (bf16[4,64,256]{2,1,0:T(8,128)(2,1)}, bf16[4,64,256]{2,1,0:T(8,128)(2,1)S(1)}, u32[]{:S(2)}, u32[]{:S(2)}) collective-permute-start(bf16[4,64,256]{2,1,0:T(8,128)(2,1)} %get-tuple-element.39), channel_id=1, source_target_pairs={{0,12},{4,0},{8,4},{12,8},{1,13},{5,1},{9,5},{13,9},{2,14},{6,2},{... | collective-permute-start | bytes 393224 | tf_op jit(solution)/shard_map/ppermute | solution.py:407
  82.7 4.0 %collective-permute-done.16.refs_1_ = bf16[4,64,2048]{2,1,0:T(8,128)(2,1)S(1)} collective-permute-done((bf16[4,64,2048]{2,1,0:T(8,128)(2,1)S(1)}, bf16[4,64,2048]{2,1,0:T(8,128)(2,1)S(1)}, u32[]{:S(2)}, u32[]{:S(2)}) %collective-permute-start.16) | collective-permute-done | bytes 1048608 | tf_op jit(solution)/shard_map/ppermute | solution.py:537
  86.7 2.0 %fusion.refs_1_.refs_0_ = bf16[4,64,2048]{2,1,0:T(8,128)(2,1)S(1)} fusion(bf16[4,64,2048]{2,1,0:T(8,128)(2,1)S(1)} %collective-permute-done.16.refs_1_, bf16[4,64,2048]{2,1,0:T(8,128)(2,1)} %shard_map.141), kind=kLoop, calls=%fused_computation.2 | loop fusion | flops 2097152 | bytes 3145728 | tf_op jit(solution)/shard_map/convert_element_type | solution.py:421
  89.7 2.1 %collective-permute-start.24 = (bf16[4,64,2048]{2,1,0:T(8,128)(2,1)}, bf16[4,64,2048]{2,1,0:T(8,128)(2,1)}, u32[]{:S(2)}, u32[]{:S(2)}) collective-permute-start(bf16[4,64,2048]{2,1,0:T(8,128)(2,1)} %shard_map.145.refs_1_), channel_id=1, source_target_pairs={{0,4},{12,8},{4,0},{8,12},{1,5},{13,9},{5,1},{9,13},{2,6},{14,10},... | collective-permute-start | bytes 3145736 | tf_op jit(solution)/shard_map/ppermute | solution.py:547
  91.8 4.8 %collective-permute-done.12.refs_3_ = bf16[1664,256]{1,0:T(8,128)(2,1)S(1)} collective-permute-done((bf16[1664,256]{1,0:T(8,128)(2,1)S(1)}, bf16[1664,256]{1,0:T(8,128)(2,1)S(1)}, u32[]{:S(2)}, u32[]{:S(2)}) %collective-permute-start.12) | collective-permute-done | bytes 852000 | tf_op jit(solution)/shard_map/ppermute | solution.py:425
  96.6 1.6 %collective-permute-start.23 = (bf16[4,64,2048]{2,1,0:T(8,128)(2,1)S(1)}, bf16[4,64,2048]{2,1,0:T(8,128)(2,1)}, u32[]{:S(2)}, u32[]{:S(2)}) collective-permute-start(bf16[4,64,2048]{2,1,0:T(8,128)(2,1)S(1)} %shard_map.146), channel_id=1, source_target_pairs={{4,8},{8,4},{5,9},{9,5},{6,10},{10,6},{7,11},{11,7},{20,24},{24,20... | collective-permute-start | bytes 3145736 | tf_op jit(solution)/shard_map/ppermute | solution.py:545
  98.3 4.4 %shard_map.139 = (bf16[1664,256]{1,0:T(8,128)(2,1)}, bf16[128,256]{1,0:T(8,128)(2,1)}) custom-call(s32[13]{0:T(128)} %refs_0_.10, bf16[1664,256]{1,0:T(8,128)(2,1)} %copy-done.22, bf16[1664,256]{1,0:T(8,128)(2,1)} %collective-permute-done.7.refs_2_, bf16[1664,256]{1,0:T(8,128)(2,1)} %copy-done.23, bf16[13,64,128]{2,1,0:T(8,128)(2,1)} %copy-done.10, ...), custom_call_target="tpu_custom_call" | custom-call | flops 99999997952 | bytes 36000000 | tf_op jit(solution)/shard_map/pallas_call | solution.py:24
  103.7 2.7 %collective-permute-start.20 = (bf16[128,256]{1,0:T(8,128)(2,1)}, bf16[128,256]{1,0:T(8,128)(2,1)S(1)}, u32[]{:S(2)}, u32[]{:S(2)}) collective-permute-start(bf16[128,256]{1,0:T(8,128)(2,1)} %shard_map.143.refs_2_), channel_id=1, source_target_pairs={{0,4},{4,8},{8,12},{12,0},{1,5},{5,9},{9,13},{13,1},{2,6},{6,10},{... | collective-permute-start | bytes 196616 | tf_op jit(solution)/shard_map/ppermute | solution.py:407
  109.3 9.7 %collective-permute-done.24 = bf16[4,64,2048]{2,1,0:T(8,128)(2,1)} collective-permute-done((bf16[4,64,2048]{2,1,0:T(8,128)(2,1)}, bf16[4,64,2048]{2,1,0:T(8,128)(2,1)}, u32[]{:S(2)}, u32[]{:S(2)}) %collective-permute-start.24) | collective-permute-done | bytes 1048608 | tf_op jit(solution)/shard_map/ppermute | solution.py:547
  119.0 2.1 %add_convert_fusion.refs_7_ = bf16[4,64,2048]{2,1,0:T(8,128)(2,1)S(1)} fusion(bf16[4,64,2048]{2,1,0:T(8,128)(2,1)} %collective-permute-done.24, f32[4,64,2048]{2,1,0:T(8,128)S(1)} %fusion.1, bf16[4,64,2048]{2,1,0:T(8,128)(2,1)} %collective-permute-done.23), kind=kLoop, calls=%fused_computation.4 | loop fusion | flops 2621440 | bytes 5242880 | tf_op jit(solution)/shard_map/convert_element_type | solution.py:551
  121.1 7.2 %collective-permute-done.21.refs_4_ = bf16[128,256]{1,0:T(8,128)(2,1)S(1)} collective-permute-done((bf16[128,256]{1,0:T(8,128)(2,1)}, bf16[128,256]{1,0:T(8,128)(2,1)S(1)}, u32[]{:S(2)}, u32[]{:S(2)}) %collective-permute-start.21) | collective-permute-done | bytes 65568 | tf_op jit(solution)/shard_map/ppermute | solution.py:407
  128.3 2.0 %shard_map.147 = bf16[1664,256]{1,0:T(8,128)(2,1)} custom-call(s32[4]{0:T(128)S(1)} %copy-done.20, s32[1]{0:T(128)} %bitcast.refs_2_.refs_1_, bf16[128,256]{1,0:T(8,128)(2,1)} %shard_map.143.refs_2_, bf16[128,256]{1,0:T(8,128)(2,1)S(1)} %collective-permute-done.20.refs_3_, ...), custom_call_target="tpu_custom_call", output_to_operand_aliasing={{}: (6, {})} | custom-call | flops 1000000000 | bytes 360000 | tf_op jit(solution)/shard_map/pallas_call | solution.py:24
  (112 shorter events, 21.9 us)
Async XLA Ops:
  0.6 13.6 %copy-start.12 = (s32[13]{0:T(128)S(1)}, s32[13]{0:T(128)}, u32[]{:S(2)}) copy-start(s32[13]{0:T(128)} %refs_0_.10) | copy-start | bytes 160
  0.7 13.6 %copy-start.7 = (bf16[1664,256]{1,0:T(8,128)(2,1)S(1)}, bf16[1664,256]{1,0:T(8,128)(2,1)}, u32[]{:S(2)}) copy-start(bf16[1664,256]{1,0:T(8,128)(2,1)} %refs_5_.9) | copy-start | bytes 2555908
  0.7 13.6 %copy-start.20 = (s32[4]{0:T(128)S(1)}, s32[4]{0:T(128)}, u32[]{:S(2)}) copy-start(s32[4]{0:T(128)} %refs_0_.11) | copy-start | bytes 52
  3.9 9.0 %collective-permute-start = (bf16[1,64,256]{2,1,0:T(8,128)(2,1)}, bf16[1,64,256]{2,1,0:T(8,128)(2,1)S(1)}, u32[]{:S(2)}, u32[]{:S(2)}) collective-permute-start(bf16[1,64,256]{2,1,0:T(8,128)(2,1)} %get-tuple-element.23.refs_3_), channel_id=1, source_target_pairs={{0,4},{4,8},{8,12},{12,0},{1,5},{5,9},{9,13},{13,1},{2,6},{6,10},{... | collective-permute-start | bytes 98312 | tf_op jit(solution)/shard_map/ppermute | solution.py:407
  6.9 6.0 %collective-permute-start.1 = (bf16[1,64,256]{2,1,0:T(8,128)(2,1)}, bf16[1,64,256]{2,1,0:T(8,128)(2,1)S(1)}, u32[]{:S(2)}, u32[]{:S(2)}) collective-permute-start(bf16[1,64,256]{2,1,0:T(8,128)(2,1)} %get-tuple-element.23.refs_3_), channel_id=1, source_target_pairs={{0,8},{4,12},{8,0},{12,4},{1,9},{5,13},{9,1},{13,5},{2,10},{6,14},... | collective-permute-start | bytes 98312 | tf_op jit(solution)/shard_map/ppermute | solution.py:407
  9.5 4.1 %collective-permute-start.2 = (bf16[1,64,256]{2,1,0:T(8,128)(2,1)}, bf16[1,64,256]{2,1,0:T(8,128)(2,1)S(1)}, u32[]{:S(2)}, u32[]{:S(2)}) collective-permute-start(bf16[1,64,256]{2,1,0:T(8,128)(2,1)} %get-tuple-element.23.refs_3_), channel_id=1, source_target_pairs={{0,12},{4,0},{8,4},{12,8},{1,13},{5,1},{9,5},{13,9},{2,14},{6,2},{... | collective-permute-start | bytes 98312 | tf_op jit(solution)/shard_map/ppermute | solution.py:407
  16.7 23.0 %slice-start = ((s8[6815744]{0:T(1024)(128)(4,1)}), s8[2621440]{0:T(1024)(128)(4,1)S(1)}, s32[]{:S(2)}) async-start(s8[6815744]{0:T(1024)(128)(4,1)} %bitcast.7), calls=%async_computation | async-start | bytes 5242880
  17.4 1.5 %collective-permute-start.3 = (bf16[13,64,128]{2,1,0:T(8,128)(2,1)S(1)}, bf16[13,64,128]{2,1,0:T(8,128)(2,1)S(1)}, u32[]{:S(2)}, u32[]{:S(2)}) collective-permute-start(bf16[13,64,128]{2,1,0:T(8,128)(2,1)S(1)} %get-tuple-element.25), channel_id=1, source_target_pairs={{0,1},{1,0},{2,3},{3,2},{4,5},{5,4},{6,7},{7,6},{8,9},{9,8},{10,11... | collective-permute-start | bytes 638984 | tf_op jit(solution)/shard_map/ppermute | solution.py:425
  19.0 7.4 %collective-permute-start.4 = (bf16[13,64,128]{2,1,0:T(8,128)(2,1)S(1)}, bf16[13,64,128]{2,1,0:T(8,128)(2,1)S(1)}, u32[]{:S(2)}, u32[]{:S(2)}) collective-permute-start(bf16[13,64,128]{2,1,0:T(8,128)(2,1)S(1)} %add_convert_fusion.3.refs_1_), channel_id=1, source_target_pairs={{0,2},{1,3},{2,0},{3,1},{4,6},{5,7},{6,4},{7,5},{8,10},{9,11},{10,... | collective-permute-start | bytes 638984 | tf_op jit(solution)/shard_map/ppermute | solution.py:425
  20.6 15.6 %collective-permute-start.5 = (bf16[1,64,2048]{2,1,0:T(8,128)(2,1)}, bf16[1,64,2048]{2,1,0:T(8,128)(2,1)S(1)}, u32[]{:S(2)}, u32[]{:S(2)}) collective-permute-start(bf16[1,64,2048]{2,1,0:T(8,128)(2,1)} %shard_map.133.refs_2_.refs_11_), channel_id=1, source_target_pairs={{0,4},{4,8},{8,12},{1,5},{5,9},{9,13},{2,6},{6,10},{10,14},{3,7},{... | collective-permute-start | bytes 786440 | tf_op jit(solution)/shard_map/ppermute | solution.py:528
  22.7 13.4 %collective-permute-start.6 = (bf16[1,64,2048]{2,1,0:T(8,128)(2,1)}, bf16[1,64,2048]{2,1,0:T(8,128)(2,1)}, u32[]{:S(2)}, u32[]{:S(2)}) collective-permute-start(bf16[1,64,2048]{2,1,0:T(8,128)(2,1)} %shard_map.133.refs_2_.refs_11_), channel_id=1, source_target_pairs={{12,8},{8,4},{4,0},{13,9},{9,5},{5,1},{14,10},{10,6},{6,2},{15,11}... | collective-permute-start | bytes 786440 | tf_op jit(solution)/shard_map/ppermute | solution.py:529
  31.7 25.6 %collective-permute-start.10 = (bf16[4,64,2048]{2,1,0:T(8,128)(2,1)}, bf16[4,64,2048]{2,1,0:T(8,128)(2,1)}, u32[]{:S(2)}, u32[]{:S(2)}) collective-permute-start(bf16[4,64,2048]{2,1,0:T(8,128)(2,1)} %shard_map.132.refs_5_.refs_6_.refs_0_), channel_id=1, source_target_pairs={{0,4},{12,8},{1,5},{13,9},{2,6},{14,10},{3,7},{15,11},{16,20},{28,... | collective-permute-start | bytes 3145736 | tf_op jit(solution)/shard_map/ppermute | solution.py:527
  37.8 13.1 %collective-permute-start.8 = (bf16[1,64,2048]{2,1,0:T(8,128)(2,1)S(1)}, bf16[1,64,2048]{2,1,0:T(8,128)(2,1)S(1)}, u32[]{:S(2)}, u32[]{:S(2)}) collective-permute-start(bf16[1,64,2048]{2,1,0:T(8,128)(2,1)S(1)} %get-tuple-element.27.refs_7_), channel_id=1, source_target_pairs={{4,8},{8,4},{5,9},{9,5},{6,10},{10,6},{7,11},{11,7},{20,24},{24,20... | collective-permute-start | bytes 786440 | tf_op jit(solution)/shard_map/ppermute | solution.py:532
  38.4 12.7 %collective-permute-start.9 = (bf16[1,64,2048]{2,1,0:T(8,128)(2,1)S(1)}, bf16[1,64,2048]{2,1,0:T(8,128)(2,1)S(1)}, u32[]{:S(2)}, u32[]{:S(2)}) collective-permute-start(bf16[1,64,2048]{2,1,0:T(8,128)(2,1)S(1)} %get-tuple-element.31), channel_id=1, source_target_pairs={{4,12},{8,0},{5,13},{9,1},{6,14},{10,2},{7,15},{11,3},{20,28},{24,... | collective-permute-start | bytes 786440 | tf_op jit(solution)/shard_map/ppermute | solution.py:533
  50.3 39.4 %collective-permute-start.7 = (bf16[1664,256]{1,0:T(8,128)(2,1)}, bf16[1664,256]{1,0:T(8,128)(2,1)}, u32[]{:S(2)}, u32[]{:S(2)}) collective-permute-start(bf16[1664,256]{1,0:T(8,128)(2,1)} %get-tuple-element.29), channel_id=1, source_target_pairs={{0,1},{1,0},{2,3},{3,2},{4,5},{5,4},{6,7},{7,6},{8,9},{9,8},{10,11... | collective-permute-start | bytes 2555912 | tf_op jit(solution)/shard_map/ppermute | solution.py:425
  50.3 16.4 %collective-permute-start.11 = (bf16[1664,256]{1,0:T(8,128)(2,1)}, bf16[1664,256]{1,0:T(8,128)(2,1)}, u32[]{:S(2)}, u32[]{:S(2)}) collective-permute-start(bf16[1664,256]{1,0:T(8,128)(2,1)} %get-tuple-element.32.refs_8_), channel_id=1, source_target_pairs={{0,1},{1,0},{2,3},{3,2},{4,5},{5,4},{6,7},{7,6},{8,9},{9,8},{10,11... | collective-permute-start | bytes 2555912 | tf_op jit(solution)/shard_map/ppermute | solution.py:425
  57.7 29.0 %collective-permute-start.16 = (bf16[4,64,2048]{2,1,0:T(8,128)(2,1)S(1)}, bf16[4,64,2048]{2,1,0:T(8,128)(2,1)S(1)}, u32[]{:S(2)}, u32[]{:S(2)}) collective-permute-start(bf16[4,64,2048]{2,1,0:T(8,128)(2,1)S(1)} %add_convert_fusion.1.refs_16_), channel_id=1, source_target_pairs={{0,4},{12,8},{4,12},{8,0},{1,5},{13,9},{5,13},{9,1},{2,6},{14,10},... | collective-permute-start | bytes 3145736 | tf_op jit(solution)/shard_map/ppermute | solution.py:537
  66.0 11.9 %copy-start.10 = (bf16[13,64,128]{2,1,0:T(8,128)(2,1)}, bf16[13,64,128]{2,1,0:T(8,128)(2,1)S(1)}, u32[]{:S(2)}) copy-start(bf16[13,64,128]{2,1,0:T(8,128)(2,1)S(1)} %shard_map.137.refs_1_.refs_4_) | copy-start | bytes 638980
  66.0 3.4 %collective-permute-start.13 = (bf16[13,64,128]{2,1,0:T(8,128)(2,1)S(1)}, bf16[13,64,128]{2,1,0:T(8,128)(2,1)S(1)}, u32[]{:S(2)}, u32[]{:S(2)}) collective-permute-start(bf16[13,64,128]{2,1,0:T(8,128)(2,1)S(1)} %shard_map.137.refs_1_.refs_4_), channel_id=1, source_target_pairs={{0,1},{1,0},{2,3},{3,2},{4,5},{5,4},{6,7},{7,6},{8,9},{9,8},{10,11... | collective-permute-start | bytes 638984 | tf_op jit(solution)/shard_map/ppermute | solution.py:425
  66.1 8.1 %collective-permute-start.14 = (bf16[13,64,128]{2,1,0:T(8,128)(2,1)S(1)}, bf16[13,64,128]{2,1,0:T(8,128)(2,1)S(1)}, u32[]{:S(2)}, u32[]{:S(2)}) collective-permute-start(bf16[13,64,128]{2,1,0:T(8,128)(2,1)S(1)} %shard_map.137.refs_1_.refs_4_), channel_id=1, source_target_pairs={{0,2},{1,3},{2,0},{3,1},{4,6},{5,7},{6,4},{7,5},{8,10},{9,11},{10,... | collective-permute-start | bytes 638984 | tf_op jit(solution)/shard_map/ppermute | solution.py:425
  66.7 11.2 %copy-start.8 = (bf16[1664,256]{1,0:T(8,128)(2,1)S(1)}, bf16[1664,256]{1,0:T(8,128)(2,1)}, u32[]{:S(2)}) copy-start(bf16[1664,256]{1,0:T(8,128)(2,1)} %refs_5_.9) | copy-start | bytes 2555908
  66.7 11.2 %collective-permute-start.15 = (bf16[13,64,128]{2,1,0:T(8,128)(2,1)S(1)}, bf16[13,64,128]{2,1,0:T(8,128)(2,1)S(1)}, u32[]{:S(2)}, u32[]{:S(2)}) collective-permute-start(bf16[13,64,128]{2,1,0:T(8,128)(2,1)S(1)} %shard_map.137.refs_1_.refs_4_), channel_id=1, source_target_pairs={{0,3},{1,2},{2,1},{3,0},{4,7},{5,6},{6,5},{7,4},{8,11},{9,10},{10,... | collective-permute-start | bytes 638984 | tf_op jit(solution)/shard_map/ppermute | solution.py:425
  69.4 13.3 %copy-start.14 = (bf16[13,64,128]{2,1,0:T(8,128)(2,1)}, bf16[13,64,128]{2,1,0:T(8,128)(2,1)S(1)}, u32[]{:S(2)}) copy-start(bf16[13,64,128]{2,1,0:T(8,128)(2,1)S(1)} %collective-permute-done.13.refs_5_.refs_2_) | copy-start | bytes 638980
  69.4 27.2 %collective-permute-start.12 = (bf16[1664,256]{1,0:T(8,128)(2,1)S(1)}, bf16[1664,256]{1,0:T(8,128)(2,1)S(1)}, u32[]{:S(2)}, u32[]{:S(2)}) collective-permute-start(bf16[1664,256]{1,0:T(8,128)(2,1)S(1)} %add_convert_fusion.2), channel_id=1, source_target_pairs={{0,2},{1,3},{2,0},{3,1},{4,6},{5,7},{6,4},{7,5},{8,10},{9,11},{10,... | collective-permute-start | bytes 2555912 | tf_op jit(solution)/shard_map/ppermute | solution.py:425
  79.4 23.3 %collective-permute-start.19 = (bf16[4,64,256]{2,1,0:T(8,128)(2,1)}, bf16[4,64,256]{2,1,0:T(8,128)(2,1)S(1)}, u32[]{:S(2)}, u32[]{:S(2)}) collective-permute-start(bf16[4,64,256]{2,1,0:T(8,128)(2,1)} %get-tuple-element.39), channel_id=1, source_target_pairs={{0,12},{4,0},{8,4},{12,8},{1,13},{5,1},{9,5},{13,9},{2,14},{6,2},{... | collective-permute-start | bytes 393224 | tf_op jit(solution)/shard_map/ppermute | solution.py:407
  82.7 20.0 %collective-permute-start.18 = (bf16[4,64,256]{2,1,0:T(8,128)(2,1)}, bf16[4,64,256]{2,1,0:T(8,128)(2,1)}, u32[]{:S(2)}, u32[]{:S(2)}) collective-permute-start(bf16[4,64,256]{2,1,0:T(8,128)(2,1)} %get-tuple-element.38), channel_id=1, source_target_pairs={{0,8},{4,12},{8,0},{12,4},{1,9},{5,13},{9,1},{13,5},{2,10},{6,14},... | collective-permute-start | bytes 393224 | tf_op jit(solution)/shard_map/ppermute | solution.py:407
  86.7 16.0 %collective-permute-start.17 = (bf16[4,64,256]{2,1,0:T(8,128)(2,1)S(1)}, bf16[4,64,256]{2,1,0:T(8,128)(2,1)S(1)}, u32[]{:S(2)}, u32[]{:S(2)}) collective-permute-start(bf16[4,64,256]{2,1,0:T(8,128)(2,1)S(1)} %get-tuple-element.37), channel_id=1, source_target_pairs={{0,4},{4,8},{8,12},{12,0},{1,5},{5,9},{9,13},{13,1},{2,6},{6,10},{... | collective-permute-start | bytes 393224 | tf_op jit(solution)/shard_map/ppermute | solution.py:407
  89.7 29.3 %collective-permute-start.24 = (bf16[4,64,2048]{2,1,0:T(8,128)(2,1)}, bf16[4,64,2048]{2,1,0:T(8,128)(2,1)}, u32[]{:S(2)}, u32[]{:S(2)}) collective-permute-start(bf16[4,64,2048]{2,1,0:T(8,128)(2,1)} %shard_map.145.refs_1_), channel_id=1, source_target_pairs={{0,4},{12,8},{4,0},{8,12},{1,5},{13,9},{5,1},{9,13},{2,6},{14,10},... | collective-permute-start | bytes 3145736 | tf_op jit(solution)/shard_map/ppermute | solution.py:547
  96.6 22.4 %collective-permute-start.23 = (bf16[4,64,2048]{2,1,0:T(8,128)(2,1)S(1)}, bf16[4,64,2048]{2,1,0:T(8,128)(2,1)}, u32[]{:S(2)}, u32[]{:S(2)}) collective-permute-start(bf16[4,64,2048]{2,1,0:T(8,128)(2,1)S(1)} %shard_map.146), channel_id=1, source_target_pairs={{4,8},{8,4},{5,9},{9,5},{6,10},{10,6},{7,11},{11,7},{20,24},{24,20... | collective-permute-start | bytes 3145736 | tf_op jit(solution)/shard_map/ppermute | solution.py:545
  103.7 17.4 %collective-permute-start.20 = (bf16[128,256]{1,0:T(8,128)(2,1)}, bf16[128,256]{1,0:T(8,128)(2,1)S(1)}, u32[]{:S(2)}, u32[]{:S(2)}) collective-permute-start(bf16[128,256]{1,0:T(8,128)(2,1)} %shard_map.143.refs_2_), channel_id=1, source_target_pairs={{0,4},{4,8},{8,12},{12,0},{1,5},{5,9},{9,13},{13,1},{2,6},{6,10},{... | collective-permute-start | bytes 196616 | tf_op jit(solution)/shard_map/ppermute | solution.py:407
  106.5 21.9 %collective-permute-start.21 = (bf16[128,256]{1,0:T(8,128)(2,1)}, bf16[128,256]{1,0:T(8,128)(2,1)S(1)}, u32[]{:S(2)}, u32[]{:S(2)}) collective-permute-start(bf16[128,256]{1,0:T(8,128)(2,1)} %shard_map.143.refs_2_), channel_id=1, source_target_pairs={{0,8},{4,12},{8,0},{12,4},{1,9},{5,13},{9,1},{13,5},{2,10},{6,14},... | collective-permute-start | bytes 196616 | tf_op jit(solution)/shard_map/ppermute | solution.py:407
  107.6 20.8 %collective-permute-start.22 = (bf16[128,256]{1,0:T(8,128)(2,1)}, bf16[128,256]{1,0:T(8,128)(2,1)S(1)}, u32[]{:S(2)}, u32[]{:S(2)}) collective-permute-start(bf16[128,256]{1,0:T(8,128)(2,1)} %shard_map.143.refs_2_), channel_id=1, source_target_pairs={{0,12},{4,0},{8,4},{12,8},{1,13},{5,1},{9,5},{13,9},{2,14},{6,2},{... | collective-permute-start | bytes 196616 | tf_op jit(solution)/shard_map/ppermute | solution.py:407
  (22 other events, 126.1 us)

commit v16 on v15

--- a/solution.py
+++ b/solution.py
@@ -550,8 +550,7 @@
         )
         down_out = (near_total + from_inner.astype(jnp.float32) + from_third.astype(jnp.float32)).astype(own.dtype)
 
-        values, last_values = values_of(lengths, base_sums, rank_in, adapter_up_matrix, up_last)
-        last_values = after(last_values, up_out)
+        values, last_values = values_of(lengths, base_sums, rank_in, adapter_up_matrix, up_last, [up_out])
         tokens = [down_out]
     else:
         codes = codes_of(order)

time: 131 us -> 126 us (0.962)
  waiting for transfers between devices: 39 us -> 34.2 us
  Pallas kernels: 34.6 us -> 33.2 us
    ppermute x8, waiting for transfers between devices: 15.4 us -> 10.5 us  [crossed(): lax.ppermute(array, 'tensor', [(i, i ^ by) for i in range(lax.axis_size('...]
    ppermute x9, waiting for transfers between devices: 7.93 us -> 5.15 us  [shift(): lax.ppermute(array, 'dp', [(i, (i + by) % size) for i in range(size)])]
    ppermute x1, waiting for transfers between devices: 9.74 us -> 12.1 us  [body(): from_third = lax.ppermute(third, 'dp', [(0, 1), (3, 2), (1, 0), (2, 3)])]
    ppermute x1, starting transfers between devices: 2.08 us -> 3.87 us  [body(): from_third = lax.ppermute(third, 'dp', [(0, 1), (3, 2), (1, 0), (2, 3)])]
    pallas_call x18 -> x17, Pallas kernels: 34.6 us -> 33.2 us  [call(): pl.pallas_call(run, grid_spec=pltpu.PrefetchScalarGridSpec(num_scalar_pre...]
where the time goes in v16:
time: 126 us
  starting transfers between devices  38 us (30%)
  waiting for transfers between devices  34.2 us (27%)
  Pallas kernels  33.2 us (26%)
  other arithmetic  10.1 us (8%)
  local copies, waits for them, and re-layouts  9.02 us (7%)
    pallas_call x17, Pallas kernels, call(): pl.pallas_call(run, grid_spec=pltpu.PrefetchScalarGridSpec(num_scalar_pre...  33.2 us
    ppermute x9, starting transfers between devices, shift(): lax.ppermute(array, 'dp', [(i, (i + by) % size) for i in range(size)])  14.3 us
    ppermute x1, waiting for transfers between devices, body(): from_third = lax.ppermute(third, 'dp', [(0, 1), (3, 2), (1, 0), (2, 3)])  12.1 us
    ppermute x8, waiting for transfers between devices, crossed(): lax.ppermute(array, 'tensor', [(i, i ^ by) for i in range(lax.axis_size('...  10.5 us
    unnamed x58, local copies, waits for them, and re-layouts  8.85 us
    ppermute x9, waiting for transfers between devices, shift(): lax.ppermute(array, 'dp', [(i, (i + by) % size) for i in range(size)])  5.15 us
    ppermute x8, starting transfers between devices, crossed(): lax.ppermute(array, 'tensor', [(i, i ^ by) for i in range(lax.axis_size('...  4.64 us
    convert_element_type x5, other arithmetic, add(): sum((array.astype(jnp.float32) for array in arrays)).astype(arrays[0].dtype)  4.57 us
  transfers between devices with their start and end apart: 25, of which 11 were waited for; matrix products, arithmetic and copies ran while one was open for 8% of the time, Pallas kernels for 22%

profile of v16, /device:TPU:0, one launch (start us, length us, event | category | flops | bytes accessed | tf_op | source)
XLA Modules:
  0.0 125.5 jit_solution(16726675565287653718)
XLA Ops:
  0.7 3.2 %shard_map.130 = (bf16[13,64,128]{2,1,0:T(8,128)(2,1)}, bf16[1,64,256]{2,1,0:T(8,128)(2,1)}, bf16[1,64,2048]{2,1,0:T(8,128)(2,1)}) custom-call(s32[13]{0:T(128)} %refs_0_.10, bf16[13,64,256]{2,1,0:T(8,128)(2,1)} %refs_8_.3, bf16[1664,256]{1,0:T(8,128)(2,1)} %refs_5_.9, bf16[13,64,2048]{2,1,0:T(8,128)(2,1)} %refs_6_.5), custom_call_target="tpu_custom_call" | custom-call | flops 1000000000 | bytes 360000 | tf_op jit(solution)/shard_map/pallas_call | solution.py:24
  3.9 3.0 %collective-permute-start = (bf16[1,64,256]{2,1,0:T(8,128)(2,1)}, bf16[1,64,256]{2,1,0:T(8,128)(2,1)S(1)}, u32[]{:S(2)}, u32[]{:S(2)}) collective-permute-start(bf16[1,64,256]{2,1,0:T(8,128)(2,1)} %get-tuple-element.23.refs_3_), channel_id=1, source_target_pairs={{0,4},{4,8},{8,12},{12,0},{1,5},{5,9},{9,13},{13,1},{2,6},{6,10},{... | collective-permute-start | bytes 98312 | tf_op jit(solution)/shard_map/ppermute | solution.py:407
  6.9 2.6 %collective-permute-start.1 = (bf16[1,64,256]{2,1,0:T(8,128)(2,1)}, bf16[1,64,256]{2,1,0:T(8,128)(2,1)S(1)}, u32[]{:S(2)}, u32[]{:S(2)}) collective-permute-start(bf16[1,64,256]{2,1,0:T(8,128)(2,1)} %get-tuple-element.23.refs_3_), channel_id=1, source_target_pairs={{0,8},{4,12},{8,0},{12,4},{1,9},{5,13},{9,1},{13,5},{2,10},{6,14},... | collective-permute-start | bytes 98312 | tf_op jit(solution)/shard_map/ppermute | solution.py:407
  9.5 1.3 %collective-permute-start.2 = (bf16[1,64,256]{2,1,0:T(8,128)(2,1)}, bf16[1,64,256]{2,1,0:T(8,128)(2,1)S(1)}, u32[]{:S(2)}, u32[]{:S(2)}) collective-permute-start(bf16[1,64,256]{2,1,0:T(8,128)(2,1)} %get-tuple-element.23.refs_3_), channel_id=1, source_target_pairs={{0,12},{4,0},{8,4},{12,8},{1,13},{5,1},{9,5},{13,9},{2,14},{6,2},{... | collective-permute-start | bytes 98312 | tf_op jit(solution)/shard_map/ppermute | solution.py:407
  17.6 1.4 %collective-permute-done.3 = bf16[13,64,128]{2,1,0:T(8,128)(2,1)S(1)} collective-permute-done((bf16[13,64,128]{2,1,0:T(8,128)(2,1)S(1)}, bf16[13,64,128]{2,1,0:T(8,128)(2,1)S(1)}, u32[]{:S(2)}, u32[]{:S(2)}) %collective-permute-start.3) | collective-permute-done | bytes 213024 | tf_op jit(solution)/shard_map/ppermute | solution.py:425
  19.0 1.6 %collective-permute-start.4 = (bf16[13,64,128]{2,1,0:T(8,128)(2,1)S(1)}, bf16[13,64,128]{2,1,0:T(8,128)(2,1)S(1)}, u32[]{:S(2)}, u32[]{:S(2)}) collective-permute-start(bf16[13,64,128]{2,1,0:T(8,128)(2,1)S(1)} %add_convert_fusion.3.refs_1_), channel_id=1, source_target_pairs={{0,2},{1,3},{2,0},{3,1},{4,6},{5,7},{6,4},{7,5},{8,10},{9,11},{10,... | collective-permute-start | bytes 638984 | tf_op jit(solution)/shard_map/ppermute | solution.py:425
  20.6 2.1 %collective-permute-start.5 = (bf16[1,64,2048]{2,1,0:T(8,128)(2,1)}, bf16[1,64,2048]{2,1,0:T(8,128)(2,1)S(1)}, u32[]{:S(2)}, u32[]{:S(2)}) collective-permute-start(bf16[1,64,2048]{2,1,0:T(8,128)(2,1)} %shard_map.133.refs_2_.refs_11_), channel_id=1, source_target_pairs={{0,4},{4,8},{8,12},{1,5},{5,9},{9,13},{2,6},{6,10},{10,14},{3,7},{... | collective-permute-start | bytes 786440 | tf_op jit(solution)/shard_map/ppermute | solution.py:528
  22.7 1.3 %collective-permute-start.6 = (bf16[1,64,2048]{2,1,0:T(8,128)(2,1)}, bf16[1,64,2048]{2,1,0:T(8,128)(2,1)}, u32[]{:S(2)}, u32[]{:S(2)}) collective-permute-start(bf16[1,64,2048]{2,1,0:T(8,128)(2,1)} %shard_map.133.refs_2_.refs_11_), channel_id=1, source_target_pairs={{12,8},{8,4},{4,0},{13,9},{9,5},{5,1},{14,10},{10,6},{6,2},{15,11}... | collective-permute-start | bytes 786440 | tf_op jit(solution)/shard_map/ppermute | solution.py:529
  26.4 2.9 %copy-done = bf16[1664,2048]{1,0:T(8,128)(2,1)S(1)} copy-done((bf16[1664,2048]{1,0:T(8,128)(2,1)S(1)}, bf16[1664,2048]{1,0:T(8,128)(2,1)}, u32[]{:S(2)}) %copy-start) | copy-done | bytes 6815768
  29.3 2.4 %shard_map.132.refs_5_.refs_6_.refs_0_ = bf16[4,64,2048]{2,1,0:T(8,128)(2,1)} custom-call(s32[16]{0:T(128)S(1)} %get-tuple-element.44.refs_0_, bf16[13,64,128]{2,1,0:T(8,128)(2,1)S(1)} %add_convert_fusion.3.refs_1_, bf16[13,64,128]{2,1,0:T(8,128)(2,1)S(1)} %collective-permute-done.4.refs_2_, bf16[1664,2048]{1,0:T(8,128)(2,1)S(1)} %copy-done, ...), custom_call_target="tpu_custom_call" | custom-call | flops 1000000000 | bytes 360000 | tf_op jit(solution)/shard_map/pallas_call | solution.py:24
  31.7 4.4 %collective-permute-start.10 = (bf16[4,64,2048]{2,1,0:T(8,128)(2,1)}, bf16[4,64,2048]{2,1,0:T(8,128)(2,1)}, u32[]{:S(2)}, u32[]{:S(2)}) collective-permute-start(bf16[4,64,2048]{2,1,0:T(8,128)(2,1)} %shard_map.132.refs_5_.refs_6_.refs_0_), channel_id=1, source_target_pairs={{0,4},{12,8},{1,5},{13,9},{2,6},{14,10},{3,7},{15,11},{16,20},{28,... | collective-permute-start | bytes 3145736 | tf_op jit(solution)/shard_map/ppermute | solution.py:527
  36.2 1.6 %shard_map.134 = (bf16[1,64,2048]{2,1,0:T(8,128)(2,1)S(1)}, bf16[1,64,2048]{2,1,0:T(8,128)(2,1)S(1)}) custom-call(s32[4]{0:T(128)S(1)} %copy-done.20, s32[1]{0:T(128)} %bitcast.refs_2_.refs_1_, bf16[1,64,2048]{2,1,0:T(8,128)(2,1)} %shard_map.133.refs_2_.refs_11_, bf16[1,64,2048]{2,1,0:T(8,128)(2,1)S(1)} %collective-permute-done.5.refs_3_.refs_12_, ...), custom_call_target="tpu_custom_call" | custom-call | flops 1000000000 | bytes 360000 | tf_op jit(solution)/shard_map/pallas_call | solution.py:24
  39.8 9.6 %shard_map.135 = (bf16[1664,256]{1,0:T(8,128)(2,1)}, bf16[1664,256]{1,0:T(8,128)(2,1)S(1)}, bf16[1664,256]{1,0:T(8,128)(2,1)}, bf16[1664,256]{1,0:T(8,128)(2,1)S(1)}) custom-call(s32[4]{0:T(128)S(1)} %pad_add_fusion.refs_0_, bf16[1664,2048]{1,0:T(8,128)(2,1)S(1)} %bitcast.8, bf16[2048,1024]{1,0:T(8,128)(2,1)S(1)} %copy-done.12, ...), custom_call_target="tpu_custom_call" | custom-call | flops 99999997952 | bytes 36000000 | tf_op jit(solution)/shard_map/pallas_call | solution.py:24
  51.2 4.5 %shard_map.136 = (bf16[4,64,2048]{2,1,0:T(8,128)(2,1)S(1)}, bf16[4,64,2048]{2,1,0:T(8,128)(2,1)}, bf16[4,64,2048]{2,1,0:T(8,128)(2,1)S(1)}) custom-call(s32[16]{0:T(128)S(1)} %get-tuple-element.44.refs_0_, bf16[13,64,128]{2,1,0:T(8,128)(2,1)S(1)} %add_convert_fusion.3.refs_1_, bf16[13,64,128]{2,1,0:T(8,128)(2,1)S(1)} %collective-permute-done.4.refs_2_, ...), custom_call_target="tpu_custom_call" | custom-call | flops 99999997952 | bytes 36000000 | tf_op jit(solution)/shard_map/pallas_call | solution.py:24
  55.7 1.6 %collective-permute-done.10 = bf16[4,64,2048]{2,1,0:T(8,128)(2,1)} collective-permute-done((bf16[4,64,2048]{2,1,0:T(8,128)(2,1)}, bf16[4,64,2048]{2,1,0:T(8,128)(2,1)}, u32[]{:S(2)}, u32[]{:S(2)}) %collective-permute-start.10) | collective-permute-done | bytes 1048608 | tf_op jit(solution)/shard_map/ppermute | solution.py:527
  57.7 3.8 %collective-permute-start.16 = (bf16[4,64,2048]{2,1,0:T(8,128)(2,1)S(1)}, bf16[4,64,2048]{2,1,0:T(8,128)(2,1)S(1)}, u32[]{:S(2)}, u32[]{:S(2)}) collective-permute-start(bf16[4,64,2048]{2,1,0:T(8,128)(2,1)S(1)} %add_convert_fusion.1.refs_16_), channel_id=1, source_target_pairs={{0,4},{12,8},{4,12},{8,0},{1,5},{13,9},{5,13},{9,1},{2,6},{14,10},... | collective-permute-start | bytes 3145736 | tf_op jit(solution)/shard_map/ppermute | solution.py:537
  61.5 4.6 %shard_map.137.refs_1_.refs_4_ = bf16[13,64,128]{2,1,0:T(8,128)(2,1)S(1)} custom-call(s32[13]{0:T(128)S(1)} %copy-done.11, s32[4]{0:T(128)S(1)} %copy-done.20, s32[1]{0:T(128)} %bitcast.refs_2_.refs_1_, bf16[13,64,2048]{2,1,0:T(8,128)(2,1)S(1)} %copy-done.5, bf16[13,64,2048]{2,1,0:T(8,128)(2,1)S(1)} %copy-done.5, bf16[13,64,2048]{2,1,0:T(8,128)(2,1)S(1)} %copy-done.5, ...), custom_call_target="tpu_custom_call" | custom-call | flops 99999997952 | bytes 36000000 | tf_op jit(solution)/shard_map/pallas_call | solution.py:24
  68.0 1.4 %add_convert_fusion.2 = bf16[1664,256]{1,0:T(8,128)(2,1)S(1)} fusion(bf16[1664,256]{1,0:T(8,128)(2,1)} %collective-permute-done.11, bf16[1664,256]{1,0:T(8,128)(2,1)S(1)} %shard_map.138), kind=kLoop, calls=%fused_computation.6 | loop fusion | flops 1703936 | bytes 2555904 | tf_op jit(solution)/shard_map/convert_element_type | solution.py:421
  70.0 4.2 %collective-permute-done.14.refs_3_.refs_6_ = bf16[13,64,128]{2,1,0:T(8,128)(2,1)S(1)} collective-permute-done((bf16[13,64,128]{2,1,0:T(8,128)(2,1)S(1)}, bf16[13,64,128]{2,1,0:T(8,128)(2,1)S(1)}, u32[]{:S(2)}, u32[]{:S(2)}) %collective-permute-start.14) | collective-permute-done | bytes 213024 | tf_op jit(solution)/shard_map/ppermute | solution.py:425
  74.3 3.7 %collective-permute-done.15.refs_4_.refs_7_ = bf16[13,64,128]{2,1,0:T(8,128)(2,1)S(1)} collective-permute-done((bf16[13,64,128]{2,1,0:T(8,128)(2,1)S(1)}, bf16[13,64,128]{2,1,0:T(8,128)(2,1)S(1)}, u32[]{:S(2)}, u32[]{:S(2)}) %collective-permute-start.15) | collective-permute-done | bytes 213024 | tf_op jit(solution)/shard_map/ppermute | solution.py:425
  78.8 3.5 %collective-permute-start.19 = (bf16[4,64,256]{2,1,0:T(8,128)(2,1)S(1)}, bf16[4,64,256]{2,1,0:T(8,128)(2,1)S(1)}, u32[]{:S(2)}, u32[]{:S(2)}) collective-permute-start(bf16[4,64,256]{2,1,0:T(8,128)(2,1)S(1)} %get-tuple-element.38), channel_id=1, source_target_pairs={{0,12},{4,0},{8,4},{12,8},{1,13},{5,1},{9,5},{13,9},{2,14},{6,2},{... | collective-permute-start | bytes 393224 | tf_op jit(solution)/shard_map/ppermute | solution.py:407
  82.3 4.4 %collective-permute-done.16.refs_1_ = bf16[4,64,2048]{2,1,0:T(8,128)(2,1)S(1)} collective-permute-done((bf16[4,64,2048]{2,1,0:T(8,128)(2,1)S(1)}, bf16[4,64,2048]{2,1,0:T(8,128)(2,1)S(1)}, u32[]{:S(2)}, u32[]{:S(2)}) %collective-permute-start.16) | collective-permute-done | bytes 1048608 | tf_op jit(solution)/shard_map/ppermute | solution.py:537
  86.8 2.0 %fusion.refs_1_.refs_0_ = bf16[4,64,2048]{2,1,0:T(8,128)(2,1)S(1)} fusion(bf16[4,64,2048]{2,1,0:T(8,128)(2,1)S(1)} %collective-permute-done.16.refs_1_, bf16[4,64,2048]{2,1,0:T(8,128)(2,1)} %shard_map.140), kind=kLoop, calls=%fused_computation.2 | loop fusion | flops 2097152 | bytes 3145728 | tf_op jit(solution)/shard_map/convert_element_type | solution.py:421
  89.8 3.9 %collective-permute-start.24 = (bf16[4,64,2048]{2,1,0:T(8,128)(2,1)}, bf16[4,64,2048]{2,1,0:T(8,128)(2,1)}, u32[]{:S(2)}, u32[]{:S(2)}) collective-permute-start(bf16[4,64,2048]{2,1,0:T(8,128)(2,1)} %shard_map.144.refs_1_), channel_id=1, source_target_pairs={{0,4},{12,8},{4,0},{8,12},{1,5},{13,9},{5,1},{9,13},{2,6},{14,10},... | collective-permute-start | bytes 3145736 | tf_op jit(solution)/shard_map/ppermute | solution.py:547
  93.7 2.3 %collective-permute-done.18 = bf16[4,64,256]{2,1,0:T(8,128)(2,1)S(1)} collective-permute-done((bf16[4,64,256]{2,1,0:T(8,128)(2,1)S(1)}, bf16[4,64,256]{2,1,0:T(8,128)(2,1)S(1)}, u32[]{:S(2)}, u32[]{:S(2)}) %collective-permute-start.18) | collective-permute-done | bytes 131104 | tf_op jit(solution)/shard_map/ppermute | solution.py:407
  96.0 1.6 %collective-permute-start.23 = (bf16[4,64,2048]{2,1,0:T(8,128)(2,1)S(1)}, bf16[4,64,2048]{2,1,0:T(8,128)(2,1)}, u32[]{:S(2)}, u32[]{:S(2)}) collective-permute-start(bf16[4,64,2048]{2,1,0:T(8,128)(2,1)S(1)} %shard_map.145), channel_id=1, source_target_pairs={{4,8},{8,4},{5,9},{9,5},{6,10},{10,6},{7,11},{11,7},{20,24},{24,20... | collective-permute-start | bytes 3145736 | tf_op jit(solution)/shard_map/ppermute | solution.py:545
  99.2 4.4 %shard_map.142 = (bf16[1664,256]{1,0:T(8,128)(2,1)}, bf16[128,256]{1,0:T(8,128)(2,1)}) custom-call(s32[13]{0:T(128)} %refs_0_.10, bf16[1664,256]{1,0:T(8,128)(2,1)} %copy-done.22, bf16[1664,256]{1,0:T(8,128)(2,1)} %collective-permute-done.7.refs_2_, bf16[1664,256]{1,0:T(8,128)(2,1)} %copy-done.23, bf16[13,64,128]{2,1,0:T(8,128)(2,1)} %copy-done.10, ...), custom_call_target="tpu_custom_call" | custom-call | flops 99999997952 | bytes 36000000 | tf_op jit(solution)/shard_map/pallas_call | solution.py:24
  103.9 1.9 %collective-permute-start.21 = (bf16[128,256]{1,0:T(8,128)(2,1)}, bf16[128,256]{1,0:T(8,128)(2,1)S(1)}, u32[]{:S(2)}, u32[]{:S(2)}) collective-permute-start(bf16[128,256]{1,0:T(8,128)(2,1)} %get-tuple-element.39.refs_2_), channel_id=1, source_target_pairs={{0,8},{4,12},{8,0},{12,4},{1,9},{5,13},{9,1},{13,5},{2,10},{6,14},... | collective-permute-start | bytes 196616 | tf_op jit(solution)/shard_map/ppermute | solution.py:407
  105.8 1.7 %collective-permute-start.22 = (bf16[128,256]{1,0:T(8,128)(2,1)}, bf16[128,256]{1,0:T(8,128)(2,1)S(1)}, u32[]{:S(2)}, u32[]{:S(2)}) collective-permute-start(bf16[128,256]{1,0:T(8,128)(2,1)} %get-tuple-element.39.refs_2_), channel_id=1, source_target_pairs={{0,12},{4,0},{8,4},{12,8},{1,13},{5,1},{9,5},{13,9},{2,14},{6,2},{... | collective-permute-start | bytes 196616 | tf_op jit(solution)/shard_map/ppermute | solution.py:407
  107.9 12.1 %collective-permute-done.24 = bf16[4,64,2048]{2,1,0:T(8,128)(2,1)} collective-permute-done((bf16[4,64,2048]{2,1,0:T(8,128)(2,1)}, bf16[4,64,2048]{2,1,0:T(8,128)(2,1)}, u32[]{:S(2)}, u32[]{:S(2)}) %collective-permute-start.24) | collective-permute-done | bytes 1048608 | tf_op jit(solution)/shard_map/ppermute | solution.py:547
  120.0 2.1 %add_convert_fusion.refs_7_ = bf16[4,64,2048]{2,1,0:T(8,128)(2,1)S(1)} fusion(bf16[4,64,2048]{2,1,0:T(8,128)(2,1)} %collective-permute-done.24, f32[4,64,2048]{2,1,0:T(8,128)S(1)} %fusion.1, bf16[4,64,2048]{2,1,0:T(8,128)(2,1)} %collective-permute-done.23), kind=kLoop, calls=%fused_computation.4 | loop fusion | flops 2621440 | bytes 5242880 | tf_op jit(solution)/shard_map/convert_element_type | solution.py:551
  122.2 2.2 %collective-permute-done.21.refs_4_ = bf16[128,256]{1,0:T(8,128)(2,1)S(1)} collective-permute-done((bf16[128,256]{1,0:T(8,128)(2,1)}, bf16[128,256]{1,0:T(8,128)(2,1)S(1)}, u32[]{:S(2)}, u32[]{:S(2)}) %collective-permute-start.21) | collective-permute-done | bytes 65568 | tf_op jit(solution)/shard_map/ppermute | solution.py:407
  (111 shorter events, 21.1 us)
Async XLA Ops:
  0.6 13.6 %copy-start.11 = (s32[13]{0:T(128)S(1)}, s32[13]{0:T(128)}, u32[]{:S(2)}) copy-start(s32[13]{0:T(128)} %refs_0_.10) | copy-start | bytes 160
  0.7 13.6 %copy-start.7 = (bf16[1664,256]{1,0:T(8,128)(2,1)S(1)}, bf16[1664,256]{1,0:T(8,128)(2,1)}, u32[]{:S(2)}) copy-start(bf16[1664,256]{1,0:T(8,128)(2,1)} %refs_5_.9) | copy-start | bytes 2555908
  0.7 13.6 %copy-start.20 = (s32[4]{0:T(128)S(1)}, s32[4]{0:T(128)}, u32[]{:S(2)}) copy-start(s32[4]{0:T(128)} %refs_0_.11) | copy-start | bytes 52
  3.9 9.0 %collective-permute-start = (bf16[1,64,256]{2,1,0:T(8,128)(2,1)}, bf16[1,64,256]{2,1,0:T(8,128)(2,1)S(1)}, u32[]{:S(2)}, u32[]{:S(2)}) collective-permute-start(bf16[1,64,256]{2,1,0:T(8,128)(2,1)} %get-tuple-element.23.refs_3_), channel_id=1, source_target_pairs={{0,4},{4,8},{8,12},{12,0},{1,5},{5,9},{9,13},{13,1},{2,6},{6,10},{... | collective-permute-start | bytes 98312 | tf_op jit(solution)/shard_map/ppermute | solution.py:407
  6.9 6.0 %collective-permute-start.1 = (bf16[1,64,256]{2,1,0:T(8,128)(2,1)}, bf16[1,64,256]{2,1,0:T(8,128)(2,1)S(1)}, u32[]{:S(2)}, u32[]{:S(2)}) collective-permute-start(bf16[1,64,256]{2,1,0:T(8,128)(2,1)} %get-tuple-element.23.refs_3_), channel_id=1, source_target_pairs={{0,8},{4,12},{8,0},{12,4},{1,9},{5,13},{9,1},{13,5},{2,10},{6,14},... | collective-permute-start | bytes 98312 | tf_op jit(solution)/shard_map/ppermute | solution.py:407
  9.5 4.1 %collective-permute-start.2 = (bf16[1,64,256]{2,1,0:T(8,128)(2,1)}, bf16[1,64,256]{2,1,0:T(8,128)(2,1)S(1)}, u32[]{:S(2)}, u32[]{:S(2)}) collective-permute-start(bf16[1,64,256]{2,1,0:T(8,128)(2,1)} %get-tuple-element.23.refs_3_), channel_id=1, source_target_pairs={{0,12},{4,0},{8,4},{12,8},{1,13},{5,1},{9,5},{13,9},{2,14},{6,2},{... | collective-permute-start | bytes 98312 | tf_op jit(solution)/shard_map/ppermute | solution.py:407
  16.7 23.1 %slice-start = ((s8[6815744]{0:T(1024)(128)(4,1)}), s8[2621440]{0:T(1024)(128)(4,1)S(1)}, s32[]{:S(2)}) async-start(s8[6815744]{0:T(1024)(128)(4,1)} %bitcast.7), calls=%async_computation | async-start | bytes 5242880
  17.4 1.5 %collective-permute-start.3 = (bf16[13,64,128]{2,1,0:T(8,128)(2,1)S(1)}, bf16[13,64,128]{2,1,0:T(8,128)(2,1)S(1)}, u32[]{:S(2)}, u32[]{:S(2)}) collective-permute-start(bf16[13,64,128]{2,1,0:T(8,128)(2,1)S(1)} %get-tuple-element.25), channel_id=1, source_target_pairs={{0,1},{1,0},{2,3},{3,2},{4,5},{5,4},{6,7},{7,6},{8,9},{9,8},{10,11... | collective-permute-start | bytes 638984 | tf_op jit(solution)/shard_map/ppermute | solution.py:425
  19.0 7.4 %collective-permute-start.4 = (bf16[13,64,128]{2,1,0:T(8,128)(2,1)S(1)}, bf16[13,64,128]{2,1,0:T(8,128)(2,1)S(1)}, u32[]{:S(2)}, u32[]{:S(2)}) collective-permute-start(bf16[13,64,128]{2,1,0:T(8,128)(2,1)S(1)} %add_convert_fusion.3.refs_1_), channel_id=1, source_target_pairs={{0,2},{1,3},{2,0},{3,1},{4,6},{5,7},{6,4},{7,5},{8,10},{9,11},{10,... | collective-permute-start | bytes 638984 | tf_op jit(solution)/shard_map/ppermute | solution.py:425
  20.6 15.6 %collective-permute-start.5 = (bf16[1,64,2048]{2,1,0:T(8,128)(2,1)}, bf16[1,64,2048]{2,1,0:T(8,128)(2,1)S(1)}, u32[]{:S(2)}, u32[]{:S(2)}) collective-permute-start(bf16[1,64,2048]{2,1,0:T(8,128)(2,1)} %shard_map.133.refs_2_.refs_11_), channel_id=1, source_target_pairs={{0,4},{4,8},{8,12},{1,5},{5,9},{9,13},{2,6},{6,10},{10,14},{3,7},{... | collective-permute-start | bytes 786440 | tf_op jit(solution)/shard_map/ppermute | solution.py:528
  22.7 13.4 %collective-permute-start.6 = (bf16[1,64,2048]{2,1,0:T(8,128)(2,1)}, bf16[1,64,2048]{2,1,0:T(8,128)(2,1)}, u32[]{:S(2)}, u32[]{:S(2)}) collective-permute-start(bf16[1,64,2048]{2,1,0:T(8,128)(2,1)} %shard_map.133.refs_2_.refs_11_), channel_id=1, source_target_pairs={{12,8},{8,4},{4,0},{13,9},{9,5},{5,1},{14,10},{10,6},{6,2},{15,11}... | collective-permute-start | bytes 786440 | tf_op jit(solution)/shard_map/ppermute | solution.py:529
  31.7 25.6 %collective-permute-start.10 = (bf16[4,64,2048]{2,1,0:T(8,128)(2,1)}, bf16[4,64,2048]{2,1,0:T(8,128)(2,1)}, u32[]{:S(2)}, u32[]{:S(2)}) collective-permute-start(bf16[4,64,2048]{2,1,0:T(8,128)(2,1)} %shard_map.132.refs_5_.refs_6_.refs_0_), channel_id=1, source_target_pairs={{0,4},{12,8},{1,5},{13,9},{2,6},{14,10},{3,7},{15,11},{16,20},{28,... | collective-permute-start | bytes 3145736 | tf_op jit(solution)/shard_map/ppermute | solution.py:527
  37.8 13.1 %collective-permute-start.8 = (bf16[1,64,2048]{2,1,0:T(8,128)(2,1)S(1)}, bf16[1,64,2048]{2,1,0:T(8,128)(2,1)S(1)}, u32[]{:S(2)}, u32[]{:S(2)}) collective-permute-start(bf16[1,64,2048]{2,1,0:T(8,128)(2,1)S(1)} %get-tuple-element.27.refs_7_), channel_id=1, source_target_pairs={{4,8},{8,4},{5,9},{9,5},{6,10},{10,6},{7,11},{11,7},{20,24},{24,20... | collective-permute-start | bytes 786440 | tf_op jit(solution)/shard_map/ppermute | solution.py:532
  38.5 12.7 %collective-permute-start.9 = (bf16[1,64,2048]{2,1,0:T(8,128)(2,1)S(1)}, bf16[1,64,2048]{2,1,0:T(8,128)(2,1)S(1)}, u32[]{:S(2)}, u32[]{:S(2)}) collective-permute-start(bf16[1,64,2048]{2,1,0:T(8,128)(2,1)S(1)} %get-tuple-element.31), channel_id=1, source_target_pairs={{4,12},{8,0},{5,13},{9,1},{6,14},{10,2},{7,15},{11,3},{20,28},{24,... | collective-permute-start | bytes 786440 | tf_op jit(solution)/shard_map/ppermute | solution.py:533
  50.3 48.0 %collective-permute-start.7 = (bf16[1664,256]{1,0:T(8,128)(2,1)}, bf16[1664,256]{1,0:T(8,128)(2,1)}, u32[]{:S(2)}, u32[]{:S(2)}) collective-permute-start(bf16[1664,256]{1,0:T(8,128)(2,1)} %get-tuple-element.29), channel_id=1, source_target_pairs={{0,1},{1,0},{2,3},{3,2},{4,5},{5,4},{6,7},{7,6},{8,9},{9,8},{10,11... | collective-permute-start | bytes 2555912 | tf_op jit(solution)/shard_map/ppermute | solution.py:425
  50.3 16.4 %collective-permute-start.11 = (bf16[1664,256]{1,0:T(8,128)(2,1)}, bf16[1664,256]{1,0:T(8,128)(2,1)}, u32[]{:S(2)}, u32[]{:S(2)}) collective-permute-start(bf16[1664,256]{1,0:T(8,128)(2,1)} %get-tuple-element.32.refs_8_), channel_id=1, source_target_pairs={{0,1},{1,0},{2,3},{3,2},{4,5},{5,4},{6,7},{7,6},{8,9},{9,8},{10,11... | collective-permute-start | bytes 2555912 | tf_op jit(solution)/shard_map/ppermute | solution.py:425
  57.7 29.1 %collective-permute-start.16 = (bf16[4,64,2048]{2,1,0:T(8,128)(2,1)S(1)}, bf16[4,64,2048]{2,1,0:T(8,128)(2,1)S(1)}, u32[]{:S(2)}, u32[]{:S(2)}) collective-permute-start(bf16[4,64,2048]{2,1,0:T(8,128)(2,1)S(1)} %add_convert_fusion.1.refs_16_), channel_id=1, source_target_pairs={{0,4},{12,8},{4,12},{8,0},{1,5},{13,9},{5,13},{9,1},{2,6},{14,10},... | collective-permute-start | bytes 3145736 | tf_op jit(solution)/shard_map/ppermute | solution.py:537
  66.1 11.9 %copy-start.10 = (bf16[13,64,128]{2,1,0:T(8,128)(2,1)}, bf16[13,64,128]{2,1,0:T(8,128)(2,1)S(1)}, u32[]{:S(2)}) copy-start(bf16[13,64,128]{2,1,0:T(8,128)(2,1)S(1)} %shard_map.137.refs_1_.refs_4_) | copy-start | bytes 638980
  66.1 3.4 %collective-permute-start.13 = (bf16[13,64,128]{2,1,0:T(8,128)(2,1)S(1)}, bf16[13,64,128]{2,1,0:T(8,128)(2,1)S(1)}, u32[]{:S(2)}, u32[]{:S(2)}) collective-permute-start(bf16[13,64,128]{2,1,0:T(8,128)(2,1)S(1)} %shard_map.137.refs_1_.refs_4_), channel_id=1, source_target_pairs={{0,1},{1,0},{2,3},{3,2},{4,5},{5,4},{6,7},{7,6},{8,9},{9,8},{10,11... | collective-permute-start | bytes 638984 | tf_op jit(solution)/shard_map/ppermute | solution.py:425
  66.1 8.1 %collective-permute-start.14 = (bf16[13,64,128]{2,1,0:T(8,128)(2,1)S(1)}, bf16[13,64,128]{2,1,0:T(8,128)(2,1)S(1)}, u32[]{:S(2)}, u32[]{:S(2)}) collective-permute-start(bf16[13,64,128]{2,1,0:T(8,128)(2,1)S(1)} %shard_map.137.refs_1_.refs_4_), channel_id=1, source_target_pairs={{0,2},{1,3},{2,0},{3,1},{4,6},{5,7},{6,4},{7,5},{8,10},{9,11},{10,... | collective-permute-start | bytes 638984 | tf_op jit(solution)/shard_map/ppermute | solution.py:425
  66.8 11.2 %collective-permute-start.15 = (bf16[13,64,128]{2,1,0:T(8,128)(2,1)S(1)}, bf16[13,64,128]{2,1,0:T(8,128)(2,1)S(1)}, u32[]{:S(2)}, u32[]{:S(2)}) collective-permute-start(bf16[13,64,128]{2,1,0:T(8,128)(2,1)S(1)} %shard_map.137.refs_1_.refs_4_), channel_id=1, source_target_pairs={{0,3},{1,2},{2,1},{3,0},{4,7},{5,6},{6,5},{7,4},{8,11},{9,10},{10,... | collective-permute-start | bytes 638984 | tf_op jit(solution)/shard_map/ppermute | solution.py:425
  69.4 12.9 %copy-start.13 = (bf16[13,64,128]{2,1,0:T(8,128)(2,1)}, bf16[13,64,128]{2,1,0:T(8,128)(2,1)S(1)}, u32[]{:S(2)}) copy-start(bf16[13,64,128]{2,1,0:T(8,128)(2,1)S(1)} %collective-permute-done.13.refs_2_.refs_5_) | copy-start | bytes 638980
  69.4 28.9 %collective-permute-start.12 = (bf16[1664,256]{1,0:T(8,128)(2,1)S(1)}, bf16[1664,256]{1,0:T(8,128)(2,1)S(1)}, u32[]{:S(2)}, u32[]{:S(2)}) collective-permute-start(bf16[1664,256]{1,0:T(8,128)(2,1)S(1)} %add_convert_fusion.2), channel_id=1, source_target_pairs={{0,2},{1,3},{2,0},{3,1},{4,6},{5,7},{6,4},{7,5},{8,10},{9,11},{10,... | collective-permute-start | bytes 2555912 | tf_op jit(solution)/shard_map/ppermute | solution.py:425
  78.8 11.0 %collective-permute-start.19 = (bf16[4,64,256]{2,1,0:T(8,128)(2,1)S(1)}, bf16[4,64,256]{2,1,0:T(8,128)(2,1)S(1)}, u32[]{:S(2)}, u32[]{:S(2)}) collective-permute-start(bf16[4,64,256]{2,1,0:T(8,128)(2,1)S(1)} %get-tuple-element.38), channel_id=1, source_target_pairs={{0,12},{4,0},{8,4},{12,8},{1,13},{5,1},{9,5},{13,9},{2,14},{6,2},{... | collective-permute-start | bytes 393224 | tf_op jit(solution)/shard_map/ppermute | solution.py:407
  82.3 13.6 %collective-permute-start.18 = (bf16[4,64,256]{2,1,0:T(8,128)(2,1)S(1)}, bf16[4,64,256]{2,1,0:T(8,128)(2,1)S(1)}, u32[]{:S(2)}, u32[]{:S(2)}) collective-permute-start(bf16[4,64,256]{2,1,0:T(8,128)(2,1)S(1)} %get-tuple-element.37), channel_id=1, source_target_pairs={{0,8},{4,12},{8,0},{12,4},{1,9},{5,13},{9,1},{13,5},{2,10},{6,14},... | collective-permute-start | bytes 393224 | tf_op jit(solution)/shard_map/ppermute | solution.py:407
  86.8 10.8 %collective-permute-start.17 = (bf16[4,64,256]{2,1,0:T(8,128)(2,1)S(1)}, bf16[4,64,256]{2,1,0:T(8,128)(2,1)S(1)}, u32[]{:S(2)}, u32[]{:S(2)}) collective-permute-start(bf16[4,64,256]{2,1,0:T(8,128)(2,1)S(1)} %get-tuple-element.36), channel_id=1, source_target_pairs={{0,4},{4,8},{8,12},{12,0},{1,5},{5,9},{9,13},{13,1},{2,6},{6,10},{... | collective-permute-start | bytes 393224 | tf_op jit(solution)/shard_map/ppermute | solution.py:407
  89.8 30.3 %collective-permute-start.24 = (bf16[4,64,2048]{2,1,0:T(8,128)(2,1)}, bf16[4,64,2048]{2,1,0:T(8,128)(2,1)}, u32[]{:S(2)}, u32[]{:S(2)}) collective-permute-start(bf16[4,64,2048]{2,1,0:T(8,128)(2,1)} %shard_map.144.refs_1_), channel_id=1, source_target_pairs={{0,4},{12,8},{4,0},{8,12},{1,5},{13,9},{5,1},{9,13},{2,6},{14,10},... | collective-permute-start | bytes 3145736 | tf_op jit(solution)/shard_map/ppermute | solution.py:547
  96.0 24.1 %collective-permute-start.23 = (bf16[4,64,2048]{2,1,0:T(8,128)(2,1)S(1)}, bf16[4,64,2048]{2,1,0:T(8,128)(2,1)}, u32[]{:S(2)}, u32[]{:S(2)}) collective-permute-start(bf16[4,64,2048]{2,1,0:T(8,128)(2,1)S(1)} %shard_map.145), channel_id=1, source_target_pairs={{4,8},{8,4},{5,9},{9,5},{6,10},{10,6},{7,11},{11,7},{20,24},{24,20... | collective-permute-start | bytes 3145736 | tf_op jit(solution)/shard_map/ppermute | solution.py:545
  103.7 18.5 %collective-permute-start.20 = (bf16[128,256]{1,0:T(8,128)(2,1)}, bf16[128,256]{1,0:T(8,128)(2,1)S(1)}, u32[]{:S(2)}, u32[]{:S(2)}) collective-permute-start(bf16[128,256]{1,0:T(8,128)(2,1)} %get-tuple-element.39.refs_2_), channel_id=1, source_target_pairs={{0,4},{4,8},{8,12},{12,0},{1,5},{5,9},{9,13},{13,1},{2,6},{6,10},{... | collective-permute-start | bytes 196616 | tf_op jit(solution)/shard_map/ppermute | solution.py:407
  103.9 20.4 %collective-permute-start.21 = (bf16[128,256]{1,0:T(8,128)(2,1)}, bf16[128,256]{1,0:T(8,128)(2,1)S(1)}, u32[]{:S(2)}, u32[]{:S(2)}) collective-permute-start(bf16[128,256]{1,0:T(8,128)(2,1)} %get-tuple-element.39.refs_2_), channel_id=1, source_target_pairs={{0,8},{4,12},{8,0},{12,4},{1,9},{5,13},{9,1},{13,5},{2,10},{6,14},... | collective-permute-start | bytes 196616 | tf_op jit(solution)/shard_map/ppermute | solution.py:407
  105.8 18.5 %collective-permute-start.22 = (bf16[128,256]{1,0:T(8,128)(2,1)}, bf16[128,256]{1,0:T(8,128)(2,1)S(1)}, u32[]{:S(2)}, u32[]{:S(2)}) collective-permute-start(bf16[128,256]{1,0:T(8,128)(2,1)} %get-tuple-element.39.refs_2_), channel_id=1, source_target_pairs={{0,12},{4,0},{8,4},{12,8},{1,13},{5,1},{9,5},{13,9},{2,14},{6,2},{... | collective-permute-start | bytes 196616 | tf_op jit(solution)/shard_map/ppermute | solution.py:407
  107.9 16.4 %copy-start.16 = (bf16[128,256]{1,0:T(8,128)(2,1)S(1)}, bf16[128,256]{1,0:T(8,128)(2,1)}, u32[]{:S(2)}) copy-start(bf16[128,256]{1,0:T(8,128)(2,1)} %get-tuple-element.39.refs_2_) | copy-start | bytes 196612
  (22 other events, 119.7 us)

commit v17 on v16

--- a/solution.py
+++ b/solution.py
@@ -148,6 +148,7 @@
             (shape, features.dtype, constant_spec(shape)),
         ],
         aliases={4 + len(choices): 0},
+        vmem=60,
     )
 
 

time: 126 us -> 126 us (level)
  local copies, waits for them, and re-layouts: 9.02 us -> 6.56 us
  Pallas kernels: 33.2 us -> 35 us
  waiting for transfers between devices: 34.2 us -> 35.6 us
    unnamed x58 -> x56, local copies, waits for them, and re-layouts: 8.85 us -> 6.4 us
    pallas_call x17, Pallas kernels: 33.2 us -> 35 us  [call(): pl.pallas_call(run, grid_spec=pltpu.PrefetchScalarGridSpec(num_scalar_pre...]
  transfers between devices with their start and end apart: 25 -> 25, of which waited for: 11 -> 11; matrix products, arithmetic and copies ran while one was open for 8% -> 7% of each run, Pallas kernels for 22% -> 22%
where the time goes in v17:
time: 126 us; the launch traced here: 125 us
  starting transfers between devices  37.9 us (30%)
  waiting for transfers between devices  35.6 us (28%)
  Pallas kernels  35 us (28%)
  other arithmetic  9.26 us (7%)
  local copies, waits for them, and re-layouts  6.56 us (5%)
    pallas_call x17, Pallas kernels, call(): pl.pallas_call(run, grid_spec=pltpu.PrefetchScalarGridSpec(num_scalar_pre...  35 us
    ppermute x9, starting transfers between devices, shift(): lax.ppermute(array, 'dp', [(i, (i + by) % size) for i in range(size)])  13.6 us
    ppermute x1, waiting for transfers between devices, body(): from_third = lax.ppermute(third, 'dp', [(0, 1), (3, 2), (1, 0), (2, 3)])  12.6 us
    ppermute x8, waiting for transfers between devices, crossed(): lax.ppermute(array, 'tensor', [(i, i ^ by) for i in range(lax.axis_size('...  10.7 us
    unnamed x56, local copies, waits for them, and re-layouts  6.4 us
    ppermute x9, waiting for transfers between devices, shift(): lax.ppermute(array, 'dp', [(i, (i + by) % size) for i in range(size)])  5.82 us
    convert_element_type x5, other arithmetic, add(): sum((array.astype(jnp.float32) for array in arrays)).astype(arrays[0].dtype)  5.5 us
    ppermute x8, starting transfers between devices, crossed(): lax.ppermute(array, 'tensor', [(i, i ^ by) for i in range(lax.axis_size('...  4.6 us
  transfers between devices with their start and end apart: 25, of which 11 were waited for; matrix products, arithmetic and copies ran while one was open for 7% of the time, Pallas kernels for 22%

profile of v17, /device:TPU:0, one launch (start us, length us, event | category | flops | bytes accessed | tf_op | source)
XLA Modules:
  0.0 125.3 jit_solution(15286080674095362868)
XLA Ops:
  0.7 3.2 %shard_map.130 = (bf16[13,64,128]{2,1,0:T(8,128)(2,1)}, bf16[1,64,256]{2,1,0:T(8,128)(2,1)}, bf16[1,64,2048]{2,1,0:T(8,128)(2,1)}) custom-call(s32[13]{0:T(128)} %refs_0_.10, bf16[13,64,256]{2,1,0:T(8,128)(2,1)} %refs_8_.3, bf16[1664,256]{1,0:T(8,128)(2,1)} %refs_5_.9, bf16[13,64,2048]{2,1,0:T(8,128)(2,1)} %refs_6_.5), custom_call_target="tpu_custom_call" | custom-call | flops 1000000000 | bytes 360000 | tf_op jit(solution)/shard_map/pallas_call | solution.py:24
  3.9 3.0 %collective-permute-start = (bf16[1,64,256]{2,1,0:T(8,128)(2,1)}, bf16[1,64,256]{2,1,0:T(8,128)(2,1)S(1)}, u32[]{:S(2)}, u32[]{:S(2)}) collective-permute-start(bf16[1,64,256]{2,1,0:T(8,128)(2,1)} %get-tuple-element.23.refs_3_), channel_id=1, source_target_pairs={{0,4},{4,8},{8,12},{12,0},{1,5},{5,9},{9,13},{13,1},{2,6},{6,10},{... | collective-permute-start | bytes 98312 | tf_op jit(solution)/shard_map/ppermute | solution.py:408
  6.9 2.6 %collective-permute-start.1 = (bf16[1,64,256]{2,1,0:T(8,128)(2,1)}, bf16[1,64,256]{2,1,0:T(8,128)(2,1)S(1)}, u32[]{:S(2)}, u32[]{:S(2)}) collective-permute-start(bf16[1,64,256]{2,1,0:T(8,128)(2,1)} %get-tuple-element.23.refs_3_), channel_id=1, source_target_pairs={{0,8},{4,12},{8,0},{12,4},{1,9},{5,13},{9,1},{13,5},{2,10},{6,14},... | collective-permute-start | bytes 98312 | tf_op jit(solution)/shard_map/ppermute | solution.py:408
  9.5 1.3 %collective-permute-start.2 = (bf16[1,64,256]{2,1,0:T(8,128)(2,1)}, bf16[1,64,256]{2,1,0:T(8,128)(2,1)S(1)}, u32[]{:S(2)}, u32[]{:S(2)}) collective-permute-start(bf16[1,64,256]{2,1,0:T(8,128)(2,1)} %get-tuple-element.23.refs_3_), channel_id=1, source_target_pairs={{0,12},{4,0},{8,4},{12,8},{1,13},{5,1},{9,5},{13,9},{2,14},{6,2},{... | collective-permute-start | bytes 98312 | tf_op jit(solution)/shard_map/ppermute | solution.py:408
  14.2 2.5 %shard_map.131 = (bf16[13,64,128]{2,1,0:T(8,128)(2,1)}, bf16[1,64,256]{2,1,0:T(8,128)(2,1)}) custom-call(s32[13]{0:T(128)} %refs_0_.10, s32[4]{0:T(128)} %refs_0_.11, s32[1]{0:T(128)} %bitcast.refs_2_.refs_1_, bf16[1,64,256]{2,1,0:T(8,128)(2,1)} %get-tuple-element.23.refs_3_, bf16[1,64,256]{2,1,0:T(8,128)(2,1)} %copy-done.20, ...), custom_call_target="tpu_custom_call", output_to_operand_aliasing={{0}: (8, {})} | custom-call | flops 1000000000 | bytes 360000 | tf_op jit(solution)/shard_map/pallas_call | solution.py:24
  16.8 1.6 %collective-permute-done.3 = bf16[13,64,128]{2,1,0:T(8,128)(2,1)S(1)} collective-permute-done((bf16[13,64,128]{2,1,0:T(8,128)(2,1)}, bf16[13,64,128]{2,1,0:T(8,128)(2,1)S(1)}, u32[]{:S(2)}, u32[]{:S(2)}) %collective-permute-start.3) | collective-permute-done | bytes 213024 | tf_op jit(solution)/shard_map/ppermute | solution.py:426
  19.4 1.6 %collective-permute-start.4 = (bf16[13,64,128]{2,1,0:T(8,128)(2,1)S(1)}, bf16[13,64,128]{2,1,0:T(8,128)(2,1)S(1)}, u32[]{:S(2)}, u32[]{:S(2)}) collective-permute-start(bf16[13,64,128]{2,1,0:T(8,128)(2,1)S(1)} %add_convert_fusion.3.refs_1_), channel_id=1, source_target_pairs={{0,2},{1,3},{2,0},{3,1},{4,6},{5,7},{6,4},{7,5},{8,10},{9,11},{10,... | collective-permute-start | bytes 638984 | tf_op jit(solution)/shard_map/ppermute | solution.py:426
  21.0 2.8 %collective-permute-start.5 = (bf16[1,64,2048]{2,1,0:T(8,128)(2,1)S(1)}, bf16[1,64,2048]{2,1,0:T(8,128)(2,1)}, u32[]{:S(2)}, u32[]{:S(2)}) collective-permute-start(bf16[1,64,2048]{2,1,0:T(8,128)(2,1)S(1)} %shard_map.133.refs_2_.refs_11_), channel_id=1, source_target_pairs={{0,4},{4,8},{8,12},{1,5},{5,9},{9,13},{2,6},{6,10},{10,14},{3,7},{... | collective-permute-start | bytes 786440 | tf_op jit(solution)/shard_map/ppermute | solution.py:529
  26.8 2.9 %copy-done = bf16[1664,2048]{1,0:T(8,128)(2,1)S(1)} copy-done((bf16[1664,2048]{1,0:T(8,128)(2,1)S(1)}, bf16[1664,2048]{1,0:T(8,128)(2,1)}, u32[]{:S(2)}) %copy-start) | copy-done | bytes 6815768
  29.7 2.4 %shard_map.132.refs_5_.refs_6_.refs_0_ = bf16[4,64,2048]{2,1,0:T(8,128)(2,1)} custom-call(s32[16]{0:T(128)S(1)} %get-tuple-element.44.refs_0_, bf16[13,64,128]{2,1,0:T(8,128)(2,1)S(1)} %add_convert_fusion.3.refs_1_, bf16[13,64,128]{2,1,0:T(8,128)(2,1)S(1)} %collective-permute-done.4.refs_2_, bf16[1664,2048]{1,0:T(8,128)(2,1)S(1)} %copy-done, ...), custom_call_target="tpu_custom_call" | custom-call | flops 1000000000 | bytes 360000 | tf_op jit(solution)/shard_map/pallas_call | solution.py:24
  32.1 4.4 %collective-permute-start.10 = (bf16[4,64,2048]{2,1,0:T(8,128)(2,1)}, bf16[4,64,2048]{2,1,0:T(8,128)(2,1)}, u32[]{:S(2)}, u32[]{:S(2)}) collective-permute-start(bf16[4,64,2048]{2,1,0:T(8,128)(2,1)} %shard_map.132.refs_5_.refs_6_.refs_0_), channel_id=1, source_target_pairs={{0,4},{12,8},{1,5},{13,9},{2,6},{14,10},{3,7},{15,11},{16,20},{28,... | collective-permute-start | bytes 3145736 | tf_op jit(solution)/shard_map/ppermute | solution.py:528
  36.6 1.6 %shard_map.134 = (bf16[1,64,2048]{2,1,0:T(8,128)(2,1)S(1)}, bf16[1,64,2048]{2,1,0:T(8,128)(2,1)S(1)}) custom-call(s32[4]{0:T(128)S(1)} %copy-done.16, s32[1]{0:T(128)} %bitcast.refs_2_.refs_1_, bf16[1,64,2048]{2,1,0:T(8,128)(2,1)S(1)} %shard_map.133.refs_2_.refs_11_, bf16[1,64,2048]{2,1,0:T(8,128)(2,1)} %collective-permute-done.5.refs_3_.refs_12_, ...), custom_call_target="tpu_custom_call" | custom-call | flops 1000000000 | bytes 360000 | tf_op jit(solution)/shard_map/pallas_call | solution.py:24
  40.2 9.6 %shard_map.135 = (bf16[1664,256]{1,0:T(8,128)(2,1)}, bf16[1664,256]{1,0:T(8,128)(2,1)S(1)}, bf16[1664,256]{1,0:T(8,128)(2,1)}, bf16[1664,256]{1,0:T(8,128)(2,1)S(1)}) custom-call(s32[4]{0:T(128)S(1)} %pad_add_fusion.refs_0_, bf16[1664,2048]{1,0:T(8,128)(2,1)S(1)} %bitcast.8, bf16[2048,1024]{1,0:T(8,128)(2,1)S(1)} %copy-done.11, ...), custom_call_target="tpu_custom_call" | custom-call | flops 99999997952 | bytes 36000000 | tf_op jit(solution)/shard_map/pallas_call | solution.py:24
  51.3 4.5 %shard_map.136 = (bf16[4,64,2048]{2,1,0:T(8,128)(2,1)S(1)}, bf16[4,64,2048]{2,1,0:T(8,128)(2,1)}, bf16[4,64,2048]{2,1,0:T(8,128)(2,1)S(1)}) custom-call(s32[16]{0:T(128)S(1)} %get-tuple-element.44.refs_0_, bf16[13,64,128]{2,1,0:T(8,128)(2,1)S(1)} %add_convert_fusion.3.refs_1_, bf16[13,64,128]{2,1,0:T(8,128)(2,1)S(1)} %collective-permute-done.4.refs_2_, ...), custom_call_target="tpu_custom_call" | custom-call | flops 99999997952 | bytes 36000000 | tf_op jit(solution)/shard_map/pallas_call | solution.py:24
  55.9 1.9 %collective-permute-done.10 = bf16[4,64,2048]{2,1,0:T(8,128)(2,1)} collective-permute-done((bf16[4,64,2048]{2,1,0:T(8,128)(2,1)}, bf16[4,64,2048]{2,1,0:T(8,128)(2,1)}, u32[]{:S(2)}, u32[]{:S(2)}) %collective-permute-start.10) | collective-permute-done | bytes 1048608 | tf_op jit(solution)/shard_map/ppermute | solution.py:528
  58.2 3.8 %collective-permute-start.16 = (bf16[4,64,2048]{2,1,0:T(8,128)(2,1)S(1)}, bf16[4,64,2048]{2,1,0:T(8,128)(2,1)S(1)}, u32[]{:S(2)}, u32[]{:S(2)}) collective-permute-start(bf16[4,64,2048]{2,1,0:T(8,128)(2,1)S(1)} %add_convert_fusion.1.refs_16_), channel_id=1, source_target_pairs={{0,4},{12,8},{4,12},{8,0},{1,5},{13,9},{5,13},{9,1},{2,6},{14,10},... | collective-permute-start | bytes 3145736 | tf_op jit(solution)/shard_map/ppermute | solution.py:538
  61.9 4.6 %shard_map.137.refs_1_.refs_4_ = bf16[13,64,128]{2,1,0:T(8,128)(2,1)S(1)} custom-call(s32[13]{0:T(128)S(1)} %copy-done.10, s32[4]{0:T(128)S(1)} %copy-done.17, s32[1]{0:T(128)} %bitcast.refs_2_.refs_1_, bf16[13,64,2048]{2,1,0:T(8,128)(2,1)S(1)} %copy-done.5, bf16[13,64,2048]{2,1,0:T(8,128)(2,1)S(1)} %copy-done.5, bf16[13,64,2048]{2,1,0:T(8,128)(2,1)S(1)} %copy-done.5, ...), custom_call_target="tpu_custom_call" | custom-call | flops 99999997952 | bytes 36000000 | tf_op jit(solution)/shard_map/pallas_call | solution.py:24
  68.5 1.4 %add_convert_fusion.2 = bf16[1664,256]{1,0:T(8,128)(2,1)S(1)} fusion(bf16[1664,256]{1,0:T(8,128)(2,1)} %collective-permute-done.11, bf16[1664,256]{1,0:T(8,128)(2,1)S(1)} %shard_map.138), kind=kLoop, calls=%fused_computation.6 | loop fusion | flops 1703936 | bytes 2555904 | tf_op jit(solution)/shard_map/convert_element_type | solution.py:422
  70.5 4.2 %collective-permute-done.14.refs_3_.refs_6_ = bf16[13,64,128]{2,1,0:T(8,128)(2,1)S(1)} collective-permute-done((bf16[13,64,128]{2,1,0:T(8,128)(2,1)S(1)}, bf16[13,64,128]{2,1,0:T(8,128)(2,1)S(1)}, u32[]{:S(2)}, u32[]{:S(2)}) %collective-permute-start.14) | collective-permute-done | bytes 213024 | tf_op jit(solution)/shard_map/ppermute | solution.py:426
  74.7 3.7 %collective-permute-done.15.refs_4_.refs_7_ = bf16[13,64,128]{2,1,0:T(8,128)(2,1)S(1)} collective-permute-done((bf16[13,64,128]{2,1,0:T(8,128)(2,1)S(1)}, bf16[13,64,128]{2,1,0:T(8,128)(2,1)S(1)}, u32[]{:S(2)}, u32[]{:S(2)}) %collective-permute-start.15) | collective-permute-done | bytes 213024 | tf_op jit(solution)/shard_map/ppermute | solution.py:426
  79.2 2.8 %collective-permute-start.19 = (bf16[4,64,256]{2,1,0:T(8,128)(2,1)S(1)}, bf16[4,64,256]{2,1,0:T(8,128)(2,1)S(1)}, u32[]{:S(2)}, u32[]{:S(2)}) collective-permute-start(bf16[4,64,256]{2,1,0:T(8,128)(2,1)S(1)} %get-tuple-element.38), channel_id=1, source_target_pairs={{0,12},{4,0},{8,4},{12,8},{1,13},{5,1},{9,5},{13,9},{2,14},{6,2},{... | collective-permute-start | bytes 393224 | tf_op jit(solution)/shard_map/ppermute | solution.py:408
  82.1 4.5 %collective-permute-done.16.refs_1_ = bf16[4,64,2048]{2,1,0:T(8,128)(2,1)S(1)} collective-permute-done((bf16[4,64,2048]{2,1,0:T(8,128)(2,1)S(1)}, bf16[4,64,2048]{2,1,0:T(8,128)(2,1)S(1)}, u32[]{:S(2)}, u32[]{:S(2)}) %collective-permute-start.16) | collective-permute-done | bytes 1048608 | tf_op jit(solution)/shard_map/ppermute | solution.py:538
  86.6 2.0 %fusion.refs_1_.refs_0_ = bf16[4,64,2048]{2,1,0:T(8,128)(2,1)S(1)} fusion(bf16[4,64,2048]{2,1,0:T(8,128)(2,1)S(1)} %collective-permute-done.16.refs_1_, bf16[4,64,2048]{2,1,0:T(8,128)(2,1)} %shard_map.140), kind=kLoop, calls=%fused_computation.2 | loop fusion | flops 2097152 | bytes 3145728 | tf_op jit(solution)/shard_map/convert_element_type | solution.py:422
  89.6 3.8 %collective-permute-start.24 = (bf16[4,64,2048]{2,1,0:T(8,128)(2,1)}, bf16[4,64,2048]{2,1,0:T(8,128)(2,1)}, u32[]{:S(2)}, u32[]{:S(2)}) collective-permute-start(bf16[4,64,2048]{2,1,0:T(8,128)(2,1)} %shard_map.144.refs_1_), channel_id=1, source_target_pairs={{0,4},{12,8},{4,0},{8,12},{1,5},{13,9},{5,1},{9,13},{2,6},{14,10},... | collective-permute-start | bytes 3145736 | tf_op jit(solution)/shard_map/ppermute | solution.py:548
  93.4 2.3 %collective-permute-done.18 = bf16[4,64,256]{2,1,0:T(8,128)(2,1)S(1)} collective-permute-done((bf16[4,64,256]{2,1,0:T(8,128)(2,1)S(1)}, bf16[4,64,256]{2,1,0:T(8,128)(2,1)S(1)}, u32[]{:S(2)}, u32[]{:S(2)}) %collective-permute-start.18) | collective-permute-done | bytes 131104 | tf_op jit(solution)/shard_map/ppermute | solution.py:408
  95.7 1.6 %collective-permute-start.23 = (bf16[4,64,2048]{2,1,0:T(8,128)(2,1)S(1)}, bf16[4,64,2048]{2,1,0:T(8,128)(2,1)}, u32[]{:S(2)}, u32[]{:S(2)}) collective-permute-start(bf16[4,64,2048]{2,1,0:T(8,128)(2,1)S(1)} %shard_map.145), channel_id=1, source_target_pairs={{4,8},{8,4},{5,9},{9,5},{6,10},{10,6},{7,11},{11,7},{20,24},{24,20... | collective-permute-start | bytes 3145736 | tf_op jit(solution)/shard_map/ppermute | solution.py:546
  99.0 4.4 %shard_map.142 = (bf16[1664,256]{1,0:T(8,128)(2,1)}, bf16[128,256]{1,0:T(8,128)(2,1)}) custom-call(s32[13]{0:T(128)} %refs_0_.10, bf16[1664,256]{1,0:T(8,128)(2,1)} %copy-done.18, bf16[1664,256]{1,0:T(8,128)(2,1)} %collective-permute-done.7.refs_2_, bf16[1664,256]{1,0:T(8,128)(2,1)} %copy-done.19, bf16[13,64,128]{2,1,0:T(8,128)(2,1)} %copy-done.9, ...), custom_call_target="tpu_custom_call" | custom-call | flops 99999997952 | bytes 36000000 | tf_op jit(solution)/shard_map/pallas_call | solution.py:24
  103.6 2.0 %collective-permute-start.21 = (bf16[128,256]{1,0:T(8,128)(2,1)}, bf16[128,256]{1,0:T(8,128)(2,1)S(1)}, u32[]{:S(2)}, u32[]{:S(2)}) collective-permute-start(bf16[128,256]{1,0:T(8,128)(2,1)} %get-tuple-element.39.refs_2_), channel_id=1, source_target_pairs={{0,8},{4,12},{8,0},{12,4},{1,9},{5,13},{9,1},{13,5},{2,10},{6,14},... | collective-permute-start | bytes 196616 | tf_op jit(solution)/shard_map/ppermute | solution.py:408
  105.6 1.7 %collective-permute-start.22 = (bf16[128,256]{1,0:T(8,128)(2,1)}, bf16[128,256]{1,0:T(8,128)(2,1)S(1)}, u32[]{:S(2)}, u32[]{:S(2)}) collective-permute-start(bf16[128,256]{1,0:T(8,128)(2,1)} %get-tuple-element.39.refs_2_), channel_id=1, source_target_pairs={{0,12},{4,0},{8,4},{12,8},{1,13},{5,1},{9,5},{13,9},{2,14},{6,2},{... | collective-permute-start | bytes 196616 | tf_op jit(solution)/shard_map/ppermute | solution.py:408
  107.6 12.6 %collective-permute-done.24 = bf16[4,64,2048]{2,1,0:T(8,128)(2,1)} collective-permute-done((bf16[4,64,2048]{2,1,0:T(8,128)(2,1)}, bf16[4,64,2048]{2,1,0:T(8,128)(2,1)}, u32[]{:S(2)}, u32[]{:S(2)}) %collective-permute-start.24) | collective-permute-done | bytes 1048608 | tf_op jit(solution)/shard_map/ppermute | solution.py:548
  120.2 2.1 %add_convert_fusion.refs_7_ = bf16[4,64,2048]{2,1,0:T(8,128)(2,1)S(1)} fusion(bf16[4,64,2048]{2,1,0:T(8,128)(2,1)} %collective-permute-done.24, f32[4,64,2048]{2,1,0:T(8,128)S(1)} %fusion.1, bf16[4,64,2048]{2,1,0:T(8,128)(2,1)} %collective-permute-done.23), kind=kLoop, calls=%fused_computation.4 | loop fusion | flops 2621440 | bytes 5242880 | tf_op jit(solution)/shard_map/convert_element_type | solution.py:552
  122.3 1.7 %collective-permute-done.21.refs_4_ = bf16[128,256]{1,0:T(8,128)(2,1)S(1)} collective-permute-done((bf16[128,256]{1,0:T(8,128)(2,1)}, bf16[128,256]{1,0:T(8,128)(2,1)S(1)}, u32[]{:S(2)}, u32[]{:S(2)}) %collective-permute-start.21) | collective-permute-done | bytes 65568 | tf_op jit(solution)/shard_map/ppermute | solution.py:408
  (109 shorter events, 19.1 us)
Async XLA Ops:
  3.9 7.9 %collective-permute-start = (bf16[1,64,256]{2,1,0:T(8,128)(2,1)}, bf16[1,64,256]{2,1,0:T(8,128)(2,1)S(1)}, u32[]{:S(2)}, u32[]{:S(2)}) collective-permute-start(bf16[1,64,256]{2,1,0:T(8,128)(2,1)} %get-tuple-element.23.refs_3_), channel_id=1, source_target_pairs={{0,4},{4,8},{8,12},{12,0},{1,5},{5,9},{9,13},{13,1},{2,6},{6,10},{... | collective-permute-start | bytes 98312 | tf_op jit(solution)/shard_map/ppermute | solution.py:408
  6.9 5.4 %collective-permute-start.1 = (bf16[1,64,256]{2,1,0:T(8,128)(2,1)}, bf16[1,64,256]{2,1,0:T(8,128)(2,1)S(1)}, u32[]{:S(2)}, u32[]{:S(2)}) collective-permute-start(bf16[1,64,256]{2,1,0:T(8,128)(2,1)} %get-tuple-element.23.refs_3_), channel_id=1, source_target_pairs={{0,8},{4,12},{8,0},{12,4},{1,9},{5,13},{9,1},{13,5},{2,10},{6,14},... | collective-permute-start | bytes 98312 | tf_op jit(solution)/shard_map/ppermute | solution.py:408
  9.5 4.1 %collective-permute-start.2 = (bf16[1,64,256]{2,1,0:T(8,128)(2,1)}, bf16[1,64,256]{2,1,0:T(8,128)(2,1)S(1)}, u32[]{:S(2)}, u32[]{:S(2)}) collective-permute-start(bf16[1,64,256]{2,1,0:T(8,128)(2,1)} %get-tuple-element.23.refs_3_), channel_id=1, source_target_pairs={{0,12},{4,0},{8,4},{12,8},{1,13},{5,1},{9,5},{13,9},{2,14},{6,2},{... | collective-permute-start | bytes 98312 | tf_op jit(solution)/shard_map/ppermute | solution.py:408
  14.2 26.0 %slice-start = ((s8[6815744]{0:T(1024)(128)(4,1)}), s8[2621440]{0:T(1024)(128)(4,1)S(1)}, s32[]{:S(2)}) async-start(s8[6815744]{0:T(1024)(128)(4,1)} %bitcast.7), calls=%async_computation | async-start | bytes 5242880
  16.7 1.7 %collective-permute-start.3 = (bf16[13,64,128]{2,1,0:T(8,128)(2,1)}, bf16[13,64,128]{2,1,0:T(8,128)(2,1)S(1)}, u32[]{:S(2)}, u32[]{:S(2)}) collective-permute-start(bf16[13,64,128]{2,1,0:T(8,128)(2,1)} %get-tuple-element.25), channel_id=1, source_target_pairs={{0,1},{1,0},{2,3},{3,2},{4,5},{5,4},{6,7},{7,6},{8,9},{9,8},{10,11... | collective-permute-start | bytes 638984 | tf_op jit(solution)/shard_map/ppermute | solution.py:426
  19.4 7.4 %collective-permute-start.4 = (bf16[13,64,128]{2,1,0:T(8,128)(2,1)S(1)}, bf16[13,64,128]{2,1,0:T(8,128)(2,1)S(1)}, u32[]{:S(2)}, u32[]{:S(2)}) collective-permute-start(bf16[13,64,128]{2,1,0:T(8,128)(2,1)S(1)} %add_convert_fusion.3.refs_1_), channel_id=1, source_target_pairs={{0,2},{1,3},{2,0},{3,1},{4,6},{5,7},{6,4},{7,5},{8,10},{9,11},{10,... | collective-permute-start | bytes 638984 | tf_op jit(solution)/shard_map/ppermute | solution.py:426
  21.0 15.6 %collective-permute-start.5 = (bf16[1,64,2048]{2,1,0:T(8,128)(2,1)S(1)}, bf16[1,64,2048]{2,1,0:T(8,128)(2,1)}, u32[]{:S(2)}, u32[]{:S(2)}) collective-permute-start(bf16[1,64,2048]{2,1,0:T(8,128)(2,1)S(1)} %shard_map.133.refs_2_.refs_11_), channel_id=1, source_target_pairs={{0,4},{4,8},{8,12},{1,5},{5,9},{9,13},{2,6},{6,10},{10,14},{3,7},{... | collective-permute-start | bytes 786440 | tf_op jit(solution)/shard_map/ppermute | solution.py:529
  23.8 12.8 %collective-permute-start.6 = (bf16[1,64,2048]{2,1,0:T(8,128)(2,1)S(1)}, bf16[1,64,2048]{2,1,0:T(8,128)(2,1)}, u32[]{:S(2)}, u32[]{:S(2)}) collective-permute-start(bf16[1,64,2048]{2,1,0:T(8,128)(2,1)S(1)} %shard_map.133.refs_2_.refs_11_), channel_id=1, source_target_pairs={{12,8},{8,4},{4,0},{13,9},{9,5},{5,1},{14,10},{10,6},{6,2},{15,11}... | collective-permute-start | bytes 786440 | tf_op jit(solution)/shard_map/ppermute | solution.py:530
  29.7 10.5 %copy-start.11 = (bf16[2048,1024]{1,0:T(8,128)(2,1)S(1)}, bf16[2048,1024]{1,0:T(8,128)(2,1)}, u32[]{:S(2)}) copy-start(bf16[2048,1024]{1,0:T(8,128)(2,1)} %refs_5_.6) | copy-start | bytes 12582916
  32.1 25.6 %collective-permute-start.10 = (bf16[4,64,2048]{2,1,0:T(8,128)(2,1)}, bf16[4,64,2048]{2,1,0:T(8,128)(2,1)}, u32[]{:S(2)}, u32[]{:S(2)}) collective-permute-start(bf16[4,64,2048]{2,1,0:T(8,128)(2,1)} %shard_map.132.refs_5_.refs_6_.refs_0_), channel_id=1, source_target_pairs={{0,4},{12,8},{1,5},{13,9},{2,6},{14,10},{3,7},{15,11},{16,20},{28,... | collective-permute-start | bytes 3145736 | tf_op jit(solution)/shard_map/ppermute | solution.py:528
  38.2 13.1 %collective-permute-start.8 = (bf16[1,64,2048]{2,1,0:T(8,128)(2,1)S(1)}, bf16[1,64,2048]{2,1,0:T(8,128)(2,1)S(1)}, u32[]{:S(2)}, u32[]{:S(2)}) collective-permute-start(bf16[1,64,2048]{2,1,0:T(8,128)(2,1)S(1)} %get-tuple-element.27.refs_7_), channel_id=1, source_target_pairs={{4,8},{8,4},{5,9},{9,5},{6,10},{10,6},{7,11},{11,7},{20,24},{24,20... | collective-permute-start | bytes 786440 | tf_op jit(solution)/shard_map/ppermute | solution.py:533
  38.9 12.4 %collective-permute-start.9 = (bf16[1,64,2048]{2,1,0:T(8,128)(2,1)S(1)}, bf16[1,64,2048]{2,1,0:T(8,128)(2,1)S(1)}, u32[]{:S(2)}, u32[]{:S(2)}) collective-permute-start(bf16[1,64,2048]{2,1,0:T(8,128)(2,1)S(1)} %get-tuple-element.31), channel_id=1, source_target_pairs={{4,12},{8,0},{5,13},{9,1},{6,14},{10,2},{7,15},{11,3},{20,28},{24,... | collective-permute-start | bytes 786440 | tf_op jit(solution)/shard_map/ppermute | solution.py:534
  50.8 47.3 %collective-permute-start.7 = (bf16[1664,256]{1,0:T(8,128)(2,1)}, bf16[1664,256]{1,0:T(8,128)(2,1)}, u32[]{:S(2)}, u32[]{:S(2)}) collective-permute-start(bf16[1664,256]{1,0:T(8,128)(2,1)} %get-tuple-element.29), channel_id=1, source_target_pairs={{0,1},{1,0},{2,3},{3,2},{4,5},{5,4},{6,7},{7,6},{8,9},{9,8},{10,11... | collective-permute-start | bytes 2555912 | tf_op jit(solution)/shard_map/ppermute | solution.py:426
  50.8 16.4 %collective-permute-start.11 = (bf16[1664,256]{1,0:T(8,128)(2,1)}, bf16[1664,256]{1,0:T(8,128)(2,1)}, u32[]{:S(2)}, u32[]{:S(2)}) collective-permute-start(bf16[1664,256]{1,0:T(8,128)(2,1)} %get-tuple-element.32.refs_8_), channel_id=1, source_target_pairs={{0,1},{1,0},{2,3},{3,2},{4,5},{5,4},{6,7},{7,6},{8,9},{9,8},{10,11... | collective-permute-start | bytes 2555912 | tf_op jit(solution)/shard_map/ppermute | solution.py:426
  51.3 10.6 %copy-start.5 = (bf16[13,64,2048]{2,1,0:T(8,128)(2,1)S(1)}, bf16[13,64,2048]{2,1,0:T(8,128)(2,1)}, u32[]{:S(2)}) copy-start(bf16[13,64,2048]{2,1,0:T(8,128)(2,1)} %refs_6_.5) | copy-start | bytes 10223620
  58.2 28.4 %collective-permute-start.16 = (bf16[4,64,2048]{2,1,0:T(8,128)(2,1)S(1)}, bf16[4,64,2048]{2,1,0:T(8,128)(2,1)S(1)}, u32[]{:S(2)}, u32[]{:S(2)}) collective-permute-start(bf16[4,64,2048]{2,1,0:T(8,128)(2,1)S(1)} %add_convert_fusion.1.refs_16_), channel_id=1, source_target_pairs={{0,4},{12,8},{4,12},{8,0},{1,5},{13,9},{5,13},{9,1},{2,6},{14,10},... | collective-permute-start | bytes 3145736 | tf_op jit(solution)/shard_map/ppermute | solution.py:538
  66.5 11.9 %copy-start.9 = (bf16[13,64,128]{2,1,0:T(8,128)(2,1)}, bf16[13,64,128]{2,1,0:T(8,128)(2,1)S(1)}, u32[]{:S(2)}) copy-start(bf16[13,64,128]{2,1,0:T(8,128)(2,1)S(1)} %shard_map.137.refs_1_.refs_4_) | copy-start | bytes 638980
  66.5 3.4 %collective-permute-start.13 = (bf16[13,64,128]{2,1,0:T(8,128)(2,1)S(1)}, bf16[13,64,128]{2,1,0:T(8,128)(2,1)S(1)}, u32[]{:S(2)}, u32[]{:S(2)}) collective-permute-start(bf16[13,64,128]{2,1,0:T(8,128)(2,1)S(1)} %shard_map.137.refs_1_.refs_4_), channel_id=1, source_target_pairs={{0,1},{1,0},{2,3},{3,2},{4,5},{5,4},{6,7},{7,6},{8,9},{9,8},{10,11... | collective-permute-start | bytes 638984 | tf_op jit(solution)/shard_map/ppermute | solution.py:426
  66.6 8.1 %collective-permute-start.14 = (bf16[13,64,128]{2,1,0:T(8,128)(2,1)S(1)}, bf16[13,64,128]{2,1,0:T(8,128)(2,1)S(1)}, u32[]{:S(2)}, u32[]{:S(2)}) collective-permute-start(bf16[13,64,128]{2,1,0:T(8,128)(2,1)S(1)} %shard_map.137.refs_1_.refs_4_), channel_id=1, source_target_pairs={{0,2},{1,3},{2,0},{3,1},{4,6},{5,7},{6,4},{7,5},{8,10},{9,11},{10,... | collective-permute-start | bytes 638984 | tf_op jit(solution)/shard_map/ppermute | solution.py:426
  67.2 11.2 %copy-start.7 = (bf16[1664,256]{1,0:T(8,128)(2,1)S(1)}, bf16[1664,256]{1,0:T(8,128)(2,1)}, u32[]{:S(2)}) copy-start(bf16[1664,256]{1,0:T(8,128)(2,1)} %refs_5_.9) | copy-start | bytes 2555908
  67.2 11.2 %collective-permute-start.15 = (bf16[13,64,128]{2,1,0:T(8,128)(2,1)S(1)}, bf16[13,64,128]{2,1,0:T(8,128)(2,1)S(1)}, u32[]{:S(2)}, u32[]{:S(2)}) collective-permute-start(bf16[13,64,128]{2,1,0:T(8,128)(2,1)S(1)} %shard_map.137.refs_1_.refs_4_), channel_id=1, source_target_pairs={{0,3},{1,2},{2,1},{3,0},{4,7},{5,6},{6,5},{7,4},{8,11},{9,10},{10,... | collective-permute-start | bytes 638984 | tf_op jit(solution)/shard_map/ppermute | solution.py:426
  69.9 12.2 %copy-start.12 = (bf16[13,64,128]{2,1,0:T(8,128)(2,1)}, bf16[13,64,128]{2,1,0:T(8,128)(2,1)S(1)}, u32[]{:S(2)}) copy-start(bf16[13,64,128]{2,1,0:T(8,128)(2,1)S(1)} %collective-permute-done.13.refs_2_.refs_5_) | copy-start | bytes 638980
  69.9 28.2 %collective-permute-start.12 = (bf16[1664,256]{1,0:T(8,128)(2,1)S(1)}, bf16[1664,256]{1,0:T(8,128)(2,1)S(1)}, u32[]{:S(2)}, u32[]{:S(2)}) collective-permute-start(bf16[1664,256]{1,0:T(8,128)(2,1)S(1)} %add_convert_fusion.2), channel_id=1, source_target_pairs={{0,2},{1,3},{2,0},{3,1},{4,6},{5,7},{6,4},{7,5},{8,10},{9,11},{10,... | collective-permute-start | bytes 2555912 | tf_op jit(solution)/shard_map/ppermute | solution.py:426
  79.2 10.3 %collective-permute-start.19 = (bf16[4,64,256]{2,1,0:T(8,128)(2,1)S(1)}, bf16[4,64,256]{2,1,0:T(8,128)(2,1)S(1)}, u32[]{:S(2)}, u32[]{:S(2)}) collective-permute-start(bf16[4,64,256]{2,1,0:T(8,128)(2,1)S(1)} %get-tuple-element.38), channel_id=1, source_target_pairs={{0,12},{4,0},{8,4},{12,8},{1,13},{5,1},{9,5},{13,9},{2,14},{6,2},{... | collective-permute-start | bytes 393224 | tf_op jit(solution)/shard_map/ppermute | solution.py:408
  82.1 13.6 %collective-permute-start.18 = (bf16[4,64,256]{2,1,0:T(8,128)(2,1)S(1)}, bf16[4,64,256]{2,1,0:T(8,128)(2,1)S(1)}, u32[]{:S(2)}, u32[]{:S(2)}) collective-permute-start(bf16[4,64,256]{2,1,0:T(8,128)(2,1)S(1)} %get-tuple-element.37), channel_id=1, source_target_pairs={{0,8},{4,12},{8,0},{12,4},{1,9},{5,13},{9,1},{13,5},{2,10},{6,14},... | collective-permute-start | bytes 393224 | tf_op jit(solution)/shard_map/ppermute | solution.py:408
  86.6 10.7 %collective-permute-start.17 = (bf16[4,64,256]{2,1,0:T(8,128)(2,1)S(1)}, bf16[4,64,256]{2,1,0:T(8,128)(2,1)S(1)}, u32[]{:S(2)}, u32[]{:S(2)}) collective-permute-start(bf16[4,64,256]{2,1,0:T(8,128)(2,1)S(1)} %get-tuple-element.36), channel_id=1, source_target_pairs={{0,4},{4,8},{8,12},{12,0},{1,5},{5,9},{9,13},{13,1},{2,6},{6,10},{... | collective-permute-start | bytes 393224 | tf_op jit(solution)/shard_map/ppermute | solution.py:408
  89.6 30.6 %collective-permute-start.24 = (bf16[4,64,2048]{2,1,0:T(8,128)(2,1)}, bf16[4,64,2048]{2,1,0:T(8,128)(2,1)}, u32[]{:S(2)}, u32[]{:S(2)}) collective-permute-start(bf16[4,64,2048]{2,1,0:T(8,128)(2,1)} %shard_map.144.refs_1_), channel_id=1, source_target_pairs={{0,4},{12,8},{4,0},{8,12},{1,5},{13,9},{5,1},{9,13},{2,6},{14,10},... | collective-permute-start | bytes 3145736 | tf_op jit(solution)/shard_map/ppermute | solution.py:548
  95.7 24.5 %collective-permute-start.23 = (bf16[4,64,2048]{2,1,0:T(8,128)(2,1)S(1)}, bf16[4,64,2048]{2,1,0:T(8,128)(2,1)}, u32[]{:S(2)}, u32[]{:S(2)}) collective-permute-start(bf16[4,64,2048]{2,1,0:T(8,128)(2,1)S(1)} %shard_map.145), channel_id=1, source_target_pairs={{4,8},{8,4},{5,9},{9,5},{6,10},{10,6},{7,11},{11,7},{20,24},{24,20... | collective-permute-start | bytes 3145736 | tf_op jit(solution)/shard_map/ppermute | solution.py:546
  103.4 18.9 %collective-permute-start.20 = (bf16[128,256]{1,0:T(8,128)(2,1)}, bf16[128,256]{1,0:T(8,128)(2,1)S(1)}, u32[]{:S(2)}, u32[]{:S(2)}) collective-permute-start(bf16[128,256]{1,0:T(8,128)(2,1)} %get-tuple-element.39.refs_2_), channel_id=1, source_target_pairs={{0,4},{4,8},{8,12},{12,0},{1,5},{5,9},{9,13},{13,1},{2,6},{6,10},{... | collective-permute-start | bytes 196616 | tf_op jit(solution)/shard_map/ppermute | solution.py:408
  103.6 20.4 %collective-permute-start.21 = (bf16[128,256]{1,0:T(8,128)(2,1)}, bf16[128,256]{1,0:T(8,128)(2,1)S(1)}, u32[]{:S(2)}, u32[]{:S(2)}) collective-permute-start(bf16[128,256]{1,0:T(8,128)(2,1)} %get-tuple-element.39.refs_2_), channel_id=1, source_target_pairs={{0,8},{4,12},{8,0},{12,4},{1,9},{5,13},{9,1},{13,5},{2,10},{6,14},... | collective-permute-start | bytes 196616 | tf_op jit(solution)/shard_map/ppermute | solution.py:408
  105.6 18.5 %collective-permute-start.22 = (bf16[128,256]{1,0:T(8,128)(2,1)}, bf16[128,256]{1,0:T(8,128)(2,1)S(1)}, u32[]{:S(2)}, u32[]{:S(2)}) collective-permute-start(bf16[128,256]{1,0:T(8,128)(2,1)} %get-tuple-element.39.refs_2_), channel_id=1, source_target_pairs={{0,12},{4,0},{8,4},{12,8},{1,13},{5,1},{9,5},{13,9},{2,14},{6,2},{... | collective-permute-start | bytes 196616 | tf_op jit(solution)/shard_map/ppermute | solution.py:408
  107.6 16.4 %copy-start.15 = (bf16[128,256]{1,0:T(8,128)(2,1)S(1)}, bf16[128,256]{1,0:T(8,128)(2,1)}, u32[]{:S(2)}) copy-start(bf16[128,256]{1,0:T(8,128)(2,1)} %get-tuple-element.39.refs_2_) | copy-start | bytes 196612
  (21 other events, 109.1 us)
